TPU v7x, 32 devices: a whole 2x2x4 slice. The times are simulated.
32 devices in a mesh: groups: 2 (over y), dp: 4 (over z), tensor: 2 (over x), replica: 2 (over core).
Axes of the slice: x: 2, y: 2, z: 4, core: 2. Of those that a mesh axis runs over, the one named last changes fastest.
Arguments:
- tokens: bfloat16 [2048, 4096], P(('groups', 'dp')), parts along dimension 0, may hold values from -6 to 6
- upstream: bfloat16 [2048, 4096], P(('groups', 'dp'), ('tensor', 'replica')), parts along dimension 0, may hold values from -6 to 6
- blocks: bfloat16 [1024, 128, 128], P(('dp', 'tensor', 'replica')), may hold values from -0.125 to 0.125
- block_ids: int32 [1024], P(('dp', 'tensor', 'replica')), may hold values from 0 to 256, as said below
Outputs:
- projected: bfloat16 [2048, 4096], P(('groups', 'dp'), ('tensor', 'replica')), parts along dimension 0
- token_grad: bfloat16 [2048, 4096], P(('groups', 'dp')), parts along dimension 0
- block_grad: bfloat16 [2048, 128, 128], P(('groups', 'dp', 'tensor', 'replica')), parts along dimension 0
There are 2 independent parts, one for each index of `groups`. A program takes and returns all parts, laid end to end along the dimension named above; an argument that names none is the same for every part. Nothing has to cross between parts.
Inputs may be any that keep to these rules, and one draw needn't show every extreme that they name: `block_ids`: within each slab, every block column holds exactly half of the 32 block rows, each filled block stands in exactly one slot, empty slots carry the id (32) * (4096 // (128 * 2 * 2)), and some device of each slab has all 64 slots filled.
All inputs are finite; a program needn't handle non-finite values.
Results may differ from a plain program's by a relative error of at most 0.012.
Values may be sent and summed in bfloat16 or wider, within the bound.
No kernel may reach another device: no remote copies, remote signals or barrier semaphores. Data moves between devices by JAX's collectives and lax.ppermute only.
A program may use at most 128 MiB of HBM per device.

v0:
```python
import math

import jax
import jax.numpy as jnp
from jax import lax
from jax.sharding import PartitionSpec as P


def one_hots(ids, rows_n, cols_n):
    row_hot = (ids // cols_n)[:, None] == jnp.arange(rows_n, dtype=jnp.int32)[None, :]
    filled = ids < rows_n * cols_n
    col_hot = ((ids % cols_n)[:, None] == jnp.arange(cols_n, dtype=jnp.int32)[None, :]) & filled[
        :, None
    ]
    return (row_hot, col_hot)


def forward_piece(tokens, weight_piece, ids, rows_n, cols_n):
    row_hot, col_hot = one_hots(ids, rows_n, cols_n)
    x_view = tokens.reshape(tokens.shape[0], rows_n, -1)
    x_sel = jnp.einsum(
        "trk,nr->tnk", x_view, row_hot.astype(jnp.bfloat16), preferred_element_type=jnp.float32
    ).astype(jnp.bfloat16)
    partial_out = jnp.einsum(
        "tnk,nkj->tnj", x_sel, weight_piece, preferred_element_type=jnp.float32
    )
    placed = jnp.einsum(
        "tnj,nc->tcj", partial_out, col_hot.astype(jnp.float32), precision=lax.Precision.HIGHEST
    )
    return placed.reshape(tokens.shape[0], -1)


def backward_piece(tokens, upstream, weight_piece, ids, rows_n, cols_n):
    row_hot, col_hot = one_hots(ids, rows_n, cols_n)
    x_view = tokens.reshape(tokens.shape[0], rows_n, -1)
    d_view = upstream.reshape(upstream.shape[0], cols_n, -1)
    x_sel = jnp.einsum(
        "trk,nr->tnk", x_view, row_hot.astype(jnp.bfloat16), preferred_element_type=jnp.float32
    ).astype(jnp.bfloat16)
    d_sel = jnp.einsum(
        "tcj,nc->tnj", d_view, col_hot.astype(jnp.bfloat16), preferred_element_type=jnp.float32
    ).astype(jnp.bfloat16)
    back = jnp.einsum("tnj,nkj->tnk", d_sel, weight_piece, preferred_element_type=jnp.float32)
    placed = jnp.einsum(
        "tnk,nr->trk", back, row_hot.astype(jnp.float32), precision=lax.Precision.HIGHEST
    )
    weight_term = jnp.einsum("tnk,tnj->nkj", x_sel, d_sel, preferred_element_type=jnp.float32)
    return (placed.reshape(tokens.shape[0], -1), weight_term)


def body(tokens, upstream, blocks, block_ids):
    block_size = blocks.shape[1]
    rows_n = tokens.shape[1] // block_size
    cols_n = upstream.shape[1] // block_size
    n_dp = lax.axis_size("dp")
    all_slots = n_dp * blocks.shape[0]
    out_start = jnp.zeros((tokens.shape[0], upstream.shape[1]), jnp.float32)
    back_start = jnp.zeros(tokens.shape, jnp.float32)
    gathered, gathered_ids = (
        lax.all_gather(blocks, "dp", axis=0, tiled=True),
        lax.all_gather(block_ids, "dp", axis=0, tiled=True),
    )
    steps_n = math.gcd(8, n_dp)
    weight_steps = gathered.reshape(steps_n, -1, block_size, block_size)
    id_steps = gathered_ids.reshape(steps_n, -1)

    def forward_step(total, pair):
        return (total + forward_piece(tokens, pair[0], pair[1], rows_n, cols_n), None)

    projected_sum, unused = lax.scan(forward_step, out_start, (weight_steps, id_steps))

    def backward_step(total, pair):
        placed, weight_term = backward_piece(tokens, upstream, pair[0], pair[1], rows_n, cols_n)
        return (total + placed, weight_term)

    back_sum, grad_steps = lax.scan(backward_step, back_start, (weight_steps, id_steps))
    grad_all = grad_steps.reshape(all_slots, block_size, block_size)
    token_grad = lax.psum(back_sum.astype(jnp.bfloat16), ("tensor", "replica"))
    rounded = grad_all.astype(jnp.bfloat16)
    block_grad = lax.psum_scatter(
        rounded.astype(jnp.float32).astype(jnp.bfloat16), "dp", scatter_dimension=0, tiled=True
    )
    return (projected_sum.astype(jnp.bfloat16), token_grad, block_grad)


def solution(mesh):
    return jax.shard_map(
        body,
        mesh=mesh,
        in_specs=(
            P(("groups", "dp"), None),
            P(("groups", "dp"), ("tensor", "replica")),
            P(("dp", "tensor", "replica"), None, None),
            P(("dp", "tensor", "replica")),
        ),
        out_specs=(
            P(("groups", "dp"), ("tensor", "replica")),
            P(("groups", "dp"), None),
            P(("groups", "dp", "tensor", "replica"), None, None),
        ),
        check_vma=False,
    )
```

profile of v0, /device:TPU:0, one launch (start us, length us, event | category | flops | bytes accessed | tf_op | source)
XLA Modules:
  0.0 580.9 jit_solution(16737698837698174089)
XLA Ops:
  8.0 1.2 dynamic-slice
  10.7 9.9 %all-reduce = s32[256]{0:T(256)S(1)} all-reduce(s32[256]{0:T(256)S(1)} %dynamic-update-slice), channel_id=1, replica_groups=mesh['groups'=2,'dp'=4,'tensor'=2,'replica'=2] {'dp'}, use_global_device_ids=true, to_apply=%add | all-reduce | flops 256 | bytes 2048
  20.7 141.2 %all-gather.2.cloned.1.call-done = bf16[256,128,128]{2,1,0:T(8,128)(2,1)} async-done(((bf16[64,128,128]{2,1,0:T(8,128)(2,1)}), bf16[256,128,128]{2,1,0:T(8,128)(2,1)}) %all-gather.2.cloned.1.call-update) | async-done | bytes 8388624 | tf_op jit(solution)/shard_map/all_gather | solution.py:60
  161.9 208.1 %while.29 = (s32[]{:T(128)}, f32[256,4096]{1,0:T(8,128)}, bf16[4,64,128,128]{3,2,1,0:T(8,128)(2,1)}, s32[4,64]{1,0:T(4,128)S(1)}, bf16[4,64,128,128]{3,2,1,0:T(8...) while((s32[]{:T(128)}, f32[256,4096]{1,0:T(8,128)}, ...), condition=%wide.region_3.4_spmd.clone, body=%wide.region_2.3_spmd.clone.sunk | while | flops 2051021056 | bytes 144181872 | solution.py:76
  163.1 2.1 copy.51
  165.2 3.2 fusion.90
  168.4 6.9 %copy.52 = bf16[64,256,128]{1,2,0:T(8,128)(2,1)} copy(bf16[64,256,128]{2,0,1:T(8,128)(2,1)} %fusion.90) | data formatting | bytes 8388608 | tf_op jit(solution)/shard_map/while/body/eval_jaxpr/trk,nr->tnk/dot_general | solution.py:37
  175.3 1.3 convert_bitcast_fusion.2
  177.5 6.6 %bitcast_dynamic-update-slice_fusion.2 = bf16[4,64,128,128]{3,2,1,0:T(8,128)(2,1)} fusion(bf16[4,64,128,128]{3,2,1,0:T(8,128)(2,1)} %get-tuple-element.351, s32[]{:T(128)S(6)} %copy.64, bf16[256,64,128]{2,1,0:T(8,128)(2,1)S(1)} %convert_bitcast_fusion.2, bf16[64,256,128]{1,2,0:T(8,128)(2,1)S(1)} %copy-done), kind=kOutput, calls=%fused_computation.29.clone.1 | convolution fusion | flops 536870912 | bytes 12582916 | tf_op jit(solution)/shard_map/while/body/eval_jaxpr/tnk,tnj->nkj/dot_general | solution.py:47
  184.1 9.4 %fusion.88 = f32[64,128,256]{2,1,0:T(8,128)} fusion(bf16[256,64,128]{2,1,0:T(8,128)(2,1)S(1)} %convert_bitcast_fusion.2, bf16[4,64,128,128]{3,2,1,0:T(8,128)(2,1)} %get-tuple-element.362, s32[]{:T(128)S(6)} %copy.64), kind=kOutput, calls=%fused_computation.34.clone.1 | convolution fusion | flops 536870912 | bytes 14680068 | tf_op jit(solution)/shard_map/while/body/eval_jaxpr/tnj,nkj->tnk/dot_general | solution.py:43
  193.5 8.7 %copy.50 = f32[64,128,256]{1,0,2:T(8,128)} copy(f32[64,128,256]{2,1,0:T(8,128)} %fusion.88) | data formatting | bytes 16777216 | tf_op jit(solution)/shard_map/while/body/eval_jaxpr/tnj,nkj->tnk/dot_general | solution.py:43
  202.3 5.6 fusion.89
  207.8 4.1 bitcast_add_fusion.5
  211.9 2.1 copy-done.3
  215.2 2.1 copy.51
  217.2 3.2 fusion.90
  220.5 6.9 %copy.52 = bf16[64,256,128]{1,2,0:T(8,128)(2,1)} copy(bf16[64,256,128]{2,0,1:T(8,128)(2,1)} %fusion.90) | data formatting | bytes 8388608 | tf_op jit(solution)/shard_map/while/body/eval_jaxpr/trk,nr->tnk/dot_general | solution.py:37
  227.4 1.3 convert_bitcast_fusion.2
  229.5 6.6 %bitcast_dynamic-update-slice_fusion.2 = bf16[4,64,128,128]{3,2,1,0:T(8,128)(2,1)} fusion(bf16[4,64,128,128]{3,2,1,0:T(8,128)(2,1)} %get-tuple-element.351, s32[]{:T(128)S(6)} %copy.64, bf16[256,64,128]{2,1,0:T(8,128)(2,1)S(1)} %convert_bitcast_fusion.2, bf16[64,256,128]{1,2,0:T(8,128)(2,1)S(1)} %copy-done), kind=kOutput, calls=%fused_computation.29.clone.1 | convolution fusion | flops 536870912 | bytes 12582916 | tf_op jit(solution)/shard_map/while/body/eval_jaxpr/tnk,tnj->nkj/dot_general | solution.py:47
  236.1 9.4 %fusion.88 = f32[64,128,256]{2,1,0:T(8,128)} fusion(bf16[256,64,128]{2,1,0:T(8,128)(2,1)S(1)} %convert_bitcast_fusion.2, bf16[4,64,128,128]{3,2,1,0:T(8,128)(2,1)} %get-tuple-element.362, s32[]{:T(128)S(6)} %copy.64), kind=kOutput, calls=%fused_computation.34.clone.1 | convolution fusion | flops 536870912 | bytes 14680068 | tf_op jit(solution)/shard_map/while/body/eval_jaxpr/tnj,nkj->tnk/dot_general | solution.py:43
  245.5 8.7 %copy.50 = f32[64,128,256]{1,0,2:T(8,128)} copy(f32[64,128,256]{2,1,0:T(8,128)} %fusion.88) | data formatting | bytes 16777216 | tf_op jit(solution)/shard_map/while/body/eval_jaxpr/tnj,nkj->tnk/dot_general | solution.py:43
  254.3 5.6 fusion.89
  259.8 4.1 bitcast_add_fusion.5
  263.9 2.1 copy-done.3
  267.2 2.1 copy.51
  269.2 3.2 fusion.90
  272.5 6.9 %copy.52 = bf16[64,256,128]{1,2,0:T(8,128)(2,1)} copy(bf16[64,256,128]{2,0,1:T(8,128)(2,1)} %fusion.90) | data formatting | bytes 8388608 | tf_op jit(solution)/shard_map/while/body/eval_jaxpr/trk,nr->tnk/dot_general | solution.py:37
  279.4 1.3 convert_bitcast_fusion.2
  281.5 6.6 %bitcast_dynamic-update-slice_fusion.2 = bf16[4,64,128,128]{3,2,1,0:T(8,128)(2,1)} fusion(bf16[4,64,128,128]{3,2,1,0:T(8,128)(2,1)} %get-tuple-element.351, s32[]{:T(128)S(6)} %copy.64, bf16[256,64,128]{2,1,0:T(8,128)(2,1)S(1)} %convert_bitcast_fusion.2, bf16[64,256,128]{1,2,0:T(8,128)(2,1)S(1)} %copy-done), kind=kOutput, calls=%fused_computation.29.clone.1 | convolution fusion | flops 536870912 | bytes 12582916 | tf_op jit(solution)/shard_map/while/body/eval_jaxpr/tnk,tnj->nkj/dot_general | solution.py:47
  288.1 9.4 %fusion.88 = f32[64,128,256]{2,1,0:T(8,128)} fusion(bf16[256,64,128]{2,1,0:T(8,128)(2,1)S(1)} %convert_bitcast_fusion.2, bf16[4,64,128,128]{3,2,1,0:T(8,128)(2,1)} %get-tuple-element.362, s32[]{:T(128)S(6)} %copy.64), kind=kOutput, calls=%fused_computation.34.clone.1 | convolution fusion | flops 536870912 | bytes 14680068 | tf_op jit(solution)/shard_map/while/body/eval_jaxpr/tnj,nkj->tnk/dot_general | solution.py:43
  297.6 8.7 %copy.50 = f32[64,128,256]{1,0,2:T(8,128)} copy(f32[64,128,256]{2,1,0:T(8,128)} %fusion.88) | data formatting | bytes 16777216 | tf_op jit(solution)/shard_map/while/body/eval_jaxpr/tnj,nkj->tnk/dot_general | solution.py:43
  306.3 5.6 fusion.89
  311.8 4.1 bitcast_add_fusion.5
  315.9 2.1 copy-done.3
  319.2 2.1 copy.51
  321.3 3.2 fusion.90
  324.5 6.9 %copy.52 = bf16[64,256,128]{1,2,0:T(8,128)(2,1)} copy(bf16[64,256,128]{2,0,1:T(8,128)(2,1)} %fusion.90) | data formatting | bytes 8388608 | tf_op jit(solution)/shard_map/while/body/eval_jaxpr/trk,nr->tnk/dot_general | solution.py:37
  331.4 1.3 convert_bitcast_fusion.2
  333.6 6.6 %bitcast_dynamic-update-slice_fusion.2 = bf16[4,64,128,128]{3,2,1,0:T(8,128)(2,1)} fusion(bf16[4,64,128,128]{3,2,1,0:T(8,128)(2,1)} %get-tuple-element.351, s32[]{:T(128)S(6)} %copy.64, bf16[256,64,128]{2,1,0:T(8,128)(2,1)S(1)} %convert_bitcast_fusion.2, bf16[64,256,128]{1,2,0:T(8,128)(2,1)S(1)} %copy-done), kind=kOutput, calls=%fused_computation.29.clone.1 | convolution fusion | flops 536870912 | bytes 12582916 | tf_op jit(solution)/shard_map/while/body/eval_jaxpr/tnk,tnj->nkj/dot_general | solution.py:47
  340.1 9.4 %fusion.88 = f32[64,128,256]{2,1,0:T(8,128)} fusion(bf16[256,64,128]{2,1,0:T(8,128)(2,1)S(1)} %convert_bitcast_fusion.2, bf16[4,64,128,128]{3,2,1,0:T(8,128)(2,1)} %get-tuple-element.362, s32[]{:T(128)S(6)} %copy.64), kind=kOutput, calls=%fused_computation.34.clone.1 | convolution fusion | flops 536870912 | bytes 14680068 | tf_op jit(solution)/shard_map/while/body/eval_jaxpr/tnj,nkj->tnk/dot_general | solution.py:43
  349.5 8.7 %copy.50 = f32[64,128,256]{1,0,2:T(8,128)} copy(f32[64,128,256]{2,1,0:T(8,128)} %fusion.88) | data formatting | bytes 16777216 | tf_op jit(solution)/shard_map/while/body/eval_jaxpr/tnj,nkj->tnk/dot_general | solution.py:43
  358.3 5.6 fusion.89
  363.8 4.1 bitcast_add_fusion.5
  367.9 2.1 copy-done.3
  370.0 3.8 convert_element_type.47
  375.5 102.8 %while.28 = (s32[]{:T(128)}, f32[256,1024]{1,0:T(8,128)S(1)}, s32[4,64]{1,0:T(4,128)S(1)}, bf16[4,64,128,128]{3,2,1,0:T(8,128)(2,1)}, bf16[256,4096]{1,0:T(8,128)(2,1)S(1)}, /*index=5*/s32[]{:T(128)}, s32[]{:T(128)}) while((s32[]{:T(128)}, f32[256,1024]{1,0:T(8,128)S(1)}, s32[4,64]{1,0:T(4,128)S(1)}, ...), condition=%wide.region_1.2_spmd.clone, body=%wide.region_0.1_spmd.clone.sunk | while | flops 872944128 | bytes 54528492 | solution.py:70
  376.0 1.3 fusion.75
  377.3 9.6 %fusion.76 = f32[64,128,256]{2,1,0:T(8,128)} fusion(bf16[64,256,128]{2,0,1:T(8,128)(2,1)S(1)} %fusion.75, bf16[4,64,128,128]{3,2,1,0:T(8,128)(2,1)} %get-tuple-element.336, s32[]{:T(128)S(6)} %copy.57), kind=kOutput, calls=%fused_computation.4.clone.1 | convolution fusion | flops 536870912 | bytes 14680068 | tf_op jit(solution)/shard_map/while/body/eval_jaxpr/tnk,nkj->tnj/dot_general | solution.py:24
  386.9 8.8 %copy.45 = f32[64,128,256]{1,0,2:T(8,128)} copy(f32[64,128,256]{2,1,0:T(8,128)} %fusion.76) | data formatting | bytes 16777216 | tf_op jit(solution)/shard_map/while/body/eval_jaxpr/tnk,nkj->tnj/dot_general | solution.py:24
  395.6 5.1 fusion.77
  401.8 1.3 fusion.75
  403.1 9.6 %fusion.76 = f32[64,128,256]{2,1,0:T(8,128)} fusion(bf16[64,256,128]{2,0,1:T(8,128)(2,1)S(1)} %fusion.75, bf16[4,64,128,128]{3,2,1,0:T(8,128)(2,1)} %get-tuple-element.336, s32[]{:T(128)S(6)} %copy.57), kind=kOutput, calls=%fused_computation.4.clone.1 | convolution fusion | flops 536870912 | bytes 14680068 | tf_op jit(solution)/shard_map/while/body/eval_jaxpr/tnk,nkj->tnj/dot_general | solution.py:24
  412.7 8.8 %copy.45 = f32[64,128,256]{1,0,2:T(8,128)} copy(f32[64,128,256]{2,1,0:T(8,128)} %fusion.76) | data formatting | bytes 16777216 | tf_op jit(solution)/shard_map/while/body/eval_jaxpr/tnk,nkj->tnj/dot_general | solution.py:24
  421.4 5.1 fusion.77
  427.5 1.3 fusion.75
  428.8 9.5 %fusion.76 = f32[64,128,256]{2,1,0:T(8,128)} fusion(bf16[64,256,128]{2,0,1:T(8,128)(2,1)S(1)} %fusion.75, bf16[4,64,128,128]{3,2,1,0:T(8,128)(2,1)} %get-tuple-element.336, s32[]{:T(128)S(6)} %copy.57), kind=kOutput, calls=%fused_computation.4.clone.1 | convolution fusion | flops 536870912 | bytes 14680068 | tf_op jit(solution)/shard_map/while/body/eval_jaxpr/tnk,nkj->tnj/dot_general | solution.py:24
  438.3 8.8 %copy.45 = f32[64,128,256]{1,0,2:T(8,128)} copy(f32[64,128,256]{2,1,0:T(8,128)} %fusion.76) | data formatting | bytes 16777216 | tf_op jit(solution)/shard_map/while/body/eval_jaxpr/tnk,nkj->tnj/dot_general | solution.py:24
  447.0 5.1 fusion.77
  453.2 1.3 fusion.75
  454.5 9.5 %fusion.76 = f32[64,128,256]{2,1,0:T(8,128)} fusion(bf16[64,256,128]{2,0,1:T(8,128)(2,1)S(1)} %fusion.75, bf16[4,64,128,128]{3,2,1,0:T(8,128)(2,1)} %get-tuple-element.336, s32[]{:T(128)S(6)} %copy.57), kind=kOutput, calls=%fused_computation.4.clone.1 | convolution fusion | flops 536870912 | bytes 14680068 | tf_op jit(solution)/shard_map/while/body/eval_jaxpr/tnk,nkj->tnj/dot_general | solution.py:24
  463.9 8.8 %copy.45 = f32[64,128,256]{1,0,2:T(8,128)} copy(f32[64,128,256]{2,1,0:T(8,128)} %fusion.76) | data formatting | bytes 16777216 | tf_op jit(solution)/shard_map/while/body/eval_jaxpr/tnk,nkj->tnj/dot_general | solution.py:24
  472.7 5.1 fusion.77
  479.1 92.1 %reduce-scatter.2.cloned.1.call-done = bf16[64,128,128]{2,1,0:T(8,128)(2,1)} async-done(((bf16[256,128,128]{2,1,0:T(8,128)(2,1)}), bf16[64,128,128]{2,1,0:T(8,128)(2,1)}) %reduce-scatter.2.cloned.1.call-update) | async-done | bytes 2097168 | tf_op jit(solution)/shard_map/reduce_scatter | solution.py:80
  571.2 3.1 copy.71
  (72 shorter events, 16.1 us)
Async XLA Ops:
  7.2 154.8 %all-gather.2.cloned.1.call-start = ((), (), s32[]{:S(2)}) async-start(), calls=%async_computation.1 | async-start | bytes 10485760 | tf_op jit(solution)/shard_map/all_gather | solution.py:60
  7.9 471.2 %all-reduce.3.cloned.1.call-start = ((), (), s32[]{:S(2)}) async-start(), calls=%async_computation.2 | async-start | bytes 4194304 | tf_op jit(solution)/shard_map/psum | solution.py:78
  175.3 2.2 copy-start
  202.3 5.6 copy-start.2
  211.9 2.1 copy-start.3
  227.4 2.2 copy-start
  254.3 5.6 copy-start.2
  263.9 2.1 copy-start.3
  279.4 2.2 copy-start
  306.3 5.6 copy-start.2
  315.9 2.1 copy-start.3
  331.4 2.2 copy-start
  358.3 5.6 copy-start.2
  367.9 2.1 copy-start.3
  373.8 197.4 %reduce-scatter.2.cloned.1.call-start = ((), (), s32[]{:S(2)}) async-start(), calls=%async_computation.3 | async-start | bytes 10485760 | tf_op jit(solution)/shard_map/reduce_scatter | solution.py:80
  373.9 1.6 copy-start.1
Sparse Core Ops, SparseCore 0:
  9.6 152.3 all-gather.1
  373.9 49.5 all-reduce.2
  426.6 144.5 reduce-scatter.1
where the time goes:
time: 583 us; the launch traced here: 581 us
  waiting for transfers between devices  235 us (40%)
  matrix products  168 us (29%)
  local copies, waits for them, and re-layouts  130 us (22%)
  other arithmetic  22.9 us (4%)
  between operations  14.5 us (2%)
  blocking collectives  9.89 us (2%)
    all_gather x1, waiting for transfers between devices, body(): lax.all_gather(blocks, 'dp', axis=0, tiled=True)  141 us
    reduce_scatter x1, waiting for transfers between devices, body(): lax.psum_scatter(rounded.astype(jnp.float32).astype(jnp.bfloat16), 'dp',...  92.1 us
    dot_general x4, matrix products, forward_piece(): jnp.einsum('tnk,nkj->tnj', x_sel, weight_piece, preferred_element_type=jn...  38.1 us
    dot_general x4, matrix products, backward_piece(): jnp.einsum('tnj,nkj->tnk', d_sel, weight_piece, preferred_element_type=jn...  37.7 us
    dot_general x4, local copies, waits for them, and re-layouts, forward_piece(): jnp.einsum('tnk,nkj->tnj', x_sel, weight_piece, preferred_element_type=jn...  35.1 us
    dot_general x4, local copies, waits for them, and re-layouts, backward_piece(): jnp.einsum('tnj,nkj->tnk', d_sel, weight_piece, preferred_element_type=jn...  34.8 us
    dot_general x4, local copies, waits for them, and re-layouts, backward_piece(): jnp.einsum('trk,nr->tnk', x_view, row_hot.astype(jnp.bfloat16), preferred...  27.5 us
    while x36, local copies, waits for them, and re-layouts  26.6 us
  transfers between devices with their start and end apart: 3, of which 2 were waited for; matrix products, arithmetic and copies ran while one was open for 18% of the time, Pallas kernels for 0%

commit v1 on v0

v1 whole, which is shorter than its diff:
```python
import functools

import jax
import jax.numpy as jnp
from jax import lax
from jax.experimental import pallas as pl
from jax.experimental.pallas import tpu as pltpu
from jax.sharding import PartitionSpec as P

VMEM_LIMIT = 60 * 1024 * 1024
INNER = ("tensor", "replica")


def whole(space=pltpu.VMEM):
    return pl.BlockSpec(memory_space=space)


def project_kernel(ids, blocks, tokens, upstream, proj, back, weight):
    slots, size = blocks.shape[0], blocks.shape[1]
    depth, width = weight.shape
    cols_n = width // size
    total = (depth // size) * cols_n
    weight[...] = jnp.zeros_like(weight)

    @pl.loop(0, slots)
    def place(s):
        b = ids[s]

        @pl.when(b < total)
        def put():
            r = pl.multiple_of((b // cols_n) * size, size)
            c = pl.multiple_of((b % cols_n) * size, size)
            weight[pl.ds(r, size), pl.ds(c, size)] = blocks[s]

    step = 256

    @pl.loop(0, width // step)
    def forward(n):
        c = pl.multiple_of(n * step, step)
        proj[:, pl.ds(c, step)] = jnp.dot(
            tokens[...], weight[:, pl.ds(c, step)], preferred_element_type=jnp.float32
        ).astype(proj.dtype)

    @pl.loop(0, depth // step)
    def backward(n):
        r = pl.multiple_of(n * step, step)
        back[:, pl.ds(r, step)] = lax.dot_general(
            upstream[...],
            weight[pl.ds(r, step), :],
            (((1,), (1,)), ((), ())),
            preferred_element_type=jnp.float32,
        ).astype(back.dtype)


def project(ids, blocks, tokens, upstream):
    rows, depth = tokens.shape
    width = upstream.shape[1]
    return pl.pallas_call(
        project_kernel,
        out_shape=(
            jax.ShapeDtypeStruct((rows, width), jnp.bfloat16),
            jax.ShapeDtypeStruct((rows, depth), jnp.bfloat16),
        ),
        in_specs=[whole(pltpu.SMEM), whole(), whole(), whole()],
        out_specs=(whole(), whole()),
        scratch_shapes=[pltpu.VMEM((depth, width), jnp.bfloat16)],
        compiler_params=pltpu.CompilerParams(vmem_limit_bytes=VMEM_LIMIT),
        cost_estimate=pl.CostEstimate(
            flops=4 * rows * depth * width,
            bytes_accessed=blocks.size * 2 + rows * (depth + width) * 4,
            transcendentals=0,
        ),
        name="project",
    )(ids, blocks, tokens, upstream)


def block_grad_kernel(ids, tokens, upstream, grads):
    slots, size = grads.shape[0], grads.shape[1]
    parts, slabs, _, part_width = tokens.shape
    cols_n = upstream.shape[2] // size
    per_part = part_width // size
    total = parts * per_part * cols_n

    @pl.loop(0, slots)
    def one(s):
        b = ids[s]

        @pl.when(b < total)
        def fill():
            row = b // cols_n
            part = row // per_part
            r = pl.multiple_of((row % per_part) * size, size)
            c = pl.multiple_of((b % cols_n) * size, size)
            acc = jnp.zeros((size, size), jnp.float32)
            for k in range(slabs):
                acc += lax.dot_general(
                    tokens[part, k, :, pl.ds(r, size)],
                    upstream[k, :, pl.ds(c, size)],
                    (((0,), (0,)), ((), ())),
                    preferred_element_type=jnp.float32,
                )
            grads[s] = acc.astype(grads.dtype)

        @pl.when(b >= total)
        def clear():
            grads[s] = jnp.zeros((size, size), grads.dtype)


def block_grads(ids, tokens, upstream, size):
    slots = ids.shape[0]
    parts, slabs, rows, part_width = tokens.shape
    return pl.pallas_call(
        block_grad_kernel,
        out_shape=jax.ShapeDtypeStruct((slots, size, size), jnp.bfloat16),
        in_specs=[whole(pltpu.SMEM), whole(), whole()],
        out_specs=whole(),
        compiler_params=pltpu.CompilerParams(vmem_limit_bytes=VMEM_LIMIT),
        cost_estimate=pl.CostEstimate(
            flops=2 * slots * slabs * rows * size * size,
            bytes_accessed=2 * (tokens.size + upstream.size + slots * size * size),
            transcendentals=0,
        ),
        name="block_grads",
    )(ids, tokens, upstream)


def general_body(tokens, upstream, blocks, block_ids):
    size = blocks.shape[1]
    all_blocks = lax.all_gather(blocks, "dp", axis=0, tiled=True)
    all_ids = lax.all_gather(block_ids, "dp", axis=0, tiled=True)
    proj, back = project(all_ids, all_blocks, tokens, upstream)
    terms = block_grads(all_ids, tokens[None, None], upstream[None], size)
    grads = lax.psum_scatter(terms, "dp", scatter_dimension=0, tiled=True)
    return proj, lax.psum(back, INNER), grads


def body(tokens, upstream, blocks, block_ids):
    size = blocks.shape[1]
    inner_n = lax.axis_size("tensor") * lax.axis_size("replica")
    inner = lax.axis_index(INNER)
    quarter_width = tokens.shape[1] // inner_n
    all_blocks = lax.all_gather(blocks, "dp", axis=0, tiled=True)
    all_ids = lax.all_gather(block_ids, "dp", axis=0, tiled=True)
    quarter = lax.dynamic_slice_in_dim(tokens, inner * quarter_width, quarter_width, 1)
    quarters = lax.all_gather(quarter, "dp")
    all_tokens = lax.all_gather(quarters, INNER)
    all_upstream = lax.all_gather(upstream, "dp")
    proj, back = project(all_ids, all_blocks, tokens, upstream)
    token_grad = lax.psum(back, INNER)
    grads = block_grads(block_ids, all_tokens, all_upstream, size)
    return proj, token_grad, grads


def solution(mesh):
    small = mesh.shape["dp"] <= 4
    return jax.shard_map(
        body if small else general_body,
        mesh=mesh,
        in_specs=(
            P(("groups", "dp"), None),
            P(("groups", "dp"), INNER),
            P(("dp",) + INNER, None, None),
            P(("dp",) + INNER),
        ),
        out_specs=(
            P(("groups", "dp"), INNER),
            P(("groups", "dp"), None),
            P(("groups", "dp") + INNER, None, None),
        ),
        check_vma=False,
    )
```

time: 583 us -> 377 us (0.65)
  matrix products: 168 us -> 0 us
  local copies, waits for them, and re-layouts: 130 us -> 5.85 us
  waiting for transfers between devices: 235 us -> 323 us
  Pallas kernels: 0 us -> 25.8 us
  other arithmetic: 22.9 us -> 0 us
    dot_general x32 -> x0, matrix products: 168 us -> none  [the longest x4 38.1 us: forward_piece(): jnp.einsum('tnk,nkj->tnj', x_sel, weight_piece, preferred_element_type=jn...]
    all_gather x1 -> x4, waiting for transfers between devices: 141 us -> 274 us  [the longest x1 141 us: body(): all_blocks = lax.all_gather(blocks, 'dp', axis=0, tiled=True)]
    dot_general x12 -> x0, local copies, waits for them, and re-layouts: 97.4 us -> none  [the longest x4 35.1 us: forward_piece(): jnp.einsum('tnk,nkj->tnj', x_sel, weight_piece, preferred_element_type=jn...]
    reduce_scatter x1 -> x0, waiting for transfers between devices: 92.1 us -> none  [body(): lax.psum_scatter(rounded.astype(jnp.float32).astype(jnp.bfloat16), 'dp',...]
    psum x1, waiting for transfers between devices: 0.01 us -> 47.6 us  [body(): token_grad = lax.psum(back, INNER)]
    while x36 -> x0, local copies, waits for them, and re-layouts: 26.6 us -> none
    pallas_call x0 -> x2, Pallas kernels: none -> 25.8 us  [the longest x1 19.2 us: project(): pl.pallas_call(project_kernel, out_shape=(jax.ShapeDtypeStruct((rows, wid...]
    add x8 -> x0, other arithmetic: 18 us -> none  [the longest x4 16.3 us: backward_step(): return (total + placed, weight_term)]
  transfers between devices with their start and end apart: 3 -> 5, of which waited for: 2 -> 5; matrix products, arithmetic and copies ran while one was open for 18% -> 0% of each run, Pallas kernels for 0% -> 7%
where the time goes in v1:
time: 377 us
  waiting for transfers between devices  323 us (86%)
  Pallas kernels  25.8 us (7%)
  between operations  14.5 us (4%)
  blocking collectives  7.45 us (2%)
  local copies, waits for them, and re-layouts  5.85 us (2%)
    all_gather x1, waiting for transfers between devices, body(): all_blocks = lax.all_gather(blocks, 'dp', axis=0, tiled=True)  141 us
    all_gather x1, waiting for transfers between devices, body(): all_tokens = lax.all_gather(quarters, INNER)  58.3 us
    all_gather x1, waiting for transfers between devices, body(): quarters = lax.all_gather(quarter, 'dp')  48.1 us
    psum x1, waiting for transfers between devices, body(): token_grad = lax.psum(back, INNER)  47.6 us
    all_gather x1, waiting for transfers between devices, body(): all_upstream = lax.all_gather(upstream, 'dp')  26.6 us
    pallas_call x1, Pallas kernels, project(): pl.pallas_call(project_kernel, out_shape=(jax.ShapeDtypeStruct((rows, wid...  19.2 us
  transfers between devices with their start and end apart: 5, of which 5 were waited for; matrix products, arithmetic and copies ran while one was open for 0% of the time, Pallas kernels for 7%

profile of v1, /device:TPU:0, one launch (start us, length us, event | category | flops | bytes accessed | tf_op | source)
XLA Modules:
  0.0 376.8 jit_solution(5144170306912792196)
XLA Ops:
  7.2 0.0 all-gather.10.cloned.1.call-start
  7.2 1.9 constant_dynamic-slice_fusion
  9.1 0.0 all-gather.10.cloned.1.call-update
  9.1 0.0 copy-start.1
  9.1 0.0 copy-start
  9.1 0.0 all-gather.8.cloned.1.call-start
  9.2 0.7 all-gather.8.cloned.1.call-update
  9.9 0.0 all-gather.14.cloned.1.call-start
  9.9 0.7 all-gather.14.cloned.1.call-update
  10.6 0.0 all-gather.12.cloned.1.call-start
  10.7 48.1 %all-gather.10.cloned.1.call-done = bf16[1024,1024]{1,0:T(8,128)(2,1)} async-done(((bf16[256,1024]{1,0:T(8,128)(2,1)}), bf16[1024,1024]{1,0:T(8,128)(2,1)}) %all-gather.10.cloned.1.call-update) | async-done | bytes 2097168 | tf_op jit(solution)/shard_map/all_gather | solution.py:145
  58.8 0.0 all-gather.12.cloned.1.call-update
  58.8 0.0 all-reduce.3.cloned.1.call-start
  58.9 0.0 copy-done.1
  58.9 0.6 dynamic-slice
  60.1 0.0 copy-done
  60.2 0.2 dynamic-update-slice
  60.4 7.5 %all-reduce.ids = s32[256]{0:T(256)} all-reduce(s32[256]{0:T(256)S(1)} %dynamic-update-slice), channel_id=1, replica_groups=mesh['groups'=2,'dp'=4,'tensor'=2,'replica'=2] {'dp'}, use_global_device_ids=true, to_apply=%add | all-reduce | flops 256 | bytes 2048
  67.9 140.9 %all-gather.8.cloned.1.call-done.blocks = bf16[256,128,128]{2,1,0:T(8,128)(2,1)} async-done(((bf16[64,128,128]{2,1,0:T(8,128)(2,1)}), bf16[256,128,128]{2,1,0:T(8,128)(2,1)}) %all-gather.8.cloned.1.call-update) | async-done | bytes 8388624 | tf_op jit(solution)/shard_map/all_gather | solution.py:142
  208.8 19.2 %project.1 = (bf16[256,1024]{1,0:T(8,128)(2,1)}, bf16[256,4096]{1,0:T(8,128)(2,1)}) custom-call(s32[256]{0:T(256)} %all-reduce.ids, bf16[256,128,128]{2,1,0:T(8,128)(2,1)} %all-gather.8.cloned.1.call-done.blocks, bf16[256,4096]{1,0:T(8,128)(2,1)} %tokens.1, bf16[256,1024]{1,0:T(8,128)(2,1)} %upstream.1), custom_call_target="tpu_custom_call" | custom-call | flops 4294967296 | bytes 13631488 | tf_op jit(solution)/shard_map/project/pallas_call | solution.py:58
  228.0 0.0 all-reduce.3.cloned.1.call-update
  228.0 26.6 %all-gather.14.cloned.1.call-done = bf16[1024,1024]{1,0:T(8,128)(2,1)} async-done(((bf16[256,1024]{1,0:T(8,128)(2,1)}), bf16[1024,1024]{1,0:T(8,128)(2,1)}) %all-gather.14.cloned.1.call-update) | async-done | bytes 2097168 | tf_op jit(solution)/shard_map/all_gather | solution.py:147
  254.6 58.3 %all-gather.12.cloned.1.call-done = bf16[16,256,1024]{2,1,0:T(8,128)(2,1)} async-done(((bf16[4,256,1024]{2,1,0:T(8,128)(2,1)}), bf16[16,256,1024]{2,1,0:T(8,128)(2,1)}) %all-gather.12.cloned.1.call-update) | async-done | bytes 8388624 | tf_op jit(solution)/shard_map/all_gather | solution.py:146
  312.9 6.6 %block_grads.1 = bf16[64,128,128]{2,1,0:T(8,128)(2,1)} custom-call(s32[64]{0:T(128)} %ids.1, bf16[4,4,256,1024]{3,2,1,0:T(8,128)(2,1)} %bitcast.4, bf16[4,256,1024]{2,1,0:T(8,128)(2,1)} %bitcast.5), custom_call_target="tpu_custom_call" | custom-call | flops 2147483648 | bytes 12582912 | tf_op jit(solution)/shard_map/block_grads/pallas_call | solution.py:112
  319.5 47.6 %all-reduce.3.cloned.1.call-done = bf16[256,4096]{1,0:T(8,128)(2,1)} async-done(((bf16[256,4096]{1,0:T(8,128)(2,1)}), bf16[256,4096]{1,0:T(8,128)(2,1)}) %all-reduce.3.cloned.1.call-update) | async-done | bytes 2097168 | tf_op jit(solution)/shard_map/psum | solution.py:149
  367.1 3.1 copy.9
  (1 shorter events, 0.0 us)
Async XLA Ops:
  7.2 51.6 %all-gather.10.cloned.1.call-start = ((), (), s32[]{:S(2)}) async-start(), calls=%async_computation.2 | async-start | bytes 2621440 | tf_op jit(solution)/shard_map/all_gather | solution.py:145
  9.1 49.8 %copy-start.1 = (u32[32]{0:T(128)S(1)}, u32[32]{0:T(128)}, u32[]{:S(2)}) copy-start(u32[32]{0:T(128)} %constant.16) | copy-start | bytes 388
  9.1 51.0 %copy-start = (s32[64]{0:T(128)S(1)}, s32[64]{0:T(128)}, u32[]{:S(2)}) copy-start(s32[64]{0:T(128)} %ids.1) | copy-start | bytes 772
  9.1 199.6 %all-gather.8.cloned.1.call-start = ((), (), s32[]{:S(2)}) async-start(), calls=%async_computation | async-start | bytes 10485760 | tf_op jit(solution)/shard_map/all_gather | solution.py:142
  9.9 244.7 %all-gather.14.cloned.1.call-start = ((), (), s32[]{:S(2)}) async-start(), calls=%async_computation.4 | async-start | bytes 2621440 | tf_op jit(solution)/shard_map/all_gather | solution.py:147
  10.6 302.3 %all-gather.12.cloned.1.call-start = ((), (), s32[]{:S(2)}) async-start(), calls=%async_computation.3 | async-start | bytes 10485760 | tf_op jit(solution)/shard_map/all_gather | solution.py:146
  58.8 308.3 %all-reduce.3.cloned.1.call-start = ((), (), s32[]{:S(2)}) async-start(), calls=%async_computation.1 | async-start | bytes 4194304 | tf_op jit(solution)/shard_map/psum | solution.py:149
Sparse Core Ops, SparseCore 0:
  10.1 48.6 all-gather.9
  60.4 148.3 all-gather.7
  210.3 44.2 all-gather.13
  256.0 56.8 all-gather.11
  315.7 51.3 all-reduce.2

commit v2 on v1

--- a/solution.py
+++ b/solution.py
@@ -134,27 +134,242 @@
     return proj, lax.psum(back, INNER), grads
 
 
-def body(tokens, upstream, blocks, block_ids):
+def place_blocks(ids, first, blocks, weight):
+    slots, size = blocks.shape[0], blocks.shape[1]
+    depth, width = weight.shape
+    cols_n = width // size
+    total = (depth // size) * cols_n
+
+    @pl.loop(0, slots)
+    def place(s):
+        b = ids[first + s]
+
+        @pl.when(b < total)
+        def put():
+            r = pl.multiple_of((b // cols_n) * size, size)
+            c = pl.multiple_of((b % cols_n) * size, size)
+            weight[pl.ds(r, size), pl.ds(c, size)] = blocks[s]
+
+
+def middle_kernel(
+    place_of, ids_0, ids_1, ids_2, ids_3, own, near_a, near_b, far_a, far_b, end_a, end_b,
+    tokens, end_tokens, upstream, end_upstream,
+    proj, end_proj, back, end_back, weight,
+):
+    is_middle, half = place_of[0], place_of[1]
+    half_slots = near_a.shape[0]
+    mine, other = half * half_slots, (1 - half) * half_slots
+    depth, width = weight.shape
+    parts, rows, part_width = end_tokens.shape
+    step = 256
+
+    @pl.when(is_middle == 1)
+    def work():
+        weight[...] = jnp.zeros_like(weight)
+        place_blocks(ids_0, 0, own, weight)
+        place_blocks(ids_1, mine, near_a, weight)
+        place_blocks(ids_1, other, near_b, weight)
+        place_blocks(ids_2, mine, far_a, weight)
+        place_blocks(ids_2, other, far_b, weight)
+        place_blocks(ids_3, mine, end_a, weight)
+        place_blocks(ids_3, other, end_b, weight)
+
+        per_part = part_width // step
+
+        @pl.loop(0, depth // step)
+        def backward(n):
+            r = pl.multiple_of(n * step, step)
+            at = pl.multiple_of((n % per_part) * step, step)
+            rows_of_w = weight[pl.ds(r, step), :]
+            for source, target in ((end_upstream, end_back), (upstream, back)):
+                target[n // per_part, :, pl.ds(at, step)] = lax.dot_general(
+                    source[...],
+                    rows_of_w,
+                    (((1,), (1,)), ((), ())),
+                    preferred_element_type=jnp.float32,
+                ).astype(target.dtype)
+
+        @pl.loop(0, width // step)
+        def forward(n):
+            c = pl.multiple_of(n * step, step)
+            acc = jnp.zeros((rows, step), jnp.float32)
+            for q in range(parts):
+                acc += jnp.dot(
+                    end_tokens[q],
+                    weight[q * part_width : (q + 1) * part_width, pl.ds(c, step)],
+                    preferred_element_type=jnp.float32,
+                )
+            end_proj[:, pl.ds(c, step)] = acc.astype(end_proj.dtype)
+            proj[:, pl.ds(c, step)] = jnp.dot(
+                tokens[...], weight[:, pl.ds(c, step)], preferred_element_type=jnp.float32
+            ).astype(proj.dtype)
+
+
+def middle_project(place_of, ids, pieces, tokens, end_tokens, upstream, end_upstream):
+    rows, depth = tokens.shape
+    width = upstream.shape[1]
+    parts, _, part_width = end_tokens.shape
+    out_proj = jax.ShapeDtypeStruct((rows, width), jnp.bfloat16)
+    out_back = jax.ShapeDtypeStruct((parts, rows, part_width), jnp.bfloat16)
+    return pl.pallas_call(
+        middle_kernel,
+        out_shape=(out_proj, out_proj, out_back, out_back),
+        in_specs=[whole(pltpu.SMEM)] * 5 + [whole()] * 11,
+        out_specs=(whole(),) * 4,
+        scratch_shapes=[pltpu.VMEM((depth, width), jnp.bfloat16)],
+        compiler_params=pltpu.CompilerParams(vmem_limit_bytes=VMEM_LIMIT),
+        cost_estimate=pl.CostEstimate(
+            flops=8 * rows * depth * width,
+            bytes_accessed=depth * width * 2 + rows * (depth + width) * 8,
+            transcendentals=0,
+        ),
+        name="middle_project",
+    )(place_of, *ids, *pieces, tokens, end_tokens, upstream, end_upstream)
+
+
+def line_grads_kernel(
+    ids, tokens, tokens_1, tokens_2, tokens_3,
+    upstream, upstream_1, upstream_2m, upstream_2o, upstream_3m, upstream_3o,
+    grads, sum_2, sum_3,
+):
+    slots, size = grads.shape[0], grads.shape[1]
+    parts, _, part_width = tokens_1.shape
+    cols_n = upstream.shape[1] // size
+    per_part = part_width // size
+    total = parts * per_part * cols_n
+    sum_2[...] = upstream_2m[...] + upstream_2o[...]
+    sum_3[...] = upstream_3m[...] + upstream_3o[...]
+
+    @pl.loop(0, slots)
+    def one(s):
+        b = ids[s]
+
+        @pl.when(b < total)
+        def fill():
+            row = b // cols_n
+            part = row // per_part
+            r = pl.multiple_of((row % per_part) * size, size)
+            c = pl.multiple_of((b % cols_n) * size, size)
+            whole_r = pl.multiple_of(row * size, size)
+            pairs = (
+                (tokens[:, pl.ds(whole_r, size)], upstream),
+                (tokens_1[part, :, pl.ds(r, size)], upstream_1),
+                (tokens_2[part, :, pl.ds(r, size)], sum_2),
+                (tokens_3[part, :, pl.ds(r, size)], sum_3),
+            )
+            acc = jnp.zeros((size, size), jnp.float32)
+            for x, d in pairs:
+                acc += lax.dot_general(
+                    x,
+                    d[:, pl.ds(c, size)],
+                    (((0,), (0,)), ((), ())),
+                    preferred_element_type=jnp.float32,
+                )
+            grads[s] = acc.astype(grads.dtype)
+
+        @pl.when(b >= total)
+        def clear():
+            grads[s] = jnp.zeros((size, size), grads.dtype)
+
+
+def line_grads(ids, tokens, gathered, upstreams, size):
+    slots = ids.shape[0]
+    rows, width = upstreams[0].shape
+    return pl.pallas_call(
+        line_grads_kernel,
+        out_shape=jax.ShapeDtypeStruct((slots, size, size), jnp.bfloat16),
+        in_specs=[whole(pltpu.SMEM)] + [whole()] * 10,
+        out_specs=whole(),
+        scratch_shapes=[pltpu.VMEM((rows, width), jnp.bfloat16)] * 2,
+        compiler_params=pltpu.CompilerParams(vmem_limit_bytes=VMEM_LIMIT),
+        cost_estimate=pl.CostEstimate(
+            flops=8 * slots * rows * size * size,
+            bytes_accessed=2 * (4 * tokens.size + 6 * rows * width + slots * size * size),
+            transcendentals=0,
+        ),
+        name="line_grads",
+    )(ids, tokens, *gathered, *upstreams)
+
+
+INWARD = ((0, 1), (3, 2))
+OUTWARD = ((1, 0), (2, 3))
+PAIRS = INWARD + OUTWARD
+MIDDLE = ((1, 2), (2, 1))
+
+
+def after(first, then):
+    return lax.optimization_barrier((first, then))[1]
+
+
+def line_body(tokens, upstream, blocks, block_ids):
     size = blocks.shape[1]
+    half_slots = blocks.shape[0] // 2
     inner_n = lax.axis_size("tensor") * lax.axis_size("replica")
-    inner = lax.axis_index(INNER)
-    quarter_width = tokens.shape[1] // inner_n
-    all_blocks = lax.all_gather(blocks, "dp", axis=0, tiled=True)
-    all_ids = lax.all_gather(block_ids, "dp", axis=0, tiled=True)
-    quarter = lax.dynamic_slice_in_dim(tokens, inner * quarter_width, quarter_width, 1)
-    quarters = lax.all_gather(quarter, "dp")
-    all_tokens = lax.all_gather(quarters, INNER)
-    all_upstream = lax.all_gather(upstream, "dp")
-    proj, back = project(all_ids, all_blocks, tokens, upstream)
-    token_grad = lax.psum(back, INNER)
-    grads = block_grads(block_ids, all_tokens, all_upstream, size)
-    return proj, token_grad, grads
+    part_width = tokens.shape[1] // inner_n
+    at_z, half = lax.axis_index("dp"), lax.axis_index("groups")
+    middle = (at_z == 1) | (at_z == 2)
+    along = functools.partial(lax.ppermute, axis_name="dp")
+    across = functools.partial(lax.ppermute, axis_name="groups", perm=((0, 1), (1, 0)))
+
+    ids_1 = along(block_ids, perm=PAIRS)
+    ids_2 = along(block_ids, perm=MIDDLE)
+    ids_3 = along(ids_1, perm=MIDDLE)
+    mine = lax.dynamic_slice_in_dim(blocks, half * half_slots, half_slots, 0)
+    other = lax.dynamic_slice_in_dim(blocks, (1 - half) * half_slots, half_slots, 0)
+    part = lax.dynamic_slice_in_dim(
+        tokens, lax.axis_index(INNER) * part_width, part_width, 1
+    )
+    near_a = along(mine, perm=INWARD)
+    far_a = along(mine, perm=MIDDLE)
+    part_1 = along(after(near_a, part), perm=PAIRS)
+    end_a = along(after(far_a, near_a), perm=MIDDLE)
+    far_b = across(far_a)
+    near_b = along(after(part_1, other), perm=INWARD)
+    upstream_1 = along(after(near_b, upstream), perm=PAIRS)
+    part_2m = along(after(end_a, part), perm=MIDDLE)
+    end_b = across(end_a)
+    part_3m = along(after(part_2m, part_1), perm=MIDDLE)
+    part_2o = along(part_2m, perm=OUTWARD)
+    upstream_2m = along(after(part_3m, upstream), perm=MIDDLE)
+    part_3o = along(part_3m, perm=OUTWARD)
+    upstream_3m = along(after(upstream_2m, upstream_1), perm=MIDDLE)
+    upstream_2o = along(upstream_2m, perm=OUTWARD)
+    upstream_3o = along(upstream_3m, perm=OUTWARD)
+
+    tokens_1 = lax.all_gather(part_1, INNER)
+    tokens_2 = lax.all_gather(part_2m + part_2o, INNER)
+    tokens_3 = lax.all_gather(part_3m + part_3o, INNER)
+
+    place_of = jnp.stack([middle.astype(jnp.int32), half.astype(jnp.int32)])
+    proj, end_proj, back, end_back = middle_project(
+        place_of,
+        (block_ids, ids_1, ids_2, ids_3),
+        (blocks, near_a, near_b, far_a, far_b, end_a, end_b),
+        tokens,
+        tokens_1,
+        upstream,
+        upstream_1,
+    )
+    proj_out = along(end_proj, perm=OUTWARD)
+    end_sum = lax.psum_scatter(end_back, INNER, scatter_dimension=0)
+    own_sum = lax.psum_scatter(back, INNER, scatter_dimension=0)
+    sum_out = along(end_sum, perm=OUTWARD)
+    projected = jnp.where(middle, proj, proj_out)
+    token_grad = lax.all_gather(jnp.where(middle, own_sum, sum_out), INNER, axis=1, tiled=True)
+    grads = line_grads(
+        block_ids,
+        tokens,
+        (tokens_1, tokens_2, tokens_3),
+        (upstream, upstream_1, upstream_2m, upstream_2o, upstream_3m, upstream_3o),
+        size,
+    )
+    return projected, token_grad, grads
 
 
 def solution(mesh):
-    small = mesh.shape["dp"] <= 4
+    line = mesh.shape["dp"] == 4 and mesh.shape["groups"] == 2
     return jax.shard_map(
-        body if small else general_body,
+        line_body if line else general_body,
         mesh=mesh,
         in_specs=(
             P(("groups", "dp"), None),

time: 377 us -> 299 us (0.79)
  waiting for transfers between devices: 323 us -> 191 us
  starting transfers between devices: 0.19 us -> 47.4 us
  Pallas kernels: 25.8 us -> 33.9 us
  blocking collectives: 7.45 us -> 0 us
  other arithmetic: 0 us -> 5.32 us
    all_gather x4, waiting for transfers between devices: 274 us -> 0.01 us  [the longest x1 0.01 us: line_body(): tokens_2 = lax.all_gather(part_2m + part_2o, INNER)]
    ppermute x0 -> x21, waiting for transfers between devices: none -> 174 us  [the longest x1 38.7 us: line_body(): part_2o = along(part_2m, perm=OUTWARD)]
    psum x1 -> x0, waiting for transfers between devices: 47.6 us -> none  [body(): token_grad = lax.psum(back, INNER)]
    ppermute x0 -> x21, starting transfers between devices: none -> 47.2 us  [the longest x1 18.8 us: line_body(): near_b = along(after(part_1, other), perm=INWARD)]
    reduce_scatter x0 -> x2, waiting for transfers between devices: none -> 15.9 us  [the longest x1 15.9 us: line_body(): own_sum = lax.psum_scatter(back, INNER, scatter_dimension=0)]
    pallas_call x2, Pallas kernels: 25.8 us -> 33.9 us  [the longest x1 26.7 us: line_grads(): pl.pallas_call(line_grads_kernel, out_shape=jax.ShapeDtypeStruct((slots,...]
    unnamed x1 -> x0, blocking collectives: 7.45 us -> none
  transfers between devices with their start and end apart: 5 -> 27, of which waited for: 5 -> 11; matrix products, arithmetic and copies ran while one was open for 0% -> 2% of each run, Pallas kernels for 7% -> 9%
where the time goes in v2:
time: 299 us; the launch traced here: 300 us
  waiting for transfers between devices  191 us (64%)
  starting transfers between devices  47.4 us (16%)
  Pallas kernels  33.9 us (11%)
  between operations  14.5 us (5%)
  local copies, waits for them, and re-layouts  8.31 us (3%)
  other arithmetic  5.32 us (2%)
    ppermute x1, waiting for transfers between devices, line_body(): part_2o = along(part_2m, perm=OUTWARD)  38.7 us
    ppermute x1, waiting for transfers between devices, line_body(): proj_out = along(end_proj, perm=OUTWARD)  29.2 us
    pallas_call x1, Pallas kernels, line_grads(): pl.pallas_call(line_grads_kernel, out_shape=jax.ShapeDtypeStruct((slots,...  26.7 us
    ppermute x1, waiting for transfers between devices, line_body(): near_a = along(mine, perm=INWARD)  20.3 us
    ppermute x1, waiting for transfers between devices, line_body(): part_3o = along(part_3m, perm=OUTWARD)  18.9 us
    ppermute x1, starting transfers between devices, line_body(): near_b = along(after(part_1, other), perm=INWARD)  18.8 us
    ppermute x1, waiting for transfers between devices, line_body(): near_b = along(after(part_1, other), perm=INWARD)  18.3 us
    reduce_scatter x1, waiting for transfers between devices, line_body(): own_sum = lax.psum_scatter(back, INNER, scatter_dimension=0)  15.9 us
  transfers between devices with their start and end apart: 27, of which 11 were waited for; matrix products, arithmetic and copies ran while one was open for 2% of the time, Pallas kernels for 9%

profile of v2, /device:TPU:0, one launch (start us, length us, event | category | flops | bytes accessed | tf_op | source)
XLA Modules:
  0.0 300.2 jit_solution(4662089947937930104)
XLA Ops:
  7.2 0.0 all-gather.10.cloned.1.call-start
  7.2 0.0 copy-start.10
  7.2 1.7 constant_dynamic-slice_fusion
  8.9 5.9 %collective-permute-start.3 = (bf16[32,128,128]{2,1,0:T(8,128)(2,1)S(1)}, bf16[32,128,128]{2,1,0:T(8,128)(2,1)}, u32[]{:S(2)}, u32[]{:S(2)}) collective-permute-start(bf16[32,128,128]{2,1,0:T(8,128)(2,1)S(1)} %get-tuple-element.28), channel_id=1, source_target_pairs={{0,4},{12,8},{1,5},{13,9},{2,6},{14,10},{3,7},{15,11},{16,20},{28,... | collective-permute-start | bytes 3145736 | tf_op jit(solution)/shard_map/ppermute | solution.py:322
  14.8 1.1 constant_dynamic-slice_fusion.1
  15.9 20.3 %collective-permute-done.3.near_a = bf16[32,128,128]{2,1,0:T(8,128)(2,1)} collective-permute-done((bf16[32,128,128]{2,1,0:T(8,128)(2,1)S(1)}, bf16[32,128,128]{2,1,0:T(8,128)(2,1)}, u32[]{:S(2)}, u32[]{:S(2)}) %collective-permute-start.3) | collective-permute-done | bytes 1048608 | tf_op jit(solution)/shard_map/ppermute | solution.py:322
  36.3 2.6 collective-permute-start.4
  38.8 1.6 collective-permute-start.6
  40.5 9.4 %collective-permute-done.4 = bf16[256,1024]{1,0:T(8,128)(2,1)S(1)} collective-permute-done((bf16[256,1024]{1,0:T(8,128)(2,1)S(1)}, bf16[256,1024]{1,0:T(8,128)(2,1)S(1)}, u32[]{:S(2)}, u32[]{:S(2)}) %collective-permute-start.4) | collective-permute-done | bytes 524320 | tf_op jit(solution)/shard_map/ppermute | solution.py:324
  49.9 0.8 copy-done
  50.7 0.0 all-gather.10.cloned.1.call-update
  50.7 0.0 reduce-scatter.5.cloned.1.call-start
  50.8 0.0 collective-permute-done.6.far_a
  50.8 0.7 collective-permute-start.8
  51.5 18.8 %collective-permute-start.5 = (bf16[32,128,128]{2,1,0:T(8,128)(2,1)S(1)}, bf16[32,128,128]{2,1,0:T(8,128)(2,1)S(1)}, u32[]{:S(2)}, u32[]{:S(2)}) collective-permute-start(bf16[32,128,128]{2,1,0:T(8,128)(2,1)S(1)} %get-tuple-element.16), channel_id=1, source_target_pairs={{0,4},{12,8},{1,5},{13,9},{2,6},{14,10},{3,7},{15,11},{16,20},{28,... | collective-permute-start | bytes 3145736 | tf_op jit(solution)/shard_map/ppermute | solution.py:327
  70.3 1.6 collective-permute-start.7
  71.9 0.5 collective-permute-start.9
  72.4 18.3 %collective-permute-done.5.near_b = bf16[32,128,128]{2,1,0:T(8,128)(2,1)S(1)} collective-permute-done((bf16[32,128,128]{2,1,0:T(8,128)(2,1)S(1)}, bf16[32,128,128]{2,1,0:T(8,128)(2,1)S(1)}, u32[]{:S(2)}, u32[]{:S(2)}) %collective-permute-start.5) | collective-permute-done | bytes 1048608 | tf_op jit(solution)/shard_map/ppermute | solution.py:327
  90.8 2.5 collective-permute-start.10
  93.2 1.0 collective-permute-start
  94.2 0.6 collective-permute-start.1
  94.9 7.5 %collective-permute-done.ids_1 = s32[64]{0:T(128)S(1)} collective-permute-done((s32[64]{0:T(128)S(1)}, s32[64]{0:T(128)S(1)}, u32[]{:S(2)}, u32[]{:S(2)}) %collective-permute-start) | collective-permute-done | bytes 288 | tf_op jit(solution)/shard_map/ppermute | solution.py:314
  102.4 0.7 collective-permute-start.2
  103.0 0.6 pad_add_fusion.place_of
  103.7 0.0 collective-permute-done.7.far_b
  103.7 12.0 %collective-permute-done.9.end_b = bf16[32,128,128]{2,1,0:T(8,128)(2,1)} collective-permute-done((bf16[32,128,128]{2,1,0:T(8,128)(2,1)S(1)}, bf16[32,128,128]{2,1,0:T(8,128)(2,1)}, u32[]{:S(2)}, u32[]{:S(2)}) %collective-permute-start.9) | collective-permute-done | bytes 1048608 | tf_op jit(solution)/shard_map/ppermute | solution.py:330
  115.7 0.0 collective-permute-done.10.end_upstream.upstream_1
  115.8 0.8 copy-done.4
  116.5 7.2 %middle_project.1 = (bf16[256,1024]{1,0:T(8,128)(2,1)}, bf16[256,1024]{1,0:T(8,128)(2,1)}, bf16[4,256,1024]{2,1,0:T(8,128)(2,1)}, bf16[4,256,1024]{2,1,0:T(8,128)(2,1)}) custom-call(s32[2]{0:T(128)} %pad_add_fusion.place_of, s32[64]{0:T(128)} %ids.1, s32[64]{0:T(128)} %copy-done.14, s32[64]{0:T(128)} %copy-done.15, s32[64]{0:T(128)} %copy-done.16, ...), custom_call_target="tpu_custom_call" | custom-call | flops 8589934592 | bytes 18874368 | tf_op jit(solution)/shard_map/middle_project/pallas_call | solution.py:214
  123.8 0.0 reduce-scatter.5.cloned.1.call-update
  123.8 0.0 reduce-scatter.3.cloned.1.call-start
  123.8 0.0 copy-start.1
  123.8 0.7 reduce-scatter.3.cloned.1.call-update
  124.5 0.0 all-gather.12.cloned.1.call-start
  124.6 0.7 collective-permute-start.13
  125.3 1.3 collective-permute-start.14
  126.6 38.7 %collective-permute-done.14 = bf16[256,1024]{1,0:T(8,128)(2,1)S(1)} collective-permute-done((bf16[256,1024]{1,0:T(8,128)(2,1)S(1)}, bf16[256,1024]{1,0:T(8,128)(2,1)S(1)}, u32[]{:S(2)}, u32[]{:S(2)}) %collective-permute-start.14) | collective-permute-done | bytes 524320 | tf_op jit(solution)/shard_map/ppermute | solution.py:332
  165.3 1.0 add.26
  166.3 0.0 all-gather.12.cloned.1.call-update
  166.3 0.0 copy-start.3
  166.3 0.0 all-gather.14.cloned.1.call-start
  166.4 0.8 collective-permute-start.15
  167.2 1.3 collective-permute-start.16
  168.5 18.9 %collective-permute-done.16 = bf16[256,1024]{1,0:T(8,128)(2,1)S(1)} collective-permute-done((bf16[256,1024]{1,0:T(8,128)(2,1)S(1)}, bf16[256,1024]{1,0:T(8,128)(2,1)S(1)}, u32[]{:S(2)}, u32[]{:S(2)}) %collective-permute-start.16) | collective-permute-done | bytes 524320 | tf_op jit(solution)/shard_map/ppermute | solution.py:334
  187.4 1.0 add.27
  188.4 0.0 all-gather.14.cloned.1.call-update
  188.4 0.0 all-gather.8.cloned.1.call-start
  188.5 0.0 reduce-scatter.5.cloned.1.call-done
  188.5 1.3 collective-permute-start.12
  189.8 15.9 %reduce-scatter.3.cloned.1.call-done = bf16[1,256,1024]{2,1,0:T(8,128)(2,1)} async-done(((bf16[4,256,1024]{2,1,0:T(8,128)(2,1)}), bf16[1,256,1024]{2,1,0:T(8,128)(2,1)}) %reduce-scatter.3.cloned.1.call-update) | async-done | bytes 524304 | tf_op jit(solution)/shard_map/reduce_scatter | solution.py:355
  205.7 1.9 bitcast_select_fusion
  207.6 0.0 all-gather.8.cloned.1.call-update
  207.6 0.7 collective-permute-start.17
  208.4 0.7 collective-permute-start.19
  209.1 1.3 collective-permute-start.11
  210.4 1.3 collective-permute-start.18
  211.7 1.3 collective-permute-start.20
  213.0 29.2 %collective-permute-done.11 = bf16[256,1024]{1,0:T(8,128)(2,1)S(1)} collective-permute-done((bf16[256,1024]{1,0:T(8,128)(2,1)S(1)}, bf16[256,1024]{1,0:T(8,128)(2,1)S(1)}, u32[]{:S(2)}, u32[]{:S(2)}) %collective-permute-start.11) | collective-permute-done | bytes 524320 | tf_op jit(solution)/shard_map/ppermute | solution.py:353
  242.2 0.8 broadcast_select_fusion
  243.1 10.4 %collective-permute-done.18.upstream_2o = bf16[256,1024]{1,0:T(8,128)(2,1)S(1)} collective-permute-done((bf16[256,1024]{1,0:T(8,128)(2,1)S(1)}, bf16[256,1024]{1,0:T(8,128)(2,1)S(1)}, u32[]{:S(2)}, u32[]{:S(2)}) %collective-permute-start.18) | collective-permute-done | bytes 524320 | tf_op jit(solution)/shard_map/ppermute | solution.py:336
  253.4 9.3 %collective-permute-done.20.upstream_3o = bf16[256,1024]{1,0:T(8,128)(2,1)S(1)} collective-permute-done((bf16[256,1024]{1,0:T(8,128)(2,1)S(1)}, bf16[256,1024]{1,0:T(8,128)(2,1)S(1)}, u32[]{:S(2)}, u32[]{:S(2)}) %collective-permute-start.20) | collective-permute-done | bytes 524320 | tf_op jit(solution)/shard_map/ppermute | solution.py:337
  262.7 0.8 copy-done.9
  263.5 26.7 %line_grads.1 = bf16[64,128,128]{2,1,0:T(8,128)(2,1)} custom-call(s32[64]{0:T(128)} %ids.1, bf16[256,4096]{1,0:T(8,128)(2,1)} %tokens.3, bf16[4,256,1024]{2,1,0:T(8,128)(2,1)} %bitcast.9, bf16[4,256,1024]{2,1,0:T(8,128)(2,1)} %bitcast.10, bf16[4,256,1024]{2,1,0:T(8,128)(2,1)} %bitcast.11, bf16[256,1024]{1,0:T(8,128)(2,1)} %upstream.3, ...), custom_call_target="tpu_custom_call" | custom-call | flops 2147483648 | bytes 13631488 | tf_op jit(solution)/shard_map/line_grads/pallas_call | solution.py:278
  290.2 3.1 %copy.8 = bf16[256,4096]{1,0:T(8,128)(2,1)} copy(bf16[256,4096]{1,0:T(8,128)(2,1)} %all-gather.8.cloned.1.call-done) | data formatting | bytes 4194304
  (40 shorter events, 0.1 us)
Async XLA Ops:
  7.2 108.6 %all-gather.10.cloned.1.call-start = ((), (), s32[]{:S(2)}) async-start(), calls=%async_computation.5 | async-start | bytes 2621440 | tf_op jit(solution)/shard_map/all_gather | solution.py:339
  7.2 86.0 %copy-start.10 = (s32[64]{0:T(128)S(1)}, s32[64]{0:T(128)}, u32[]{:S(2)}) copy-start(s32[64]{0:T(128)} %ids.1) | copy-start | bytes 772
  8.9 27.3 %collective-permute-start.3 = (bf16[32,128,128]{2,1,0:T(8,128)(2,1)S(1)}, bf16[32,128,128]{2,1,0:T(8,128)(2,1)}, u32[]{:S(2)}, u32[]{:S(2)}) collective-permute-start(bf16[32,128,128]{2,1,0:T(8,128)(2,1)S(1)} %get-tuple-element.28), channel_id=1, source_target_pairs={{0,4},{12,8},{1,5},{13,9},{2,6},{14,10},{3,7},{15,11},{16,20},{28,... | collective-permute-start | bytes 3145736 | tf_op jit(solution)/shard_map/ppermute | solution.py:322
  36.3 13.6 %collective-permute-start.4 = (bf16[256,1024]{1,0:T(8,128)(2,1)S(1)}, bf16[256,1024]{1,0:T(8,128)(2,1)S(1)}, u32[]{:S(2)}, u32[]{:S(2)}) collective-permute-start(bf16[256,1024]{1,0:T(8,128)(2,1)S(1)} %constant_dynamic-slice_fusion.1), channel_id=1, source_target_pairs={{0,4},{12,8},{4,0},{8,12},{1,5},{13,9},{5,1},{9,13},{2,6},{14,10},... | collective-permute-start | bytes 1572872 | tf_op jit(solution)/shard_map/ppermute | solution.py:324
  38.8 11.9 %collective-permute-start.6 = (bf16[32,128,128]{2,1,0:T(8,128)(2,1)S(1)}, bf16[32,128,128]{2,1,0:T(8,128)(2,1)}, u32[]{:S(2)}, u32[]{:S(2)}) collective-permute-start(bf16[32,128,128]{2,1,0:T(8,128)(2,1)S(1)} %get-tuple-element.28), channel_id=1, source_target_pairs={{4,8},{8,4},{5,9},{9,5},{6,10},{10,6},{7,11},{11,7},{20,24},{24,20... | collective-permute-start | bytes 3145736 | tf_op jit(solution)/shard_map/ppermute | solution.py:323
  49.9 0.8 copy-start
  50.7 137.8 %reduce-scatter.5.cloned.1.call-start = ((), (), s32[]{:S(2)}) async-start(), calls=%async_computation.3 | async-start | bytes 2621440 | tf_op jit(solution)/shard_map/reduce_scatter | solution.py:354
  50.8 21.1 %collective-permute-start.8 = (bf16[32,128,128]{2,1,0:T(8,128)(2,1)}, bf16[32,128,128]{2,1,0:T(8,128)(2,1)S(1)}, u32[]{:S(2)}, u32[]{:S(2)}) collective-permute-start(bf16[32,128,128]{2,1,0:T(8,128)(2,1)} %collective-permute-done.3.near_a), channel_id=1, source_target_pairs={{4,8},{8,4},{5,9},{9,5},{6,10},{10,6},{7,11},{11,7},{20,24},{24,20... | collective-permute-start | bytes 3145736 | tf_op jit(solution)/shard_map/ppermute | solution.py:325
  51.5 39.3 %collective-permute-start.5 = (bf16[32,128,128]{2,1,0:T(8,128)(2,1)S(1)}, bf16[32,128,128]{2,1,0:T(8,128)(2,1)S(1)}, u32[]{:S(2)}, u32[]{:S(2)}) collective-permute-start(bf16[32,128,128]{2,1,0:T(8,128)(2,1)S(1)} %get-tuple-element.16), channel_id=1, source_target_pairs={{0,4},{12,8},{1,5},{13,9},{2,6},{14,10},{3,7},{15,11},{16,20},{28,... | collective-permute-start | bytes 3145736 | tf_op jit(solution)/shard_map/ppermute | solution.py:327
  70.3 33.3 %collective-permute-start.7 = (bf16[32,128,128]{2,1,0:T(8,128)(2,1)}, bf16[32,128,128]{2,1,0:T(8,128)(2,1)}, u32[]{:S(2)}, u32[]{:S(2)}) collective-permute-start(bf16[32,128,128]{2,1,0:T(8,128)(2,1)} %collective-permute-done.6.far_a), channel_id=1, source_target_pairs={{0,16},{16,0},{1,17},{17,1},{2,18},{18,2},{3,19},{19,3},{4,20},{20... | collective-permute-start | bytes 3145736 | tf_op jit(solution)/shard_map/ppermute | solution.py:326
  71.9 43.8 %copy-start.11 = (bf16[32,128,128]{2,1,0:T(8,128)(2,1)}, bf16[32,128,128]{2,1,0:T(8,128)(2,1)S(1)}, u32[]{:S(2)}) copy-start(bf16[32,128,128]{2,1,0:T(8,128)(2,1)S(1)} %collective-permute-done.8.end_a) | copy-start | bytes 3145732
  71.9 43.8 %collective-permute-start.9 = (bf16[32,128,128]{2,1,0:T(8,128)(2,1)S(1)}, bf16[32,128,128]{2,1,0:T(8,128)(2,1)}, u32[]{:S(2)}, u32[]{:S(2)}) collective-permute-start(bf16[32,128,128]{2,1,0:T(8,128)(2,1)S(1)} %collective-permute-done.8.end_a), channel_id=1, source_target_pairs={{0,16},{16,0},{1,17},{17,1},{2,18},{18,2},{3,19},{19,3},{4,20},{20... | collective-permute-start | bytes 3145736 | tf_op jit(solution)/shard_map/ppermute | solution.py:330
  90.8 2.5 copy-start.12
  90.8 25.0 %collective-permute-start.10 = (bf16[256,1024]{1,0:T(8,128)(2,1)}, bf16[256,1024]{1,0:T(8,128)(2,1)S(1)}, u32[]{:S(2)}, u32[]{:S(2)}) collective-permute-start(bf16[256,1024]{1,0:T(8,128)(2,1)} %upstream.3), channel_id=1, source_target_pairs={{0,4},{12,8},{4,0},{8,12},{1,5},{13,9},{5,1},{9,13},{2,6},{14,10},... | collective-permute-start | bytes 1572872 | tf_op jit(solution)/shard_map/ppermute | solution.py:328
  93.2 9.1 %collective-permute-start = (s32[64]{0:T(128)S(1)}, s32[64]{0:T(128)S(1)}, u32[]{:S(2)}, u32[]{:S(2)}) collective-permute-start(s32[64]{0:T(128)S(1)} %copy-done.10), channel_id=1, source_target_pairs={{0,4},{12,8},{4,0},{8,12},{1,5},{13,9},{5,1},{9,13},{2,6},{14,10},... | collective-permute-start | bytes 776 | tf_op jit(solution)/shard_map/ppermute | solution.py:314
  94.2 9.4 %collective-permute-start.1 = (s32[64]{0:T(128)S(1)}, s32[64]{0:T(128)S(1)}, u32[]{:S(2)}, u32[]{:S(2)}) collective-permute-start(s32[64]{0:T(128)S(1)} %copy-done.10), channel_id=1, source_target_pairs={{4,8},{8,4},{5,9},{9,5},{6,10},{10,6},{7,11},{11,7},{20,24},{24,20... | collective-permute-start | bytes 776 | tf_op jit(solution)/shard_map/ppermute | solution.py:315
  102.4 13.4 %copy-start.14 = (s32[64]{0:T(128)}, s32[64]{0:T(128)S(1)}, u32[]{:S(2)}) copy-start(s32[64]{0:T(128)S(1)} %collective-permute-done.ids_1) | copy-start | bytes 772
  102.4 1.3 collective-permute-start.2
  103.6 12.1 %copy-start.15 = (s32[64]{0:T(128)}, s32[64]{0:T(128)S(1)}, u32[]{:S(2)}) copy-start(s32[64]{0:T(128)S(1)} %collective-permute-done.1.ids_2) | copy-start | bytes 772
  103.6 12.1 %copy-start.16 = (s32[64]{0:T(128)}, s32[64]{0:T(128)S(1)}, u32[]{:S(2)}) copy-start(s32[64]{0:T(128)S(1)} %collective-permute-done.2.ids_3) | copy-start | bytes 772
  115.7 0.8 copy-start.4
  123.8 81.9 %reduce-scatter.3.cloned.1.call-start = ((), (), s32[]{:S(2)}) async-start(), calls=%async_computation.2 | async-start | bytes 2621440 | tf_op jit(solution)/shard_map/reduce_scatter | solution.py:355
  123.8 42.5 %copy-start.1 = (bf16[256,1024]{1,0:T(8,128)(2,1)S(1)}, bf16[256,1024]{1,0:T(8,128)(2,1)}, u32[]{:S(2)}) copy-start(bf16[256,1024]{1,0:T(8,128)(2,1)} %copy-done) | copy-start | bytes 1572868
  124.5 138.2 %all-gather.12.cloned.1.call-start = ((), (), s32[]{:S(2)}) async-start(), calls=%async_computation.6 | async-start | bytes 2621440 | tf_op jit(solution)/shard_map/all_gather | solution.py:340
  124.6 0.7 collective-permute-start.13
  125.3 40.0 %collective-permute-start.14 = (bf16[256,1024]{1,0:T(8,128)(2,1)S(1)}, bf16[256,1024]{1,0:T(8,128)(2,1)S(1)}, u32[]{:S(2)}, u32[]{:S(2)}) collective-permute-start(bf16[256,1024]{1,0:T(8,128)(2,1)S(1)} %collective-permute-done.13), channel_id=1, source_target_pairs={{4,0},{8,12},{5,1},{9,13},{6,2},{10,14},{7,3},{11,15},{20,16},{24,... | collective-permute-start | bytes 1572872 | tf_op jit(solution)/shard_map/ppermute | solution.py:332
  166.3 41.3 %copy-start.3 = (bf16[256,1024]{1,0:T(8,128)(2,1)S(1)}, bf16[256,1024]{1,0:T(8,128)(2,1)}, u32[]{:S(2)}) copy-start(bf16[256,1024]{1,0:T(8,128)(2,1)} %upstream.3) | copy-start | bytes 1572868
  166.3 42.0 %copy-start.5 = (bf16[256,1024]{1,0:T(8,128)(2,1)S(1)}, bf16[256,1024]{1,0:T(8,128)(2,1)}, u32[]{:S(2)}) copy-start(bf16[256,1024]{1,0:T(8,128)(2,1)} %copy-done.4) | copy-start | bytes 1572868
  166.3 42.8 %copy-start.13 = (bf16[256,1024]{1,0:T(8,128)(2,1)S(1)}, bf16[256,1024]{1,0:T(8,128)(2,1)}, u32[]{:S(2)}) copy-start(bf16[256,1024]{1,0:T(8,128)(2,1)} %get-tuple-element.20) | copy-start | bytes 1572868
  166.3 75.9 %copy-start.2 = (bf16[256,1024]{1,0:T(8,128)(2,1)S(1)}, bf16[256,1024]{1,0:T(8,128)(2,1)}, u32[]{:S(2)}) copy-start(bf16[256,1024]{1,0:T(8,128)(2,1)} %get-tuple-element.19) | copy-start | bytes 1572868
  166.3 96.4 %all-gather.14.cloned.1.call-start = ((), (), s32[]{:S(2)}) async-start(), calls=%async_computation.7 | async-start | bytes 2621440 | tf_op jit(solution)/shard_map/all_gather | solution.py:341
  166.4 0.8 collective-permute-start.15
  167.2 20.2 %collective-permute-start.16 = (bf16[256,1024]{1,0:T(8,128)(2,1)S(1)}, bf16[256,1024]{1,0:T(8,128)(2,1)S(1)}, u32[]{:S(2)}, u32[]{:S(2)}) collective-permute-start(bf16[256,1024]{1,0:T(8,128)(2,1)S(1)} %collective-permute-done.15), channel_id=1, source_target_pairs={{4,0},{8,12},{5,1},{9,13},{6,2},{10,14},{7,3},{11,15},{20,16},{24,... | collective-permute-start | bytes 1572872 | tf_op jit(solution)/shard_map/ppermute | solution.py:334
  188.4 101.8 %all-gather.8.cloned.1.call-start = ((), (), s32[]{:S(2)}) async-start(), calls=%async_computation.4 | async-start | bytes 2621440 | tf_op jit(solution)/shard_map/all_gather | solution.py:358
  188.5 17.2 %collective-permute-start.12 = (bf16[256,1024]{1,0:T(8,128)(2,1)}, bf16[256,1024]{1,0:T(8,128)(2,1)S(1)}, u32[]{:S(2)}, u32[]{:S(2)}) collective-permute-start(bf16[256,1024]{1,0:T(8,128)(2,1)} %bitcast.12), channel_id=1, source_target_pairs={{4,0},{8,12},{5,1},{9,13},{6,2},{10,14},{7,3},{11,15},{20,16},{24,... | collective-permute-start | bytes 1572872 | tf_op jit(solution)/shard_map/ppermute | solution.py:356
  207.6 0.7 collective-permute-start.17
  208.3 54.4 %copy-start.6 = (bf16[256,1024]{1,0:T(8,128)(2,1)}, bf16[256,1024]{1,0:T(8,128)(2,1)S(1)}, u32[]{:S(2)}) copy-start(bf16[256,1024]{1,0:T(8,128)(2,1)S(1)} %collective-permute-done.17.upstream_2m) | copy-start | bytes 1572868
  208.4 3.3 %collective-permute-start.19 = (bf16[256,1024]{1,0:T(8,128)(2,1)S(1)}, bf16[256,1024]{1,0:T(8,128)(2,1)S(1)}, u32[]{:S(2)}, u32[]{:S(2)}) collective-permute-start(bf16[256,1024]{1,0:T(8,128)(2,1)S(1)} %copy-done.5), channel_id=1, source_target_pairs={{4,8},{8,4},{5,9},{9,5},{6,10},{10,6},{7,11},{11,7},{20,24},{24,20... | collective-permute-start | bytes 1572872 | tf_op jit(solution)/shard_map/ppermute | solution.py:335
  209.1 33.1 %collective-permute-start.11 = (bf16[256,1024]{1,0:T(8,128)(2,1)S(1)}, bf16[256,1024]{1,0:T(8,128)(2,1)S(1)}, u32[]{:S(2)}, u32[]{:S(2)}) collective-permute-start(bf16[256,1024]{1,0:T(8,128)(2,1)S(1)} %copy-done.13), channel_id=1, source_target_pairs={{4,0},{8,12},{5,1},{9,13},{6,2},{10,14},{7,3},{11,15},{20,16},{24,... | collective-permute-start | bytes 1572872 | tf_op jit(solution)/shard_map/ppermute | solution.py:353
  210.4 43.1 %collective-permute-start.18 = (bf16[256,1024]{1,0:T(8,128)(2,1)S(1)}, bf16[256,1024]{1,0:T(8,128)(2,1)S(1)}, u32[]{:S(2)}, u32[]{:S(2)}) collective-permute-start(bf16[256,1024]{1,0:T(8,128)(2,1)S(1)} %collective-permute-done.17.upstream_2m), channel_id=1, source_target_pairs={{4,0},{8,12},{5,1},{9,13},{6,2},{10,14},{7,3},{11,15},{20,16},{24,... | collective-permute-start | bytes 1572872 | tf_op jit(solution)/shard_map/ppermute | solution.py:336
  211.7 51.0 %copy-start.7 = (bf16[256,1024]{1,0:T(8,128)(2,1)}, bf16[256,1024]{1,0:T(8,128)(2,1)S(1)}, u32[]{:S(2)}) copy-start(bf16[256,1024]{1,0:T(8,128)(2,1)S(1)} %collective-permute-done.19.upstream_3m) | copy-start | bytes 1572868
  211.7 51.0 %collective-permute-start.20 = (bf16[256,1024]{1,0:T(8,128)(2,1)S(1)}, bf16[256,1024]{1,0:T(8,128)(2,1)S(1)}, u32[]{:S(2)}, u32[]{:S(2)}) collective-permute-start(bf16[256,1024]{1,0:T(8,128)(2,1)S(1)} %collective-permute-done.19.upstream_3m), channel_id=1, source_target_pairs={{4,0},{8,12},{5,1},{9,13},{6,2},{10,14},{7,3},{11,15},{20,16},{24,... | collective-permute-start | bytes 1572872 | tf_op jit(solution)/shard_map/ppermute | solution.py:337
  253.4 9.3 %copy-start.8 = (bf16[256,1024]{1,0:T(8,128)(2,1)}, bf16[256,1024]{1,0:T(8,128)(2,1)S(1)}, u32[]{:S(2)}) copy-start(bf16[256,1024]{1,0:T(8,128)(2,1)S(1)} %collective-permute-done.18.upstream_2o) | copy-start | bytes 1572868
  262.7 0.8 copy-start.9
Sparse Core Ops, SparseCore 0:
  50.8 22.9 all-gather.9
  123.9 47.0 reduce-scatter.4
  174.2 31.4 reduce-scatter.2
  207.1 22.5 all-gather.11
  231.1 22.5 all-gather.13
  255.8 22.5 all-gather.7

commit v3 on v2

--- a/solution.py
+++ b/solution.py
@@ -151,17 +151,13 @@
             weight[pl.ds(r, size), pl.ds(c, size)] = blocks[s]
 
 
-def middle_kernel(
+def weight_kernel(
     place_of, ids_0, ids_1, ids_2, ids_3, own, near_a, near_b, far_a, far_b, end_a, end_b,
-    tokens, end_tokens, upstream, end_upstream,
-    proj, end_proj, back, end_back, weight,
+    end_upstream, weight, end_back,
 ):
     is_middle, half = place_of[0], place_of[1]
     half_slots = near_a.shape[0]
     mine, other = half * half_slots, (1 - half) * half_slots
-    depth, width = weight.shape
-    parts, rows, part_width = end_tokens.shape
-    step = 256
 
     @pl.when(is_middle == 1)
     def work():
@@ -173,22 +169,77 @@
         place_blocks(ids_2, other, far_b, weight)
         place_blocks(ids_3, mine, end_a, weight)
         place_blocks(ids_3, other, end_b, weight)
-
-        per_part = part_width // step
-
-        @pl.loop(0, depth // step)
-        def backward(n):
-            r = pl.multiple_of(n * step, step)
-            at = pl.multiple_of((n % per_part) * step, step)
-            rows_of_w = weight[pl.ds(r, step), :]
-            for source, target in ((end_upstream, end_back), (upstream, back)):
-                target[n // per_part, :, pl.ds(at, step)] = lax.dot_general(
-                    source[...],
-                    rows_of_w,
-                    (((1,), (1,)), ((), ())),
-                    preferred_element_type=jnp.float32,
-                ).astype(target.dtype)
-
+        backward_rows(end_upstream, weight, end_back)
+
+
+def backward_rows(upstream, weight, back):
+    depth = weight.shape[0]
+    step = 256
+    per_part = back.shape[2] // step
+
+    @pl.loop(0, depth // step)
+    def backward(n):
+        r = pl.multiple_of(n * step, step)
+        at = pl.multiple_of((n % per_part) * step, step)
+        back[n // per_part, :, pl.ds(at, step)] = lax.dot_general(
+            upstream[...],
+            weight[pl.ds(r, step), :],
+            (((1,), (1,)), ((), ())),
+            preferred_element_type=jnp.float32,
+        ).astype(back.dtype)
+
+
+def build_weight(place_of, ids, pieces, end_upstream, depth, parts):
+    rows, width = end_upstream.shape
+    return pl.pallas_call(
+        weight_kernel,
+        out_shape=(
+            jax.ShapeDtypeStruct((depth, width), jnp.bfloat16),
+            jax.ShapeDtypeStruct((parts, rows, depth // parts), jnp.bfloat16),
+        ),
+        in_specs=[whole(pltpu.SMEM)] * 5 + [whole()] * 8,
+        out_specs=(whole(),) * 2,
+        compiler_params=pltpu.CompilerParams(vmem_limit_bytes=VMEM_LIMIT),
+        cost_estimate=pl.CostEstimate(
+            flops=2 * rows * depth * width,
+            bytes_accessed=depth * width * 4 + rows * (depth + width) * 2,
+            transcendentals=0,
+        ),
+        name="build_weight",
+    )(place_of, *ids, *pieces, end_upstream)
+
+
+def backward_kernel(place_of, weight, upstream, back):
+    @pl.when(place_of[0] == 1)
+    def work():
+        backward_rows(upstream, weight, back)
+
+
+def project_back(place_of, weight, upstream, parts):
+    depth, width = weight.shape
+    rows = upstream.shape[0]
+    return pl.pallas_call(
+        backward_kernel,
+        out_shape=jax.ShapeDtypeStruct((parts, rows, depth // parts), jnp.bfloat16),
+        in_specs=[whole(pltpu.SMEM)] + [whole()] * 2,
+        out_specs=whole(),
+        compiler_params=pltpu.CompilerParams(vmem_limit_bytes=VMEM_LIMIT),
+        cost_estimate=pl.CostEstimate(
+            flops=2 * rows * depth * width,
+            bytes_accessed=depth * width * 2 + rows * (depth + width) * 2,
+            transcendentals=0,
+        ),
+        name="project_back",
+    )(place_of, weight, upstream)
+
+
+def forward_kernel(place_of, weight, tokens, end_tokens, proj, end_proj):
+    width = weight.shape[1]
+    parts, rows, part_width = end_tokens.shape
+    step = 256
+
+    @pl.when(place_of[0] == 1)
+    def work():
         @pl.loop(0, width // step)
         def forward(n):
             c = pl.multiple_of(n * step, step)
@@ -205,40 +256,35 @@
             ).astype(proj.dtype)
 
 
-def middle_project(place_of, ids, pieces, tokens, end_tokens, upstream, end_upstream):
-    rows, depth = tokens.shape
-    width = upstream.shape[1]
-    parts, _, part_width = end_tokens.shape
-    out_proj = jax.ShapeDtypeStruct((rows, width), jnp.bfloat16)
-    out_back = jax.ShapeDtypeStruct((parts, rows, part_width), jnp.bfloat16)
-    return pl.pallas_call(
-        middle_kernel,
-        out_shape=(out_proj, out_proj, out_back, out_back),
-        in_specs=[whole(pltpu.SMEM)] * 5 + [whole()] * 11,
-        out_specs=(whole(),) * 4,
-        scratch_shapes=[pltpu.VMEM((depth, width), jnp.bfloat16)],
-        compiler_params=pltpu.CompilerParams(vmem_limit_bytes=VMEM_LIMIT),
-        cost_estimate=pl.CostEstimate(
-            flops=8 * rows * depth * width,
-            bytes_accessed=depth * width * 2 + rows * (depth + width) * 8,
-            transcendentals=0,
-        ),
-        name="middle_project",
-    )(place_of, *ids, *pieces, tokens, end_tokens, upstream, end_upstream)
-
-
-def line_grads_kernel(
-    ids, tokens, tokens_1, tokens_2, tokens_3,
-    upstream, upstream_1, upstream_2m, upstream_2o, upstream_3m, upstream_3o,
-    grads, sum_2, sum_3,
-):
+def project_forward(place_of, weight, tokens, end_tokens):
+    depth, width = weight.shape
+    rows = tokens.shape[0]
+    out = jax.ShapeDtypeStruct((rows, width), jnp.bfloat16)
+    return pl.pallas_call(
+        forward_kernel,
+        out_shape=(out, out),
+        in_specs=[whole(pltpu.SMEM)] + [whole()] * 3,
+        out_specs=(whole(),) * 2,
+        compiler_params=pltpu.CompilerParams(vmem_limit_bytes=VMEM_LIMIT),
+        cost_estimate=pl.CostEstimate(
+            flops=4 * rows * depth * width,
+            bytes_accessed=depth * width * 2 + rows * (depth + width) * 4,
+            transcendentals=0,
+        ),
+        name="project_forward",
+    )(place_of, weight, tokens, end_tokens)
+
+
+def line_grads_kernel(pairs_n, has_start, parted, ids, *refs):
+    refs = list(refs)
+    start = refs.pop(0) if has_start else None
+    pairs = [(refs[2 * k], refs[2 * k + 1]) for k in range(pairs_n)]
+    grads = refs[2 * pairs_n]
     slots, size = grads.shape[0], grads.shape[1]
-    parts, _, part_width = tokens_1.shape
-    cols_n = upstream.shape[1] // size
+    parts, _, part_width = pairs[-1][0].shape
+    cols_n = pairs[0][1].shape[1] // size
     per_part = part_width // size
     total = parts * per_part * cols_n
-    sum_2[...] = upstream_2m[...] + upstream_2o[...]
-    sum_3[...] = upstream_3m[...] + upstream_3o[...]
 
     @pl.loop(0, slots)
     def one(s):
@@ -251,16 +297,10 @@
             r = pl.multiple_of((row % per_part) * size, size)
             c = pl.multiple_of((b % cols_n) * size, size)
             whole_r = pl.multiple_of(row * size, size)
-            pairs = (
-                (tokens[:, pl.ds(whole_r, size)], upstream),
-                (tokens_1[part, :, pl.ds(r, size)], upstream_1),
-                (tokens_2[part, :, pl.ds(r, size)], sum_2),
-                (tokens_3[part, :, pl.ds(r, size)], sum_3),
-            )
-            acc = jnp.zeros((size, size), jnp.float32)
-            for x, d in pairs:
+            acc = start[s] if has_start else jnp.zeros((size, size), jnp.float32)
+            for (x, d), cut in zip(pairs, parted):
                 acc += lax.dot_general(
-                    x,
+                    x[part, :, pl.ds(r, size)] if cut else x[:, pl.ds(whole_r, size)],
                     d[:, pl.ds(c, size)],
                     (((0,), (0,)), ((), ())),
                     preferred_element_type=jnp.float32,
@@ -272,102 +312,156 @@
             grads[s] = jnp.zeros((size, size), grads.dtype)
 
 
-def line_grads(ids, tokens, gathered, upstreams, size):
+def line_grads(ids, start, pairs, size, out_dtype):
     slots = ids.shape[0]
-    rows, width = upstreams[0].shape
-    return pl.pallas_call(
-        line_grads_kernel,
-        out_shape=jax.ShapeDtypeStruct((slots, size, size), jnp.bfloat16),
-        in_specs=[whole(pltpu.SMEM)] + [whole()] * 10,
+    rows = pairs[0][1].shape[0]
+    flat = [a for pair in pairs for a in pair]
+    starts = [] if start is None else [start]
+    return pl.pallas_call(
+        functools.partial(
+            line_grads_kernel,
+            len(pairs),
+            start is not None,
+            tuple(x.ndim == 3 for x, _ in pairs),
+        ),
+        out_shape=jax.ShapeDtypeStruct((slots, size, size), out_dtype),
+        in_specs=[whole(pltpu.SMEM)] + [whole()] * (len(starts) + len(flat)),
         out_specs=whole(),
-        scratch_shapes=[pltpu.VMEM((rows, width), jnp.bfloat16)] * 2,
-        compiler_params=pltpu.CompilerParams(vmem_limit_bytes=VMEM_LIMIT),
-        cost_estimate=pl.CostEstimate(
-            flops=8 * slots * rows * size * size,
-            bytes_accessed=2 * (4 * tokens.size + 6 * rows * width + slots * size * size),
+        compiler_params=pltpu.CompilerParams(vmem_limit_bytes=VMEM_LIMIT),
+        cost_estimate=pl.CostEstimate(
+            flops=4 * len(pairs) * slots * rows * size * size,
+            bytes_accessed=sum(2 * a.size for a in flat) + 4 * slots * size * size,
             transcendentals=0,
         ),
         name="line_grads",
-    )(ids, tokens, *gathered, *upstreams)
+    )(ids, *starts, *flat)
 
 
 INWARD = ((0, 1), (3, 2))
 OUTWARD = ((1, 0), (2, 3))
 PAIRS = INWARD + OUTWARD
 MIDDLE = ((1, 2), (2, 1))
-
-
-def after(first, then):
-    return lax.optimization_barrier((first, then))[1]
+SWAP = ((0, 1), (1, 0))
+
+
+def plus(a, b):
+    return (a.astype(jnp.float32) + b.astype(jnp.float32)).astype(a.dtype)
+
+
+def scatter_sum(parts, at_tensor, at_replica):
+    by_core = parts.reshape((2, 2) + parts.shape[1:])
+    keep = lax.dynamic_index_in_dim(by_core, at_replica, 1, keepdims=False)
+    give = lax.dynamic_index_in_dim(by_core, 1 - at_replica, 1, keepdims=False)
+    chip = plus(keep, lax.ppermute(give, "replica", SWAP))
+    keep = lax.dynamic_index_in_dim(chip, at_tensor, 0, keepdims=False)
+    give = lax.dynamic_index_in_dim(chip, 1 - at_tensor, 0, keepdims=False)
+    return plus(keep, lax.ppermute(give, "tensor", SWAP))
+
+
+def gather_parts(part, at_tensor, at_replica):
+    other = lax.ppermute(part, "tensor", SWAP)
+    pair = jnp.where(
+        at_tensor == 0, jnp.stack([part, other]), jnp.stack([other, part])
+    )
+    core = lax.ppermute(pair, "replica", SWAP)
+    parts = jnp.where(
+        at_replica == 0, jnp.stack([pair, core], 1), jnp.stack([core, pair], 1)
+    )
+    rows, width = part.shape
+    return parts.reshape(4, rows, width).transpose(1, 0, 2).reshape(rows, 4 * width)
 
 
 def line_body(tokens, upstream, blocks, block_ids):
     size = blocks.shape[1]
+    depth = tokens.shape[1]
     half_slots = blocks.shape[0] // 2
-    inner_n = lax.axis_size("tensor") * lax.axis_size("replica")
-    part_width = tokens.shape[1] // inner_n
+    parts = 4
+    part_width = depth // parts
     at_z, half = lax.axis_index("dp"), lax.axis_index("groups")
+    at_tensor, at_replica = lax.axis_index("tensor"), lax.axis_index("replica")
     middle = (at_z == 1) | (at_z == 2)
+    place_of = jnp.stack([middle.astype(jnp.int32), half.astype(jnp.int32)])
     along = functools.partial(lax.ppermute, axis_name="dp")
-    across = functools.partial(lax.ppermute, axis_name="groups", perm=((0, 1), (1, 0)))
-
+    across = functools.partial(lax.ppermute, axis_name="groups", perm=SWAP)
+    stage = lax.optimization_barrier
+
+    mine = lax.dynamic_slice_in_dim(blocks, half * half_slots, half_slots, 0)
+    other = lax.dynamic_slice_in_dim(blocks, (1 - half) * half_slots, half_slots, 0)
+    part = lax.dynamic_slice_in_dim(tokens, lax.axis_index(INNER) * part_width, part_width, 1)
+    mine, other, part = stage((mine, other, part))
+
+    near_a = along(mine, perm=INWARD)
+    far_a = along(mine, perm=MIDDLE)
+    part_1o = along(part, perm=OUTWARD)
+    upstream_1o = along(upstream, perm=OUTWARD)
     ids_1 = along(block_ids, perm=PAIRS)
     ids_2 = along(block_ids, perm=MIDDLE)
+    near_a, far_a, part_1o, upstream_1o, ids_1, ids_2, part, upstream_s, other = stage(
+        (near_a, far_a, part_1o, upstream_1o, ids_1, ids_2, part, upstream, other)
+    )
+
+    part_1i = along(part, perm=INWARD)
+    upstream_1i = along(upstream_s, perm=INWARD)
+    end_a = along(near_a, perm=MIDDLE)
+    far_b = across(far_a)
     ids_3 = along(ids_1, perm=MIDDLE)
-    mine = lax.dynamic_slice_in_dim(blocks, half * half_slots, half_slots, 0)
-    other = lax.dynamic_slice_in_dim(blocks, (1 - half) * half_slots, half_slots, 0)
-    part = lax.dynamic_slice_in_dim(
-        tokens, lax.axis_index(INNER) * part_width, part_width, 1
-    )
-    near_a = along(mine, perm=INWARD)
-    far_a = along(mine, perm=MIDDLE)
-    part_1 = along(after(near_a, part), perm=PAIRS)
-    end_a = along(after(far_a, near_a), perm=MIDDLE)
-    far_b = across(far_a)
-    near_b = along(after(part_1, other), perm=INWARD)
-    upstream_1 = along(after(near_b, upstream), perm=PAIRS)
-    part_2m = along(after(end_a, part), perm=MIDDLE)
+    part_1i, upstream_1i, end_a, far_b, ids_3, part, upstream_s, other = stage(
+        (part_1i, upstream_1i, end_a, far_b, ids_3, part, upstream_s, other)
+    )
+    tokens_1 = lax.all_gather(part_1i + part_1o, INNER)
+    upstream_1 = upstream_1i + upstream_1o
+
+    near_b = along(other, perm=INWARD)
+    part_2m = along(part, perm=MIDDLE)
+    part_3m = along(part_1i, perm=MIDDLE)
     end_b = across(end_a)
-    part_3m = along(after(part_2m, part_1), perm=MIDDLE)
-    part_2o = along(part_2m, perm=OUTWARD)
-    upstream_2m = along(after(part_3m, upstream), perm=MIDDLE)
-    part_3o = along(part_3m, perm=OUTWARD)
-    upstream_3m = along(after(upstream_2m, upstream_1), perm=MIDDLE)
-    upstream_2o = along(upstream_2m, perm=OUTWARD)
-    upstream_3o = along(upstream_3m, perm=OUTWARD)
-
-    tokens_1 = lax.all_gather(part_1, INNER)
-    tokens_2 = lax.all_gather(part_2m + part_2o, INNER)
-    tokens_3 = lax.all_gather(part_3m + part_3o, INNER)
-
-    place_of = jnp.stack([middle.astype(jnp.int32), half.astype(jnp.int32)])
-    proj, end_proj, back, end_back = middle_project(
+    near_b, part_2m, part_3m, end_b, upstream_s, upstream_1i = stage(
+        (near_b, part_2m, part_3m, end_b, upstream_s, upstream_1i)
+    )
+
+    weight, end_back = build_weight(
         place_of,
         (block_ids, ids_1, ids_2, ids_3),
         (blocks, near_a, near_b, far_a, far_b, end_a, end_b),
-        tokens,
-        tokens_1,
-        upstream,
-        upstream_1,
-    )
+        upstream_1i,
+        depth,
+        parts,
+    )
+    part_2o = along(part_2m, perm=OUTWARD)
+    part_3o = along(part_3m, perm=OUTWARD)
+    upstream_2m = along(upstream_s, perm=MIDDLE)
+    upstream_3m = along(upstream_1i, perm=MIDDLE)
+    part_2o, part_3o, upstream_2m, upstream_3m = stage(
+        (part_2o, part_3o, upstream_2m, upstream_3m)
+    )
+    tokens_2 = lax.all_gather(part_2m + part_2o, INNER)
+    tokens_3 = lax.all_gather(part_3m + part_3o, INNER)
+    upstream_2o = along(upstream_2m, perm=OUTWARD)
+    upstream_3o = along(upstream_3m, perm=OUTWARD)
+
+    end_sum = scatter_sum(end_back, at_tensor, at_replica)
+    back = project_back(place_of, weight, upstream, parts)
+    own_sum = scatter_sum(back, at_tensor, at_replica)
+    proj, end_proj = project_forward(place_of, weight, tokens, tokens_1)
     proj_out = along(end_proj, perm=OUTWARD)
-    end_sum = lax.psum_scatter(end_back, INNER, scatter_dimension=0)
-    own_sum = lax.psum_scatter(back, INNER, scatter_dimension=0)
     sum_out = along(end_sum, perm=OUTWARD)
     projected = jnp.where(middle, proj, proj_out)
-    token_grad = lax.all_gather(jnp.where(middle, own_sum, sum_out), INNER, axis=1, tiled=True)
+    token_grad = gather_parts(jnp.where(middle, own_sum, sum_out), at_tensor, at_replica)
+
     grads = line_grads(
-        block_ids,
-        tokens,
-        (tokens_1, tokens_2, tokens_3),
-        (upstream, upstream_1, upstream_2m, upstream_2o, upstream_3m, upstream_3o),
-        size,
+        block_ids, None, ((tokens, upstream), (tokens_1, upstream_1)), size, jnp.float32
+    )
+    grads = line_grads(
+        block_ids, grads, ((tokens_2, upstream_2m + upstream_2o),), size, jnp.float32
+    )
+    grads = line_grads(
+        block_ids, grads, ((tokens_3, upstream_3m + upstream_3o),), size, jnp.bfloat16
     )
     return projected, token_grad, grads
 
 
 def solution(mesh):
-    line = mesh.shape["dp"] == 4 and mesh.shape["groups"] == 2
+    line = tuple(mesh.shape[a] for a in ("groups", "dp", "tensor", "replica")) == (2, 4, 2, 2)
     return jax.shard_map(
         line_body if line else general_body,
         mesh=mesh,

time: 299 us -> 312 us (1.043)
  waiting for transfers between devices: 191 us -> 132 us
  Pallas kernels: 33.9 us -> 79.7 us
  other arithmetic: 5.32 us -> 18.5 us
  local copies, waits for them, and re-layouts: 8.31 us -> 19 us
    pallas_call x2 -> x6, Pallas kernels: 33.9 us -> 79.7 us  [the longest x3 61.6 us: line_grads(): pl.pallas_call(functools.partial(line_grads_kernel, len(pairs), start is...]
    ppermute x1, waiting for transfers between devices: 29.2 us -> 0.01 us  [line_body(): proj_out = along(end_proj, perm=OUTWARD)]
    ppermute x8 -> x16, waiting for transfers between devices: 27.8 us -> 56.3 us  [the longest x1 16.9 us: line_body(): near_b = along(other, perm=INWARD)]
    ppermute x1, waiting for transfers between devices: 38.7 us -> 10.8 us  [line_body(): part_2o = along(part_2m, perm=OUTWARD)]
    ppermute x1, waiting for transfers between devices: 0.01 us -> 24.7 us  [line_body(): sum_out = along(end_sum, perm=OUTWARD)]
    ppermute x1, waiting for transfers between devices: 20.3 us -> 0.01 us  [line_body(): near_a = along(mine, perm=INWARD)]
    reduce_scatter x2 -> x0, waiting for transfers between devices: 15.9 us -> none  [the longest x1 15.9 us: line_body(): own_sum = lax.psum_scatter(back, INNER, scatter_dimension=0)]
    ppermute x1, waiting for transfers between devices: 7.46 us -> 21.2 us  [line_body(): ids_1 = along(block_ids, perm=PAIRS)]
  transfers between devices with their start and end apart: 27 -> 32, of which waited for: 11 -> 13; matrix products, arithmetic and copies ran while one was open for 2% -> 9% of each run, Pallas kernels for 9% -> 20%
where the time goes in v3:
time: 312 us; the launch traced here: 310 us
  waiting for transfers between devices  132 us (42%)
  Pallas kernels  79.7 us (26%)
  starting transfers between devices  47.1 us (15%)
  local copies, waits for them, and re-layouts  19 us (6%)
  other arithmetic  18.5 us (6%)
  between operations  14.2 us (5%)
    pallas_call x3, Pallas kernels, line_grads(): pl.pallas_call(functools.partial(line_grads_kernel, len(pairs), start is...  61.6 us
    ppermute x1, waiting for transfers between devices, line_body(): sum_out = along(end_sum, perm=OUTWARD)  24.7 us
    ppermute x1, waiting for transfers between devices, line_body(): ids_1 = along(block_ids, perm=PAIRS)  21.2 us
    ppermute x1, waiting for transfers between devices, line_body(): near_b = along(other, perm=INWARD)  16.9 us
    ppermute x2, waiting for transfers between devices, scatter_sum(): return plus(keep, lax.ppermute(give, 'tensor', SWAP))  16.7 us
    ppermute x1, waiting for transfers between devices, line_body(): part_2o = along(part_2m, perm=OUTWARD)  10.8 us
    ppermute x1, waiting for transfers between devices, line_body(): part_1i = along(part, perm=INWARD)  10.3 us
    ppermute x1, starting transfers between devices, line_body(): part_1i = along(part, perm=INWARD)  8.94 us
  transfers between devices with their start and end apart: 32, of which 13 were waited for; matrix products, arithmetic and copies ran while one was open for 9% of the time, Pallas kernels for 20%

profile of v3, /device:TPU:0, one launch (start us, length us, event | category | flops | bytes accessed | tf_op | source)
XLA Modules:
  0.0 310.4 jit_solution(3389106796743044529)
XLA Ops:
  7.2 1.1 constant_dynamic-slice_fusion
  8.3 2.9 constant_dynamic-slice_fusion.1
  11.3 5.0 %collective-permute-start = (bf16[32,128,128]{2,1,0:T(8,128)(2,1)S(1)}, bf16[32,128,128]{2,1,0:T(8,128)(2,1)S(1)}, u32[]{:S(2)}, u32[]{:S(2)}) collective-permute-start(bf16[32,128,128]{2,1,0:T(8,128)(2,1)S(1)} %get-tuple-element.37), channel_id=1, source_target_pairs={{0,4},{12,8},{1,5},{13,9},{2,6},{14,10},{3,7},{15,11},{16,20},{28,... | collective-permute-start | bytes 3145736 | tf_op jit(solution)/shard_map/ppermute | solution.py:393
  16.2 0.7 collective-permute-start.1
  17.0 1.3 collective-permute-start.2
  18.3 1.3 collective-permute-start.3
  19.6 2.8 collective-permute-start.4
  22.4 21.2 %collective-permute-done.4.ids_1 = s32[64]{0:T(128)S(1)} collective-permute-done((s32[64]{0:T(128)S(1)}, s32[64]{0:T(128)S(1)}, u32[]{:S(2)}, u32[]{:S(2)}) %collective-permute-start.4) | collective-permute-done | bytes 288 | tf_op jit(solution)/shard_map/ppermute | solution.py:397
  44.3 0.8 copy-done.10
  45.1 0.7 collective-permute-start.8
  45.8 1.6 collective-permute-start.9
  47.4 8.9 %collective-permute-start.6 = (bf16[256,1024]{1,0:T(8,128)(2,1)S(1)}, bf16[256,1024]{1,0:T(8,128)(2,1)S(1)}, u32[]{:S(2)}, u32[]{:S(2)}) collective-permute-start(bf16[256,1024]{1,0:T(8,128)(2,1)S(1)} %constant_dynamic-slice_fusion), channel_id=1, source_target_pairs={{0,4},{12,8},{1,5},{13,9},{2,6},{14,10},{3,7},{15,11},{16,20},{28,... | collective-permute-start | bytes 1572872 | tf_op jit(solution)/shard_map/ppermute | solution.py:403
  56.3 1.3 collective-permute-start.7
  57.6 0.7 collective-permute-start.10
  58.3 10.3 %collective-permute-done.6 = bf16[256,1024]{1,0:T(8,128)(2,1)S(1)} collective-permute-done((bf16[256,1024]{1,0:T(8,128)(2,1)S(1)}, bf16[256,1024]{1,0:T(8,128)(2,1)S(1)}, u32[]{:S(2)}, u32[]{:S(2)}) %collective-permute-start.6) | collective-permute-done | bytes 524320 | tf_op jit(solution)/shard_map/ppermute | solution.py:403
  68.6 7.1 %collective-permute-done.7.end_upstream = bf16[256,1024]{1,0:T(8,128)(2,1)S(1)} collective-permute-done((bf16[256,1024]{1,0:T(8,128)(2,1)S(1)}, bf16[256,1024]{1,0:T(8,128)(2,1)S(1)}, u32[]{:S(2)}, u32[]{:S(2)}) %collective-permute-start.7) | collective-permute-done | bytes 524320 | tf_op jit(solution)/shard_map/ppermute | solution.py:404
  75.8 1.0 copy-done.7
  76.8 1.0 add.66
  77.9 4.5 %collective-permute-start.11 = (bf16[32,128,128]{2,1,0:T(8,128)(2,1)}, bf16[32,128,128]{2,1,0:T(8,128)(2,1)S(1)}, u32[]{:S(2)}, u32[]{:S(2)}) collective-permute-start(bf16[32,128,128]{2,1,0:T(8,128)(2,1)} %get-tuple-element.48), channel_id=1, source_target_pairs={{0,4},{12,8},{1,5},{13,9},{2,6},{14,10},{3,7},{15,11},{16,20},{28,... | collective-permute-start | bytes 3145736 | tf_op jit(solution)/shard_map/ppermute | solution.py:414
  82.9 0.7 collective-permute-start.12
  83.6 0.7 collective-permute-start.13
  84.4 16.9 %collective-permute-done.11.near_b = bf16[32,128,128]{2,1,0:T(8,128)(2,1)S(1)} collective-permute-done((bf16[32,128,128]{2,1,0:T(8,128)(2,1)}, bf16[32,128,128]{2,1,0:T(8,128)(2,1)S(1)}, u32[]{:S(2)}, u32[]{:S(2)}) %collective-permute-start.11) | collective-permute-done | bytes 1048608 | tf_op jit(solution)/shard_map/ppermute | solution.py:414
  101.3 2.2 collective-permute-done.14.end_b
  103.5 1.3 collective-permute-start.23
  104.8 1.3 collective-permute-start.24
  106.1 1.5 collective-permute-start.25
  107.6 1.4 collective-permute-start.26
  109.0 10.8 %collective-permute-done.23 = bf16[256,1024]{1,0:T(8,128)(2,1)S(1)} collective-permute-done((bf16[256,1024]{1,0:T(8,128)(2,1)S(1)}, bf16[256,1024]{1,0:T(8,128)(2,1)S(1)}, u32[]{:S(2)}, u32[]{:S(2)}) %collective-permute-start.23) | collective-permute-done | bytes 524320 | tf_op jit(solution)/shard_map/ppermute | solution.py:430
  119.8 5.6 %collective-permute-done.24 = bf16[256,1024]{1,0:T(8,128)(2,1)S(1)} collective-permute-done((bf16[256,1024]{1,0:T(8,128)(2,1)S(1)}, bf16[256,1024]{1,0:T(8,128)(2,1)S(1)}, u32[]{:S(2)}, u32[]{:S(2)}) %collective-permute-start.24) | collective-permute-done | bytes 524320 | tf_op jit(solution)/shard_map/ppermute | solution.py:431
  125.5 0.8 copy-done.13
  126.3 1.0 add.76
  128.0 7.6 %build_weight.1 = (bf16[4096,1024]{1,0:T(8,128)(2,1)}, bf16[4,256,1024]{2,1,0:T(8,128)(2,1)}) custom-call(s32[2]{0:T(128)} %pad_add_fusion.place_of, s32[64]{0:T(128)} %ids.5, s32[64]{0:T(128)} %copy-done.18, s32[64]{0:T(128)} %copy-done.19, s32[64]{0:T(128)} %copy-done.20, bf16[64,128,128]{2,1,0:T(8,128)(2,1)} %own.1, bf16[32,128,128]{2,1,0:T(8,128)(2,1)} %copy-done.5, ...), custom_call_target="tpu_custom_call" | custom-call | flops 2147483648 | bytes 19398656 | tf_op jit(solution)/shard_map/build_weight/pallas_call | solution.py:194
  135.6 1.3 dynamic-slice_bitcast_fusion
  137.0 4.8 %project_back.1 = bf16[4,256,1024]{2,1,0:T(8,128)(2,1)} custom-call(s32[2]{0:T(128)} %pad_add_fusion.place_of, bf16[4096,1024]{1,0:T(8,128)(2,1)} %get-tuple-element.58.weight, bf16[256,1024]{1,0:T(8,128)(2,1)} %refs_1_.1), custom_call_target="tpu_custom_call" | custom-call | flops 2147483648 | bytes 11010048 | tf_op jit(solution)/shard_map/project_back/pallas_call | solution.py:221
  141.9 2.5 dynamic-slice_bitcast_fusion.1
  144.8 1.6 fusion
  146.5 0.8 dynamic-slice_bitcast_fusion.2
  147.3 1.5 collective-permute-start.19
  148.8 2.2 add.78
  151.1 1.6 fusion.1
  153.3 9.1 %collective-permute-done.19 = bf16[256,1024]{1,0:T(8,128)(2,1)} collective-permute-done((bf16[256,1024]{1,0:T(8,128)(2,1)}, bf16[256,1024]{1,0:T(8,128)(2,1)}, u32[]{:S(2)}, u32[]{:S(2)}) %collective-permute-start.19) | collective-permute-done | bytes 524320 | tf_op jit(solution)/shard_map/ppermute | solution.py:358
  162.4 1.2 fusion.2
  163.6 1.3 collective-permute-start.20
  164.9 7.7 %collective-permute-done.17 = bf16[256,1024]{1,0:T(8,128)(2,1)S(1)} collective-permute-done((bf16[256,1024]{1,0:T(8,128)(2,1)S(1)}, bf16[256,1024]{1,0:T(8,128)(2,1)S(1)}, u32[]{:S(2)}, u32[]{:S(2)}) %collective-permute-start.17) | collective-permute-done | bytes 524320 | tf_op jit(solution)/shard_map/ppermute | solution.py:358
  172.6 24.7 %collective-permute-done.20 = bf16[256,1024]{1,0:T(8,128)(2,1)S(1)} collective-permute-done((bf16[256,1024]{1,0:T(8,128)(2,1)S(1)}, bf16[256,1024]{1,0:T(8,128)(2,1)S(1)}, u32[]{:S(2)}, u32[]{:S(2)}) %collective-permute-start.20) | collective-permute-done | bytes 524320 | tf_op jit(solution)/shard_map/ppermute | solution.py:447
  197.6 2.4 collective-permute-start.21
  200.0 1.3 collective-permute-start.27
  201.3 1.3 collective-permute-start.28
  202.6 5.2 %collective-permute-done.21 = bf16[256,1024]{1,0:T(8,128)(2,1)S(1)} collective-permute-done((bf16[256,1024]{1,0:T(8,128)(2,1)S(1)}, bf16[256,1024]{1,0:T(8,128)(2,1)S(1)}, u32[]{:S(2)}, u32[]{:S(2)}) %collective-permute-start.21) | collective-permute-done | bytes 524320 | tf_op jit(solution)/shard_map/ppermute | solution.py:362
  207.8 1.1 maximum_select_fusion.2
  209.0 5.7 %project_forward.1 = (bf16[256,1024]{1,0:T(8,128)(2,1)}, bf16[256,1024]{1,0:T(8,128)(2,1)}) custom-call(s32[2]{0:T(128)} %pad_add_fusion.place_of, bf16[4096,1024]{1,0:T(8,128)(2,1)} %get-tuple-element.58.weight, bf16[256,4096]{1,0:T(8,128)(2,1)} %refs_0_.1, bf16[4,256,1024]{2,1,0:T(8,128)(2,1)} %bitcast.46), custom_call_target="tpu_custom_call" | custom-call | flops 4294967296 | bytes 13631488 | tf_op jit(solution)/shard_map/project_forward/pallas_call | solution.py:263
  214.7 1.3 collective-permute-start.15
  216.0 1.0 add.75.refs_3_
  217.0 3.6 %collective-permute-done.27 = bf16[256,1024]{1,0:T(8,128)(2,1)} collective-permute-done((bf16[256,1024]{1,0:T(8,128)(2,1)}, bf16[256,1024]{1,0:T(8,128)(2,1)}, u32[]{:S(2)}, u32[]{:S(2)}) %collective-permute-start.27) | collective-permute-done | bytes 524320 | tf_op jit(solution)/shard_map/ppermute | solution.py:439
  220.6 2.2 add.77.refs_2_
  222.7 7.2 %collective-permute-done.28 = bf16[256,1024]{1,0:T(8,128)(2,1)} collective-permute-done((bf16[256,1024]{1,0:T(8,128)(2,1)}, bf16[256,1024]{1,0:T(8,128)(2,1)}, u32[]{:S(2)}, u32[]{:S(2)}) %collective-permute-start.28) | collective-permute-done | bytes 524320 | tf_op jit(solution)/shard_map/ppermute | solution.py:440
  229.9 2.2 add.79.refs_2_
  232.1 22.7 %line_grads.3.refs_0_ = f32[64,128,128]{2,1,0:T(8,128)} custom-call(s32[64]{0:T(128)} %ids.5, bf16[256,4096]{1,0:T(8,128)(2,1)} %refs_0_.1, bf16[256,1024]{1,0:T(8,128)(2,1)} %refs_1_.1, bf16[4,256,1024]{2,1,0:T(8,128)(2,1)} %bitcast.47, bf16[256,1024]{1,0:T(8,128)(2,1)} %add.75.refs_3_), custom_call_target="tpu_custom_call" | custom-call | flops 2147483648 | bytes 9437184 | tf_op jit(solution)/shard_map/line_grads/pallas_call | solution.py:320
  255.0 0.9 copy-done.15
  255.9 1.9 broadcast_select_fusion
  258.3 2.6 copy.14
  260.9 4.1 %copy.15 = bf16[256,4096]{1,0:T(8,128)(2,1)} copy(bf16[256,4096]{0,1:T(8,128)(2,1)} %bitcast.41) | data formatting | bytes 4194304
  264.9 19.8 %line_grads.4.refs_0_ = f32[64,128,128]{2,1,0:T(8,128)} custom-call(s32[64]{0:T(128)} %ids.5, f32[64,128,128]{2,1,0:T(8,128)} %line_grads.3.refs_0_, bf16[4,256,1024]{2,1,0:T(8,128)(2,1)} %bitcast.53, bf16[256,1024]{1,0:T(8,128)(2,1)} %add.77.refs_2_), custom_call_target="tpu_custom_call" | custom-call | flops 1073741824 | bytes 6815744 | tf_op jit(solution)/shard_map/line_grads/pallas_call | solution.py:320
  284.7 19.1 %line_grads.5 = bf16[64,128,128]{2,1,0:T(8,128)(2,1)} custom-call(s32[64]{0:T(128)} %ids.5, f32[64,128,128]{2,1,0:T(8,128)} %line_grads.4.refs_0_, bf16[4,256,1024]{2,1,0:T(8,128)(2,1)} %bitcast.48, bf16[256,1024]{1,0:T(8,128)(2,1)} %add.79.refs_2_), custom_call_target="tpu_custom_call" | custom-call | flops 1073741824 | bytes 6815744 | tf_op jit(solution)/shard_map/line_grads/pallas_call | solution.py:320
  (75 shorter events, 4.3 us)
Async XLA Ops:
  7.2 201.8 %all-gather.7.cloned.1.call-start = ((), (), s32[]{:S(2)}) async-start(), calls=%async_computation | async-start | bytes 2621440 | tf_op jit(solution)/shard_map/all_gather | solution.py:411
  8.3 39.1 %copy-start.16 = (bf16[256,1024]{1,0:T(8,128)(2,1)}, bf16[256,1024]{1,0:T(8,128)(2,1)S(1)}, u32[]{:S(2)}) copy-start(bf16[256,1024]{1,0:T(8,128)(2,1)S(1)} %constant_dynamic-slice_fusion) | copy-start | bytes 1572868
  8.3 10.0 %copy-start.1 = (bf16[256,1024]{1,0:T(8,128)(2,1)S(1)}, bf16[256,1024]{1,0:T(8,128)(2,1)}, u32[]{:S(2)}) copy-start(bf16[256,1024]{1,0:T(8,128)(2,1)} %refs_1_.1) | copy-start | bytes 1572868
  8.3 11.3 %copy-start.17 = (s32[64]{0:T(128)S(1)}, s32[64]{0:T(128)}, u32[]{:S(2)}) copy-start(s32[64]{0:T(128)} %ids.5) | copy-start | bytes 772
  11.3 33.0 %collective-permute-start = (bf16[32,128,128]{2,1,0:T(8,128)(2,1)S(1)}, bf16[32,128,128]{2,1,0:T(8,128)(2,1)S(1)}, u32[]{:S(2)}, u32[]{:S(2)}) collective-permute-start(bf16[32,128,128]{2,1,0:T(8,128)(2,1)S(1)} %get-tuple-element.37), channel_id=1, source_target_pairs={{0,4},{12,8},{1,5},{13,9},{2,6},{14,10},{3,7},{15,11},{16,20},{28,... | collective-permute-start | bytes 3145736 | tf_op jit(solution)/shard_map/ppermute | solution.py:393
  16.2 28.8 %collective-permute-start.1 = (bf16[32,128,128]{2,1,0:T(8,128)(2,1)S(1)}, bf16[32,128,128]{2,1,0:T(8,128)(2,1)S(1)}, u32[]{:S(2)}, u32[]{:S(2)}) collective-permute-start(bf16[32,128,128]{2,1,0:T(8,128)(2,1)S(1)} %get-tuple-element.37), channel_id=1, source_target_pairs={{4,8},{8,4},{5,9},{9,5},{6,10},{10,6},{7,11},{11,7},{20,24},{24,20... | collective-permute-start | bytes 3145736 | tf_op jit(solution)/shard_map/ppermute | solution.py:394
  17.0 27.3 %collective-permute-start.2 = (bf16[256,1024]{1,0:T(8,128)(2,1)S(1)}, bf16[256,1024]{1,0:T(8,128)(2,1)S(1)}, u32[]{:S(2)}, u32[]{:S(2)}) collective-permute-start(bf16[256,1024]{1,0:T(8,128)(2,1)S(1)} %constant_dynamic-slice_fusion), channel_id=1, source_target_pairs={{4,0},{8,12},{5,1},{9,13},{6,2},{10,14},{7,3},{11,15},{20,16},{24,... | collective-permute-start | bytes 1572872 | tf_op jit(solution)/shard_map/ppermute | solution.py:395
  18.3 26.0 %collective-permute-start.3 = (bf16[256,1024]{1,0:T(8,128)(2,1)S(1)}, bf16[256,1024]{1,0:T(8,128)(2,1)S(1)}, u32[]{:S(2)}, u32[]{:S(2)}) collective-permute-start(bf16[256,1024]{1,0:T(8,128)(2,1)S(1)} %copy-done.1), channel_id=1, source_target_pairs={{4,0},{8,12},{5,1},{9,13},{6,2},{10,14},{7,3},{11,15},{20,16},{24,... | collective-permute-start | bytes 1572872 | tf_op jit(solution)/shard_map/ppermute | solution.py:396
  19.6 24.0 %collective-permute-start.4 = (s32[64]{0:T(128)S(1)}, s32[64]{0:T(128)S(1)}, u32[]{:S(2)}, u32[]{:S(2)}) collective-permute-start(s32[64]{0:T(128)S(1)} %copy-done.17), channel_id=1, source_target_pairs={{0,4},{12,8},{4,0},{8,12},{1,5},{13,9},{5,1},{9,13},{2,6},{14,10},... | collective-permute-start | bytes 776 | tf_op jit(solution)/shard_map/ppermute | solution.py:397
  43.6 84.5 %copy-start.18 = (s32[64]{0:T(128)}, s32[64]{0:T(128)S(1)}, u32[]{:S(2)}) copy-start(s32[64]{0:T(128)S(1)} %collective-permute-done.4.ids_1) | copy-start | bytes 772
  43.6 0.7 collective-permute-start.5
  44.2 83.8 %copy-start.19 = (s32[64]{0:T(128)}, s32[64]{0:T(128)S(1)}, u32[]{:S(2)}) copy-start(s32[64]{0:T(128)S(1)} %collective-permute-done.5.ids_2) | copy-start | bytes 772
  44.3 0.8 copy-start.10
  45.0 82.3 %copy-start.5 = (bf16[32,128,128]{2,1,0:T(8,128)(2,1)}, bf16[32,128,128]{2,1,0:T(8,128)(2,1)S(1)}, u32[]{:S(2)}) copy-start(bf16[32,128,128]{2,1,0:T(8,128)(2,1)S(1)} %collective-permute-done.near_a) | copy-start | bytes 3145732
  45.0 82.3 %copy-start.6 = (bf16[32,128,128]{2,1,0:T(8,128)(2,1)}, bf16[32,128,128]{2,1,0:T(8,128)(2,1)S(1)}, u32[]{:S(2)}) copy-start(bf16[32,128,128]{2,1,0:T(8,128)(2,1)S(1)} %collective-permute-done.1.far_a) | copy-start | bytes 3145732
  45.1 30.7 %collective-permute-start.8 = (bf16[32,128,128]{2,1,0:T(8,128)(2,1)S(1)}, bf16[32,128,128]{2,1,0:T(8,128)(2,1)S(1)}, u32[]{:S(2)}, u32[]{:S(2)}) collective-permute-start(bf16[32,128,128]{2,1,0:T(8,128)(2,1)S(1)} %collective-permute-done.near_a), channel_id=1, source_target_pairs={{4,8},{8,4},{5,9},{9,5},{6,10},{10,6},{7,11},{11,7},{20,24},{24,20... | collective-permute-start | bytes 3145736 | tf_op jit(solution)/shard_map/ppermute | solution.py:405
  45.8 31.0 %collective-permute-start.9 = (bf16[32,128,128]{2,1,0:T(8,128)(2,1)S(1)}, bf16[32,128,128]{2,1,0:T(8,128)(2,1)}, u32[]{:S(2)}, u32[]{:S(2)}) collective-permute-start(bf16[32,128,128]{2,1,0:T(8,128)(2,1)S(1)} %collective-permute-done.1.far_a), channel_id=1, source_target_pairs={{0,16},{16,0},{1,17},{17,1},{2,18},{18,2},{3,19},{19,3},{4,20},{20... | collective-permute-start | bytes 3145736 | tf_op jit(solution)/shard_map/ppermute | solution.py:406
  47.4 21.3 %collective-permute-start.6 = (bf16[256,1024]{1,0:T(8,128)(2,1)S(1)}, bf16[256,1024]{1,0:T(8,128)(2,1)S(1)}, u32[]{:S(2)}, u32[]{:S(2)}) collective-permute-start(bf16[256,1024]{1,0:T(8,128)(2,1)S(1)} %constant_dynamic-slice_fusion), channel_id=1, source_target_pairs={{0,4},{12,8},{1,5},{13,9},{2,6},{14,10},{3,7},{15,11},{16,20},{28,... | collective-permute-start | bytes 1572872 | tf_op jit(solution)/shard_map/ppermute | solution.py:403
  56.3 19.5 %collective-permute-start.7 = (bf16[256,1024]{1,0:T(8,128)(2,1)S(1)}, bf16[256,1024]{1,0:T(8,128)(2,1)S(1)}, u32[]{:S(2)}, u32[]{:S(2)}) collective-permute-start(bf16[256,1024]{1,0:T(8,128)(2,1)S(1)} %copy-done.1), channel_id=1, source_target_pairs={{0,4},{12,8},{1,5},{13,9},{2,6},{14,10},{3,7},{15,11},{16,20},{28,... | collective-permute-start | bytes 1572872 | tf_op jit(solution)/shard_map/ppermute | solution.py:404
  57.6 0.7 collective-permute-start.10
  58.3 69.7 %copy-start.20 = (s32[64]{0:T(128)}, s32[64]{0:T(128)S(1)}, u32[]{:S(2)}) copy-start(s32[64]{0:T(128)S(1)} %collective-permute-done.10.ids_3) | copy-start | bytes 772
  68.6 8.2 %copy-start.14 = (bf16[256,1024]{1,0:T(8,128)(2,1)}, bf16[256,1024]{1,0:T(8,128)(2,1)S(1)}, u32[]{:S(2)}) copy-start(bf16[256,1024]{1,0:T(8,128)(2,1)S(1)} %collective-permute-done.6) | copy-start | bytes 1572868
  75.8 51.5 %copy-start.2 = (bf16[256,1024]{1,0:T(8,128)(2,1)}, bf16[256,1024]{1,0:T(8,128)(2,1)S(1)}, u32[]{:S(2)}) copy-start(bf16[256,1024]{1,0:T(8,128)(2,1)S(1)} %collective-permute-done.7.end_upstream) | copy-start | bytes 1572868
  75.8 1.0 copy-start.7
  77.8 187.1 %all-gather.9.cloned.1.call-start = ((), (), s32[]{:S(2)}) async-start(), calls=%async_computation.1 | async-start | bytes 2621440 | tf_op jit(solution)/shard_map/all_gather | solution.py:437
  77.9 23.4 %collective-permute-start.11 = (bf16[32,128,128]{2,1,0:T(8,128)(2,1)}, bf16[32,128,128]{2,1,0:T(8,128)(2,1)S(1)}, u32[]{:S(2)}, u32[]{:S(2)}) collective-permute-start(bf16[32,128,128]{2,1,0:T(8,128)(2,1)} %get-tuple-element.48), channel_id=1, source_target_pairs={{0,4},{12,8},{1,5},{13,9},{2,6},{14,10},{3,7},{15,11},{16,20},{28,... | collective-permute-start | bytes 3145736 | tf_op jit(solution)/shard_map/ppermute | solution.py:414
  82.4 21.2 %collective-permute-start.14 = (bf16[32,128,128]{2,1,0:T(8,128)(2,1)}, bf16[32,128,128]{2,1,0:T(8,128)(2,1)S(1)}, u32[]{:S(2)}, u32[]{:S(2)}) collective-permute-start(bf16[32,128,128]{2,1,0:T(8,128)(2,1)} %copy-done.7), channel_id=1, source_target_pairs={{0,16},{16,0},{1,17},{17,1},{2,18},{18,2},{3,19},{19,3},{4,20},{20... | collective-permute-start | bytes 3145736 | tf_op jit(solution)/shard_map/ppermute | solution.py:417
  82.9 1.4 collective-permute-start.12
  83.6 0.7 collective-permute-start.13
  84.3 41.1 %copy-start.12 = (bf16[256,1024]{1,0:T(8,128)(2,1)}, bf16[256,1024]{1,0:T(8,128)(2,1)S(1)}, u32[]{:S(2)}) copy-start(bf16[256,1024]{1,0:T(8,128)(2,1)S(1)} %collective-permute-done.13) | copy-start | bytes 1572868
  101.3 24.2 %copy-start.8 = (bf16[32,128,128]{2,1,0:T(8,128)(2,1)}, bf16[32,128,128]{2,1,0:T(8,128)(2,1)S(1)}, u32[]{:S(2)}) copy-start(bf16[32,128,128]{2,1,0:T(8,128)(2,1)S(1)} %collective-permute-done.11.near_b) | copy-start | bytes 3145732
  103.5 21.9 %copy-start.9 = (bf16[32,128,128]{2,1,0:T(8,128)(2,1)}, bf16[32,128,128]{2,1,0:T(8,128)(2,1)S(1)}, u32[]{:S(2)}) copy-start(bf16[32,128,128]{2,1,0:T(8,128)(2,1)S(1)} %collective-permute-done.14.end_b) | copy-start | bytes 3145732
  103.5 16.3 %collective-permute-start.23 = (bf16[256,1024]{1,0:T(8,128)(2,1)S(1)}, bf16[256,1024]{1,0:T(8,128)(2,1)S(1)}, u32[]{:S(2)}, u32[]{:S(2)}) collective-permute-start(bf16[256,1024]{1,0:T(8,128)(2,1)S(1)} %collective-permute-done.12), channel_id=1, source_target_pairs={{4,0},{8,12},{5,1},{9,13},{6,2},{10,14},{7,3},{11,15},{20,16},{24,... | collective-permute-start | bytes 1572872 | tf_op jit(solution)/shard_map/ppermute | solution.py:430
  104.8 20.6 %collective-permute-start.24 = (bf16[256,1024]{1,0:T(8,128)(2,1)S(1)}, bf16[256,1024]{1,0:T(8,128)(2,1)S(1)}, u32[]{:S(2)}, u32[]{:S(2)}) collective-permute-start(bf16[256,1024]{1,0:T(8,128)(2,1)S(1)} %collective-permute-done.13), channel_id=1, source_target_pairs={{4,0},{8,12},{5,1},{9,13},{6,2},{10,14},{7,3},{11,15},{20,16},{24,... | collective-permute-start | bytes 1572872 | tf_op jit(solution)/shard_map/ppermute | solution.py:431
  106.1 19.3 %collective-permute-start.25 = (bf16[256,1024]{1,0:T(8,128)(2,1)S(1)}, bf16[256,1024]{1,0:T(8,128)(2,1)}, u32[]{:S(2)}, u32[]{:S(2)}) collective-permute-start(bf16[256,1024]{1,0:T(8,128)(2,1)S(1)} %copy-done.1), channel_id=1, source_target_pairs={{4,8},{8,4},{5,9},{9,5},{6,10},{10,6},{7,11},{11,7},{20,24},{24,20... | collective-permute-start | bytes 1572872 | tf_op jit(solution)/shard_map/ppermute | solution.py:432
  107.6 18.7 %collective-permute-start.26 = (bf16[256,1024]{1,0:T(8,128)(2,1)S(1)}, bf16[256,1024]{1,0:T(8,128)(2,1)}, u32[]{:S(2)}, u32[]{:S(2)}) collective-permute-start(bf16[256,1024]{1,0:T(8,128)(2,1)S(1)} %collective-permute-done.7.end_upstream), channel_id=1, source_target_pairs={{4,8},{8,4},{5,9},{9,5},{6,10},{10,6},{7,11},{11,7},{20,24},{24,20... | collective-permute-start | bytes 1572872 | tf_op jit(solution)/shard_map/ppermute | solution.py:433
  125.5 0.8 copy-start.13
  127.3 157.4 %all-gather.11.cloned.1.call-start = ((), (), s32[]{:S(2)}) async-start(), calls=%async_computation.2 | async-start | bytes 2621440 | tf_op jit(solution)/shard_map/all_gather | solution.py:438
  137.0 7.9 %collective-permute-start.18 = (bf16[2,256,1024]{2,1,0:T(8,128)(2,1)S(1)}, bf16[2,256,1024]{2,1,0:T(8,128)(2,1)}, u32[]{:S(2)}, u32[]{:S(2)}) collective-permute-start(bf16[2,256,1024]{2,1,0:T(8,128)(2,1)S(1)} %dynamic-slice_bitcast_fusion), channel_id=1, source_target_pairs={{0,1},{1,0},{2,3},{3,2},{4,5},{5,4},{6,7},{7,6},{8,9},{9,8},{10,11... | collective-permute-start | bytes 3145736 | tf_op jit(solution)/shard_map/ppermute | solution.py:355
  141.9 3.0 copy-start.4
  144.3 6.7 %collective-permute-start.16 = (bf16[2,256,1024]{2,1,0:T(8,128)(2,1)}, bf16[2,256,1024]{2,1,0:T(8,128)(2,1)}, u32[]{:S(2)}, u32[]{:S(2)}) collective-permute-start(bf16[2,256,1024]{2,1,0:T(8,128)(2,1)} %dynamic-slice_bitcast_fusion.1), channel_id=1, source_target_pairs={{0,1},{1,0},{2,3},{3,2},{4,5},{5,4},{6,7},{7,6},{8,9},{9,8},{10,11... | collective-permute-start | bytes 3145736 | tf_op jit(solution)/shard_map/ppermute | solution.py:355
  146.5 4.6 %copy-start = (bf16[4,256,1024]{2,1,0:T(8,128)(2,1)S(1)}, bf16[4,256,1024]{2,1,0:T(8,128)(2,1)}, u32[]{:S(2)}) copy-start(bf16[4,256,1024]{2,1,0:T(8,128)(2,1)} %project_back.1) | copy-start | bytes 6291460
  147.3 15.1 %collective-permute-start.19 = (bf16[256,1024]{1,0:T(8,128)(2,1)}, bf16[256,1024]{1,0:T(8,128)(2,1)}, u32[]{:S(2)}, u32[]{:S(2)}) collective-permute-start(bf16[256,1024]{1,0:T(8,128)(2,1)} %dynamic-slice_bitcast_fusion.2), channel_id=1, source_target_pairs={{0,2},{2,0},{1,3},{3,1},{4,6},{6,4},{5,7},{7,5},{8,10},{10,8},{9,1... | collective-permute-start | bytes 1572872 | tf_op jit(solution)/shard_map/ppermute | solution.py:358
  152.7 19.9 %collective-permute-start.17 = (bf16[256,1024]{1,0:T(8,128)(2,1)S(1)}, bf16[256,1024]{1,0:T(8,128)(2,1)S(1)}, u32[]{:S(2)}, u32[]{:S(2)}) collective-permute-start(bf16[256,1024]{1,0:T(8,128)(2,1)S(1)} %dynamic-slice_bitcast_fusion.3), channel_id=1, source_target_pairs={{0,2},{2,0},{1,3},{3,1},{4,6},{6,4},{5,7},{7,5},{8,10},{10,8},{9,1... | collective-permute-start | bytes 1572872 | tf_op jit(solution)/shard_map/ppermute | solution.py:358
  163.6 33.7 %collective-permute-start.20 = (bf16[256,1024]{1,0:T(8,128)(2,1)S(1)}, bf16[256,1024]{1,0:T(8,128)(2,1)S(1)}, u32[]{:S(2)}, u32[]{:S(2)}) collective-permute-start(bf16[256,1024]{1,0:T(8,128)(2,1)S(1)} %fusion.2), channel_id=1, source_target_pairs={{4,0},{8,12},{5,1},{9,13},{6,2},{10,14},{7,3},{11,15},{20,16},{24,... | collective-permute-start | bytes 1572872 | tf_op jit(solution)/shard_map/ppermute | solution.py:447
  197.6 10.2 %collective-permute-start.21 = (bf16[256,1024]{1,0:T(8,128)(2,1)S(1)}, bf16[256,1024]{1,0:T(8,128)(2,1)S(1)}, u32[]{:S(2)}, u32[]{:S(2)}) collective-permute-start(bf16[256,1024]{1,0:T(8,128)(2,1)S(1)} %fusion.4), channel_id=1, source_target_pairs={{0,2},{2,0},{1,3},{3,1},{4,6},{6,4},{5,7},{7,5},{8,10},{10,8},{9,1... | collective-permute-start | bytes 1572872 | tf_op jit(solution)/shard_map/ppermute | solution.py:362
  200.0 20.5 %collective-permute-start.27 = (bf16[256,1024]{1,0:T(8,128)(2,1)}, bf16[256,1024]{1,0:T(8,128)(2,1)}, u32[]{:S(2)}, u32[]{:S(2)}) collective-permute-start(bf16[256,1024]{1,0:T(8,128)(2,1)} %collective-permute-done.25), channel_id=1, source_target_pairs={{4,0},{8,12},{5,1},{9,13},{6,2},{10,14},{7,3},{11,15},{20,16},{24,... | collective-permute-start | bytes 1572872 | tf_op jit(solution)/shard_map/ppermute | solution.py:439
  201.3 28.6 %collective-permute-start.28 = (bf16[256,1024]{1,0:T(8,128)(2,1)}, bf16[256,1024]{1,0:T(8,128)(2,1)}, u32[]{:S(2)}, u32[]{:S(2)}) collective-permute-start(bf16[256,1024]{1,0:T(8,128)(2,1)} %collective-permute-done.26), channel_id=1, source_target_pairs={{4,0},{8,12},{5,1},{9,13},{6,2},{10,14},{7,3},{11,15},{20,16},{24,... | collective-permute-start | bytes 1572872 | tf_op jit(solution)/shard_map/ppermute | solution.py:440
  209.0 48.8 %collective-permute-start.22 = (bf16[2,256,1024]{2,1,0:T(8,128)(2,1)}, bf16[2,256,1024]{2,1,0:T(8,128)(2,1)S(1)}, u32[]{:S(2)}, u32[]{:S(2)}) collective-permute-start(bf16[2,256,1024]{2,1,0:T(8,128)(2,1)} %maximum_select_fusion.2), channel_id=1, source_target_pairs={{0,1},{1,0},{2,3},{3,2},{4,5},{5,4},{6,7},{7,6},{8,9},{9,8},{10,11... | collective-permute-start | bytes 3145736 | tf_op jit(solution)/shard_map/ppermute | solution.py:366
  209.0 7.0 %copy-start.3 = (bf16[256,1024]{1,0:T(8,128)(2,1)S(1)}, bf16[256,1024]{1,0:T(8,128)(2,1)}, u32[]{:S(2)}) copy-start(bf16[256,1024]{1,0:T(8,128)(2,1)} %copy-done.2) | copy-start | bytes 1572868
  209.0 7.0 %copy-start.11 = (bf16[256,1024]{1,0:T(8,128)(2,1)S(1)}, bf16[256,1024]{1,0:T(8,128)(2,1)}, u32[]{:S(2)}) copy-start(bf16[256,1024]{1,0:T(8,128)(2,1)} %copy-done.10) | copy-start | bytes 1572868
  214.7 40.3 %collective-permute-start.15 = (bf16[256,1024]{1,0:T(8,128)(2,1)}, bf16[256,1024]{1,0:T(8,128)(2,1)}, u32[]{:S(2)}, u32[]{:S(2)}) collective-permute-start(bf16[256,1024]{1,0:T(8,128)(2,1)} %get-tuple-element.61), channel_id=1, source_target_pairs={{4,0},{8,12},{5,1},{9,13},{6,2},{10,14},{7,3},{11,15},{20,16},{24,... | collective-permute-start | bytes 1572872 | tf_op jit(solution)/shard_map/ppermute | solution.py:446
  254.8 1.0 copy-start.15
Sparse Core Ops, SparseCore 0:
  78.0 21.7 all-gather.6
  127.4 23.8 all-gather.8
  152.9 37.5 all-gather.10

commit v4 on v3

--- a/solution.py
+++ b/solution.py
@@ -1,4 +1,5 @@
 import functools
+import math
 
 import jax
 import jax.numpy as jnp
@@ -134,8 +135,8 @@
     return proj, lax.psum(back, INNER), grads
 
 
-def place_blocks(ids, first, blocks, weight):
-    slots, size = blocks.shape[0], blocks.shape[1]
+def place_blocks(ids, first, blocks, weight, slots):
+    size = blocks.shape[1]
     depth, width = weight.shape
     cols_n = width // size
     total = (depth // size) * cols_n
@@ -151,78 +152,121 @@
             weight[pl.ds(r, size), pl.ds(c, size)] = blocks[s]
 
 
-def weight_kernel(
-    place_of, ids_0, ids_1, ids_2, ids_3, own, near_a, near_b, far_a, far_b, end_a, end_b,
-    end_upstream, weight, end_back,
-):
+def place_kernel(place_of, ids_0, ids_1, ids_2, ids_3, own, near_a, far_a, far_b, end_a, weight):
     is_middle, half = place_of[0], place_of[1]
-    half_slots = near_a.shape[0]
+    half_slots = far_b.shape[0] - 1
     mine, other = half * half_slots, (1 - half) * half_slots
 
     @pl.when(is_middle == 1)
     def work():
         weight[...] = jnp.zeros_like(weight)
-        place_blocks(ids_0, 0, own, weight)
-        place_blocks(ids_1, mine, near_a, weight)
-        place_blocks(ids_1, other, near_b, weight)
-        place_blocks(ids_2, mine, far_a, weight)
-        place_blocks(ids_2, other, far_b, weight)
-        place_blocks(ids_3, mine, end_a, weight)
-        place_blocks(ids_3, other, end_b, weight)
-        backward_rows(end_upstream, weight, end_back)
-
-
-def backward_rows(upstream, weight, back):
+        place_blocks(ids_0, 0, own, weight, own.shape[0])
+        place_blocks(ids_1, mine, near_a, weight, half_slots)
+        place_blocks(ids_2, mine, far_a, weight, half_slots)
+        place_blocks(ids_2, other, far_b, weight, half_slots)
+        place_blocks(ids_3, mine, end_a, weight, half_slots)
+
+
+def place_first(place_of, ids, pieces, depth, width):
+    return pl.pallas_call(
+        place_kernel,
+        out_shape=jax.ShapeDtypeStruct((depth, width), jnp.bfloat16),
+        in_specs=[whole(pltpu.SMEM)] * 5 + [whole()] * 5,
+        out_specs=whole(),
+        compiler_params=pltpu.CompilerParams(vmem_limit_bytes=VMEM_LIMIT),
+        cost_estimate=pl.CostEstimate(
+            flops=0, bytes_accessed=depth * width * 4, transcendentals=0
+        ),
+        name="place_first",
+    )(place_of, *ids, *pieces)
+
+
+def backward_rows(place_of, upstream, weight, keep, give):
     depth = weight.shape[0]
     step = 256
-    per_part = back.shape[2] // step
+    per_part = keep.shape[2] // step
+    at_replica = place_of[3]
 
     @pl.loop(0, depth // step)
     def backward(n):
         r = pl.multiple_of(n * step, step)
+        part = n // per_part
         at = pl.multiple_of((n % per_part) * step, step)
-        back[n // per_part, :, pl.ds(at, step)] = lax.dot_general(
+        result = lax.dot_general(
             upstream[...],
             weight[pl.ds(r, step), :],
             (((1,), (1,)), ((), ())),
             preferred_element_type=jnp.float32,
-        ).astype(back.dtype)
-
-
-def build_weight(place_of, ids, pieces, end_upstream, depth, parts):
-    rows, width = end_upstream.shape
-    return pl.pallas_call(
-        weight_kernel,
-        out_shape=(
-            jax.ShapeDtypeStruct((depth, width), jnp.bfloat16),
-            jax.ShapeDtypeStruct((parts, rows, depth // parts), jnp.bfloat16),
-        ),
-        in_specs=[whole(pltpu.SMEM)] * 5 + [whole()] * 8,
-        out_specs=(whole(),) * 2,
+        ).astype(keep.dtype)
+
+        @pl.when(part % 2 == at_replica)
+        def mine():
+            keep[part // 2, :, pl.ds(at, step)] = result
+
+        @pl.when(part % 2 != at_replica)
+        def theirs():
+            give[part // 2, :, pl.ds(at, step)] = result
+
+
+def finish_kernel(
+    place_of, ids_1, ids_3, partial, near_b, end_b, upstream, weight, keep, give,
+    held, sem_in, sem_out,
+):
+    half_slots = near_b.shape[0]
+    other = (1 - place_of[1]) * half_slots
+
+    @pl.when(place_of[0] == 1)
+    def work():
+        load = pltpu.make_async_copy(partial, held, sem_in)
+        load.start()
+        load.wait()
+        place_blocks(ids_1, other, near_b, held, half_slots)
+        place_blocks(ids_3, other, end_b, held, half_slots)
+        store = pltpu.make_async_copy(held, weight, sem_out)
+        store.start()
+        backward_rows(place_of, upstream, held, keep, give)
+        store.wait()
+
+
+def finish_weight(place_of, ids_1, ids_3, partial, near_b, end_b, upstream):
+    depth, width = partial.shape
+    rows = upstream.shape[0]
+    half = jax.ShapeDtypeStruct((2, rows, depth // 4), jnp.bfloat16)
+    return pl.pallas_call(
+        finish_kernel,
+        out_shape=(jax.ShapeDtypeStruct((depth, width), jnp.bfloat16), half, half),
+        in_specs=[whole(pltpu.SMEM)] * 3 + [whole(pl.ANY)] + [whole()] * 3,
+        out_specs=(whole(pl.ANY), whole(), whole()),
+        scratch_shapes=[
+            pltpu.VMEM((depth, width), jnp.bfloat16),
+            pltpu.SemaphoreType.DMA,
+            pltpu.SemaphoreType.DMA,
+        ],
         compiler_params=pltpu.CompilerParams(vmem_limit_bytes=VMEM_LIMIT),
         cost_estimate=pl.CostEstimate(
             flops=2 * rows * depth * width,
             bytes_accessed=depth * width * 4 + rows * (depth + width) * 2,
             transcendentals=0,
         ),
-        name="build_weight",
-    )(place_of, *ids, *pieces, end_upstream)
-
-
-def backward_kernel(place_of, weight, upstream, back):
+        name="finish_weight",
+    )(place_of, ids_1, ids_3, partial, near_b, end_b, upstream)
+
+
+def backward_kernel(place_of, weight, upstream, keep, give):
     @pl.when(place_of[0] == 1)
     def work():
-        backward_rows(upstream, weight, back)
-
-
-def project_back(place_of, weight, upstream, parts):
+        backward_rows(place_of, upstream, weight, keep, give)
+
+
+def project_back(place_of, weight, upstream):
     depth, width = weight.shape
     rows = upstream.shape[0]
+    half = jax.ShapeDtypeStruct((2, rows, depth // 4), jnp.bfloat16)
     return pl.pallas_call(
         backward_kernel,
-        out_shape=jax.ShapeDtypeStruct((parts, rows, depth // parts), jnp.bfloat16),
+        out_shape=(half, half),
         in_specs=[whole(pltpu.SMEM)] + [whole()] * 2,
-        out_specs=whole(),
+        out_specs=(whole(),) * 2,
         compiler_params=pltpu.CompilerParams(vmem_limit_bytes=VMEM_LIMIT),
         cost_estimate=pl.CostEstimate(
             flops=2 * rows * depth * width,
@@ -275,16 +319,62 @@
     )(place_of, weight, tokens, end_tokens)
 
 
+def split_kernel(place_of, keep, got, own, give):
+    x = place_of[2]
+    for ref, at in ((own, x), (give, 1 - x)):
+        ref[...] = (keep[at].astype(jnp.float32) + got[at].astype(jnp.float32)).astype(ref.dtype)
+
+
+def add_split(place_of, keep, got):
+    out = jax.ShapeDtypeStruct(keep.shape[1:], keep.dtype)
+    return pl.pallas_call(
+        split_kernel,
+        out_shape=(out, out),
+        in_specs=[whole(pltpu.SMEM), whole(), whole()],
+        out_specs=(whole(), whole()),
+        compiler_params=pltpu.CompilerParams(vmem_limit_bytes=VMEM_LIMIT),
+        cost_estimate=pl.CostEstimate(
+            flops=keep.size, bytes_accessed=keep.size * 6, transcendentals=0
+        ),
+        name="add_split",
+    )(place_of, keep, got)
+
+
+def assemble_kernel(place_of, own, by_core, by_tensor, by_both, full):
+    x, c = place_of[2], place_of[3]
+    width = own.shape[1]
+    for ref, xx, cc in (
+        (own, x, c), (by_core, x, 1 - c), (by_tensor, 1 - x, c), (by_both, 1 - x, 1 - c)
+    ):
+        at = pl.multiple_of((xx * 2 + cc) * width, width)
+        full[:, pl.ds(at, width)] = ref[...]
+
+
+def assemble(place_of, quarters):
+    rows, width = quarters[0].shape
+    return pl.pallas_call(
+        assemble_kernel,
+        out_shape=jax.ShapeDtypeStruct((rows, 4 * width), quarters[0].dtype),
+        in_specs=[whole(pltpu.SMEM)] + [whole()] * 4,
+        out_specs=whole(),
+        compiler_params=pltpu.CompilerParams(vmem_limit_bytes=VMEM_LIMIT),
+        cost_estimate=pl.CostEstimate(
+            flops=0, bytes_accessed=rows * width * 16, transcendentals=0
+        ),
+        name="assemble",
+    )(place_of, *quarters)
+
+
 def line_grads_kernel(pairs_n, has_start, parted, ids, *refs):
     refs = list(refs)
     start = refs.pop(0) if has_start else None
     pairs = [(refs[2 * k], refs[2 * k + 1]) for k in range(pairs_n)]
     grads = refs[2 * pairs_n]
     slots, size = grads.shape[0], grads.shape[1]
-    parts, _, part_width = pairs[-1][0].shape
     cols_n = pairs[0][1].shape[1] // size
-    per_part = part_width // size
-    total = parts * per_part * cols_n
+    rows_n = math.prod(pairs[0][0].shape[::2] if parted[0] else pairs[0][0].shape[1:]) // size
+    per_part = pairs[0][0].shape[-1] // size
+    total = rows_n * cols_n
 
     @pl.loop(0, slots)
     def one(s):
@@ -296,11 +386,10 @@
             part = row // per_part
             r = pl.multiple_of((row % per_part) * size, size)
             c = pl.multiple_of((b % cols_n) * size, size)
-            whole_r = pl.multiple_of(row * size, size)
             acc = start[s] if has_start else jnp.zeros((size, size), jnp.float32)
             for (x, d), cut in zip(pairs, parted):
                 acc += lax.dot_general(
-                    x[part, :, pl.ds(r, size)] if cut else x[:, pl.ds(whole_r, size)],
+                    x[part, :, pl.ds(r, size)] if cut else x[:, pl.ds(r, size)],
                     d[:, pl.ds(c, size)],
                     (((0,), (0,)), ((), ())),
                     preferred_element_type=jnp.float32,
@@ -339,124 +428,100 @@
 
 INWARD = ((0, 1), (3, 2))
 OUTWARD = ((1, 0), (2, 3))
-PAIRS = INWARD + OUTWARD
 MIDDLE = ((1, 2), (2, 1))
 SWAP = ((0, 1), (1, 0))
 
 
-def plus(a, b):
-    return (a.astype(jnp.float32) + b.astype(jnp.float32)).astype(a.dtype)
-
-
-def scatter_sum(parts, at_tensor, at_replica):
-    by_core = parts.reshape((2, 2) + parts.shape[1:])
-    keep = lax.dynamic_index_in_dim(by_core, at_replica, 1, keepdims=False)
-    give = lax.dynamic_index_in_dim(by_core, 1 - at_replica, 1, keepdims=False)
-    chip = plus(keep, lax.ppermute(give, "replica", SWAP))
-    keep = lax.dynamic_index_in_dim(chip, at_tensor, 0, keepdims=False)
-    give = lax.dynamic_index_in_dim(chip, 1 - at_tensor, 0, keepdims=False)
-    return plus(keep, lax.ppermute(give, "tensor", SWAP))
-
-
-def gather_parts(part, at_tensor, at_replica):
-    other = lax.ppermute(part, "tensor", SWAP)
-    pair = jnp.where(
-        at_tensor == 0, jnp.stack([part, other]), jnp.stack([other, part])
-    )
-    core = lax.ppermute(pair, "replica", SWAP)
-    parts = jnp.where(
-        at_replica == 0, jnp.stack([pair, core], 1), jnp.stack([core, pair], 1)
-    )
-    rows, width = part.shape
-    return parts.reshape(4, rows, width).transpose(1, 0, 2).reshape(rows, 4 * width)
+def ids_block(block_ids, size):
+    rows = size * size // block_ids.shape[0]
+    return jnp.broadcast_to(block_ids, (rows, block_ids.shape[0])).reshape(1, size, size)
+
+
+def ids_of(piece, slots):
+    return piece[-1, 0, :slots].astype(jnp.int32)
 
 
 def line_body(tokens, upstream, blocks, block_ids):
-    size = blocks.shape[1]
-    depth = tokens.shape[1]
-    half_slots = blocks.shape[0] // 2
-    parts = 4
-    part_width = depth // parts
+    slots, size = blocks.shape[0], blocks.shape[1]
+    rows, depth = tokens.shape
+    width = upstream.shape[1]
+    half_slots = slots // 2
+    part_width = depth // 4
     at_z, half = lax.axis_index("dp"), lax.axis_index("groups")
     at_tensor, at_replica = lax.axis_index("tensor"), lax.axis_index("replica")
     middle = (at_z == 1) | (at_z == 2)
-    place_of = jnp.stack([middle.astype(jnp.int32), half.astype(jnp.int32)])
+    place_of = jnp.stack([middle.astype(jnp.int32), half, at_tensor, at_replica])
     along = functools.partial(lax.ppermute, axis_name="dp")
     across = functools.partial(lax.ppermute, axis_name="groups", perm=SWAP)
+    sideways = functools.partial(lax.ppermute, axis_name="tensor", perm=SWAP)
+    cores = functools.partial(lax.ppermute, axis_name="replica", perm=SWAP)
     stage = lax.optimization_barrier
 
     mine = lax.dynamic_slice_in_dim(blocks, half * half_slots, half_slots, 0)
     other = lax.dynamic_slice_in_dim(blocks, (1 - half) * half_slots, half_slots, 0)
+    mine = jnp.concatenate([mine, ids_block(block_ids, size).astype(jnp.bfloat16)])
     part = lax.dynamic_slice_in_dim(tokens, lax.axis_index(INNER) * part_width, part_width, 1)
-    mine, other, part = stage((mine, other, part))
+    both = jnp.concatenate([part, upstream])
+    mine, other, both = stage((mine, other, both))
 
     near_a = along(mine, perm=INWARD)
     far_a = along(mine, perm=MIDDLE)
-    part_1o = along(part, perm=OUTWARD)
-    upstream_1o = along(upstream, perm=OUTWARD)
-    ids_1 = along(block_ids, perm=PAIRS)
-    ids_2 = along(block_ids, perm=MIDDLE)
-    near_a, far_a, part_1o, upstream_1o, ids_1, ids_2, part, upstream_s, other = stage(
-        (near_a, far_a, part_1o, upstream_1o, ids_1, ids_2, part, upstream, other)
+    both_1o = along(both, perm=OUTWARD)
+    grads = line_grads(block_ids, None, ((tokens, upstream),), size, jnp.float32)
+    near_a, far_a, both_1o, grads, both_s, other = stage(
+        (near_a, far_a, both_1o, grads, both, other)
     )
 
-    part_1i = along(part, perm=INWARD)
-    upstream_1i = along(upstream_s, perm=INWARD)
+    both_1i = along(both_s, perm=INWARD)
     end_a = along(near_a, perm=MIDDLE)
     far_b = across(far_a)
-    ids_3 = along(ids_1, perm=MIDDLE)
-    part_1i, upstream_1i, end_a, far_b, ids_3, part, upstream_s, other = stage(
-        (part_1i, upstream_1i, end_a, far_b, ids_3, part, upstream_s, other)
+    both_1i, end_a, far_b, both_s, other = stage((both_1i, end_a, far_b, both_s, other))
+    tokens_1 = lax.all_gather(both_1i[:rows] + both_1o[:rows], INNER)
+    upstream_1 = both_1i[rows:] + both_1o[rows:]
+
+    near_b = along(other, perm=INWARD)
+    both_2m = along(both_s, perm=MIDDLE)
+    end_b = across(end_a)
+    ids_1, ids_2, ids_3 = (ids_of(piece, slots) for piece in (near_a, far_a, end_a))
+    partial = place_first(
+        place_of, (block_ids, ids_1, ids_2, ids_3), (blocks, near_a, far_a, far_b, end_a), depth, width
     )
-    tokens_1 = lax.all_gather(part_1i + part_1o, INNER)
-    upstream_1 = upstream_1i + upstream_1o
-
-    near_b = along(other, perm=INWARD)
-    part_2m = along(part, perm=MIDDLE)
-    part_3m = along(part_1i, perm=MIDDLE)
-    end_b = across(end_a)
-    near_b, part_2m, part_3m, end_b, upstream_s, upstream_1i = stage(
-        (near_b, part_2m, part_3m, end_b, upstream_s, upstream_1i)
+    near_b, both_2m, end_b, partial, both_1i = stage((near_b, both_2m, end_b, partial, both_1i))
+
+    both_3m = along(both_1i, perm=MIDDLE)
+    both_2o = along(both_2m, perm=OUTWARD)
+    weight, keep, give = finish_weight(
+        place_of, ids_1, ids_3, partial, near_b, end_b, upstream_1
     )
-
-    weight, end_back = build_weight(
-        place_of,
-        (block_ids, ids_1, ids_2, ids_3),
-        (blocks, near_a, near_b, far_a, far_b, end_a, end_b),
-        upstream_1i,
-        depth,
-        parts,
+    end_keep, end_give = add_split(place_of, keep, cores(give))
+    end_got = sideways(end_give)
+    own_keep, own_give = project_back(place_of, weight, upstream)
+    both_3m, both_2o, end_got, own_keep, own_give = stage(
+        (both_3m, both_2o, end_got, own_keep, own_give)
     )
-    part_2o = along(part_2m, perm=OUTWARD)
-    part_3o = along(part_3m, perm=OUTWARD)
-    upstream_2m = along(upstream_s, perm=MIDDLE)
-    upstream_3m = along(upstream_1i, perm=MIDDLE)
-    part_2o, part_3o, upstream_2m, upstream_3m = stage(
-        (part_2o, part_3o, upstream_2m, upstream_3m)
+    sum_out = along(end_keep + end_got, perm=OUTWARD)
+    tokens_2 = lax.all_gather(both_2m[:rows] + both_2o[:rows], INNER)
+    upstream_2 = both_2m[rows:] + both_2o[rows:]
+    token_3o = along(both_3m[:rows], perm=OUTWARD)
+    own_keep, own_give = add_split(place_of, own_keep, cores(own_give))
+    own_sum = own_keep + sideways(own_give)
+    proj, end_proj = project_forward(place_of, weight, tokens, tokens_1)
+    sum_out, own_sum, token_3o, proj, end_proj = stage(
+        (sum_out, own_sum, token_3o, proj, end_proj)
     )
-    tokens_2 = lax.all_gather(part_2m + part_2o, INNER)
-    tokens_3 = lax.all_gather(part_3m + part_3o, INNER)
-    upstream_2o = along(upstream_2m, perm=OUTWARD)
-    upstream_3o = along(upstream_3m, perm=OUTWARD)
-
-    end_sum = scatter_sum(end_back, at_tensor, at_replica)
-    back = project_back(place_of, weight, upstream, parts)
-    own_sum = scatter_sum(back, at_tensor, at_replica)
-    proj, end_proj = project_forward(place_of, weight, tokens, tokens_1)
+    tokens_3 = lax.all_gather(both_3m[:rows] + token_3o, INNER)
+    quarter = jnp.where(middle, own_sum, sum_out)
+    by_tensor, by_core = sideways(quarter), cores(quarter)
     proj_out = along(end_proj, perm=OUTWARD)
-    sum_out = along(end_sum, perm=OUTWARD)
+    upstream_3o = along(both_3m[rows:], perm=OUTWARD)
+    upstream_3 = both_3m[rows:] + upstream_3o
+    grads = line_grads(block_ids, grads, ((tokens_1, upstream_1),), size, jnp.float32)
+    by_tensor, by_core, grads = stage((by_tensor, by_core, grads))
+    by_both = cores(by_tensor)
     projected = jnp.where(middle, proj, proj_out)
-    token_grad = gather_parts(jnp.where(middle, own_sum, sum_out), at_tensor, at_replica)
-
-    grads = line_grads(
-        block_ids, None, ((tokens, upstream), (tokens_1, upstream_1)), size, jnp.float32
-    )
-    grads = line_grads(
-        block_ids, grads, ((tokens_2, upstream_2m + upstream_2o),), size, jnp.float32
-    )
-    grads = line_grads(
-        block_ids, grads, ((tokens_3, upstream_3m + upstream_3o),), size, jnp.bfloat16
-    )
+    grads = line_grads(block_ids, grads, ((tokens_2, upstream_2),), size, jnp.float32)
+    token_grad = assemble(place_of, (quarter, by_core, by_tensor, by_both))
+    grads = line_grads(block_ids, grads, ((tokens_3, upstream_3),), size, jnp.bfloat16)
     return projected, token_grad, grads
 
 

time: 312 us -> 266 us (0.85)
  waiting for transfers between devices: 132 us -> 92.1 us
  Pallas kernels: 79.7 us -> 105 us
  starting transfers between devices: 47.1 us -> 32.4 us
  local copies, waits for them, and re-layouts: 19 us -> 7.8 us
  other arithmetic: 18.5 us -> 13.2 us
    ppermute x22 -> x15, waiting for transfers between devices: 113 us -> 82.8 us  [the longest x1 29.9 us: line_body(): both_2o = along(both_2m, perm=OUTWARD)]
    ppermute x22 -> x15, starting transfers between devices: 32.7 us -> 17.2 us  [the longest x1 4.25 us: line_body(): both_1i = along(both_s, perm=INWARD)]
    pallas_call x3 -> x4, Pallas kernels: 61.6 us -> 76.9 us  [line_grads(): pl.pallas_call(functools.partial(line_grads_kernel, len(pairs), start is...]
    pallas_call x2 -> x6, Pallas kernels: 12.4 us -> 22.5 us  [the longest x1 6.17 us: place_first(): pl.pallas_call(place_kernel, out_shape=jax.ShapeDtypeStruct((depth, width...]
    ppermute x1, waiting for transfers between devices: 16.9 us -> 9.26 us  [line_body(): near_b = along(other, perm=INWARD)]
    unnamed x43 -> x34, local copies, waits for them, and re-layouts: 7.57 us -> 2.78 us
    squeeze x4 -> x0, local copies, waits for them, and re-layouts: 4.67 us -> none  [the longest x2 3.79 us: scatter_sum(): give = lax.dynamic_index_in_dim(by_core, 1 - at_replica, 1, keepdims=False)]
    add x6 -> x5, other arithmetic: 9.63 us -> 8.45 us  [the longest x1 2.49 us: line_body(): upstream_2 = both_2m[rows:] + both_2o[rows:]]
  transfers between devices with their start and end apart: 32 -> 25, of which waited for: 13 -> 9; matrix products, arithmetic and copies ran while one was open for 9% -> 4% of each run, Pallas kernels for 20% -> 32%
where the time goes in v4:
time: 266 us; the launch traced here: 265 us
  Pallas kernels  105 us (39%)
  waiting for transfers between devices  92.1 us (35%)
  starting transfers between devices  32.4 us (12%)
  between operations  14.1 us (5%)
  other arithmetic  13.2 us (5%)
  local copies, waits for them, and re-layouts  7.8 us (3%)
    pallas_call x4, Pallas kernels, line_grads(): pl.pallas_call(functools.partial(line_grads_kernel, len(pairs), start is...  76.9 us
    ppermute x1, waiting for transfers between devices, line_body(): both_2o = along(both_2m, perm=OUTWARD)  29.9 us
    ppermute x1, waiting for transfers between devices, line_body(): both_1i = along(both_s, perm=INWARD)  20.9 us
    ppermute x1, waiting for transfers between devices, line_body(): own_sum = own_keep + sideways(own_give)  15.6 us
    ppermute x1, waiting for transfers between devices, line_body(): near_b = along(other, perm=INWARD)  9.26 us
    ppermute x1, waiting for transfers between devices, line_body(): both_1o = along(both, perm=OUTWARD)  7.3 us
    ppermute x1, waiting for transfers between devices, line_body(): upstream_3o = along(both_3m[rows:], perm=OUTWARD)  6.91 us
    pallas_call x1, Pallas kernels, place_first(): pl.pallas_call(place_kernel, out_shape=jax.ShapeDtypeStruct((depth, width...  6.17 us
  transfers between devices with their start and end apart: 25, of which 9 were waited for; matrix products, arithmetic and copies ran while one was open for 4% of the time, Pallas kernels for 32%

profile of v4, /device:TPU:0, one launch (start us, length us, event | category | flops | bytes accessed | tf_op | source)
XLA Modules:
  0.0 264.7 jit_solution(2345311751821987943)
XLA Ops:
  7.2 0.0 all-gather.7.cloned.1.call-start
  7.2 0.7 convert_element_type.26
  7.9 0.1 convert_element_type.27
  8.0 2.7 %constant_dynamic-slice_fusion.1 = (bf16[32,128,128]{2,1,0:T(8,128)(2,1)}, bf16[32,128,128]{2,1,0:T(8,128)(2,1)S(1)}) fusion(bf16[64,128,128]{2,1,0:T(8,128)(2,1)} %own.1, s32[]{:T(128)S(6)} %select_n.23, s32[]{:T(128)S(6)} %select_n.22), kind=kLoop, calls=%fused_computation.9 | loop fusion | bytes 4194312 | tf_op jit(solution)/shard_map/dynamic_slice | solution.py:461
  10.7 0.1 pad_maximum_fusion
  10.8 1.1 constant_dynamic-slice_fusion
  11.9 1.1 pad_maximum_fusion.1
  13.0 5.0 %collective-permute-start = (bf16[33,128,128]{2,1,0:T(8,128)(2,1)S(1)}, bf16[33,128,128]{2,1,0:T(8,128)(2,1)S(1)}, u32[]{:S(2)}, u32[]{:S(2)}) collective-permute-start(bf16[33,128,128]{2,1,0:T(8,128)(2,1)S(1)} %pad_maximum_fusion), channel_id=1, source_target_pairs={{0,4},{12,8},{1,5},{13,9},{2,6},{14,10},{3,7},{15,11},{16,20},{28,... | collective-permute-start | bytes 3244040 | tf_op jit(solution)/shard_map/ppermute | solution.py:467
  18.0 0.7 collective-permute-start.1
  18.7 1.3 collective-permute-start.2
  20.0 18.2 %line_grads.4.refs_0_ = f32[64,128,128]{2,1,0:T(8,128)} custom-call(s32[64]{0:T(128)} %ids.7, bf16[256,4096]{1,0:T(8,128)(2,1)} %tokens.1, bf16[256,1024]{1,0:T(8,128)(2,1)} %upstream.1), custom_call_target="tpu_custom_call" | custom-call | flops 1073741824 | bytes 6815744 | tf_op jit(solution)/shard_map/line_grads/pallas_call | solution.py:409
  38.2 7.3 %collective-permute-done.2 = bf16[512,1024]{1,0:T(8,128)(2,1)} collective-permute-done((bf16[512,1024]{1,0:T(8,128)(2,1)}, bf16[512,1024]{1,0:T(8,128)(2,1)}, u32[]{:S(2)}, u32[]{:S(2)}) %collective-permute-start.2) | collective-permute-done | bytes 1048608 | tf_op jit(solution)/shard_map/ppermute | solution.py:469
  45.6 0.7 collective-permute-start.4
  46.3 1.6 collective-permute-start.5
  47.9 4.2 %collective-permute-start.3 = (bf16[512,1024]{1,0:T(8,128)(2,1)}, bf16[512,1024]{1,0:T(8,128)(2,1)S(1)}, u32[]{:S(2)}, u32[]{:S(2)}) collective-permute-start(bf16[512,1024]{1,0:T(8,128)(2,1)} %pad_maximum_fusion.1), channel_id=1, source_target_pairs={{0,4},{12,8},{1,5},{13,9},{2,6},{14,10},{3,7},{15,11},{16,20},{28,... | collective-permute-start | bytes 3145736 | tf_op jit(solution)/shard_map/ppermute | solution.py:475
  52.1 20.9 %collective-permute-done.3 = bf16[512,1024]{1,0:T(8,128)(2,1)S(1)} collective-permute-done((bf16[512,1024]{1,0:T(8,128)(2,1)}, bf16[512,1024]{1,0:T(8,128)(2,1)S(1)}, u32[]{:S(2)}, u32[]{:S(2)}) %collective-permute-start.3) | collective-permute-done | bytes 1048608 | tf_op jit(solution)/shard_map/ppermute | solution.py:475
  73.1 0.9 copy-done.5
  74.0 2.3 slice_add_fusion.2
  76.3 0.0 all-gather.9.cloned.1.call-start
  76.4 0.6 collective-permute-start.8
  77.0 5.2 %collective-permute-start.6 = (bf16[32,128,128]{2,1,0:T(8,128)(2,1)}, bf16[32,128,128]{2,1,0:T(8,128)(2,1)}, u32[]{:S(2)}, u32[]{:S(2)}) collective-permute-start(bf16[32,128,128]{2,1,0:T(8,128)(2,1)} %get-tuple-element.54), channel_id=1, source_target_pairs={{0,4},{12,8},{1,5},{13,9},{2,6},{14,10},{3,7},{15,11},{16,20},{28,... | collective-permute-start | bytes 3145736 | tf_op jit(solution)/shard_map/ppermute | solution.py:482
  82.2 1.7 collective-permute-start.7
  83.9 0.6 pad_add_fusion.place_of
  84.5 0.6 bitcast_convert_fusion
  85.1 0.6 bitcast_convert_fusion.1.ids_3
  85.7 6.2 %place_first.1.partial = bf16[4096,1024]{1,0:T(8,128)(2,1)} custom-call(s32[4]{0:T(128)} %pad_add_fusion.place_of, s32[64]{0:T(128)} %ids.7, s32[64]{0:T(128)} %get-tuple-element.100.ids_1, s32[64]{0:T(128)} %get-tuple-element.99.ids_2, s32[64]{0:T(128)} %bitcast_convert_fusion.1.ids_3, bf16[64,128,128]{2,1,0:T(8,128)(2,1)} %own.1, ...), custom_call_target="tpu_custom_call" | custom-call | bytes 16777216 | tf_op jit(solution)/shard_map/place_first/pallas_call | solution.py:171
  91.9 9.3 %collective-permute-done.6.near_b = bf16[32,128,128]{2,1,0:T(8,128)(2,1)} collective-permute-done((bf16[32,128,128]{2,1,0:T(8,128)(2,1)}, bf16[32,128,128]{2,1,0:T(8,128)(2,1)}, u32[]{:S(2)}, u32[]{:S(2)}) %collective-permute-start.6) | collective-permute-done | bytes 1048608 | tf_op jit(solution)/shard_map/ppermute | solution.py:482
  101.1 3.1 %finish_weight.1 = (bf16[4096,1024]{1,0:T(8,128)(2,1)}, bf16[2,256,1024]{2,1,0:T(8,128)(2,1)}, bf16[2,256,1024]{2,1,0:T(8,128)(2,1)}) custom-call(s32[4]{0:T(128)} %pad_add_fusion.place_of, s32[64]{0:T(128)} %get-tuple-element.100.ids_1, s32[64]{0:T(128)} %bitcast_convert_fusion.1.ids_3, bf16[4096,1024]{1,0:T(8,128)(2,1)} %place_first.1.partial, ...), custom_call_target="tpu_custom_call" | custom-call | flops 2147483648 | bytes 19398656 | tf_op jit(solution)/shard_map/finish_weight/pallas_call | solution.py:235
  104.3 0.1 collective-permute-start.9
  104.3 0.7 collective-permute-start.10
  105.1 1.3 collective-permute-start.11
  106.4 0.9 collective-permute-done.9.got
  107.3 2.7 %add_split.2 = (bf16[256,1024]{1,0:T(8,128)(2,1)}, bf16[256,1024]{1,0:T(8,128)(2,1)}) custom-call(s32[4]{0:T(128)} %pad_add_fusion.place_of, bf16[2,256,1024]{2,1,0:T(8,128)(2,1)} %get-tuple-element.62.keep, bf16[2,256,1024]{2,1,0:T(8,128)(2,1)} %collective-permute-done.9.got), custom_call_target="tpu_custom_call" | custom-call | flops 524288 | bytes 3145728 | tf_op jit(solution)/shard_map/add_split/pallas_call | solution.py:330
  110.0 1.5 collective-permute-start.12
  111.5 4.8 %project_back.1 = (bf16[2,256,1024]{2,1,0:T(8,128)(2,1)}, bf16[2,256,1024]{2,1,0:T(8,128)(2,1)}) custom-call(s32[4]{0:T(128)} %pad_add_fusion.place_of, bf16[4096,1024]{1,0:T(8,128)(2,1)} %get-tuple-element.68.weight, bf16[256,1024]{1,0:T(8,128)(2,1)} %upstream.1), custom_call_target="tpu_custom_call" | custom-call | flops 2147483648 | bytes 11010048 | tf_op jit(solution)/shard_map/project_back/pallas_call | solution.py:265
  116.3 29.9 %collective-permute-done.11 = bf16[512,1024]{1,0:T(8,128)(2,1)S(1)} collective-permute-done((bf16[512,1024]{1,0:T(8,128)(2,1)}, bf16[512,1024]{1,0:T(8,128)(2,1)S(1)}, u32[]{:S(2)}, u32[]{:S(2)}) %collective-permute-start.11) | collective-permute-done | bytes 1048608 | tf_op jit(solution)/shard_map/ppermute | solution.py:492
  146.2 2.5 slice_add_fusion
  148.7 0.0 all-gather.11.cloned.1.call-start
  148.7 0.1 collective-permute-start.14
  148.8 1.1 fusion
  149.9 1.3 collective-permute-start.16
  151.2 0.5 collective-permute-done.14.got
  151.7 1.0 copy-done.7
  152.6 2.7 %add_split.3 = (bf16[256,1024]{1,0:T(8,128)(2,1)}, bf16[256,1024]{1,0:T(8,128)(2,1)}) custom-call(s32[4]{0:T(128)} %pad_add_fusion.place_of, bf16[2,256,1024]{2,1,0:T(8,128)(2,1)} %get-tuple-element.72.keep, bf16[2,256,1024]{2,1,0:T(8,128)(2,1)} %copy-done.7), custom_call_target="tpu_custom_call" | custom-call | flops 524288 | bytes 3145728 | tf_op jit(solution)/shard_map/add_split/pallas_call | solution.py:330
  155.4 1.1 collective-permute-start.15
  156.5 0.2 add.41
  156.7 1.3 collective-permute-start.13
  158.0 1.3 collective-permute-start.21
  159.4 5.7 %project_forward.1 = (bf16[256,1024]{1,0:T(8,128)(2,1)}, bf16[256,1024]{1,0:T(8,128)(2,1)}) custom-call(s32[4]{0:T(128)} %pad_add_fusion.place_of, bf16[4096,1024]{1,0:T(8,128)(2,1)} %get-tuple-element.68.weight, bf16[256,4096]{1,0:T(8,128)(2,1)} %tokens.1, bf16[4,256,1024]{2,1,0:T(8,128)(2,1)} %bitcast.17), custom_call_target="tpu_custom_call" | custom-call | flops 4294967296 | bytes 13631488 | tf_op jit(solution)/shard_map/project_forward/pallas_call | solution.py:307
  165.0 15.6 %collective-permute-done.15 = bf16[256,1024]{1,0:T(8,128)(2,1)} collective-permute-done((bf16[256,1024]{1,0:T(8,128)(2,1)}, bf16[256,1024]{1,0:T(8,128)(2,1)}, u32[]{:S(2)}, u32[]{:S(2)}) %collective-permute-start.15) | collective-permute-done | bytes 524320 | tf_op jit(solution)/shard_map/ppermute | solution.py:507
  180.6 1.3 add.42
  181.9 6.9 %collective-permute-done.21 = bf16[256,1024]{1,0:T(8,128)(2,1)S(1)} collective-permute-done((bf16[256,1024]{1,0:T(8,128)(2,1)}, bf16[256,1024]{1,0:T(8,128)(2,1)S(1)}, u32[]{:S(2)}, u32[]{:S(2)}) %collective-permute-start.21) | collective-permute-done | bytes 524320 | tf_op jit(solution)/shard_map/ppermute | solution.py:516
  188.8 2.2 slice_add_fusion.4
  191.0 0.1 broadcast_select_fusion.own
  191.1 1.2 collective-permute-start.18
  192.3 1.3 collective-permute-start.17
  193.6 19.8 %line_grads.5.refs_0_ = f32[64,128,128]{2,1,0:T(8,128)} custom-call(s32[64]{0:T(128)} %ids.7, f32[64,128,128]{2,1,0:T(8,128)} %line_grads.4.refs_0_, bf16[4,256,1024]{2,1,0:T(8,128)(2,1)} %bitcast.18, bf16[256,1024]{1,0:T(8,128)(2,1)} %get-tuple-element.92.upstream.refs_2_), custom_call_target="tpu_custom_call" | custom-call | flops 1073741824 | bytes 6815744 | tf_op jit(solution)/shard_map/line_grads/pallas_call | solution.py:409
  213.5 0.1 collective-permute-start.20
  213.6 1.1 broadcast_select_fusion.1
  214.7 0.8 collective-permute-done.20.by_both
  215.5 0.8 copy-done.14
  216.3 3.0 %assemble.1 = bf16[256,4096]{1,0:T(8,128)(2,1)} custom-call(s32[4]{0:T(128)} %pad_add_fusion.place_of, bf16[256,1024]{1,0:T(8,128)(2,1)} %copy-done.1, bf16[256,1024]{1,0:T(8,128)(2,1)} %copy-done.13, bf16[256,1024]{1,0:T(8,128)(2,1)} %copy-done.11, bf16[256,1024]{1,0:T(8,128)(2,1)} %copy-done.14), custom_call_target="tpu_custom_call" | custom-call | bytes 4194304 | tf_op jit(solution)/shard_map/assemble/pallas_call | solution.py:355
  219.3 19.8 %line_grads.6.refs_0_ = f32[64,128,128]{2,1,0:T(8,128)} custom-call(s32[64]{0:T(128)} %ids.7, f32[64,128,128]{2,1,0:T(8,128)} %line_grads.5.refs_0_, bf16[4,256,1024]{2,1,0:T(8,128)(2,1)} %bitcast.19, bf16[256,1024]{1,0:T(8,128)(2,1)} %get-tuple-element.89.refs_2_), custom_call_target="tpu_custom_call" | custom-call | flops 1073741824 | bytes 6815744 | tf_op jit(solution)/shard_map/line_grads/pallas_call | solution.py:409
  239.0 19.1 %line_grads.7 = bf16[64,128,128]{2,1,0:T(8,128)(2,1)} custom-call(s32[64]{0:T(128)} %ids.7, f32[64,128,128]{2,1,0:T(8,128)} %line_grads.6.refs_0_, bf16[4,256,1024]{2,1,0:T(8,128)(2,1)} %bitcast.16, bf16[256,1024]{1,0:T(8,128)(2,1)} %get-tuple-element.95.refs_2_), custom_call_target="tpu_custom_call" | custom-call | flops 1073741824 | bytes 6815744 | tf_op jit(solution)/shard_map/line_grads/pallas_call | solution.py:409
  (53 shorter events, 0.2 us)
Async XLA Ops:
  7.2 152.2 %all-gather.7.cloned.1.call-start = ((), (), s32[]{:S(2)}) async-start(), calls=%async_computation | async-start | bytes 2621440 | tf_op jit(solution)/shard_map/all_gather | solution.py:479
  10.7 1.2 copy-start
  13.0 32.6 %collective-permute-start = (bf16[33,128,128]{2,1,0:T(8,128)(2,1)S(1)}, bf16[33,128,128]{2,1,0:T(8,128)(2,1)S(1)}, u32[]{:S(2)}, u32[]{:S(2)}) collective-permute-start(bf16[33,128,128]{2,1,0:T(8,128)(2,1)S(1)} %pad_maximum_fusion), channel_id=1, source_target_pairs={{0,4},{12,8},{1,5},{13,9},{2,6},{14,10},{3,7},{15,11},{16,20},{28,... | collective-permute-start | bytes 3244040 | tf_op jit(solution)/shard_map/ppermute | solution.py:467
  18.0 27.6 %collective-permute-start.1 = (bf16[33,128,128]{2,1,0:T(8,128)(2,1)S(1)}, bf16[33,128,128]{2,1,0:T(8,128)(2,1)S(1)}, u32[]{:S(2)}, u32[]{:S(2)}) collective-permute-start(bf16[33,128,128]{2,1,0:T(8,128)(2,1)S(1)} %pad_maximum_fusion), channel_id=1, source_target_pairs={{4,8},{8,4},{5,9},{9,5},{6,10},{10,6},{7,11},{11,7},{20,24},{24,20... | collective-permute-start | bytes 3244040 | tf_op jit(solution)/shard_map/ppermute | solution.py:468
  18.7 26.8 %collective-permute-start.2 = (bf16[512,1024]{1,0:T(8,128)(2,1)}, bf16[512,1024]{1,0:T(8,128)(2,1)}, u32[]{:S(2)}, u32[]{:S(2)}) collective-permute-start(bf16[512,1024]{1,0:T(8,128)(2,1)} %pad_maximum_fusion.1), channel_id=1, source_target_pairs={{4,0},{8,12},{5,1},{9,13},{6,2},{10,14},{7,3},{11,15},{20,16},{24,... | collective-permute-start | bytes 3145736 | tf_op jit(solution)/shard_map/ppermute | solution.py:469
  45.5 40.1 %copy-start.2 = (bf16[33,128,128]{2,1,0:T(8,128)(2,1)}, bf16[33,128,128]{2,1,0:T(8,128)(2,1)S(1)}, u32[]{:S(2)}) copy-start(bf16[33,128,128]{2,1,0:T(8,128)(2,1)S(1)} %collective-permute-done.near_a) | copy-start | bytes 3244036
  45.5 40.1 %copy-start.3 = (bf16[33,128,128]{2,1,0:T(8,128)(2,1)}, bf16[33,128,128]{2,1,0:T(8,128)(2,1)S(1)}, u32[]{:S(2)}) copy-start(bf16[33,128,128]{2,1,0:T(8,128)(2,1)S(1)} %collective-permute-done.1.far_a) | copy-start | bytes 3244036
  45.6 27.5 %collective-permute-start.4 = (bf16[33,128,128]{2,1,0:T(8,128)(2,1)S(1)}, bf16[33,128,128]{2,1,0:T(8,128)(2,1)S(1)}, u32[]{:S(2)}, u32[]{:S(2)}) collective-permute-start(bf16[33,128,128]{2,1,0:T(8,128)(2,1)S(1)} %collective-permute-done.near_a), channel_id=1, source_target_pairs={{4,8},{8,4},{5,9},{9,5},{6,10},{10,6},{7,11},{11,7},{20,24},{24,20... | collective-permute-start | bytes 3244040 | tf_op jit(solution)/shard_map/ppermute | solution.py:476
  46.3 26.8 %collective-permute-start.5 = (bf16[33,128,128]{2,1,0:T(8,128)(2,1)S(1)}, bf16[33,128,128]{2,1,0:T(8,128)(2,1)}, u32[]{:S(2)}, u32[]{:S(2)}) collective-permute-start(bf16[33,128,128]{2,1,0:T(8,128)(2,1)S(1)} %collective-permute-done.1.far_a), channel_id=1, source_target_pairs={{0,16},{16,0},{1,17},{17,1},{2,18},{18,2},{3,19},{19,3},{4,20},{20... | collective-permute-start | bytes 3244040 | tf_op jit(solution)/shard_map/ppermute | solution.py:477
  47.9 25.2 %collective-permute-start.3 = (bf16[512,1024]{1,0:T(8,128)(2,1)}, bf16[512,1024]{1,0:T(8,128)(2,1)S(1)}, u32[]{:S(2)}, u32[]{:S(2)}) collective-permute-start(bf16[512,1024]{1,0:T(8,128)(2,1)} %pad_maximum_fusion.1), channel_id=1, source_target_pairs={{0,4},{12,8},{1,5},{13,9},{2,6},{14,10},{3,7},{15,11},{16,20},{28,... | collective-permute-start | bytes 3145736 | tf_op jit(solution)/shard_map/ppermute | solution.py:475
  73.0 1.0 copy-start.5
  73.0 12.6 %copy-start.4 = (bf16[33,128,128]{2,1,0:T(8,128)(2,1)}, bf16[33,128,128]{2,1,0:T(8,128)(2,1)S(1)}, u32[]{:S(2)}) copy-start(bf16[33,128,128]{2,1,0:T(8,128)(2,1)S(1)} %collective-permute-done.4.end_a) | copy-start | bytes 3244036
  76.3 142.9 %all-gather.9.cloned.1.call-start = ((), (), s32[]{:S(2)}) async-start(), calls=%async_computation.1 | async-start | bytes 2621440 | tf_op jit(solution)/shard_map/all_gather | solution.py:503
  76.4 24.7 %collective-permute-start.8 = (bf16[33,128,128]{2,1,0:T(8,128)(2,1)S(1)}, bf16[33,128,128]{2,1,0:T(8,128)(2,1)}, u32[]{:S(2)}, u32[]{:S(2)}) collective-permute-start(bf16[33,128,128]{2,1,0:T(8,128)(2,1)S(1)} %collective-permute-done.4.end_a), channel_id=1, source_target_pairs={{0,16},{16,0},{1,17},{17,1},{2,18},{18,2},{3,19},{19,3},{4,20},{20... | collective-permute-start | bytes 3244040 | tf_op jit(solution)/shard_map/ppermute | solution.py:484
  77.0 24.1 %collective-permute-start.6 = (bf16[32,128,128]{2,1,0:T(8,128)(2,1)}, bf16[32,128,128]{2,1,0:T(8,128)(2,1)}, u32[]{:S(2)}, u32[]{:S(2)}) collective-permute-start(bf16[32,128,128]{2,1,0:T(8,128)(2,1)} %get-tuple-element.54), channel_id=1, source_target_pairs={{0,4},{12,8},{1,5},{13,9},{2,6},{14,10},{3,7},{15,11},{16,20},{28,... | collective-permute-start | bytes 3145736 | tf_op jit(solution)/shard_map/ppermute | solution.py:482
  82.2 18.9 %collective-permute-start.7 = (bf16[512,1024]{1,0:T(8,128)(2,1)}, bf16[512,1024]{1,0:T(8,128)(2,1)}, u32[]{:S(2)}, u32[]{:S(2)}) collective-permute-start(bf16[512,1024]{1,0:T(8,128)(2,1)} %pad_maximum_fusion.1), channel_id=1, source_target_pairs={{4,8},{8,4},{5,9},{9,5},{6,10},{10,6},{7,11},{11,7},{20,24},{24,20... | collective-permute-start | bytes 3145736 | tf_op jit(solution)/shard_map/ppermute | solution.py:483
  101.1 3.2 %copy-start.6 = (bf16[512,1024]{1,0:T(8,128)(2,1)S(1)}, bf16[512,1024]{1,0:T(8,128)(2,1)}, u32[]{:S(2)}) copy-start(bf16[512,1024]{1,0:T(8,128)(2,1)} %copy-done.5) | copy-start | bytes 3145732
  104.3 3.1 %collective-permute-start.9 = (bf16[2,256,1024]{2,1,0:T(8,128)(2,1)}, bf16[2,256,1024]{2,1,0:T(8,128)(2,1)}, u32[]{:S(2)}, u32[]{:S(2)}) collective-permute-start(bf16[2,256,1024]{2,1,0:T(8,128)(2,1)} %get-tuple-element.63), channel_id=1, source_target_pairs={{0,1},{1,0},{2,3},{3,2},{4,5},{5,4},{6,7},{7,6},{8,9},{9,8},{10,11... | collective-permute-start | bytes 3145736 | tf_op jit(solution)/shard_map/ppermute | solution.py:496
  104.3 11.9 %collective-permute-start.10 = (bf16[512,1024]{1,0:T(8,128)(2,1)S(1)}, bf16[512,1024]{1,0:T(8,128)(2,1)S(1)}, u32[]{:S(2)}, u32[]{:S(2)}) collective-permute-start(bf16[512,1024]{1,0:T(8,128)(2,1)S(1)} %copy-done.6), channel_id=1, source_target_pairs={{4,8},{8,4},{5,9},{9,5},{6,10},{10,6},{7,11},{11,7},{20,24},{24,20... | collective-permute-start | bytes 3145736 | tf_op jit(solution)/shard_map/ppermute | solution.py:491
  105.1 41.1 %collective-permute-start.11 = (bf16[512,1024]{1,0:T(8,128)(2,1)}, bf16[512,1024]{1,0:T(8,128)(2,1)S(1)}, u32[]{:S(2)}, u32[]{:S(2)}) collective-permute-start(bf16[512,1024]{1,0:T(8,128)(2,1)} %collective-permute-done.7), channel_id=1, source_target_pairs={{4,0},{8,12},{5,1},{9,13},{6,2},{10,14},{7,3},{11,15},{20,16},{24,... | collective-permute-start | bytes 3145736 | tf_op jit(solution)/shard_map/ppermute | solution.py:492
  110.0 36.1 %collective-permute-start.12 = (bf16[256,1024]{1,0:T(8,128)(2,1)}, bf16[256,1024]{1,0:T(8,128)(2,1)S(1)}, u32[]{:S(2)}, u32[]{:S(2)}) collective-permute-start(bf16[256,1024]{1,0:T(8,128)(2,1)} %get-tuple-element.67), channel_id=1, source_target_pairs={{0,2},{2,0},{1,3},{3,1},{4,6},{6,4},{5,7},{7,5},{8,10},{10,8},{9,1... | collective-permute-start | bytes 1572872 | tf_op jit(solution)/shard_map/ppermute | solution.py:497
  146.2 2.5 copy-start.9
  148.7 7.8 %copy-start.8 = (bf16[256,1024]{1,0:T(8,128)(2,1)S(1)}, bf16[256,1024]{1,0:T(8,128)(2,1)}, u32[]{:S(2)}) copy-start(bf16[256,1024]{1,0:T(8,128)(2,1)} %get-tuple-element.64) | copy-start | bytes 1572868
  148.7 7.8 %copy-start.10 = (bf16[256,1024]{1,0:T(8,128)(2,1)S(1)}, bf16[256,1024]{1,0:T(8,128)(2,1)}, u32[]{:S(2)}) copy-start(bf16[256,1024]{1,0:T(8,128)(2,1)} %copy-done.9) | copy-start | bytes 1572868
  148.7 90.3 %all-gather.11.cloned.1.call-start = ((), (), s32[]{:S(2)}) async-start(), calls=%async_computation.2 | async-start | bytes 2621440 | tf_op jit(solution)/shard_map/all_gather | solution.py:512
  148.7 2.9 %collective-permute-start.14 = (bf16[2,256,1024]{2,1,0:T(8,128)(2,1)}, bf16[2,256,1024]{2,1,0:T(8,128)(2,1)S(1)}, u32[]{:S(2)}, u32[]{:S(2)}) collective-permute-start(bf16[2,256,1024]{2,1,0:T(8,128)(2,1)} %get-tuple-element.73), channel_id=1, source_target_pairs={{0,1},{1,0},{2,3},{3,2},{4,5},{5,4},{6,7},{7,6},{8,9},{9,8},{10,11... | collective-permute-start | bytes 3145736 | tf_op jit(solution)/shard_map/ppermute | solution.py:506
  149.9 32.0 %collective-permute-start.16 = (bf16[256,1024]{1,0:T(8,128)(2,1)}, bf16[256,1024]{1,0:T(8,128)(2,1)}, u32[]{:S(2)}, u32[]{:S(2)}) collective-permute-start(bf16[256,1024]{1,0:T(8,128)(2,1)} %get-tuple-element.98), channel_id=1, source_target_pairs={{4,0},{8,12},{5,1},{9,13},{6,2},{10,14},{7,3},{11,15},{20,16},{24,... | collective-permute-start | bytes 1572872 | tf_op jit(solution)/shard_map/ppermute | solution.py:505
  151.7 1.0 copy-start.7
  155.4 25.2 %collective-permute-start.15 = (bf16[256,1024]{1,0:T(8,128)(2,1)}, bf16[256,1024]{1,0:T(8,128)(2,1)}, u32[]{:S(2)}, u32[]{:S(2)}) collective-permute-start(bf16[256,1024]{1,0:T(8,128)(2,1)} %get-tuple-element.75), channel_id=1, source_target_pairs={{0,2},{2,0},{1,3},{3,1},{4,6},{6,4},{5,7},{7,5},{8,10},{10,8},{9,1... | collective-permute-start | bytes 1572872 | tf_op jit(solution)/shard_map/ppermute | solution.py:507
  156.7 25.2 %collective-permute-start.13 = (bf16[256,1024]{1,0:T(8,128)(2,1)S(1)}, bf16[256,1024]{1,0:T(8,128)(2,1)S(1)}, u32[]{:S(2)}, u32[]{:S(2)}) collective-permute-start(bf16[256,1024]{1,0:T(8,128)(2,1)S(1)} %add.41), channel_id=1, source_target_pairs={{4,0},{8,12},{5,1},{9,13},{6,2},{10,14},{7,3},{11,15},{20,16},{24,... | collective-permute-start | bytes 1572872 | tf_op jit(solution)/shard_map/ppermute | solution.py:502
  158.0 30.8 %collective-permute-start.21 = (bf16[256,1024]{1,0:T(8,128)(2,1)}, bf16[256,1024]{1,0:T(8,128)(2,1)S(1)}, u32[]{:S(2)}, u32[]{:S(2)}) collective-permute-start(bf16[256,1024]{1,0:T(8,128)(2,1)} %get-tuple-element.97), channel_id=1, source_target_pairs={{4,0},{8,12},{5,1},{9,13},{6,2},{10,14},{7,3},{11,15},{20,16},{24,... | collective-permute-start | bytes 1572872 | tf_op jit(solution)/shard_map/ppermute | solution.py:516
  159.3 21.3 %copy-start.12 = (bf16[256,1024]{1,0:T(8,128)(2,1)S(1)}, bf16[256,1024]{1,0:T(8,128)(2,1)}, u32[]{:S(2)}) copy-start(bf16[256,1024]{1,0:T(8,128)(2,1)} %get-tuple-element.74) | copy-start | bytes 1572868
  181.9 10.5 %copy-start.16 = (bf16[256,1024]{1,0:T(8,128)(2,1)S(1)}, bf16[256,1024]{1,0:T(8,128)(2,1)}, u32[]{:S(2)}) copy-start(bf16[256,1024]{1,0:T(8,128)(2,1)} %get-tuple-element.80) | copy-start | bytes 1572868
  191.1 22.4 %copy-start.1 = (bf16[256,1024]{1,0:T(8,128)(2,1)}, bf16[256,1024]{1,0:T(8,128)(2,1)S(1)}, u32[]{:S(2)}) copy-start(bf16[256,1024]{1,0:T(8,128)(2,1)S(1)} %broadcast_select_fusion.own) | copy-start | bytes 1572868
  191.1 22.5 %copy-start.15 = (bf16[256,1024]{1,0:T(8,128)(2,1)S(1)}, bf16[256,1024]{1,0:T(8,128)(2,1)}, u32[]{:S(2)}) copy-start(bf16[256,1024]{1,0:T(8,128)(2,1)} %get-tuple-element.79) | copy-start | bytes 1572868
  191.1 22.3 %collective-permute-start.18 = (bf16[256,1024]{1,0:T(8,128)(2,1)S(1)}, bf16[256,1024]{1,0:T(8,128)(2,1)S(1)}, u32[]{:S(2)}, u32[]{:S(2)}) collective-permute-start(bf16[256,1024]{1,0:T(8,128)(2,1)S(1)} %broadcast_select_fusion.own), channel_id=1, source_target_pairs={{0,2},{2,0},{1,3},{3,1},{4,6},{6,4},{5,7},{7,5},{8,10},{10,8},{9,1... | collective-permute-start | bytes 1572872 | tf_op jit(solution)/shard_map/ppermute | solution.py:514
  192.3 21.1 %collective-permute-start.19 = (bf16[256,1024]{1,0:T(8,128)(2,1)S(1)}, bf16[256,1024]{1,0:T(8,128)(2,1)S(1)}, u32[]{:S(2)}, u32[]{:S(2)}) collective-permute-start(bf16[256,1024]{1,0:T(8,128)(2,1)S(1)} %broadcast_select_fusion.own), channel_id=1, source_target_pairs={{0,1},{1,0},{2,3},{3,2},{4,5},{5,4},{6,7},{7,6},{8,9},{9,8},{10,11... | collective-permute-start | bytes 1572872 | tf_op jit(solution)/shard_map/ppermute | solution.py:514
  192.3 21.2 %collective-permute-start.17 = (bf16[256,1024]{1,0:T(8,128)(2,1)S(1)}, bf16[256,1024]{1,0:T(8,128)(2,1)S(1)}, u32[]{:S(2)}, u32[]{:S(2)}) collective-permute-start(bf16[256,1024]{1,0:T(8,128)(2,1)S(1)} %copy-done.16), channel_id=1, source_target_pairs={{4,0},{8,12},{5,1},{9,13},{6,2},{10,14},{7,3},{11,15},{20,16},{24,... | collective-permute-start | bytes 1572872 | tf_op jit(solution)/shard_map/ppermute | solution.py:515
  213.4 2.0 copy-start.11
  213.5 2.0 copy-start.13
  213.5 2.0 collective-permute-start.20
  215.5 0.8 copy-start.14
Sparse Core Ops, SparseCore 0:
  76.5 21.6 all-gather.6
  148.8 32.9 all-gather.8
  191.1 26.2 all-gather.10

commit v5 on v4

--- a/solution.py
+++ b/solution.py
@@ -23,7 +23,7 @@
     total = (depth // size) * cols_n
     weight[...] = jnp.zeros_like(weight)
 
-    @pl.loop(0, slots)
+    @pl.loop(0, slots, unroll=4)
     def place(s):
         b = ids[s]
 
@@ -42,7 +42,7 @@
             tokens[...], weight[:, pl.ds(c, step)], preferred_element_type=jnp.float32
         ).astype(proj.dtype)
 
-    @pl.loop(0, depth // step)
+    @pl.loop(0, depth // step, unroll=4)
     def backward(n):
         r = pl.multiple_of(n * step, step)
         back[:, pl.ds(r, step)] = lax.dot_general(
@@ -141,7 +141,7 @@
     cols_n = width // size
     total = (depth // size) * cols_n
 
-    @pl.loop(0, slots)
+    @pl.loop(0, slots, unroll=4)
     def place(s):
         b = ids[first + s]
 
@@ -181,35 +181,36 @@
     )(place_of, *ids, *pieces)
 
 
-def backward_rows(place_of, upstream, weight, keep, give):
+def backward_rows(place_of, sources, weight, keep, give):
     depth = weight.shape[0]
     step = 256
-    per_part = keep.shape[2] // step
+    per_part = keep.shape[3] // step
     at_replica = place_of[3]
 
-    @pl.loop(0, depth // step)
+    @pl.loop(0, depth // step, unroll=2)
     def backward(n):
         r = pl.multiple_of(n * step, step)
         part = n // per_part
         at = pl.multiple_of((n % per_part) * step, step)
-        result = lax.dot_general(
-            upstream[...],
-            weight[pl.ds(r, step), :],
-            (((1,), (1,)), ((), ())),
-            preferred_element_type=jnp.float32,
-        ).astype(keep.dtype)
-
-        @pl.when(part % 2 == at_replica)
-        def mine():
-            keep[part // 2, :, pl.ds(at, step)] = result
-
-        @pl.when(part % 2 != at_replica)
-        def theirs():
-            give[part // 2, :, pl.ds(at, step)] = result
+        for k, source in enumerate(sources):
+            result = lax.dot_general(
+                source[...],
+                weight[pl.ds(r, step), :],
+                (((1,), (1,)), ((), ())),
+                preferred_element_type=jnp.float32,
+            ).astype(keep.dtype)
+
+            @pl.when(part % 2 == at_replica)
+            def mine():
+                keep[k, part // 2, :, pl.ds(at, step)] = result
+
+            @pl.when(part % 2 != at_replica)
+            def theirs():
+                give[k, part // 2, :, pl.ds(at, step)] = result
 
 
 def finish_kernel(
-    place_of, ids_1, ids_3, partial, near_b, end_b, upstream, weight, keep, give,
+    place_of, ids_1, ids_3, partial, near_b, end_b, end_upstream, upstream, weight, keep, give,
     held, sem_in, sem_out,
 ):
     half_slots = near_b.shape[0]
@@ -224,18 +225,18 @@
         place_blocks(ids_3, other, end_b, held, half_slots)
         store = pltpu.make_async_copy(held, weight, sem_out)
         store.start()
-        backward_rows(place_of, upstream, held, keep, give)
+        backward_rows(place_of, (end_upstream, upstream), held, keep, give)
         store.wait()
 
 
-def finish_weight(place_of, ids_1, ids_3, partial, near_b, end_b, upstream):
+def finish_weight(place_of, ids_1, ids_3, partial, near_b, end_b, end_upstream, upstream):
     depth, width = partial.shape
     rows = upstream.shape[0]
-    half = jax.ShapeDtypeStruct((2, rows, depth // 4), jnp.bfloat16)
+    half = jax.ShapeDtypeStruct((2, 2, rows, depth // 4), jnp.bfloat16)
     return pl.pallas_call(
         finish_kernel,
         out_shape=(jax.ShapeDtypeStruct((depth, width), jnp.bfloat16), half, half),
-        in_specs=[whole(pltpu.SMEM)] * 3 + [whole(pl.ANY)] + [whole()] * 3,
+        in_specs=[whole(pltpu.SMEM)] * 3 + [whole(pl.ANY)] + [whole()] * 4,
         out_specs=(whole(pl.ANY), whole(), whole()),
         scratch_shapes=[
             pltpu.VMEM((depth, width), jnp.bfloat16),
@@ -244,37 +245,12 @@
         ],
         compiler_params=pltpu.CompilerParams(vmem_limit_bytes=VMEM_LIMIT),
         cost_estimate=pl.CostEstimate(
-            flops=2 * rows * depth * width,
-            bytes_accessed=depth * width * 4 + rows * (depth + width) * 2,
+            flops=4 * rows * depth * width,
+            bytes_accessed=depth * width * 4 + rows * (depth + width) * 4,
             transcendentals=0,
         ),
         name="finish_weight",
-    )(place_of, ids_1, ids_3, partial, near_b, end_b, upstream)
-
-
-def backward_kernel(place_of, weight, upstream, keep, give):
-    @pl.when(place_of[0] == 1)
-    def work():
-        backward_rows(place_of, upstream, weight, keep, give)
-
-
-def project_back(place_of, weight, upstream):
-    depth, width = weight.shape
-    rows = upstream.shape[0]
-    half = jax.ShapeDtypeStruct((2, rows, depth // 4), jnp.bfloat16)
-    return pl.pallas_call(
-        backward_kernel,
-        out_shape=(half, half),
-        in_specs=[whole(pltpu.SMEM)] + [whole()] * 2,
-        out_specs=(whole(),) * 2,
-        compiler_params=pltpu.CompilerParams(vmem_limit_bytes=VMEM_LIMIT),
-        cost_estimate=pl.CostEstimate(
-            flops=2 * rows * depth * width,
-            bytes_accessed=depth * width * 2 + rows * (depth + width) * 2,
-            transcendentals=0,
-        ),
-        name="project_back",
-    )(place_of, weight, upstream)
+    )(place_of, ids_1, ids_3, partial, near_b, end_b, end_upstream, upstream)
 
 
 def forward_kernel(place_of, weight, tokens, end_tokens, proj, end_proj):
@@ -284,7 +260,7 @@
 
     @pl.when(place_of[0] == 1)
     def work():
-        @pl.loop(0, width // step)
+        @pl.loop(0, width // step, unroll=2)
         def forward(n):
             c = pl.multiple_of(n * step, step)
             acc = jnp.zeros((rows, step), jnp.float32)
@@ -319,19 +295,21 @@
     )(place_of, weight, tokens, end_tokens)
 
 
-def split_kernel(place_of, keep, got, own, give):
+def split_kernel(place_of, keep, got, *outs):
     x = place_of[2]
-    for ref, at in ((own, x), (give, 1 - x)):
-        ref[...] = (keep[at].astype(jnp.float32) + got[at].astype(jnp.float32)).astype(ref.dtype)
+    for n, ref in enumerate(outs):
+        k, at = n // 2, (x, 1 - x)[n % 2]
+        total = keep[k, at].astype(jnp.float32) + got[k, at].astype(jnp.float32)
+        ref[...] = total.astype(ref.dtype)
 
 
 def add_split(place_of, keep, got):
-    out = jax.ShapeDtypeStruct(keep.shape[1:], keep.dtype)
+    out = jax.ShapeDtypeStruct(keep.shape[2:], keep.dtype)
     return pl.pallas_call(
         split_kernel,
-        out_shape=(out, out),
+        out_shape=(out,) * 4,
         in_specs=[whole(pltpu.SMEM), whole(), whole()],
-        out_specs=(whole(), whole()),
+        out_specs=(whole(),) * 4,
         compiler_params=pltpu.CompilerParams(vmem_limit_bytes=VMEM_LIMIT),
         cost_estimate=pl.CostEstimate(
             flops=keep.size, bytes_accessed=keep.size * 6, transcendentals=0
@@ -376,12 +354,12 @@
     per_part = pairs[0][0].shape[-1] // size
     total = rows_n * cols_n
 
-    @pl.loop(0, slots)
-    def one(s):
-        b = ids[s]
-
-        @pl.when(b < total)
-        def fill():
+    group = math.gcd(slots, 8)
+
+    @pl.loop(0, slots // group)
+    def some(g):
+        for s in [g * group + j for j in range(group)]:
+            b = jnp.minimum(ids[s], total - 1)
             row = b // cols_n
             part = row // per_part
             r = pl.multiple_of((row % per_part) * size, size)
@@ -394,11 +372,7 @@
                     (((0,), (0,)), ((), ())),
                     preferred_element_type=jnp.float32,
                 )
-            grads[s] = acc.astype(grads.dtype)
-
-        @pl.when(b >= total)
-        def clear():
-            grads[s] = jnp.zeros((size, size), grads.dtype)
+            grads[s] = jnp.where(ids[s] < total, acc, 0.0).astype(grads.dtype)
 
 
 def line_grads(ids, start, pairs, size, out_dtype):
@@ -428,6 +402,7 @@
 
 INWARD = ((0, 1), (3, 2))
 OUTWARD = ((1, 0), (2, 3))
+PAIRS = INWARD + OUTWARD
 MIDDLE = ((1, 2), (2, 1))
 SWAP = ((0, 1), (1, 0))
 
@@ -466,57 +441,53 @@
 
     near_a = along(mine, perm=INWARD)
     far_a = along(mine, perm=MIDDLE)
-    both_1o = along(both, perm=OUTWARD)
     grads = line_grads(block_ids, None, ((tokens, upstream),), size, jnp.float32)
-    near_a, far_a, both_1o, grads, both_s, other = stage(
-        (near_a, far_a, both_1o, grads, both, other)
-    )
-
-    both_1i = along(both_s, perm=INWARD)
+    near_a, far_a, grads, both, other = stage((near_a, far_a, grads, both, other))
+
     end_a = along(near_a, perm=MIDDLE)
+    both_1 = along(both, perm=PAIRS)
     far_b = across(far_a)
-    both_1i, end_a, far_b, both_s, other = stage((both_1i, end_a, far_b, both_s, other))
-    tokens_1 = lax.all_gather(both_1i[:rows] + both_1o[:rows], INNER)
-    upstream_1 = both_1i[rows:] + both_1o[rows:]
+    both_1, end_a, far_b, both, other = stage((both_1, end_a, far_b, both, other))
+    tokens_1 = lax.all_gather(both_1[:rows], INNER)
+    upstream_1 = both_1[rows:]
 
     near_b = along(other, perm=INWARD)
-    both_2m = along(both_s, perm=MIDDLE)
+    both_2m = along(both, perm=MIDDLE)
     end_b = across(end_a)
     ids_1, ids_2, ids_3 = (ids_of(piece, slots) for piece in (near_a, far_a, end_a))
     partial = place_first(
         place_of, (block_ids, ids_1, ids_2, ids_3), (blocks, near_a, far_a, far_b, end_a), depth, width
     )
-    near_b, both_2m, end_b, partial, both_1i = stage((near_b, both_2m, end_b, partial, both_1i))
-
-    both_3m = along(both_1i, perm=MIDDLE)
+    near_b, both_2m, end_b, partial, both_1, tokens_1 = stage(
+        (near_b, both_2m, end_b, partial, both_1, tokens_1)
+    )
+
+    both_3m = along(both_1, perm=MIDDLE)
     both_2o = along(both_2m, perm=OUTWARD)
     weight, keep, give = finish_weight(
-        place_of, ids_1, ids_3, partial, near_b, end_b, upstream_1
+        place_of, ids_1, ids_3, partial, near_b, end_b, upstream_1, upstream
     )
-    end_keep, end_give = add_split(place_of, keep, cores(give))
+    end_keep, end_give, own_keep, own_give = add_split(place_of, keep, cores(give))
     end_got = sideways(end_give)
-    own_keep, own_give = project_back(place_of, weight, upstream)
-    both_3m, both_2o, end_got, own_keep, own_give = stage(
-        (both_3m, both_2o, end_got, own_keep, own_give)
+    proj, end_proj = project_forward(place_of, weight, tokens, tokens_1)
+    end_got, own_give, both_3m, both_2o, proj, end_proj = stage(
+        (end_got, own_give, both_3m, both_2o, proj, end_proj)
     )
     sum_out = along(end_keep + end_got, perm=OUTWARD)
+    own_got = sideways(own_give)
+    token_3o = along(both_3m[:rows], perm=OUTWARD)
     tokens_2 = lax.all_gather(both_2m[:rows] + both_2o[:rows], INNER)
     upstream_2 = both_2m[rows:] + both_2o[rows:]
-    token_3o = along(both_3m[:rows], perm=OUTWARD)
-    own_keep, own_give = add_split(place_of, own_keep, cores(own_give))
-    own_sum = own_keep + sideways(own_give)
-    proj, end_proj = project_forward(place_of, weight, tokens, tokens_1)
-    sum_out, own_sum, token_3o, proj, end_proj = stage(
-        (sum_out, own_sum, token_3o, proj, end_proj)
-    )
+    grads = line_grads(block_ids, grads, ((tokens_1, upstream_1),), size, jnp.float32)
+    sum_out, own_got, token_3o, grads = stage((sum_out, own_got, token_3o, grads))
+    own_sum = own_keep + own_got
     tokens_3 = lax.all_gather(both_3m[:rows] + token_3o, INNER)
     quarter = jnp.where(middle, own_sum, sum_out)
     by_tensor, by_core = sideways(quarter), cores(quarter)
     proj_out = along(end_proj, perm=OUTWARD)
     upstream_3o = along(both_3m[rows:], perm=OUTWARD)
     upstream_3 = both_3m[rows:] + upstream_3o
-    grads = line_grads(block_ids, grads, ((tokens_1, upstream_1),), size, jnp.float32)
-    by_tensor, by_core, grads = stage((by_tensor, by_core, grads))
+    by_tensor, by_core = stage((by_tensor, by_core))
     by_both = cores(by_tensor)
     projected = jnp.where(middle, proj, proj_out)
     grads = line_grads(block_ids, grads, ((tokens_2, upstream_2),), size, jnp.float32)

time: 266 us -> 244 us (0.917)
  Pallas kernels: 105 us -> 56.2 us
  waiting for transfers between devices: 92.1 us -> 121 us
  other arithmetic: 13.2 us -> 9.64 us
    pallas_call x4, Pallas kernels: 76.9 us -> 33.5 us  [line_grads(): pl.pallas_call(functools.partial(line_grads_kernel, len(pairs), start is...]
    ppermute x7 -> x5, waiting for transfers between devices: 45.2 us -> 24.3 us  [the longest x1 21.9 us: line_body(): both_1 = along(both, perm=PAIRS)]
    ppermute x1, waiting for transfers between devices: 0.01 us -> 14.8 us  [line_body(): near_a = along(mine, perm=INWARD)]
    ppermute x2, waiting for transfers between devices: 0.01 us -> 14.7 us  [line_body(): by_tensor, by_core = (sideways(quarter), cores(quarter))]
    ppermute x1, waiting for transfers between devices: 0.01 us -> 11.2 us  [line_body(): token_3o = along(both_3m[:rows], perm=OUTWARD)]
    pallas_call x3 -> x1, Pallas kernels: 10.2 us -> 4.01 us  [add_split(): pl.pallas_call(split_kernel, out_shape=(out,) * 4, in_specs=[whole(pltpu....]
    ppermute x1, waiting for transfers between devices: 29.9 us -> 34 us  [line_body(): both_2o = along(both_2m, perm=OUTWARD)]
    add x2 -> x0, other arithmetic: 3.58 us -> none  [the longest x1 2.32 us: line_body(): tokens_1 = lax.all_gather(both_1i[:rows] + both_1o[:rows], INNER)]
  transfers between devices with their start and end apart: 25 -> 23, of which waited for: 9 -> 11; matrix products, arithmetic and copies ran while one was open for 4% -> 3% of each run, Pallas kernels for 32% -> 18%
where the time goes in v5:
time: 244 us; the launch traced here: 243 us
  waiting for transfers between devices  121 us (50%)
  Pallas kernels  56.2 us (23%)
  starting transfers between devices  33.3 us (14%)
  between operations  14 us (6%)
  other arithmetic  9.64 us (4%)
  local copies, waits for them, and re-layouts  9.17 us (4%)
    ppermute x1, waiting for transfers between devices, line_body(): both_2o = along(both_2m, perm=OUTWARD)  34 us
    pallas_call x4, Pallas kernels, line_grads(): pl.pallas_call(functools.partial(line_grads_kernel, len(pairs), start is...  33.5 us
    ppermute x1, waiting for transfers between devices, line_body(): both_1 = along(both, perm=PAIRS)  21.9 us
    ppermute x1, waiting for transfers between devices, line_body(): near_a = along(mine, perm=INWARD)  14.8 us
    ppermute x2, waiting for transfers between devices, line_body(): by_tensor, by_core = (sideways(quarter), cores(quarter))  14.7 us
    ppermute x1, waiting for transfers between devices, line_body(): token_3o = along(both_3m[:rows], perm=OUTWARD)  11.2 us
    ppermute x1, waiting for transfers between devices, line_body(): upstream_3o = along(both_3m[rows:], perm=OUTWARD)  10 us
    ppermute x1, waiting for transfers between devices, line_body(): near_b = along(other, perm=INWARD)  9.61 us
  transfers between devices with their start and end apart: 23, of which 11 were waited for; matrix products, arithmetic and copies ran while one was open for 3% of the time, Pallas kernels for 18%

profile of v5, /device:TPU:0, one launch (start us, length us, event | category | flops | bytes accessed | tf_op | source)
XLA Modules:
  0.0 243.1 jit_solution(7073983091450063509)
XLA Ops:
  7.2 0.0 all-gather.7.cloned.1.call-start
  7.2 0.7 convert_element_type.26
  7.9 0.1 convert_element_type.27
  8.0 2.7 %constant_dynamic-slice_fusion.1 = (bf16[32,128,128]{2,1,0:T(8,128)(2,1)}, bf16[32,128,128]{2,1,0:T(8,128)(2,1)S(1)}) fusion(bf16[64,128,128]{2,1,0:T(8,128)(2,1)} %own.1, s32[]{:T(128)S(6)} %select_n.23, s32[]{:T(128)S(6)} %select_n.22), kind=kLoop, calls=%fused_computation.7 | loop fusion | bytes 4194312 | tf_op jit(solution)/shard_map/dynamic_slice | solution.py:436
  10.7 0.1 pad_maximum_fusion
  10.8 1.1 constant_dynamic-slice_fusion
  11.9 1.1 pad_maximum_fusion.1
  13.0 5.0 %collective-permute-start = (bf16[33,128,128]{2,1,0:T(8,128)(2,1)S(1)}, bf16[33,128,128]{2,1,0:T(8,128)(2,1)S(1)}, u32[]{:S(2)}, u32[]{:S(2)}) collective-permute-start(bf16[33,128,128]{2,1,0:T(8,128)(2,1)S(1)} %pad_maximum_fusion), channel_id=1, source_target_pairs={{0,4},{12,8},{1,5},{13,9},{2,6},{14,10},{3,7},{15,11},{16,20},{28,... | collective-permute-start | bytes 3244040 | tf_op jit(solution)/shard_map/ppermute | solution.py:442
  18.0 0.7 collective-permute-start.1
  18.8 7.5 %line_grads.4.refs_0_ = f32[64,128,128]{2,1,0:T(8,128)} custom-call(s32[64]{0:T(128)} %ids.7, bf16[256,4096]{1,0:T(8,128)(2,1)} %tokens.1, bf16[256,1024]{1,0:T(8,128)(2,1)} %upstream.1), custom_call_target="tpu_custom_call" | custom-call | flops 1073741824 | bytes 6815744 | tf_op jit(solution)/shard_map/line_grads/pallas_call | solution.py:383
  26.2 14.8 %collective-permute-done.near_a = bf16[33,128,128]{2,1,0:T(8,128)(2,1)S(1)} collective-permute-done((bf16[33,128,128]{2,1,0:T(8,128)(2,1)S(1)}, bf16[33,128,128]{2,1,0:T(8,128)(2,1)S(1)}, u32[]{:S(2)}, u32[]{:S(2)}) %collective-permute-start) | collective-permute-done | bytes 1081376 | tf_op jit(solution)/shard_map/ppermute | solution.py:442
  41.1 0.7 collective-permute-start.3
  41.8 1.6 collective-permute-start.4
  43.4 6.5 %collective-permute-start.2 = (bf16[512,1024]{1,0:T(8,128)(2,1)}, bf16[512,1024]{1,0:T(8,128)(2,1)S(1)}, u32[]{:S(2)}, u32[]{:S(2)}) collective-permute-start(bf16[512,1024]{1,0:T(8,128)(2,1)} %pad_maximum_fusion.1), channel_id=1, source_target_pairs={{0,4},{12,8},{4,0},{8,12},{1,5},{13,9},{5,1},{9,13},{2,6},{14,10},... | collective-permute-start | bytes 3145736 | tf_op jit(solution)/shard_map/ppermute | solution.py:448
  49.9 21.9 %collective-permute-done.2 = bf16[512,1024]{1,0:T(8,128)(2,1)S(1)} collective-permute-done((bf16[512,1024]{1,0:T(8,128)(2,1)}, bf16[512,1024]{1,0:T(8,128)(2,1)S(1)}, u32[]{:S(2)}, u32[]{:S(2)}) %collective-permute-start.2) | collective-permute-done | bytes 1048608 | tf_op jit(solution)/shard_map/ppermute | solution.py:448
  71.8 1.0 copy-done.6
  72.9 1.1 fusion.1
  73.9 0.0 all-gather.7.cloned.1.call-update
  73.9 0.0 all-gather.9.cloned.1.call-start
  74.0 0.6 collective-permute-start.7
  74.6 4.6 %collective-permute-start.5 = (bf16[32,128,128]{2,1,0:T(8,128)(2,1)}, bf16[32,128,128]{2,1,0:T(8,128)(2,1)}, u32[]{:S(2)}, u32[]{:S(2)}) collective-permute-start(bf16[32,128,128]{2,1,0:T(8,128)(2,1)} %get-tuple-element.51), channel_id=1, source_target_pairs={{0,4},{12,8},{1,5},{13,9},{2,6},{14,10},{3,7},{15,11},{16,20},{28,... | collective-permute-start | bytes 3145736 | tf_op jit(solution)/shard_map/ppermute | solution.py:454
  79.2 1.6 collective-permute-start.6
  80.8 0.7 pad_add_fusion.place_of
  81.4 0.6 bitcast_convert_fusion
  82.0 0.6 bitcast_convert_fusion.1.ids_3
  82.6 6.2 %place_first.1.partial = bf16[4096,1024]{1,0:T(8,128)(2,1)} custom-call(s32[4]{0:T(128)} %pad_add_fusion.place_of, s32[64]{0:T(128)} %ids.7, s32[64]{0:T(128)} %get-tuple-element.94.ids_1, s32[64]{0:T(128)} %get-tuple-element.93.ids_2, s32[64]{0:T(128)} %bitcast_convert_fusion.1.ids_3, bf16[64,128,128]{2,1,0:T(8,128)(2,1)} %own.1, ...), custom_call_target="tpu_custom_call" | custom-call | bytes 16777216 | tf_op jit(solution)/shard_map/place_first/pallas_call | solution.py:171
  88.8 9.6 %collective-permute-done.5.near_b = bf16[32,128,128]{2,1,0:T(8,128)(2,1)} collective-permute-done((bf16[32,128,128]{2,1,0:T(8,128)(2,1)}, bf16[32,128,128]{2,1,0:T(8,128)(2,1)}, u32[]{:S(2)}, u32[]{:S(2)}) %collective-permute-start.5) | collective-permute-done | bytes 1048608 | tf_op jit(solution)/shard_map/ppermute | solution.py:454
  98.4 3.9 %finish_weight.1 = (bf16[4096,1024]{1,0:T(8,128)(2,1)}, bf16[2,2,256,1024]{3,2,1,0:T(8,128)(2,1)}, bf16[2,2,256,1024]{3,2,1,0:T(8,128)(2,1)}) custom-call(s32[4]{0:T(128)} %pad_add_fusion.place_of, s32[64]{0:T(128)} %get-tuple-element.94.ids_1, s32[64]{0:T(128)} %bitcast_convert_fusion.1.ids_3, bf16[4096,1024]{1,0:T(8,128)(2,1)} %place_first.1.partial, ...), custom_call_target="tpu_custom_call" | custom-call | flops 4294967296 | bytes 22020096 | tf_op jit(solution)/shard_map/finish_weight/pallas_call | solution.py:236
  102.3 0.1 collective-permute-start.8
  102.4 0.7 collective-permute-start.10
  103.1 1.3 collective-permute-start.11
  104.4 2.3 collective-permute-done.8.got
  106.7 1.3 copy-done.1
  108.1 4.0 %add_split.1 = (bf16[256,1024]{1,0:T(8,128)(2,1)}, bf16[256,1024]{1,0:T(8,128)(2,1)}, bf16[256,1024]{1,0:T(8,128)(2,1)}, bf16[256,1024]{1,0:T(8,128)(2,1)}) custom-call(s32[4]{0:T(128)} %pad_add_fusion.place_of, bf16[2,2,256,1024]{3,2,1,0:T(8,128)(2,1)} %get-tuple-element.58.keep, bf16[2,2,256,1024]{3,2,1,0:T(8,128)(2,1)} %copy-done.1), custom_call_target="tpu_custom_call" | custom-call | flops 1048576 | bytes 6291456 | tf_op jit(solution)/shard_map/add_split/pallas_call | solution.py:308
  112.1 1.5 collective-permute-start.9
  113.6 5.6 %project_forward.1 = (bf16[256,1024]{1,0:T(8,128)(2,1)}, bf16[256,1024]{1,0:T(8,128)(2,1)}) custom-call(s32[4]{0:T(128)} %pad_add_fusion.place_of, bf16[4096,1024]{1,0:T(8,128)(2,1)} %get-tuple-element.64.weight, bf16[256,4096]{1,0:T(8,128)(2,1)} %tokens.1, bf16[4,256,1024]{2,1,0:T(8,128)(2,1)} %bitcast.17), custom_call_target="tpu_custom_call" | custom-call | flops 4294967296 | bytes 13631488 | tf_op jit(solution)/shard_map/project_forward/pallas_call | solution.py:283
  119.2 34.0 %collective-permute-done.11 = bf16[512,1024]{1,0:T(8,128)(2,1)} collective-permute-done((bf16[512,1024]{1,0:T(8,128)(2,1)}, bf16[512,1024]{1,0:T(8,128)(2,1)}, u32[]{:S(2)}, u32[]{:S(2)}) %collective-permute-start.11) | collective-permute-done | bytes 1048608 | tf_op jit(solution)/shard_map/ppermute | solution.py:466
  153.2 2.6 %slice_add_fusion = (bf16[256,1024]{1,0:T(8,128)(2,1)}, bf16[256,1024]{1,0:T(8,128)(2,1)}) fusion(bf16[512,1024]{1,0:T(8,128)(2,1)} %collective-permute-done.11, bf16[512,1024]{1,0:T(8,128)(2,1)} %collective-permute-done.6), kind=kLoop, calls=%fused_computation.2 | loop fusion | flops 524288 | bytes 3145728 | tf_op jit(solution)/shard_map/add | solution.py:480
  155.8 0.0 all-gather.9.cloned.1.call-update
  155.9 0.0 all-gather.11.cloned.1.call-start
  155.9 0.2 add.34
  156.1 1.3 collective-permute-start.13
  157.4 1.0 fusion
  158.5 1.3 collective-permute-start.15
  159.7 1.6 collective-permute-start.14
  161.3 1.3 collective-permute-start.19
  162.6 9.2 %line_grads.5.refs_0_ = f32[64,128,128]{2,1,0:T(8,128)} custom-call(s32[64]{0:T(128)} %ids.7, f32[64,128,128]{2,1,0:T(8,128)} %line_grads.4.refs_0_, bf16[4,256,1024]{2,1,0:T(8,128)(2,1)} %bitcast.18, bf16[256,1024]{1,0:T(8,128)(2,1)} %get-tuple-element.91.end_upstream.refs_2_), custom_call_target="tpu_custom_call" | custom-call | flops 1073741824 | bytes 6815744 | tf_op jit(solution)/shard_map/line_grads/pallas_call | solution.py:383
  171.8 1.1 collective-permute-done.13
  172.8 11.2 %collective-permute-done.15 = bf16[256,1024]{1,0:T(8,128)(2,1)S(1)} collective-permute-done((bf16[256,1024]{1,0:T(8,128)(2,1)}, bf16[256,1024]{1,0:T(8,128)(2,1)S(1)}, u32[]{:S(2)}, u32[]{:S(2)}) %collective-permute-start.15) | collective-permute-done | bytes 524320 | tf_op jit(solution)/shard_map/ppermute | solution.py:478
  184.1 10.0 %collective-permute-done.19 = bf16[256,1024]{1,0:T(8,128)(2,1)} collective-permute-done((bf16[256,1024]{1,0:T(8,128)(2,1)}, bf16[256,1024]{1,0:T(8,128)(2,1)}, u32[]{:S(2)}, u32[]{:S(2)}) %collective-permute-start.19) | collective-permute-done | bytes 524320 | tf_op jit(solution)/shard_map/ppermute | solution.py:488
  194.1 2.1 slice_add_fusion.2
  196.2 0.0 all-gather.11.cloned.1.call-update
  196.3 0.1 add_select_fusion.own
  196.4 1.6 collective-permute-start.16
  198.0 1.3 collective-permute-start.12
  199.2 14.7 %collective-permute-done.16.by_tensor = bf16[256,1024]{1,0:T(8,128)(2,1)S(1)} collective-permute-done((bf16[256,1024]{1,0:T(8,128)(2,1)S(1)}, bf16[256,1024]{1,0:T(8,128)(2,1)S(1)}, u32[]{:S(2)}, u32[]{:S(2)}) %collective-permute-start.16) | collective-permute-done | bytes 524320 | tf_op jit(solution)/shard_map/ppermute | solution.py:486
  214.0 0.2 collective-permute-done.12
  214.2 0.9 broadcast_select_fusion
  215.1 0.8 collective-permute-done.18.by_both
  215.9 0.0 copy-start.11
  215.9 0.8 copy-done.11
  216.7 3.0 %assemble.1 = bf16[256,4096]{1,0:T(8,128)(2,1)} custom-call(s32[4]{0:T(128)} %pad_add_fusion.place_of, bf16[256,1024]{1,0:T(8,128)(2,1)} %copy-done, bf16[256,1024]{1,0:T(8,128)(2,1)} %copy-done.10, bf16[256,1024]{1,0:T(8,128)(2,1)} %copy-done.9, bf16[256,1024]{1,0:T(8,128)(2,1)} %copy-done.11), custom_call_target="tpu_custom_call" | custom-call | bytes 4194304 | tf_op jit(solution)/shard_map/assemble/pallas_call | solution.py:333
  219.7 8.8 %line_grads.6.refs_0_ = f32[64,128,128]{2,1,0:T(8,128)} custom-call(s32[64]{0:T(128)} %ids.7, f32[64,128,128]{2,1,0:T(8,128)} %line_grads.5.refs_0_, bf16[4,256,1024]{2,1,0:T(8,128)(2,1)} %bitcast.19, bf16[256,1024]{1,0:T(8,128)(2,1)} %get-tuple-element.83.refs_2_), custom_call_target="tpu_custom_call" | custom-call | flops 1073741824 | bytes 6815744 | tf_op jit(solution)/shard_map/line_grads/pallas_call | solution.py:383
  228.5 8.1 %line_grads.7 = bf16[64,128,128]{2,1,0:T(8,128)(2,1)} custom-call(s32[64]{0:T(128)} %ids.7, f32[64,128,128]{2,1,0:T(8,128)} %line_grads.6.refs_0_, bf16[4,256,1024]{2,1,0:T(8,128)(2,1)} %bitcast.16, bf16[256,1024]{1,0:T(8,128)(2,1)} %get-tuple-element.87.refs_2_), custom_call_target="tpu_custom_call" | custom-call | flops 1073741824 | bytes 6815744 | tf_op jit(solution)/shard_map/line_grads/pallas_call | solution.py:383
  (40 shorter events, 0.1 us)
Async XLA Ops:
  7.2 91.2 %all-gather.7.cloned.1.call-start = ((), (), s32[]{:S(2)}) async-start(), calls=%async_computation | async-start | bytes 2621440 | tf_op jit(solution)/shard_map/all_gather | solution.py:451
  10.7 1.2 copy-start.2
  13.0 28.0 %collective-permute-start = (bf16[33,128,128]{2,1,0:T(8,128)(2,1)S(1)}, bf16[33,128,128]{2,1,0:T(8,128)(2,1)S(1)}, u32[]{:S(2)}, u32[]{:S(2)}) collective-permute-start(bf16[33,128,128]{2,1,0:T(8,128)(2,1)S(1)} %pad_maximum_fusion), channel_id=1, source_target_pairs={{0,4},{12,8},{1,5},{13,9},{2,6},{14,10},{3,7},{15,11},{16,20},{28,... | collective-permute-start | bytes 3244040 | tf_op jit(solution)/shard_map/ppermute | solution.py:442
  18.0 23.0 %collective-permute-start.1 = (bf16[33,128,128]{2,1,0:T(8,128)(2,1)S(1)}, bf16[33,128,128]{2,1,0:T(8,128)(2,1)S(1)}, u32[]{:S(2)}, u32[]{:S(2)}) collective-permute-start(bf16[33,128,128]{2,1,0:T(8,128)(2,1)S(1)} %pad_maximum_fusion), channel_id=1, source_target_pairs={{4,8},{8,4},{5,9},{9,5},{6,10},{10,6},{7,11},{11,7},{20,24},{24,20... | collective-permute-start | bytes 3244040 | tf_op jit(solution)/shard_map/ppermute | solution.py:443
  41.0 41.5 %copy-start.3 = (bf16[33,128,128]{2,1,0:T(8,128)(2,1)}, bf16[33,128,128]{2,1,0:T(8,128)(2,1)S(1)}, u32[]{:S(2)}) copy-start(bf16[33,128,128]{2,1,0:T(8,128)(2,1)S(1)} %collective-permute-done.near_a) | copy-start | bytes 3244036
  41.1 41.5 %copy-start.4 = (bf16[33,128,128]{2,1,0:T(8,128)(2,1)}, bf16[33,128,128]{2,1,0:T(8,128)(2,1)S(1)}, u32[]{:S(2)}) copy-start(bf16[33,128,128]{2,1,0:T(8,128)(2,1)S(1)} %collective-permute-done.1.far_a) | copy-start | bytes 3244036
  41.1 30.8 %collective-permute-start.3 = (bf16[33,128,128]{2,1,0:T(8,128)(2,1)S(1)}, bf16[33,128,128]{2,1,0:T(8,128)(2,1)S(1)}, u32[]{:S(2)}, u32[]{:S(2)}) collective-permute-start(bf16[33,128,128]{2,1,0:T(8,128)(2,1)S(1)} %collective-permute-done.near_a), channel_id=1, source_target_pairs={{4,8},{8,4},{5,9},{9,5},{6,10},{10,6},{7,11},{11,7},{20,24},{24,20... | collective-permute-start | bytes 3244040 | tf_op jit(solution)/shard_map/ppermute | solution.py:447
  41.8 30.1 %collective-permute-start.4 = (bf16[33,128,128]{2,1,0:T(8,128)(2,1)S(1)}, bf16[33,128,128]{2,1,0:T(8,128)(2,1)}, u32[]{:S(2)}, u32[]{:S(2)}) collective-permute-start(bf16[33,128,128]{2,1,0:T(8,128)(2,1)S(1)} %collective-permute-done.1.far_a), channel_id=1, source_target_pairs={{0,16},{16,0},{1,17},{17,1},{2,18},{18,2},{3,19},{19,3},{4,20},{20... | collective-permute-start | bytes 3244040 | tf_op jit(solution)/shard_map/ppermute | solution.py:449
  43.4 28.5 %collective-permute-start.2 = (bf16[512,1024]{1,0:T(8,128)(2,1)}, bf16[512,1024]{1,0:T(8,128)(2,1)S(1)}, u32[]{:S(2)}, u32[]{:S(2)}) collective-permute-start(bf16[512,1024]{1,0:T(8,128)(2,1)} %pad_maximum_fusion.1), channel_id=1, source_target_pairs={{0,4},{12,8},{4,0},{8,12},{1,5},{13,9},{5,1},{9,13},{2,6},{14,10},... | collective-permute-start | bytes 3145736 | tf_op jit(solution)/shard_map/ppermute | solution.py:448
  71.8 1.0 copy-start.6
  71.8 10.8 %copy-start.5 = (bf16[33,128,128]{2,1,0:T(8,128)(2,1)}, bf16[33,128,128]{2,1,0:T(8,128)(2,1)S(1)}, u32[]{:S(2)}) copy-start(bf16[33,128,128]{2,1,0:T(8,128)(2,1)S(1)} %collective-permute-done.3.end_a) | copy-start | bytes 3244036
  73.9 145.7 %all-gather.9.cloned.1.call-start = ((), (), s32[]{:S(2)}) async-start(), calls=%async_computation.1 | async-start | bytes 2621440 | tf_op jit(solution)/shard_map/all_gather | solution.py:479
  74.0 24.4 %collective-permute-start.7 = (bf16[33,128,128]{2,1,0:T(8,128)(2,1)S(1)}, bf16[33,128,128]{2,1,0:T(8,128)(2,1)}, u32[]{:S(2)}, u32[]{:S(2)}) collective-permute-start(bf16[33,128,128]{2,1,0:T(8,128)(2,1)S(1)} %collective-permute-done.3.end_a), channel_id=1, source_target_pairs={{0,16},{16,0},{1,17},{17,1},{2,18},{18,2},{3,19},{19,3},{4,20},{20... | collective-permute-start | bytes 3244040 | tf_op jit(solution)/shard_map/ppermute | solution.py:456
  74.6 23.8 %collective-permute-start.5 = (bf16[32,128,128]{2,1,0:T(8,128)(2,1)}, bf16[32,128,128]{2,1,0:T(8,128)(2,1)}, u32[]{:S(2)}, u32[]{:S(2)}) collective-permute-start(bf16[32,128,128]{2,1,0:T(8,128)(2,1)} %get-tuple-element.51), channel_id=1, source_target_pairs={{0,4},{12,8},{1,5},{13,9},{2,6},{14,10},{3,7},{15,11},{16,20},{28,... | collective-permute-start | bytes 3145736 | tf_op jit(solution)/shard_map/ppermute | solution.py:454
  79.2 19.2 %collective-permute-start.6 = (bf16[512,1024]{1,0:T(8,128)(2,1)}, bf16[512,1024]{1,0:T(8,128)(2,1)}, u32[]{:S(2)}, u32[]{:S(2)}) collective-permute-start(bf16[512,1024]{1,0:T(8,128)(2,1)} %pad_maximum_fusion.1), channel_id=1, source_target_pairs={{4,8},{8,4},{5,9},{9,5},{6,10},{10,6},{7,11},{11,7},{20,24},{24,20... | collective-permute-start | bytes 3145736 | tf_op jit(solution)/shard_map/ppermute | solution.py:455
  102.3 4.4 %collective-permute-start.8 = (bf16[2,2,256,1024]{3,2,1,0:T(8,128)(2,1)}, bf16[2,2,256,1024]{3,2,1,0:T(8,128)(2,1)S(1)}, u32[]{:S(2)}, u32[]{:S(2)}) collective-permute-start(bf16[2,2,256,1024]{3,2,1,0:T(8,128)(2,1)} %get-tuple-element.59), channel_id=1, source_target_pairs={{0,1},{1,0},{2,3},{3,2},{4,5},{5,4},{6,7},{7,6},{8,9},{9,8},{10,11... | collective-permute-start | bytes 6291464 | tf_op jit(solution)/shard_map/ppermute | solution.py:470
  102.4 16.8 %collective-permute-start.10 = (bf16[512,1024]{1,0:T(8,128)(2,1)}, bf16[512,1024]{1,0:T(8,128)(2,1)S(1)}, u32[]{:S(2)}, u32[]{:S(2)}) collective-permute-start(bf16[512,1024]{1,0:T(8,128)(2,1)} %copy-done.6), channel_id=1, source_target_pairs={{4,8},{8,4},{5,9},{9,5},{6,10},{10,6},{7,11},{11,7},{20,24},{24,20... | collective-permute-start | bytes 3145736 | tf_op jit(solution)/shard_map/ppermute | solution.py:465
  103.1 50.1 %collective-permute-start.11 = (bf16[512,1024]{1,0:T(8,128)(2,1)}, bf16[512,1024]{1,0:T(8,128)(2,1)}, u32[]{:S(2)}, u32[]{:S(2)}) collective-permute-start(bf16[512,1024]{1,0:T(8,128)(2,1)} %collective-permute-done.6), channel_id=1, source_target_pairs={{4,0},{8,12},{5,1},{9,13},{6,2},{10,14},{7,3},{11,15},{20,16},{24,... | collective-permute-start | bytes 3145736 | tf_op jit(solution)/shard_map/ppermute | solution.py:466
  106.7 1.3 copy-start.1
  112.1 41.1 %collective-permute-start.9 = (bf16[256,1024]{1,0:T(8,128)(2,1)}, bf16[256,1024]{1,0:T(8,128)(2,1)S(1)}, u32[]{:S(2)}, u32[]{:S(2)}) collective-permute-start(bf16[256,1024]{1,0:T(8,128)(2,1)} %get-tuple-element.60), channel_id=1, source_target_pairs={{0,2},{2,0},{1,3},{3,1},{4,6},{6,4},{5,7},{7,5},{8,10},{10,8},{9,1... | collective-permute-start | bytes 1572872 | tf_op jit(solution)/shard_map/ppermute | solution.py:471
  119.2 36.8 %copy-start.8 = (bf16[256,1024]{1,0:T(8,128)(2,1)S(1)}, bf16[256,1024]{1,0:T(8,128)(2,1)}, u32[]{:S(2)}) copy-start(bf16[256,1024]{1,0:T(8,128)(2,1)} %get-tuple-element.71) | copy-start | bytes 1572868
  155.9 72.6 %all-gather.11.cloned.1.call-start = ((), (), s32[]{:S(2)}) async-start(), calls=%async_computation.2 | async-start | bytes 2621440 | tf_op jit(solution)/shard_map/all_gather | solution.py:484
  156.1 16.7 %collective-permute-start.13 = (bf16[256,1024]{1,0:T(8,128)(2,1)S(1)}, bf16[256,1024]{1,0:T(8,128)(2,1)S(1)}, u32[]{:S(2)}, u32[]{:S(2)}) collective-permute-start(bf16[256,1024]{1,0:T(8,128)(2,1)S(1)} %add.34), channel_id=1, source_target_pairs={{4,0},{8,12},{5,1},{9,13},{6,2},{10,14},{7,3},{11,15},{20,16},{24,... | collective-permute-start | bytes 1572872 | tf_op jit(solution)/shard_map/ppermute | solution.py:476
  158.5 25.6 %collective-permute-start.15 = (bf16[256,1024]{1,0:T(8,128)(2,1)}, bf16[256,1024]{1,0:T(8,128)(2,1)S(1)}, u32[]{:S(2)}, u32[]{:S(2)}) collective-permute-start(bf16[256,1024]{1,0:T(8,128)(2,1)} %get-tuple-element.90), channel_id=1, source_target_pairs={{4,0},{8,12},{5,1},{9,13},{6,2},{10,14},{7,3},{11,15},{20,16},{24,... | collective-permute-start | bytes 1572872 | tf_op jit(solution)/shard_map/ppermute | solution.py:478
  159.7 24.3 %collective-permute-start.14 = (bf16[256,1024]{1,0:T(8,128)(2,1)}, bf16[256,1024]{1,0:T(8,128)(2,1)S(1)}, u32[]{:S(2)}, u32[]{:S(2)}) collective-permute-start(bf16[256,1024]{1,0:T(8,128)(2,1)} %get-tuple-element.73), channel_id=1, source_target_pairs={{0,2},{2,0},{1,3},{3,1},{4,6},{6,4},{5,7},{7,5},{8,10},{10,8},{9,1... | collective-permute-start | bytes 1572872 | tf_op jit(solution)/shard_map/ppermute | solution.py:477
  161.3 32.8 %collective-permute-start.19 = (bf16[256,1024]{1,0:T(8,128)(2,1)}, bf16[256,1024]{1,0:T(8,128)(2,1)}, u32[]{:S(2)}, u32[]{:S(2)}) collective-permute-start(bf16[256,1024]{1,0:T(8,128)(2,1)} %get-tuple-element.89), channel_id=1, source_target_pairs={{4,0},{8,12},{5,1},{9,13},{6,2},{10,14},{7,3},{11,15},{20,16},{24,... | collective-permute-start | bytes 1572872 | tf_op jit(solution)/shard_map/ppermute | solution.py:488
  171.8 24.5 %copy-start.7 = (bf16[256,1024]{1,0:T(8,128)(2,1)S(1)}, bf16[256,1024]{1,0:T(8,128)(2,1)}, u32[]{:S(2)}) copy-start(bf16[256,1024]{1,0:T(8,128)(2,1)} %get-tuple-element.70) | copy-start | bytes 1572868
  196.2 1.7 copy-start.13
  196.2 17.9 %copy-start.12 = (bf16[256,1024]{1,0:T(8,128)(2,1)S(1)}, bf16[256,1024]{1,0:T(8,128)(2,1)}, u32[]{:S(2)}) copy-start(bf16[256,1024]{1,0:T(8,128)(2,1)} %get-tuple-element.68) | copy-start | bytes 1572868
  196.4 19.5 %copy-start = (bf16[256,1024]{1,0:T(8,128)(2,1)}, bf16[256,1024]{1,0:T(8,128)(2,1)S(1)}, u32[]{:S(2)}) copy-start(bf16[256,1024]{1,0:T(8,128)(2,1)S(1)} %add_select_fusion.own) | copy-start | bytes 1572868
  196.4 17.6 %collective-permute-start.16 = (bf16[256,1024]{1,0:T(8,128)(2,1)S(1)}, bf16[256,1024]{1,0:T(8,128)(2,1)S(1)}, u32[]{:S(2)}, u32[]{:S(2)}) collective-permute-start(bf16[256,1024]{1,0:T(8,128)(2,1)S(1)} %add_select_fusion.own), channel_id=1, source_target_pairs={{0,2},{2,0},{1,3},{3,1},{4,6},{6,4},{5,7},{7,5},{8,10},{10,8},{9,1... | collective-permute-start | bytes 1572872 | tf_op jit(solution)/shard_map/ppermute | solution.py:486
  197.9 16.0 %collective-permute-start.17 = (bf16[256,1024]{1,0:T(8,128)(2,1)S(1)}, bf16[256,1024]{1,0:T(8,128)(2,1)S(1)}, u32[]{:S(2)}, u32[]{:S(2)}) collective-permute-start(bf16[256,1024]{1,0:T(8,128)(2,1)S(1)} %add_select_fusion.own), channel_id=1, source_target_pairs={{0,1},{1,0},{2,3},{3,2},{4,5},{5,4},{6,7},{7,6},{8,9},{9,8},{10,11... | collective-permute-start | bytes 1572872 | tf_op jit(solution)/shard_map/ppermute | solution.py:486
  198.0 16.2 %collective-permute-start.12 = (bf16[256,1024]{1,0:T(8,128)(2,1)S(1)}, bf16[256,1024]{1,0:T(8,128)(2,1)S(1)}, u32[]{:S(2)}, u32[]{:S(2)}) collective-permute-start(bf16[256,1024]{1,0:T(8,128)(2,1)S(1)} %copy-done.13), channel_id=1, source_target_pairs={{4,0},{8,12},{5,1},{9,13},{6,2},{10,14},{7,3},{11,15},{20,16},{24,... | collective-permute-start | bytes 1572872 | tf_op jit(solution)/shard_map/ppermute | solution.py:487
  214.0 1.9 copy-start.9
  214.0 1.9 copy-start.10
  214.0 1.9 collective-permute-start.18
  215.9 0.8 copy-start.11
Sparse Core Ops, SparseCore 0:
  74.1 21.0 all-gather.6
  156.0 30.2 all-gather.8
  196.4 25.4 all-gather.10

commit v6 on v5

v6 whole, which is shorter than its diff:
```python
import functools
import math

import jax
import jax.numpy as jnp
from jax import lax
from jax.experimental import pallas as pl
from jax.experimental.pallas import tpu as pltpu
from jax.sharding import PartitionSpec as P

VMEM_LIMIT = 60 * 1024 * 1024
INNER = ("tensor", "replica")


def whole(space=pltpu.VMEM):
    return pl.BlockSpec(memory_space=space)


def project_kernel(ids, blocks, tokens, upstream, proj, back, weight):
    slots, size = blocks.shape[0], blocks.shape[1]
    depth, width = weight.shape
    cols_n = width // size
    total = (depth // size) * cols_n
    weight[...] = jnp.zeros_like(weight)

    @pl.loop(0, slots, unroll=4)
    def place(s):
        b = ids[s]

        @pl.when(b < total)
        def put():
            r = pl.multiple_of((b // cols_n) * size, size)
            c = pl.multiple_of((b % cols_n) * size, size)
            weight[pl.ds(r, size), pl.ds(c, size)] = blocks[s]

    step = 256

    @pl.loop(0, width // step)
    def forward(n):
        c = pl.multiple_of(n * step, step)
        proj[:, pl.ds(c, step)] = jnp.dot(
            tokens[...], weight[:, pl.ds(c, step)], preferred_element_type=jnp.float32
        ).astype(proj.dtype)

    @pl.loop(0, depth // step, unroll=4)
    def backward(n):
        r = pl.multiple_of(n * step, step)
        back[:, pl.ds(r, step)] = lax.dot_general(
            upstream[...],
            weight[pl.ds(r, step), :],
            (((1,), (1,)), ((), ())),
            preferred_element_type=jnp.float32,
        ).astype(back.dtype)


def project(ids, blocks, tokens, upstream):
    rows, depth = tokens.shape
    width = upstream.shape[1]
    return pl.pallas_call(
        project_kernel,
        out_shape=(
            jax.ShapeDtypeStruct((rows, width), jnp.bfloat16),
            jax.ShapeDtypeStruct((rows, depth), jnp.bfloat16),
        ),
        in_specs=[whole(pltpu.SMEM), whole(), whole(), whole()],
        out_specs=(whole(), whole()),
        scratch_shapes=[pltpu.VMEM((depth, width), jnp.bfloat16)],
        compiler_params=pltpu.CompilerParams(vmem_limit_bytes=VMEM_LIMIT),
        cost_estimate=pl.CostEstimate(
            flops=4 * rows * depth * width,
            bytes_accessed=blocks.size * 2 + rows * (depth + width) * 4,
            transcendentals=0,
        ),
        name="project",
    )(ids, blocks, tokens, upstream)


def block_grad_kernel(ids, tokens, upstream, grads):
    slots, size = grads.shape[0], grads.shape[1]
    parts, slabs, _, part_width = tokens.shape
    cols_n = upstream.shape[2] // size
    per_part = part_width // size
    total = parts * per_part * cols_n

    @pl.loop(0, slots)
    def one(s):
        b = ids[s]

        @pl.when(b < total)
        def fill():
            row = b // cols_n
            part = row // per_part
            r = pl.multiple_of((row % per_part) * size, size)
            c = pl.multiple_of((b % cols_n) * size, size)
            acc = jnp.zeros((size, size), jnp.float32)
            for k in range(slabs):
                acc += lax.dot_general(
                    tokens[part, k, :, pl.ds(r, size)],
                    upstream[k, :, pl.ds(c, size)],
                    (((0,), (0,)), ((), ())),
                    preferred_element_type=jnp.float32,
                )
            grads[s] = acc.astype(grads.dtype)

        @pl.when(b >= total)
        def clear():
            grads[s] = jnp.zeros((size, size), grads.dtype)


def block_grads(ids, tokens, upstream, size):
    slots = ids.shape[0]
    parts, slabs, rows, part_width = tokens.shape
    return pl.pallas_call(
        block_grad_kernel,
        out_shape=jax.ShapeDtypeStruct((slots, size, size), jnp.bfloat16),
        in_specs=[whole(pltpu.SMEM), whole(), whole()],
        out_specs=whole(),
        compiler_params=pltpu.CompilerParams(vmem_limit_bytes=VMEM_LIMIT),
        cost_estimate=pl.CostEstimate(
            flops=2 * slots * slabs * rows * size * size,
            bytes_accessed=2 * (tokens.size + upstream.size + slots * size * size),
            transcendentals=0,
        ),
        name="block_grads",
    )(ids, tokens, upstream)


def general_body(tokens, upstream, blocks, block_ids):
    size = blocks.shape[1]
    all_blocks = lax.all_gather(blocks, "dp", axis=0, tiled=True)
    all_ids = lax.all_gather(block_ids, "dp", axis=0, tiled=True)
    proj, back = project(all_ids, all_blocks, tokens, upstream)
    terms = block_grads(all_ids, tokens[None, None], upstream[None], size)
    grads = lax.psum_scatter(terms, "dp", scatter_dimension=0, tiled=True)
    return proj, lax.psum(back, INNER), grads


def place_blocks(ids, first, blocks, weight, turned, slots):
    size = blocks.shape[1]
    depth, width = turned.shape[::-1] if weight is None else weight.shape
    cols_n = width // size
    total = (depth // size) * cols_n

    @pl.loop(0, slots, unroll=4)
    def place(s):
        b = ids[first + s]

        @pl.when(b < total)
        def put():
            r = pl.multiple_of((b // cols_n) * size, size)
            c = pl.multiple_of((b % cols_n) * size, size)
            if weight is not None:
                weight[pl.ds(r, size), pl.ds(c, size)] = blocks[s]
            if turned is not None:
                turned[pl.ds(c, size), pl.ds(r, size)] = blocks[s].T


def place_kernel(
    place_of, ids_0, ids_1, ids_2, ids_3, own, near_a, far_a, far_b, end_a, weight, turned
):
    is_middle, half = place_of[0], place_of[1]
    half_slots = far_b.shape[0] - 1
    mine, other = half * half_slots, (1 - half) * half_slots

    @pl.when(is_middle == 1)
    def work():
        weight[...] = jnp.zeros_like(weight)
        turned[...] = jnp.zeros_like(turned)
        place_blocks(ids_0, 0, own, weight, turned, own.shape[0])
        place_blocks(ids_1, mine, near_a, weight, turned, half_slots)
        place_blocks(ids_2, mine, far_a, weight, turned, half_slots)
        place_blocks(ids_2, other, far_b, weight, turned, half_slots)
        place_blocks(ids_3, mine, end_a, weight, turned, half_slots)


def place_first(place_of, ids, pieces, depth, width):
    return pl.pallas_call(
        place_kernel,
        out_shape=(
            jax.ShapeDtypeStruct((depth, width), jnp.bfloat16),
            jax.ShapeDtypeStruct((width, depth), jnp.bfloat16),
        ),
        in_specs=[whole(pltpu.SMEM)] * 5 + [whole()] * 5,
        out_specs=(whole(), whole()),
        compiler_params=pltpu.CompilerParams(vmem_limit_bytes=VMEM_LIMIT),
        cost_estimate=pl.CostEstimate(
            flops=0, bytes_accessed=depth * width * 6, transcendentals=0
        ),
        name="place_first",
    )(place_of, *ids, *pieces)


def back_kernel(
    place_of, ids_1, ids_3, partial, near_b, end_b, all_upstream, upstream, keep, give,
    held, sources, sem,
):
    half_slots = near_b.shape[0]
    other = (1 - place_of[1]) * half_slots
    rows, width = upstream.shape
    depth = held.shape[1]
    step = 256
    per_part = keep.shape[3] // step

    @pl.when(place_of[0] == 1)
    def work():
        load = pltpu.make_async_copy(partial, held, sem)
        load.start()
        sources[:rows] = all_upstream[place_of[5]]
        sources[rows:] = upstream[...]
        load.wait()
        place_blocks(ids_1, other, near_b, None, held, half_slots)
        place_blocks(ids_3, other, end_b, None, held, half_slots)

        def column(part, target, x):
            @pl.loop(0, per_part, unroll=2)
            def backward(n):
                at = pl.multiple_of(n * step, step)
                result = jnp.dot(
                    sources[...],
                    held[:, pl.ds(pl.multiple_of(part * per_part * step + at, step), step)],
                    preferred_element_type=jnp.float32,
                ).astype(target.dtype)
                target[0, x, :, pl.ds(at, step)] = result[:rows]
                target[1, x, :, pl.ds(at, step)] = result[rows:]

        for x in range(2):
            column(2 * x + place_of[3], keep, x)
            column(2 * x + 1 - place_of[3], give, x)


def project_back(place_of, ids_1, ids_3, partial, near_b, end_b, all_upstream, upstream):
    width, depth = partial.shape
    rows = upstream.shape[0]
    half = jax.ShapeDtypeStruct((2, 2, rows, depth // 4), jnp.bfloat16)
    return pl.pallas_call(
        back_kernel,
        out_shape=(half, half),
        in_specs=[whole(pltpu.SMEM)] * 3 + [whole(pl.ANY)] + [whole()] * 4,
        out_specs=(whole(), whole()),
        scratch_shapes=[
            pltpu.VMEM((width, depth), jnp.bfloat16),
            pltpu.VMEM((2 * rows, width), jnp.bfloat16),
            pltpu.SemaphoreType.DMA,
        ],
        compiler_params=pltpu.CompilerParams(vmem_limit_bytes=VMEM_LIMIT),
        cost_estimate=pl.CostEstimate(
            flops=4 * rows * depth * width,
            bytes_accessed=depth * width * 2 + rows * (depth + width) * 4,
            transcendentals=0,
        ),
        name="project_back",
    )(place_of, ids_1, ids_3, partial, near_b, end_b, all_upstream, upstream)


def forward_kernel(
    place_of, ids_1, ids_3, partial, near_b, end_b, tokens, gathered, proj, end_proj, held, sem
):
    half_slots = near_b.shape[0]
    other = (1 - place_of[1]) * half_slots
    depth, width = held.shape
    parts, _, rows, part_width = gathered.shape
    step = 256

    @pl.when(place_of[0] == 1)
    def work():
        load = pltpu.make_async_copy(partial, held, sem)
        load.start()
        load.wait()
        place_blocks(ids_1, other, near_b, held, None, half_slots)
        place_blocks(ids_3, other, end_b, held, None, half_slots)

        @pl.loop(0, width // step, unroll=2)
        def forward(n):
            c = pl.multiple_of(n * step, step)
            acc = jnp.zeros((rows, step), jnp.float32)
            for q in range(parts):
                acc += jnp.dot(
                    gathered[q, place_of[4]],
                    held[q * part_width : (q + 1) * part_width, pl.ds(c, step)],
                    preferred_element_type=jnp.float32,
                )
            end_proj[:, pl.ds(c, step)] = acc.astype(end_proj.dtype)
            proj[:, pl.ds(c, step)] = jnp.dot(
                tokens[...], held[:, pl.ds(c, step)], preferred_element_type=jnp.float32
            ).astype(proj.dtype)


def project_forward(place_of, ids_1, ids_3, partial, near_b, end_b, tokens, gathered):
    depth, width = partial.shape
    rows = tokens.shape[0]
    out = jax.ShapeDtypeStruct((rows, width), jnp.bfloat16)
    return pl.pallas_call(
        forward_kernel,
        out_shape=(out, out),
        in_specs=[whole(pltpu.SMEM)] * 3 + [whole(pl.ANY)] + [whole()] * 4,
        out_specs=(whole(),) * 2,
        scratch_shapes=[pltpu.VMEM((depth, width), jnp.bfloat16), pltpu.SemaphoreType.DMA],
        compiler_params=pltpu.CompilerParams(vmem_limit_bytes=VMEM_LIMIT),
        cost_estimate=pl.CostEstimate(
            flops=4 * rows * depth * width,
            bytes_accessed=depth * width * 2 + rows * (depth + width) * 4,
            transcendentals=0,
        ),
        name="project_forward",
    )(place_of, ids_1, ids_3, partial, near_b, end_b, tokens, gathered)


def others_kernel(place_of, quarters, others):
    count = quarters.shape[0]
    for j in range(count - 1):
        others[j] = quarters[lax.rem(place_of[6] + 1 + j, count)]


def other_slabs(place_of, quarters):
    return pl.pallas_call(
        others_kernel,
        out_shape=jax.ShapeDtypeStruct((quarters.shape[0] - 1,) + quarters.shape[1:], quarters.dtype),
        in_specs=[whole(pltpu.SMEM), whole()],
        out_specs=whole(),
        compiler_params=pltpu.CompilerParams(vmem_limit_bytes=VMEM_LIMIT),
        cost_estimate=pl.CostEstimate(
            flops=0, bytes_accessed=quarters.size * 4, transcendentals=0
        ),
        name="other_slabs",
    )(place_of, quarters)


def split_kernel(place_of, keep, got, *outs):
    x = place_of[2]
    for n, ref in enumerate(outs):
        k, at = n // 2, (x, 1 - x)[n % 2]
        total = keep[k, at].astype(jnp.float32) + got[k, at].astype(jnp.float32)
        ref[...] = total.astype(ref.dtype)


def add_split(place_of, keep, got):
    out = jax.ShapeDtypeStruct(keep.shape[2:], keep.dtype)
    return pl.pallas_call(
        split_kernel,
        out_shape=(out,) * 4,
        in_specs=[whole(pltpu.SMEM), whole(), whole()],
        out_specs=(whole(),) * 4,
        compiler_params=pltpu.CompilerParams(vmem_limit_bytes=VMEM_LIMIT),
        cost_estimate=pl.CostEstimate(
            flops=keep.size, bytes_accessed=keep.size * 6, transcendentals=0
        ),
        name="add_split",
    )(place_of, keep, got)


def assemble_kernel(place_of, own, by_core, by_tensor, by_both, full):
    x, c = place_of[2], place_of[3]
    width = own.shape[1]
    for ref, xx, cc in (
        (own, x, c), (by_core, x, 1 - c), (by_tensor, 1 - x, c), (by_both, 1 - x, 1 - c)
    ):
        at = pl.multiple_of((xx * 2 + cc) * width, width)
        full[:, pl.ds(at, width)] = ref[...]


def assemble(place_of, quarters):
    rows, width = quarters[0].shape
    return pl.pallas_call(
        assemble_kernel,
        out_shape=jax.ShapeDtypeStruct((rows, 4 * width), quarters[0].dtype),
        in_specs=[whole(pltpu.SMEM)] + [whole()] * 4,
        out_specs=whole(),
        compiler_params=pltpu.CompilerParams(vmem_limit_bytes=VMEM_LIMIT),
        cost_estimate=pl.CostEstimate(
            flops=0, bytes_accessed=rows * width * 16, transcendentals=0
        ),
        name="assemble",
    )(place_of, *quarters)


def line_grads_kernel(place_of, ids, tokens, upstream, gathered, all_upstream, grads):
    slots, size = grads.shape[0], grads.shape[1]
    cols_n = upstream.shape[1] // size
    total = (tokens.shape[1] // size) * cols_n
    parts, others_n, _, part_width = gathered.shape
    per_part = part_width // size
    group = math.gcd(slots, 8)
    contract = (((0,), (0,)), ((), ()))

    @pl.loop(0, slots // group)
    def some(g):
        for s in [g * group + j for j in range(group)]:
            b = jnp.minimum(ids[s], total - 1)
            row = b // cols_n
            part = row // per_part
            at = pl.ds(pl.multiple_of((row % per_part) * size, size), size)
            c = pl.ds(pl.multiple_of((b % cols_n) * size, size), size)
            acc = lax.dot_general(
                tokens[:, pl.ds(pl.multiple_of(row * size, size), size)],
                upstream[:, c],
                contract,
                preferred_element_type=jnp.float32,
            )
            for j in range(others_n):
                slab = lax.rem(place_of[6] + 1 + j, others_n + 1)
                acc += lax.dot_general(
                    gathered[part, j, :, at],
                    all_upstream[slab, :, c],
                    contract,
                    preferred_element_type=jnp.float32,
                )
            grads[s] = jnp.where(ids[s] < total, acc, 0.0).astype(grads.dtype)


def line_grads(place_of, ids, tokens, upstream, gathered, all_upstream, size):
    slots = ids.shape[0]
    rows = upstream.shape[0]
    return pl.pallas_call(
        line_grads_kernel,
        out_shape=jax.ShapeDtypeStruct((slots, size, size), jnp.bfloat16),
        in_specs=[whole(pltpu.SMEM)] * 2 + [whole()] * 4,
        out_specs=whole(),
        compiler_params=pltpu.CompilerParams(vmem_limit_bytes=VMEM_LIMIT),
        cost_estimate=pl.CostEstimate(
            flops=8 * slots * rows * size * size,
            bytes_accessed=2 * (4 * tokens.size + 5 * upstream.size + slots * size * size),
            transcendentals=0,
        ),
        name="line_grads",
    )(place_of, ids, tokens, upstream, gathered, all_upstream)


INWARD = ((0, 1), (3, 2))
OUTWARD = ((1, 0), (2, 3))
MIDDLE = ((1, 2), (2, 1))
SWAP = ((0, 1), (1, 0))


def ids_block(block_ids, size):
    rows = size * size // block_ids.shape[0]
    return jnp.broadcast_to(block_ids, (rows, block_ids.shape[0])).reshape(1, size, size)


def ids_of(piece, slots):
    return piece[-1, 0, :slots].astype(jnp.int32)


def line_body(tokens, upstream, blocks, block_ids):
    slots, size = blocks.shape[0], blocks.shape[1]
    depth, width = tokens.shape[1], upstream.shape[1]
    half_slots = slots // 2
    part_width = depth // 4
    at_z, half = lax.axis_index("dp"), lax.axis_index("groups")
    at_tensor, at_replica = lax.axis_index("tensor"), lax.axis_index("replica")
    middle = (at_z == 1) | (at_z == 2)
    end = jnp.where(at_z == 1, 0, 3)
    place_of = jnp.stack(
        [middle.astype(jnp.int32), half, at_tensor, at_replica, (end + 3 - at_z) % 4, end, at_z]
    )
    along = functools.partial(lax.ppermute, axis_name="dp")
    across = functools.partial(lax.ppermute, axis_name="groups", perm=SWAP)
    sideways = functools.partial(lax.ppermute, axis_name="tensor", perm=SWAP)
    cores = functools.partial(lax.ppermute, axis_name="replica", perm=SWAP)
    stage = lax.optimization_barrier

    mine = lax.dynamic_slice_in_dim(blocks, half * half_slots, half_slots, 0)
    other = lax.dynamic_slice_in_dim(blocks, (1 - half) * half_slots, half_slots, 0)
    mine = jnp.concatenate([mine, ids_block(block_ids, size).astype(jnp.bfloat16)])
    part = lax.dynamic_slice_in_dim(tokens, lax.axis_index(INNER) * part_width, part_width, 1)
    all_upstream = lax.all_gather(upstream, "dp")
    quarters = lax.all_gather(part, "dp")
    mine, other = stage((mine, other))

    near_a = along(mine, perm=INWARD)
    far_a = along(mine, perm=MIDDLE)
    near_a, far_a, other = stage((near_a, far_a, other))

    end_a = along(near_a, perm=MIDDLE)
    far_b = across(far_a)
    end_a, far_b, other = stage((end_a, far_b, other))

    near_b = along(other, perm=INWARD)
    end_b = across(end_a)
    ids_1, ids_2, ids_3 = (ids_of(piece, slots) for piece in (near_a, far_a, end_a))
    partial, turned = place_first(
        place_of, (block_ids, ids_1, ids_2, ids_3), (blocks, near_a, far_a, far_b, end_a), depth, width
    )
    near_b, end_b, partial, turned = stage((near_b, end_b, partial, turned))

    gathered = lax.all_gather(other_slabs(place_of, quarters), INNER)
    last = (near_b, end_b)
    keep, give = project_back(place_of, ids_1, ids_3, turned, *last, all_upstream, upstream)
    end_keep, end_give, own_keep, own_give = add_split(place_of, keep, cores(give))
    end_got, own_give = stage((sideways(end_give), own_give))
    sum_out = along(end_keep + end_got, perm=OUTWARD)
    own_got = sideways(own_give)
    sum_out, own_got = stage((sum_out, own_got))
    quarter = jnp.where(middle, own_keep + own_got, sum_out)
    by_tensor, by_core = stage((sideways(quarter), cores(quarter)))
    by_both = cores(by_tensor)
    token_grad = assemble(place_of, (quarter, by_core, by_tensor, by_both))
    proj, end_proj = project_forward(place_of, ids_1, ids_3, partial, *last, tokens, gathered)
    projected = jnp.where(middle, proj, along(end_proj, perm=OUTWARD))
    grads = line_grads(place_of, block_ids, tokens, upstream, gathered, all_upstream, size)
    return projected, token_grad, grads


def solution(mesh):
    line = tuple(mesh.shape[a] for a in ("groups", "dp", "tensor", "replica")) == (2, 4, 2, 2)
    return jax.shard_map(
        line_body if line else general_body,
        mesh=mesh,
        in_specs=(
            P(("groups", "dp"), None),
            P(("groups", "dp"), INNER),
            P(("dp",) + INNER, None, None),
            P(("dp",) + INNER),
        ),
        out_specs=(
            P(("groups", "dp"), INNER),
            P(("groups", "dp"), None),
            P(("groups", "dp") + INNER, None, None),
        ),
        check_vma=False,
    )
```

time: 244 us -> 294 us (1.20)
  the two profiles are of different devices: /device:TPU:0 before, /device:TPU:13 now
where the time goes in v6:
time: 294 us
  waiting for transfers between devices  166 us (56%)
  Pallas kernels  74.3 us (25%)
  starting transfers between devices  25.9 us (9%)
  between operations  14 us (5%)
  local copies, waits for them, and re-layouts  7.93 us (3%)
  other arithmetic  5.67 us (2%)
    all_gather x1, waiting for transfers between devices, line_body(): quarters = lax.all_gather(part, 'dp')  44.7 us
    ppermute x1, waiting for transfers between devices, line_body(): near_a = along(mine, perm=INWARD)  40.4 us
    ppermute x1, waiting for transfers between devices, line_body(): end_a = along(near_a, perm=MIDDLE)  22.1 us
    pallas_call x1, Pallas kernels, project_back(): pl.pallas_call(back_kernel, out_shape=(half, half), in_specs=[whole(pltpu...  17.6 us
    pallas_call x1, Pallas kernels, place_first(): pl.pallas_call(place_kernel, out_shape=(jax.ShapeDtypeStruct((depth, widt...  16.7 us
    ppermute x1, waiting for transfers between devices, line_body(): far_a = along(mine, perm=MIDDLE)  16.6 us
    pallas_call x1, Pallas kernels, line_grads(): pl.pallas_call(line_grads_kernel, out_shape=jax.ShapeDtypeStruct((slots,...  15.7 us
    pallas_call x1, Pallas kernels, project_forward(): pl.pallas_call(forward_kernel, out_shape=(out, out), in_specs=[whole(pltp...  14.4 us
  transfers between devices with their start and end apart: 17, of which 11 were waited for; matrix products, arithmetic and copies ran while one was open for 2% of the time, Pallas kernels for 25%

profile of v6, /device:TPU:13, one launch (start us, length us, event | category | flops | bytes accessed | tf_op | source)
XLA Modules:
  0.0 293.6 jit_solution(837728463200481885)
XLA Ops:
  7.2 0.0 all-gather.7.cloned.1.call-start
  7.2 1.9 constant_dynamic-slice_fusion
  9.1 0.0 all-gather.7.cloned.1.call-update
  9.1 0.0 all-gather.11.cloned.1.call-start
  9.2 0.7 all-gather.11.cloned.1.call-update
  9.9 0.0 all-gather.9.cloned.1.call-start
  9.9 0.7 stack.35.place_of
  10.6 44.7 %all-gather.7.cloned.1.call-done = bf16[1024,1024]{1,0:T(8,128)(2,1)} async-done(((bf16[256,1024]{1,0:T(8,128)(2,1)}), bf16[1024,1024]{1,0:T(8,128)(2,1)}) %all-gather.7.cloned.1.call-update) | async-done | bytes 2097168 | tf_op jit(solution)/shard_map/all_gather | solution.py:466
  55.4 3.0 %other_slabs.1 = bf16[3,256,1024]{2,1,0:T(8,128)(2,1)} custom-call(s32[7]{0:T(128)} %stack.35.place_of, bf16[4,256,1024]{2,1,0:T(8,128)(2,1)} %bitcast.21), custom_call_target="tpu_custom_call" | custom-call | bytes 4194304 | tf_op jit(solution)/shard_map/other_slabs/pallas_call | solution.py:315
  58.4 0.0 all-gather.9.cloned.1.call-update
  58.4 0.0 copy-done.11
  58.4 0.1 convert_element_type.27
  58.5 0.0 copy-done
  58.5 1.1 constant_dynamic-slice_fusion.1
  59.7 0.1 pad_maximum_fusion
  59.8 1.3 collective-permute-start
  61.1 3.6 %collective-permute-start.1 = (bf16[33,128,128]{2,1,0:T(8,128)(2,1)S(1)}, bf16[33,128,128]{2,1,0:T(8,128)(2,1)S(1)}, u32[]{:S(2)}, u32[]{:S(2)}) collective-permute-start(bf16[33,128,128]{2,1,0:T(8,128)(2,1)S(1)} %pad_maximum_fusion), channel_id=1, source_target_pairs={{4,8},{8,4},{5,9},{9,5},{6,10},{10,6},{7,11},{11,7},{20,24},{24,20... | collective-permute-start | bytes 3244040 | tf_op jit(solution)/shard_map/ppermute | solution.py:470
  64.7 40.4 %collective-permute-done.near_a = bf16[33,128,128]{2,1,0:T(8,128)(2,1)S(1)} collective-permute-done((bf16[33,128,128]{2,1,0:T(8,128)(2,1)S(1)}, bf16[33,128,128]{2,1,0:T(8,128)(2,1)S(1)}, u32[]{:S(2)}, u32[]{:S(2)}) %collective-permute-start) | collective-permute-done | bytes 1081376 | tf_op jit(solution)/shard_map/ppermute | solution.py:469
  105.0 16.6 %collective-permute-done.1.far_a = bf16[33,128,128]{2,1,0:T(8,128)(2,1)S(1)} collective-permute-done((bf16[33,128,128]{2,1,0:T(8,128)(2,1)S(1)}, bf16[33,128,128]{2,1,0:T(8,128)(2,1)S(1)}, u32[]{:S(2)}, u32[]{:S(2)}) %collective-permute-start.1) | collective-permute-done | bytes 1081376 | tf_op jit(solution)/shard_map/ppermute | solution.py:470
  121.7 3.4 %collective-permute-start.2 = (bf16[33,128,128]{2,1,0:T(8,128)(2,1)S(1)}, bf16[33,128,128]{2,1,0:T(8,128)(2,1)}, u32[]{:S(2)}, u32[]{:S(2)}) collective-permute-start(bf16[33,128,128]{2,1,0:T(8,128)(2,1)S(1)} %collective-permute-done.near_a), channel_id=1, source_target_pairs={{4,8},{8,4},{5,9},{9,5},{6,10},{10,6},{7,11},{11,7},{20,24},{24,20... | collective-permute-start | bytes 3244040 | tf_op jit(solution)/shard_map/ppermute | solution.py:473
  125.1 0.4 collective-permute-start.3
  125.5 22.1 %collective-permute-done.2.end_a = bf16[33,128,128]{2,1,0:T(8,128)(2,1)} collective-permute-done((bf16[33,128,128]{2,1,0:T(8,128)(2,1)S(1)}, bf16[33,128,128]{2,1,0:T(8,128)(2,1)}, u32[]{:S(2)}, u32[]{:S(2)}) %collective-permute-start.2) | collective-permute-done | bytes 1081376 | tf_op jit(solution)/shard_map/ppermute | solution.py:473
  147.6 1.3 collective-permute-done.3.far_b
  148.9 1.0 copy-done.6
  149.9 0.4 collective-permute-start.5
  150.3 1.3 collective-permute-start.4
  151.6 0.0 copy-done.5
  151.6 0.5 bitcast_convert_fusion.ids_2
  152.1 0.6 bitcast_convert_fusion.2.ids_1
  152.7 1.3 bitcast_convert_fusion.1.ids_3
  154.0 0.0 copy-done.4
  154.0 16.7 %place_first.1 = (bf16[4096,1024]{1,0:T(8,128)(2,1)}, bf16[1024,4096]{1,0:T(8,128)(2,1)}) custom-call(s32[7]{0:T(128)} %stack.35.place_of, s32[64]{0:T(128)} %ids.1, s32[64]{0:T(128)} %bitcast_convert_fusion.2.ids_1, s32[64]{0:T(128)} %bitcast_convert_fusion.ids_2, s32[64]{0:T(128)} %bitcast_convert_fusion.1.ids_3, bf16[64,128,128]{2,1,0:T(8,128)(2,1)} %own.1, ...), custom_call_target="tpu_custom_call" | custom-call | bytes 25165824 | tf_op jit(solution)/shard_map/place_first/pallas_call | solution.py:177
  170.6 3.8 %collective-permute-done.4.near_b = bf16[32,128,128]{2,1,0:T(8,128)(2,1)} collective-permute-done((bf16[32,128,128]{2,1,0:T(8,128)(2,1)}, bf16[32,128,128]{2,1,0:T(8,128)(2,1)}, u32[]{:S(2)}, u32[]{:S(2)}) %collective-permute-start.4) | collective-permute-done | bytes 1048608 | tf_op jit(solution)/shard_map/ppermute | solution.py:477
  174.4 0.0 collective-permute-done.5.end_b
  174.4 1.0 copy-done.3
  175.4 17.6 %project_back.1 = (bf16[2,2,256,1024]{3,2,1,0:T(8,128)(2,1)}, bf16[2,2,256,1024]{3,2,1,0:T(8,128)(2,1)}) custom-call(s32[7]{0:T(128)} %stack.35.place_of, s32[64]{0:T(128)} %bitcast_convert_fusion.2.ids_1, s32[64]{0:T(128)} %bitcast_convert_fusion.1.ids_3, bf16[1024,4096]{1,0:T(8,128)(2,1)} %get-tuple-element.46.partial, ...), custom_call_target="tpu_custom_call" | custom-call | flops 4294967296 | bytes 13631488 | tf_op jit(solution)/shard_map/project_back/pallas_call | solution.py:235
  193.0 3.3 %collective-permute-start.7 = (bf16[2,2,256,1024]{3,2,1,0:T(8,128)(2,1)}, bf16[2,2,256,1024]{3,2,1,0:T(8,128)(2,1)S(1)}, u32[]{:S(2)}, u32[]{:S(2)}) collective-permute-start(bf16[2,2,256,1024]{3,2,1,0:T(8,128)(2,1)} %get-tuple-element.48), channel_id=1, source_target_pairs={{0,1},{1,0},{2,3},{3,2},{4,5},{5,4},{6,7},{7,6},{8,9},{9,8},{10,11... | collective-permute-start | bytes 6291464 | tf_op jit(solution)/shard_map/ppermute | solution.py:488
  196.3 4.0 %collective-permute-done.7.got = bf16[2,2,256,1024]{3,2,1,0:T(8,128)(2,1)S(1)} collective-permute-done((bf16[2,2,256,1024]{3,2,1,0:T(8,128)(2,1)}, bf16[2,2,256,1024]{3,2,1,0:T(8,128)(2,1)S(1)}, u32[]{:S(2)}, u32[]{:S(2)}) %collective-permute-start.7) | collective-permute-done | bytes 2097184 | tf_op jit(solution)/shard_map/ppermute | solution.py:488
  200.3 1.3 copy-done.2
  201.6 4.0 %add_split.1 = (bf16[256,1024]{1,0:T(8,128)(2,1)}, bf16[256,1024]{1,0:T(8,128)(2,1)}, bf16[256,1024]{1,0:T(8,128)(2,1)}, bf16[256,1024]{1,0:T(8,128)(2,1)}) custom-call(s32[7]{0:T(128)} %stack.35.place_of, bf16[2,2,256,1024]{3,2,1,0:T(8,128)(2,1)} %get-tuple-element.47.keep, bf16[2,2,256,1024]{3,2,1,0:T(8,128)(2,1)} %copy-done.2), custom_call_target="tpu_custom_call" | custom-call | flops 1048576 | bytes 6291456 | tf_op jit(solution)/shard_map/add_split/pallas_call | solution.py:338
  205.6 2.1 collective-permute-start.8
  207.7 12.2 %collective-permute-done.8 = bf16[256,1024]{1,0:T(8,128)(2,1)S(1)} collective-permute-done((bf16[256,1024]{1,0:T(8,128)(2,1)}, bf16[256,1024]{1,0:T(8,128)(2,1)S(1)}, u32[]{:S(2)}, u32[]{:S(2)}) %collective-permute-start.8) | collective-permute-done | bytes 524320 | tf_op jit(solution)/shard_map/ppermute | solution.py:489
  219.9 1.2 add.31
  221.2 1.3 collective-permute-start.9
  222.5 1.2 collective-permute-start.10
  223.7 9.4 %collective-permute-done.9 = bf16[256,1024]{1,0:T(8,128)(2,1)S(1)} collective-permute-done((bf16[256,1024]{1,0:T(8,128)(2,1)S(1)}, bf16[256,1024]{1,0:T(8,128)(2,1)S(1)}, u32[]{:S(2)}, u32[]{:S(2)}) %collective-permute-start.9) | collective-permute-done | bytes 524320 | tf_op jit(solution)/shard_map/ppermute | solution.py:490
  233.1 2.2 collective-permute-done.10
  235.3 1.1 add_select_fusion.own
  236.4 0.0 copy-start.1
  236.5 0.9 collective-permute-start.11
  237.3 2.4 collective-permute-start.12
  239.7 8.4 %collective-permute-done.11.by_tensor = bf16[256,1024]{1,0:T(8,128)(2,1)S(1)} collective-permute-done((bf16[256,1024]{1,0:T(8,128)(2,1)S(1)}, bf16[256,1024]{1,0:T(8,128)(2,1)S(1)}, u32[]{:S(2)}, u32[]{:S(2)}) %collective-permute-start.11) | collective-permute-done | bytes 524320 | tf_op jit(solution)/shard_map/ppermute | solution.py:494
  248.2 0.0 collective-permute-done.12.by_core
  248.2 2.8 collective-permute-start.13
  250.9 14.4 %project_forward.1 = (bf16[256,1024]{1,0:T(8,128)(2,1)}, bf16[256,1024]{1,0:T(8,128)(2,1)}) custom-call(s32[7]{0:T(128)} %stack.35.place_of, s32[64]{0:T(128)} %bitcast_convert_fusion.2.ids_1, s32[64]{0:T(128)} %bitcast_convert_fusion.1.ids_3, bf16[4096,1024]{1,0:T(8,128)(2,1)} %get-tuple-element.41.partial, ...), custom_call_target="tpu_custom_call" | custom-call | flops 4294967296 | bytes 13631488 | tf_op jit(solution)/shard_map/project_forward/pallas_call | solution.py:292
  265.4 0.0 copy-done.1
  265.4 0.0 copy-done.7
  265.4 1.3 collective-permute-start.6
  266.7 0.0 collective-permute-done.13.by_both
  266.7 0.8 copy-done.9
  267.6 3.0 %assemble.1 = bf16[256,4096]{1,0:T(8,128)(2,1)} custom-call(s32[7]{0:T(128)} %stack.35.place_of, bf16[256,1024]{1,0:T(8,128)(2,1)} %copy-done.1, bf16[256,1024]{1,0:T(8,128)(2,1)} %copy-done.8, bf16[256,1024]{1,0:T(8,128)(2,1)} %copy-done.7, bf16[256,1024]{1,0:T(8,128)(2,1)} %copy-done.9), custom_call_target="tpu_custom_call" | custom-call | bytes 4194304 | tf_op jit(solution)/shard_map/assemble/pallas_call | solution.py:363
  270.6 15.7 %line_grads.1 = bf16[64,128,128]{2,1,0:T(8,128)(2,1)} custom-call(s32[7]{0:T(128)} %stack.35.place_of, s32[64]{0:T(128)} %ids.1, bf16[256,4096]{1,0:T(8,128)(2,1)} %tokens.3, bf16[256,1024]{1,0:T(8,128)(2,1)} %upstream.3, bf16[4,3,256,1024]{3,2,1,0:T(8,128)(2,1)} %bitcast.20, bf16[4,256,1024]{2,1,0:T(8,128)(2,1)} %bitcast.23), custom_call_target="tpu_custom_call" | custom-call | flops 2147483648 | bytes 13107200 | tf_op jit(solution)/shard_map/line_grads/pallas_call | solution.py:413
  286.2 0.0 collective-permute-done.6
  286.2 0.9 broadcast_select_fusion
  (18 shorter events, 0.0 us)
Async XLA Ops:
  7.2 48.2 %all-gather.7.cloned.1.call-start = ((), (), s32[]{:S(2)}) async-start(), calls=%async_computation | async-start | bytes 2621440 | tf_op jit(solution)/shard_map/all_gather | solution.py:466
  9.1 165.3 %all-gather.11.cloned.1.call-start = ((), (), s32[]{:S(2)}) async-start(), calls=%async_computation.2 | async-start | bytes 2621440 | tf_op jit(solution)/shard_map/all_gather | solution.py:465
  9.9 241.1 %all-gather.9.cloned.1.call-start = ((), (), s32[]{:S(2)}) async-start(), calls=%async_computation.1 | async-start | bytes 7864320 | tf_op jit(solution)/shard_map/all_gather | solution.py:485
  55.4 3.0 %copy-start.11 = (s32[64]{0:T(128)S(1)}, s32[64]{0:T(128)}, u32[]{:S(2)}) copy-start(s32[64]{0:T(128)} %ids.1) | copy-start | bytes 772
  55.4 3.2 %copy-start = (bf16[64,128,128]{2,1,0:T(8,128)(2,1)S(1)}, bf16[64,128,128]{2,1,0:T(8,128)(2,1)}, u32[]{:S(2)}) copy-start(bf16[64,128,128]{2,1,0:T(8,128)(2,1)} %own.1) | copy-start | bytes 6291460
  59.8 45.3 %collective-permute-start = (bf16[33,128,128]{2,1,0:T(8,128)(2,1)S(1)}, bf16[33,128,128]{2,1,0:T(8,128)(2,1)S(1)}, u32[]{:S(2)}, u32[]{:S(2)}) collective-permute-start(bf16[33,128,128]{2,1,0:T(8,128)(2,1)S(1)} %pad_maximum_fusion), channel_id=1, source_target_pairs={{0,4},{12,8},{1,5},{13,9},{2,6},{14,10},{3,7},{15,11},{16,20},{28,... | collective-permute-start | bytes 3244040 | tf_op jit(solution)/shard_map/ppermute | solution.py:469
  61.1 60.6 %collective-permute-start.1 = (bf16[33,128,128]{2,1,0:T(8,128)(2,1)S(1)}, bf16[33,128,128]{2,1,0:T(8,128)(2,1)S(1)}, u32[]{:S(2)}, u32[]{:S(2)}) collective-permute-start(bf16[33,128,128]{2,1,0:T(8,128)(2,1)S(1)} %pad_maximum_fusion), channel_id=1, source_target_pairs={{4,8},{8,4},{5,9},{9,5},{6,10},{10,6},{7,11},{11,7},{20,24},{24,20... | collective-permute-start | bytes 3244040 | tf_op jit(solution)/shard_map/ppermute | solution.py:470
  105.0 48.9 %copy-start.4 = (bf16[33,128,128]{2,1,0:T(8,128)(2,1)}, bf16[33,128,128]{2,1,0:T(8,128)(2,1)S(1)}, u32[]{:S(2)}) copy-start(bf16[33,128,128]{2,1,0:T(8,128)(2,1)S(1)} %collective-permute-done.near_a) | copy-start | bytes 3244036
  121.7 29.9 %copy-start.5 = (bf16[33,128,128]{2,1,0:T(8,128)(2,1)}, bf16[33,128,128]{2,1,0:T(8,128)(2,1)S(1)}, u32[]{:S(2)}) copy-start(bf16[33,128,128]{2,1,0:T(8,128)(2,1)S(1)} %collective-permute-done.1.far_a) | copy-start | bytes 3244036
  121.7 26.0 %collective-permute-start.2 = (bf16[33,128,128]{2,1,0:T(8,128)(2,1)S(1)}, bf16[33,128,128]{2,1,0:T(8,128)(2,1)}, u32[]{:S(2)}, u32[]{:S(2)}) collective-permute-start(bf16[33,128,128]{2,1,0:T(8,128)(2,1)S(1)} %collective-permute-done.near_a), channel_id=1, source_target_pairs={{4,8},{8,4},{5,9},{9,5},{6,10},{10,6},{7,11},{11,7},{20,24},{24,20... | collective-permute-start | bytes 3244040 | tf_op jit(solution)/shard_map/ppermute | solution.py:473
  125.1 23.8 %collective-permute-start.3 = (bf16[33,128,128]{2,1,0:T(8,128)(2,1)S(1)}, bf16[33,128,128]{2,1,0:T(8,128)(2,1)S(1)}, u32[]{:S(2)}, u32[]{:S(2)}) collective-permute-start(bf16[33,128,128]{2,1,0:T(8,128)(2,1)S(1)} %collective-permute-done.1.far_a), channel_id=1, source_target_pairs={{0,16},{16,0},{1,17},{17,1},{2,18},{18,2},{3,19},{19,3},{4,20},{20... | collective-permute-start | bytes 3244040 | tf_op jit(solution)/shard_map/ppermute | solution.py:474
  148.9 1.0 copy-start.6
  149.9 24.5 %collective-permute-start.5 = (bf16[33,128,128]{2,1,0:T(8,128)(2,1)}, bf16[33,128,128]{2,1,0:T(8,128)(2,1)S(1)}, u32[]{:S(2)}, u32[]{:S(2)}) collective-permute-start(bf16[33,128,128]{2,1,0:T(8,128)(2,1)} %collective-permute-done.2.end_a), channel_id=1, source_target_pairs={{0,16},{16,0},{1,17},{17,1},{2,18},{18,2},{3,19},{19,3},{4,20},{20... | collective-permute-start | bytes 3244040 | tf_op jit(solution)/shard_map/ppermute | solution.py:478
  150.3 24.1 %collective-permute-start.4 = (bf16[32,128,128]{2,1,0:T(8,128)(2,1)}, bf16[32,128,128]{2,1,0:T(8,128)(2,1)}, u32[]{:S(2)}, u32[]{:S(2)}) collective-permute-start(bf16[32,128,128]{2,1,0:T(8,128)(2,1)} %get-tuple-element.37), channel_id=1, source_target_pairs={{0,4},{12,8},{1,5},{13,9},{2,6},{14,10},{3,7},{15,11},{16,20},{28,... | collective-permute-start | bytes 3145736 | tf_op jit(solution)/shard_map/ppermute | solution.py:477
  174.4 1.0 copy-start.3
  193.0 7.3 %collective-permute-start.7 = (bf16[2,2,256,1024]{3,2,1,0:T(8,128)(2,1)}, bf16[2,2,256,1024]{3,2,1,0:T(8,128)(2,1)S(1)}, u32[]{:S(2)}, u32[]{:S(2)}) collective-permute-start(bf16[2,2,256,1024]{3,2,1,0:T(8,128)(2,1)} %get-tuple-element.48), channel_id=1, source_target_pairs={{0,1},{1,0},{2,3},{3,2},{4,5},{5,4},{6,7},{7,6},{8,9},{9,8},{10,11... | collective-permute-start | bytes 6291464 | tf_op jit(solution)/shard_map/ppermute | solution.py:488
  200.3 1.3 copy-start.2
  205.6 14.3 %collective-permute-start.8 = (bf16[256,1024]{1,0:T(8,128)(2,1)}, bf16[256,1024]{1,0:T(8,128)(2,1)S(1)}, u32[]{:S(2)}, u32[]{:S(2)}) collective-permute-start(bf16[256,1024]{1,0:T(8,128)(2,1)} %get-tuple-element.51), channel_id=1, source_target_pairs={{0,2},{2,0},{1,3},{3,1},{4,6},{6,4},{5,7},{7,5},{8,10},{10,8},{9,1... | collective-permute-start | bytes 1572872 | tf_op jit(solution)/shard_map/ppermute | solution.py:489
  221.2 12.0 %collective-permute-start.9 = (bf16[256,1024]{1,0:T(8,128)(2,1)S(1)}, bf16[256,1024]{1,0:T(8,128)(2,1)S(1)}, u32[]{:S(2)}, u32[]{:S(2)}) collective-permute-start(bf16[256,1024]{1,0:T(8,128)(2,1)S(1)} %add.31), channel_id=1, source_target_pairs={{4,0},{8,12},{5,1},{9,13},{6,2},{10,14},{7,3},{11,15},{20,16},{24,... | collective-permute-start | bytes 1572872 | tf_op jit(solution)/shard_map/ppermute | solution.py:490
  222.5 12.8 %collective-permute-start.10 = (bf16[256,1024]{1,0:T(8,128)(2,1)}, bf16[256,1024]{1,0:T(8,128)(2,1)S(1)}, u32[]{:S(2)}, u32[]{:S(2)}) collective-permute-start(bf16[256,1024]{1,0:T(8,128)(2,1)} %get-tuple-element.54), channel_id=1, source_target_pairs={{0,2},{2,0},{1,3},{3,1},{4,6},{6,4},{5,7},{7,5},{8,10},{10,8},{9,1... | collective-permute-start | bytes 1572872 | tf_op jit(solution)/shard_map/ppermute | solution.py:491
  236.4 28.9 %copy-start.1 = (bf16[256,1024]{1,0:T(8,128)(2,1)}, bf16[256,1024]{1,0:T(8,128)(2,1)S(1)}, u32[]{:S(2)}) copy-start(bf16[256,1024]{1,0:T(8,128)(2,1)S(1)} %add_select_fusion.own) | copy-start | bytes 1572868
  236.5 11.7 %collective-permute-start.11 = (bf16[256,1024]{1,0:T(8,128)(2,1)S(1)}, bf16[256,1024]{1,0:T(8,128)(2,1)S(1)}, u32[]{:S(2)}, u32[]{:S(2)}) collective-permute-start(bf16[256,1024]{1,0:T(8,128)(2,1)S(1)} %add_select_fusion.own), channel_id=1, source_target_pairs={{0,2},{2,0},{1,3},{3,1},{4,6},{6,4},{5,7},{7,5},{8,10},{10,8},{9,1... | collective-permute-start | bytes 1572872 | tf_op jit(solution)/shard_map/ppermute | solution.py:494
  237.3 10.8 %collective-permute-start.12 = (bf16[256,1024]{1,0:T(8,128)(2,1)S(1)}, bf16[256,1024]{1,0:T(8,128)(2,1)S(1)}, u32[]{:S(2)}, u32[]{:S(2)}) collective-permute-start(bf16[256,1024]{1,0:T(8,128)(2,1)S(1)} %add_select_fusion.own), channel_id=1, source_target_pairs={{0,1},{1,0},{2,3},{3,2},{4,5},{5,4},{6,7},{7,6},{8,9},{9,8},{10,11... | collective-permute-start | bytes 1572872 | tf_op jit(solution)/shard_map/ppermute | solution.py:494
  248.2 17.2 %copy-start.7 = (bf16[256,1024]{1,0:T(8,128)(2,1)}, bf16[256,1024]{1,0:T(8,128)(2,1)S(1)}, u32[]{:S(2)}) copy-start(bf16[256,1024]{1,0:T(8,128)(2,1)S(1)} %collective-permute-done.11.by_tensor) | copy-start | bytes 1572868
  248.2 17.2 %copy-start.8 = (bf16[256,1024]{1,0:T(8,128)(2,1)}, bf16[256,1024]{1,0:T(8,128)(2,1)S(1)}, u32[]{:S(2)}) copy-start(bf16[256,1024]{1,0:T(8,128)(2,1)S(1)} %collective-permute-done.12.by_core) | copy-start | bytes 1572868
  248.2 18.6 %collective-permute-start.13 = (bf16[256,1024]{1,0:T(8,128)(2,1)S(1)}, bf16[256,1024]{1,0:T(8,128)(2,1)S(1)}, u32[]{:S(2)}, u32[]{:S(2)}) collective-permute-start(bf16[256,1024]{1,0:T(8,128)(2,1)S(1)} %collective-permute-done.11.by_tensor), channel_id=1, source_target_pairs={{0,1},{1,0},{2,3},{3,2},{4,5},{5,4},{6,7},{7,6},{8,9},{9,8},{10,11... | collective-permute-start | bytes 1572872 | tf_op jit(solution)/shard_map/ppermute | solution.py:495
  265.4 20.8 %collective-permute-start.6 = (bf16[256,1024]{1,0:T(8,128)(2,1)}, bf16[256,1024]{1,0:T(8,128)(2,1)S(1)}, u32[]{:S(2)}, u32[]{:S(2)}) collective-permute-start(bf16[256,1024]{1,0:T(8,128)(2,1)} %get-tuple-element.45), channel_id=1, source_target_pairs={{4,0},{8,12},{5,1},{9,13},{6,2},{10,14},{7,3},{11,15},{20,16},{24,... | collective-permute-start | bytes 1572872 | tf_op jit(solution)/shard_map/ppermute | solution.py:498
  266.7 0.8 copy-start.9
  270.5 15.7 %copy-start.10 = (bf16[256,1024]{1,0:T(8,128)(2,1)S(1)}, bf16[256,1024]{1,0:T(8,128)(2,1)}, u32[]{:S(2)}) copy-start(bf16[256,1024]{1,0:T(8,128)(2,1)} %get-tuple-element.44) | copy-start | bytes 1572868
Sparse Core Ops, SparseCore 0:
  10.1 45.1 all-gather.6
  56.9 64.7 all-gather.10
  123.3 46.9 all-gather.8

commit v7 on v6

--- a/solution.py
+++ b/solution.py
@@ -191,27 +191,26 @@
 
 
 def back_kernel(
-    place_of, ids_1, ids_3, partial, near_b, end_b, all_upstream, upstream, keep, give,
-    held, sources, sem,
+    place_of, ids_1, ids_3, partial, near_b, end_b, end_upstream, upstream,
+    end_keep, own_keep, own_give, end_give_0, end_give_1, held, sources, sem,
 ):
     half_slots = near_b.shape[0]
     other = (1 - place_of[1]) * half_slots
     rows, width = upstream.shape
-    depth = held.shape[1]
     step = 256
-    per_part = keep.shape[3] // step
+    per_part = end_keep.shape[2] // step
 
     @pl.when(place_of[0] == 1)
     def work():
         load = pltpu.make_async_copy(partial, held, sem)
         load.start()
-        sources[:rows] = all_upstream[place_of[5]]
+        sources[:rows] = end_upstream[...]
         sources[rows:] = upstream[...]
         load.wait()
         place_blocks(ids_1, other, near_b, None, held, half_slots)
         place_blocks(ids_3, other, end_b, None, held, half_slots)
 
-        def column(part, target, x):
+        def column(part, end_target, own_target):
             @pl.loop(0, per_part, unroll=2)
             def backward(n):
                 at = pl.multiple_of(n * step, step)
@@ -219,24 +218,25 @@
                     sources[...],
                     held[:, pl.ds(pl.multiple_of(part * per_part * step + at, step), step)],
                     preferred_element_type=jnp.float32,
-                ).astype(target.dtype)
-                target[0, x, :, pl.ds(at, step)] = result[:rows]
-                target[1, x, :, pl.ds(at, step)] = result[rows:]
-
-        for x in range(2):
-            column(2 * x + place_of[3], keep, x)
-            column(2 * x + 1 - place_of[3], give, x)
-
-
-def project_back(place_of, ids_1, ids_3, partial, near_b, end_b, all_upstream, upstream):
+                ).astype(own_target.dtype)
+                end_target[:, pl.ds(at, step)] = result[:rows]
+                own_target[:, pl.ds(at, step)] = result[rows:]
+
+        for x, end_give in enumerate((end_give_0, end_give_1)):
+            column(2 * x + place_of[3], end_keep.at[x], own_keep.at[x])
+            column(2 * x + 1 - place_of[3], end_give, own_give.at[x])
+
+
+def project_back(place_of, ids_1, ids_3, partial, near_b, end_b, end_upstream, upstream):
     width, depth = partial.shape
     rows = upstream.shape[0]
-    half = jax.ShapeDtypeStruct((2, 2, rows, depth // 4), jnp.bfloat16)
+    quarter = jax.ShapeDtypeStruct((rows, depth // 4), jnp.bfloat16)
+    half = jax.ShapeDtypeStruct((2, rows, depth // 4), jnp.bfloat16)
     return pl.pallas_call(
         back_kernel,
-        out_shape=(half, half),
+        out_shape=(half, half, half, quarter, quarter),
         in_specs=[whole(pltpu.SMEM)] * 3 + [whole(pl.ANY)] + [whole()] * 4,
-        out_specs=(whole(), whole()),
+        out_specs=(whole(),) * 5,
         scratch_shapes=[
             pltpu.VMEM((width, depth), jnp.bfloat16),
             pltpu.VMEM((2 * rows, width), jnp.bfloat16),
@@ -249,7 +249,7 @@
             transcendentals=0,
         ),
         name="project_back",
-    )(place_of, ids_1, ids_3, partial, near_b, end_b, all_upstream, upstream)
+    )(place_of, ids_1, ids_3, partial, near_b, end_b, end_upstream, upstream)
 
 
 def forward_kernel(
@@ -258,7 +258,7 @@
     half_slots = near_b.shape[0]
     other = (1 - place_of[1]) * half_slots
     depth, width = held.shape
-    parts, _, rows, part_width = gathered.shape
+    parts, rows, part_width = gathered.shape
     step = 256
 
     @pl.when(place_of[0] == 1)
@@ -275,7 +275,7 @@
             acc = jnp.zeros((rows, step), jnp.float32)
             for q in range(parts):
                 acc += jnp.dot(
-                    gathered[q, place_of[4]],
+                    gathered[q],
                     held[q * part_width : (q + 1) * part_width, pl.ds(c, step)],
                     preferred_element_type=jnp.float32,
                 )
@@ -305,47 +305,35 @@
     )(place_of, ids_1, ids_3, partial, near_b, end_b, tokens, gathered)
 
 
-def others_kernel(place_of, quarters, others):
-    count = quarters.shape[0]
-    for j in range(count - 1):
-        others[j] = quarters[lax.rem(place_of[6] + 1 + j, count)]
-
-
-def other_slabs(place_of, quarters):
-    return pl.pallas_call(
-        others_kernel,
-        out_shape=jax.ShapeDtypeStruct((quarters.shape[0] - 1,) + quarters.shape[1:], quarters.dtype),
-        in_specs=[whole(pltpu.SMEM), whole()],
-        out_specs=whole(),
-        compiler_params=pltpu.CompilerParams(vmem_limit_bytes=VMEM_LIMIT),
-        cost_estimate=pl.CostEstimate(
-            flops=0, bytes_accessed=quarters.size * 4, transcendentals=0
-        ),
-        name="other_slabs",
-    )(place_of, quarters)
-
-
-def split_kernel(place_of, keep, got, *outs):
+def split_kernel(place_of, keep, *refs):
     x = place_of[2]
-    for n, ref in enumerate(outs):
-        k, at = n // 2, (x, 1 - x)[n % 2]
-        total = keep[k, at].astype(jnp.float32) + got[k, at].astype(jnp.float32)
-        ref[...] = total.astype(ref.dtype)
-
-
-def add_split(place_of, keep, got):
-    out = jax.ShapeDtypeStruct(keep.shape[2:], keep.dtype)
+    own, give = refs[-2:]
+    got = refs[:-2] if len(refs) > 3 else (refs[0].at[0], refs[0].at[1])
+    for at in range(2):
+        total = (keep[at].astype(jnp.float32) + got[at][...].astype(jnp.float32)).astype(own.dtype)
+
+        @pl.when(x == at)
+        def mine():
+            own[...] = total
+
+        @pl.when(x != at)
+        def theirs():
+            give[...] = total
+
+
+def add_split(place_of, keep, *got):
+    out = jax.ShapeDtypeStruct(keep.shape[1:], keep.dtype)
     return pl.pallas_call(
         split_kernel,
-        out_shape=(out,) * 4,
-        in_specs=[whole(pltpu.SMEM), whole(), whole()],
-        out_specs=(whole(),) * 4,
+        out_shape=(out, out),
+        in_specs=[whole(pltpu.SMEM), whole()] + [whole()] * len(got),
+        out_specs=(whole(), whole()),
         compiler_params=pltpu.CompilerParams(vmem_limit_bytes=VMEM_LIMIT),
         cost_estimate=pl.CostEstimate(
             flops=keep.size, bytes_accessed=keep.size * 6, transcendentals=0
         ),
         name="add_split",
-    )(place_of, keep, got)
+    )(place_of, keep, *got)
 
 
 def assemble_kernel(place_of, own, by_core, by_tensor, by_both, full):
@@ -373,60 +361,58 @@
     )(place_of, *quarters)
 
 
-def line_grads_kernel(place_of, ids, tokens, upstream, gathered, all_upstream, grads):
+def line_grads_kernel(pairs_n, ids, *refs):
+    pairs = [(refs[2 * k], refs[2 * k + 1]) for k in range(pairs_n)]
+    grads = refs[-1]
+    start = refs[2 * pairs_n] if len(refs) > 2 * pairs_n + 1 else None
     slots, size = grads.shape[0], grads.shape[1]
-    cols_n = upstream.shape[1] // size
-    total = (tokens.shape[1] // size) * cols_n
-    parts, others_n, _, part_width = gathered.shape
-    per_part = part_width // size
+    first = pairs[0][0]
+    cols_n = pairs[0][1].shape[1] // size
+    rows_n = first.shape[-1] // size * (first.shape[0] if len(first.shape) == 3 else 1)
+    total = rows_n * cols_n
     group = math.gcd(slots, 8)
-    contract = (((0,), (0,)), ((), ()))
 
     @pl.loop(0, slots // group)
     def some(g):
         for s in [g * group + j for j in range(group)]:
             b = jnp.minimum(ids[s], total - 1)
             row = b // cols_n
-            part = row // per_part
-            at = pl.ds(pl.multiple_of((row % per_part) * size, size), size)
             c = pl.ds(pl.multiple_of((b % cols_n) * size, size), size)
-            acc = lax.dot_general(
-                tokens[:, pl.ds(pl.multiple_of(row * size, size), size)],
-                upstream[:, c],
-                contract,
-                preferred_element_type=jnp.float32,
-            )
-            for j in range(others_n):
-                slab = lax.rem(place_of[6] + 1 + j, others_n + 1)
+            acc = jnp.zeros((size, size), jnp.float32) if start is None else start[s]
+            for x, d in pairs:
+                per_part = x.shape[-1] // size
+                at = pl.ds(pl.multiple_of((row % per_part) * size, size), size)
                 acc += lax.dot_general(
-                    gathered[part, j, :, at],
-                    all_upstream[slab, :, c],
-                    contract,
+                    x[row // per_part, :, at] if len(x.shape) == 3 else x[:, at],
+                    d[:, c],
+                    (((0,), (0,)), ((), ())),
                     preferred_element_type=jnp.float32,
                 )
             grads[s] = jnp.where(ids[s] < total, acc, 0.0).astype(grads.dtype)
 
 
-def line_grads(place_of, ids, tokens, upstream, gathered, all_upstream, size):
+def line_grads(ids, pairs, start, size, out_dtype):
     slots = ids.shape[0]
-    rows = upstream.shape[0]
-    return pl.pallas_call(
-        line_grads_kernel,
-        out_shape=jax.ShapeDtypeStruct((slots, size, size), jnp.bfloat16),
-        in_specs=[whole(pltpu.SMEM)] * 2 + [whole()] * 4,
+    rows = pairs[0][1].shape[0]
+    flat = [a for pair in pairs for a in pair] + ([] if start is None else [start])
+    return pl.pallas_call(
+        functools.partial(line_grads_kernel, len(pairs)),
+        out_shape=jax.ShapeDtypeStruct((slots, size, size), out_dtype),
+        in_specs=[whole(pltpu.SMEM)] + [whole()] * len(flat),
         out_specs=whole(),
         compiler_params=pltpu.CompilerParams(vmem_limit_bytes=VMEM_LIMIT),
         cost_estimate=pl.CostEstimate(
-            flops=8 * slots * rows * size * size,
-            bytes_accessed=2 * (4 * tokens.size + 5 * upstream.size + slots * size * size),
+            flops=2 * len(pairs) * slots * rows * size * size,
+            bytes_accessed=sum(2 * a.size for a in flat) + 4 * slots * size * size,
             transcendentals=0,
         ),
         name="line_grads",
-    )(place_of, ids, tokens, upstream, gathered, all_upstream)
+    )(ids, *flat)
 
 
 INWARD = ((0, 1), (3, 2))
 OUTWARD = ((1, 0), (2, 3))
+PAIRS = INWARD + OUTWARD
 MIDDLE = ((1, 2), (2, 1))
 SWAP = ((0, 1), (1, 0))
 
@@ -442,16 +428,14 @@
 
 def line_body(tokens, upstream, blocks, block_ids):
     slots, size = blocks.shape[0], blocks.shape[1]
-    depth, width = tokens.shape[1], upstream.shape[1]
+    rows, depth = tokens.shape
+    width = upstream.shape[1]
     half_slots = slots // 2
     part_width = depth // 4
     at_z, half = lax.axis_index("dp"), lax.axis_index("groups")
     at_tensor, at_replica = lax.axis_index("tensor"), lax.axis_index("replica")
     middle = (at_z == 1) | (at_z == 2)
-    end = jnp.where(at_z == 1, 0, 3)
-    place_of = jnp.stack(
-        [middle.astype(jnp.int32), half, at_tensor, at_replica, (end + 3 - at_z) % 4, end, at_z]
-    )
+    place_of = jnp.stack([middle.astype(jnp.int32), half, at_tensor, at_replica])
     along = functools.partial(lax.ppermute, axis_name="dp")
     across = functools.partial(lax.ppermute, axis_name="groups", perm=SWAP)
     sideways = functools.partial(lax.ppermute, axis_name="tensor", perm=SWAP)
@@ -462,41 +446,65 @@
     other = lax.dynamic_slice_in_dim(blocks, (1 - half) * half_slots, half_slots, 0)
     mine = jnp.concatenate([mine, ids_block(block_ids, size).astype(jnp.bfloat16)])
     part = lax.dynamic_slice_in_dim(tokens, lax.axis_index(INNER) * part_width, part_width, 1)
-    all_upstream = lax.all_gather(upstream, "dp")
-    quarters = lax.all_gather(part, "dp")
-    mine, other = stage((mine, other))
+    both = jnp.concatenate([part, upstream])
+    mine, other, both = stage((mine, other, both))
 
     near_a = along(mine, perm=INWARD)
     far_a = along(mine, perm=MIDDLE)
-    near_a, far_a, other = stage((near_a, far_a, other))
+    near_a, far_a, both, other = stage((near_a, far_a, both, other))
 
     end_a = along(near_a, perm=MIDDLE)
     far_b = across(far_a)
-    end_a, far_b, other = stage((end_a, far_b, other))
+    both_1 = along(both, perm=PAIRS)
+    both_1, end_a, far_b, both, other = stage((both_1, end_a, far_b, both, other))
+    upstream_1 = both_1[rows:]
 
     near_b = along(other, perm=INWARD)
     end_b = across(end_a)
+    both_2m = along(both, perm=MIDDLE)
+    tokens_1 = lax.all_gather(both_1[:rows], INNER)
     ids_1, ids_2, ids_3 = (ids_of(piece, slots) for piece in (near_a, far_a, end_a))
     partial, turned = place_first(
         place_of, (block_ids, ids_1, ids_2, ids_3), (blocks, near_a, far_a, far_b, end_a), depth, width
     )
-    near_b, end_b, partial, turned = stage((near_b, end_b, partial, turned))
-
-    gathered = lax.all_gather(other_slabs(place_of, quarters), INNER)
+    near_b, end_b, both_2m, both_1, tokens_1, partial, turned = stage(
+        (near_b, end_b, both_2m, both_1, tokens_1, partial, turned)
+    )
+
+    both_3m = along(both_1, perm=MIDDLE)
+    both_2o = along(both_2m, perm=OUTWARD)
     last = (near_b, end_b)
-    keep, give = project_back(place_of, ids_1, ids_3, turned, *last, all_upstream, upstream)
-    end_keep, end_give, own_keep, own_give = add_split(place_of, keep, cores(give))
-    end_got, own_give = stage((sideways(end_give), own_give))
+    end_keep, own_keep, own_give, *end_give = project_back(
+        place_of, ids_1, ids_3, turned, *last, upstream_1, upstream
+    )
+    end_keep, end_give = add_split(place_of, end_keep, *[cores(a) for a in end_give])
+    end_keep, end_give, own_give, both_3m, both_2o = stage(
+        (end_keep, end_give, own_give, both_3m, both_2o)
+    )
+
+    end_got = sideways(end_give)
+    own_keep, own_give = add_split(place_of, own_keep, cores(own_give))
+    both_3o = along(both_3m, perm=OUTWARD)
+    tokens_2 = lax.all_gather(both_2m[:rows] + both_2o[:rows], INNER)
+    upstream_2 = both_2m[rows:] + both_2o[rows:]
+    end_got, own_give, own_keep = stage((end_got, own_give, own_keep))
+
     sum_out = along(end_keep + end_got, perm=OUTWARD)
     own_got = sideways(own_give)
-    sum_out, own_got = stage((sum_out, own_got))
+    proj, end_proj = project_forward(place_of, ids_1, ids_3, partial, *last, tokens, tokens_1)
+    sum_out, own_got, both_3o, proj, end_proj = stage((sum_out, own_got, both_3o, proj, end_proj))
+
+    tokens_3 = lax.all_gather(both_3m[:rows] + both_3o[:rows], INNER)
+    upstream_3 = both_3m[rows:] + both_3o[rows:]
     quarter = jnp.where(middle, own_keep + own_got, sum_out)
-    by_tensor, by_core = stage((sideways(quarter), cores(quarter)))
+    proj_out = along(end_proj, perm=OUTWARD)
+    pairs = ((tokens, upstream), (tokens_1, upstream_1), (tokens_2, upstream_2))
+    grads = line_grads(block_ids, pairs, None, size, jnp.float32)
+    by_tensor, by_core, grads = stage((sideways(quarter), cores(quarter), grads))
     by_both = cores(by_tensor)
+    projected = jnp.where(middle, proj, proj_out)
     token_grad = assemble(place_of, (quarter, by_core, by_tensor, by_both))
-    proj, end_proj = project_forward(place_of, ids_1, ids_3, partial, *last, tokens, gathered)
-    projected = jnp.where(middle, proj, along(end_proj, perm=OUTWARD))
-    grads = line_grads(place_of, block_ids, tokens, upstream, gathered, all_upstream, size)
+    grads = line_grads(block_ids, ((tokens_3, upstream_3),), grads, size, jnp.bfloat16)
     return projected, token_grad, grads
 
 

time: 294 us -> 212 us (0.72)
  the two profiles are of different devices: /device:TPU:13 before, /device:TPU:0 now
where the time goes in v7:
time: 212 us; the launch traced here: 211 us
  waiting for transfers between devices  101 us (48%)
  Pallas kernels  47.3 us (22%)
  starting transfers between devices  29.8 us (14%)
  between operations  14 us (7%)
  other arithmetic  10.3 us (5%)
  local copies, waits for them, and re-layouts  8.53 us (4%)
    ppermute x1, waiting for transfers between devices, line_body(): near_a = along(mine, perm=INWARD)  22.3 us
    ppermute x1, waiting for transfers between devices, line_body(): both_1 = along(both, perm=PAIRS)  21.7 us
    pallas_call x2, Pallas kernels, line_grads(): pl.pallas_call(functools.partial(line_grads_kernel, len(pairs)), out_shap...  21.7 us
    ppermute x1, waiting for transfers between devices, line_body(): both_2o = along(both_2m, perm=OUTWARD)  16 us
    ppermute x1, waiting for transfers between devices, line_body(): end_got = sideways(end_give)  10.7 us
    ppermute x1, waiting for transfers between devices, line_body(): sum_out = along(end_keep + end_got, perm=OUTWARD)  10.7 us
    pallas_call x1, Pallas kernels, place_first(): pl.pallas_call(place_kernel, out_shape=(jax.ShapeDtypeStruct((depth, widt...  8.76 us
    ppermute x1, waiting for transfers between devices, line_body(): near_b = along(other, perm=INWARD)  6.87 us
  transfers between devices with their start and end apart: 24, of which 13 were waited for; matrix products, arithmetic and copies ran while one was open for 3% of the time, Pallas kernels for 18%

profile of v7, /device:TPU:0, one launch (start us, length us, event | category | flops | bytes accessed | tf_op | source)
XLA Modules:
  0.0 211.2 jit_solution(13625152111497601599)
XLA Ops:
  7.2 0.0 all-gather.7.cloned.1.call-start
  7.2 0.7 convert_element_type.26
  7.9 0.1 convert_element_type.27
  8.0 2.7 %constant_dynamic-slice_fusion.1 = (bf16[32,128,128]{2,1,0:T(8,128)(2,1)}, bf16[32,128,128]{2,1,0:T(8,128)(2,1)S(1)}) fusion(bf16[64,128,128]{2,1,0:T(8,128)(2,1)} %own.1, s32[]{:T(128)S(6)} %select_n.23, s32[]{:T(128)S(6)} %select_n.22), kind=kLoop, calls=%fused_computation.9 | loop fusion | bytes 4194312 | tf_op jit(solution)/shard_map/dynamic_slice | solution.py:446
  10.7 0.1 pad_maximum_fusion
  10.8 1.1 constant_dynamic-slice_fusion
  11.9 0.1 pad_maximum_fusion.1
  12.0 5.0 %collective-permute-start = (bf16[33,128,128]{2,1,0:T(8,128)(2,1)S(1)}, bf16[33,128,128]{2,1,0:T(8,128)(2,1)S(1)}, u32[]{:S(2)}, u32[]{:S(2)}) collective-permute-start(bf16[33,128,128]{2,1,0:T(8,128)(2,1)S(1)} %pad_maximum_fusion), channel_id=1, source_target_pairs={{0,4},{12,8},{1,5},{13,9},{2,6},{14,10},{3,7},{15,11},{16,20},{28,... | collective-permute-start | bytes 3244040 | tf_op jit(solution)/shard_map/ppermute | solution.py:452
  17.0 0.7 collective-permute-start.1
  17.7 22.3 %collective-permute-done.near_a = bf16[33,128,128]{2,1,0:T(8,128)(2,1)S(1)} collective-permute-done((bf16[33,128,128]{2,1,0:T(8,128)(2,1)S(1)}, bf16[33,128,128]{2,1,0:T(8,128)(2,1)S(1)}, u32[]{:S(2)}, u32[]{:S(2)}) %collective-permute-start) | collective-permute-done | bytes 1081376 | tf_op jit(solution)/shard_map/ppermute | solution.py:452
  40.0 0.7 collective-permute-start.3
  40.8 1.6 collective-permute-start.4
  42.4 6.5 %collective-permute-start.2 = (bf16[512,1024]{1,0:T(8,128)(2,1)S(1)}, bf16[512,1024]{1,0:T(8,128)(2,1)S(1)}, u32[]{:S(2)}, u32[]{:S(2)}) collective-permute-start(bf16[512,1024]{1,0:T(8,128)(2,1)S(1)} %pad_maximum_fusion.1), channel_id=1, source_target_pairs={{0,4},{12,8},{4,0},{8,12},{1,5},{13,9},{5,1},{9,13},{2,6},{14,10},... | collective-permute-start | bytes 3145736 | tf_op jit(solution)/shard_map/ppermute | solution.py:458
  48.9 21.7 %collective-permute-done.2 = bf16[512,1024]{1,0:T(8,128)(2,1)S(1)} collective-permute-done((bf16[512,1024]{1,0:T(8,128)(2,1)S(1)}, bf16[512,1024]{1,0:T(8,128)(2,1)S(1)}, u32[]{:S(2)}, u32[]{:S(2)}) %collective-permute-start.2) | collective-permute-done | bytes 1048608 | tf_op jit(solution)/shard_map/ppermute | solution.py:458
  70.6 1.0 copy-done.6
  71.6 1.0 fusion
  72.7 0.0 all-gather.9.cloned.1.call-start
  72.7 0.6 collective-permute-start.6
  73.3 4.6 %collective-permute-start.5 = (bf16[32,128,128]{2,1,0:T(8,128)(2,1)}, bf16[32,128,128]{2,1,0:T(8,128)(2,1)}, u32[]{:S(2)}, u32[]{:S(2)}) collective-permute-start(bf16[32,128,128]{2,1,0:T(8,128)(2,1)} %get-tuple-element.59), channel_id=1, source_target_pairs={{0,4},{12,8},{1,5},{13,9},{2,6},{14,10},{3,7},{15,11},{16,20},{28,... | collective-permute-start | bytes 3145736 | tf_op jit(solution)/shard_map/ppermute | solution.py:462
  77.9 1.7 collective-permute-start.7
  79.6 0.7 pad_add_fusion.place_of
  80.3 0.6 bitcast_convert_fusion
  80.9 0.6 bitcast_convert_fusion.1.ids_3
  81.5 8.8 %place_first.1 = (bf16[4096,1024]{1,0:T(8,128)(2,1)}, bf16[1024,4096]{1,0:T(8,128)(2,1)}) custom-call(s32[4]{0:T(128)} %pad_add_fusion.place_of, s32[64]{0:T(128)} %ids.3, s32[64]{0:T(128)} %get-tuple-element.108.ids_1, s32[64]{0:T(128)} %get-tuple-element.107.ids_2, s32[64]{0:T(128)} %bitcast_convert_fusion.1.ids_3, bf16[64,128,128]{2,1,0:T(8,128)(2,1)} %own.1, ...), custom_call_target="tpu_custom_call" | custom-call | bytes 25165824 | tf_op jit(solution)/shard_map/place_first/pallas_call | solution.py:177
  90.2 6.9 %collective-permute-done.5.near_b = bf16[32,128,128]{2,1,0:T(8,128)(2,1)} collective-permute-done((bf16[32,128,128]{2,1,0:T(8,128)(2,1)}, bf16[32,128,128]{2,1,0:T(8,128)(2,1)}, u32[]{:S(2)}, u32[]{:S(2)}) %collective-permute-start.5) | collective-permute-done | bytes 1048608 | tf_op jit(solution)/shard_map/ppermute | solution.py:462
  97.1 0.7 collective-permute-start.10
  97.9 1.3 collective-permute-start.11
  99.2 3.9 %project_back.1 = (bf16[2,256,1024]{2,1,0:T(8,128)(2,1)}, bf16[2,256,1024]{2,1,0:T(8,128)(2,1)}, bf16[2,256,1024]{2,1,0:T(8,128)(2,1)}, bf16[256,1024]{1,0:T(8,128)(2,1)}, bf16[256,1024]{1,0:T(8,128)(2,1)}) custom-call(s32[4]{0:T(128)} %pad_add_fusion.place_of, s32[64]{0:T(128)} %get-tuple-element.108.ids_1, s32[64]{0:T(128)} %bitcast_convert_fusion.1.ids_3, ...), custom_call_target="tpu_custom_call" | custom-call | flops 4294967296 | bytes 13631488 | tf_op jit(solution)/shard_map/project_back/pallas_call | solution.py:235
  103.0 0.1 collective-permute-start.8
  103.1 0.5 collective-permute-start.9
  103.6 1.6 collective-permute-done.8.refs_0_
  105.2 0.7 collective-permute-done.9.refs_1_
  106.0 0.0 copy-done.12
  106.0 0.8 copy-done.14
  106.8 3.0 %add_split.2 = (bf16[256,1024]{1,0:T(8,128)(2,1)}, bf16[256,1024]{1,0:T(8,128)(2,1)}) custom-call(s32[4]{0:T(128)} %pad_add_fusion.place_of, bf16[2,256,1024]{2,1,0:T(8,128)(2,1)} %get-tuple-element.68.keep, bf16[256,1024]{1,0:T(8,128)(2,1)} %copy-done.12, bf16[256,1024]{1,0:T(8,128)(2,1)} %copy-done.14), custom_call_target="tpu_custom_call" | custom-call | flops 524288 | bytes 3145728 | tf_op jit(solution)/shard_map/add_split/pallas_call | solution.py:326
  109.8 16.0 %collective-permute-done.11 = bf16[512,1024]{1,0:T(8,128)(2,1)S(1)} collective-permute-done((bf16[512,1024]{1,0:T(8,128)(2,1)}, bf16[512,1024]{1,0:T(8,128)(2,1)S(1)}, u32[]{:S(2)}, u32[]{:S(2)}) %collective-permute-start.11) | collective-permute-done | bytes 1048608 | tf_op jit(solution)/shard_map/ppermute | solution.py:475
  125.9 2.3 %slice_add_fusion.2 = (bf16[256,1024]{1,0:T(8,128)(2,1)}, bf16[256,1024]{1,0:T(8,128)(2,1)}) fusion(bf16[512,1024]{1,0:T(8,128)(2,1)S(1)} %collective-permute-done.11, bf16[512,1024]{1,0:T(8,128)(2,1)} %collective-permute-done.7), kind=kLoop, calls=%fused_computation.4 | loop fusion | flops 524288 | bytes 3145728 | tf_op jit(solution)/shard_map/add | solution.py:489
  128.2 0.0 all-gather.11.cloned.1.call-start
  128.2 0.1 collective-permute-start.13
  128.3 0.3 collective-permute-start.12
  128.6 1.3 collective-permute-start.16
  129.9 1.3 collective-permute-done.13.refs_0_
  131.2 1.0 copy-done.5
  132.1 3.0 %add_split.3 = (bf16[256,1024]{1,0:T(8,128)(2,1)}, bf16[256,1024]{1,0:T(8,128)(2,1)}) custom-call(s32[4]{0:T(128)} %pad_add_fusion.place_of, bf16[2,256,1024]{2,1,0:T(8,128)(2,1)} %get-tuple-element.78.keep, bf16[2,256,1024]{2,1,0:T(8,128)(2,1)} %copy-done.5), custom_call_target="tpu_custom_call" | custom-call | flops 524288 | bytes 3145728 | tf_op jit(solution)/shard_map/add_split/pallas_call | solution.py:326
  135.2 10.7 %collective-permute-done.12 = bf16[256,1024]{1,0:T(8,128)(2,1)S(1)} collective-permute-done((bf16[256,1024]{1,0:T(8,128)(2,1)}, bf16[256,1024]{1,0:T(8,128)(2,1)S(1)}, u32[]{:S(2)}, u32[]{:S(2)}) %collective-permute-start.12) | collective-permute-done | bytes 524320 | tf_op jit(solution)/shard_map/ppermute | solution.py:485
  145.9 2.1 add.34
  147.9 1.3 collective-permute-start.14
  149.2 0.2 collective-permute-start.15
  149.4 3.9 %project_forward.1 = (bf16[256,1024]{1,0:T(8,128)(2,1)}, bf16[256,1024]{1,0:T(8,128)(2,1)}) custom-call(s32[4]{0:T(128)} %pad_add_fusion.place_of, s32[64]{0:T(128)} %get-tuple-element.108.ids_1, s32[64]{0:T(128)} %bitcast_convert_fusion.1.ids_3, bf16[4096,1024]{1,0:T(8,128)(2,1)} %get-tuple-element.85.partial, ...), custom_call_target="tpu_custom_call" | custom-call | flops 4294967296 | bytes 13631488 | tf_op jit(solution)/shard_map/project_forward/pallas_call | solution.py:292
  153.3 3.6 %collective-permute-done.16 = bf16[512,1024]{1,0:T(8,128)(2,1)S(1)} collective-permute-done((bf16[512,1024]{1,0:T(8,128)(2,1)S(1)}, bf16[512,1024]{1,0:T(8,128)(2,1)S(1)}, u32[]{:S(2)}, u32[]{:S(2)}) %collective-permute-start.16) | collective-permute-done | bytes 1048608 | tf_op jit(solution)/shard_map/ppermute | solution.py:487
  156.9 10.7 %collective-permute-done.14 = bf16[256,1024]{1,0:T(8,128)(2,1)S(1)} collective-permute-done((bf16[256,1024]{1,0:T(8,128)(2,1)}, bf16[256,1024]{1,0:T(8,128)(2,1)S(1)}, u32[]{:S(2)}, u32[]{:S(2)}) %collective-permute-start.14) | collective-permute-done | bytes 524320 | tf_op jit(solution)/shard_map/ppermute | solution.py:492
  167.6 1.2 slice_add_fusion
  168.8 1.1 add_select_fusion.own
  170.0 1.2 collective-permute-start.18
  171.1 1.3 collective-permute-start.17
  172.5 13.3 %line_grads.2.refs_2_ = f32[64,128,128]{2,1,0:T(8,128)} custom-call(s32[64]{0:T(128)} %ids.3, bf16[256,4096]{1,0:T(8,128)(2,1)} %refs_0_.1, bf16[256,1024]{1,0:T(8,128)(2,1)} %refs_1_.1, bf16[4,256,1024]{2,1,0:T(8,128)(2,1)} %bitcast.18, bf16[256,1024]{1,0:T(8,128)(2,1)} %get-tuple-element.105.end_upstream.refs_3_, bf16[4,256,1024]{2,1,0:T(8,128)(2,1)} %bitcast.19, ...), custom_call_target="tpu_custom_call" | custom-call | flops 1610612736 | bytes 12058624 | tf_op jit(solution)/shard_map/line_grads/pallas_call | solution.py:398
  185.8 2.9 %collective-permute-done.18.by_tensor = bf16[256,1024]{1,0:T(8,128)(2,1)S(1)} collective-permute-done((bf16[256,1024]{1,0:T(8,128)(2,1)S(1)}, bf16[256,1024]{1,0:T(8,128)(2,1)S(1)}, u32[]{:S(2)}, u32[]{:S(2)}) %collective-permute-start.18) | collective-permute-done | bytes 524320 | tf_op jit(solution)/shard_map/ppermute | solution.py:503
  188.7 0.1 collective-permute-start.20
  188.8 1.0 broadcast_select_fusion
  189.8 0.8 collective-permute-done.20.by_both
  190.7 0.8 copy-done.13
  191.5 3.0 %assemble.1 = bf16[256,4096]{1,0:T(8,128)(2,1)} custom-call(s32[4]{0:T(128)} %pad_add_fusion.place_of, bf16[256,1024]{1,0:T(8,128)(2,1)} %copy-done, bf16[256,1024]{1,0:T(8,128)(2,1)} %copy-done.10, bf16[256,1024]{1,0:T(8,128)(2,1)} %copy-done.9, bf16[256,1024]{1,0:T(8,128)(2,1)} %copy-done.13), custom_call_target="tpu_custom_call" | custom-call | bytes 4194304 | tf_op jit(solution)/shard_map/assemble/pallas_call | solution.py:351
  194.4 1.7 all-gather.11.cloned.1.call-done
  196.2 8.4 %line_grads.3 = bf16[64,128,128]{2,1,0:T(8,128)(2,1)} custom-call(s32[64]{0:T(128)} %ids.3, bf16[4,256,1024]{2,1,0:T(8,128)(2,1)} %bitcast.16, bf16[256,1024]{1,0:T(8,128)(2,1)} %get-tuple-element.99.refs_1_, f32[64,128,128]{2,1,0:T(8,128)} %line_grads.2.refs_2_), custom_call_target="tpu_custom_call" | custom-call | flops 536870912 | bytes 8912896 | tf_op jit(solution)/shard_map/line_grads/pallas_call | solution.py:398
  (44 shorter events, 0.2 us)
Async XLA Ops:
  7.2 90.0 %all-gather.7.cloned.1.call-start = ((), (), s32[]{:S(2)}) async-start(), calls=%async_computation | async-start | bytes 2621440 | tf_op jit(solution)/shard_map/all_gather | solution.py:465
  10.7 1.2 copy-start.1
  12.0 60.6 %copy-start.7 = (bf16[512,1024]{1,0:T(8,128)(2,1)}, bf16[512,1024]{1,0:T(8,128)(2,1)S(1)}, u32[]{:S(2)}) copy-start(bf16[512,1024]{1,0:T(8,128)(2,1)S(1)} %pad_maximum_fusion.1) | copy-start | bytes 3145732
  12.0 28.0 %collective-permute-start = (bf16[33,128,128]{2,1,0:T(8,128)(2,1)S(1)}, bf16[33,128,128]{2,1,0:T(8,128)(2,1)S(1)}, u32[]{:S(2)}, u32[]{:S(2)}) collective-permute-start(bf16[33,128,128]{2,1,0:T(8,128)(2,1)S(1)} %pad_maximum_fusion), channel_id=1, source_target_pairs={{0,4},{12,8},{1,5},{13,9},{2,6},{14,10},{3,7},{15,11},{16,20},{28,... | collective-permute-start | bytes 3244040 | tf_op jit(solution)/shard_map/ppermute | solution.py:452
  17.0 23.0 %collective-permute-start.1 = (bf16[33,128,128]{2,1,0:T(8,128)(2,1)S(1)}, bf16[33,128,128]{2,1,0:T(8,128)(2,1)S(1)}, u32[]{:S(2)}, u32[]{:S(2)}) collective-permute-start(bf16[33,128,128]{2,1,0:T(8,128)(2,1)S(1)} %pad_maximum_fusion), channel_id=1, source_target_pairs={{4,8},{8,4},{5,9},{9,5},{6,10},{10,6},{7,11},{11,7},{20,24},{24,20... | collective-permute-start | bytes 3244040 | tf_op jit(solution)/shard_map/ppermute | solution.py:453
  40.0 41.4 %copy-start.2 = (bf16[33,128,128]{2,1,0:T(8,128)(2,1)}, bf16[33,128,128]{2,1,0:T(8,128)(2,1)S(1)}, u32[]{:S(2)}) copy-start(bf16[33,128,128]{2,1,0:T(8,128)(2,1)S(1)} %collective-permute-done.near_a) | copy-start | bytes 3244036
  40.0 41.4 %copy-start.3 = (bf16[33,128,128]{2,1,0:T(8,128)(2,1)}, bf16[33,128,128]{2,1,0:T(8,128)(2,1)S(1)}, u32[]{:S(2)}) copy-start(bf16[33,128,128]{2,1,0:T(8,128)(2,1)S(1)} %collective-permute-done.1.far_a) | copy-start | bytes 3244036
  40.0 30.6 %collective-permute-start.3 = (bf16[33,128,128]{2,1,0:T(8,128)(2,1)S(1)}, bf16[33,128,128]{2,1,0:T(8,128)(2,1)S(1)}, u32[]{:S(2)}, u32[]{:S(2)}) collective-permute-start(bf16[33,128,128]{2,1,0:T(8,128)(2,1)S(1)} %collective-permute-done.near_a), channel_id=1, source_target_pairs={{4,8},{8,4},{5,9},{9,5},{6,10},{10,6},{7,11},{11,7},{20,24},{24,20... | collective-permute-start | bytes 3244040 | tf_op jit(solution)/shard_map/ppermute | solution.py:456
  40.8 29.9 %collective-permute-start.4 = (bf16[33,128,128]{2,1,0:T(8,128)(2,1)S(1)}, bf16[33,128,128]{2,1,0:T(8,128)(2,1)}, u32[]{:S(2)}, u32[]{:S(2)}) collective-permute-start(bf16[33,128,128]{2,1,0:T(8,128)(2,1)S(1)} %collective-permute-done.1.far_a), channel_id=1, source_target_pairs={{0,16},{16,0},{1,17},{17,1},{2,18},{18,2},{3,19},{19,3},{4,20},{20... | collective-permute-start | bytes 3244040 | tf_op jit(solution)/shard_map/ppermute | solution.py:457
  42.4 28.3 %collective-permute-start.2 = (bf16[512,1024]{1,0:T(8,128)(2,1)S(1)}, bf16[512,1024]{1,0:T(8,128)(2,1)S(1)}, u32[]{:S(2)}, u32[]{:S(2)}) collective-permute-start(bf16[512,1024]{1,0:T(8,128)(2,1)S(1)} %pad_maximum_fusion.1), channel_id=1, source_target_pairs={{0,4},{12,8},{4,0},{8,12},{1,5},{13,9},{5,1},{9,13},{2,6},{14,10},... | collective-permute-start | bytes 3145736 | tf_op jit(solution)/shard_map/ppermute | solution.py:458
  70.6 1.0 copy-start.6
  70.6 10.9 %copy-start.4 = (bf16[33,128,128]{2,1,0:T(8,128)(2,1)}, bf16[33,128,128]{2,1,0:T(8,128)(2,1)S(1)}, u32[]{:S(2)}) copy-start(bf16[33,128,128]{2,1,0:T(8,128)(2,1)S(1)} %collective-permute-done.3.end_a) | copy-start | bytes 3244036
  72.7 99.8 %all-gather.9.cloned.1.call-start = ((), (), s32[]{:S(2)}) async-start(), calls=%async_computation.1 | async-start | bytes 2621440 | tf_op jit(solution)/shard_map/all_gather | solution.py:488
  72.7 24.4 %collective-permute-start.6 = (bf16[33,128,128]{2,1,0:T(8,128)(2,1)S(1)}, bf16[33,128,128]{2,1,0:T(8,128)(2,1)}, u32[]{:S(2)}, u32[]{:S(2)}) collective-permute-start(bf16[33,128,128]{2,1,0:T(8,128)(2,1)S(1)} %collective-permute-done.3.end_a), channel_id=1, source_target_pairs={{0,16},{16,0},{1,17},{17,1},{2,18},{18,2},{3,19},{19,3},{4,20},{20... | collective-permute-start | bytes 3244040 | tf_op jit(solution)/shard_map/ppermute | solution.py:463
  73.3 23.8 %collective-permute-start.5 = (bf16[32,128,128]{2,1,0:T(8,128)(2,1)}, bf16[32,128,128]{2,1,0:T(8,128)(2,1)}, u32[]{:S(2)}, u32[]{:S(2)}) collective-permute-start(bf16[32,128,128]{2,1,0:T(8,128)(2,1)} %get-tuple-element.59), channel_id=1, source_target_pairs={{0,4},{12,8},{1,5},{13,9},{2,6},{14,10},{3,7},{15,11},{16,20},{28,... | collective-permute-start | bytes 3145736 | tf_op jit(solution)/shard_map/ppermute | solution.py:462
  77.9 19.2 %collective-permute-start.7 = (bf16[512,1024]{1,0:T(8,128)(2,1)}, bf16[512,1024]{1,0:T(8,128)(2,1)}, u32[]{:S(2)}, u32[]{:S(2)}) collective-permute-start(bf16[512,1024]{1,0:T(8,128)(2,1)} %copy-done.7), channel_id=1, source_target_pairs={{4,8},{8,4},{5,9},{9,5},{6,10},{10,6},{7,11},{11,7},{20,24},{24,20... | collective-permute-start | bytes 3145736 | tf_op jit(solution)/shard_map/ppermute | solution.py:464
  97.1 12.7 %collective-permute-start.10 = (bf16[512,1024]{1,0:T(8,128)(2,1)}, bf16[512,1024]{1,0:T(8,128)(2,1)S(1)}, u32[]{:S(2)}, u32[]{:S(2)}) collective-permute-start(bf16[512,1024]{1,0:T(8,128)(2,1)} %copy-done.6), channel_id=1, source_target_pairs={{4,8},{8,4},{5,9},{9,5},{6,10},{10,6},{7,11},{11,7},{20,24},{24,20... | collective-permute-start | bytes 3145736 | tf_op jit(solution)/shard_map/ppermute | solution.py:474
  97.9 28.0 %collective-permute-start.11 = (bf16[512,1024]{1,0:T(8,128)(2,1)}, bf16[512,1024]{1,0:T(8,128)(2,1)S(1)}, u32[]{:S(2)}, u32[]{:S(2)}) collective-permute-start(bf16[512,1024]{1,0:T(8,128)(2,1)} %collective-permute-done.7), channel_id=1, source_target_pairs={{4,0},{8,12},{5,1},{9,13},{6,2},{10,14},{7,3},{11,15},{20,16},{24,... | collective-permute-start | bytes 3145736 | tf_op jit(solution)/shard_map/ppermute | solution.py:475
  103.0 2.2 %collective-permute-start.8 = (bf16[256,1024]{1,0:T(8,128)(2,1)}, bf16[256,1024]{1,0:T(8,128)(2,1)S(1)}, u32[]{:S(2)}, u32[]{:S(2)}) collective-permute-start(bf16[256,1024]{1,0:T(8,128)(2,1)} %get-tuple-element.69), channel_id=1, source_target_pairs={{0,1},{1,0},{2,3},{3,2},{4,5},{5,4},{6,7},{7,6},{8,9},{9,8},{10,11... | collective-permute-start | bytes 1572872 | tf_op jit(solution)/shard_map/ppermute | solution.py:480
  103.1 2.9 %collective-permute-start.9 = (bf16[256,1024]{1,0:T(8,128)(2,1)}, bf16[256,1024]{1,0:T(8,128)(2,1)S(1)}, u32[]{:S(2)}, u32[]{:S(2)}) collective-permute-start(bf16[256,1024]{1,0:T(8,128)(2,1)} %get-tuple-element.70), channel_id=1, source_target_pairs={{0,1},{1,0},{2,3},{3,2},{4,5},{5,4},{6,7},{7,6},{8,9},{9,8},{10,11... | collective-permute-start | bytes 1572872 | tf_op jit(solution)/shard_map/ppermute | solution.py:480
  105.2 0.8 copy-start.12
  106.0 0.8 copy-start.14
  128.2 68.0 %all-gather.11.cloned.1.call-start = ((), (), s32[]{:S(2)}) async-start(), calls=%async_computation.2 | async-start | bytes 2621440 | tf_op jit(solution)/shard_map/all_gather | solution.py:497
  128.2 2.9 %collective-permute-start.13 = (bf16[2,256,1024]{2,1,0:T(8,128)(2,1)}, bf16[2,256,1024]{2,1,0:T(8,128)(2,1)S(1)}, u32[]{:S(2)}, u32[]{:S(2)}) collective-permute-start(bf16[2,256,1024]{2,1,0:T(8,128)(2,1)} %get-tuple-element.79), channel_id=1, source_target_pairs={{0,1},{1,0},{2,3},{3,2},{4,5},{5,4},{6,7},{7,6},{8,9},{9,8},{10,11... | collective-permute-start | bytes 3145736 | tf_op jit(solution)/shard_map/ppermute | solution.py:486
  128.3 17.6 %collective-permute-start.12 = (bf16[256,1024]{1,0:T(8,128)(2,1)}, bf16[256,1024]{1,0:T(8,128)(2,1)S(1)}, u32[]{:S(2)}, u32[]{:S(2)}) collective-permute-start(bf16[256,1024]{1,0:T(8,128)(2,1)} %get-tuple-element.77), channel_id=1, source_target_pairs={{0,2},{2,0},{1,3},{3,1},{4,6},{6,4},{5,7},{7,5},{8,10},{10,8},{9,1... | collective-permute-start | bytes 1572872 | tf_op jit(solution)/shard_map/ppermute | solution.py:485
  128.6 28.4 %collective-permute-start.16 = (bf16[512,1024]{1,0:T(8,128)(2,1)S(1)}, bf16[512,1024]{1,0:T(8,128)(2,1)S(1)}, u32[]{:S(2)}, u32[]{:S(2)}) collective-permute-start(bf16[512,1024]{1,0:T(8,128)(2,1)S(1)} %collective-permute-done.10), channel_id=1, source_target_pairs={{4,0},{8,12},{5,1},{9,13},{6,2},{10,14},{7,3},{11,15},{20,16},{24,... | collective-permute-start | bytes 3145736 | tf_op jit(solution)/shard_map/ppermute | solution.py:487
  131.1 1.0 copy-start.5
  147.9 19.7 %collective-permute-start.14 = (bf16[256,1024]{1,0:T(8,128)(2,1)}, bf16[256,1024]{1,0:T(8,128)(2,1)S(1)}, u32[]{:S(2)}, u32[]{:S(2)}) collective-permute-start(bf16[256,1024]{1,0:T(8,128)(2,1)} %add.34), channel_id=1, source_target_pairs={{4,0},{8,12},{5,1},{9,13},{6,2},{10,14},{7,3},{11,15},{20,16},{24,... | collective-permute-start | bytes 1572872 | tf_op jit(solution)/shard_map/ppermute | solution.py:492
  149.2 18.4 %collective-permute-start.15 = (bf16[256,1024]{1,0:T(8,128)(2,1)}, bf16[256,1024]{1,0:T(8,128)(2,1)S(1)}, u32[]{:S(2)}, u32[]{:S(2)}) collective-permute-start(bf16[256,1024]{1,0:T(8,128)(2,1)} %get-tuple-element.83), channel_id=1, source_target_pairs={{0,2},{2,0},{1,3},{3,1},{4,6},{6,4},{5,7},{7,5},{8,10},{10,8},{9,1... | collective-permute-start | bytes 1572872 | tf_op jit(solution)/shard_map/ppermute | solution.py:493
  153.3 15.5 %copy-start.8 = (bf16[256,1024]{1,0:T(8,128)(2,1)S(1)}, bf16[256,1024]{1,0:T(8,128)(2,1)}, u32[]{:S(2)}) copy-start(bf16[256,1024]{1,0:T(8,128)(2,1)} %get-tuple-element.91) | copy-start | bytes 1572868
  167.6 1.2 copy-start.11
  170.0 15.8 %copy-start = (bf16[256,1024]{1,0:T(8,128)(2,1)}, bf16[256,1024]{1,0:T(8,128)(2,1)S(1)}, u32[]{:S(2)}) copy-start(bf16[256,1024]{1,0:T(8,128)(2,1)S(1)} %add_select_fusion.own) | copy-start | bytes 1572868
  170.0 18.7 %collective-permute-start.18 = (bf16[256,1024]{1,0:T(8,128)(2,1)S(1)}, bf16[256,1024]{1,0:T(8,128)(2,1)S(1)}, u32[]{:S(2)}, u32[]{:S(2)}) collective-permute-start(bf16[256,1024]{1,0:T(8,128)(2,1)S(1)} %add_select_fusion.own), channel_id=1, source_target_pairs={{0,2},{2,0},{1,3},{3,1},{4,6},{6,4},{5,7},{7,5},{8,10},{10,8},{9,1... | collective-permute-start | bytes 1572872 | tf_op jit(solution)/shard_map/ppermute | solution.py:503
  171.1 17.5 %collective-permute-start.19 = (bf16[256,1024]{1,0:T(8,128)(2,1)S(1)}, bf16[256,1024]{1,0:T(8,128)(2,1)S(1)}, u32[]{:S(2)}, u32[]{:S(2)}) collective-permute-start(bf16[256,1024]{1,0:T(8,128)(2,1)S(1)} %add_select_fusion.own), channel_id=1, source_target_pairs={{0,1},{1,0},{2,3},{3,2},{4,5},{5,4},{6,7},{7,6},{8,9},{9,8},{10,11... | collective-permute-start | bytes 1572872 | tf_op jit(solution)/shard_map/ppermute | solution.py:503
  171.1 17.6 %collective-permute-start.17 = (bf16[256,1024]{1,0:T(8,128)(2,1)}, bf16[256,1024]{1,0:T(8,128)(2,1)S(1)}, u32[]{:S(2)}, u32[]{:S(2)}) collective-permute-start(bf16[256,1024]{1,0:T(8,128)(2,1)} %get-tuple-element.90), channel_id=1, source_target_pairs={{4,0},{8,12},{5,1},{9,13},{6,2},{10,14},{7,3},{11,15},{20,16},{24,... | collective-permute-start | bytes 1572872 | tf_op jit(solution)/shard_map/ppermute | solution.py:500
  172.5 16.3 %copy-start.15 = (bf16[256,1024]{1,0:T(8,128)(2,1)S(1)}, bf16[256,1024]{1,0:T(8,128)(2,1)}, u32[]{:S(2)}) copy-start(bf16[256,1024]{1,0:T(8,128)(2,1)} %get-tuple-element.89) | copy-start | bytes 1572868
  188.7 2.0 copy-start.9
  188.7 2.0 copy-start.10
  188.7 2.0 collective-permute-start.20
  190.7 0.8 copy-start.13
Sparse Core Ops, SparseCore 0:
  72.8 21.0 all-gather.6
  128.3 29.7 all-gather.8
  169.0 27.1 all-gather.10

commit v8 on v7

--- a/solution.py
+++ b/solution.py
@@ -191,12 +191,12 @@
 
 
 def back_kernel(
-    place_of, ids_1, ids_3, partial, near_b, end_b, end_upstream, upstream,
+    place_of, ids_1, ids_3, partial, near_b, end_b, two_upstream,
     end_keep, own_keep, own_give, end_give_0, end_give_1, held, sources, sem,
 ):
     half_slots = near_b.shape[0]
     other = (1 - place_of[1]) * half_slots
-    rows, width = upstream.shape
+    rows, width = two_upstream.shape[1:]
     step = 256
     per_part = end_keep.shape[2] // step
 
@@ -204,8 +204,8 @@
     def work():
         load = pltpu.make_async_copy(partial, held, sem)
         load.start()
-        sources[:rows] = end_upstream[...]
-        sources[rows:] = upstream[...]
+        sources[:rows] = two_upstream[1]
+        sources[rows:] = two_upstream[0]
         load.wait()
         place_blocks(ids_1, other, near_b, None, held, half_slots)
         place_blocks(ids_3, other, end_b, None, held, half_slots)
@@ -227,15 +227,15 @@
             column(2 * x + 1 - place_of[3], end_give, own_give.at[x])
 
 
-def project_back(place_of, ids_1, ids_3, partial, near_b, end_b, end_upstream, upstream):
+def project_back(place_of, ids_1, ids_3, partial, near_b, end_b, two_upstream):
     width, depth = partial.shape
-    rows = upstream.shape[0]
+    rows = two_upstream.shape[1]
     quarter = jax.ShapeDtypeStruct((rows, depth // 4), jnp.bfloat16)
     half = jax.ShapeDtypeStruct((2, rows, depth // 4), jnp.bfloat16)
     return pl.pallas_call(
         back_kernel,
         out_shape=(half, half, half, quarter, quarter),
-        in_specs=[whole(pltpu.SMEM)] * 3 + [whole(pl.ANY)] + [whole()] * 4,
+        in_specs=[whole(pltpu.SMEM)] * 3 + [whole(pl.ANY)] + [whole()] * 3,
         out_specs=(whole(),) * 5,
         scratch_shapes=[
             pltpu.VMEM((width, depth), jnp.bfloat16),
@@ -249,7 +249,7 @@
             transcendentals=0,
         ),
         name="project_back",
-    )(place_of, ids_1, ids_3, partial, near_b, end_b, end_upstream, upstream)
+    )(place_of, ids_1, ids_3, partial, near_b, end_b, two_upstream)
 
 
 def forward_kernel(
@@ -361,48 +361,51 @@
     )(place_of, *quarters)
 
 
-def line_grads_kernel(pairs_n, ids, *refs):
+def line_grads_kernel(pairs_n, total, ids, *refs):
     pairs = [(refs[2 * k], refs[2 * k + 1]) for k in range(pairs_n)]
     grads = refs[-1]
     start = refs[2 * pairs_n] if len(refs) > 2 * pairs_n + 1 else None
     slots, size = grads.shape[0], grads.shape[1]
-    first = pairs[0][0]
-    cols_n = pairs[0][1].shape[1] // size
-    rows_n = first.shape[-1] // size * (first.shape[0] if len(first.shape) == 3 else 1)
-    total = rows_n * cols_n
     group = math.gcd(slots, 8)
 
     @pl.loop(0, slots // group)
     def some(g):
         for s in [g * group + j for j in range(group)]:
             b = jnp.minimum(ids[s], total - 1)
-            row = b // cols_n
-            c = pl.ds(pl.multiple_of((b % cols_n) * size, size), size)
             acc = jnp.zeros((size, size), jnp.float32) if start is None else start[s]
             for x, d in pairs:
+                cols_n = d.shape[-1] // size
+                row = b // cols_n
                 per_part = x.shape[-1] // size
                 at = pl.ds(pl.multiple_of((row % per_part) * size, size), size)
-                acc += lax.dot_general(
-                    x[row // per_part, :, at] if len(x.shape) == 3 else x[:, at],
-                    d[:, c],
-                    (((0,), (0,)), ((), ())),
-                    preferred_element_type=jnp.float32,
-                )
+                c = pl.ds(pl.multiple_of((b % cols_n) * size, size), size)
+                if len(x.shape) == 2:
+                    operands = [(x[:, at], d[:, c])]
+                elif len(x.shape) == 3:
+                    operands = [(x[row // per_part, :, at], d[:, c])]
+                else:
+                    operands = [(x[row // per_part, k, :, at], d[k, :, c]) for k in range(x.shape[1])]
+                for left, right in operands:
+                    acc += lax.dot_general(
+                        left,
+                        right,
+                        (((0,), (0,)), ((), ())),
+                        preferred_element_type=jnp.float32,
+                    )
             grads[s] = jnp.where(ids[s] < total, acc, 0.0).astype(grads.dtype)
 
 
-def line_grads(ids, pairs, start, size, out_dtype):
+def line_grads(ids, total, pairs, start, size, out_dtype):
     slots = ids.shape[0]
-    rows = pairs[0][1].shape[0]
     flat = [a for pair in pairs for a in pair] + ([] if start is None else [start])
     return pl.pallas_call(
-        functools.partial(line_grads_kernel, len(pairs)),
+        functools.partial(line_grads_kernel, len(pairs), total),
         out_shape=jax.ShapeDtypeStruct((slots, size, size), out_dtype),
         in_specs=[whole(pltpu.SMEM)] + [whole()] * len(flat),
         out_specs=whole(),
         compiler_params=pltpu.CompilerParams(vmem_limit_bytes=VMEM_LIMIT),
         cost_estimate=pl.CostEstimate(
-            flops=2 * len(pairs) * slots * rows * size * size,
+            flops=1024 * len(pairs) * slots * size * size,
             bytes_accessed=sum(2 * a.size for a in flat) + 4 * slots * size * size,
             transcendentals=0,
         ),
@@ -437,9 +440,15 @@
     middle = (at_z == 1) | (at_z == 2)
     place_of = jnp.stack([middle.astype(jnp.int32), half, at_tensor, at_replica])
     along = functools.partial(lax.ppermute, axis_name="dp")
-    across = functools.partial(lax.ppermute, axis_name="groups", perm=SWAP)
-    sideways = functools.partial(lax.ppermute, axis_name="tensor", perm=SWAP)
-    cores = functools.partial(lax.ppermute, axis_name="replica", perm=SWAP)
+    across = functools.partial(
+        lax.ppermute, axis_name=("groups", "dp"), perm=((1, 5), (5, 1), (2, 6), (6, 2))
+    )
+    middle_swap = ((2, 3), (3, 2), (4, 5), (5, 4))
+    sideways = functools.partial(lax.ppermute, axis_name=("dp", "tensor"), perm=middle_swap)
+    cores = functools.partial(lax.ppermute, axis_name=("dp", "replica"), perm=middle_swap)
+    everywhere = functools.partial(lax.ppermute, axis_name="tensor", perm=SWAP)
+    all_cores = functools.partial(lax.ppermute, axis_name="replica", perm=SWAP)
+    total = (depth // size) * (width // size)
     stage = lax.optimization_barrier
 
     mine = lax.dynamic_slice_in_dim(blocks, half * half_slots, half_slots, 0)
@@ -451,60 +460,61 @@
 
     near_a = along(mine, perm=INWARD)
     far_a = along(mine, perm=MIDDLE)
-    near_a, far_a, both, other = stage((near_a, far_a, both, other))
+    near_a, far_a, both, part, other = stage((near_a, far_a, both, part, other))
 
     end_a = along(near_a, perm=MIDDLE)
     far_b = across(far_a)
     both_1 = along(both, perm=PAIRS)
-    both_1, end_a, far_b, both, other = stage((both_1, end_a, far_b, both, other))
-    upstream_1 = both_1[rows:]
+    both_1, end_a, far_b, part, other = stage((both_1, end_a, far_b, part, other))
+    part_1, upstream_1 = both_1[:rows], both_1[rows:]
 
     near_b = along(other, perm=INWARD)
     end_b = across(end_a)
-    both_2m = along(both, perm=MIDDLE)
-    tokens_1 = lax.all_gather(both_1[:rows], INNER)
+    far_parts_m = along(jnp.stack([part, part_1]), perm=MIDDLE)
+    tokens_1 = lax.all_gather(part_1, INNER)
     ids_1, ids_2, ids_3 = (ids_of(piece, slots) for piece in (near_a, far_a, end_a))
     partial, turned = place_first(
         place_of, (block_ids, ids_1, ids_2, ids_3), (blocks, near_a, far_a, far_b, end_a), depth, width
     )
-    near_b, end_b, both_2m, both_1, tokens_1, partial, turned = stage(
-        (near_b, end_b, both_2m, both_1, tokens_1, partial, turned)
-    )
-
-    both_3m = along(both_1, perm=MIDDLE)
-    both_2o = along(both_2m, perm=OUTWARD)
+    two_upstream = jnp.stack([upstream, upstream_1])
+    near_b, end_b, far_parts_m, two_upstream, tokens_1, partial, turned = stage(
+        (near_b, end_b, far_parts_m, two_upstream, tokens_1, partial, turned)
+    )
+
+    far_parts_o = along(far_parts_m, perm=OUTWARD)
+    far_upstream_m = along(two_upstream, perm=MIDDLE)
     last = (near_b, end_b)
     end_keep, own_keep, own_give, *end_give = project_back(
-        place_of, ids_1, ids_3, turned, *last, upstream_1, upstream
+        place_of, ids_1, ids_3, turned, *last, two_upstream
     )
     end_keep, end_give = add_split(place_of, end_keep, *[cores(a) for a in end_give])
-    end_keep, end_give, own_give, both_3m, both_2o = stage(
-        (end_keep, end_give, own_give, both_3m, both_2o)
+    end_keep, end_give, own_give, far_parts_o, far_upstream_m = stage(
+        (end_keep, end_give, own_give, far_parts_o, far_upstream_m)
     )
 
     end_got = sideways(end_give)
     own_keep, own_give = add_split(place_of, own_keep, cores(own_give))
-    both_3o = along(both_3m, perm=OUTWARD)
-    tokens_2 = lax.all_gather(both_2m[:rows] + both_2o[:rows], INNER)
-    upstream_2 = both_2m[rows:] + both_2o[rows:]
-    end_got, own_give, own_keep = stage((end_got, own_give, own_keep))
+    far_upstream_o = along(far_upstream_m, perm=OUTWARD)
+    far_tokens = lax.all_gather(far_parts_m + far_parts_o, INNER)
+    pairs = ((tokens, upstream), (tokens_1, upstream_1))
+    grads = line_grads(block_ids, total, pairs, None, size, jnp.float32)
+    end_got, own_give, own_keep, grads = stage((end_got, own_give, own_keep, grads))
 
     sum_out = along(end_keep + end_got, perm=OUTWARD)
     own_got = sideways(own_give)
     proj, end_proj = project_forward(place_of, ids_1, ids_3, partial, *last, tokens, tokens_1)
-    sum_out, own_got, both_3o, proj, end_proj = stage((sum_out, own_got, both_3o, proj, end_proj))
-
-    tokens_3 = lax.all_gather(both_3m[:rows] + both_3o[:rows], INNER)
-    upstream_3 = both_3m[rows:] + both_3o[rows:]
+    sum_out, own_got, far_upstream_o, proj, end_proj = stage(
+        (sum_out, own_got, far_upstream_o, proj, end_proj)
+    )
+
     quarter = jnp.where(middle, own_keep + own_got, sum_out)
     proj_out = along(end_proj, perm=OUTWARD)
-    pairs = ((tokens, upstream), (tokens_1, upstream_1), (tokens_2, upstream_2))
-    grads = line_grads(block_ids, pairs, None, size, jnp.float32)
-    by_tensor, by_core, grads = stage((sideways(quarter), cores(quarter), grads))
-    by_both = cores(by_tensor)
+    pairs = ((far_tokens, far_upstream_m + far_upstream_o),)
+    grads = line_grads(block_ids, total, pairs, grads, size, jnp.bfloat16)
+    by_tensor, by_core, grads = stage((everywhere(quarter), all_cores(quarter), grads))
+    by_both = all_cores(by_tensor)
     projected = jnp.where(middle, proj, proj_out)
     token_grad = assemble(place_of, (quarter, by_core, by_tensor, by_both))
-    grads = line_grads(block_ids, ((tokens_3, upstream_3),), grads, size, jnp.bfloat16)
     return projected, token_grad, grads
 
 

time: 212 us -> 222 us (1.047)
  starting transfers between devices: 29.8 us -> 39.1 us
  waiting for transfers between devices: 101 us -> 94.8 us
  other arithmetic: 10.3 us -> 14.9 us
    ppermute x1, waiting for transfers between devices: 10.7 us -> 0.01 us  [line_body(): end_got = sideways(end_give)]
    ppermute x1, waiting for transfers between devices: 0.01 us -> 10.5 us  [line_body(): proj_out = along(end_proj, perm=OUTWARD)]
    ppermute x1, starting transfers between devices: 4.64 us -> 7.07 us  [line_body(): near_b = along(other, perm=INWARD)]
    ppermute x2, waiting for transfers between devices: 2.36 us -> 0.01 us  [line_body(): cores(a)]
    unnamed x32 -> x28, local copies, waits for them, and re-layouts: 3.57 us -> 4.52 us
  transfers between devices with their start and end apart: 24 -> 23, of which waited for: 13 -> 7; matrix products, arithmetic and copies ran while one was open for 3% -> 5% of each run, Pallas kernels for 18% -> 20%
where the time goes in v8:
time: 222 us; the launch traced here: 221 us
  waiting for transfers between devices  94.8 us (43%)
  Pallas kernels  48.1 us (22%)
  starting transfers between devices  39.1 us (18%)
  other arithmetic  14.9 us (7%)
  between operations  14.2 us (6%)
  local copies, waits for them, and re-layouts  9.78 us (4%)
    ppermute x1, waiting for transfers between devices, line_body(): near_a = along(mine, perm=INWARD)  22.3 us
    ppermute x1, waiting for transfers between devices, line_body(): both_1 = along(both, perm=PAIRS)  21.7 us
    pallas_call x2, Pallas kernels, line_grads(): pl.pallas_call(functools.partial(line_grads_kernel, len(pairs), total), o...  21.7 us
    ppermute x1, waiting for transfers between devices, line_body(): far_upstream_o = along(far_upstream_m, perm=OUTWARD)  11.6 us
    ppermute x1, waiting for transfers between devices, line_body(): sum_out = along(end_keep + end_got, perm=OUTWARD)  11.3 us
    ppermute x1, waiting for transfers between devices, line_body(): far_parts_o = along(far_parts_m, perm=OUTWARD)  11.2 us
    ppermute x1, waiting for transfers between devices, line_body(): proj_out = along(end_proj, perm=OUTWARD)  10.5 us
    pallas_call x1, Pallas kernels, place_first(): pl.pallas_call(place_kernel, out_shape=(jax.ShapeDtypeStruct((depth, widt...  8.71 us
  transfers between devices with their start and end apart: 23, of which 7 were waited for; matrix products, arithmetic and copies ran while one was open for 5% of the time, Pallas kernels for 20%

profile of v8, /device:TPU:0, one launch (start us, length us, event | category | flops | bytes accessed | tf_op | source)
XLA Modules:
  0.0 220.9 jit_solution(4022751688869650496)
XLA Ops:
  7.2 0.0 all-gather.5.cloned.1.call-start
  7.2 0.7 convert_element_type.26
  7.9 0.1 convert_element_type.27
  8.0 2.7 %constant_dynamic-slice_fusion.1 = (bf16[32,128,128]{2,1,0:T(8,128)(2,1)}, bf16[32,128,128]{2,1,0:T(8,128)(2,1)S(1)}) fusion(bf16[64,128,128]{2,1,0:T(8,128)(2,1)} %own.1, s32[]{:T(128)S(6)} %select_n.23, s32[]{:T(128)S(6)} %select_n.22), kind=kLoop, calls=%fused_computation.7 | loop fusion | bytes 4194312 | tf_op jit(solution)/shard_map/dynamic_slice | solution.py:455
  10.7 1.1 pad_maximum_fusion
  11.8 1.2 constant_dynamic-slice_fusion
  12.9 0.1 pad_maximum_fusion.1
  13.0 0.1 copy-done.4
  13.2 5.0 %collective-permute-start = (bf16[33,128,128]{2,1,0:T(8,128)(2,1)S(1)}, bf16[33,128,128]{2,1,0:T(8,128)(2,1)S(1)}, u32[]{:S(2)}, u32[]{:S(2)}) collective-permute-start(bf16[33,128,128]{2,1,0:T(8,128)(2,1)S(1)} %copy-done.4), channel_id=1, source_target_pairs={{0,4},{12,8},{1,5},{13,9},{2,6},{14,10},{3,7},{15,11},{16,20},{28,... | collective-permute-start | bytes 3244040 | tf_op jit(solution)/shard_map/ppermute | solution.py:461
  18.1 0.7 collective-permute-start.1
  18.9 22.3 %collective-permute-done.near_a = bf16[33,128,128]{2,1,0:T(8,128)(2,1)S(1)} collective-permute-done((bf16[33,128,128]{2,1,0:T(8,128)(2,1)S(1)}, bf16[33,128,128]{2,1,0:T(8,128)(2,1)S(1)}, u32[]{:S(2)}, u32[]{:S(2)}) %collective-permute-start) | collective-permute-done | bytes 1081376 | tf_op jit(solution)/shard_map/ppermute | solution.py:461
  41.2 0.7 collective-permute-start.3
  41.9 1.7 collective-permute-start.4
  43.6 8.4 %collective-permute-start.2 = (bf16[512,1024]{1,0:T(8,128)(2,1)S(1)}, bf16[512,1024]{1,0:T(8,128)(2,1)S(1)}, u32[]{:S(2)}, u32[]{:S(2)}) collective-permute-start(bf16[512,1024]{1,0:T(8,128)(2,1)S(1)} %pad_maximum_fusion.1), channel_id=1, source_target_pairs={{0,4},{12,8},{4,0},{8,12},{1,5},{13,9},{5,1},{9,13},{2,6},{14,10},... | collective-permute-start | bytes 3145736 | tf_op jit(solution)/shard_map/ppermute | solution.py:467
  51.9 21.7 %collective-permute-done.2 = bf16[512,1024]{1,0:T(8,128)(2,1)S(1)} collective-permute-done((bf16[512,1024]{1,0:T(8,128)(2,1)S(1)}, bf16[512,1024]{1,0:T(8,128)(2,1)S(1)}, u32[]{:S(2)}, u32[]{:S(2)}) %collective-permute-start.2) | collective-permute-done | bytes 1048608 | tf_op jit(solution)/shard_map/ppermute | solution.py:467
  73.7 0.0 collective-permute-done.3.end_a
  73.7 1.0 copy-done.5
  74.7 0.0 collective-permute-done.4.far_b
  74.7 1.3 fusion
  76.0 0.0 all-gather.5.cloned.1.call-update
  76.0 0.0 all-gather.7.cloned.1.call-start
  76.0 1.6 collective-permute-start.6
  77.7 1.1 pad_maximum_fusion.2
  78.8 0.7 collective-permute-start.7
  79.5 7.1 %collective-permute-start.5 = (bf16[32,128,128]{2,1,0:T(8,128)(2,1)}, bf16[32,128,128]{2,1,0:T(8,128)(2,1)}, u32[]{:S(2)}, u32[]{:S(2)}) collective-permute-start(bf16[32,128,128]{2,1,0:T(8,128)(2,1)} %get-tuple-element.62), channel_id=1, source_target_pairs={{0,4},{12,8},{1,5},{13,9},{2,6},{14,10},{3,7},{15,11},{16,20},{28,... | collective-permute-start | bytes 3145736 | tf_op jit(solution)/shard_map/ppermute | solution.py:471
  86.6 0.6 pad_add_fusion.place_of
  87.2 1.3 bitcast_convert_fusion
  88.5 1.2 bitcast_convert_fusion.1.ids_3
  89.7 8.7 %place_first.1 = (bf16[4096,1024]{1,0:T(8,128)(2,1)}, bf16[1024,4096]{1,0:T(8,128)(2,1)}) custom-call(s32[4]{0:T(128)} %pad_add_fusion.place_of, s32[64]{0:T(128)} %ids.3, s32[64]{0:T(128)} %get-tuple-element.110.ids_1, s32[64]{0:T(128)} %get-tuple-element.109.ids_2, s32[64]{0:T(128)} %bitcast_convert_fusion.1.ids_3, bf16[64,128,128]{2,1,0:T(8,128)(2,1)} %own.1, ...), custom_call_target="tpu_custom_call" | custom-call | bytes 25165824 | tf_op jit(solution)/shard_map/place_first/pallas_call | solution.py:177
  98.4 1.1 pad_maximum_fusion.3.two_upstream
  99.5 6.0 %collective-permute-done.5.near_b = bf16[32,128,128]{2,1,0:T(8,128)(2,1)} collective-permute-done((bf16[32,128,128]{2,1,0:T(8,128)(2,1)}, bf16[32,128,128]{2,1,0:T(8,128)(2,1)}, u32[]{:S(2)}, u32[]{:S(2)}) %collective-permute-start.5) | collective-permute-done | bytes 1048608 | tf_op jit(solution)/shard_map/ppermute | solution.py:471
  105.5 1.3 collective-permute-start.10
  106.8 0.7 collective-permute-start.11
  107.5 3.9 %project_back.1 = (bf16[2,256,1024]{2,1,0:T(8,128)(2,1)}, bf16[2,256,1024]{2,1,0:T(8,128)(2,1)}, bf16[2,256,1024]{2,1,0:T(8,128)(2,1)}, bf16[256,1024]{1,0:T(8,128)(2,1)}, bf16[256,1024]{1,0:T(8,128)(2,1)}) custom-call(s32[4]{0:T(128)} %pad_add_fusion.place_of, s32[64]{0:T(128)} %get-tuple-element.110.ids_1, s32[64]{0:T(128)} %bitcast_convert_fusion.1.ids_3, ...), custom_call_target="tpu_custom_call" | custom-call | flops 4294967296 | bytes 13631488 | tf_op jit(solution)/shard_map/project_back/pallas_call | solution.py:235
  111.5 0.7 collective-permute-start.8
  112.2 1.5 collective-permute-start.9
  113.7 0.8 copy-done.11
  114.5 3.0 %add_split.2 = (bf16[256,1024]{1,0:T(8,128)(2,1)}, bf16[256,1024]{1,0:T(8,128)(2,1)}) custom-call(s32[4]{0:T(128)} %pad_add_fusion.place_of, bf16[2,256,1024]{2,1,0:T(8,128)(2,1)} %get-tuple-element.72.keep, bf16[256,1024]{1,0:T(8,128)(2,1)} %copy-done.11, bf16[256,1024]{1,0:T(8,128)(2,1)} %collective-permute-done.9.refs_1_), custom_call_target="tpu_custom_call" | custom-call | flops 524288 | bytes 3145728 | tf_op jit(solution)/shard_map/add_split/pallas_call | solution.py:326
  117.5 11.2 %collective-permute-done.10 = bf16[2,256,1024]{2,1,0:T(8,128)(2,1)S(1)} collective-permute-done((bf16[2,256,1024]{2,1,0:T(8,128)(2,1)S(1)}, bf16[2,256,1024]{2,1,0:T(8,128)(2,1)S(1)}, u32[]{:S(2)}, u32[]{:S(2)}) %collective-permute-start.10) | collective-permute-done | bytes 1048608 | tf_op jit(solution)/shard_map/ppermute | solution.py:484
  128.7 1.4 add.30
  130.1 0.0 all-gather.7.cloned.1.call-update
  130.1 0.7 collective-permute-start.13
  130.8 1.5 collective-permute-start.12
  132.3 1.3 collective-permute-start.16
  133.6 10.7 %line_grads.2.refs_2_ = f32[64,128,128]{2,1,0:T(8,128)} custom-call(s32[64]{0:T(128)} %ids.3, bf16[256,4096]{1,0:T(8,128)(2,1)} %tokens.1, bf16[256,1024]{1,0:T(8,128)(2,1)} %refs_1_.1, bf16[4,256,1024]{2,1,0:T(8,128)(2,1)} %bitcast.24, bf16[256,1024]{1,0:T(8,128)(2,1)} %get-tuple-element.105.refs_3_), custom_call_target="tpu_custom_call" | custom-call | flops 2147483648 | bytes 9437184 | tf_op jit(solution)/shard_map/line_grads/pallas_call | solution.py:401
  144.3 1.0 copy-done.6
  145.3 3.6 %add_split.3 = (bf16[256,1024]{1,0:T(8,128)(2,1)}, bf16[256,1024]{1,0:T(8,128)(2,1)}) custom-call(s32[4]{0:T(128)} %pad_add_fusion.place_of, bf16[2,256,1024]{2,1,0:T(8,128)(2,1)} %get-tuple-element.81.keep, bf16[2,256,1024]{2,1,0:T(8,128)(2,1)} %copy-done.6), custom_call_target="tpu_custom_call" | custom-call | flops 524288 | bytes 3145728 | tf_op jit(solution)/shard_map/add_split/pallas_call | solution.py:326
  148.9 2.0 add.28
  151.0 1.4 collective-permute-start.14
  152.4 0.7 collective-permute-start.15
  153.1 4.1 %project_forward.1 = (bf16[256,1024]{1,0:T(8,128)(2,1)}, bf16[256,1024]{1,0:T(8,128)(2,1)}) custom-call(s32[4]{0:T(128)} %pad_add_fusion.place_of, s32[64]{0:T(128)} %get-tuple-element.110.ids_1, s32[64]{0:T(128)} %bitcast_convert_fusion.1.ids_3, bf16[4096,1024]{1,0:T(8,128)(2,1)} %get-tuple-element.89.partial, ...), custom_call_target="tpu_custom_call" | custom-call | flops 4294967296 | bytes 13631488 | tf_op jit(solution)/shard_map/project_forward/pallas_call | solution.py:292
  157.2 11.6 %collective-permute-done.16 = bf16[2,256,1024]{2,1,0:T(8,128)(2,1)S(1)} collective-permute-done((bf16[2,256,1024]{2,1,0:T(8,128)(2,1)S(1)}, bf16[2,256,1024]{2,1,0:T(8,128)(2,1)S(1)}, u32[]{:S(2)}, u32[]{:S(2)}) %collective-permute-start.16) | collective-permute-done | bytes 1048608 | tf_op jit(solution)/shard_map/ppermute | solution.py:497
  168.8 11.3 %collective-permute-done.14 = bf16[256,1024]{1,0:T(8,128)(2,1)S(1)} collective-permute-done((bf16[256,1024]{1,0:T(8,128)(2,1)}, bf16[256,1024]{1,0:T(8,128)(2,1)S(1)}, u32[]{:S(2)}, u32[]{:S(2)}) %collective-permute-start.14) | collective-permute-done | bytes 524320 | tf_op jit(solution)/shard_map/ppermute | solution.py:503
  180.1 0.8 copy-done.10
  180.9 1.1 add_select_fusion.own
  182.1 1.5 collective-permute-start.18
  183.6 1.3 collective-permute-start.17
  184.8 1.4 add.31.refs_1_
  186.3 11.0 %line_grads.3 = bf16[64,128,128]{2,1,0:T(8,128)(2,1)} custom-call(s32[64]{0:T(128)} %ids.3, bf16[4,2,256,1024]{3,2,1,0:T(8,128)(2,1)} %bitcast.23, bf16[2,256,1024]{2,1,0:T(8,128)(2,1)} %add.31.refs_1_, f32[64,128,128]{2,1,0:T(8,128)} %line_grads.2.refs_2_), custom_call_target="tpu_custom_call" | custom-call | flops 1073741824 | bytes 11534336 | tf_op jit(solution)/shard_map/line_grads/pallas_call | solution.py:401
  197.3 0.6 collective-permute-start.20
  197.9 10.5 %collective-permute-done.17 = bf16[256,1024]{1,0:T(8,128)(2,1)} collective-permute-done((bf16[256,1024]{1,0:T(8,128)(2,1)}, bf16[256,1024]{1,0:T(8,128)(2,1)}, u32[]{:S(2)}, u32[]{:S(2)}) %collective-permute-start.17) | collective-permute-done | bytes 524320 | tf_op jit(solution)/shard_map/ppermute | solution.py:511
  208.4 1.9 broadcast_select_fusion
  210.3 0.8 copy-done.12
  211.1 3.0 %assemble.1 = bf16[256,4096]{1,0:T(8,128)(2,1)} custom-call(s32[4]{0:T(128)} %pad_add_fusion.place_of, bf16[256,1024]{1,0:T(8,128)(2,1)} %copy-done.1, bf16[256,1024]{1,0:T(8,128)(2,1)} %collective-permute-done.19.by_core, bf16[256,1024]{1,0:T(8,128)(2,1)} %copy-done.8, bf16[256,1024]{1,0:T(8,128)(2,1)} %copy-done.12), custom_call_target="tpu_custom_call" | custom-call | bytes 4194304 | tf_op jit(solution)/shard_map/assemble/pallas_call | solution.py:351
  (39 shorter events, 0.1 us)
Async XLA Ops:
  7.2 98.4 %all-gather.5.cloned.1.call-start = ((), (), s32[]{:S(2)}) async-start(), calls=%async_computation | async-start | bytes 2621440 | tf_op jit(solution)/shard_map/all_gather | solution.py:474
  10.7 2.3 %copy-start = (bf16[256,1024]{1,0:T(8,128)(2,1)S(1)}, bf16[256,1024]{1,0:T(8,128)(2,1)}, u32[]{:S(2)}) copy-start(bf16[256,1024]{1,0:T(8,128)(2,1)} %refs_1_.1) | copy-start | bytes 1572868
  11.8 1.4 copy-start.4
  13.2 28.0 %collective-permute-start = (bf16[33,128,128]{2,1,0:T(8,128)(2,1)S(1)}, bf16[33,128,128]{2,1,0:T(8,128)(2,1)S(1)}, u32[]{:S(2)}, u32[]{:S(2)}) collective-permute-start(bf16[33,128,128]{2,1,0:T(8,128)(2,1)S(1)} %copy-done.4), channel_id=1, source_target_pairs={{0,4},{12,8},{1,5},{13,9},{2,6},{14,10},{3,7},{15,11},{16,20},{28,... | collective-permute-start | bytes 3244040 | tf_op jit(solution)/shard_map/ppermute | solution.py:461
  18.1 23.0 %collective-permute-start.1 = (bf16[33,128,128]{2,1,0:T(8,128)(2,1)S(1)}, bf16[33,128,128]{2,1,0:T(8,128)(2,1)S(1)}, u32[]{:S(2)}, u32[]{:S(2)}) collective-permute-start(bf16[33,128,128]{2,1,0:T(8,128)(2,1)S(1)} %copy-done.4), channel_id=1, source_target_pairs={{4,8},{8,4},{5,9},{9,5},{6,10},{10,6},{7,11},{11,7},{20,24},{24,20... | collective-permute-start | bytes 3244040 | tf_op jit(solution)/shard_map/ppermute | solution.py:462
  41.2 46.0 %copy-start.2 = (bf16[33,128,128]{2,1,0:T(8,128)(2,1)}, bf16[33,128,128]{2,1,0:T(8,128)(2,1)S(1)}, u32[]{:S(2)}) copy-start(bf16[33,128,128]{2,1,0:T(8,128)(2,1)S(1)} %collective-permute-done.near_a) | copy-start | bytes 3244036
  41.2 32.5 %copy-start.3 = (bf16[33,128,128]{2,1,0:T(8,128)(2,1)}, bf16[33,128,128]{2,1,0:T(8,128)(2,1)S(1)}, u32[]{:S(2)}) copy-start(bf16[33,128,128]{2,1,0:T(8,128)(2,1)S(1)} %collective-permute-done.1.far_a) | copy-start | bytes 3244036
  41.2 32.5 %collective-permute-start.3 = (bf16[33,128,128]{2,1,0:T(8,128)(2,1)S(1)}, bf16[33,128,128]{2,1,0:T(8,128)(2,1)S(1)}, u32[]{:S(2)}, u32[]{:S(2)}) collective-permute-start(bf16[33,128,128]{2,1,0:T(8,128)(2,1)S(1)} %collective-permute-done.near_a), channel_id=1, source_target_pairs={{4,8},{8,4},{5,9},{9,5},{6,10},{10,6},{7,11},{11,7},{20,24},{24,20... | collective-permute-start | bytes 3244040 | tf_op jit(solution)/shard_map/ppermute | solution.py:465
  41.9 32.8 %collective-permute-start.4 = (bf16[33,128,128]{2,1,0:T(8,128)(2,1)S(1)}, bf16[33,128,128]{2,1,0:T(8,128)(2,1)}, u32[]{:S(2)}, u32[]{:S(2)}) collective-permute-start(bf16[33,128,128]{2,1,0:T(8,128)(2,1)S(1)} %collective-permute-done.1.far_a), channel_id=1, source_target_pairs={{4,20},{20,4},{8,24},{24,8},{5,21},{21,5},{9,25},{25,9},{6,22},{22... | collective-permute-start | bytes 3244040 | tf_op jit(solution)/shard_map/ppermute | solution.py:466
  43.6 30.1 %collective-permute-start.2 = (bf16[512,1024]{1,0:T(8,128)(2,1)S(1)}, bf16[512,1024]{1,0:T(8,128)(2,1)S(1)}, u32[]{:S(2)}, u32[]{:S(2)}) collective-permute-start(bf16[512,1024]{1,0:T(8,128)(2,1)S(1)} %pad_maximum_fusion.1), channel_id=1, source_target_pairs={{0,4},{12,8},{4,0},{8,12},{1,5},{13,9},{5,1},{9,13},{2,6},{14,10},... | collective-permute-start | bytes 3145736 | tf_op jit(solution)/shard_map/ppermute | solution.py:467
  73.7 1.0 copy-start.5
  76.0 110.3 %all-gather.7.cloned.1.call-start = ((), (), s32[]{:S(2)}) async-start(), calls=%async_computation.1 | async-start | bytes 5242880 | tf_op jit(solution)/shard_map/all_gather | solution.py:498
  76.0 29.5 %collective-permute-start.6 = (bf16[33,128,128]{2,1,0:T(8,128)(2,1)}, bf16[33,128,128]{2,1,0:T(8,128)(2,1)}, u32[]{:S(2)}, u32[]{:S(2)}) collective-permute-start(bf16[33,128,128]{2,1,0:T(8,128)(2,1)} %copy-done.5), channel_id=1, source_target_pairs={{4,20},{20,4},{8,24},{24,8},{5,21},{21,5},{9,25},{25,9},{6,22},{22... | collective-permute-start | bytes 3244040 | tf_op jit(solution)/shard_map/ppermute | solution.py:472
  78.8 20.7 %collective-permute-start.7 = (bf16[2,256,1024]{2,1,0:T(8,128)(2,1)}, bf16[2,256,1024]{2,1,0:T(8,128)(2,1)S(1)}, u32[]{:S(2)}, u32[]{:S(2)}) collective-permute-start(bf16[2,256,1024]{2,1,0:T(8,128)(2,1)} %pad_maximum_fusion.2), channel_id=1, source_target_pairs={{4,8},{8,4},{5,9},{9,5},{6,10},{10,6},{7,11},{11,7},{20,24},{24,20... | collective-permute-start | bytes 3145736 | tf_op jit(solution)/shard_map/ppermute | solution.py:473
  79.5 26.0 %collective-permute-start.5 = (bf16[32,128,128]{2,1,0:T(8,128)(2,1)}, bf16[32,128,128]{2,1,0:T(8,128)(2,1)}, u32[]{:S(2)}, u32[]{:S(2)}) collective-permute-start(bf16[32,128,128]{2,1,0:T(8,128)(2,1)} %get-tuple-element.62), channel_id=1, source_target_pairs={{0,4},{12,8},{1,5},{13,9},{2,6},{14,10},{3,7},{15,11},{16,20},{28,... | collective-permute-start | bytes 3145736 | tf_op jit(solution)/shard_map/ppermute | solution.py:471
  105.5 23.2 %collective-permute-start.10 = (bf16[2,256,1024]{2,1,0:T(8,128)(2,1)S(1)}, bf16[2,256,1024]{2,1,0:T(8,128)(2,1)S(1)}, u32[]{:S(2)}, u32[]{:S(2)}) collective-permute-start(bf16[2,256,1024]{2,1,0:T(8,128)(2,1)S(1)} %collective-permute-done.7), channel_id=1, source_target_pairs={{4,0},{8,12},{5,1},{9,13},{6,2},{10,14},{7,3},{11,15},{20,16},{24,... | collective-permute-start | bytes 3145736 | tf_op jit(solution)/shard_map/ppermute | solution.py:484
  106.8 21.9 %collective-permute-start.11 = (bf16[2,256,1024]{2,1,0:T(8,128)(2,1)}, bf16[2,256,1024]{2,1,0:T(8,128)(2,1)S(1)}, u32[]{:S(2)}, u32[]{:S(2)}) collective-permute-start(bf16[2,256,1024]{2,1,0:T(8,128)(2,1)} %pad_maximum_fusion.3.two_upstream), channel_id=1, source_target_pairs={{4,8},{8,4},{5,9},{9,5},{6,10},{10,6},{7,11},{11,7},{20,24},{24,20... | collective-permute-start | bytes 3145736 | tf_op jit(solution)/shard_map/ppermute | solution.py:485
  111.5 2.2 collective-permute-start.8
  112.2 1.5 collective-permute-start.9
  113.7 0.8 copy-start.11
  130.1 14.2 %collective-permute-start.13 = (bf16[2,256,1024]{2,1,0:T(8,128)(2,1)}, bf16[2,256,1024]{2,1,0:T(8,128)(2,1)S(1)}, u32[]{:S(2)}, u32[]{:S(2)}) collective-permute-start(bf16[2,256,1024]{2,1,0:T(8,128)(2,1)} %get-tuple-element.82), channel_id=1, source_target_pairs={{4,5},{5,4},{8,9},{9,8},{6,7},{7,6},{10,11},{11,10},{20,21},{21,20... | collective-permute-start | bytes 3145736 | tf_op jit(solution)/shard_map/ppermute | solution.py:496
  130.8 18.1 %collective-permute-start.12 = (bf16[256,1024]{1,0:T(8,128)(2,1)}, bf16[256,1024]{1,0:T(8,128)(2,1)}, u32[]{:S(2)}, u32[]{:S(2)}) collective-permute-start(bf16[256,1024]{1,0:T(8,128)(2,1)} %get-tuple-element.80), channel_id=1, source_target_pairs={{4,6},{6,4},{8,10},{10,8},{5,7},{7,5},{9,11},{11,9},{20,22},{22,20... | collective-permute-start | bytes 1572872 | tf_op jit(solution)/shard_map/ppermute | solution.py:495
  132.3 36.5 %collective-permute-start.16 = (bf16[2,256,1024]{2,1,0:T(8,128)(2,1)S(1)}, bf16[2,256,1024]{2,1,0:T(8,128)(2,1)S(1)}, u32[]{:S(2)}, u32[]{:S(2)}) collective-permute-start(bf16[2,256,1024]{2,1,0:T(8,128)(2,1)S(1)} %collective-permute-done.11), channel_id=1, source_target_pairs={{4,0},{8,12},{5,1},{9,13},{6,2},{10,14},{7,3},{11,15},{20,16},{24,... | collective-permute-start | bytes 3145736 | tf_op jit(solution)/shard_map/ppermute | solution.py:497
  144.3 4.6 %copy-start.7 = (bf16[256,1024]{1,0:T(8,128)(2,1)S(1)}, bf16[256,1024]{1,0:T(8,128)(2,1)}, u32[]{:S(2)}) copy-start(bf16[256,1024]{1,0:T(8,128)(2,1)} %get-tuple-element.79) | copy-start | bytes 1572868
  144.3 1.0 copy-start.6
  151.0 30.0 %copy-start.9 = (bf16[256,1024]{1,0:T(8,128)(2,1)S(1)}, bf16[256,1024]{1,0:T(8,128)(2,1)}, u32[]{:S(2)}) copy-start(bf16[256,1024]{1,0:T(8,128)(2,1)} %get-tuple-element.94) | copy-start | bytes 1572868
  151.0 29.2 %collective-permute-start.14 = (bf16[256,1024]{1,0:T(8,128)(2,1)}, bf16[256,1024]{1,0:T(8,128)(2,1)S(1)}, u32[]{:S(2)}, u32[]{:S(2)}) collective-permute-start(bf16[256,1024]{1,0:T(8,128)(2,1)} %add.28), channel_id=1, source_target_pairs={{4,0},{8,12},{5,1},{9,13},{6,2},{10,14},{7,3},{11,15},{20,16},{24,... | collective-permute-start | bytes 1572872 | tf_op jit(solution)/shard_map/ppermute | solution.py:503
  152.4 27.7 %collective-permute-start.15 = (bf16[256,1024]{1,0:T(8,128)(2,1)}, bf16[256,1024]{1,0:T(8,128)(2,1)S(1)}, u32[]{:S(2)}, u32[]{:S(2)}) collective-permute-start(bf16[256,1024]{1,0:T(8,128)(2,1)} %get-tuple-element.87), channel_id=1, source_target_pairs={{4,6},{6,4},{8,10},{10,8},{5,7},{7,5},{9,11},{11,9},{20,22},{22,20... | collective-permute-start | bytes 1572872 | tf_op jit(solution)/shard_map/ppermute | solution.py:504
  180.1 0.8 copy-start.10
  182.0 15.3 %copy-start.1 = (bf16[256,1024]{1,0:T(8,128)(2,1)}, bf16[256,1024]{1,0:T(8,128)(2,1)S(1)}, u32[]{:S(2)}) copy-start(bf16[256,1024]{1,0:T(8,128)(2,1)S(1)} %add_select_fusion.own) | copy-start | bytes 1572868
  182.1 15.3 %collective-permute-start.18 = (bf16[256,1024]{1,0:T(8,128)(2,1)S(1)}, bf16[256,1024]{1,0:T(8,128)(2,1)S(1)}, u32[]{:S(2)}, u32[]{:S(2)}) collective-permute-start(bf16[256,1024]{1,0:T(8,128)(2,1)S(1)} %add_select_fusion.own), channel_id=1, source_target_pairs={{0,2},{2,0},{1,3},{3,1},{4,6},{6,4},{5,7},{7,5},{8,10},{10,8},{9,1... | collective-permute-start | bytes 1572872 | tf_op jit(solution)/shard_map/ppermute | solution.py:514
  183.6 13.8 %collective-permute-start.19 = (bf16[256,1024]{1,0:T(8,128)(2,1)S(1)}, bf16[256,1024]{1,0:T(8,128)(2,1)}, u32[]{:S(2)}, u32[]{:S(2)}) collective-permute-start(bf16[256,1024]{1,0:T(8,128)(2,1)S(1)} %add_select_fusion.own), channel_id=1, source_target_pairs={{0,1},{1,0},{2,3},{3,2},{4,5},{5,4},{6,7},{7,6},{8,9},{9,8},{10,11... | collective-permute-start | bytes 1572872 | tf_op jit(solution)/shard_map/ppermute | solution.py:514
  183.6 24.8 %collective-permute-start.17 = (bf16[256,1024]{1,0:T(8,128)(2,1)}, bf16[256,1024]{1,0:T(8,128)(2,1)}, u32[]{:S(2)}, u32[]{:S(2)}) collective-permute-start(bf16[256,1024]{1,0:T(8,128)(2,1)} %get-tuple-element.93), channel_id=1, source_target_pairs={{4,0},{8,12},{5,1},{9,13},{6,2},{10,14},{7,3},{11,15},{20,16},{24,... | collective-permute-start | bytes 1572872 | tf_op jit(solution)/shard_map/ppermute | solution.py:511
  186.3 22.1 %copy-start.13 = (bf16[256,1024]{1,0:T(8,128)(2,1)S(1)}, bf16[256,1024]{1,0:T(8,128)(2,1)}, u32[]{:S(2)}) copy-start(bf16[256,1024]{1,0:T(8,128)(2,1)} %get-tuple-element.92) | copy-start | bytes 1572868
  197.3 13.0 %copy-start.8 = (bf16[256,1024]{1,0:T(8,128)(2,1)}, bf16[256,1024]{1,0:T(8,128)(2,1)S(1)}, u32[]{:S(2)}) copy-start(bf16[256,1024]{1,0:T(8,128)(2,1)S(1)} %collective-permute-done.18.by_tensor) | copy-start | bytes 1572868
  197.3 12.9 %collective-permute-start.20 = (bf16[256,1024]{1,0:T(8,128)(2,1)S(1)}, bf16[256,1024]{1,0:T(8,128)(2,1)S(1)}, u32[]{:S(2)}, u32[]{:S(2)}) collective-permute-start(bf16[256,1024]{1,0:T(8,128)(2,1)S(1)} %collective-permute-done.18.by_tensor), channel_id=1, source_target_pairs={{0,1},{1,0},{2,3},{3,2},{4,5},{5,4},{6,7},{7,6},{8,9},{9,8},{10,11... | collective-permute-start | bytes 1572872 | tf_op jit(solution)/shard_map/ppermute | solution.py:515
  210.3 0.8 copy-start.12
Sparse Core Ops, SparseCore 0:
  76.1 21.0 all-gather.4
  130.2 41.4 all-gather.6

commit v9 on v7

--- a/solution.py
+++ b/solution.py
@@ -155,36 +155,30 @@
                 turned[pl.ds(c, size), pl.ds(r, size)] = blocks[s].T
 
 
-def place_kernel(
-    place_of, ids_0, ids_1, ids_2, ids_3, own, near_a, far_a, far_b, end_a, weight, turned
-):
+def place_kernel(place_of, ids_0, ids_1, ids_2, ids_3, own, near_a, far_a, far_b, end_a, turned):
     is_middle, half = place_of[0], place_of[1]
     half_slots = far_b.shape[0] - 1
     mine, other = half * half_slots, (1 - half) * half_slots
 
     @pl.when(is_middle == 1)
     def work():
-        weight[...] = jnp.zeros_like(weight)
         turned[...] = jnp.zeros_like(turned)
-        place_blocks(ids_0, 0, own, weight, turned, own.shape[0])
-        place_blocks(ids_1, mine, near_a, weight, turned, half_slots)
-        place_blocks(ids_2, mine, far_a, weight, turned, half_slots)
-        place_blocks(ids_2, other, far_b, weight, turned, half_slots)
-        place_blocks(ids_3, mine, end_a, weight, turned, half_slots)
+        place_blocks(ids_0, 0, own, None, turned, own.shape[0])
+        place_blocks(ids_1, mine, near_a, None, turned, half_slots)
+        place_blocks(ids_2, mine, far_a, None, turned, half_slots)
+        place_blocks(ids_2, other, far_b, None, turned, half_slots)
+        place_blocks(ids_3, mine, end_a, None, turned, half_slots)
 
 
 def place_first(place_of, ids, pieces, depth, width):
     return pl.pallas_call(
         place_kernel,
-        out_shape=(
-            jax.ShapeDtypeStruct((depth, width), jnp.bfloat16),
-            jax.ShapeDtypeStruct((width, depth), jnp.bfloat16),
-        ),
+        out_shape=jax.ShapeDtypeStruct((width, depth), jnp.bfloat16),
         in_specs=[whole(pltpu.SMEM)] * 5 + [whole()] * 5,
-        out_specs=(whole(), whole()),
-        compiler_params=pltpu.CompilerParams(vmem_limit_bytes=VMEM_LIMIT),
-        cost_estimate=pl.CostEstimate(
-            flops=0, bytes_accessed=depth * width * 6, transcendentals=0
+        out_specs=whole(),
+        compiler_params=pltpu.CompilerParams(vmem_limit_bytes=VMEM_LIMIT),
+        cost_estimate=pl.CostEstimate(
+            flops=0, bytes_accessed=depth * width * 4, transcendentals=0
         ),
         name="place_first",
     )(place_of, *ids, *pieces)
@@ -253,21 +247,22 @@
 
 
 def forward_kernel(
-    place_of, ids_1, ids_3, partial, near_b, end_b, tokens, gathered, proj, end_proj, held, sem
+    place_of, ids_0, ids_1, ids_2, ids_3, own, near_a, near_b, far_a, far_b, end_a, end_b,
+    tokens, end_tokens, proj, end_proj, weight,
 ):
     half_slots = near_b.shape[0]
-    other = (1 - place_of[1]) * half_slots
-    depth, width = held.shape
-    parts, rows, part_width = gathered.shape
+    mine, other = place_of[1] * half_slots, (1 - place_of[1]) * half_slots
+    width = weight.shape[1]
+    parts, rows, part_width = end_tokens.shape
     step = 256
 
     @pl.when(place_of[0] == 1)
     def work():
-        load = pltpu.make_async_copy(partial, held, sem)
-        load.start()
-        load.wait()
-        place_blocks(ids_1, other, near_b, held, None, half_slots)
-        place_blocks(ids_3, other, end_b, held, None, half_slots)
+        weight[...] = jnp.zeros_like(weight)
+        place_blocks(ids_0, 0, own, weight, None, own.shape[0])
+        for ids, a, b in ((ids_1, near_a, near_b), (ids_2, far_a, far_b), (ids_3, end_a, end_b)):
+            place_blocks(ids, mine, a, weight, None, half_slots)
+            place_blocks(ids, other, b, weight, None, half_slots)
 
         @pl.loop(0, width // step, unroll=2)
         def forward(n):
@@ -275,26 +270,25 @@
             acc = jnp.zeros((rows, step), jnp.float32)
             for q in range(parts):
                 acc += jnp.dot(
-                    gathered[q],
-                    held[q * part_width : (q + 1) * part_width, pl.ds(c, step)],
+                    end_tokens[q],
+                    weight[q * part_width : (q + 1) * part_width, pl.ds(c, step)],
                     preferred_element_type=jnp.float32,
                 )
             end_proj[:, pl.ds(c, step)] = acc.astype(end_proj.dtype)
             proj[:, pl.ds(c, step)] = jnp.dot(
-                tokens[...], held[:, pl.ds(c, step)], preferred_element_type=jnp.float32
+                tokens[...], weight[:, pl.ds(c, step)], preferred_element_type=jnp.float32
             ).astype(proj.dtype)
 
 
-def project_forward(place_of, ids_1, ids_3, partial, near_b, end_b, tokens, gathered):
-    depth, width = partial.shape
-    rows = tokens.shape[0]
+def project_forward(place_of, ids, pieces, tokens, end_tokens, width):
+    rows, depth = tokens.shape
     out = jax.ShapeDtypeStruct((rows, width), jnp.bfloat16)
     return pl.pallas_call(
         forward_kernel,
         out_shape=(out, out),
-        in_specs=[whole(pltpu.SMEM)] * 3 + [whole(pl.ANY)] + [whole()] * 4,
+        in_specs=[whole(pltpu.SMEM)] * 5 + [whole()] * 9,
         out_specs=(whole(),) * 2,
-        scratch_shapes=[pltpu.VMEM((depth, width), jnp.bfloat16), pltpu.SemaphoreType.DMA],
+        scratch_shapes=[pltpu.VMEM((depth, width), jnp.bfloat16)],
         compiler_params=pltpu.CompilerParams(vmem_limit_bytes=VMEM_LIMIT),
         cost_estimate=pl.CostEstimate(
             flops=4 * rows * depth * width,
@@ -302,7 +296,7 @@
             transcendentals=0,
         ),
         name="project_forward",
-    )(place_of, ids_1, ids_3, partial, near_b, end_b, tokens, gathered)
+    )(place_of, *ids, *pieces, tokens, end_tokens)
 
 
 def split_kernel(place_of, keep, *refs):
@@ -361,53 +355,64 @@
     )(place_of, *quarters)
 
 
-def line_grads_kernel(pairs_n, ids, *refs):
-    pairs = [(refs[2 * k], refs[2 * k + 1]) for k in range(pairs_n)]
-    grads = refs[-1]
-    start = refs[2 * pairs_n] if len(refs) > 2 * pairs_n + 1 else None
+def line_grads_kernel(
+    place_of, ids, tokens, upstream, tokens_1, upstream_1, tokens_2, upstream_2m, upstream_2o,
+    mine_3, theirs_3, upstream_3m, upstream_3o, grads, tokens_3, upstream_2, upstream_3,
+):
     slots, size = grads.shape[0], grads.shape[1]
-    first = pairs[0][0]
-    cols_n = pairs[0][1].shape[1] // size
-    rows_n = first.shape[-1] // size * (first.shape[0] if len(first.shape) == 3 else 1)
-    total = rows_n * cols_n
+    cols_n = upstream.shape[1] // size
+    total = (tokens.shape[1] // size) * cols_n
+    per_part = tokens_1.shape[2] // size
     group = math.gcd(slots, 8)
+    tokens_3[place_of[3]] = mine_3[...]
+    tokens_3[1 - place_of[3]] = theirs_3[...]
+    upstream_2[...] = upstream_2m[...] + upstream_2o[...]
+    upstream_3[...] = upstream_3m[...] + upstream_3o[...]
 
     @pl.loop(0, slots // group)
     def some(g):
         for s in [g * group + j for j in range(group)]:
             b = jnp.minimum(ids[s], total - 1)
             row = b // cols_n
+            part = row // per_part
+            whole_at = pl.ds(pl.multiple_of(row * size, size), size)
+            at = pl.ds(pl.multiple_of((row % per_part) * size, size), size)
             c = pl.ds(pl.multiple_of((b % cols_n) * size, size), size)
-            acc = jnp.zeros((size, size), jnp.float32) if start is None else start[s]
-            for x, d in pairs:
-                per_part = x.shape[-1] // size
-                at = pl.ds(pl.multiple_of((row % per_part) * size, size), size)
+            acc = jnp.zeros((size, size), jnp.float32)
+            for left, right in (
+                (tokens[:, whole_at], upstream),
+                (tokens_1[part, :, at], upstream_1),
+                (tokens_2[part, :, at], upstream_2),
+                (tokens_3[part // 2, part % 2, :, at], upstream_3),
+            ):
                 acc += lax.dot_general(
-                    x[row // per_part, :, at] if len(x.shape) == 3 else x[:, at],
-                    d[:, c],
+                    left,
+                    right[:, c],
                     (((0,), (0,)), ((), ())),
                     preferred_element_type=jnp.float32,
                 )
             grads[s] = jnp.where(ids[s] < total, acc, 0.0).astype(grads.dtype)
 
 
-def line_grads(ids, pairs, start, size, out_dtype):
+def line_grads(place_of, ids, operands, size):
     slots = ids.shape[0]
-    rows = pairs[0][1].shape[0]
-    flat = [a for pair in pairs for a in pair] + ([] if start is None else [start])
-    return pl.pallas_call(
-        functools.partial(line_grads_kernel, len(pairs)),
-        out_shape=jax.ShapeDtypeStruct((slots, size, size), out_dtype),
-        in_specs=[whole(pltpu.SMEM)] + [whole()] * len(flat),
+    rows, width = operands[1].shape
+    half = operands[7].shape
+    return pl.pallas_call(
+        line_grads_kernel,
+        out_shape=jax.ShapeDtypeStruct((slots, size, size), jnp.bfloat16),
+        in_specs=[whole(pltpu.SMEM)] * 2 + [whole()] * len(operands),
         out_specs=whole(),
-        compiler_params=pltpu.CompilerParams(vmem_limit_bytes=VMEM_LIMIT),
-        cost_estimate=pl.CostEstimate(
-            flops=2 * len(pairs) * slots * rows * size * size,
-            bytes_accessed=sum(2 * a.size for a in flat) + 4 * slots * size * size,
+        scratch_shapes=[pltpu.VMEM((2,) + half, jnp.bfloat16)]
+        + [pltpu.VMEM((rows, width), jnp.bfloat16)] * 2,
+        compiler_params=pltpu.CompilerParams(vmem_limit_bytes=VMEM_LIMIT),
+        cost_estimate=pl.CostEstimate(
+            flops=8 * slots * rows * size * size,
+            bytes_accessed=2 * sum(a.size for a in operands) + 2 * slots * size * size,
             transcendentals=0,
         ),
         name="line_grads",
-    )(ids, *flat)
+    )(place_of, ids, *operands)
 
 
 INWARD = ((0, 1), (3, 2))
@@ -437,74 +442,86 @@
     middle = (at_z == 1) | (at_z == 2)
     place_of = jnp.stack([middle.astype(jnp.int32), half, at_tensor, at_replica])
     along = functools.partial(lax.ppermute, axis_name="dp")
-    across = functools.partial(lax.ppermute, axis_name="groups", perm=SWAP)
-    sideways = functools.partial(lax.ppermute, axis_name="tensor", perm=SWAP)
-    cores = functools.partial(lax.ppermute, axis_name="replica", perm=SWAP)
+    across = functools.partial(
+        lax.ppermute, axis_name=("groups", "dp"), perm=((1, 5), (5, 1), (2, 6), (6, 2))
+    )
+    middle_swap = ((2, 3), (3, 2), (4, 5), (5, 4))
+    sideways = functools.partial(lax.ppermute, axis_name=("dp", "tensor"), perm=middle_swap)
+    cores = functools.partial(lax.ppermute, axis_name=("dp", "replica"), perm=middle_swap)
+    everywhere = functools.partial(lax.ppermute, axis_name="tensor", perm=SWAP)
+    all_cores = functools.partial(lax.ppermute, axis_name="replica", perm=SWAP)
     stage = lax.optimization_barrier
 
     mine = lax.dynamic_slice_in_dim(blocks, half * half_slots, half_slots, 0)
+    mine = jnp.concatenate([mine, ids_block(block_ids, size).astype(jnp.bfloat16)])
+    (mine,) = stage((mine,))
+
+    near_a = along(mine, perm=INWARD)
+    far_a = along(mine, perm=MIDDLE)
     other = lax.dynamic_slice_in_dim(blocks, (1 - half) * half_slots, half_slots, 0)
-    mine = jnp.concatenate([mine, ids_block(block_ids, size).astype(jnp.bfloat16)])
     part = lax.dynamic_slice_in_dim(tokens, lax.axis_index(INNER) * part_width, part_width, 1)
     both = jnp.concatenate([part, upstream])
-    mine, other, both = stage((mine, other, both))
-
-    near_a = along(mine, perm=INWARD)
-    far_a = along(mine, perm=MIDDLE)
     near_a, far_a, both, other = stage((near_a, far_a, both, other))
 
     end_a = along(near_a, perm=MIDDLE)
     far_b = across(far_a)
     both_1 = along(both, perm=PAIRS)
     both_1, end_a, far_b, both, other = stage((both_1, end_a, far_b, both, other))
-    upstream_1 = both_1[rows:]
 
     near_b = along(other, perm=INWARD)
     end_b = across(end_a)
     both_2m = along(both, perm=MIDDLE)
+    upstream_1 = both_1[rows:]
     tokens_1 = lax.all_gather(both_1[:rows], INNER)
-    ids_1, ids_2, ids_3 = (ids_of(piece, slots) for piece in (near_a, far_a, end_a))
-    partial, turned = place_first(
-        place_of, (block_ids, ids_1, ids_2, ids_3), (blocks, near_a, far_a, far_b, end_a), depth, width
-    )
-    near_b, end_b, both_2m, both_1, tokens_1, partial, turned = stage(
-        (near_b, end_b, both_2m, both_1, tokens_1, partial, turned)
-    )
-
-    both_3m = along(both_1, perm=MIDDLE)
+    ids = (block_ids,) + tuple(ids_of(piece, slots) for piece in (near_a, far_a, end_a))
+    turned = place_first(place_of, ids, (blocks, near_a, far_a, far_b, end_a), depth, width)
+    half_1 = lax.dynamic_slice_in_dim(tokens_1, 2 * at_replica, 2, 0)
+    near_b, end_b, both_2m, upstream_1, tokens_1, half_1, turned = stage(
+        (near_b, end_b, both_2m, upstream_1, tokens_1, half_1, turned)
+    )
+
+    half_3m = along(half_1, perm=MIDDLE)
     both_2o = along(both_2m, perm=OUTWARD)
-    last = (near_b, end_b)
     end_keep, own_keep, own_give, *end_give = project_back(
-        place_of, ids_1, ids_3, turned, *last, upstream_1, upstream
+        place_of, ids[1], ids[3], turned, near_b, end_b, upstream_1, upstream
     )
     end_keep, end_give = add_split(place_of, end_keep, *[cores(a) for a in end_give])
-    end_keep, end_give, own_give, both_3m, both_2o = stage(
-        (end_keep, end_give, own_give, both_3m, both_2o)
+    end_keep, end_give, own_give, half_3m, both_2o = stage(
+        (end_keep, end_give, own_give, half_3m, both_2o)
     )
 
     end_got = sideways(end_give)
+    half_3o = along(half_3m, perm=OUTWARD)
+    upstream_3m = along(upstream_1, perm=MIDDLE)
     own_keep, own_give = add_split(place_of, own_keep, cores(own_give))
-    both_3o = along(both_3m, perm=OUTWARD)
-    tokens_2 = lax.all_gather(both_2m[:rows] + both_2o[:rows], INNER)
-    upstream_2 = both_2m[rows:] + both_2o[rows:]
-    end_got, own_give, own_keep = stage((end_got, own_give, own_keep))
+    part_2 = both_2m[:rows] + both_2o[:rows]
+    end_got, own_give, own_keep, part_2, upstream_3m = stage(
+        (end_got, own_give, own_keep, part_2, upstream_3m)
+    )
 
     sum_out = along(end_keep + end_got, perm=OUTWARD)
     own_got = sideways(own_give)
-    proj, end_proj = project_forward(place_of, ids_1, ids_3, partial, *last, tokens, tokens_1)
-    sum_out, own_got, both_3o, proj, end_proj = stage((sum_out, own_got, both_3o, proj, end_proj))
-
-    tokens_3 = lax.all_gather(both_3m[:rows] + both_3o[:rows], INNER)
-    upstream_3 = both_3m[rows:] + both_3o[rows:]
+    tokens_2 = lax.all_gather(part_2, INNER)
+    pieces = (blocks, near_a, near_b, far_a, far_b, end_a, end_b)
+    proj, end_proj = project_forward(place_of, ids, pieces, tokens, tokens_1, width)
+    upstream_3o = along(upstream_3m, perm=OUTWARD)
+    sum_out, own_got, half_3o, upstream_3o, proj, end_proj = stage(
+        (sum_out, own_got, half_3o, upstream_3o, proj, end_proj)
+    )
+
     quarter = jnp.where(middle, own_keep + own_got, sum_out)
+    by_tensor, by_core = everywhere(quarter), all_cores(quarter)
     proj_out = along(end_proj, perm=OUTWARD)
-    pairs = ((tokens, upstream), (tokens_1, upstream_1), (tokens_2, upstream_2))
-    grads = line_grads(block_ids, pairs, None, size, jnp.float32)
-    by_tensor, by_core, grads = stage((sideways(quarter), cores(quarter), grads))
-    by_both = cores(by_tensor)
+    half_3 = half_3m + half_3o
+    operands = (
+        tokens, upstream, tokens_1, upstream_1, tokens_2, both_2m[rows:], both_2o[rows:],
+        half_3, all_cores(half_3), upstream_3m, upstream_3o,
+    )
+    grads = line_grads(place_of, block_ids, operands, size)
+    by_tensor, by_core, grads = stage((by_tensor, by_core, grads))
+    by_both = all_cores(by_tensor)
     projected = jnp.where(middle, proj, proj_out)
     token_grad = assemble(place_of, (quarter, by_core, by_tensor, by_both))
-    grads = line_grads(block_ids, ((tokens_3, upstream_3),), grads, size, jnp.bfloat16)
     return projected, token_grad, grads
 
 

time: 212 us -> 238 us (1.12)
  waiting for transfers between devices: 101 us -> 119 us
  starting transfers between devices: 29.8 us -> 39.9 us
  Pallas kernels: 47.3 us -> 41 us
  local copies, waits for them, and re-layouts: 8.53 us -> 12 us
    ppermute x5 -> x8, waiting for transfers between devices: 7.38 us -> 40.8 us  [the longest x1 31.2 us: line_body(): half_3o = along(half_3m, perm=OUTWARD)]
    ppermute x1, waiting for transfers between devices: 10.7 us -> 0.01 us  [line_body(): end_got = sideways(end_give)]
    pallas_call x3 -> x2, Pallas kernels: 30.5 us -> 22.1 us  [the longest x1 15.9 us: line_grads(): pl.pallas_call(line_grads_kernel, out_shape=jax.ShapeDtypeStruct((slots,...]
    all_gather x1, waiting for transfers between devices: 0.01 us -> 5.38 us  [line_body(): tokens_1 = lax.all_gather(both_1[:rows], INNER)]
    ppermute x1, waiting for transfers between devices: 6.87 us -> 1.76 us  [line_body(): near_b = along(other, perm=INWARD)]
    add x2 -> x1, other arithmetic: 3.45 us -> 0.41 us  [line_body(): half_3 = half_3m + half_3o]
    ppermute x1, starting transfers between devices: 5 us -> 7.75 us  [line_body(): near_a = along(mine, perm=INWARD)]
    ppermute x5 -> x8, starting transfers between devices: 3.24 us -> 5.81 us  [the longest x1 1.46 us: line_body(): upstream_3m = along(upstream_1, perm=MIDDLE)]
  transfers between devices with their start and end apart: 24 -> 26, of which waited for: 13 -> 9; matrix products, arithmetic and copies ran while one was open for 3% -> 5% of each run, Pallas kernels for 18% -> 16%
where the time goes in v9:
time: 238 us; the launch traced here: 237 us
  waiting for transfers between devices  119 us (50%)
  Pallas kernels  41 us (17%)
  starting transfers between devices  39.9 us (17%)
  between operations  14.4 us (6%)
  local copies, waits for them, and re-layouts  12 us (5%)
  other arithmetic  10.6 us (4%)
    ppermute x1, waiting for transfers between devices, line_body(): half_3o = along(half_3m, perm=OUTWARD)  31.2 us
    ppermute x1, waiting for transfers between devices, line_body(): near_a = along(mine, perm=INWARD)  21.9 us
    ppermute x1, waiting for transfers between devices, line_body(): both_1 = along(both, perm=PAIRS)  21.4 us
    ppermute x1, waiting for transfers between devices, line_body(): both_2o = along(both_2m, perm=OUTWARD)  16.5 us
    pallas_call x1, Pallas kernels, line_grads(): pl.pallas_call(line_grads_kernel, out_shape=jax.ShapeDtypeStruct((slots,...  15.9 us
    ppermute x1, waiting for transfers between devices, line_body(): sum_out = along(end_keep + end_got, perm=OUTWARD)  11.2 us
    ppermute x1, waiting for transfers between devices, line_body(): upstream_3o = along(upstream_3m, perm=OUTWARD)  9.46 us
    ppermute x1, starting transfers between devices, line_body(): near_a = along(mine, perm=INWARD)  7.75 us
  transfers between devices with their start and end apart: 26, of which 9 were waited for; matrix products, arithmetic and copies ran while one was open for 5% of the time, Pallas kernels for 16%

profile of v9, /device:TPU:0, one launch (start us, length us, event | category | flops | bytes accessed | tf_op | source)
XLA Modules:
  0.0 237.0 jit_solution(17848828133650556067)
XLA Ops:
  7.2 0.7 convert_element_type.26
  7.9 0.1 convert_element_type.27
  8.0 2.7 %constant_dynamic-slice_fusion.1 = (bf16[32,128,128]{2,1,0:T(8,128)(2,1)}, bf16[32,128,128]{2,1,0:T(8,128)(2,1)S(1)}) fusion(bf16[64,128,128]{2,1,0:T(8,128)(2,1)} %own.3, s32[]{:T(128)S(6)} %select_n.27, s32[]{:T(128)S(6)} %select_n.25), kind=kLoop, calls=%fused_computation.6 | loop fusion | bytes 4194312 | tf_op jit(solution)/shard_map/dynamic_slice | solution.py:461
  10.7 1.1 pad_maximum_fusion
  11.8 0.7 collective-permute-start.1
  12.5 7.8 %collective-permute-start = (bf16[33,128,128]{2,1,0:T(8,128)(2,1)}, bf16[33,128,128]{2,1,0:T(8,128)(2,1)S(1)}, u32[]{:S(2)}, u32[]{:S(2)}) collective-permute-start(bf16[33,128,128]{2,1,0:T(8,128)(2,1)} %pad_maximum_fusion), channel_id=1, source_target_pairs={{0,4},{12,8},{1,5},{13,9},{2,6},{14,10},{3,7},{15,11},{16,20},{28,... | collective-permute-start | bytes 3244040 | tf_op jit(solution)/shard_map/ppermute | solution.py:459
  20.3 1.1 constant_dynamic-slice_fusion.2
  21.4 0.1 pad_maximum_fusion.1
  21.5 21.9 %collective-permute-done.near_a = bf16[33,128,128]{2,1,0:T(8,128)(2,1)S(1)} collective-permute-done((bf16[33,128,128]{2,1,0:T(8,128)(2,1)}, bf16[33,128,128]{2,1,0:T(8,128)(2,1)S(1)}, u32[]{:S(2)}, u32[]{:S(2)}) %collective-permute-start) | collective-permute-done | bytes 1081376 | tf_op jit(solution)/shard_map/ppermute | solution.py:459
  43.3 0.7 collective-permute-start.3
  44.1 1.7 collective-permute-start.4
  45.7 5.9 %collective-permute-start.2 = (bf16[512,1024]{1,0:T(8,128)(2,1)S(1)}, bf16[512,1024]{1,0:T(8,128)(2,1)S(1)}, u32[]{:S(2)}, u32[]{:S(2)}) collective-permute-start(bf16[512,1024]{1,0:T(8,128)(2,1)S(1)} %pad_maximum_fusion.1), channel_id=1, source_target_pairs={{0,4},{12,8},{4,0},{8,12},{1,5},{13,9},{5,1},{9,13},{2,6},{14,10},... | collective-permute-start | bytes 3145736 | tf_op jit(solution)/shard_map/ppermute | solution.py:468
  51.6 21.4 %collective-permute-done.2 = bf16[512,1024]{1,0:T(8,128)(2,1)S(1)} collective-permute-done((bf16[512,1024]{1,0:T(8,128)(2,1)S(1)}, bf16[512,1024]{1,0:T(8,128)(2,1)S(1)}, u32[]{:S(2)}, u32[]{:S(2)}) %collective-permute-start.2) | collective-permute-done | bytes 1048608 | tf_op jit(solution)/shard_map/ppermute | solution.py:468
  73.0 1.1 fusion.1
  74.2 0.0 all-gather.7.cloned.1.call-start
  74.2 1.7 collective-permute-start.6
  75.9 5.8 %collective-permute-start.5 = (bf16[32,128,128]{2,1,0:T(8,128)(2,1)}, bf16[32,128,128]{2,1,0:T(8,128)(2,1)}, u32[]{:S(2)}, u32[]{:S(2)}) collective-permute-start(bf16[32,128,128]{2,1,0:T(8,128)(2,1)} %get-tuple-element.54), channel_id=1, source_target_pairs={{0,4},{12,8},{1,5},{13,9},{2,6},{14,10},{3,7},{15,11},{16,20},{28,... | collective-permute-start | bytes 3145736 | tf_op jit(solution)/shard_map/ppermute | solution.py:471
  81.7 1.7 collective-permute-start.7
  83.3 0.7 pad_add_fusion.place_of
  84.0 0.5 bitcast_convert_fusion
  84.5 0.6 bitcast_convert_fusion.1.ids_3
  85.1 6.2 %place_first.1.partial = bf16[1024,4096]{1,0:T(8,128)(2,1)} custom-call(s32[4]{0:T(128)} %pad_add_fusion.place_of, s32[64]{0:T(128)} %ids.1, s32[64]{0:T(128)} %get-tuple-element.103.ids_1, s32[64]{0:T(128)} %get-tuple-element.102.ids_2, s32[64]{0:T(128)} %bitcast_convert_fusion.1.ids_3, bf16[64,128,128]{2,1,0:T(8,128)(2,1)} %own.3, ...), custom_call_target="tpu_custom_call" | custom-call | bytes 16777216 | tf_op jit(solution)/shard_map/place_first/pallas_call | solution.py:174
  91.3 5.4 %all-gather.5.cloned.1.call-done = bf16[1024,1024]{1,0:T(8,128)(2,1)} async-done(((bf16[256,1024]{1,0:T(8,128)(2,1)}), bf16[1024,1024]{1,0:T(8,128)(2,1)}) %all-gather.5.cloned.1.call-update) | async-done | bytes 2097168 | tf_op jit(solution)/shard_map/all_gather | solution.py:475
  96.7 2.3 constant_dynamic-slice_fusion
  99.0 1.8 collective-permute-done.5.near_b
  100.7 0.7 collective-permute-start.10
  101.5 1.3 collective-permute-start.11
  102.8 3.9 %project_back.1 = (bf16[2,256,1024]{2,1,0:T(8,128)(2,1)}, bf16[2,256,1024]{2,1,0:T(8,128)(2,1)}, bf16[2,256,1024]{2,1,0:T(8,128)(2,1)}, bf16[256,1024]{1,0:T(8,128)(2,1)}, bf16[256,1024]{1,0:T(8,128)(2,1)}) custom-call(s32[4]{0:T(128)} %pad_add_fusion.place_of, s32[64]{0:T(128)} %get-tuple-element.103.ids_1, s32[64]{0:T(128)} %bitcast_convert_fusion.1.ids_3, ...), custom_call_target="tpu_custom_call" | custom-call | flops 4294967296 | bytes 13631488 | tf_op jit(solution)/shard_map/project_back/pallas_call | solution.py:229
  106.7 0.8 collective-permute-start.8
  107.5 0.7 collective-permute-start.9
  108.3 0.8 copy-done.17
  109.0 0.2 copy-done.19
  109.2 3.0 %add_split.2 = (bf16[256,1024]{1,0:T(8,128)(2,1)}, bf16[256,1024]{1,0:T(8,128)(2,1)}) custom-call(s32[4]{0:T(128)} %pad_add_fusion.place_of, bf16[2,256,1024]{2,1,0:T(8,128)(2,1)} %get-tuple-element.62.keep, bf16[256,1024]{1,0:T(8,128)(2,1)} %copy-done.17, bf16[256,1024]{1,0:T(8,128)(2,1)} %copy-done.19), custom_call_target="tpu_custom_call" | custom-call | flops 524288 | bytes 3145728 | tf_op jit(solution)/shard_map/add_split/pallas_call | solution.py:320
  112.2 16.5 %collective-permute-done.11 = bf16[512,1024]{1,0:T(8,128)(2,1)S(1)} collective-permute-done((bf16[512,1024]{1,0:T(8,128)(2,1)}, bf16[512,1024]{1,0:T(8,128)(2,1)S(1)}, u32[]{:S(2)}, u32[]{:S(2)}) %collective-permute-start.11) | collective-permute-done | bytes 1048608 | tf_op jit(solution)/shard_map/ppermute | solution.py:484
  128.8 0.7 collective-permute-start.13
  129.5 1.5 collective-permute-start.14
  131.0 1.4 collective-permute-start.12
  132.4 2.4 %fusion = (bf16[256,1024]{1,0:T(8,128)(2,1)}, bf16[256,1024]{1,0:T(8,128)(2,1)}, bf16[256,1024]{1,0:T(8,128)(2,1)}) fusion(bf16[512,1024]{1,0:T(8,128)(2,1)S(1)} %collective-permute-done.11, bf16[512,1024]{1,0:T(8,128)(2,1)} %collective-permute-done.7), kind=kLoop, calls=%fused_computation.13 | loop fusion | flops 262144 | bytes 3670016 | tf_op jit(solution)/shard_map/slice | solution.py:517
  134.8 1.0 copy-done.7
  135.8 3.1 %add_split.3 = (bf16[256,1024]{1,0:T(8,128)(2,1)}, bf16[256,1024]{1,0:T(8,128)(2,1)}) custom-call(s32[4]{0:T(128)} %pad_add_fusion.place_of, bf16[2,256,1024]{2,1,0:T(8,128)(2,1)} %get-tuple-element.72.keep, bf16[2,256,1024]{2,1,0:T(8,128)(2,1)} %copy-done.7), custom_call_target="tpu_custom_call" | custom-call | flops 524288 | bytes 3145728 | tf_op jit(solution)/shard_map/add_split/pallas_call | solution.py:320
  139.0 1.3 collective-permute-start.17
  140.3 2.2 add.33
  142.5 1.3 collective-permute-start.15
  143.7 0.7 collective-permute-start.16
  144.4 1.3 collective-permute-start.18
  145.7 5.9 %project_forward.1 = (bf16[256,1024]{1,0:T(8,128)(2,1)}, bf16[256,1024]{1,0:T(8,128)(2,1)}) custom-call(s32[4]{0:T(128)} %pad_add_fusion.place_of, s32[64]{0:T(128)} %ids.1, s32[64]{0:T(128)} %get-tuple-element.103.ids_1, s32[64]{0:T(128)} %get-tuple-element.102.ids_2, s32[64]{0:T(128)} %bitcast_convert_fusion.1.ids_3, bf16[64,128,128]{2,1,0:T(8,128)(2,1)} %own.3, ...), custom_call_target="tpu_custom_call" | custom-call | flops 4294967296 | bytes 13631488 | tf_op jit(solution)/shard_map/project_forward/pallas_call | solution.py:286
  151.6 31.2 %collective-permute-done.17 = bf16[2,256,1024]{2,1,0:T(8,128)(2,1)S(1)} collective-permute-done((bf16[2,256,1024]{2,1,0:T(8,128)(2,1)S(1)}, bf16[2,256,1024]{2,1,0:T(8,128)(2,1)S(1)}, u32[]{:S(2)}, u32[]{:S(2)}) %collective-permute-start.17) | collective-permute-done | bytes 1048608 | tf_op jit(solution)/shard_map/ppermute | solution.py:494
  182.9 11.2 %collective-permute-done.15 = bf16[256,1024]{1,0:T(8,128)(2,1)S(1)} collective-permute-done((bf16[256,1024]{1,0:T(8,128)(2,1)}, bf16[256,1024]{1,0:T(8,128)(2,1)S(1)}, u32[]{:S(2)}, u32[]{:S(2)}) %collective-permute-start.15) | collective-permute-done | bytes 524320 | tf_op jit(solution)/shard_map/ppermute | solution.py:502
  194.1 9.5 %collective-permute-done.18.upstream_3o = bf16[256,1024]{1,0:T(8,128)(2,1)S(1)} collective-permute-done((bf16[256,1024]{1,0:T(8,128)(2,1)}, bf16[256,1024]{1,0:T(8,128)(2,1)S(1)}, u32[]{:S(2)}, u32[]{:S(2)}) %collective-permute-start.18) | collective-permute-done | bytes 524320 | tf_op jit(solution)/shard_map/ppermute | solution.py:507
  203.6 0.4 add.35.mine_3
  204.0 0.1 collective-permute-start.22
  204.1 0.7 copy-done.14
  204.8 0.3 copy-done.16
  205.1 0.1 add_select_fusion.own
  205.2 0.1 collective-permute-start.21
  205.3 0.7 collective-permute-start.20
  206.0 1.3 collective-permute-start.19
  207.3 0.9 copy-done.9
  208.2 15.9 %line_grads.1 = bf16[64,128,128]{2,1,0:T(8,128)(2,1)} custom-call(s32[4]{0:T(128)} %pad_add_fusion.place_of, s32[64]{0:T(128)} %ids.1, bf16[256,4096]{1,0:T(8,128)(2,1)} %tokens.3, bf16[256,1024]{1,0:T(8,128)(2,1)} %upstream.3, bf16[4,256,1024]{2,1,0:T(8,128)(2,1)} %bitcast.17, bf16[256,1024]{1,0:T(8,128)(2,1)} %get-tuple-element.61.end_upstream.upstream_1, ...), custom_call_target="tpu_custom_call" | custom-call | flops 2147483648 | bytes 13631488 | tf_op jit(solution)/shard_map/line_grads/pallas_call | solution.py:401
  224.2 0.2 collective-permute-start.23
  224.4 1.9 broadcast_select_fusion
  226.3 0.1 collective-permute-done.23.by_both
  226.4 0.8 copy-done.18
  227.2 3.0 %assemble.1 = bf16[256,4096]{1,0:T(8,128)(2,1)} custom-call(s32[4]{0:T(128)} %pad_add_fusion.place_of, bf16[256,1024]{1,0:T(8,128)(2,1)} %copy-done.1, bf16[256,1024]{1,0:T(8,128)(2,1)} %copy-done.12, bf16[256,1024]{1,0:T(8,128)(2,1)} %collective-permute-done.20.by_tensor, bf16[256,1024]{1,0:T(8,128)(2,1)} %copy-done.18), custom_call_target="tpu_custom_call" | custom-call | bytes 4194304 | tf_op jit(solution)/shard_map/assemble/pallas_call | solution.py:345
  (55 shorter events, 0.2 us)
Async XLA Ops:
  7.2 89.5 %all-gather.5.cloned.1.call-start = ((), (), s32[]{:S(2)}) async-start(), calls=%async_computation | async-start | bytes 2621440 | tf_op jit(solution)/shard_map/all_gather | solution.py:475
  10.7 10.7 %copy-start.2 = (bf16[256,1024]{1,0:T(8,128)(2,1)S(1)}, bf16[256,1024]{1,0:T(8,128)(2,1)}, u32[]{:S(2)}) copy-start(bf16[256,1024]{1,0:T(8,128)(2,1)} %upstream.3) | copy-start | bytes 1572868
  11.8 9.7 %collective-permute-start.1 = (bf16[33,128,128]{2,1,0:T(8,128)(2,1)}, bf16[33,128,128]{2,1,0:T(8,128)(2,1)S(1)}, u32[]{:S(2)}, u32[]{:S(2)}) collective-permute-start(bf16[33,128,128]{2,1,0:T(8,128)(2,1)} %pad_maximum_fusion), channel_id=1, source_target_pairs={{4,8},{8,4},{5,9},{9,5},{6,10},{10,6},{7,11},{11,7},{20,24},{24,20... | collective-permute-start | bytes 3244040 | tf_op jit(solution)/shard_map/ppermute | solution.py:460
  12.5 30.8 %collective-permute-start = (bf16[33,128,128]{2,1,0:T(8,128)(2,1)}, bf16[33,128,128]{2,1,0:T(8,128)(2,1)S(1)}, u32[]{:S(2)}, u32[]{:S(2)}) collective-permute-start(bf16[33,128,128]{2,1,0:T(8,128)(2,1)} %pad_maximum_fusion), channel_id=1, source_target_pairs={{0,4},{12,8},{1,5},{13,9},{2,6},{14,10},{3,7},{15,11},{16,20},{28,... | collective-permute-start | bytes 3244040 | tf_op jit(solution)/shard_map/ppermute | solution.py:459
  21.4 51.5 %copy-start.8 = (bf16[512,1024]{1,0:T(8,128)(2,1)}, bf16[512,1024]{1,0:T(8,128)(2,1)S(1)}, u32[]{:S(2)}) copy-start(bf16[512,1024]{1,0:T(8,128)(2,1)S(1)} %pad_maximum_fusion.1) | copy-start | bytes 3145732
  21.5 63.6 %copy-start.4 = (bf16[33,128,128]{2,1,0:T(8,128)(2,1)}, bf16[33,128,128]{2,1,0:T(8,128)(2,1)S(1)}, u32[]{:S(2)}) copy-start(bf16[33,128,128]{2,1,0:T(8,128)(2,1)S(1)} %collective-permute-done.1.far_a) | copy-start | bytes 3244036
  43.3 41.8 %copy-start.5 = (bf16[33,128,128]{2,1,0:T(8,128)(2,1)}, bf16[33,128,128]{2,1,0:T(8,128)(2,1)S(1)}, u32[]{:S(2)}) copy-start(bf16[33,128,128]{2,1,0:T(8,128)(2,1)S(1)} %collective-permute-done.near_a) | copy-start | bytes 3244036
  43.3 29.6 %collective-permute-start.3 = (bf16[33,128,128]{2,1,0:T(8,128)(2,1)S(1)}, bf16[33,128,128]{2,1,0:T(8,128)(2,1)S(1)}, u32[]{:S(2)}, u32[]{:S(2)}) collective-permute-start(bf16[33,128,128]{2,1,0:T(8,128)(2,1)S(1)} %collective-permute-done.near_a), channel_id=1, source_target_pairs={{4,8},{8,4},{5,9},{9,5},{6,10},{10,6},{7,11},{11,7},{20,24},{24,20... | collective-permute-start | bytes 3244040 | tf_op jit(solution)/shard_map/ppermute | solution.py:466
  44.1 28.9 %collective-permute-start.4 = (bf16[33,128,128]{2,1,0:T(8,128)(2,1)S(1)}, bf16[33,128,128]{2,1,0:T(8,128)(2,1)}, u32[]{:S(2)}, u32[]{:S(2)}) collective-permute-start(bf16[33,128,128]{2,1,0:T(8,128)(2,1)S(1)} %collective-permute-done.1.far_a), channel_id=1, source_target_pairs={{4,20},{20,4},{8,24},{24,8},{5,21},{21,5},{9,25},{25,9},{6,22},{22... | collective-permute-start | bytes 3244040 | tf_op jit(solution)/shard_map/ppermute | solution.py:467
  45.7 27.3 %collective-permute-start.2 = (bf16[512,1024]{1,0:T(8,128)(2,1)S(1)}, bf16[512,1024]{1,0:T(8,128)(2,1)S(1)}, u32[]{:S(2)}, u32[]{:S(2)}) collective-permute-start(bf16[512,1024]{1,0:T(8,128)(2,1)S(1)} %pad_maximum_fusion.1), channel_id=1, source_target_pairs={{0,4},{12,8},{4,0},{8,12},{1,5},{13,9},{5,1},{9,13},{2,6},{14,10},... | collective-permute-start | bytes 3145736 | tf_op jit(solution)/shard_map/ppermute | solution.py:468
  73.0 12.1 %copy-start.6 = (bf16[33,128,128]{2,1,0:T(8,128)(2,1)}, bf16[33,128,128]{2,1,0:T(8,128)(2,1)S(1)}, u32[]{:S(2)}) copy-start(bf16[33,128,128]{2,1,0:T(8,128)(2,1)S(1)} %collective-permute-done.3.end_a) | copy-start | bytes 3244036
  74.2 133.1 %all-gather.7.cloned.1.call-start = ((), (), s32[]{:S(2)}) async-start(), calls=%async_computation.1 | async-start | bytes 2621440 | tf_op jit(solution)/shard_map/all_gather | solution.py:504
  74.2 26.5 %collective-permute-start.6 = (bf16[33,128,128]{2,1,0:T(8,128)(2,1)S(1)}, bf16[33,128,128]{2,1,0:T(8,128)(2,1)}, u32[]{:S(2)}, u32[]{:S(2)}) collective-permute-start(bf16[33,128,128]{2,1,0:T(8,128)(2,1)S(1)} %collective-permute-done.3.end_a), channel_id=1, source_target_pairs={{4,20},{20,4},{8,24},{24,8},{5,21},{21,5},{9,25},{25,9},{6,22},{22... | collective-permute-start | bytes 3244040 | tf_op jit(solution)/shard_map/ppermute | solution.py:472
  75.9 24.9 %collective-permute-start.5 = (bf16[32,128,128]{2,1,0:T(8,128)(2,1)}, bf16[32,128,128]{2,1,0:T(8,128)(2,1)}, u32[]{:S(2)}, u32[]{:S(2)}) collective-permute-start(bf16[32,128,128]{2,1,0:T(8,128)(2,1)} %get-tuple-element.54), channel_id=1, source_target_pairs={{0,4},{12,8},{1,5},{13,9},{2,6},{14,10},{3,7},{15,11},{16,20},{28,... | collective-permute-start | bytes 3145736 | tf_op jit(solution)/shard_map/ppermute | solution.py:471
  81.7 19.1 %collective-permute-start.7 = (bf16[512,1024]{1,0:T(8,128)(2,1)}, bf16[512,1024]{1,0:T(8,128)(2,1)}, u32[]{:S(2)}, u32[]{:S(2)}) collective-permute-start(bf16[512,1024]{1,0:T(8,128)(2,1)} %copy-done.8), channel_id=1, source_target_pairs={{4,8},{8,4},{5,9},{9,5},{6,10},{10,6},{7,11},{11,7},{20,24},{24,20... | collective-permute-start | bytes 3145736 | tf_op jit(solution)/shard_map/ppermute | solution.py:473
  100.7 11.5 %collective-permute-start.10 = (bf16[2,256,1024]{2,1,0:T(8,128)(2,1)}, bf16[2,256,1024]{2,1,0:T(8,128)(2,1)S(1)}, u32[]{:S(2)}, u32[]{:S(2)}) collective-permute-start(bf16[2,256,1024]{2,1,0:T(8,128)(2,1)} %constant_dynamic-slice_fusion), channel_id=1, source_target_pairs={{4,8},{8,4},{5,9},{9,5},{6,10},{10,6},{7,11},{11,7},{20,24},{24,20... | collective-permute-start | bytes 3145736 | tf_op jit(solution)/shard_map/ppermute | solution.py:483
  101.5 27.3 %collective-permute-start.11 = (bf16[512,1024]{1,0:T(8,128)(2,1)}, bf16[512,1024]{1,0:T(8,128)(2,1)S(1)}, u32[]{:S(2)}, u32[]{:S(2)}) collective-permute-start(bf16[512,1024]{1,0:T(8,128)(2,1)} %collective-permute-done.7), channel_id=1, source_target_pairs={{4,0},{8,12},{5,1},{9,13},{6,2},{10,14},{7,3},{11,15},{20,16},{24,... | collective-permute-start | bytes 3145736 | tf_op jit(solution)/shard_map/ppermute | solution.py:484
  106.7 22.8 %copy-start.3 = (bf16[256,1024]{1,0:T(8,128)(2,1)S(1)}, bf16[256,1024]{1,0:T(8,128)(2,1)}, u32[]{:S(2)}) copy-start(bf16[256,1024]{1,0:T(8,128)(2,1)} %get-tuple-element.61.end_upstream.upstream_1) | copy-start | bytes 1572868
  106.7 1.5 collective-permute-start.8
  107.5 0.7 collective-permute-start.9
  108.2 0.8 copy-start.17
  108.2 1.0 copy-start.19
  128.8 6.1 %collective-permute-start.13 = (bf16[2,256,1024]{2,1,0:T(8,128)(2,1)}, bf16[2,256,1024]{2,1,0:T(8,128)(2,1)S(1)}, u32[]{:S(2)}, u32[]{:S(2)}) collective-permute-start(bf16[2,256,1024]{2,1,0:T(8,128)(2,1)} %get-tuple-element.73), channel_id=1, source_target_pairs={{4,5},{5,4},{8,9},{9,8},{6,7},{7,6},{10,11},{11,10},{20,21},{21,20... | collective-permute-start | bytes 3145736 | tf_op jit(solution)/shard_map/ppermute | solution.py:496
  129.5 9.4 %collective-permute-start.14 = (bf16[256,1024]{1,0:T(8,128)(2,1)S(1)}, bf16[256,1024]{1,0:T(8,128)(2,1)}, u32[]{:S(2)}, u32[]{:S(2)}) collective-permute-start(bf16[256,1024]{1,0:T(8,128)(2,1)S(1)} %copy-done.3), channel_id=1, source_target_pairs={{4,8},{8,4},{5,9},{9,5},{6,10},{10,6},{7,11},{11,7},{20,24},{24,20... | collective-permute-start | bytes 1572872 | tf_op jit(solution)/shard_map/ppermute | solution.py:495
  131.0 8.0 %collective-permute-start.12 = (bf16[256,1024]{1,0:T(8,128)(2,1)}, bf16[256,1024]{1,0:T(8,128)(2,1)}, u32[]{:S(2)}, u32[]{:S(2)}) collective-permute-start(bf16[256,1024]{1,0:T(8,128)(2,1)} %get-tuple-element.71), channel_id=1, source_target_pairs={{4,6},{6,4},{8,10},{10,8},{5,7},{7,5},{9,11},{11,9},{20,22},{22,20... | collective-permute-start | bytes 1572872 | tf_op jit(solution)/shard_map/ppermute | solution.py:493
  134.8 1.0 copy-start.7
  139.0 43.9 %collective-permute-start.17 = (bf16[2,256,1024]{2,1,0:T(8,128)(2,1)S(1)}, bf16[2,256,1024]{2,1,0:T(8,128)(2,1)S(1)}, u32[]{:S(2)}, u32[]{:S(2)}) collective-permute-start(bf16[2,256,1024]{2,1,0:T(8,128)(2,1)S(1)} %collective-permute-done.10), channel_id=1, source_target_pairs={{4,0},{8,12},{5,1},{9,13},{6,2},{10,14},{7,3},{11,15},{20,16},{24,... | collective-permute-start | bytes 3145736 | tf_op jit(solution)/shard_map/ppermute | solution.py:494
  142.5 51.7 %collective-permute-start.15 = (bf16[256,1024]{1,0:T(8,128)(2,1)}, bf16[256,1024]{1,0:T(8,128)(2,1)S(1)}, u32[]{:S(2)}, u32[]{:S(2)}) collective-permute-start(bf16[256,1024]{1,0:T(8,128)(2,1)} %add.33), channel_id=1, source_target_pairs={{4,0},{8,12},{5,1},{9,13},{6,2},{10,14},{7,3},{11,15},{20,16},{24,... | collective-permute-start | bytes 1572872 | tf_op jit(solution)/shard_map/ppermute | solution.py:502
  143.7 50.4 %collective-permute-start.16 = (bf16[256,1024]{1,0:T(8,128)(2,1)}, bf16[256,1024]{1,0:T(8,128)(2,1)S(1)}, u32[]{:S(2)}, u32[]{:S(2)}) collective-permute-start(bf16[256,1024]{1,0:T(8,128)(2,1)} %get-tuple-element.78), channel_id=1, source_target_pairs={{4,6},{6,4},{8,10},{10,8},{5,7},{7,5},{9,11},{11,9},{20,22},{22,20... | collective-permute-start | bytes 1572872 | tf_op jit(solution)/shard_map/ppermute | solution.py:503
  144.4 59.1 %collective-permute-start.18 = (bf16[256,1024]{1,0:T(8,128)(2,1)}, bf16[256,1024]{1,0:T(8,128)(2,1)S(1)}, u32[]{:S(2)}, u32[]{:S(2)}) collective-permute-start(bf16[256,1024]{1,0:T(8,128)(2,1)} %collective-permute-done.14.upstream_3m), channel_id=1, source_target_pairs={{4,0},{8,12},{5,1},{9,13},{6,2},{10,14},{7,3},{11,15},{20,16},{24,... | collective-permute-start | bytes 1572872 | tf_op jit(solution)/shard_map/ppermute | solution.py:507
  151.6 52.5 %copy-start.10 = (bf16[256,1024]{1,0:T(8,128)(2,1)S(1)}, bf16[256,1024]{1,0:T(8,128)(2,1)}, u32[]{:S(2)}) copy-start(bf16[256,1024]{1,0:T(8,128)(2,1)} %get-tuple-element.86) | copy-start | bytes 1572868
  194.1 9.5 %copy-start.13 = (bf16[256,1024]{1,0:T(8,128)(2,1)}, bf16[256,1024]{1,0:T(8,128)(2,1)S(1)}, u32[]{:S(2)}) copy-start(bf16[256,1024]{1,0:T(8,128)(2,1)S(1)} %collective-permute-done.15) | copy-start | bytes 1572868
  194.1 9.5 %copy-start.15 = (bf16[256,1024]{1,0:T(8,128)(2,1)}, bf16[256,1024]{1,0:T(8,128)(2,1)S(1)}, u32[]{:S(2)}) copy-start(bf16[256,1024]{1,0:T(8,128)(2,1)S(1)} %collective-permute-done.16) | copy-start | bytes 1572868
  203.6 1.6 copy-start.11
  203.6 1.2 copy-start.14
  203.6 1.5 copy-start.16
  204.0 3.3 %copy-start = (bf16[2,256,1024]{2,1,0:T(8,128)(2,1)}, bf16[2,256,1024]{2,1,0:T(8,128)(2,1)S(1)}, u32[]{:S(2)}) copy-start(bf16[2,256,1024]{2,1,0:T(8,128)(2,1)S(1)} %add.35.mine_3) | copy-start | bytes 3145732
  204.0 3.2 %collective-permute-start.22 = (bf16[2,256,1024]{2,1,0:T(8,128)(2,1)S(1)}, bf16[2,256,1024]{2,1,0:T(8,128)(2,1)S(1)}, u32[]{:S(2)}, u32[]{:S(2)}) collective-permute-start(bf16[2,256,1024]{2,1,0:T(8,128)(2,1)S(1)} %add.35.mine_3), channel_id=1, source_target_pairs={{0,1},{1,0},{2,3},{3,2},{4,5},{5,4},{6,7},{7,6},{8,9},{9,8},{10,11... | collective-permute-start | bytes 3145736 | tf_op jit(solution)/shard_map/ppermute | solution.py:518
  205.2 19.0 %copy-start.1 = (bf16[256,1024]{1,0:T(8,128)(2,1)}, bf16[256,1024]{1,0:T(8,128)(2,1)S(1)}, u32[]{:S(2)}) copy-start(bf16[256,1024]{1,0:T(8,128)(2,1)S(1)} %add_select_fusion.own) | copy-start | bytes 1572868
  205.2 19.0 %collective-permute-start.21 = (bf16[256,1024]{1,0:T(8,128)(2,1)S(1)}, bf16[256,1024]{1,0:T(8,128)(2,1)S(1)}, u32[]{:S(2)}, u32[]{:S(2)}) collective-permute-start(bf16[256,1024]{1,0:T(8,128)(2,1)S(1)} %add_select_fusion.own), channel_id=1, source_target_pairs={{0,1},{1,0},{2,3},{3,2},{4,5},{5,4},{6,7},{7,6},{8,9},{9,8},{10,11... | collective-permute-start | bytes 1572872 | tf_op jit(solution)/shard_map/ppermute | solution.py:513
  205.3 18.9 %collective-permute-start.20 = (bf16[256,1024]{1,0:T(8,128)(2,1)S(1)}, bf16[256,1024]{1,0:T(8,128)(2,1)}, u32[]{:S(2)}, u32[]{:S(2)}) collective-permute-start(bf16[256,1024]{1,0:T(8,128)(2,1)S(1)} %add_select_fusion.own), channel_id=1, source_target_pairs={{0,2},{2,0},{1,3},{3,1},{4,6},{6,4},{5,7},{7,5},{8,10},{10,8},{9,1... | collective-permute-start | bytes 1572872 | tf_op jit(solution)/shard_map/ppermute | solution.py:513
  206.0 18.5 %collective-permute-start.19 = (bf16[256,1024]{1,0:T(8,128)(2,1)}, bf16[256,1024]{1,0:T(8,128)(2,1)}, u32[]{:S(2)}, u32[]{:S(2)}) collective-permute-start(bf16[256,1024]{1,0:T(8,128)(2,1)} %get-tuple-element.85), channel_id=1, source_target_pairs={{4,0},{8,12},{5,1},{9,13},{6,2},{10,14},{7,3},{11,15},{20,16},{24,... | collective-permute-start | bytes 1572872 | tf_op jit(solution)/shard_map/ppermute | solution.py:514
  207.3 1.0 copy-start.9
  224.2 2.2 copy-start.12
  224.2 2.2 collective-permute-start.23
  226.4 0.8 copy-start.18
Sparse Core Ops, SparseCore 0:
  74.3 22.3 all-gather.4
  139.1 38.5 all-gather.6

commit v10 on v9

--- a/solution.py
+++ b/solution.py
@@ -184,13 +184,39 @@
     )(place_of, *ids, *pieces)
 
 
+def plain_kernel(place_of, ids_0, ids_1, ids_2, own, near_a, far_a, weight):
+    half_slots = near_a.shape[0] - 1
+    mine = place_of[1] * half_slots
+
+    @pl.when(place_of[0] == 1)
+    def work():
+        weight[...] = jnp.zeros_like(weight)
+        place_blocks(ids_0, 0, own, weight, None, own.shape[0])
+        place_blocks(ids_1, mine, near_a, weight, None, half_slots)
+        place_blocks(ids_2, mine, far_a, weight, None, half_slots)
+
+
+def place_plain(place_of, ids, pieces, depth, width):
+    return pl.pallas_call(
+        plain_kernel,
+        out_shape=jax.ShapeDtypeStruct((depth, width), jnp.bfloat16),
+        in_specs=[whole(pltpu.SMEM)] * 4 + [whole()] * 3,
+        out_specs=whole(),
+        compiler_params=pltpu.CompilerParams(vmem_limit_bytes=VMEM_LIMIT),
+        cost_estimate=pl.CostEstimate(
+            flops=0, bytes_accessed=depth * width * 3, transcendentals=0
+        ),
+        name="place_plain",
+    )(place_of, *ids, *pieces)
+
+
 def back_kernel(
-    place_of, ids_1, ids_3, partial, near_b, end_b, end_upstream, upstream,
+    place_of, ids_1, ids_3, partial, near_b, end_b, two_upstream,
     end_keep, own_keep, own_give, end_give_0, end_give_1, held, sources, sem,
 ):
     half_slots = near_b.shape[0]
     other = (1 - place_of[1]) * half_slots
-    rows, width = upstream.shape
+    rows, width = two_upstream.shape[1:]
     step = 256
     per_part = end_keep.shape[2] // step
 
@@ -198,8 +224,8 @@
     def work():
         load = pltpu.make_async_copy(partial, held, sem)
         load.start()
-        sources[:rows] = end_upstream[...]
-        sources[rows:] = upstream[...]
+        sources[:rows] = two_upstream[1]
+        sources[rows:] = two_upstream[0]
         load.wait()
         place_blocks(ids_1, other, near_b, None, held, half_slots)
         place_blocks(ids_3, other, end_b, None, held, half_slots)
@@ -221,15 +247,15 @@
             column(2 * x + 1 - place_of[3], end_give, own_give.at[x])
 
 
-def project_back(place_of, ids_1, ids_3, partial, near_b, end_b, end_upstream, upstream):
+def project_back(place_of, ids_1, ids_3, partial, near_b, end_b, two_upstream):
     width, depth = partial.shape
-    rows = upstream.shape[0]
+    rows = two_upstream.shape[1]
     quarter = jax.ShapeDtypeStruct((rows, depth // 4), jnp.bfloat16)
     half = jax.ShapeDtypeStruct((2, rows, depth // 4), jnp.bfloat16)
     return pl.pallas_call(
         back_kernel,
         out_shape=(half, half, half, quarter, quarter),
-        in_specs=[whole(pltpu.SMEM)] * 3 + [whole(pl.ANY)] + [whole()] * 4,
+        in_specs=[whole(pltpu.SMEM)] * 3 + [whole(pl.ANY)] + [whole()] * 3,
         out_specs=(whole(),) * 5,
         scratch_shapes=[
             pltpu.VMEM((width, depth), jnp.bfloat16),
@@ -243,12 +269,12 @@
             transcendentals=0,
         ),
         name="project_back",
-    )(place_of, ids_1, ids_3, partial, near_b, end_b, end_upstream, upstream)
+    )(place_of, ids_1, ids_3, partial, near_b, end_b, two_upstream)
 
 
 def forward_kernel(
-    place_of, ids_0, ids_1, ids_2, ids_3, own, near_a, near_b, far_a, far_b, end_a, end_b,
-    tokens, end_tokens, proj, end_proj, weight,
+    place_of, ids_1, ids_2, ids_3, partial, near_b, far_b, end_a, end_b,
+    tokens, end_tokens, proj, end_proj, weight, sem,
 ):
     half_slots = near_b.shape[0]
     mine, other = place_of[1] * half_slots, (1 - place_of[1]) * half_slots
@@ -258,11 +284,13 @@
 
     @pl.when(place_of[0] == 1)
     def work():
-        weight[...] = jnp.zeros_like(weight)
-        place_blocks(ids_0, 0, own, weight, None, own.shape[0])
-        for ids, a, b in ((ids_1, near_a, near_b), (ids_2, far_a, far_b), (ids_3, end_a, end_b)):
-            place_blocks(ids, mine, a, weight, None, half_slots)
-            place_blocks(ids, other, b, weight, None, half_slots)
+        load = pltpu.make_async_copy(partial, weight, sem)
+        load.start()
+        load.wait()
+        place_blocks(ids_1, other, near_b, weight, None, half_slots)
+        place_blocks(ids_2, other, far_b, weight, None, half_slots)
+        place_blocks(ids_3, mine, end_a, weight, None, half_slots)
+        place_blocks(ids_3, other, end_b, weight, None, half_slots)
 
         @pl.loop(0, width // step, unroll=2)
         def forward(n):
@@ -280,23 +308,20 @@
             ).astype(proj.dtype)
 
 
-def project_forward(place_of, ids, pieces, tokens, end_tokens, width):
+def project_forward(place_of, ids, partial, pieces, tokens, end_tokens):
     rows, depth = tokens.shape
+    width = partial.shape[1]
     out = jax.ShapeDtypeStruct((rows, width), jnp.bfloat16)
     return pl.pallas_call(
         forward_kernel,
         out_shape=(out, out),
-        in_specs=[whole(pltpu.SMEM)] * 5 + [whole()] * 9,
+        in_specs=[whole(pltpu.SMEM)] * 4 + [whole(pl.ANY)] + [whole()] * 6,
         out_specs=(whole(),) * 2,
-        scratch_shapes=[pltpu.VMEM((depth, width), jnp.bfloat16)],
-        compiler_params=pltpu.CompilerParams(vmem_limit_bytes=VMEM_LIMIT),
-        cost_estimate=pl.CostEstimate(
-            flops=4 * rows * depth * width,
-            bytes_accessed=depth * width * 2 + rows * (depth + width) * 4,
-            transcendentals=0,
-        ),
+        scratch_shapes=[pltpu.VMEM((depth, width), jnp.bfloat16), pltpu.SemaphoreType.DMA],
+        compiler_params=pltpu.CompilerParams(vmem_limit_bytes=VMEM_LIMIT),
+        cost_estimate=pl.CostEstimate(flops=0, bytes_accessed=0, transcendentals=0),
         name="project_forward",
-    )(place_of, *ids, *pieces, tokens, end_tokens)
+    )(place_of, *ids, partial, *pieces, tokens, end_tokens)
 
 
 def split_kernel(place_of, keep, *refs):
@@ -356,18 +381,27 @@
 
 
 def line_grads_kernel(
-    place_of, ids, tokens, upstream, tokens_1, upstream_1, tokens_2, upstream_2m, upstream_2o,
-    mine_3, theirs_3, upstream_3m, upstream_3o, grads, tokens_3, upstream_2, upstream_3,
+    place_of, ids, tokens, tokens_1, own_far, core_far, side_far, both_far,
+    two_upstream, far_upstream_m, far_upstream_o, grads, far, turned,
 ):
     slots, size = grads.shape[0], grads.shape[1]
-    cols_n = upstream.shape[1] // size
-    total = (tokens.shape[1] // size) * cols_n
-    per_part = tokens_1.shape[2] // size
+    parts, rows, part_width = tokens_1.shape
+    cols_n = two_upstream.shape[2] // size
+    total = parts * (part_width // size) * cols_n
+    per_part = part_width // size
     group = math.gcd(slots, 8)
-    tokens_3[place_of[3]] = mine_3[...]
-    tokens_3[1 - place_of[3]] = theirs_3[...]
-    upstream_2[...] = upstream_2m[...] + upstream_2o[...]
-    upstream_3[...] = upstream_3m[...] + upstream_3o[...]
+    x, c = place_of[2], place_of[3]
+    for ref, xx, cc in (
+        (own_far, x, c), (core_far, x, 1 - c), (side_far, 1 - x, c), (both_far, 1 - x, 1 - c)
+    ):
+        far[2 * xx + cc] = ref[...]
+
+    @pl.loop(0, cols_n)
+    def turn(n):
+        at = pl.ds(pl.multiple_of(n * size, size), size)
+        for k in range(2):
+            turned[k, at, :] = two_upstream[k, :, at].T
+            turned[2 + k, at, :] = (far_upstream_m[k, :, at] + far_upstream_o[k, :, at]).T
 
     @pl.loop(0, slots // group)
     def some(g):
@@ -377,34 +411,28 @@
             part = row // per_part
             whole_at = pl.ds(pl.multiple_of(row * size, size), size)
             at = pl.ds(pl.multiple_of((row % per_part) * size, size), size)
-            c = pl.ds(pl.multiple_of((b % cols_n) * size, size), size)
+            col = pl.ds(pl.multiple_of((b % cols_n) * size, size), size)
             acc = jnp.zeros((size, size), jnp.float32)
-            for left, right in (
-                (tokens[:, whole_at], upstream),
-                (tokens_1[part, :, at], upstream_1),
-                (tokens_2[part, :, at], upstream_2),
-                (tokens_3[part // 2, part % 2, :, at], upstream_3),
+            for k, right in enumerate(
+                (tokens[:, whole_at], tokens_1[part, :, at], far[part, 0, :, at], far[part, 1, :, at])
             ):
-                acc += lax.dot_general(
-                    left,
-                    right[:, c],
-                    (((0,), (0,)), ((), ())),
-                    preferred_element_type=jnp.float32,
-                )
-            grads[s] = jnp.where(ids[s] < total, acc, 0.0).astype(grads.dtype)
+                acc += jnp.dot(turned[k, col, :], right, preferred_element_type=jnp.float32)
+            grads[s] = jnp.where(ids[s] < total, acc.T, 0.0).astype(grads.dtype)
 
 
 def line_grads(place_of, ids, operands, size):
     slots = ids.shape[0]
-    rows, width = operands[1].shape
-    half = operands[7].shape
+    rows, depth = operands[0].shape
+    width = operands[-1].shape[2]
     return pl.pallas_call(
         line_grads_kernel,
         out_shape=jax.ShapeDtypeStruct((slots, size, size), jnp.bfloat16),
         in_specs=[whole(pltpu.SMEM)] * 2 + [whole()] * len(operands),
         out_specs=whole(),
-        scratch_shapes=[pltpu.VMEM((2,) + half, jnp.bfloat16)]
-        + [pltpu.VMEM((rows, width), jnp.bfloat16)] * 2,
+        scratch_shapes=[
+            pltpu.VMEM((4, 2, rows, depth // 4), jnp.bfloat16),
+            pltpu.VMEM((4, width, rows), jnp.bfloat16),
+        ],
         compiler_params=pltpu.CompilerParams(vmem_limit_bytes=VMEM_LIMIT),
         cost_estimate=pl.CostEstimate(
             flops=8 * slots * rows * size * size,
@@ -448,6 +476,9 @@
     middle_swap = ((2, 3), (3, 2), (4, 5), (5, 4))
     sideways = functools.partial(lax.ppermute, axis_name=("dp", "tensor"), perm=middle_swap)
     cores = functools.partial(lax.ppermute, axis_name=("dp", "replica"), perm=middle_swap)
+    end_sideways = functools.partial(
+        lax.ppermute, axis_name=("dp", "tensor"), perm=((0, 1), (1, 0), (6, 7), (7, 6))
+    )
     everywhere = functools.partial(lax.ppermute, axis_name="tensor", perm=SWAP)
     all_cores = functools.partial(lax.ppermute, axis_name="replica", perm=SWAP)
     stage = lax.optimization_barrier
@@ -460,62 +491,71 @@
     far_a = along(mine, perm=MIDDLE)
     other = lax.dynamic_slice_in_dim(blocks, (1 - half) * half_slots, half_slots, 0)
     part = lax.dynamic_slice_in_dim(tokens, lax.axis_index(INNER) * part_width, part_width, 1)
-    both = jnp.concatenate([part, upstream])
-    near_a, far_a, both, other = stage((near_a, far_a, both, other))
+    near_a, far_a, part, other = stage((near_a, far_a, part, other))
 
     end_a = along(near_a, perm=MIDDLE)
     far_b = across(far_a)
-    both_1 = along(both, perm=PAIRS)
-    both_1, end_a, far_b, both, other = stage((both_1, end_a, far_b, both, other))
+    part_1 = along(part, perm=PAIRS)
+    upstream_1 = along(upstream, perm=PAIRS)
+    ids_1, ids_2 = ids_of(near_a, slots), ids_of(far_a, slots)
+    plain = place_plain(place_of, (block_ids, ids_1, ids_2), (blocks, near_a, far_a), depth, width)
+    part_1, upstream_1, end_a, far_b, part, other, plain = stage(
+        (part_1, upstream_1, end_a, far_b, part, other, plain)
+    )
 
     near_b = along(other, perm=INWARD)
     end_b = across(end_a)
-    both_2m = along(both, perm=MIDDLE)
-    upstream_1 = both_1[rows:]
-    tokens_1 = lax.all_gather(both_1[:rows], INNER)
-    ids = (block_ids,) + tuple(ids_of(piece, slots) for piece in (near_a, far_a, end_a))
-    turned = place_first(place_of, ids, (blocks, near_a, far_a, far_b, end_a), depth, width)
-    half_1 = lax.dynamic_slice_in_dim(tokens_1, 2 * at_replica, 2, 0)
-    near_b, end_b, both_2m, upstream_1, tokens_1, half_1, turned = stage(
-        (near_b, end_b, both_2m, upstream_1, tokens_1, half_1, turned)
-    )
-
-    half_3m = along(half_1, perm=MIDDLE)
-    both_2o = along(both_2m, perm=OUTWARD)
+    part_2m = along(part, perm=MIDDLE)
+    part_3m = along(part_1, perm=MIDDLE)
+    tokens_1 = lax.all_gather(part_1, INNER)
+    two_upstream = jnp.stack([upstream, upstream_1])
+    ids_3 = ids_of(end_a, slots)
+    turned = place_first(
+        place_of, (block_ids, ids_1, ids_2, ids_3), (blocks, near_a, far_a, far_b, end_a), depth, width
+    )
+    near_b, end_b, part_2m, part_3m, two_upstream, tokens_1, turned = stage(
+        (near_b, end_b, part_2m, part_3m, two_upstream, tokens_1, turned)
+    )
+
+    far_m = jnp.stack([part_2m, part_3m])
+    far_o = along(far_m, perm=OUTWARD)
+    far_upstream_m = along(two_upstream, perm=MIDDLE)
+    side_m = sideways(far_m)
     end_keep, own_keep, own_give, *end_give = project_back(
-        place_of, ids[1], ids[3], turned, near_b, end_b, upstream_1, upstream
+        place_of, ids_1, ids_3, turned, near_b, end_b, two_upstream
     )
     end_keep, end_give = add_split(place_of, end_keep, *[cores(a) for a in end_give])
-    end_keep, end_give, own_give, half_3m, both_2o = stage(
-        (end_keep, end_give, own_give, half_3m, both_2o)
+    end_keep, end_give, own_give, far_o, far_upstream_m, side_m = stage(
+        (end_keep, end_give, own_give, far_o, far_upstream_m, side_m)
     )
 
     end_got = sideways(end_give)
-    half_3o = along(half_3m, perm=OUTWARD)
-    upstream_3m = along(upstream_1, perm=MIDDLE)
+    side_o = end_sideways(far_o)
+    far_upstream_o = along(far_upstream_m, perm=OUTWARD)
     own_keep, own_give = add_split(place_of, own_keep, cores(own_give))
-    part_2 = both_2m[:rows] + both_2o[:rows]
-    end_got, own_give, own_keep, part_2, upstream_3m = stage(
-        (end_got, own_give, own_keep, part_2, upstream_3m)
+    own_far = far_m + far_o
+    core_far = all_cores(own_far)
+    end_got, own_give, own_keep, core_far, own_far = stage(
+        (end_got, own_give, own_keep, core_far, own_far)
     )
 
     sum_out = along(end_keep + end_got, perm=OUTWARD)
     own_got = sideways(own_give)
-    tokens_2 = lax.all_gather(part_2, INNER)
-    pieces = (blocks, near_a, near_b, far_a, far_b, end_a, end_b)
-    proj, end_proj = project_forward(place_of, ids, pieces, tokens, tokens_1, width)
-    upstream_3o = along(upstream_3m, perm=OUTWARD)
-    sum_out, own_got, half_3o, upstream_3o, proj, end_proj = stage(
-        (sum_out, own_got, half_3o, upstream_3o, proj, end_proj)
-    )
-
+    proj, end_proj = project_forward(
+        place_of, (ids_1, ids_2, ids_3), plain, (near_b, far_b, end_a, end_b), tokens, tokens_1
+    )
+    sum_out, own_got, side_o, far_upstream_o, proj, end_proj = stage(
+        (sum_out, own_got, side_o, far_upstream_o, proj, end_proj)
+    )
+
+    side_far = side_m + side_o
+    both_far = all_cores(side_far)
     quarter = jnp.where(middle, own_keep + own_got, sum_out)
     by_tensor, by_core = everywhere(quarter), all_cores(quarter)
     proj_out = along(end_proj, perm=OUTWARD)
-    half_3 = half_3m + half_3o
     operands = (
-        tokens, upstream, tokens_1, upstream_1, tokens_2, both_2m[rows:], both_2o[rows:],
-        half_3, all_cores(half_3), upstream_3m, upstream_3o,
+        tokens, tokens_1, own_far, core_far, side_far, both_far,
+        two_upstream, far_upstream_m, far_upstream_o,
     )
     grads = line_grads(place_of, block_ids, operands, size)
     by_tensor, by_core, grads = stage((by_tensor, by_core, grads))

time: 238 us -> 218 us (0.916)
  waiting for transfers between devices: 119 us -> 90.3 us
  starting transfers between devices: 39.9 us -> 45 us
  Pallas kernels: 41 us -> 44.6 us
    ppermute x8 -> x11, waiting for transfers between devices: 78.7 us -> 49.8 us  [the longest x1 12.6 us: line_body(): far_upstream_o = along(far_upstream_m, perm=OUTWARD)]
    ppermute x1, waiting for transfers between devices: 1.76 us -> 9.24 us  [line_body(): near_b = along(other, perm=INWARD)]
    pallas_call x0 -> x1, Pallas kernels: none -> 5.52 us  [place_plain(): pl.pallas_call(plain_kernel, out_shape=jax.ShapeDtypeStruct((depth, width...]
    ppermute x8 -> x11, starting transfers between devices: 13.6 us -> 19.1 us  [the longest x1 8.37 us: line_body(): upstream_1 = along(upstream, perm=PAIRS)]
    all_gather x2 -> x1, waiting for transfers between devices: 5.4 us -> 0.01 us  [line_body(): tokens_1 = lax.all_gather(part_1, INNER)]
    another operation x0 -> x2, other arithmetic: none -> 3.26 us  [the longest x1 2.11 us: line_body(): far_m = jnp.stack([part_2m, part_3m])]
    ppermute x1, starting transfers between devices: 7.75 us -> 5 us  [line_body(): near_a = along(mine, perm=INWARD)]
    slice x1 -> x0, other arithmetic: 2.41 us -> none  [line_body(): both_2o[rows:]]
  transfers between devices with their start and end apart: 26 -> 28, of which waited for: 9 -> 8; matrix products, arithmetic and copies ran while one was open for 5% -> 5% of each run, Pallas kernels for 16% -> 19%
where the time goes in v10:
time: 218 us; the launch traced here: 217 us
  waiting for transfers between devices  90.3 us (41%)
  starting transfers between devices  45 us (21%)
  Pallas kernels  44.6 us (20%)
  between operations  14.4 us (7%)
  other arithmetic  11.6 us (5%)
  local copies, waits for them, and re-layouts  10.9 us (5%)
    ppermute x1, waiting for transfers between devices, line_body(): near_a = along(mine, perm=INWARD)  20.4 us
    pallas_call x1, Pallas kernels, line_grads(): pl.pallas_call(line_grads_kernel, out_shape=jax.ShapeDtypeStruct((slots,...  15.1 us
    ppermute x1, waiting for transfers between devices, line_body(): far_upstream_o = along(far_upstream_m, perm=OUTWARD)  12.6 us
    ppermute x1, waiting for transfers between devices, line_body(): far_o = along(far_m, perm=OUTWARD)  12.1 us
    ppermute x1, waiting for transfers between devices, line_body(): sum_out = along(end_keep + end_got, perm=OUTWARD)  10.8 us
    ppermute x1, waiting for transfers between devices, line_body(): side_o = end_sideways(far_o)  9.82 us
    ppermute x1, waiting for transfers between devices, line_body(): near_b = along(other, perm=INWARD)  9.24 us
    ppermute x1, waiting for transfers between devices, line_body(): part_1 = along(part, perm=PAIRS)  8.89 us
  transfers between devices with their start and end apart: 28, of which 8 were waited for; matrix products, arithmetic and copies ran while one was open for 5% of the time, Pallas kernels for 19%

profile of v10, /device:TPU:0, one launch (start us, length us, event | category | flops | bytes accessed | tf_op | source)
XLA Modules:
  0.0 216.9 jit_solution(1262170541099350694)
XLA Ops:
  7.2 0.7 convert_element_type.26
  7.9 0.1 convert_element_type.27
  8.0 2.7 %constant_dynamic-slice_fusion = (bf16[32,128,128]{2,1,0:T(8,128)(2,1)}, bf16[32,128,128]{2,1,0:T(8,128)(2,1)S(1)}) fusion(bf16[64,128,128]{2,1,0:T(8,128)(2,1)} %own.3, s32[]{:T(128)S(6)} %select_n.24, s32[]{:T(128)S(6)} %select_n.22), kind=kLoop, calls=%fused_computation.5 | loop fusion | bytes 4194312 | tf_op jit(solution)/shard_map/dynamic_slice | solution.py:492
  10.7 0.1 pad_maximum_fusion
  10.8 5.0 %collective-permute-start = (bf16[33,128,128]{2,1,0:T(8,128)(2,1)S(1)}, bf16[33,128,128]{2,1,0:T(8,128)(2,1)S(1)}, u32[]{:S(2)}, u32[]{:S(2)}) collective-permute-start(bf16[33,128,128]{2,1,0:T(8,128)(2,1)S(1)} %pad_maximum_fusion), channel_id=1, source_target_pairs={{0,4},{12,8},{1,5},{13,9},{2,6},{14,10},{3,7},{15,11},{16,20},{28,... | collective-permute-start | bytes 3244040 | tf_op jit(solution)/shard_map/ppermute | solution.py:490
  15.8 0.7 collective-permute-start.1
  16.5 1.9 constant_dynamic-slice_fusion.1
  18.4 20.4 %collective-permute-done.near_a = bf16[33,128,128]{2,1,0:T(8,128)(2,1)S(1)} collective-permute-done((bf16[33,128,128]{2,1,0:T(8,128)(2,1)S(1)}, bf16[33,128,128]{2,1,0:T(8,128)(2,1)S(1)}, u32[]{:S(2)}, u32[]{:S(2)}) %collective-permute-start) | collective-permute-done | bytes 1081376 | tf_op jit(solution)/shard_map/ppermute | solution.py:490
  38.8 0.7 collective-permute-start.4
  39.6 1.7 collective-permute-start.5
  41.2 8.4 %collective-permute-start.3 = (bf16[256,1024]{1,0:T(8,128)(2,1)}, bf16[256,1024]{1,0:T(8,128)(2,1)}, u32[]{:S(2)}, u32[]{:S(2)}) collective-permute-start(bf16[256,1024]{1,0:T(8,128)(2,1)} %param.5), channel_id=1, source_target_pairs={{0,4},{12,8},{4,0},{8,12},{1,5},{13,9},{5,1},{9,13},{2,6},{14,10},... | collective-permute-start | bytes 1572872 | tf_op jit(solution)/shard_map/ppermute | solution.py:499
  49.6 0.1 collective-permute-start.2
  49.7 0.6 pad_add_fusion.place_of
  50.3 0.5 bitcast_convert_fusion.1
  50.8 5.5 %place_plain.1.partial = bf16[4096,1024]{1,0:T(8,128)(2,1)} custom-call(s32[4]{0:T(128)} %pad_add_fusion.place_of, s32[64]{0:T(128)} %ids.1, s32[64]{0:T(128)} %get-tuple-element.104.ids_1, s32[64]{0:T(128)} %get-tuple-element.103.ids_2, bf16[64,128,128]{2,1,0:T(8,128)(2,1)} %own.3, bf16[33,128,128]{2,1,0:T(8,128)(2,1)} %copy-done, ...), custom_call_target="tpu_custom_call" | custom-call | bytes 12582912 | tf_op jit(solution)/shard_map/place_plain/pallas_call | solution.py:200
  56.4 6.4 %collective-permute-done.3 = bf16[256,1024]{1,0:T(8,128)(2,1)} collective-permute-done((bf16[256,1024]{1,0:T(8,128)(2,1)}, bf16[256,1024]{1,0:T(8,128)(2,1)}, u32[]{:S(2)}, u32[]{:S(2)}) %collective-permute-start.3) | collective-permute-done | bytes 524320 | tf_op jit(solution)/shard_map/ppermute | solution.py:499
  62.8 8.9 %collective-permute-done.2 = bf16[256,1024]{1,0:T(8,128)(2,1)} collective-permute-done((bf16[256,1024]{1,0:T(8,128)(2,1)}, bf16[256,1024]{1,0:T(8,128)(2,1)}, u32[]{:S(2)}, u32[]{:S(2)}) %collective-permute-start.2) | collective-permute-done | bytes 524320 | tf_op jit(solution)/shard_map/ppermute | solution.py:498
  71.7 1.7 collective-permute-start.7
  73.4 5.5 %collective-permute-start.6 = (bf16[32,128,128]{2,1,0:T(8,128)(2,1)}, bf16[32,128,128]{2,1,0:T(8,128)(2,1)}, u32[]{:S(2)}, u32[]{:S(2)}) collective-permute-start(bf16[32,128,128]{2,1,0:T(8,128)(2,1)} %get-tuple-element.57), channel_id=1, source_target_pairs={{0,4},{12,8},{1,5},{13,9},{2,6},{14,10},{3,7},{15,11},{16,20},{28,... | collective-permute-start | bytes 3145736 | tf_op jit(solution)/shard_map/ppermute | solution.py:506
  78.9 0.7 collective-permute-start.8
  79.6 1.5 collective-permute-start.9
  81.1 0.5 bitcast_convert_fusion.ids_3
  81.6 6.2 %place_first.1.partial = bf16[1024,4096]{1,0:T(8,128)(2,1)} custom-call(s32[4]{0:T(128)} %pad_add_fusion.place_of, s32[64]{0:T(128)} %ids.1, s32[64]{0:T(128)} %get-tuple-element.104.ids_1, s32[64]{0:T(128)} %get-tuple-element.103.ids_2, s32[64]{0:T(128)} %bitcast_convert_fusion.ids_3, bf16[64,128,128]{2,1,0:T(8,128)(2,1)} %own.3, ...), custom_call_target="tpu_custom_call" | custom-call | bytes 16777216 | tf_op jit(solution)/shard_map/place_first/pallas_call | solution.py:174
  87.9 1.2 pad_maximum_fusion.1.two_upstream
  89.0 9.2 %collective-permute-done.6.near_b = bf16[32,128,128]{2,1,0:T(8,128)(2,1)} collective-permute-done((bf16[32,128,128]{2,1,0:T(8,128)(2,1)}, bf16[32,128,128]{2,1,0:T(8,128)(2,1)}, u32[]{:S(2)}, u32[]{:S(2)}) %collective-permute-start.6) | collective-permute-done | bytes 1048608 | tf_op jit(solution)/shard_map/ppermute | solution.py:506
  98.3 2.1 pad_maximum_fusion.2
  100.4 1.3 collective-permute-start.12
  101.7 0.7 collective-permute-start.14
  102.4 1.7 collective-permute-start.13
  104.1 4.0 %project_back.1 = (bf16[2,256,1024]{2,1,0:T(8,128)(2,1)}, bf16[2,256,1024]{2,1,0:T(8,128)(2,1)}, bf16[2,256,1024]{2,1,0:T(8,128)(2,1)}, bf16[256,1024]{1,0:T(8,128)(2,1)}, bf16[256,1024]{1,0:T(8,128)(2,1)}) custom-call(s32[4]{0:T(128)} %pad_add_fusion.place_of, s32[64]{0:T(128)} %get-tuple-element.104.ids_1, s32[64]{0:T(128)} %bitcast_convert_fusion.ids_3, ...), custom_call_target="tpu_custom_call" | custom-call | flops 4294967296 | bytes 13631488 | tf_op jit(solution)/shard_map/project_back/pallas_call | solution.py:255
  108.1 0.7 collective-permute-start.10
  108.8 0.7 collective-permute-start.11
  109.5 0.8 copy-done.17
  110.3 0.2 copy-done.19
  110.5 3.0 %add_split.2 = (bf16[256,1024]{1,0:T(8,128)(2,1)}, bf16[256,1024]{1,0:T(8,128)(2,1)}) custom-call(s32[4]{0:T(128)} %pad_add_fusion.place_of, bf16[2,256,1024]{2,1,0:T(8,128)(2,1)} %get-tuple-element.66.keep, bf16[256,1024]{1,0:T(8,128)(2,1)} %copy-done.17, bf16[256,1024]{1,0:T(8,128)(2,1)} %copy-done.19), custom_call_target="tpu_custom_call" | custom-call | flops 524288 | bytes 3145728 | tf_op jit(solution)/shard_map/add_split/pallas_call | solution.py:345
  113.5 12.1 %collective-permute-done.12 = bf16[2,256,1024]{2,1,0:T(8,128)(2,1)} collective-permute-done((bf16[2,256,1024]{2,1,0:T(8,128)(2,1)}, bf16[2,256,1024]{2,1,0:T(8,128)(2,1)}, u32[]{:S(2)}, u32[]{:S(2)}) %collective-permute-start.12) | collective-permute-done | bytes 1048608 | tf_op jit(solution)/shard_map/ppermute | solution.py:521
  125.7 1.0 copy-done.7
  126.6 1.6 collective-permute-start.16
  128.3 1.5 fusion.own_far
  129.8 1.6 collective-permute-start.15
  131.5 3.4 %collective-permute-start.20 = (bf16[2,256,1024]{2,1,0:T(8,128)(2,1)}, bf16[2,256,1024]{2,1,0:T(8,128)(2,1)S(1)}, u32[]{:S(2)}, u32[]{:S(2)}) collective-permute-start(bf16[2,256,1024]{2,1,0:T(8,128)(2,1)} %collective-permute-done.12), channel_id=1, source_target_pairs={{0,2},{2,0},{12,14},{14,12},{1,3},{3,1},{13,15},{15,13},{16,18},{1... | collective-permute-start | bytes 3145736 | tf_op jit(solution)/shard_map/ppermute | solution.py:533
  134.9 1.3 collective-permute-start.21
  136.2 3.1 %add_split.3 = (bf16[256,1024]{1,0:T(8,128)(2,1)}, bf16[256,1024]{1,0:T(8,128)(2,1)}) custom-call(s32[4]{0:T(128)} %pad_add_fusion.place_of, bf16[2,256,1024]{2,1,0:T(8,128)(2,1)} %get-tuple-element.76.keep, bf16[2,256,1024]{2,1,0:T(8,128)(2,1)} %collective-permute-done.16.refs_0_), custom_call_target="tpu_custom_call" | custom-call | flops 524288 | bytes 3145728 | tf_op jit(solution)/shard_map/add_split/pallas_call | solution.py:345
  139.3 1.0 copy-done.9
  140.3 2.0 add.29
  142.3 1.4 collective-permute-start.18
  143.7 0.7 collective-permute-start.19
  144.4 4.7 %project_forward.1 = (bf16[256,1024]{1,0:T(8,128)(2,1)}, bf16[256,1024]{1,0:T(8,128)(2,1)}) custom-call(s32[4]{0:T(128)} %pad_add_fusion.place_of, s32[64]{0:T(128)} %get-tuple-element.104.ids_1, s32[64]{0:T(128)} %get-tuple-element.103.ids_2, s32[64]{0:T(128)} %bitcast_convert_fusion.ids_3, bf16[4096,1024]{1,0:T(8,128)(2,1)} %place_plain.1.partial, ...), custom_call_target="tpu_custom_call" | custom-call | tf_op jit(solution)/shard_map/project_forward/pallas_call | solution.py:315
  149.2 9.8 %collective-permute-done.20 = bf16[2,256,1024]{2,1,0:T(8,128)(2,1)S(1)} collective-permute-done((bf16[2,256,1024]{2,1,0:T(8,128)(2,1)}, bf16[2,256,1024]{2,1,0:T(8,128)(2,1)S(1)}, u32[]{:S(2)}, u32[]{:S(2)}) %collective-permute-start.20) | collective-permute-done | bytes 1048608 | tf_op jit(solution)/shard_map/ppermute | solution.py:533
  159.0 12.6 %collective-permute-done.21.far_upstream_o = bf16[2,256,1024]{2,1,0:T(8,128)(2,1)} collective-permute-done((bf16[2,256,1024]{2,1,0:T(8,128)(2,1)}, bf16[2,256,1024]{2,1,0:T(8,128)(2,1)}, u32[]{:S(2)}, u32[]{:S(2)}) %collective-permute-start.21) | collective-permute-done | bytes 1048608 | tf_op jit(solution)/shard_map/ppermute | solution.py:534
  171.5 10.8 %collective-permute-done.18 = bf16[256,1024]{1,0:T(8,128)(2,1)S(1)} collective-permute-done((bf16[256,1024]{1,0:T(8,128)(2,1)}, bf16[256,1024]{1,0:T(8,128)(2,1)S(1)}, u32[]{:S(2)}, u32[]{:S(2)}) %collective-permute-start.18) | collective-permute-done | bytes 524320 | tf_op jit(solution)/shard_map/ppermute | solution.py:542
  182.4 0.8 copy-done.15
  183.2 0.4 add.31.side_far
  183.7 0.5 copy-done.12
  184.2 0.2 copy-done.16
  184.4 0.1 add_select_fusion.own
  184.5 1.8 collective-permute-start.23
  186.3 1.3 collective-permute-start.22
  187.6 1.0 copy-done.10
  188.6 15.1 %line_grads.1 = bf16[64,128,128]{2,1,0:T(8,128)(2,1)} custom-call(s32[4]{0:T(128)} %pad_add_fusion.place_of, s32[64]{0:T(128)} %ids.1, bf16[256,4096]{1,0:T(8,128)(2,1)} %tokens.3, bf16[4,256,1024]{2,1,0:T(8,128)(2,1)} %bitcast.19, bf16[2,256,1024]{2,1,0:T(8,128)(2,1)} %copy-done.3, bf16[2,256,1024]{2,1,0:T(8,128)(2,1)} %copy-done.9, ...), custom_call_target="tpu_custom_call" | custom-call | flops 2147483648 | bytes 13631488 | tf_op jit(solution)/shard_map/line_grads/pallas_call | solution.py:427
  203.6 0.7 collective-permute-start.26
  204.4 1.9 broadcast_select_fusion
  206.3 0.8 copy-done.18
  207.1 3.0 %assemble.1 = bf16[256,4096]{1,0:T(8,128)(2,1)} custom-call(s32[4]{0:T(128)} %pad_add_fusion.place_of, bf16[256,1024]{1,0:T(8,128)(2,1)} %copy-done.6, bf16[256,1024]{1,0:T(8,128)(2,1)} %copy-done.14, bf16[256,1024]{1,0:T(8,128)(2,1)} %copy-done.13, bf16[256,1024]{1,0:T(8,128)(2,1)} %copy-done.18), custom_call_target="tpu_custom_call" | custom-call | bytes 4194304 | tf_op jit(solution)/shard_map/assemble/pallas_call | solution.py:370
  (60 shorter events, 0.3 us)
Async XLA Ops:
  7.2 91.1 %all-gather.3.cloned.1.call-start = ((), (), s32[]{:S(2)}) async-start(), calls=%async_computation | async-start | bytes 2621440 | tf_op jit(solution)/shard_map/all_gather | solution.py:510
  10.8 28.0 %collective-permute-start = (bf16[33,128,128]{2,1,0:T(8,128)(2,1)S(1)}, bf16[33,128,128]{2,1,0:T(8,128)(2,1)S(1)}, u32[]{:S(2)}, u32[]{:S(2)}) collective-permute-start(bf16[33,128,128]{2,1,0:T(8,128)(2,1)S(1)} %pad_maximum_fusion), channel_id=1, source_target_pairs={{0,4},{12,8},{1,5},{13,9},{2,6},{14,10},{3,7},{15,11},{16,20},{28,... | collective-permute-start | bytes 3244040 | tf_op jit(solution)/shard_map/ppermute | solution.py:490
  15.8 23.0 %collective-permute-start.1 = (bf16[33,128,128]{2,1,0:T(8,128)(2,1)S(1)}, bf16[33,128,128]{2,1,0:T(8,128)(2,1)S(1)}, u32[]{:S(2)}, u32[]{:S(2)}) collective-permute-start(bf16[33,128,128]{2,1,0:T(8,128)(2,1)S(1)} %pad_maximum_fusion), channel_id=1, source_target_pairs={{4,8},{8,4},{5,9},{9,5},{6,10},{10,6},{7,11},{11,7},{20,24},{24,20... | collective-permute-start | bytes 3244040 | tf_op jit(solution)/shard_map/ppermute | solution.py:491
  38.8 12.0 %copy-start = (bf16[33,128,128]{2,1,0:T(8,128)(2,1)}, bf16[33,128,128]{2,1,0:T(8,128)(2,1)S(1)}, u32[]{:S(2)}) copy-start(bf16[33,128,128]{2,1,0:T(8,128)(2,1)S(1)} %collective-permute-done.near_a) | copy-start | bytes 3244036
  38.8 12.0 %copy-start.1 = (bf16[33,128,128]{2,1,0:T(8,128)(2,1)}, bf16[33,128,128]{2,1,0:T(8,128)(2,1)S(1)}, u32[]{:S(2)}) copy-start(bf16[33,128,128]{2,1,0:T(8,128)(2,1)S(1)} %collective-permute-done.1.far_a) | copy-start | bytes 3244036
  38.8 32.8 %collective-permute-start.4 = (bf16[33,128,128]{2,1,0:T(8,128)(2,1)S(1)}, bf16[33,128,128]{2,1,0:T(8,128)(2,1)S(1)}, u32[]{:S(2)}, u32[]{:S(2)}) collective-permute-start(bf16[33,128,128]{2,1,0:T(8,128)(2,1)S(1)} %collective-permute-done.near_a), channel_id=1, source_target_pairs={{4,8},{8,4},{5,9},{9,5},{6,10},{10,6},{7,11},{11,7},{20,24},{24,20... | collective-permute-start | bytes 3244040 | tf_op jit(solution)/shard_map/ppermute | solution.py:496
  39.6 32.1 %collective-permute-start.5 = (bf16[33,128,128]{2,1,0:T(8,128)(2,1)S(1)}, bf16[33,128,128]{2,1,0:T(8,128)(2,1)}, u32[]{:S(2)}, u32[]{:S(2)}) collective-permute-start(bf16[33,128,128]{2,1,0:T(8,128)(2,1)S(1)} %collective-permute-done.1.far_a), channel_id=1, source_target_pairs={{4,20},{20,4},{8,24},{24,8},{5,21},{21,5},{9,25},{25,9},{6,22},{22... | collective-permute-start | bytes 3244040 | tf_op jit(solution)/shard_map/ppermute | solution.py:497
  41.2 21.5 %collective-permute-start.3 = (bf16[256,1024]{1,0:T(8,128)(2,1)}, bf16[256,1024]{1,0:T(8,128)(2,1)}, u32[]{:S(2)}, u32[]{:S(2)}) collective-permute-start(bf16[256,1024]{1,0:T(8,128)(2,1)} %param.5), channel_id=1, source_target_pairs={{0,4},{12,8},{4,0},{8,12},{1,5},{13,9},{5,1},{9,13},{2,6},{14,10},... | collective-permute-start | bytes 1572872 | tf_op jit(solution)/shard_map/ppermute | solution.py:499
  49.6 22.0 %collective-permute-start.2 = (bf16[256,1024]{1,0:T(8,128)(2,1)}, bf16[256,1024]{1,0:T(8,128)(2,1)}, u32[]{:S(2)}, u32[]{:S(2)}) collective-permute-start(bf16[256,1024]{1,0:T(8,128)(2,1)} %constant_dynamic-slice_fusion.1), channel_id=1, source_target_pairs={{0,4},{12,8},{4,0},{8,12},{1,5},{13,9},{5,1},{9,13},{2,6},{14,10},... | collective-permute-start | bytes 1572872 | tf_op jit(solution)/shard_map/ppermute | solution.py:498
  71.6 10.0 %copy-start.2 = (bf16[33,128,128]{2,1,0:T(8,128)(2,1)}, bf16[33,128,128]{2,1,0:T(8,128)(2,1)S(1)}, u32[]{:S(2)}) copy-start(bf16[33,128,128]{2,1,0:T(8,128)(2,1)S(1)} %collective-permute-done.4.end_a) | copy-start | bytes 3244036
  71.7 26.6 %collective-permute-start.7 = (bf16[33,128,128]{2,1,0:T(8,128)(2,1)S(1)}, bf16[33,128,128]{2,1,0:T(8,128)(2,1)}, u32[]{:S(2)}, u32[]{:S(2)}) collective-permute-start(bf16[33,128,128]{2,1,0:T(8,128)(2,1)S(1)} %collective-permute-done.4.end_a), channel_id=1, source_target_pairs={{4,20},{20,4},{8,24},{24,8},{5,21},{21,5},{9,25},{25,9},{6,22},{22... | collective-permute-start | bytes 3244040 | tf_op jit(solution)/shard_map/ppermute | solution.py:507
  73.4 24.9 %collective-permute-start.6 = (bf16[32,128,128]{2,1,0:T(8,128)(2,1)}, bf16[32,128,128]{2,1,0:T(8,128)(2,1)}, u32[]{:S(2)}, u32[]{:S(2)}) collective-permute-start(bf16[32,128,128]{2,1,0:T(8,128)(2,1)} %get-tuple-element.57), channel_id=1, source_target_pairs={{0,4},{12,8},{1,5},{13,9},{2,6},{14,10},{3,7},{15,11},{16,20},{28,... | collective-permute-start | bytes 3145736 | tf_op jit(solution)/shard_map/ppermute | solution.py:506
  78.9 10.1 %collective-permute-start.8 = (bf16[256,1024]{1,0:T(8,128)(2,1)}, bf16[256,1024]{1,0:T(8,128)(2,1)S(1)}, u32[]{:S(2)}, u32[]{:S(2)}) collective-permute-start(bf16[256,1024]{1,0:T(8,128)(2,1)} %constant_dynamic-slice_fusion.1), channel_id=1, source_target_pairs={{4,8},{8,4},{5,9},{9,5},{6,10},{10,6},{7,11},{11,7},{20,24},{24,20... | collective-permute-start | bytes 1572872 | tf_op jit(solution)/shard_map/ppermute | solution.py:508
  79.6 9.5 %collective-permute-start.9 = (bf16[256,1024]{1,0:T(8,128)(2,1)}, bf16[256,1024]{1,0:T(8,128)(2,1)}, u32[]{:S(2)}, u32[]{:S(2)}) collective-permute-start(bf16[256,1024]{1,0:T(8,128)(2,1)} %collective-permute-done.2), channel_id=1, source_target_pairs={{4,8},{8,4},{5,9},{9,5},{6,10},{10,6},{7,11},{11,7},{20,24},{24,20... | collective-permute-start | bytes 1572872 | tf_op jit(solution)/shard_map/ppermute | solution.py:509
  81.6 6.2 %copy-start.20 = (bf16[256,1024]{1,0:T(8,128)(2,1)S(1)}, bf16[256,1024]{1,0:T(8,128)(2,1)}, u32[]{:S(2)}) copy-start(bf16[256,1024]{1,0:T(8,128)(2,1)} %param.5) | copy-start | bytes 1572868
  89.0 15.1 %copy-start.5 = (bf16[2,256,1024]{2,1,0:T(8,128)(2,1)}, bf16[2,256,1024]{2,1,0:T(8,128)(2,1)S(1)}, u32[]{:S(2)}) copy-start(bf16[2,256,1024]{2,1,0:T(8,128)(2,1)S(1)} %pad_maximum_fusion.1.two_upstream) | copy-start | bytes 3145732
  100.4 25.3 %collective-permute-start.12 = (bf16[2,256,1024]{2,1,0:T(8,128)(2,1)}, bf16[2,256,1024]{2,1,0:T(8,128)(2,1)}, u32[]{:S(2)}, u32[]{:S(2)}) collective-permute-start(bf16[2,256,1024]{2,1,0:T(8,128)(2,1)} %pad_maximum_fusion.2), channel_id=1, source_target_pairs={{4,0},{8,12},{5,1},{9,13},{6,2},{10,14},{7,3},{11,15},{20,16},{24,... | collective-permute-start | bytes 3145736 | tf_op jit(solution)/shard_map/ppermute | solution.py:521
  101.7 24.0 %collective-permute-start.14 = (bf16[2,256,1024]{2,1,0:T(8,128)(2,1)}, bf16[2,256,1024]{2,1,0:T(8,128)(2,1)S(1)}, u32[]{:S(2)}, u32[]{:S(2)}) collective-permute-start(bf16[2,256,1024]{2,1,0:T(8,128)(2,1)} %pad_maximum_fusion.2), channel_id=1, source_target_pairs={{4,6},{6,4},{8,10},{10,8},{5,7},{7,5},{9,11},{11,9},{20,22},{22,20... | collective-permute-start | bytes 3145736 | tf_op jit(solution)/shard_map/ppermute | solution.py:523
  102.4 23.2 %collective-permute-start.13 = (bf16[2,256,1024]{2,1,0:T(8,128)(2,1)S(1)}, bf16[2,256,1024]{2,1,0:T(8,128)(2,1)}, u32[]{:S(2)}, u32[]{:S(2)}) collective-permute-start(bf16[2,256,1024]{2,1,0:T(8,128)(2,1)S(1)} %pad_maximum_fusion.1.two_upstream), channel_id=1, source_target_pairs={{4,8},{8,4},{5,9},{9,5},{6,10},{10,6},{7,11},{11,7},{20,24},{24,20... | collective-permute-start | bytes 3145736 | tf_op jit(solution)/shard_map/ppermute | solution.py:522
  108.1 1.4 collective-permute-start.10
  108.8 0.7 collective-permute-start.11
  109.5 0.8 copy-start.17
  109.5 1.0 copy-start.19
  125.7 1.0 copy-start.7
  126.6 9.5 %collective-permute-start.16 = (bf16[2,256,1024]{2,1,0:T(8,128)(2,1)}, bf16[2,256,1024]{2,1,0:T(8,128)(2,1)}, u32[]{:S(2)}, u32[]{:S(2)}) collective-permute-start(bf16[2,256,1024]{2,1,0:T(8,128)(2,1)} %get-tuple-element.77), channel_id=1, source_target_pairs={{4,5},{5,4},{8,9},{9,8},{6,7},{7,6},{10,11},{11,10},{20,21},{21,20... | collective-permute-start | bytes 3145736 | tf_op jit(solution)/shard_map/ppermute | solution.py:535
  129.7 12.6 %copy-start.3 = (bf16[2,256,1024]{2,1,0:T(8,128)(2,1)}, bf16[2,256,1024]{2,1,0:T(8,128)(2,1)S(1)}, u32[]{:S(2)}) copy-start(bf16[2,256,1024]{2,1,0:T(8,128)(2,1)S(1)} %fusion.own_far) | copy-start | bytes 3145732
  129.8 10.5 %copy-start.11 = (bf16[256,1024]{1,0:T(8,128)(2,1)S(1)}, bf16[256,1024]{1,0:T(8,128)(2,1)}, u32[]{:S(2)}) copy-start(bf16[256,1024]{1,0:T(8,128)(2,1)} %get-tuple-element.74) | copy-start | bytes 1572868
  129.8 9.5 %collective-permute-start.17 = (bf16[2,256,1024]{2,1,0:T(8,128)(2,1)S(1)}, bf16[2,256,1024]{2,1,0:T(8,128)(2,1)S(1)}, u32[]{:S(2)}, u32[]{:S(2)}) collective-permute-start(bf16[2,256,1024]{2,1,0:T(8,128)(2,1)S(1)} %fusion.own_far), channel_id=1, source_target_pairs={{0,1},{1,0},{2,3},{3,2},{4,5},{5,4},{6,7},{7,6},{8,9},{9,8},{10,11... | collective-permute-start | bytes 3145736 | tf_op jit(solution)/shard_map/ppermute | solution.py:537
  129.8 9.4 %collective-permute-start.15 = (bf16[256,1024]{1,0:T(8,128)(2,1)}, bf16[256,1024]{1,0:T(8,128)(2,1)}, u32[]{:S(2)}, u32[]{:S(2)}) collective-permute-start(bf16[256,1024]{1,0:T(8,128)(2,1)} %get-tuple-element.75), channel_id=1, source_target_pairs={{4,6},{6,4},{8,10},{10,8},{5,7},{7,5},{9,11},{11,9},{20,22},{22,20... | collective-permute-start | bytes 1572872 | tf_op jit(solution)/shard_map/ppermute | solution.py:532
  131.5 27.5 %collective-permute-start.20 = (bf16[2,256,1024]{2,1,0:T(8,128)(2,1)}, bf16[2,256,1024]{2,1,0:T(8,128)(2,1)S(1)}, u32[]{:S(2)}, u32[]{:S(2)}) collective-permute-start(bf16[2,256,1024]{2,1,0:T(8,128)(2,1)} %collective-permute-done.12), channel_id=1, source_target_pairs={{0,2},{2,0},{12,14},{14,12},{1,3},{3,1},{13,15},{15,13},{16,18},{1... | collective-permute-start | bytes 3145736 | tf_op jit(solution)/shard_map/ppermute | solution.py:533
  134.9 36.7 %collective-permute-start.21 = (bf16[2,256,1024]{2,1,0:T(8,128)(2,1)}, bf16[2,256,1024]{2,1,0:T(8,128)(2,1)}, u32[]{:S(2)}, u32[]{:S(2)}) collective-permute-start(bf16[2,256,1024]{2,1,0:T(8,128)(2,1)} %collective-permute-done.13.far_upstream_m), channel_id=1, source_target_pairs={{4,0},{8,12},{5,1},{9,13},{6,2},{10,14},{7,3},{11,15},{20,16},{24,... | collective-permute-start | bytes 3145736 | tf_op jit(solution)/shard_map/ppermute | solution.py:534
  139.3 1.0 copy-start.9
  142.3 40.8 %copy-start.8 = (bf16[2,256,1024]{2,1,0:T(8,128)(2,1)S(1)}, bf16[2,256,1024]{2,1,0:T(8,128)(2,1)}, u32[]{:S(2)}) copy-start(bf16[2,256,1024]{2,1,0:T(8,128)(2,1)} %copy-done.7) | copy-start | bytes 3145732
  142.3 40.0 %collective-permute-start.18 = (bf16[256,1024]{1,0:T(8,128)(2,1)}, bf16[256,1024]{1,0:T(8,128)(2,1)S(1)}, u32[]{:S(2)}, u32[]{:S(2)}) collective-permute-start(bf16[256,1024]{1,0:T(8,128)(2,1)} %add.29), channel_id=1, source_target_pairs={{4,0},{8,12},{5,1},{9,13},{6,2},{10,14},{7,3},{11,15},{20,16},{24,... | collective-permute-start | bytes 1572872 | tf_op jit(solution)/shard_map/ppermute | solution.py:542
  143.7 38.6 %collective-permute-start.19 = (bf16[256,1024]{1,0:T(8,128)(2,1)}, bf16[256,1024]{1,0:T(8,128)(2,1)S(1)}, u32[]{:S(2)}, u32[]{:S(2)}) collective-permute-start(bf16[256,1024]{1,0:T(8,128)(2,1)} %get-tuple-element.82), channel_id=1, source_target_pairs={{4,6},{6,4},{8,10},{10,8},{5,7},{7,5},{9,11},{11,9},{20,22},{22,20... | collective-permute-start | bytes 1572872 | tf_op jit(solution)/shard_map/ppermute | solution.py:543
  182.4 0.8 copy-start.15
  183.2 1.0 copy-start.12
  183.2 1.2 copy-start.16
  183.6 4.0 %copy-start.4 = (bf16[2,256,1024]{2,1,0:T(8,128)(2,1)}, bf16[2,256,1024]{2,1,0:T(8,128)(2,1)S(1)}, u32[]{:S(2)}) copy-start(bf16[2,256,1024]{2,1,0:T(8,128)(2,1)S(1)} %add.31.side_far) | copy-start | bytes 3145732
  183.6 4.0 %collective-permute-start.25 = (bf16[2,256,1024]{2,1,0:T(8,128)(2,1)S(1)}, bf16[2,256,1024]{2,1,0:T(8,128)(2,1)S(1)}, u32[]{:S(2)}, u32[]{:S(2)}) collective-permute-start(bf16[2,256,1024]{2,1,0:T(8,128)(2,1)S(1)} %add.31.side_far), channel_id=1, source_target_pairs={{0,1},{1,0},{2,3},{3,2},{4,5},{5,4},{6,7},{7,6},{8,9},{9,8},{10,11... | collective-permute-start | bytes 3145736 | tf_op jit(solution)/shard_map/ppermute | solution.py:552
  184.5 19.2 %copy-start.6 = (bf16[256,1024]{1,0:T(8,128)(2,1)}, bf16[256,1024]{1,0:T(8,128)(2,1)S(1)}, u32[]{:S(2)}) copy-start(bf16[256,1024]{1,0:T(8,128)(2,1)S(1)} %add_select_fusion.own) | copy-start | bytes 1572868
  184.5 19.1 %collective-permute-start.23 = (bf16[256,1024]{1,0:T(8,128)(2,1)S(1)}, bf16[256,1024]{1,0:T(8,128)(2,1)S(1)}, u32[]{:S(2)}, u32[]{:S(2)}) collective-permute-start(bf16[256,1024]{1,0:T(8,128)(2,1)S(1)} %add_select_fusion.own), channel_id=1, source_target_pairs={{0,2},{2,0},{1,3},{3,1},{4,6},{6,4},{5,7},{7,5},{8,10},{10,8},{9,1... | collective-permute-start | bytes 1572872 | tf_op jit(solution)/shard_map/ppermute | solution.py:554
  186.3 17.4 %collective-permute-start.24 = (bf16[256,1024]{1,0:T(8,128)(2,1)S(1)}, bf16[256,1024]{1,0:T(8,128)(2,1)S(1)}, u32[]{:S(2)}, u32[]{:S(2)}) collective-permute-start(bf16[256,1024]{1,0:T(8,128)(2,1)S(1)} %add_select_fusion.own), channel_id=1, source_target_pairs={{0,1},{1,0},{2,3},{3,2},{4,5},{5,4},{6,7},{7,6},{8,9},{9,8},{10,11... | collective-permute-start | bytes 1572872 | tf_op jit(solution)/shard_map/ppermute | solution.py:554
  186.3 18.1 %collective-permute-start.22 = (bf16[256,1024]{1,0:T(8,128)(2,1)}, bf16[256,1024]{1,0:T(8,128)(2,1)}, u32[]{:S(2)}, u32[]{:S(2)}) collective-permute-start(bf16[256,1024]{1,0:T(8,128)(2,1)} %get-tuple-element.89), channel_id=1, source_target_pairs={{4,0},{8,12},{5,1},{9,13},{6,2},{10,14},{7,3},{11,15},{20,16},{24,... | collective-permute-start | bytes 1572872 | tf_op jit(solution)/shard_map/ppermute | solution.py:555
  187.6 1.0 copy-start.10
  203.6 2.7 %copy-start.13 = (bf16[256,1024]{1,0:T(8,128)(2,1)}, bf16[256,1024]{1,0:T(8,128)(2,1)S(1)}, u32[]{:S(2)}) copy-start(bf16[256,1024]{1,0:T(8,128)(2,1)S(1)} %collective-permute-done.23.by_tensor) | copy-start | bytes 1572868
  203.6 2.7 %copy-start.14 = (bf16[256,1024]{1,0:T(8,128)(2,1)}, bf16[256,1024]{1,0:T(8,128)(2,1)S(1)}, u32[]{:S(2)}) copy-start(bf16[256,1024]{1,0:T(8,128)(2,1)S(1)} %collective-permute-done.24.by_core) | copy-start | bytes 1572868
  203.6 2.6 %collective-permute-start.26 = (bf16[256,1024]{1,0:T(8,128)(2,1)S(1)}, bf16[256,1024]{1,0:T(8,128)(2,1)S(1)}, u32[]{:S(2)}, u32[]{:S(2)}) collective-permute-start(bf16[256,1024]{1,0:T(8,128)(2,1)S(1)} %collective-permute-done.23.by_tensor), channel_id=1, source_target_pairs={{0,1},{1,0},{2,3},{3,2},{4,5},{5,4},{6,7},{7,6},{8,9},{9,8},{10,11... | collective-permute-start | bytes 1572872 | tf_op jit(solution)/shard_map/ppermute | solution.py:562
  206.3 0.8 copy-start.18
Sparse Core Ops, SparseCore 0:
  71.8 21.1 all-gather.2

commit v11 on v7

--- a/solution.py
+++ b/solution.py
@@ -252,13 +252,11 @@
     )(place_of, ids_1, ids_3, partial, near_b, end_b, end_upstream, upstream)
 
 
-def forward_kernel(
-    place_of, ids_1, ids_3, partial, near_b, end_b, tokens, gathered, proj, end_proj, held, sem
-):
+def forward_kernel(place_of, ids_1, ids_3, partial, near_b, end_b, tokens, proj, held, sem):
     half_slots = near_b.shape[0]
     other = (1 - place_of[1]) * half_slots
-    depth, width = held.shape
-    parts, rows, part_width = gathered.shape
+    width = held.shape[1]
+    rows = proj.shape[0]
     step = 256
 
     @pl.when(place_of[0] == 1)
@@ -271,38 +269,38 @@
 
         @pl.loop(0, width // step, unroll=2)
         def forward(n):
-            c = pl.multiple_of(n * step, step)
-            acc = jnp.zeros((rows, step), jnp.float32)
-            for q in range(parts):
-                acc += jnp.dot(
-                    gathered[q],
-                    held[q * part_width : (q + 1) * part_width, pl.ds(c, step)],
-                    preferred_element_type=jnp.float32,
-                )
-            end_proj[:, pl.ds(c, step)] = acc.astype(end_proj.dtype)
-            proj[:, pl.ds(c, step)] = jnp.dot(
-                tokens[...], held[:, pl.ds(c, step)], preferred_element_type=jnp.float32
-            ).astype(proj.dtype)
-
-
-def project_forward(place_of, ids_1, ids_3, partial, near_b, end_b, tokens, gathered):
+            c = pl.ds(pl.multiple_of(n * step, step), step)
+            if len(tokens.shape) == 2:
+                acc = jnp.dot(tokens[...], held[:, c], preferred_element_type=jnp.float32)
+            else:
+                part_width = tokens.shape[2]
+                acc = jnp.zeros((rows, step), jnp.float32)
+                for q in range(tokens.shape[0]):
+                    acc += jnp.dot(
+                        tokens[q],
+                        held[q * part_width : (q + 1) * part_width, c],
+                        preferred_element_type=jnp.float32,
+                    )
+            proj[:, c] = acc.astype(proj.dtype)
+
+
+def project_forward(place_of, ids_1, ids_3, partial, near_b, end_b, tokens):
     depth, width = partial.shape
-    rows = tokens.shape[0]
-    out = jax.ShapeDtypeStruct((rows, width), jnp.bfloat16)
+    rows = tokens.shape[-2]
     return pl.pallas_call(
         forward_kernel,
-        out_shape=(out, out),
-        in_specs=[whole(pltpu.SMEM)] * 3 + [whole(pl.ANY)] + [whole()] * 4,
-        out_specs=(whole(),) * 2,
+        out_shape=jax.ShapeDtypeStruct((rows, width), jnp.bfloat16),
+        in_specs=[whole(pltpu.SMEM)] * 3 + [whole(pl.ANY)] + [whole()] * 3,
+        out_specs=whole(),
         scratch_shapes=[pltpu.VMEM((depth, width), jnp.bfloat16), pltpu.SemaphoreType.DMA],
         compiler_params=pltpu.CompilerParams(vmem_limit_bytes=VMEM_LIMIT),
         cost_estimate=pl.CostEstimate(
-            flops=4 * rows * depth * width,
-            bytes_accessed=depth * width * 2 + rows * (depth + width) * 4,
+            flops=2 * rows * depth * width,
+            bytes_accessed=depth * width * 2 + rows * (depth + width) * 2,
             transcendentals=0,
         ),
         name="project_forward",
-    )(place_of, ids_1, ids_3, partial, near_b, end_b, tokens, gathered)
+    )(place_of, ids_1, ids_3, partial, near_b, end_b, tokens)
 
 
 def split_kernel(place_of, keep, *refs):
@@ -361,15 +359,24 @@
     )(place_of, *quarters)
 
 
-def line_grads_kernel(pairs_n, ids, *refs):
-    pairs = [(refs[2 * k], refs[2 * k + 1]) for k in range(pairs_n)]
-    grads = refs[-1]
-    start = refs[2 * pairs_n] if len(refs) > 2 * pairs_n + 1 else None
+def line_grads_kernel(kinds, place_of, ids, *refs):
+    refs = list(refs)
+    scratch = [refs.pop() for kind in kinds if kind == "split"]
+    grads = refs.pop()
+    pairs = []
+    for kind in kinds:
+        if kind == "split":
+            mine, theirs, target = refs.pop(0), refs.pop(0), scratch.pop()
+            for x in range(2):
+                target[2 * x + place_of[3]] = mine[x]
+                target[2 * x + 1 - place_of[3]] = theirs[x]
+            pairs.append((target, refs.pop(0)))
+        else:
+            pairs.append((refs.pop(0), refs.pop(0)))
+    start = refs.pop(0) if refs else None
     slots, size = grads.shape[0], grads.shape[1]
-    first = pairs[0][0]
-    cols_n = pairs[0][1].shape[1] // size
-    rows_n = first.shape[-1] // size * (first.shape[0] if len(first.shape) == 3 else 1)
-    total = rows_n * cols_n
+    first, cols_n = pairs[0][0], pairs[0][1].shape[1] // size
+    total = math.prod(first.shape) // first.shape[-2] // size * cols_n
     group = math.gcd(slots, 8)
 
     @pl.loop(0, slots // group)
@@ -391,23 +398,27 @@
             grads[s] = jnp.where(ids[s] < total, acc, 0.0).astype(grads.dtype)
 
 
-def line_grads(ids, pairs, start, size, out_dtype):
+def line_grads(place_of, ids, pairs, start, size, out_dtype):
     slots = ids.shape[0]
-    rows = pairs[0][1].shape[0]
-    flat = [a for pair in pairs for a in pair] + ([] if start is None else [start])
-    return pl.pallas_call(
-        functools.partial(line_grads_kernel, len(pairs)),
+    kinds = tuple("split" if len(p) == 3 else "plain" for p in pairs)
+    flat = [a for p in pairs for a in p] + ([] if start is None else [start])
+    split = [
+        pltpu.VMEM((4,) + p[0].shape[1:], jnp.bfloat16) for p in pairs if len(p) == 3
+    ]
+    return pl.pallas_call(
+        functools.partial(line_grads_kernel, kinds),
         out_shape=jax.ShapeDtypeStruct((slots, size, size), out_dtype),
-        in_specs=[whole(pltpu.SMEM)] + [whole()] * len(flat),
+        in_specs=[whole(pltpu.SMEM)] * 2 + [whole()] * len(flat),
         out_specs=whole(),
-        compiler_params=pltpu.CompilerParams(vmem_limit_bytes=VMEM_LIMIT),
-        cost_estimate=pl.CostEstimate(
-            flops=2 * len(pairs) * slots * rows * size * size,
+        scratch_shapes=split,
+        compiler_params=pltpu.CompilerParams(vmem_limit_bytes=VMEM_LIMIT),
+        cost_estimate=pl.CostEstimate(
+            flops=512 * len(pairs) * slots * size * size,
             bytes_accessed=sum(2 * a.size for a in flat) + 4 * slots * size * size,
             transcendentals=0,
         ),
         name="line_grads",
-    )(ids, *flat)
+    )(place_of, ids, *flat)
 
 
 INWARD = ((0, 1), (3, 2))
@@ -437,9 +448,14 @@
     middle = (at_z == 1) | (at_z == 2)
     place_of = jnp.stack([middle.astype(jnp.int32), half, at_tensor, at_replica])
     along = functools.partial(lax.ppermute, axis_name="dp")
-    across = functools.partial(lax.ppermute, axis_name="groups", perm=SWAP)
-    sideways = functools.partial(lax.ppermute, axis_name="tensor", perm=SWAP)
-    cores = functools.partial(lax.ppermute, axis_name="replica", perm=SWAP)
+    across = functools.partial(
+        lax.ppermute, axis_name=("groups", "dp"), perm=((1, 5), (5, 1), (2, 6), (6, 2))
+    )
+    middle_swap = ((2, 3), (3, 2), (4, 5), (5, 4))
+    sideways = functools.partial(lax.ppermute, axis_name=("dp", "tensor"), perm=middle_swap)
+    cores = functools.partial(lax.ppermute, axis_name=("dp", "replica"), perm=middle_swap)
+    everywhere = functools.partial(lax.ppermute, axis_name="tensor", perm=SWAP)
+    all_cores = functools.partial(lax.ppermute, axis_name="replica", perm=SWAP)
     stage = lax.optimization_barrier
 
     mine = lax.dynamic_slice_in_dim(blocks, half * half_slots, half_slots, 0)
@@ -485,26 +501,32 @@
     end_got = sideways(end_give)
     own_keep, own_give = add_split(place_of, own_keep, cores(own_give))
     both_3o = along(both_3m, perm=OUTWARD)
-    tokens_2 = lax.all_gather(both_2m[:rows] + both_2o[:rows], INNER)
-    upstream_2 = both_2m[rows:] + both_2o[rows:]
-    end_got, own_give, own_keep = stage((end_got, own_give, own_keep))
+    end_proj = project_forward(place_of, ids_1, ids_3, partial, *last, tokens_1)
+    end_got, own_give, own_keep, end_proj, both_2o = stage(
+        (end_got, own_give, own_keep, end_proj, both_2o)
+    )
 
     sum_out = along(end_keep + end_got, perm=OUTWARD)
     own_got = sideways(own_give)
-    proj, end_proj = project_forward(place_of, ids_1, ids_3, partial, *last, tokens, tokens_1)
-    sum_out, own_got, both_3o, proj, end_proj = stage((sum_out, own_got, both_3o, proj, end_proj))
-
-    tokens_3 = lax.all_gather(both_3m[:rows] + both_3o[:rows], INNER)
+    side_2 = lax.all_gather(both_2m[:rows] + both_2o[:rows], "tensor")
+    upstream_2 = both_2m[rows:] + both_2o[rows:]
+    proj = project_forward(place_of, ids_1, ids_3, partial, *last, tokens)
+    sum_out, own_got, both_3o, proj = stage((sum_out, own_got, both_3o, proj))
+
+    side_3 = lax.all_gather(both_3m[:rows] + both_3o[:rows], "tensor")
     upstream_3 = both_3m[rows:] + both_3o[rows:]
     quarter = jnp.where(middle, own_keep + own_got, sum_out)
     proj_out = along(end_proj, perm=OUTWARD)
-    pairs = ((tokens, upstream), (tokens_1, upstream_1), (tokens_2, upstream_2))
-    grads = line_grads(block_ids, pairs, None, size, jnp.float32)
-    by_tensor, by_core, grads = stage((sideways(quarter), cores(quarter), grads))
-    by_both = cores(by_tensor)
+    pairs = ((tokens, upstream), (tokens_1, upstream_1))
+    grads = line_grads(place_of, block_ids, pairs, None, size, jnp.float32)
+    by_tensor, by_core, grads, side_2, side_3 = stage(
+        (everywhere(quarter), all_cores(quarter), grads, side_2, side_3)
+    )
+    by_both = all_cores(by_tensor)
     projected = jnp.where(middle, proj, proj_out)
     token_grad = assemble(place_of, (quarter, by_core, by_tensor, by_both))
-    grads = line_grads(block_ids, ((tokens_3, upstream_3),), grads, size, jnp.bfloat16)
+    pairs = ((side_2, all_cores(side_2), upstream_2), (side_3, all_cores(side_3), upstream_3))
+    grads = line_grads(place_of, block_ids, pairs, grads, size, jnp.bfloat16)
     return projected, token_grad, grads
 
 

time: 212 us -> 254 us (1.20)
  waiting for transfers between devices: 101 us -> 130 us
  starting transfers between devices: 29.8 us -> 35.8 us
  Pallas kernels: 47.3 us -> 50 us
    ppermute x1, waiting for transfers between devices: 3.61 us -> 24.5 us  [line_body(): both_3o = along(both_3m, perm=OUTWARD)]
    ppermute x1, waiting for transfers between devices: 0.01 us -> 14.6 us  [line_body(): proj_out = along(end_proj, perm=OUTWARD)]
    ppermute x1, waiting for transfers between devices: 10.7 us -> 0.01 us  [line_body(): end_got = sideways(end_give)]
    all_gather x2, waiting for transfers between devices: 1.76 us -> 8.83 us  [the longest x1 8.83 us: line_body(): side_3 = lax.all_gather(both_3m[:rows] + both_3o[:rows], 'tensor')]
    pallas_call x3 -> x4, Pallas kernels: 25.6 us -> 28.3 us  [the longest x2 22 us: line_grads(): pl.pallas_call(functools.partial(line_grads_kernel, kinds), out_shape=jax...]
    ppermute x1, waiting for transfers between devices: 16 us -> 18.6 us  [line_body(): both_2o = along(both_2m, perm=OUTWARD)]
  transfers between devices with their start and end apart: 24 -> 26, of which waited for: 13 -> 9; matrix products, arithmetic and copies ran while one was open for 3% -> 4% of each run, Pallas kernels for 18% -> 15%
where the time goes in v11:
time: 254 us; the launch traced here: 252 us
  waiting for transfers between devices  130 us (51%)
  Pallas kernels  50 us (20%)
  starting transfers between devices  35.8 us (14%)
  between operations  14.1 us (6%)
  other arithmetic  11.8 us (5%)
  local copies, waits for them, and re-layouts  10 us (4%)
    ppermute x1, waiting for transfers between devices, line_body(): both_3o = along(both_3m, perm=OUTWARD)  24.5 us
    ppermute x1, waiting for transfers between devices, line_body(): near_a = along(mine, perm=INWARD)  22.3 us
    pallas_call x2, Pallas kernels, line_grads(): pl.pallas_call(functools.partial(line_grads_kernel, kinds), out_shape=jax...  22 us
    ppermute x1, waiting for transfers between devices, line_body(): both_1 = along(both, perm=PAIRS)  21.7 us
    ppermute x1, waiting for transfers between devices, line_body(): both_2o = along(both_2m, perm=OUTWARD)  18.6 us
    ppermute x1, waiting for transfers between devices, line_body(): proj_out = along(end_proj, perm=OUTWARD)  14.6 us
    ppermute x1, waiting for transfers between devices, line_body(): sum_out = along(end_keep + end_got, perm=OUTWARD)  9.5 us
    all_gather x1, waiting for transfers between devices, line_body(): side_3 = lax.all_gather(both_3m[:rows] + both_3o[:rows], 'tensor')  8.83 us
  transfers between devices with their start and end apart: 26, of which 9 were waited for; matrix products, arithmetic and copies ran while one was open for 4% of the time, Pallas kernels for 15%

profile of v11, /device:TPU:0, one launch (start us, length us, event | category | flops | bytes accessed | tf_op | source)
XLA Modules:
  0.0 252.0 jit_solution(17489919711586034844)
XLA Ops:
  7.2 0.7 convert_element_type.26
  7.9 0.1 convert_element_type.27
  8.0 2.7 %constant_dynamic-slice_fusion.1 = (bf16[32,128,128]{2,1,0:T(8,128)(2,1)}, bf16[32,128,128]{2,1,0:T(8,128)(2,1)S(1)}) fusion(bf16[64,128,128]{2,1,0:T(8,128)(2,1)} %own.1, s32[]{:T(128)S(6)} %select_n.23, s32[]{:T(128)S(6)} %select_n.22), kind=kLoop, calls=%fused_computation.9 | loop fusion | bytes 4194312 | tf_op jit(solution)/shard_map/dynamic_slice | solution.py:462
  10.7 0.1 pad_maximum_fusion
  10.8 1.1 constant_dynamic-slice_fusion
  11.9 0.1 pad_maximum_fusion.1
  12.0 5.0 %collective-permute-start = (bf16[33,128,128]{2,1,0:T(8,128)(2,1)S(1)}, bf16[33,128,128]{2,1,0:T(8,128)(2,1)S(1)}, u32[]{:S(2)}, u32[]{:S(2)}) collective-permute-start(bf16[33,128,128]{2,1,0:T(8,128)(2,1)S(1)} %pad_maximum_fusion), channel_id=1, source_target_pairs={{0,4},{12,8},{1,5},{13,9},{2,6},{14,10},{3,7},{15,11},{16,20},{28,... | collective-permute-start | bytes 3244040 | tf_op jit(solution)/shard_map/ppermute | solution.py:468
  17.0 0.7 collective-permute-start.1
  17.8 22.3 %collective-permute-done.near_a = bf16[33,128,128]{2,1,0:T(8,128)(2,1)S(1)} collective-permute-done((bf16[33,128,128]{2,1,0:T(8,128)(2,1)S(1)}, bf16[33,128,128]{2,1,0:T(8,128)(2,1)S(1)}, u32[]{:S(2)}, u32[]{:S(2)}) %collective-permute-start) | collective-permute-done | bytes 1081376 | tf_op jit(solution)/shard_map/ppermute | solution.py:468
  40.1 1.7 collective-permute-start.3
  41.7 1.6 collective-permute-start.4
  43.4 7.5 %collective-permute-start.2 = (bf16[512,1024]{1,0:T(8,128)(2,1)S(1)}, bf16[512,1024]{1,0:T(8,128)(2,1)S(1)}, u32[]{:S(2)}, u32[]{:S(2)}) collective-permute-start(bf16[512,1024]{1,0:T(8,128)(2,1)S(1)} %pad_maximum_fusion.1), channel_id=1, source_target_pairs={{0,4},{12,8},{4,0},{8,12},{1,5},{13,9},{5,1},{9,13},{2,6},{14,10},... | collective-permute-start | bytes 3145736 | tf_op jit(solution)/shard_map/ppermute | solution.py:474
  50.8 21.7 %collective-permute-done.2 = bf16[512,1024]{1,0:T(8,128)(2,1)S(1)} collective-permute-done((bf16[512,1024]{1,0:T(8,128)(2,1)S(1)}, bf16[512,1024]{1,0:T(8,128)(2,1)S(1)}, u32[]{:S(2)}, u32[]{:S(2)}) %collective-permute-start.2) | collective-permute-done | bytes 1048608 | tf_op jit(solution)/shard_map/ppermute | solution.py:474
  72.6 1.0 copy-done.10
  73.6 1.0 fusion
  74.6 0.0 all-gather.9.cloned.1.call-start
  74.7 0.7 collective-permute-start.6
  75.4 5.4 %collective-permute-start.5 = (bf16[32,128,128]{2,1,0:T(8,128)(2,1)}, bf16[32,128,128]{2,1,0:T(8,128)(2,1)S(1)}, u32[]{:S(2)}, u32[]{:S(2)}) collective-permute-start(bf16[32,128,128]{2,1,0:T(8,128)(2,1)} %get-tuple-element.60), channel_id=1, source_target_pairs={{0,4},{12,8},{1,5},{13,9},{2,6},{14,10},{3,7},{15,11},{16,20},{28,... | collective-permute-start | bytes 3145736 | tf_op jit(solution)/shard_map/ppermute | solution.py:478
  80.8 1.7 collective-permute-start.7
  82.5 0.7 pad_add_fusion.place_of
  83.1 1.2 bitcast_convert_fusion
  84.4 1.3 bitcast_convert_fusion.1.ids_3
  85.6 8.8 %place_first.1 = (bf16[4096,1024]{1,0:T(8,128)(2,1)}, bf16[1024,4096]{1,0:T(8,128)(2,1)}) custom-call(s32[4]{0:T(128)} %pad_add_fusion.place_of, s32[64]{0:T(128)} %ids.3, s32[64]{0:T(128)} %get-tuple-element.110.ids_1, s32[64]{0:T(128)} %get-tuple-element.109.ids_2, s32[64]{0:T(128)} %bitcast_convert_fusion.1.ids_3, bf16[64,128,128]{2,1,0:T(8,128)(2,1)} %own.1, ...), custom_call_target="tpu_custom_call" | custom-call | bytes 25165824 | tf_op jit(solution)/shard_map/place_first/pallas_call | solution.py:177
  94.4 6.5 %collective-permute-done.5.near_b = bf16[32,128,128]{2,1,0:T(8,128)(2,1)S(1)} collective-permute-done((bf16[32,128,128]{2,1,0:T(8,128)(2,1)}, bf16[32,128,128]{2,1,0:T(8,128)(2,1)S(1)}, u32[]{:S(2)}, u32[]{:S(2)}) %collective-permute-start.5) | collective-permute-done | bytes 1048608 | tf_op jit(solution)/shard_map/ppermute | solution.py:478
  101.0 0.7 collective-permute-start.10
  101.7 1.3 collective-permute-start.11
  103.0 3.9 %project_back.1 = (bf16[2,256,1024]{2,1,0:T(8,128)(2,1)}, bf16[2,256,1024]{2,1,0:T(8,128)(2,1)}, bf16[2,256,1024]{2,1,0:T(8,128)(2,1)}, bf16[256,1024]{1,0:T(8,128)(2,1)}, bf16[256,1024]{1,0:T(8,128)(2,1)}) custom-call(s32[4]{0:T(128)} %pad_add_fusion.place_of, s32[64]{0:T(128)} %get-tuple-element.110.ids_1, s32[64]{0:T(128)} %bitcast_convert_fusion.1.ids_3, ...), custom_call_target="tpu_custom_call" | custom-call | flops 4294967296 | bytes 13631488 | tf_op jit(solution)/shard_map/project_back/pallas_call | solution.py:235
  106.9 0.7 collective-permute-start.8
  107.6 0.7 collective-permute-start.9
  108.3 0.8 copy-done.17
  109.1 0.2 copy-done.19
  109.3 3.0 %add_split.2 = (bf16[256,1024]{1,0:T(8,128)(2,1)}, bf16[256,1024]{1,0:T(8,128)(2,1)}) custom-call(s32[4]{0:T(128)} %pad_add_fusion.place_of, bf16[2,256,1024]{2,1,0:T(8,128)(2,1)} %get-tuple-element.69.keep, bf16[256,1024]{1,0:T(8,128)(2,1)} %copy-done.17, bf16[256,1024]{1,0:T(8,128)(2,1)} %copy-done.19), custom_call_target="tpu_custom_call" | custom-call | flops 524288 | bytes 3145728 | tf_op jit(solution)/shard_map/add_split/pallas_call | solution.py:324
  112.3 18.6 %collective-permute-done.11 = bf16[512,1024]{1,0:T(8,128)(2,1)} collective-permute-done((bf16[512,1024]{1,0:T(8,128)(2,1)}, bf16[512,1024]{1,0:T(8,128)(2,1)}, u32[]{:S(2)}, u32[]{:S(2)}) %collective-permute-start.11) | collective-permute-done | bytes 1048608 | tf_op jit(solution)/shard_map/ppermute | solution.py:491
  130.9 0.7 collective-permute-start.13
  131.6 1.5 collective-permute-start.12
  133.1 3.1 %project_forward.2 = bf16[256,1024]{1,0:T(8,128)(2,1)} custom-call(s32[4]{0:T(128)} %pad_add_fusion.place_of, s32[64]{0:T(128)} %get-tuple-element.110.ids_1, s32[64]{0:T(128)} %bitcast_convert_fusion.1.ids_3, bf16[4096,1024]{1,0:T(8,128)(2,1)} %get-tuple-element.83.partial, bf16[32,128,128]{2,1,0:T(8,128)(2,1)} %copy-done.1, bf16[33,128,128]{2,1,0:T(8,128)(2,1)} %copy-done, ...), custom_call_target="tpu_custom_call" | custom-call | flops 2147483648 | bytes 11010048 | tf_op jit(solution)/shard_map/project_forward/pallas_call | solution.py:290
  136.2 1.3 collective-permute-start.16
  137.5 1.0 copy-done.9
  138.5 3.0 %add_split.3 = (bf16[256,1024]{1,0:T(8,128)(2,1)}, bf16[256,1024]{1,0:T(8,128)(2,1)}) custom-call(s32[4]{0:T(128)} %pad_add_fusion.place_of, bf16[2,256,1024]{2,1,0:T(8,128)(2,1)} %get-tuple-element.79.keep, bf16[2,256,1024]{2,1,0:T(8,128)(2,1)} %copy-done.9), custom_call_target="tpu_custom_call" | custom-call | flops 524288 | bytes 3145728 | tf_op jit(solution)/shard_map/add_split/pallas_call | solution.py:324
  141.5 2.7 %slice_add_fusion.1 = (bf16[256,1024]{1,0:T(8,128)(2,1)}, bf16[256,1024]{1,0:T(8,128)(2,1)}) fusion(bf16[512,1024]{1,0:T(8,128)(2,1)} %collective-permute-done.11, bf16[512,1024]{1,0:T(8,128)(2,1)} %collective-permute-done.7), kind=kLoop, calls=%fused_computation.3 | loop fusion | flops 524288 | bytes 3145728 | tf_op jit(solution)/shard_map/add | solution.py:512
  144.2 0.0 all-gather.11.cloned.1.call-start
  144.3 2.1 add.34
  146.3 1.3 collective-permute-start.14
  147.6 0.7 collective-permute-start.15
  148.3 3.2 %project_forward.3 = bf16[256,1024]{1,0:T(8,128)(2,1)} custom-call(s32[4]{0:T(128)} %pad_add_fusion.place_of, s32[64]{0:T(128)} %get-tuple-element.110.ids_1, s32[64]{0:T(128)} %bitcast_convert_fusion.1.ids_3, bf16[4096,1024]{1,0:T(8,128)(2,1)} %get-tuple-element.83.partial, bf16[32,128,128]{2,1,0:T(8,128)(2,1)} %copy-done.1, bf16[33,128,128]{2,1,0:T(8,128)(2,1)} %copy-done, ...), custom_call_target="tpu_custom_call" | custom-call | flops 2147483648 | bytes 11010048 | tf_op jit(solution)/shard_map/project_forward/pallas_call | solution.py:290
  151.6 24.5 %collective-permute-done.16 = bf16[512,1024]{1,0:T(8,128)(2,1)S(1)} collective-permute-done((bf16[512,1024]{1,0:T(8,128)(2,1)S(1)}, bf16[512,1024]{1,0:T(8,128)(2,1)S(1)}, u32[]{:S(2)}, u32[]{:S(2)}) %collective-permute-start.16) | collective-permute-done | bytes 1048608 | tf_op jit(solution)/shard_map/ppermute | solution.py:503
  176.1 9.5 %collective-permute-done.14 = bf16[256,1024]{1,0:T(8,128)(2,1)S(1)} collective-permute-done((bf16[256,1024]{1,0:T(8,128)(2,1)}, bf16[256,1024]{1,0:T(8,128)(2,1)S(1)}, u32[]{:S(2)}, u32[]{:S(2)}) %collective-permute-start.14) | collective-permute-done | bytes 524320 | tf_op jit(solution)/shard_map/ppermute | solution.py:509
  185.6 1.1 slice_add_fusion
  186.8 1.1 add_select_fusion.own
  187.9 0.6 collective-permute-start.18
  188.5 10.7 %line_grads.2.refs_6_ = f32[64,128,128]{2,1,0:T(8,128)} custom-call(s32[4]{0:T(128)} %pad_add_fusion.place_of, s32[64]{0:T(128)} %ids.3, bf16[256,4096]{1,0:T(8,128)(2,1)} %refs_0_.1, bf16[256,1024]{1,0:T(8,128)(2,1)} %refs_1_.1, bf16[4,256,1024]{2,1,0:T(8,128)(2,1)} %bitcast.17, bf16[256,1024]{1,0:T(8,128)(2,1)} %get-tuple-element.107.end_upstream.refs_3_), custom_call_target="tpu_custom_call" | custom-call | flops 1073741824 | bytes 9437184 | tf_op jit(solution)/shard_map/line_grads/pallas_call | solution.py:408
  199.2 3.6 %collective-permute-done.18.by_tensor = bf16[256,1024]{1,0:T(8,128)(2,1)S(1)} collective-permute-done((bf16[256,1024]{1,0:T(8,128)(2,1)S(1)}, bf16[256,1024]{1,0:T(8,128)(2,1)S(1)}, u32[]{:S(2)}, u32[]{:S(2)}) %collective-permute-start.18) | collective-permute-done | bytes 524320 | tf_op jit(solution)/shard_map/ppermute | solution.py:523
  202.9 8.8 %all-gather.11.cloned.1.call-done = bf16[512,1024]{1,0:T(8,128)(2,1)} async-done(((bf16[256,1024]{1,0:T(8,128)(2,1)}), bf16[512,1024]{1,0:T(8,128)(2,1)}) %all-gather.11.cloned.1.call-update) | async-done | bytes 1048592 | tf_op jit(solution)/shard_map/all_gather | solution.py:516
  211.7 0.1 collective-permute-start.21
  211.7 0.5 collective-permute-start.22
  212.2 1.3 collective-permute-start.17
  213.5 0.1 collective-permute-start.20
  213.6 14.6 %collective-permute-done.17 = bf16[256,1024]{1,0:T(8,128)(2,1)S(1)} collective-permute-done((bf16[256,1024]{1,0:T(8,128)(2,1)}, bf16[256,1024]{1,0:T(8,128)(2,1)S(1)}, u32[]{:S(2)}, u32[]{:S(2)}) %collective-permute-start.17) | collective-permute-done | bytes 524320 | tf_op jit(solution)/shard_map/ppermute | solution.py:519
  228.2 0.8 broadcast_select_fusion
  229.0 0.8 copy-done.18
  229.9 3.0 %assemble.1 = bf16[256,4096]{1,0:T(8,128)(2,1)} custom-call(s32[4]{0:T(128)} %pad_add_fusion.place_of, bf16[256,1024]{1,0:T(8,128)(2,1)} %copy-done.2, bf16[256,1024]{1,0:T(8,128)(2,1)} %copy-done.15, bf16[256,1024]{1,0:T(8,128)(2,1)} %copy-done.14, bf16[256,1024]{1,0:T(8,128)(2,1)} %copy-done.18), custom_call_target="tpu_custom_call" | custom-call | bytes 4194304 | tf_op jit(solution)/shard_map/assemble/pallas_call | solution.py:349
  232.9 1.0 copy-done.7
  233.8 0.3 copy-done.8
  234.2 11.3 %line_grads.3 = bf16[64,128,128]{2,1,0:T(8,128)(2,1)} custom-call(s32[4]{0:T(128)} %pad_add_fusion.place_of, s32[64]{0:T(128)} %ids.3, bf16[2,256,1024]{2,1,0:T(8,128)(2,1)} %bitcast.19, bf16[2,256,1024]{2,1,0:T(8,128)(2,1)} %copy-done.7, bf16[256,1024]{1,0:T(8,128)(2,1)} %get-tuple-element.103.refs_2_, bf16[2,256,1024]{2,1,0:T(8,128)(2,1)} %bitcast.21, ...), custom_call_target="tpu_custom_call" | custom-call | flops 1073741824 | bytes 11534336 | tf_op jit(solution)/shard_map/line_grads/pallas_call | solution.py:408
  (57 shorter events, 0.2 us)
Async XLA Ops:
  7.2 93.8 %all-gather.7.cloned.1.call-start = ((), (), s32[]{:S(2)}) async-start(), calls=%async_computation | async-start | bytes 2621440 | tf_op jit(solution)/shard_map/all_gather | solution.py:481
  10.7 1.2 copy-start.3
  12.0 62.6 %copy-start.11 = (bf16[512,1024]{1,0:T(8,128)(2,1)}, bf16[512,1024]{1,0:T(8,128)(2,1)S(1)}, u32[]{:S(2)}) copy-start(bf16[512,1024]{1,0:T(8,128)(2,1)S(1)} %pad_maximum_fusion.1) | copy-start | bytes 3145732
  12.0 28.0 %collective-permute-start = (bf16[33,128,128]{2,1,0:T(8,128)(2,1)S(1)}, bf16[33,128,128]{2,1,0:T(8,128)(2,1)S(1)}, u32[]{:S(2)}, u32[]{:S(2)}) collective-permute-start(bf16[33,128,128]{2,1,0:T(8,128)(2,1)S(1)} %pad_maximum_fusion), channel_id=1, source_target_pairs={{0,4},{12,8},{1,5},{13,9},{2,6},{14,10},{3,7},{15,11},{16,20},{28,... | collective-permute-start | bytes 3244040 | tf_op jit(solution)/shard_map/ppermute | solution.py:468
  17.0 23.0 %collective-permute-start.1 = (bf16[33,128,128]{2,1,0:T(8,128)(2,1)S(1)}, bf16[33,128,128]{2,1,0:T(8,128)(2,1)S(1)}, u32[]{:S(2)}, u32[]{:S(2)}) collective-permute-start(bf16[33,128,128]{2,1,0:T(8,128)(2,1)S(1)} %pad_maximum_fusion), channel_id=1, source_target_pairs={{4,8},{8,4},{5,9},{9,5},{6,10},{10,6},{7,11},{11,7},{20,24},{24,20... | collective-permute-start | bytes 3244040 | tf_op jit(solution)/shard_map/ppermute | solution.py:469
  40.1 45.6 %copy-start.5 = (bf16[33,128,128]{2,1,0:T(8,128)(2,1)}, bf16[33,128,128]{2,1,0:T(8,128)(2,1)S(1)}, u32[]{:S(2)}) copy-start(bf16[33,128,128]{2,1,0:T(8,128)(2,1)S(1)} %collective-permute-done.near_a) | copy-start | bytes 3244036
  40.1 32.5 %copy-start.6 = (bf16[33,128,128]{2,1,0:T(8,128)(2,1)}, bf16[33,128,128]{2,1,0:T(8,128)(2,1)S(1)}, u32[]{:S(2)}) copy-start(bf16[33,128,128]{2,1,0:T(8,128)(2,1)S(1)} %collective-permute-done.1.far_a) | copy-start | bytes 3244036
  40.1 32.5 %collective-permute-start.3 = (bf16[33,128,128]{2,1,0:T(8,128)(2,1)S(1)}, bf16[33,128,128]{2,1,0:T(8,128)(2,1)}, u32[]{:S(2)}, u32[]{:S(2)}) collective-permute-start(bf16[33,128,128]{2,1,0:T(8,128)(2,1)S(1)} %collective-permute-done.near_a), channel_id=1, source_target_pairs={{4,8},{8,4},{5,9},{9,5},{6,10},{10,6},{7,11},{11,7},{20,24},{24,20... | collective-permute-start | bytes 3244040 | tf_op jit(solution)/shard_map/ppermute | solution.py:472
  41.7 30.8 %collective-permute-start.4 = (bf16[33,128,128]{2,1,0:T(8,128)(2,1)S(1)}, bf16[33,128,128]{2,1,0:T(8,128)(2,1)}, u32[]{:S(2)}, u32[]{:S(2)}) collective-permute-start(bf16[33,128,128]{2,1,0:T(8,128)(2,1)S(1)} %collective-permute-done.1.far_a), channel_id=1, source_target_pairs={{4,20},{20,4},{8,24},{24,8},{5,21},{21,5},{9,25},{25,9},{6,22},{22... | collective-permute-start | bytes 3244040 | tf_op jit(solution)/shard_map/ppermute | solution.py:473
  43.4 29.2 %collective-permute-start.2 = (bf16[512,1024]{1,0:T(8,128)(2,1)S(1)}, bf16[512,1024]{1,0:T(8,128)(2,1)S(1)}, u32[]{:S(2)}, u32[]{:S(2)}) collective-permute-start(bf16[512,1024]{1,0:T(8,128)(2,1)S(1)} %pad_maximum_fusion.1), channel_id=1, source_target_pairs={{0,4},{12,8},{4,0},{8,12},{1,5},{13,9},{5,1},{9,13},{2,6},{14,10},... | collective-permute-start | bytes 3145736 | tf_op jit(solution)/shard_map/ppermute | solution.py:474
  72.6 1.0 copy-start.10
  74.6 124.6 %all-gather.9.cloned.1.call-start = ((), (), s32[]{:S(2)}) async-start(), calls=%async_computation.1 | async-start | bytes 1572864 | tf_op jit(solution)/shard_map/all_gather | solution.py:511
  74.7 26.3 %collective-permute-start.6 = (bf16[33,128,128]{2,1,0:T(8,128)(2,1)}, bf16[33,128,128]{2,1,0:T(8,128)(2,1)S(1)}, u32[]{:S(2)}, u32[]{:S(2)}) collective-permute-start(bf16[33,128,128]{2,1,0:T(8,128)(2,1)} %collective-permute-done.3.end_a), channel_id=1, source_target_pairs={{4,20},{20,4},{8,24},{24,8},{5,21},{21,5},{9,25},{25,9},{6,22},{22... | collective-permute-start | bytes 3244040 | tf_op jit(solution)/shard_map/ppermute | solution.py:479
  75.4 25.5 %collective-permute-start.5 = (bf16[32,128,128]{2,1,0:T(8,128)(2,1)}, bf16[32,128,128]{2,1,0:T(8,128)(2,1)S(1)}, u32[]{:S(2)}, u32[]{:S(2)}) collective-permute-start(bf16[32,128,128]{2,1,0:T(8,128)(2,1)} %get-tuple-element.60), channel_id=1, source_target_pairs={{0,4},{12,8},{1,5},{13,9},{2,6},{14,10},{3,7},{15,11},{16,20},{28,... | collective-permute-start | bytes 3145736 | tf_op jit(solution)/shard_map/ppermute | solution.py:478
  80.8 20.1 %collective-permute-start.7 = (bf16[512,1024]{1,0:T(8,128)(2,1)}, bf16[512,1024]{1,0:T(8,128)(2,1)}, u32[]{:S(2)}, u32[]{:S(2)}) collective-permute-start(bf16[512,1024]{1,0:T(8,128)(2,1)} %copy-done.11), channel_id=1, source_target_pairs={{4,8},{8,4},{5,9},{9,5},{6,10},{10,6},{7,11},{11,7},{20,24},{24,20... | collective-permute-start | bytes 3145736 | tf_op jit(solution)/shard_map/ppermute | solution.py:480
  100.9 2.1 copy-start.1
  100.9 2.1 copy-start
  101.0 11.3 %collective-permute-start.10 = (bf16[512,1024]{1,0:T(8,128)(2,1)}, bf16[512,1024]{1,0:T(8,128)(2,1)S(1)}, u32[]{:S(2)}, u32[]{:S(2)}) collective-permute-start(bf16[512,1024]{1,0:T(8,128)(2,1)} %copy-done.10), channel_id=1, source_target_pairs={{4,8},{8,4},{5,9},{9,5},{6,10},{10,6},{7,11},{11,7},{20,24},{24,20... | collective-permute-start | bytes 3145736 | tf_op jit(solution)/shard_map/ppermute | solution.py:490
  101.7 29.2 %collective-permute-start.11 = (bf16[512,1024]{1,0:T(8,128)(2,1)}, bf16[512,1024]{1,0:T(8,128)(2,1)}, u32[]{:S(2)}, u32[]{:S(2)}) collective-permute-start(bf16[512,1024]{1,0:T(8,128)(2,1)} %collective-permute-done.7), channel_id=1, source_target_pairs={{4,0},{8,12},{5,1},{9,13},{6,2},{10,14},{7,3},{11,15},{20,16},{24,... | collective-permute-start | bytes 3145736 | tf_op jit(solution)/shard_map/ppermute | solution.py:491
  106.9 1.4 collective-permute-start.8
  107.6 0.7 collective-permute-start.9
  108.3 0.8 copy-start.17
  108.3 0.9 copy-start.19
  130.9 6.6 %collective-permute-start.13 = (bf16[2,256,1024]{2,1,0:T(8,128)(2,1)}, bf16[2,256,1024]{2,1,0:T(8,128)(2,1)S(1)}, u32[]{:S(2)}, u32[]{:S(2)}) collective-permute-start(bf16[2,256,1024]{2,1,0:T(8,128)(2,1)} %get-tuple-element.80), channel_id=1, source_target_pairs={{4,5},{5,4},{8,9},{9,8},{6,7},{7,6},{10,11},{11,10},{20,21},{21,20... | collective-permute-start | bytes 3145736 | tf_op jit(solution)/shard_map/ppermute | solution.py:502
  131.6 9.9 %collective-permute-start.12 = (bf16[256,1024]{1,0:T(8,128)(2,1)}, bf16[256,1024]{1,0:T(8,128)(2,1)}, u32[]{:S(2)}, u32[]{:S(2)}) collective-permute-start(bf16[256,1024]{1,0:T(8,128)(2,1)} %get-tuple-element.78), channel_id=1, source_target_pairs={{4,6},{6,4},{8,10},{10,8},{5,7},{7,5},{9,11},{11,9},{20,22},{22,20... | collective-permute-start | bytes 1572872 | tf_op jit(solution)/shard_map/ppermute | solution.py:501
  136.2 39.9 %collective-permute-start.16 = (bf16[512,1024]{1,0:T(8,128)(2,1)S(1)}, bf16[512,1024]{1,0:T(8,128)(2,1)S(1)}, u32[]{:S(2)}, u32[]{:S(2)}) collective-permute-start(bf16[512,1024]{1,0:T(8,128)(2,1)S(1)} %collective-permute-done.10), channel_id=1, source_target_pairs={{4,0},{8,12},{5,1},{9,13},{6,2},{10,14},{7,3},{11,15},{20,16},{24,... | collective-permute-start | bytes 3145736 | tf_op jit(solution)/shard_map/ppermute | solution.py:503
  137.5 1.0 copy-start.9
  141.5 2.7 %copy-start.13 = (bf16[256,1024]{1,0:T(8,128)(2,1)S(1)}, bf16[256,1024]{1,0:T(8,128)(2,1)}, u32[]{:S(2)}) copy-start(bf16[256,1024]{1,0:T(8,128)(2,1)} %get-tuple-element.77) | copy-start | bytes 1572868
  144.2 67.5 %all-gather.11.cloned.1.call-start = ((), (), s32[]{:S(2)}) async-start(), calls=%async_computation.2 | async-start | bytes 1572864 | tf_op jit(solution)/shard_map/all_gather | solution.py:516
  146.3 39.3 %collective-permute-start.14 = (bf16[256,1024]{1,0:T(8,128)(2,1)}, bf16[256,1024]{1,0:T(8,128)(2,1)S(1)}, u32[]{:S(2)}, u32[]{:S(2)}) collective-permute-start(bf16[256,1024]{1,0:T(8,128)(2,1)} %add.34), channel_id=1, source_target_pairs={{4,0},{8,12},{5,1},{9,13},{6,2},{10,14},{7,3},{11,15},{20,16},{24,... | collective-permute-start | bytes 1572872 | tf_op jit(solution)/shard_map/ppermute | solution.py:509
  147.6 38.0 %collective-permute-start.15 = (bf16[256,1024]{1,0:T(8,128)(2,1)}, bf16[256,1024]{1,0:T(8,128)(2,1)S(1)}, u32[]{:S(2)}, u32[]{:S(2)}) collective-permute-start(bf16[256,1024]{1,0:T(8,128)(2,1)} %get-tuple-element.87), channel_id=1, source_target_pairs={{4,6},{6,4},{8,10},{10,8},{5,7},{7,5},{9,11},{11,9},{20,22},{22,20... | collective-permute-start | bytes 1572872 | tf_op jit(solution)/shard_map/ppermute | solution.py:510
  151.6 35.2 %copy-start.12 = (bf16[256,1024]{1,0:T(8,128)(2,1)S(1)}, bf16[256,1024]{1,0:T(8,128)(2,1)}, u32[]{:S(2)}) copy-start(bf16[256,1024]{1,0:T(8,128)(2,1)} %get-tuple-element.91) | copy-start | bytes 1572868
  185.6 1.1 copy-start.16
  187.9 11.3 %copy-start.2 = (bf16[256,1024]{1,0:T(8,128)(2,1)}, bf16[256,1024]{1,0:T(8,128)(2,1)S(1)}, u32[]{:S(2)}) copy-start(bf16[256,1024]{1,0:T(8,128)(2,1)S(1)} %add_select_fusion.own) | copy-start | bytes 1572868
  187.9 40.3 %copy-start.4 = (bf16[256,1024]{1,0:T(8,128)(2,1)S(1)}, bf16[256,1024]{1,0:T(8,128)(2,1)}, u32[]{:S(2)}) copy-start(bf16[256,1024]{1,0:T(8,128)(2,1)} %project_forward.3) | copy-start | bytes 1572868
  187.9 14.9 %collective-permute-start.18 = (bf16[256,1024]{1,0:T(8,128)(2,1)S(1)}, bf16[256,1024]{1,0:T(8,128)(2,1)S(1)}, u32[]{:S(2)}, u32[]{:S(2)}) collective-permute-start(bf16[256,1024]{1,0:T(8,128)(2,1)S(1)} %add_select_fusion.own), channel_id=1, source_target_pairs={{0,2},{2,0},{1,3},{3,1},{4,6},{6,4},{5,7},{7,5},{8,10},{10,8},{9,1... | collective-permute-start | bytes 1572872 | tf_op jit(solution)/shard_map/ppermute | solution.py:523
  188.5 14.4 %collective-permute-start.19 = (bf16[256,1024]{1,0:T(8,128)(2,1)S(1)}, bf16[256,1024]{1,0:T(8,128)(2,1)S(1)}, u32[]{:S(2)}, u32[]{:S(2)}) collective-permute-start(bf16[256,1024]{1,0:T(8,128)(2,1)S(1)} %add_select_fusion.own), channel_id=1, source_target_pairs={{0,1},{1,0},{2,3},{3,2},{4,5},{5,4},{6,7},{7,6},{8,9},{9,8},{10,11... | collective-permute-start | bytes 1572872 | tf_op jit(solution)/shard_map/ppermute | solution.py:523
  202.8 26.2 %copy-start.14 = (bf16[256,1024]{1,0:T(8,128)(2,1)}, bf16[256,1024]{1,0:T(8,128)(2,1)S(1)}, u32[]{:S(2)}) copy-start(bf16[256,1024]{1,0:T(8,128)(2,1)S(1)} %collective-permute-done.18.by_tensor) | copy-start | bytes 1572868
  202.9 8.8 %copy-start.15 = (bf16[256,1024]{1,0:T(8,128)(2,1)}, bf16[256,1024]{1,0:T(8,128)(2,1)S(1)}, u32[]{:S(2)}) copy-start(bf16[256,1024]{1,0:T(8,128)(2,1)S(1)} %collective-permute-done.19.by_core) | copy-start | bytes 1572868
  211.7 21.1 %collective-permute-start.21 = (bf16[2,256,1024]{2,1,0:T(8,128)(2,1)}, bf16[2,256,1024]{2,1,0:T(8,128)(2,1)S(1)}, u32[]{:S(2)}, u32[]{:S(2)}) collective-permute-start(bf16[2,256,1024]{2,1,0:T(8,128)(2,1)} %bitcast.18), channel_id=1, source_target_pairs={{0,1},{1,0},{2,3},{3,2},{4,5},{5,4},{6,7},{7,6},{8,9},{9,8},{10,11... | collective-permute-start | bytes 3145736 | tf_op jit(solution)/shard_map/ppermute | solution.py:528
  211.7 21.1 %collective-permute-start.22 = (bf16[2,256,1024]{2,1,0:T(8,128)(2,1)}, bf16[2,256,1024]{2,1,0:T(8,128)(2,1)S(1)}, u32[]{:S(2)}, u32[]{:S(2)}) collective-permute-start(bf16[2,256,1024]{2,1,0:T(8,128)(2,1)} %bitcast.20), channel_id=1, source_target_pairs={{0,1},{1,0},{2,3},{3,2},{4,5},{5,4},{6,7},{7,6},{8,9},{9,8},{10,11... | collective-permute-start | bytes 3145736 | tf_op jit(solution)/shard_map/ppermute | solution.py:528
  212.2 16.0 %collective-permute-start.17 = (bf16[256,1024]{1,0:T(8,128)(2,1)}, bf16[256,1024]{1,0:T(8,128)(2,1)S(1)}, u32[]{:S(2)}, u32[]{:S(2)}) collective-permute-start(bf16[256,1024]{1,0:T(8,128)(2,1)} %project_forward.2), channel_id=1, source_target_pairs={{4,0},{8,12},{5,1},{9,13},{6,2},{10,14},{7,3},{11,15},{20,16},{24,... | collective-permute-start | bytes 1572872 | tf_op jit(solution)/shard_map/ppermute | solution.py:519
  213.5 15.5 %collective-permute-start.20 = (bf16[256,1024]{1,0:T(8,128)(2,1)S(1)}, bf16[256,1024]{1,0:T(8,128)(2,1)S(1)}, u32[]{:S(2)}, u32[]{:S(2)}) collective-permute-start(bf16[256,1024]{1,0:T(8,128)(2,1)S(1)} %collective-permute-done.18.by_tensor), channel_id=1, source_target_pairs={{0,1},{1,0},{2,3},{3,2},{4,5},{5,4},{6,7},{7,6},{8,9},{9,8},{10,11... | collective-permute-start | bytes 1572872 | tf_op jit(solution)/shard_map/ppermute | solution.py:525
  229.0 0.8 copy-start.18
  232.8 1.0 copy-start.7
  232.8 1.3 copy-start.8
Sparse Core Ops, SparseCore 0:
  74.7 21.0 all-gather.6
  144.3 33.0 all-gather.8
  186.9 24.7 all-gather.10

commit v12 on v7

--- a/solution.py
+++ b/solution.py
@@ -10,6 +10,7 @@
 
 VMEM_LIMIT = 60 * 1024 * 1024
 INNER = ("tensor", "replica")
+FREE = pl.CostEstimate(flops=0, bytes_accessed=0, transcendentals=0)
 
 
 def whole(space=pltpu.VMEM):
@@ -66,11 +67,7 @@
         out_specs=(whole(), whole()),
         scratch_shapes=[pltpu.VMEM((depth, width), jnp.bfloat16)],
         compiler_params=pltpu.CompilerParams(vmem_limit_bytes=VMEM_LIMIT),
-        cost_estimate=pl.CostEstimate(
-            flops=4 * rows * depth * width,
-            bytes_accessed=blocks.size * 2 + rows * (depth + width) * 4,
-            transcendentals=0,
-        ),
+        cost_estimate=FREE,
         name="project",
     )(ids, blocks, tokens, upstream)
 
@@ -116,11 +113,7 @@
         in_specs=[whole(pltpu.SMEM), whole(), whole()],
         out_specs=whole(),
         compiler_params=pltpu.CompilerParams(vmem_limit_bytes=VMEM_LIMIT),
-        cost_estimate=pl.CostEstimate(
-            flops=2 * slots * slabs * rows * size * size,
-            bytes_accessed=2 * (tokens.size + upstream.size + slots * size * size),
-            transcendentals=0,
-        ),
+        cost_estimate=FREE,
         name="block_grads",
     )(ids, tokens, upstream)
 
@@ -155,38 +148,54 @@
                 turned[pl.ds(c, size), pl.ds(r, size)] = blocks[s].T
 
 
-def place_kernel(
-    place_of, ids_0, ids_1, ids_2, ids_3, own, near_a, far_a, far_b, end_a, weight, turned
-):
+def place_kernel(place_of, ids_0, ids_1, ids_2, ids_3, own, near_a, far_a, far_b, end_a, turned):
     is_middle, half = place_of[0], place_of[1]
     half_slots = far_b.shape[0] - 1
     mine, other = half * half_slots, (1 - half) * half_slots
 
     @pl.when(is_middle == 1)
     def work():
+        turned[...] = jnp.zeros_like(turned)
+        place_blocks(ids_0, 0, own, None, turned, own.shape[0])
+        place_blocks(ids_1, mine, near_a, None, turned, half_slots)
+        place_blocks(ids_2, mine, far_a, None, turned, half_slots)
+        place_blocks(ids_2, other, far_b, None, turned, half_slots)
+        place_blocks(ids_3, mine, end_a, None, turned, half_slots)
+
+
+def place_first(place_of, ids, pieces, depth, width):
+    return pl.pallas_call(
+        place_kernel,
+        out_shape=jax.ShapeDtypeStruct((width, depth), jnp.bfloat16),
+        in_specs=[whole(pltpu.SMEM)] * 5 + [whole()] * 5,
+        out_specs=whole(),
+        compiler_params=pltpu.CompilerParams(vmem_limit_bytes=VMEM_LIMIT),
+        cost_estimate=FREE,
+        name="place_first",
+    )(place_of, *ids, *pieces)
+
+
+def plain_kernel(place_of, ids_0, ids_1, ids_2, own, near_a, far_a, weight):
+    half_slots = near_a.shape[0] - 1
+    mine = place_of[1] * half_slots
+
+    @pl.when(place_of[0] == 1)
+    def work():
         weight[...] = jnp.zeros_like(weight)
-        turned[...] = jnp.zeros_like(turned)
-        place_blocks(ids_0, 0, own, weight, turned, own.shape[0])
-        place_blocks(ids_1, mine, near_a, weight, turned, half_slots)
-        place_blocks(ids_2, mine, far_a, weight, turned, half_slots)
-        place_blocks(ids_2, other, far_b, weight, turned, half_slots)
-        place_blocks(ids_3, mine, end_a, weight, turned, half_slots)
-
-
-def place_first(place_of, ids, pieces, depth, width):
-    return pl.pallas_call(
-        place_kernel,
-        out_shape=(
-            jax.ShapeDtypeStruct((depth, width), jnp.bfloat16),
-            jax.ShapeDtypeStruct((width, depth), jnp.bfloat16),
-        ),
-        in_specs=[whole(pltpu.SMEM)] * 5 + [whole()] * 5,
-        out_specs=(whole(), whole()),
-        compiler_params=pltpu.CompilerParams(vmem_limit_bytes=VMEM_LIMIT),
-        cost_estimate=pl.CostEstimate(
-            flops=0, bytes_accessed=depth * width * 6, transcendentals=0
-        ),
-        name="place_first",
+        place_blocks(ids_0, 0, own, weight, None, own.shape[0])
+        place_blocks(ids_1, mine, near_a, weight, None, half_slots)
+        place_blocks(ids_2, mine, far_a, weight, None, half_slots)
+
+
+def place_plain(place_of, ids, pieces, depth, width):
+    return pl.pallas_call(
+        plain_kernel,
+        out_shape=jax.ShapeDtypeStruct((depth, width), jnp.bfloat16),
+        in_specs=[whole(pltpu.SMEM)] * 4 + [whole()] * 3,
+        out_specs=whole(),
+        compiler_params=pltpu.CompilerParams(vmem_limit_bytes=VMEM_LIMIT),
+        cost_estimate=FREE,
+        name="place_plain",
     )(place_of, *ids, *pieces)
 
 
@@ -243,31 +252,30 @@
             pltpu.SemaphoreType.DMA,
         ],
         compiler_params=pltpu.CompilerParams(vmem_limit_bytes=VMEM_LIMIT),
-        cost_estimate=pl.CostEstimate(
-            flops=4 * rows * depth * width,
-            bytes_accessed=depth * width * 2 + rows * (depth + width) * 4,
-            transcendentals=0,
-        ),
+        cost_estimate=FREE,
         name="project_back",
     )(place_of, ids_1, ids_3, partial, near_b, end_b, end_upstream, upstream)
 
 
 def forward_kernel(
-    place_of, ids_1, ids_3, partial, near_b, end_b, tokens, gathered, proj, end_proj, held, sem
+    place_of, ids_1, ids_2, ids_3, partial, near_b, far_b, end_a, end_b,
+    tokens, end_tokens, proj, end_proj, weight, sem,
 ):
     half_slots = near_b.shape[0]
-    other = (1 - place_of[1]) * half_slots
-    depth, width = held.shape
-    parts, rows, part_width = gathered.shape
+    mine, other = place_of[1] * half_slots, (1 - place_of[1]) * half_slots
+    width = weight.shape[1]
+    parts, rows, part_width = end_tokens.shape
     step = 256
 
     @pl.when(place_of[0] == 1)
     def work():
-        load = pltpu.make_async_copy(partial, held, sem)
+        load = pltpu.make_async_copy(partial, weight, sem)
         load.start()
         load.wait()
-        place_blocks(ids_1, other, near_b, held, None, half_slots)
-        place_blocks(ids_3, other, end_b, held, None, half_slots)
+        place_blocks(ids_1, other, near_b, weight, None, half_slots)
+        place_blocks(ids_2, other, far_b, weight, None, half_slots)
+        place_blocks(ids_3, mine, end_a, weight, None, half_slots)
+        place_blocks(ids_3, other, end_b, weight, None, half_slots)
 
         @pl.loop(0, width // step, unroll=2)
         def forward(n):
@@ -275,34 +283,30 @@
             acc = jnp.zeros((rows, step), jnp.float32)
             for q in range(parts):
                 acc += jnp.dot(
-                    gathered[q],
-                    held[q * part_width : (q + 1) * part_width, pl.ds(c, step)],
+                    end_tokens[q],
+                    weight[q * part_width : (q + 1) * part_width, pl.ds(c, step)],
                     preferred_element_type=jnp.float32,
                 )
             end_proj[:, pl.ds(c, step)] = acc.astype(end_proj.dtype)
             proj[:, pl.ds(c, step)] = jnp.dot(
-                tokens[...], held[:, pl.ds(c, step)], preferred_element_type=jnp.float32
+                tokens[...], weight[:, pl.ds(c, step)], preferred_element_type=jnp.float32
             ).astype(proj.dtype)
 
 
-def project_forward(place_of, ids_1, ids_3, partial, near_b, end_b, tokens, gathered):
-    depth, width = partial.shape
-    rows = tokens.shape[0]
+def project_forward(place_of, ids, partial, pieces, tokens, end_tokens):
+    rows, depth = tokens.shape
+    width = partial.shape[1]
     out = jax.ShapeDtypeStruct((rows, width), jnp.bfloat16)
     return pl.pallas_call(
         forward_kernel,
         out_shape=(out, out),
-        in_specs=[whole(pltpu.SMEM)] * 3 + [whole(pl.ANY)] + [whole()] * 4,
+        in_specs=[whole(pltpu.SMEM)] * 4 + [whole(pl.ANY)] + [whole()] * 6,
         out_specs=(whole(),) * 2,
         scratch_shapes=[pltpu.VMEM((depth, width), jnp.bfloat16), pltpu.SemaphoreType.DMA],
         compiler_params=pltpu.CompilerParams(vmem_limit_bytes=VMEM_LIMIT),
-        cost_estimate=pl.CostEstimate(
-            flops=4 * rows * depth * width,
-            bytes_accessed=depth * width * 2 + rows * (depth + width) * 4,
-            transcendentals=0,
-        ),
+        cost_estimate=FREE,
         name="project_forward",
-    )(place_of, ids_1, ids_3, partial, near_b, end_b, tokens, gathered)
+    )(place_of, *ids, partial, *pieces, tokens, end_tokens)
 
 
 def split_kernel(place_of, keep, *refs):
@@ -329,9 +333,7 @@
         in_specs=[whole(pltpu.SMEM), whole()] + [whole()] * len(got),
         out_specs=(whole(), whole()),
         compiler_params=pltpu.CompilerParams(vmem_limit_bytes=VMEM_LIMIT),
-        cost_estimate=pl.CostEstimate(
-            flops=keep.size, bytes_accessed=keep.size * 6, transcendentals=0
-        ),
+        cost_estimate=FREE,
         name="add_split",
     )(place_of, keep, *got)
 
@@ -354,9 +356,7 @@
         in_specs=[whole(pltpu.SMEM)] + [whole()] * 4,
         out_specs=whole(),
         compiler_params=pltpu.CompilerParams(vmem_limit_bytes=VMEM_LIMIT),
-        cost_estimate=pl.CostEstimate(
-            flops=0, bytes_accessed=rows * width * 16, transcendentals=0
-        ),
+        cost_estimate=FREE,
         name="assemble",
     )(place_of, *quarters)
 
@@ -401,11 +401,7 @@
         in_specs=[whole(pltpu.SMEM)] + [whole()] * len(flat),
         out_specs=whole(),
         compiler_params=pltpu.CompilerParams(vmem_limit_bytes=VMEM_LIMIT),
-        cost_estimate=pl.CostEstimate(
-            flops=2 * len(pairs) * slots * rows * size * size,
-            bytes_accessed=sum(2 * a.size for a in flat) + 4 * slots * size * size,
-            transcendentals=0,
-        ),
+        cost_estimate=FREE,
         name="line_grads",
     )(ids, *flat)
 
@@ -437,45 +433,54 @@
     middle = (at_z == 1) | (at_z == 2)
     place_of = jnp.stack([middle.astype(jnp.int32), half, at_tensor, at_replica])
     along = functools.partial(lax.ppermute, axis_name="dp")
-    across = functools.partial(lax.ppermute, axis_name="groups", perm=SWAP)
-    sideways = functools.partial(lax.ppermute, axis_name="tensor", perm=SWAP)
-    cores = functools.partial(lax.ppermute, axis_name="replica", perm=SWAP)
+    across = functools.partial(
+        lax.ppermute, axis_name=("groups", "dp"), perm=((1, 5), (5, 1), (2, 6), (6, 2))
+    )
+    middle_swap = ((2, 3), (3, 2), (4, 5), (5, 4))
+    sideways = functools.partial(lax.ppermute, axis_name=("dp", "tensor"), perm=middle_swap)
+    cores = functools.partial(lax.ppermute, axis_name=("dp", "replica"), perm=middle_swap)
+    end_sideways = functools.partial(
+        lax.ppermute, axis_name=("dp", "tensor"), perm=((0, 1), (1, 0), (6, 7), (7, 6))
+    )
+    everywhere = functools.partial(lax.ppermute, axis_name="tensor", perm=SWAP)
+    all_cores = functools.partial(lax.ppermute, axis_name="replica", perm=SWAP)
     stage = lax.optimization_barrier
 
     mine = lax.dynamic_slice_in_dim(blocks, half * half_slots, half_slots, 0)
+    mine = jnp.concatenate([mine, ids_block(block_ids, size).astype(jnp.bfloat16)])
+    (mine,) = stage((mine,))
+
+    near_a = along(mine, perm=INWARD)
+    far_a = along(mine, perm=MIDDLE)
     other = lax.dynamic_slice_in_dim(blocks, (1 - half) * half_slots, half_slots, 0)
-    mine = jnp.concatenate([mine, ids_block(block_ids, size).astype(jnp.bfloat16)])
     part = lax.dynamic_slice_in_dim(tokens, lax.axis_index(INNER) * part_width, part_width, 1)
     both = jnp.concatenate([part, upstream])
-    mine, other, both = stage((mine, other, both))
-
-    near_a = along(mine, perm=INWARD)
-    far_a = along(mine, perm=MIDDLE)
     near_a, far_a, both, other = stage((near_a, far_a, both, other))
 
     end_a = along(near_a, perm=MIDDLE)
     far_b = across(far_a)
     both_1 = along(both, perm=PAIRS)
-    both_1, end_a, far_b, both, other = stage((both_1, end_a, far_b, both, other))
-    upstream_1 = both_1[rows:]
+    ids_1, ids_2 = ids_of(near_a, slots), ids_of(far_a, slots)
+    plain = place_plain(place_of, (block_ids, ids_1, ids_2), (blocks, near_a, far_a), depth, width)
+    both_1, end_a, far_b, both, other, plain = stage((both_1, end_a, far_b, both, other, plain))
 
     near_b = along(other, perm=INWARD)
     end_b = across(end_a)
     both_2m = along(both, perm=MIDDLE)
+    upstream_1 = both_1[rows:]
     tokens_1 = lax.all_gather(both_1[:rows], INNER)
-    ids_1, ids_2, ids_3 = (ids_of(piece, slots) for piece in (near_a, far_a, end_a))
-    partial, turned = place_first(
+    ids_3 = ids_of(end_a, slots)
+    turned = place_first(
         place_of, (block_ids, ids_1, ids_2, ids_3), (blocks, near_a, far_a, far_b, end_a), depth, width
     )
-    near_b, end_b, both_2m, both_1, tokens_1, partial, turned = stage(
-        (near_b, end_b, both_2m, both_1, tokens_1, partial, turned)
+    near_b, end_b, both_2m, both_1, upstream_1, tokens_1, turned = stage(
+        (near_b, end_b, both_2m, both_1, upstream_1, tokens_1, turned)
     )
 
     both_3m = along(both_1, perm=MIDDLE)
     both_2o = along(both_2m, perm=OUTWARD)
-    last = (near_b, end_b)
     end_keep, own_keep, own_give, *end_give = project_back(
-        place_of, ids_1, ids_3, turned, *last, upstream_1, upstream
+        place_of, ids_1, ids_3, turned, near_b, end_b, upstream_1, upstream
     )
     end_keep, end_give = add_split(place_of, end_keep, *[cores(a) for a in end_give])
     end_keep, end_give, own_give, both_3m, both_2o = stage(
@@ -483,25 +488,31 @@
     )
 
     end_got = sideways(end_give)
+    both_3o = along(both_3m, perm=OUTWARD)
     own_keep, own_give = add_split(place_of, own_keep, cores(own_give))
-    both_3o = along(both_3m, perm=OUTWARD)
     tokens_2 = lax.all_gather(both_2m[:rows] + both_2o[:rows], INNER)
     upstream_2 = both_2m[rows:] + both_2o[rows:]
-    end_got, own_give, own_keep = stage((end_got, own_give, own_keep))
+    proj, end_proj = project_forward(
+        place_of, (ids_1, ids_2, ids_3), plain, (near_b, far_b, end_a, end_b), tokens, tokens_1
+    )
+    end_got, own_give, own_keep, proj, end_proj = stage(
+        (end_got, own_give, own_keep, proj, end_proj)
+    )
 
     sum_out = along(end_keep + end_got, perm=OUTWARD)
     own_got = sideways(own_give)
-    proj, end_proj = project_forward(place_of, ids_1, ids_3, partial, *last, tokens, tokens_1)
-    sum_out, own_got, both_3o, proj, end_proj = stage((sum_out, own_got, both_3o, proj, end_proj))
-
-    tokens_3 = lax.all_gather(both_3m[:rows] + both_3o[:rows], INNER)
+    part_3, upstream_1 = stage((both_3m[:rows] + both_3o[:rows], upstream_1))
+    tokens_3 = lax.all_gather(part_3, INNER)
     upstream_3 = both_3m[rows:] + both_3o[rows:]
+    pairs = ((tokens, upstream), (tokens_1, upstream_1))
+    grads = line_grads(block_ids, pairs, None, size, jnp.float32)
+    sum_out, own_got, grads = stage((sum_out, own_got, grads))
+
     quarter = jnp.where(middle, own_keep + own_got, sum_out)
     proj_out = along(end_proj, perm=OUTWARD)
-    pairs = ((tokens, upstream), (tokens_1, upstream_1), (tokens_2, upstream_2))
-    grads = line_grads(block_ids, pairs, None, size, jnp.float32)
-    by_tensor, by_core, grads = stage((sideways(quarter), cores(quarter), grads))
-    by_both = cores(by_tensor)
+    grads = line_grads(block_ids, ((tokens_2, upstream_2),), grads, size, jnp.float32)
+    by_tensor, by_core, grads = stage((everywhere(quarter), all_cores(quarter), grads))
+    by_both = all_cores(by_tensor)
     projected = jnp.where(middle, proj, proj_out)
     token_grad = assemble(place_of, (quarter, by_core, by_tensor, by_both))
     grads = line_grads(block_ids, ((tokens_3, upstream_3),), grads, size, jnp.bfloat16)

time: 212 us -> 244 us (1.15)
  waiting for transfers between devices: 101 us -> 116 us
  Pallas kernels: 47.3 us -> 57.7 us
  starting transfers between devices: 29.8 us -> 36.5 us
    ppermute x1, waiting for transfers between devices: 3.61 us -> 28.2 us  [line_body(): both_3o = along(both_3m, perm=OUTWARD)]
    ppermute x1, waiting for transfers between devices: 10.7 us -> 0.01 us  [line_body(): end_got = sideways(end_give)]
    ppermute x1, waiting for transfers between devices: 21.7 us -> 15 us  [line_body(): both_1 = along(both, perm=PAIRS)]
    pallas_call x2 -> x3, Pallas kernels: 21.7 us -> 28.4 us  [line_grads(): pl.pallas_call(functools.partial(line_grads_kernel, len(pairs)), out_shap...]
    ppermute x1, waiting for transfers between devices: 10.7 us -> 16.8 us  [line_body(): sum_out = along(end_keep + end_got, perm=OUTWARD)]
    ppermute x1, waiting for transfers between devices: 0.01 us -> 4.84 us  [line_body(): proj_out = along(end_proj, perm=OUTWARD)]
    ppermute x1, waiting for transfers between devices: 6.87 us -> 10.5 us  [line_body(): near_b = along(other, perm=INWARD)]
    pallas_call x1 -> x2, Pallas kernels: 8.76 us -> 11.7 us  [the longest x1 6.15 us: place_first(): pl.pallas_call(place_kernel, out_shape=jax.ShapeDtypeStruct((width, depth...]
  transfers between devices with their start and end apart: 24 -> 24, of which waited for: 13 -> 8; matrix products, arithmetic and copies ran while one was open for 3% -> 3% of each run, Pallas kernels for 18% -> 20%
where the time goes in v12:
time: 244 us; the launch traced here: 243 us
  waiting for transfers between devices  116 us (48%)
  Pallas kernels  57.7 us (24%)
  starting transfers between devices  36.5 us (15%)
  between operations  14.1 us (6%)
  other arithmetic  10.1 us (4%)
  local copies, waits for them, and re-layouts  8.89 us (4%)
    pallas_call x3, Pallas kernels, line_grads(): pl.pallas_call(functools.partial(line_grads_kernel, len(pairs)), out_shap...  28.4 us
    ppermute x1, waiting for transfers between devices, line_body(): both_3o = along(both_3m, perm=OUTWARD)  28.2 us
    ppermute x1, waiting for transfers between devices, line_body(): near_a = along(mine, perm=INWARD)  20.9 us
    ppermute x1, waiting for transfers between devices, line_body(): both_2o = along(both_2m, perm=OUTWARD)  17.1 us
    ppermute x1, waiting for transfers between devices, line_body(): sum_out = along(end_keep + end_got, perm=OUTWARD)  16.8 us
    ppermute x1, waiting for transfers between devices, line_body(): both_1 = along(both, perm=PAIRS)  15 us
    ppermute x1, waiting for transfers between devices, line_body(): near_b = along(other, perm=INWARD)  10.5 us
    ppermute x1, starting transfers between devices, line_body(): near_a = along(mine, perm=INWARD)  7.75 us
  transfers between devices with their start and end apart: 24, of which 8 were waited for; matrix products, arithmetic and copies ran while one was open for 3% of the time, Pallas kernels for 20%

profile of v12, /device:TPU:0, one launch (start us, length us, event | category | flops | bytes accessed | tf_op | source)
XLA Modules:
  0.0 242.8 jit_solution(8192410799329088534)
XLA Ops:
  7.2 0.0 all-gather.7.cloned.1.call-start
  7.2 0.7 convert_element_type.26
  7.9 0.1 convert_element_type.27
  8.0 2.7 %constant_dynamic-slice_fusion = (bf16[32,128,128]{2,1,0:T(8,128)(2,1)}, bf16[32,128,128]{2,1,0:T(8,128)(2,1)S(1)}) fusion(bf16[64,128,128]{2,1,0:T(8,128)(2,1)} %own.3, s32[]{:T(128)S(6)} %select_n.24, s32[]{:T(128)S(6)} %select_n.22), kind=kLoop, calls=%fused_computation.8 | loop fusion | bytes 4194312 | tf_op jit(solution)/shard_map/dynamic_slice | solution.py:455
  10.7 1.1 pad_maximum_fusion
  11.7 0.7 collective-permute-start.1
  12.5 7.8 %collective-permute-start = (bf16[33,128,128]{2,1,0:T(8,128)(2,1)}, bf16[33,128,128]{2,1,0:T(8,128)(2,1)S(1)}, u32[]{:S(2)}, u32[]{:S(2)}) collective-permute-start(bf16[33,128,128]{2,1,0:T(8,128)(2,1)} %pad_maximum_fusion), channel_id=1, source_target_pairs={{0,4},{12,8},{1,5},{13,9},{2,6},{14,10},{3,7},{15,11},{16,20},{28,... | collective-permute-start | bytes 3244040 | tf_op jit(solution)/shard_map/ppermute | solution.py:453
  20.2 1.1 constant_dynamic-slice_fusion.1
  21.3 1.1 pad_maximum_fusion.1
  22.4 20.9 %collective-permute-done.near_a = bf16[33,128,128]{2,1,0:T(8,128)(2,1)S(1)} collective-permute-done((bf16[33,128,128]{2,1,0:T(8,128)(2,1)}, bf16[33,128,128]{2,1,0:T(8,128)(2,1)S(1)}, u32[]{:S(2)}, u32[]{:S(2)}) %collective-permute-start) | collective-permute-done | bytes 1081376 | tf_op jit(solution)/shard_map/ppermute | solution.py:453
  43.3 1.6 collective-permute-start.3
  44.9 1.7 collective-permute-start.4
  46.6 4.9 %collective-permute-start.2 = (bf16[512,1024]{1,0:T(8,128)(2,1)}, bf16[512,1024]{1,0:T(8,128)(2,1)}, u32[]{:S(2)}, u32[]{:S(2)}) collective-permute-start(bf16[512,1024]{1,0:T(8,128)(2,1)} %pad_maximum_fusion.1), channel_id=1, source_target_pairs={{0,4},{12,8},{4,0},{8,12},{1,5},{13,9},{5,1},{9,13},{2,6},{14,10},... | collective-permute-start | bytes 3145736 | tf_op jit(solution)/shard_map/ppermute | solution.py:462
  51.5 0.6 pad_add_fusion.place_of
  52.1 0.6 bitcast_convert_fusion.1
  52.7 5.5 %place_plain.1.partial = bf16[4096,1024]{1,0:T(8,128)(2,1)} custom-call(s32[4]{0:T(128)} %pad_add_fusion.place_of, s32[64]{0:T(128)} %ids.5, s32[64]{0:T(128)} %get-tuple-element.104.ids_1, s32[64]{0:T(128)} %get-tuple-element.103.ids_2, bf16[64,128,128]{2,1,0:T(8,128)(2,1)} %own.3, bf16[33,128,128]{2,1,0:T(8,128)(2,1)} %copy-done.2, ...), custom_call_target="tpu_custom_call" | custom-call | tf_op jit(solution)/shard_map/place_plain/pallas_call | solution.py:191
  58.2 15.0 %collective-permute-done.2 = bf16[512,1024]{1,0:T(8,128)(2,1)} collective-permute-done((bf16[512,1024]{1,0:T(8,128)(2,1)}, bf16[512,1024]{1,0:T(8,128)(2,1)}, u32[]{:S(2)}, u32[]{:S(2)}) %collective-permute-start.2) | collective-permute-done | bytes 1048608 | tf_op jit(solution)/shard_map/ppermute | solution.py:462
  73.3 2.2 fusion
  75.5 0.0 all-gather.7.cloned.1.call-update
  75.5 0.0 all-gather.9.cloned.1.call-start
  75.6 0.7 collective-permute-start.6
  76.3 5.6 %collective-permute-start.5 = (bf16[32,128,128]{2,1,0:T(8,128)(2,1)S(1)}, bf16[32,128,128]{2,1,0:T(8,128)(2,1)S(1)}, u32[]{:S(2)}, u32[]{:S(2)}) collective-permute-start(bf16[32,128,128]{2,1,0:T(8,128)(2,1)S(1)} %copy-done.6), channel_id=1, source_target_pairs={{0,4},{12,8},{1,5},{13,9},{2,6},{14,10},{3,7},{15,11},{16,20},{28,... | collective-permute-start | bytes 3145736 | tf_op jit(solution)/shard_map/ppermute | solution.py:467
  81.9 1.7 collective-permute-start.7
  83.6 1.2 bitcast_convert_fusion.ids_3
  84.9 6.2 %place_first.1.partial = bf16[1024,4096]{1,0:T(8,128)(2,1)} custom-call(s32[4]{0:T(128)} %pad_add_fusion.place_of, s32[64]{0:T(128)} %ids.5, s32[64]{0:T(128)} %get-tuple-element.104.ids_1, s32[64]{0:T(128)} %get-tuple-element.103.ids_2, s32[64]{0:T(128)} %bitcast_convert_fusion.ids_3, bf16[64,128,128]{2,1,0:T(8,128)(2,1)} %own.3, ...), custom_call_target="tpu_custom_call" | custom-call | tf_op jit(solution)/shard_map/place_first/pallas_call | solution.py:167
  91.0 10.5 %collective-permute-done.5.near_b = bf16[32,128,128]{2,1,0:T(8,128)(2,1)S(1)} collective-permute-done((bf16[32,128,128]{2,1,0:T(8,128)(2,1)S(1)}, bf16[32,128,128]{2,1,0:T(8,128)(2,1)S(1)}, u32[]{:S(2)}, u32[]{:S(2)}) %collective-permute-start.5) | collective-permute-done | bytes 1048608 | tf_op jit(solution)/shard_map/ppermute | solution.py:467
  101.6 0.0 all-gather.7.cloned.1.call-done
  101.6 0.7 collective-permute-start.10
  102.3 1.3 collective-permute-start.11
  103.6 3.9 %project_back.1 = (bf16[2,256,1024]{2,1,0:T(8,128)(2,1)}, bf16[2,256,1024]{2,1,0:T(8,128)(2,1)}, bf16[2,256,1024]{2,1,0:T(8,128)(2,1)}, bf16[256,1024]{1,0:T(8,128)(2,1)}, bf16[256,1024]{1,0:T(8,128)(2,1)}) custom-call(s32[4]{0:T(128)} %pad_add_fusion.place_of, s32[64]{0:T(128)} %get-tuple-element.104.ids_1, s32[64]{0:T(128)} %bitcast_convert_fusion.ids_3, ...), custom_call_target="tpu_custom_call" | custom-call | tf_op jit(solution)/shard_map/project_back/pallas_call | solution.py:244
  107.5 0.7 collective-permute-start.8
  108.2 0.7 collective-permute-start.9
  109.0 0.8 copy-done.12
  109.7 0.2 copy-done.14
  109.9 3.0 %add_split.2 = (bf16[256,1024]{1,0:T(8,128)(2,1)}, bf16[256,1024]{1,0:T(8,128)(2,1)}) custom-call(s32[4]{0:T(128)} %pad_add_fusion.place_of, bf16[2,256,1024]{2,1,0:T(8,128)(2,1)} %get-tuple-element.62.keep, bf16[256,1024]{1,0:T(8,128)(2,1)} %copy-done.12, bf16[256,1024]{1,0:T(8,128)(2,1)} %copy-done.14), custom_call_target="tpu_custom_call" | custom-call | tf_op jit(solution)/shard_map/add_split/pallas_call | solution.py:330
  113.0 17.1 %collective-permute-done.11 = bf16[512,1024]{1,0:T(8,128)(2,1)} collective-permute-done((bf16[512,1024]{1,0:T(8,128)(2,1)}, bf16[512,1024]{1,0:T(8,128)(2,1)}, u32[]{:S(2)}, u32[]{:S(2)}) %collective-permute-start.11) | collective-permute-done | bytes 1048608 | tf_op jit(solution)/shard_map/ppermute | solution.py:481
  130.0 2.6 %slice_add_fusion.2 = (bf16[256,1024]{1,0:T(8,128)(2,1)}, bf16[256,1024]{1,0:T(8,128)(2,1)}) fusion(bf16[512,1024]{1,0:T(8,128)(2,1)} %collective-permute-done.11, bf16[512,1024]{1,0:T(8,128)(2,1)} %collective-permute-done.7), kind=kLoop, calls=%fused_computation.4 | loop fusion | flops 524288 | bytes 3145728 | tf_op jit(solution)/shard_map/add | solution.py:494
  132.6 0.0 all-gather.11.cloned.1.call-start
  132.7 1.4 collective-permute-start.17
  134.1 28.2 %collective-permute-done.17 = bf16[512,1024]{1,0:T(8,128)(2,1)S(1)} collective-permute-done((bf16[512,1024]{1,0:T(8,128)(2,1)S(1)}, bf16[512,1024]{1,0:T(8,128)(2,1)S(1)}, u32[]{:S(2)}, u32[]{:S(2)}) %collective-permute-start.17) | collective-permute-done | bytes 1048608 | tf_op jit(solution)/shard_map/ppermute | solution.py:491
  162.3 1.1 slice_add_fusion
  163.4 0.0 all-gather.11.cloned.1.call-update
  163.4 0.7 collective-permute-start.13
  164.2 0.7 collective-permute-start.12
  164.9 4.6 %project_forward.1 = (bf16[256,1024]{1,0:T(8,128)(2,1)}, bf16[256,1024]{1,0:T(8,128)(2,1)}) custom-call(s32[4]{0:T(128)} %pad_add_fusion.place_of, s32[64]{0:T(128)} %get-tuple-element.104.ids_1, s32[64]{0:T(128)} %get-tuple-element.103.ids_2, s32[64]{0:T(128)} %bitcast_convert_fusion.ids_3, bf16[4096,1024]{1,0:T(8,128)(2,1)} %place_plain.1.partial, ...), custom_call_target="tpu_custom_call" | custom-call | tf_op jit(solution)/shard_map/project_forward/pallas_call | solution.py:300
  169.5 1.0 copy-done.7
  170.5 3.2 %add_split.3 = (bf16[256,1024]{1,0:T(8,128)(2,1)}, bf16[256,1024]{1,0:T(8,128)(2,1)}) custom-call(s32[4]{0:T(128)} %pad_add_fusion.place_of, bf16[2,256,1024]{2,1,0:T(8,128)(2,1)} %get-tuple-element.71.keep, bf16[2,256,1024]{2,1,0:T(8,128)(2,1)} %copy-done.7), custom_call_target="tpu_custom_call" | custom-call | tf_op jit(solution)/shard_map/add_split/pallas_call | solution.py:330
  173.7 0.2 add.34
  173.9 1.4 collective-permute-start.15
  175.3 0.9 collective-permute-start.16
  176.2 10.8 %line_grads.3.refs_2_ = f32[64,128,128]{2,1,0:T(8,128)} custom-call(s32[64]{0:T(128)} %ids.5, bf16[256,4096]{1,0:T(8,128)(2,1)} %refs_0_.1, bf16[256,1024]{1,0:T(8,128)(2,1)} %refs_1_.1, bf16[4,256,1024]{2,1,0:T(8,128)(2,1)} %bitcast.17, bf16[256,1024]{1,0:T(8,128)(2,1)} %get-tuple-element.86.end_upstream.refs_3_), custom_call_target="tpu_custom_call" | custom-call | tf_op jit(solution)/shard_map/line_grads/pallas_call | solution.py:398
  186.9 16.8 %collective-permute-done.15 = bf16[256,1024]{1,0:T(8,128)(2,1)S(1)} collective-permute-done((bf16[256,1024]{1,0:T(8,128)(2,1)S(1)}, bf16[256,1024]{1,0:T(8,128)(2,1)S(1)}, u32[]{:S(2)}, u32[]{:S(2)}) %collective-permute-start.15) | collective-permute-done | bytes 524320 | tf_op jit(solution)/shard_map/ppermute | solution.py:502
  203.8 0.1 add_select_fusion.own
  203.9 0.1 collective-permute-start.19
  203.9 1.8 collective-permute-start.18
  205.7 1.3 collective-permute-start.14
  207.0 0.0 all-gather.9.cloned.1.call-done
  207.0 9.2 %line_grads.4.refs_2_ = f32[64,128,128]{2,1,0:T(8,128)} custom-call(s32[64]{0:T(128)} %ids.5, bf16[4,256,1024]{2,1,0:T(8,128)(2,1)} %bitcast.19, bf16[256,1024]{1,0:T(8,128)(2,1)} %get-tuple-element.97.refs_1_, f32[64,128,128]{2,1,0:T(8,128)} %line_grads.3.refs_2_), custom_call_target="tpu_custom_call" | custom-call | tf_op jit(solution)/shard_map/line_grads/pallas_call | solution.py:398
  216.2 2.1 collective-permute-done.18.by_tensor
  218.3 4.8 %collective-permute-done.14 = bf16[256,1024]{1,0:T(8,128)(2,1)S(1)} collective-permute-done((bf16[256,1024]{1,0:T(8,128)(2,1)S(1)}, bf16[256,1024]{1,0:T(8,128)(2,1)S(1)}, u32[]{:S(2)}, u32[]{:S(2)}) %collective-permute-start.14) | collective-permute-done | bytes 524320 | tf_op jit(solution)/shard_map/ppermute | solution.py:512
  223.1 0.8 broadcast_select_fusion
  224.0 0.8 copy-done.13
  224.8 3.0 %assemble.1 = bf16[256,4096]{1,0:T(8,128)(2,1)} custom-call(s32[4]{0:T(128)} %pad_add_fusion.place_of, bf16[256,1024]{1,0:T(8,128)(2,1)} %copy-done.5, bf16[256,1024]{1,0:T(8,128)(2,1)} %copy-done.9, bf16[256,1024]{1,0:T(8,128)(2,1)} %copy-done.10, bf16[256,1024]{1,0:T(8,128)(2,1)} %copy-done.13), custom_call_target="tpu_custom_call" | custom-call | tf_op jit(solution)/shard_map/assemble/pallas_call | solution.py:353
  227.8 8.4 %line_grads.5 = bf16[64,128,128]{2,1,0:T(8,128)(2,1)} custom-call(s32[64]{0:T(128)} %ids.5, bf16[4,256,1024]{2,1,0:T(8,128)(2,1)} %bitcast.18, bf16[256,1024]{1,0:T(8,128)(2,1)} %get-tuple-element.95.refs_1_, f32[64,128,128]{2,1,0:T(8,128)} %line_grads.4.refs_2_), custom_call_target="tpu_custom_call" | custom-call | tf_op jit(solution)/shard_map/line_grads/pallas_call | solution.py:398
  (50 shorter events, 0.1 us)
Async XLA Ops:
  7.2 94.4 %all-gather.7.cloned.1.call-start = ((), (), s32[]{:S(2)}) async-start(), calls=%async_computation | async-start | bytes 2621440 | tf_op jit(solution)/shard_map/all_gather | solution.py:471
  10.7 10.7 %copy-start = (bf16[256,1024]{1,0:T(8,128)(2,1)S(1)}, bf16[256,1024]{1,0:T(8,128)(2,1)}, u32[]{:S(2)}) copy-start(bf16[256,1024]{1,0:T(8,128)(2,1)} %refs_1_.1) | copy-start | bytes 1572868
  11.7 10.7 %collective-permute-start.1 = (bf16[33,128,128]{2,1,0:T(8,128)(2,1)}, bf16[33,128,128]{2,1,0:T(8,128)(2,1)S(1)}, u32[]{:S(2)}, u32[]{:S(2)}) collective-permute-start(bf16[33,128,128]{2,1,0:T(8,128)(2,1)} %pad_maximum_fusion), channel_id=1, source_target_pairs={{4,8},{8,4},{5,9},{9,5},{6,10},{10,6},{7,11},{11,7},{20,24},{24,20... | collective-permute-start | bytes 3244040 | tf_op jit(solution)/shard_map/ppermute | solution.py:454
  12.5 30.8 %collective-permute-start = (bf16[33,128,128]{2,1,0:T(8,128)(2,1)}, bf16[33,128,128]{2,1,0:T(8,128)(2,1)S(1)}, u32[]{:S(2)}, u32[]{:S(2)}) collective-permute-start(bf16[33,128,128]{2,1,0:T(8,128)(2,1)} %pad_maximum_fusion), channel_id=1, source_target_pairs={{0,4},{12,8},{1,5},{13,9},{2,6},{14,10},{3,7},{15,11},{16,20},{28,... | collective-permute-start | bytes 3244040 | tf_op jit(solution)/shard_map/ppermute | solution.py:453
  22.4 30.3 %copy-start.1 = (bf16[33,128,128]{2,1,0:T(8,128)(2,1)}, bf16[33,128,128]{2,1,0:T(8,128)(2,1)S(1)}, u32[]{:S(2)}) copy-start(bf16[33,128,128]{2,1,0:T(8,128)(2,1)S(1)} %collective-permute-done.1.far_a) | copy-start | bytes 3244036
  43.3 9.4 %copy-start.2 = (bf16[33,128,128]{2,1,0:T(8,128)(2,1)}, bf16[33,128,128]{2,1,0:T(8,128)(2,1)S(1)}, u32[]{:S(2)}) copy-start(bf16[33,128,128]{2,1,0:T(8,128)(2,1)S(1)} %collective-permute-done.near_a) | copy-start | bytes 3244036
  43.3 30.0 %collective-permute-start.3 = (bf16[33,128,128]{2,1,0:T(8,128)(2,1)S(1)}, bf16[33,128,128]{2,1,0:T(8,128)(2,1)}, u32[]{:S(2)}, u32[]{:S(2)}) collective-permute-start(bf16[33,128,128]{2,1,0:T(8,128)(2,1)S(1)} %collective-permute-done.near_a), channel_id=1, source_target_pairs={{4,8},{8,4},{5,9},{9,5},{6,10},{10,6},{7,11},{11,7},{20,24},{24,20... | collective-permute-start | bytes 3244040 | tf_op jit(solution)/shard_map/ppermute | solution.py:460
  44.9 28.3 %collective-permute-start.4 = (bf16[33,128,128]{2,1,0:T(8,128)(2,1)S(1)}, bf16[33,128,128]{2,1,0:T(8,128)(2,1)}, u32[]{:S(2)}, u32[]{:S(2)}) collective-permute-start(bf16[33,128,128]{2,1,0:T(8,128)(2,1)S(1)} %collective-permute-done.1.far_a), channel_id=1, source_target_pairs={{4,20},{20,4},{8,24},{24,8},{5,21},{21,5},{9,25},{25,9},{6,22},{22... | collective-permute-start | bytes 3244040 | tf_op jit(solution)/shard_map/ppermute | solution.py:461
  46.6 26.7 %collective-permute-start.2 = (bf16[512,1024]{1,0:T(8,128)(2,1)}, bf16[512,1024]{1,0:T(8,128)(2,1)}, u32[]{:S(2)}, u32[]{:S(2)}) collective-permute-start(bf16[512,1024]{1,0:T(8,128)(2,1)} %pad_maximum_fusion.1), channel_id=1, source_target_pairs={{0,4},{12,8},{4,0},{8,12},{1,5},{13,9},{5,1},{9,13},{2,6},{14,10},... | collective-permute-start | bytes 3145736 | tf_op jit(solution)/shard_map/ppermute | solution.py:462
  58.2 18.1 %copy-start.6 = (bf16[32,128,128]{2,1,0:T(8,128)(2,1)S(1)}, bf16[32,128,128]{2,1,0:T(8,128)(2,1)}, u32[]{:S(2)}) copy-start(bf16[32,128,128]{2,1,0:T(8,128)(2,1)} %get-tuple-element.54) | copy-start | bytes 3145732
  75.5 131.5 %all-gather.9.cloned.1.call-start = ((), (), s32[]{:S(2)}) async-start(), calls=%async_computation.1 | async-start | bytes 2621440 | tf_op jit(solution)/shard_map/all_gather | solution.py:493
  75.6 26.0 %collective-permute-start.6 = (bf16[33,128,128]{2,1,0:T(8,128)(2,1)}, bf16[33,128,128]{2,1,0:T(8,128)(2,1)S(1)}, u32[]{:S(2)}, u32[]{:S(2)}) collective-permute-start(bf16[33,128,128]{2,1,0:T(8,128)(2,1)} %collective-permute-done.3.end_a), channel_id=1, source_target_pairs={{4,20},{20,4},{8,24},{24,8},{5,21},{21,5},{9,25},{25,9},{6,22},{22... | collective-permute-start | bytes 3244040 | tf_op jit(solution)/shard_map/ppermute | solution.py:468
  76.3 25.2 %collective-permute-start.5 = (bf16[32,128,128]{2,1,0:T(8,128)(2,1)S(1)}, bf16[32,128,128]{2,1,0:T(8,128)(2,1)S(1)}, u32[]{:S(2)}, u32[]{:S(2)}) collective-permute-start(bf16[32,128,128]{2,1,0:T(8,128)(2,1)S(1)} %copy-done.6), channel_id=1, source_target_pairs={{0,4},{12,8},{1,5},{13,9},{2,6},{14,10},{3,7},{15,11},{16,20},{28,... | collective-permute-start | bytes 3145736 | tf_op jit(solution)/shard_map/ppermute | solution.py:467
  81.9 19.7 %collective-permute-start.7 = (bf16[512,1024]{1,0:T(8,128)(2,1)}, bf16[512,1024]{1,0:T(8,128)(2,1)}, u32[]{:S(2)}, u32[]{:S(2)}) collective-permute-start(bf16[512,1024]{1,0:T(8,128)(2,1)} %pad_maximum_fusion.1), channel_id=1, source_target_pairs={{4,8},{8,4},{5,9},{9,5},{6,10},{10,6},{7,11},{11,7},{20,24},{24,20... | collective-permute-start | bytes 3145736 | tf_op jit(solution)/shard_map/ppermute | solution.py:469
  101.5 2.1 copy-start.4
  101.6 2.1 copy-start.3
  101.6 11.4 %collective-permute-start.10 = (bf16[512,1024]{1,0:T(8,128)(2,1)}, bf16[512,1024]{1,0:T(8,128)(2,1)S(1)}, u32[]{:S(2)}, u32[]{:S(2)}) collective-permute-start(bf16[512,1024]{1,0:T(8,128)(2,1)} %collective-permute-done.2), channel_id=1, source_target_pairs={{4,8},{8,4},{5,9},{9,5},{6,10},{10,6},{7,11},{11,7},{20,24},{24,20... | collective-permute-start | bytes 3145736 | tf_op jit(solution)/shard_map/ppermute | solution.py:480
  102.3 27.7 %collective-permute-start.11 = (bf16[512,1024]{1,0:T(8,128)(2,1)}, bf16[512,1024]{1,0:T(8,128)(2,1)}, u32[]{:S(2)}, u32[]{:S(2)}) collective-permute-start(bf16[512,1024]{1,0:T(8,128)(2,1)} %collective-permute-done.7), channel_id=1, source_target_pairs={{4,0},{8,12},{5,1},{9,13},{6,2},{10,14},{7,3},{11,15},{20,16},{24,... | collective-permute-start | bytes 3145736 | tf_op jit(solution)/shard_map/ppermute | solution.py:481
  107.5 1.4 collective-permute-start.8
  108.2 0.7 collective-permute-start.9
  108.9 0.8 copy-start.12
  109.0 1.0 copy-start.14
  132.6 31.6 %copy-start.17 = (bf16[256,1024]{1,0:T(8,128)(2,1)S(1)}, bf16[256,1024]{1,0:T(8,128)(2,1)}, u32[]{:S(2)}) copy-start(bf16[256,1024]{1,0:T(8,128)(2,1)} %get-tuple-element.70) | copy-start | bytes 1572868
  132.6 95.2 %all-gather.11.cloned.1.call-start = ((), (), s32[]{:S(2)}) async-start(), calls=%async_computation.2 | async-start | bytes 2621440 | tf_op jit(solution)/shard_map/all_gather | solution.py:505
  132.7 29.6 %collective-permute-start.17 = (bf16[512,1024]{1,0:T(8,128)(2,1)S(1)}, bf16[512,1024]{1,0:T(8,128)(2,1)S(1)}, u32[]{:S(2)}, u32[]{:S(2)}) collective-permute-start(bf16[512,1024]{1,0:T(8,128)(2,1)S(1)} %collective-permute-done.10), channel_id=1, source_target_pairs={{4,0},{8,12},{5,1},{9,13},{6,2},{10,14},{7,3},{11,15},{20,16},{24,... | collective-permute-start | bytes 3145736 | tf_op jit(solution)/shard_map/ppermute | solution.py:491
  163.4 6.0 %collective-permute-start.13 = (bf16[2,256,1024]{2,1,0:T(8,128)(2,1)}, bf16[2,256,1024]{2,1,0:T(8,128)(2,1)S(1)}, u32[]{:S(2)}, u32[]{:S(2)}) collective-permute-start(bf16[2,256,1024]{2,1,0:T(8,128)(2,1)} %get-tuple-element.72), channel_id=1, source_target_pairs={{4,5},{5,4},{8,9},{9,8},{6,7},{7,6},{10,11},{11,10},{20,21},{21,20... | collective-permute-start | bytes 3145736 | tf_op jit(solution)/shard_map/ppermute | solution.py:492
  164.2 9.5 %collective-permute-start.12 = (bf16[256,1024]{1,0:T(8,128)(2,1)S(1)}, bf16[256,1024]{1,0:T(8,128)(2,1)S(1)}, u32[]{:S(2)}, u32[]{:S(2)}) collective-permute-start(bf16[256,1024]{1,0:T(8,128)(2,1)S(1)} %copy-done.17), channel_id=1, source_target_pairs={{4,6},{6,4},{8,10},{10,8},{5,7},{7,5},{9,11},{11,9},{20,22},{22,20... | collective-permute-start | bytes 1572872 | tf_op jit(solution)/shard_map/ppermute | solution.py:490
  169.5 4.2 %copy-start.8 = (bf16[256,1024]{1,0:T(8,128)(2,1)S(1)}, bf16[256,1024]{1,0:T(8,128)(2,1)}, u32[]{:S(2)}) copy-start(bf16[256,1024]{1,0:T(8,128)(2,1)} %get-tuple-element.82) | copy-start | bytes 1572868
  169.5 1.0 copy-start.7
  173.8 29.9 %copy-start.11 = (bf16[256,1024]{1,0:T(8,128)(2,1)S(1)}, bf16[256,1024]{1,0:T(8,128)(2,1)}, u32[]{:S(2)}) copy-start(bf16[256,1024]{1,0:T(8,128)(2,1)} %get-tuple-element.81) | copy-start | bytes 1572868
  173.9 29.9 %collective-permute-start.15 = (bf16[256,1024]{1,0:T(8,128)(2,1)S(1)}, bf16[256,1024]{1,0:T(8,128)(2,1)S(1)}, u32[]{:S(2)}, u32[]{:S(2)}) collective-permute-start(bf16[256,1024]{1,0:T(8,128)(2,1)S(1)} %add.34), channel_id=1, source_target_pairs={{4,0},{8,12},{5,1},{9,13},{6,2},{10,14},{7,3},{11,15},{20,16},{24,... | collective-permute-start | bytes 1572872 | tf_op jit(solution)/shard_map/ppermute | solution.py:502
  175.3 28.5 %collective-permute-start.16 = (bf16[256,1024]{1,0:T(8,128)(2,1)}, bf16[256,1024]{1,0:T(8,128)(2,1)S(1)}, u32[]{:S(2)}, u32[]{:S(2)}) collective-permute-start(bf16[256,1024]{1,0:T(8,128)(2,1)} %get-tuple-element.84), channel_id=1, source_target_pairs={{4,6},{6,4},{8,10},{10,8},{5,7},{7,5},{9,11},{11,9},{20,22},{22,20... | collective-permute-start | bytes 1572872 | tf_op jit(solution)/shard_map/ppermute | solution.py:503
  186.9 18.8 %copy-start.16 = (bf16[256,1024]{1,0:T(8,128)(2,1)S(1)}, bf16[256,1024]{1,0:T(8,128)(2,1)}, u32[]{:S(2)}) copy-start(bf16[256,1024]{1,0:T(8,128)(2,1)} %get-tuple-element.80) | copy-start | bytes 1572868
  203.8 12.4 %copy-start.5 = (bf16[256,1024]{1,0:T(8,128)(2,1)}, bf16[256,1024]{1,0:T(8,128)(2,1)S(1)}, u32[]{:S(2)}) copy-start(bf16[256,1024]{1,0:T(8,128)(2,1)S(1)} %add_select_fusion.own) | copy-start | bytes 1572868
  203.9 12.3 %collective-permute-start.19 = (bf16[256,1024]{1,0:T(8,128)(2,1)S(1)}, bf16[256,1024]{1,0:T(8,128)(2,1)S(1)}, u32[]{:S(2)}, u32[]{:S(2)}) collective-permute-start(bf16[256,1024]{1,0:T(8,128)(2,1)S(1)} %add_select_fusion.own), channel_id=1, source_target_pairs={{0,1},{1,0},{2,3},{3,2},{4,5},{5,4},{6,7},{7,6},{8,9},{9,8},{10,11... | collective-permute-start | bytes 1572872 | tf_op jit(solution)/shard_map/ppermute | solution.py:514
  203.9 14.3 %collective-permute-start.18 = (bf16[256,1024]{1,0:T(8,128)(2,1)S(1)}, bf16[256,1024]{1,0:T(8,128)(2,1)S(1)}, u32[]{:S(2)}, u32[]{:S(2)}) collective-permute-start(bf16[256,1024]{1,0:T(8,128)(2,1)S(1)} %add_select_fusion.own), channel_id=1, source_target_pairs={{0,2},{2,0},{1,3},{3,1},{4,6},{6,4},{5,7},{7,5},{8,10},{10,8},{9,1... | collective-permute-start | bytes 1572872 | tf_op jit(solution)/shard_map/ppermute | solution.py:514
  205.7 17.4 %collective-permute-start.14 = (bf16[256,1024]{1,0:T(8,128)(2,1)S(1)}, bf16[256,1024]{1,0:T(8,128)(2,1)S(1)}, u32[]{:S(2)}, u32[]{:S(2)}) collective-permute-start(bf16[256,1024]{1,0:T(8,128)(2,1)S(1)} %copy-done.16), channel_id=1, source_target_pairs={{4,0},{8,12},{5,1},{9,13},{6,2},{10,14},{7,3},{11,15},{20,16},{24,... | collective-permute-start | bytes 1572872 | tf_op jit(solution)/shard_map/ppermute | solution.py:512
  207.0 16.1 %copy-start.15 = (bf16[256,1024]{1,0:T(8,128)(2,1)S(1)}, bf16[256,1024]{1,0:T(8,128)(2,1)}, u32[]{:S(2)}) copy-start(bf16[256,1024]{1,0:T(8,128)(2,1)} %get-tuple-element.79) | copy-start | bytes 1572868
  216.2 7.8 %copy-start.9 = (bf16[256,1024]{1,0:T(8,128)(2,1)}, bf16[256,1024]{1,0:T(8,128)(2,1)S(1)}, u32[]{:S(2)}) copy-start(bf16[256,1024]{1,0:T(8,128)(2,1)S(1)} %collective-permute-done.19.by_core) | copy-start | bytes 1572868
  218.3 5.7 %copy-start.10 = (bf16[256,1024]{1,0:T(8,128)(2,1)}, bf16[256,1024]{1,0:T(8,128)(2,1)S(1)}, u32[]{:S(2)}) copy-start(bf16[256,1024]{1,0:T(8,128)(2,1)S(1)} %collective-permute-done.18.by_tensor) | copy-start | bytes 1572868
  218.3 5.7 %collective-permute-start.20 = (bf16[256,1024]{1,0:T(8,128)(2,1)S(1)}, bf16[256,1024]{1,0:T(8,128)(2,1)S(1)}, u32[]{:S(2)}, u32[]{:S(2)}) collective-permute-start(bf16[256,1024]{1,0:T(8,128)(2,1)S(1)} %collective-permute-done.18.by_tensor), channel_id=1, source_target_pairs={{0,1},{1,0},{2,3},{3,2},{4,5},{5,4},{6,7},{7,6},{8,9},{9,8},{10,11... | collective-permute-start | bytes 1572872 | tf_op jit(solution)/shard_map/ppermute | solution.py:515
  224.0 0.8 copy-start.13
Sparse Core Ops, SparseCore 0:
  75.6 22.1 all-gather.6
  132.7 27.1 all-gather.8
  163.6 23.9 all-gather.10

commit v13 on v12

--- a/solution.py
+++ b/solution.py
@@ -495,14 +495,13 @@
     proj, end_proj = project_forward(
         place_of, (ids_1, ids_2, ids_3), plain, (near_b, far_b, end_a, end_b), tokens, tokens_1
     )
-    end_got, own_give, own_keep, proj, end_proj = stage(
-        (end_got, own_give, own_keep, proj, end_proj)
+    end_got, own_give, own_keep, both_3o, proj, end_proj = stage(
+        (end_got, own_give, own_keep, both_3o, proj, end_proj)
     )
 
     sum_out = along(end_keep + end_got, perm=OUTWARD)
     own_got = sideways(own_give)
-    part_3, upstream_1 = stage((both_3m[:rows] + both_3o[:rows], upstream_1))
-    tokens_3 = lax.all_gather(part_3, INNER)
+    tokens_3 = lax.all_gather(both_3m[:rows] + both_3o[:rows], INNER)
     upstream_3 = both_3m[rows:] + both_3o[rows:]
     pairs = ((tokens, upstream), (tokens_1, upstream_1))
     grads = line_grads(block_ids, pairs, None, size, jnp.float32)

time: 244 us -> 231 us (0.947)
  the two profiles are of different devices: /device:TPU:0 before, /device:TPU:5 now
where the time goes in v13:
time: 231 us; the launch traced here: 228 us
  waiting for transfers between devices  98.4 us (43%)
  Pallas kernels  57.9 us (25%)
  starting transfers between devices  38.5 us (17%)
  between operations  14.1 us (6%)
  other arithmetic  10.1 us (4%)
  local copies, waits for them, and re-layouts  8.87 us (4%)
    pallas_call x3, Pallas kernels, line_grads(): pl.pallas_call(functools.partial(line_grads_kernel, len(pairs)), out_shap...  28.4 us
    ppermute x1, waiting for transfers between devices, line_body(): both_3o = along(both_3m, perm=OUTWARD)  25 us
    ppermute x1, waiting for transfers between devices, line_body(): near_a = along(mine, perm=INWARD)  19.8 us
    ppermute x1, waiting for transfers between devices, line_body(): both_2o = along(both_2m, perm=OUTWARD)  15.1 us
    ppermute x1, waiting for transfers between devices, line_body(): both_1 = along(both, perm=PAIRS)  15 us
    ppermute x1, waiting for transfers between devices, line_body(): near_b = along(other, perm=INWARD)  9.59 us
    ppermute x1, waiting for transfers between devices, line_body(): everywhere(quarter)  7.79 us
    pallas_call x1, Pallas kernels, place_first(): pl.pallas_call(place_kernel, out_shape=jax.ShapeDtypeStruct((width, depth...  6.51 us
  transfers between devices with their start and end apart: 24, of which 8 were waited for; matrix products, arithmetic and copies ran while one was open for 3% of the time, Pallas kernels for 22%

profile of v13, /device:TPU:5, one launch (start us, length us, event | category | flops | bytes accessed | tf_op | source)
XLA Modules:
  0.0 227.8 jit_solution(15357053095764900442)
XLA Ops:
  7.2 0.0 all-gather.7.cloned.1.call-start
  7.2 0.7 convert_element_type.26
  7.9 0.1 convert_element_type.27
  8.0 2.7 %constant_dynamic-slice_fusion = (bf16[32,128,128]{2,1,0:T(8,128)(2,1)}, bf16[32,128,128]{2,1,0:T(8,128)(2,1)S(1)}) fusion(bf16[64,128,128]{2,1,0:T(8,128)(2,1)} %own.3, s32[]{:T(128)S(6)} %select_n.24, s32[]{:T(128)S(6)} %select_n.22), kind=kLoop, calls=%fused_computation.8 | loop fusion | bytes 4194312 | tf_op jit(solution)/shard_map/dynamic_slice | solution.py:455
  10.7 1.1 pad_maximum_fusion
  11.7 3.3 %collective-permute-start = (bf16[33,128,128]{2,1,0:T(8,128)(2,1)}, bf16[33,128,128]{2,1,0:T(8,128)(2,1)S(1)}, u32[]{:S(2)}, u32[]{:S(2)}) collective-permute-start(bf16[33,128,128]{2,1,0:T(8,128)(2,1)} %pad_maximum_fusion), channel_id=1, source_target_pairs={{0,4},{12,8},{1,5},{13,9},{2,6},{14,10},{3,7},{15,11},{16,20},{28,... | collective-permute-start | bytes 3244040 | tf_op jit(solution)/shard_map/ppermute | solution.py:453
  15.0 0.7 collective-permute-start.1
  15.7 1.1 constant_dynamic-slice_fusion.1
  16.8 1.1 pad_maximum_fusion.1
  17.9 19.8 %collective-permute-done.near_a = bf16[33,128,128]{2,1,0:T(8,128)(2,1)S(1)} collective-permute-done((bf16[33,128,128]{2,1,0:T(8,128)(2,1)}, bf16[33,128,128]{2,1,0:T(8,128)(2,1)S(1)}, u32[]{:S(2)}, u32[]{:S(2)}) %collective-permute-start) | collective-permute-done | bytes 1081376 | tf_op jit(solution)/shard_map/ppermute | solution.py:453
  37.8 1.7 collective-permute-start.3
  39.5 1.7 collective-permute-start.4
  41.2 5.4 %collective-permute-start.2 = (bf16[512,1024]{1,0:T(8,128)(2,1)}, bf16[512,1024]{1,0:T(8,128)(2,1)}, u32[]{:S(2)}, u32[]{:S(2)}) collective-permute-start(bf16[512,1024]{1,0:T(8,128)(2,1)} %pad_maximum_fusion.1), channel_id=1, source_target_pairs={{0,4},{12,8},{4,0},{8,12},{1,5},{13,9},{5,1},{9,13},{2,6},{14,10},... | collective-permute-start | bytes 3145736 | tf_op jit(solution)/shard_map/ppermute | solution.py:462
  46.6 0.6 pad_add_fusion.place_of
  47.1 0.6 bitcast_convert_fusion.1
  47.8 5.5 %place_plain.1.partial = bf16[4096,1024]{1,0:T(8,128)(2,1)} custom-call(s32[4]{0:T(128)} %pad_add_fusion.place_of, s32[64]{0:T(128)} %ids.5, s32[64]{0:T(128)} %get-tuple-element.102.ids_1, s32[64]{0:T(128)} %get-tuple-element.101.ids_2, bf16[64,128,128]{2,1,0:T(8,128)(2,1)} %own.3, bf16[33,128,128]{2,1,0:T(8,128)(2,1)} %copy-done.1, ...), custom_call_target="tpu_custom_call" | custom-call | tf_op jit(solution)/shard_map/place_plain/pallas_call | solution.py:191
  53.3 15.0 %collective-permute-done.2 = bf16[512,1024]{1,0:T(8,128)(2,1)} collective-permute-done((bf16[512,1024]{1,0:T(8,128)(2,1)}, bf16[512,1024]{1,0:T(8,128)(2,1)}, u32[]{:S(2)}, u32[]{:S(2)}) %collective-permute-start.2) | collective-permute-done | bytes 1048608 | tf_op jit(solution)/shard_map/ppermute | solution.py:462
  68.3 2.2 fusion
  70.5 0.0 all-gather.9.cloned.1.call-start
  70.6 0.7 collective-permute-start.6
  71.3 5.6 %collective-permute-start.5 = (bf16[32,128,128]{2,1,0:T(8,128)(2,1)S(1)}, bf16[32,128,128]{2,1,0:T(8,128)(2,1)S(1)}, u32[]{:S(2)}, u32[]{:S(2)}) collective-permute-start(bf16[32,128,128]{2,1,0:T(8,128)(2,1)S(1)} %copy-done.6), channel_id=1, source_target_pairs={{0,4},{12,8},{1,5},{13,9},{2,6},{14,10},{3,7},{15,11},{16,20},{28,... | collective-permute-start | bytes 3145736 | tf_op jit(solution)/shard_map/ppermute | solution.py:467
  76.9 1.7 collective-permute-start.7
  78.6 1.2 bitcast_convert_fusion.ids_3
  79.9 6.5 %place_first.1.partial = bf16[1024,4096]{1,0:T(8,128)(2,1)} custom-call(s32[4]{0:T(128)} %pad_add_fusion.place_of, s32[64]{0:T(128)} %ids.5, s32[64]{0:T(128)} %get-tuple-element.102.ids_1, s32[64]{0:T(128)} %get-tuple-element.101.ids_2, s32[64]{0:T(128)} %bitcast_convert_fusion.ids_3, bf16[64,128,128]{2,1,0:T(8,128)(2,1)} %own.3, ...), custom_call_target="tpu_custom_call" | custom-call | tf_op jit(solution)/shard_map/place_first/pallas_call | solution.py:167
  86.4 9.6 %collective-permute-done.5.near_b = bf16[32,128,128]{2,1,0:T(8,128)(2,1)S(1)} collective-permute-done((bf16[32,128,128]{2,1,0:T(8,128)(2,1)S(1)}, bf16[32,128,128]{2,1,0:T(8,128)(2,1)S(1)}, u32[]{:S(2)}, u32[]{:S(2)}) %collective-permute-start.5) | collective-permute-done | bytes 1048608 | tf_op jit(solution)/shard_map/ppermute | solution.py:467
  96.0 0.0 all-gather.7.cloned.1.call-done
  96.0 0.7 collective-permute-start.10
  96.7 1.3 collective-permute-start.11
  98.0 3.9 %project_back.1 = (bf16[2,256,1024]{2,1,0:T(8,128)(2,1)}, bf16[2,256,1024]{2,1,0:T(8,128)(2,1)}, bf16[2,256,1024]{2,1,0:T(8,128)(2,1)}, bf16[256,1024]{1,0:T(8,128)(2,1)}, bf16[256,1024]{1,0:T(8,128)(2,1)}) custom-call(s32[4]{0:T(128)} %pad_add_fusion.place_of, s32[64]{0:T(128)} %get-tuple-element.102.ids_1, s32[64]{0:T(128)} %bitcast_convert_fusion.ids_3, ...), custom_call_target="tpu_custom_call" | custom-call | tf_op jit(solution)/shard_map/project_back/pallas_call | solution.py:244
  101.9 0.7 collective-permute-start.8
  102.6 0.7 collective-permute-start.9
  103.4 0.8 copy-done.12
  104.1 0.2 copy-done.14
  104.3 3.0 %add_split.2 = (bf16[256,1024]{1,0:T(8,128)(2,1)}, bf16[256,1024]{1,0:T(8,128)(2,1)}) custom-call(s32[4]{0:T(128)} %pad_add_fusion.place_of, bf16[2,256,1024]{2,1,0:T(8,128)(2,1)} %get-tuple-element.61.keep, bf16[256,1024]{1,0:T(8,128)(2,1)} %copy-done.12, bf16[256,1024]{1,0:T(8,128)(2,1)} %copy-done.14), custom_call_target="tpu_custom_call" | custom-call | tf_op jit(solution)/shard_map/add_split/pallas_call | solution.py:330
  107.3 15.1 %collective-permute-done.11 = bf16[512,1024]{1,0:T(8,128)(2,1)} collective-permute-done((bf16[512,1024]{1,0:T(8,128)(2,1)}, bf16[512,1024]{1,0:T(8,128)(2,1)}, u32[]{:S(2)}, u32[]{:S(2)}) %collective-permute-start.11) | collective-permute-done | bytes 1048608 | tf_op jit(solution)/shard_map/ppermute | solution.py:481
  122.4 2.6 %slice_add_fusion.2 = (bf16[256,1024]{1,0:T(8,128)(2,1)}, bf16[256,1024]{1,0:T(8,128)(2,1)}) fusion(bf16[512,1024]{1,0:T(8,128)(2,1)} %collective-permute-done.11, bf16[512,1024]{1,0:T(8,128)(2,1)} %collective-permute-done.7), kind=kLoop, calls=%fused_computation.4 | loop fusion | flops 524288 | bytes 3145728 | tf_op jit(solution)/shard_map/add | solution.py:494
  125.1 0.0 all-gather.11.cloned.1.call-start
  125.1 0.7 collective-permute-start.13
  125.8 1.3 collective-permute-start.14
  127.1 0.7 collective-permute-start.12
  127.9 4.6 %project_forward.1 = (bf16[256,1024]{1,0:T(8,128)(2,1)}, bf16[256,1024]{1,0:T(8,128)(2,1)}) custom-call(s32[4]{0:T(128)} %pad_add_fusion.place_of, s32[64]{0:T(128)} %get-tuple-element.102.ids_1, s32[64]{0:T(128)} %get-tuple-element.101.ids_2, s32[64]{0:T(128)} %bitcast_convert_fusion.ids_3, bf16[4096,1024]{1,0:T(8,128)(2,1)} %place_plain.1.partial, ...), custom_call_target="tpu_custom_call" | custom-call | tf_op jit(solution)/shard_map/project_forward/pallas_call | solution.py:300
  132.5 1.0 copy-done.7
  133.4 3.1 %add_split.3 = (bf16[256,1024]{1,0:T(8,128)(2,1)}, bf16[256,1024]{1,0:T(8,128)(2,1)}) custom-call(s32[4]{0:T(128)} %pad_add_fusion.place_of, bf16[2,256,1024]{2,1,0:T(8,128)(2,1)} %get-tuple-element.70.keep, bf16[2,256,1024]{2,1,0:T(8,128)(2,1)} %copy-done.7), custom_call_target="tpu_custom_call" | custom-call | tf_op jit(solution)/shard_map/add_split/pallas_call | solution.py:330
  136.5 25.0 %collective-permute-done.14 = bf16[512,1024]{1,0:T(8,128)(2,1)S(1)} collective-permute-done((bf16[512,1024]{1,0:T(8,128)(2,1)S(1)}, bf16[512,1024]{1,0:T(8,128)(2,1)S(1)}, u32[]{:S(2)}, u32[]{:S(2)}) %collective-permute-start.14) | collective-permute-done | bytes 1048608 | tf_op jit(solution)/shard_map/ppermute | solution.py:491
  161.5 1.1 slice_add_fusion
  162.6 0.0 all-gather.11.cloned.1.call-update
  162.6 0.2 add.34
  162.8 1.4 collective-permute-start.16
  164.2 0.9 collective-permute-start.17
  165.1 10.8 %line_grads.3.refs_2_ = f32[64,128,128]{2,1,0:T(8,128)} custom-call(s32[64]{0:T(128)} %ids.5, bf16[256,4096]{1,0:T(8,128)(2,1)} %refs_0_.1, bf16[256,1024]{1,0:T(8,128)(2,1)} %refs_1_.1, bf16[4,256,1024]{2,1,0:T(8,128)(2,1)} %bitcast.17, bf16[256,1024]{1,0:T(8,128)(2,1)} %get-tuple-element.60.end_upstream.refs_3_), custom_call_target="tpu_custom_call" | custom-call | tf_op jit(solution)/shard_map/line_grads/pallas_call | solution.py:398
  175.9 0.2 collective-permute-done.16
  176.1 0.1 add_select_fusion.own
  176.2 3.0 %collective-permute-start.18 = (bf16[256,1024]{1,0:T(8,128)(2,1)S(1)}, bf16[256,1024]{1,0:T(8,128)(2,1)S(1)}, u32[]{:S(2)}, u32[]{:S(2)}) collective-permute-start(bf16[256,1024]{1,0:T(8,128)(2,1)S(1)} %add_select_fusion.own), channel_id=1, source_target_pairs={{0,2},{2,0},{1,3},{3,1},{4,6},{6,4},{5,7},{7,5},{8,10},{10,8},{9,1... | collective-permute-start | bytes 1572872 | tf_op jit(solution)/shard_map/ppermute | solution.py:513
  179.3 3.2 %collective-permute-start.19 = (bf16[256,1024]{1,0:T(8,128)(2,1)S(1)}, bf16[256,1024]{1,0:T(8,128)(2,1)S(1)}, u32[]{:S(2)}, u32[]{:S(2)}) collective-permute-start(bf16[256,1024]{1,0:T(8,128)(2,1)S(1)} %add_select_fusion.own), channel_id=1, source_target_pairs={{0,1},{1,0},{2,3},{3,2},{4,5},{5,4},{6,7},{7,6},{8,9},{9,8},{10,11... | collective-permute-start | bytes 1572872 | tf_op jit(solution)/shard_map/ppermute | solution.py:513
  182.5 1.3 collective-permute-start.15
  183.8 0.0 all-gather.9.cloned.1.call-done
  183.8 9.2 %line_grads.4.refs_2_ = f32[64,128,128]{2,1,0:T(8,128)} custom-call(s32[64]{0:T(128)} %ids.5, bf16[4,256,1024]{2,1,0:T(8,128)(2,1)} %bitcast.19, bf16[256,1024]{1,0:T(8,128)(2,1)} %get-tuple-element.95.refs_1_, f32[64,128,128]{2,1,0:T(8,128)} %line_grads.3.refs_2_), custom_call_target="tpu_custom_call" | custom-call | tf_op jit(solution)/shard_map/line_grads/pallas_call | solution.py:398
  193.0 7.8 %collective-permute-done.18.by_tensor = bf16[256,1024]{1,0:T(8,128)(2,1)S(1)} collective-permute-done((bf16[256,1024]{1,0:T(8,128)(2,1)S(1)}, bf16[256,1024]{1,0:T(8,128)(2,1)S(1)}, u32[]{:S(2)}, u32[]{:S(2)}) %collective-permute-start.18) | collective-permute-done | bytes 524320 | tf_op jit(solution)/shard_map/ppermute | solution.py:513
  200.8 1.6 collective-permute-start.20
  202.4 5.8 %collective-permute-done.15 = bf16[256,1024]{1,0:T(8,128)(2,1)S(1)} collective-permute-done((bf16[256,1024]{1,0:T(8,128)(2,1)S(1)}, bf16[256,1024]{1,0:T(8,128)(2,1)S(1)}, u32[]{:S(2)}, u32[]{:S(2)}) %collective-permute-start.15) | collective-permute-done | bytes 524320 | tf_op jit(solution)/shard_map/ppermute | solution.py:511
  208.2 0.8 broadcast_select_fusion
  209.0 0.8 copy-done.13
  209.8 3.0 %assemble.1 = bf16[256,4096]{1,0:T(8,128)(2,1)} custom-call(s32[4]{0:T(128)} %pad_add_fusion.place_of, bf16[256,1024]{1,0:T(8,128)(2,1)} %copy-done.5, bf16[256,1024]{1,0:T(8,128)(2,1)} %copy-done.11, bf16[256,1024]{1,0:T(8,128)(2,1)} %copy-done.10, bf16[256,1024]{1,0:T(8,128)(2,1)} %copy-done.13), custom_call_target="tpu_custom_call" | custom-call | tf_op jit(solution)/shard_map/assemble/pallas_call | solution.py:353
  212.8 8.4 %line_grads.5 = bf16[64,128,128]{2,1,0:T(8,128)(2,1)} custom-call(s32[64]{0:T(128)} %ids.5, bf16[4,256,1024]{2,1,0:T(8,128)(2,1)} %bitcast.18, bf16[256,1024]{1,0:T(8,128)(2,1)} %get-tuple-element.93.refs_1_, f32[64,128,128]{2,1,0:T(8,128)} %line_grads.4.refs_2_), custom_call_target="tpu_custom_call" | custom-call | tf_op jit(solution)/shard_map/line_grads/pallas_call | solution.py:398
  (50 shorter events, 0.2 us)
Async XLA Ops:
  7.2 88.8 %all-gather.7.cloned.1.call-start = ((), (), s32[]{:S(2)}) async-start(), calls=%async_computation | async-start | bytes 2621440 | tf_op jit(solution)/shard_map/all_gather | solution.py:471
  10.7 6.2 %copy-start = (bf16[256,1024]{1,0:T(8,128)(2,1)S(1)}, bf16[256,1024]{1,0:T(8,128)(2,1)}, u32[]{:S(2)}) copy-start(bf16[256,1024]{1,0:T(8,128)(2,1)} %refs_1_.1) | copy-start | bytes 1572868
  11.7 26.0 %collective-permute-start = (bf16[33,128,128]{2,1,0:T(8,128)(2,1)}, bf16[33,128,128]{2,1,0:T(8,128)(2,1)S(1)}, u32[]{:S(2)}, u32[]{:S(2)}) collective-permute-start(bf16[33,128,128]{2,1,0:T(8,128)(2,1)} %pad_maximum_fusion), channel_id=1, source_target_pairs={{0,4},{12,8},{1,5},{13,9},{2,6},{14,10},{3,7},{15,11},{16,20},{28,... | collective-permute-start | bytes 3244040 | tf_op jit(solution)/shard_map/ppermute | solution.py:453
  15.0 22.8 %collective-permute-start.1 = (bf16[33,128,128]{2,1,0:T(8,128)(2,1)}, bf16[33,128,128]{2,1,0:T(8,128)(2,1)S(1)}, u32[]{:S(2)}, u32[]{:S(2)}) collective-permute-start(bf16[33,128,128]{2,1,0:T(8,128)(2,1)} %pad_maximum_fusion), channel_id=1, source_target_pairs={{4,8},{8,4},{5,9},{9,5},{6,10},{10,6},{7,11},{11,7},{20,24},{24,20... | collective-permute-start | bytes 3244040 | tf_op jit(solution)/shard_map/ppermute | solution.py:454
  37.8 10.0 %copy-start.1 = (bf16[33,128,128]{2,1,0:T(8,128)(2,1)}, bf16[33,128,128]{2,1,0:T(8,128)(2,1)S(1)}, u32[]{:S(2)}) copy-start(bf16[33,128,128]{2,1,0:T(8,128)(2,1)S(1)} %collective-permute-done.near_a) | copy-start | bytes 3244036
  37.8 10.0 %copy-start.2 = (bf16[33,128,128]{2,1,0:T(8,128)(2,1)}, bf16[33,128,128]{2,1,0:T(8,128)(2,1)S(1)}, u32[]{:S(2)}) copy-start(bf16[33,128,128]{2,1,0:T(8,128)(2,1)S(1)} %collective-permute-done.1.far_a) | copy-start | bytes 3244036
  37.8 30.5 %collective-permute-start.3 = (bf16[33,128,128]{2,1,0:T(8,128)(2,1)S(1)}, bf16[33,128,128]{2,1,0:T(8,128)(2,1)}, u32[]{:S(2)}, u32[]{:S(2)}) collective-permute-start(bf16[33,128,128]{2,1,0:T(8,128)(2,1)S(1)} %collective-permute-done.near_a), channel_id=1, source_target_pairs={{4,8},{8,4},{5,9},{9,5},{6,10},{10,6},{7,11},{11,7},{20,24},{24,20... | collective-permute-start | bytes 3244040 | tf_op jit(solution)/shard_map/ppermute | solution.py:460
  39.5 28.8 %collective-permute-start.4 = (bf16[33,128,128]{2,1,0:T(8,128)(2,1)S(1)}, bf16[33,128,128]{2,1,0:T(8,128)(2,1)}, u32[]{:S(2)}, u32[]{:S(2)}) collective-permute-start(bf16[33,128,128]{2,1,0:T(8,128)(2,1)S(1)} %collective-permute-done.1.far_a), channel_id=1, source_target_pairs={{4,20},{20,4},{8,24},{24,8},{5,21},{21,5},{9,25},{25,9},{6,22},{22... | collective-permute-start | bytes 3244040 | tf_op jit(solution)/shard_map/ppermute | solution.py:461
  41.2 27.1 %collective-permute-start.2 = (bf16[512,1024]{1,0:T(8,128)(2,1)}, bf16[512,1024]{1,0:T(8,128)(2,1)}, u32[]{:S(2)}, u32[]{:S(2)}) collective-permute-start(bf16[512,1024]{1,0:T(8,128)(2,1)} %pad_maximum_fusion.1), channel_id=1, source_target_pairs={{0,4},{12,8},{4,0},{8,12},{1,5},{13,9},{5,1},{9,13},{2,6},{14,10},... | collective-permute-start | bytes 3145736 | tf_op jit(solution)/shard_map/ppermute | solution.py:462
  53.3 18.0 %copy-start.6 = (bf16[32,128,128]{2,1,0:T(8,128)(2,1)S(1)}, bf16[32,128,128]{2,1,0:T(8,128)(2,1)}, u32[]{:S(2)}) copy-start(bf16[32,128,128]{2,1,0:T(8,128)(2,1)} %get-tuple-element.53) | copy-start | bytes 3145732
  70.5 113.3 %all-gather.9.cloned.1.call-start = ((), (), s32[]{:S(2)}) async-start(), calls=%async_computation.1 | async-start | bytes 2621440 | tf_op jit(solution)/shard_map/all_gather | solution.py:493
  70.6 25.4 %collective-permute-start.6 = (bf16[33,128,128]{2,1,0:T(8,128)(2,1)}, bf16[33,128,128]{2,1,0:T(8,128)(2,1)S(1)}, u32[]{:S(2)}, u32[]{:S(2)}) collective-permute-start(bf16[33,128,128]{2,1,0:T(8,128)(2,1)} %collective-permute-done.3.end_a), channel_id=1, source_target_pairs={{4,20},{20,4},{8,24},{24,8},{5,21},{21,5},{9,25},{25,9},{6,22},{22... | collective-permute-start | bytes 3244040 | tf_op jit(solution)/shard_map/ppermute | solution.py:468
  71.3 24.6 %collective-permute-start.5 = (bf16[32,128,128]{2,1,0:T(8,128)(2,1)S(1)}, bf16[32,128,128]{2,1,0:T(8,128)(2,1)S(1)}, u32[]{:S(2)}, u32[]{:S(2)}) collective-permute-start(bf16[32,128,128]{2,1,0:T(8,128)(2,1)S(1)} %copy-done.6), channel_id=1, source_target_pairs={{0,4},{12,8},{1,5},{13,9},{2,6},{14,10},{3,7},{15,11},{16,20},{28,... | collective-permute-start | bytes 3145736 | tf_op jit(solution)/shard_map/ppermute | solution.py:467
  76.9 19.1 %collective-permute-start.7 = (bf16[512,1024]{1,0:T(8,128)(2,1)}, bf16[512,1024]{1,0:T(8,128)(2,1)}, u32[]{:S(2)}, u32[]{:S(2)}) collective-permute-start(bf16[512,1024]{1,0:T(8,128)(2,1)} %pad_maximum_fusion.1), channel_id=1, source_target_pairs={{4,8},{8,4},{5,9},{9,5},{6,10},{10,6},{7,11},{11,7},{20,24},{24,20... | collective-permute-start | bytes 3145736 | tf_op jit(solution)/shard_map/ppermute | solution.py:469
  95.9 2.1 copy-start.4
  96.0 2.1 copy-start.3
  96.0 11.3 %collective-permute-start.10 = (bf16[512,1024]{1,0:T(8,128)(2,1)}, bf16[512,1024]{1,0:T(8,128)(2,1)S(1)}, u32[]{:S(2)}, u32[]{:S(2)}) collective-permute-start(bf16[512,1024]{1,0:T(8,128)(2,1)} %collective-permute-done.2), channel_id=1, source_target_pairs={{4,8},{8,4},{5,9},{9,5},{6,10},{10,6},{7,11},{11,7},{20,24},{24,20... | collective-permute-start | bytes 3145736 | tf_op jit(solution)/shard_map/ppermute | solution.py:480
  96.7 25.7 %collective-permute-start.11 = (bf16[512,1024]{1,0:T(8,128)(2,1)}, bf16[512,1024]{1,0:T(8,128)(2,1)}, u32[]{:S(2)}, u32[]{:S(2)}) collective-permute-start(bf16[512,1024]{1,0:T(8,128)(2,1)} %collective-permute-done.7), channel_id=1, source_target_pairs={{4,0},{8,12},{5,1},{9,13},{6,2},{10,14},{7,3},{11,15},{20,16},{24,... | collective-permute-start | bytes 3145736 | tf_op jit(solution)/shard_map/ppermute | solution.py:481
  101.9 1.4 collective-permute-start.8
  102.6 0.7 collective-permute-start.9
  103.3 0.8 copy-start.12
  103.4 0.9 copy-start.14
  125.1 87.8 %all-gather.11.cloned.1.call-start = ((), (), s32[]{:S(2)}) async-start(), calls=%async_computation.2 | async-start | bytes 2621440 | tf_op jit(solution)/shard_map/all_gather | solution.py:504
  125.1 7.3 %collective-permute-start.13 = (bf16[2,256,1024]{2,1,0:T(8,128)(2,1)}, bf16[2,256,1024]{2,1,0:T(8,128)(2,1)S(1)}, u32[]{:S(2)}, u32[]{:S(2)}) collective-permute-start(bf16[2,256,1024]{2,1,0:T(8,128)(2,1)} %get-tuple-element.71), channel_id=1, source_target_pairs={{4,5},{5,4},{8,9},{9,8},{6,7},{7,6},{10,11},{11,10},{20,21},{21,20... | collective-permute-start | bytes 3145736 | tf_op jit(solution)/shard_map/ppermute | solution.py:492
  125.8 35.6 %collective-permute-start.14 = (bf16[512,1024]{1,0:T(8,128)(2,1)S(1)}, bf16[512,1024]{1,0:T(8,128)(2,1)S(1)}, u32[]{:S(2)}, u32[]{:S(2)}) collective-permute-start(bf16[512,1024]{1,0:T(8,128)(2,1)S(1)} %collective-permute-done.10), channel_id=1, source_target_pairs={{4,0},{8,12},{5,1},{9,13},{6,2},{10,14},{7,3},{11,15},{20,16},{24,... | collective-permute-start | bytes 3145736 | tf_op jit(solution)/shard_map/ppermute | solution.py:491
  127.1 9.3 %collective-permute-start.12 = (bf16[256,1024]{1,0:T(8,128)(2,1)}, bf16[256,1024]{1,0:T(8,128)(2,1)S(1)}, u32[]{:S(2)}, u32[]{:S(2)}) collective-permute-start(bf16[256,1024]{1,0:T(8,128)(2,1)} %get-tuple-element.69), channel_id=1, source_target_pairs={{4,6},{6,4},{8,10},{10,8},{5,7},{7,5},{9,11},{11,9},{20,22},{22,20... | collective-permute-start | bytes 1572872 | tf_op jit(solution)/shard_map/ppermute | solution.py:490
  132.4 1.0 copy-start.7
  136.5 26.1 %copy-start.8 = (bf16[256,1024]{1,0:T(8,128)(2,1)S(1)}, bf16[256,1024]{1,0:T(8,128)(2,1)}, u32[]{:S(2)}) copy-start(bf16[256,1024]{1,0:T(8,128)(2,1)} %get-tuple-element.82) | copy-start | bytes 1572868
  162.6 1.7 copy-start.17
  162.8 13.3 %copy-start.9 = (bf16[256,1024]{1,0:T(8,128)(2,1)S(1)}, bf16[256,1024]{1,0:T(8,128)(2,1)}, u32[]{:S(2)}) copy-start(bf16[256,1024]{1,0:T(8,128)(2,1)} %get-tuple-element.81) | copy-start | bytes 1572868
  162.8 13.3 %collective-permute-start.16 = (bf16[256,1024]{1,0:T(8,128)(2,1)S(1)}, bf16[256,1024]{1,0:T(8,128)(2,1)S(1)}, u32[]{:S(2)}, u32[]{:S(2)}) collective-permute-start(bf16[256,1024]{1,0:T(8,128)(2,1)S(1)} %add.34), channel_id=1, source_target_pairs={{4,0},{8,12},{5,1},{9,13},{6,2},{10,14},{7,3},{11,15},{20,16},{24,... | collective-permute-start | bytes 1572872 | tf_op jit(solution)/shard_map/ppermute | solution.py:502
  164.2 11.9 %collective-permute-start.17 = (bf16[256,1024]{1,0:T(8,128)(2,1)S(1)}, bf16[256,1024]{1,0:T(8,128)(2,1)S(1)}, u32[]{:S(2)}, u32[]{:S(2)}) collective-permute-start(bf16[256,1024]{1,0:T(8,128)(2,1)S(1)} %copy-done.17), channel_id=1, source_target_pairs={{4,6},{6,4},{8,10},{10,8},{5,7},{7,5},{9,11},{11,9},{20,22},{22,20... | collective-permute-start | bytes 1572872 | tf_op jit(solution)/shard_map/ppermute | solution.py:503
  175.9 6.6 %copy-start.16 = (bf16[256,1024]{1,0:T(8,128)(2,1)S(1)}, bf16[256,1024]{1,0:T(8,128)(2,1)}, u32[]{:S(2)}) copy-start(bf16[256,1024]{1,0:T(8,128)(2,1)} %get-tuple-element.80) | copy-start | bytes 1572868
  176.2 16.8 %copy-start.5 = (bf16[256,1024]{1,0:T(8,128)(2,1)}, bf16[256,1024]{1,0:T(8,128)(2,1)S(1)}, u32[]{:S(2)}) copy-start(bf16[256,1024]{1,0:T(8,128)(2,1)S(1)} %add_select_fusion.own) | copy-start | bytes 1572868
  176.2 24.6 %collective-permute-start.18 = (bf16[256,1024]{1,0:T(8,128)(2,1)S(1)}, bf16[256,1024]{1,0:T(8,128)(2,1)S(1)}, u32[]{:S(2)}, u32[]{:S(2)}) collective-permute-start(bf16[256,1024]{1,0:T(8,128)(2,1)S(1)} %add_select_fusion.own), channel_id=1, source_target_pairs={{0,2},{2,0},{1,3},{3,1},{4,6},{6,4},{5,7},{7,5},{8,10},{10,8},{9,1... | collective-permute-start | bytes 1572872 | tf_op jit(solution)/shard_map/ppermute | solution.py:513
  179.3 21.5 %collective-permute-start.19 = (bf16[256,1024]{1,0:T(8,128)(2,1)S(1)}, bf16[256,1024]{1,0:T(8,128)(2,1)S(1)}, u32[]{:S(2)}, u32[]{:S(2)}) collective-permute-start(bf16[256,1024]{1,0:T(8,128)(2,1)S(1)} %add_select_fusion.own), channel_id=1, source_target_pairs={{0,1},{1,0},{2,3},{3,2},{4,5},{5,4},{6,7},{7,6},{8,9},{9,8},{10,11... | collective-permute-start | bytes 1572872 | tf_op jit(solution)/shard_map/ppermute | solution.py:513
  182.5 25.7 %collective-permute-start.15 = (bf16[256,1024]{1,0:T(8,128)(2,1)S(1)}, bf16[256,1024]{1,0:T(8,128)(2,1)S(1)}, u32[]{:S(2)}, u32[]{:S(2)}) collective-permute-start(bf16[256,1024]{1,0:T(8,128)(2,1)S(1)} %copy-done.16), channel_id=1, source_target_pairs={{4,0},{8,12},{5,1},{9,13},{6,2},{10,14},{7,3},{11,15},{20,16},{24,... | collective-permute-start | bytes 1572872 | tf_op jit(solution)/shard_map/ppermute | solution.py:511
  183.8 24.4 %copy-start.15 = (bf16[256,1024]{1,0:T(8,128)(2,1)S(1)}, bf16[256,1024]{1,0:T(8,128)(2,1)}, u32[]{:S(2)}) copy-start(bf16[256,1024]{1,0:T(8,128)(2,1)} %get-tuple-element.79) | copy-start | bytes 1572868
  200.8 8.2 %copy-start.10 = (bf16[256,1024]{1,0:T(8,128)(2,1)}, bf16[256,1024]{1,0:T(8,128)(2,1)S(1)}, u32[]{:S(2)}) copy-start(bf16[256,1024]{1,0:T(8,128)(2,1)S(1)} %collective-permute-done.18.by_tensor) | copy-start | bytes 1572868
  200.8 8.2 %copy-start.11 = (bf16[256,1024]{1,0:T(8,128)(2,1)}, bf16[256,1024]{1,0:T(8,128)(2,1)S(1)}, u32[]{:S(2)}) copy-start(bf16[256,1024]{1,0:T(8,128)(2,1)S(1)} %collective-permute-done.19.by_core) | copy-start | bytes 1572868
  200.8 8.2 %collective-permute-start.20 = (bf16[256,1024]{1,0:T(8,128)(2,1)S(1)}, bf16[256,1024]{1,0:T(8,128)(2,1)S(1)}, u32[]{:S(2)}, u32[]{:S(2)}) collective-permute-start(bf16[256,1024]{1,0:T(8,128)(2,1)S(1)} %collective-permute-done.18.by_tensor), channel_id=1, source_target_pairs={{0,1},{1,0},{2,3},{3,2},{4,5},{5,4},{6,7},{7,6},{8,9},{9,8},{10,11... | collective-permute-start | bytes 1572872 | tf_op jit(solution)/shard_map/ppermute | solution.py:514
  209.0 0.8 copy-start.13
Sparse Core Ops, SparseCore 0:
  70.6 24.5 all-gather.6
  125.2 33.1 all-gather.8
  162.7 39.1 all-gather.10

commit v14 on v7

--- a/solution.py
+++ b/solution.py
@@ -378,7 +378,7 @@
             b = jnp.minimum(ids[s], total - 1)
             row = b // cols_n
             c = pl.ds(pl.multiple_of((b % cols_n) * size, size), size)
-            acc = jnp.zeros((size, size), jnp.float32) if start is None else start[s]
+            acc = jnp.zeros((size, size), jnp.float32) if start is None else start[s].astype(jnp.float32)
             for x, d in pairs:
                 per_part = x.shape[-1] // size
                 at = pl.ds(pl.multiple_of((row % per_part) * size, size), size)
@@ -391,13 +391,13 @@
             grads[s] = jnp.where(ids[s] < total, acc, 0.0).astype(grads.dtype)
 
 
-def line_grads(ids, pairs, start, size, out_dtype):
+def line_grads(ids, pairs, start, size):
     slots = ids.shape[0]
     rows = pairs[0][1].shape[0]
     flat = [a for pair in pairs for a in pair] + ([] if start is None else [start])
     return pl.pallas_call(
         functools.partial(line_grads_kernel, len(pairs)),
-        out_shape=jax.ShapeDtypeStruct((slots, size, size), out_dtype),
+        out_shape=jax.ShapeDtypeStruct((slots, size, size), jnp.bfloat16),
         in_specs=[whole(pltpu.SMEM)] + [whole()] * len(flat),
         out_specs=whole(),
         compiler_params=pltpu.CompilerParams(vmem_limit_bytes=VMEM_LIMIT),
@@ -487,7 +487,9 @@
     both_3o = along(both_3m, perm=OUTWARD)
     tokens_2 = lax.all_gather(both_2m[:rows] + both_2o[:rows], INNER)
     upstream_2 = both_2m[rows:] + both_2o[rows:]
-    end_got, own_give, own_keep = stage((end_got, own_give, own_keep))
+    pairs = ((tokens, upstream), (tokens_1, upstream_1))
+    grads = line_grads(block_ids, pairs, None, size)
+    end_got, own_give, own_keep, grads = stage((end_got, own_give, own_keep, grads))
 
     sum_out = along(end_keep + end_got, perm=OUTWARD)
     own_got = sideways(own_give)
@@ -498,13 +500,12 @@
     upstream_3 = both_3m[rows:] + both_3o[rows:]
     quarter = jnp.where(middle, own_keep + own_got, sum_out)
     proj_out = along(end_proj, perm=OUTWARD)
-    pairs = ((tokens, upstream), (tokens_1, upstream_1), (tokens_2, upstream_2))
-    grads = line_grads(block_ids, pairs, None, size, jnp.float32)
+    grads = line_grads(block_ids, ((tokens_2, upstream_2),), grads, size)
     by_tensor, by_core, grads = stage((sideways(quarter), cores(quarter), grads))
     by_both = cores(by_tensor)
     projected = jnp.where(middle, proj, proj_out)
     token_grad = assemble(place_of, (quarter, by_core, by_tensor, by_both))
-    grads = line_grads(block_ids, ((tokens_3, upstream_3),), grads, size, jnp.bfloat16)
+    grads = line_grads(block_ids, ((tokens_3, upstream_3),), grads, size)
     return projected, token_grad, grads
 
 

time: 212 us -> 211 us (level)
  waiting for transfers between devices: 101 us -> 92.5 us
  Pallas kernels: 47.3 us -> 51.4 us
  starting transfers between devices: 29.8 us -> 33.2 us
    ppermute x1, waiting for transfers between devices: 10.7 us -> 0.16 us  [line_body(): end_got = sideways(end_give)]
    ppermute x1, waiting for transfers between devices: 2.93 us -> 8.15 us  [line_body(): sideways(quarter)]
    pallas_call x2 -> x3, Pallas kernels: 21.7 us -> 25.8 us  [line_grads(): pl.pallas_call(functools.partial(line_grads_kernel, len(pairs)), out_shap...]
    ppermute x1, starting transfers between devices: 0.19 us -> 2.55 us  [line_body(): own_got = sideways(own_give)]
  transfers between devices with their start and end apart: 24 -> 24, of which waited for: 13 -> 12; matrix products, arithmetic and copies ran while one was open for 3% -> 3% of each run, Pallas kernels for 18% -> 21%
where the time goes in v14:
time: 211 us; the launch traced here: 210 us
  waiting for transfers between devices  92.5 us (44%)
  Pallas kernels  51.4 us (24%)
  starting transfers between devices  33.2 us (16%)
  between operations  14 us (7%)
  other arithmetic  10.2 us (5%)
  local copies, waits for them, and re-layouts  8.57 us (4%)
    pallas_call x3, Pallas kernels, line_grads(): pl.pallas_call(functools.partial(line_grads_kernel, len(pairs)), out_shap...  25.8 us
    ppermute x1, waiting for transfers between devices, line_body(): near_a = along(mine, perm=INWARD)  22.3 us
    ppermute x1, waiting for transfers between devices, line_body(): both_1 = along(both, perm=PAIRS)  21.7 us
    ppermute x1, waiting for transfers between devices, line_body(): both_2o = along(both_2m, perm=OUTWARD)  14.5 us
    ppermute x1, waiting for transfers between devices, line_body(): sum_out = along(end_keep + end_got, perm=OUTWARD)  10.7 us
    pallas_call x1, Pallas kernels, place_first(): pl.pallas_call(place_kernel, out_shape=(jax.ShapeDtypeStruct((depth, widt...  8.77 us
    ppermute x1, waiting for transfers between devices, line_body(): sideways(quarter)  8.15 us
    ppermute x1, waiting for transfers between devices, line_body(): near_b = along(other, perm=INWARD)  6.84 us
  transfers between devices with their start and end apart: 24, of which 12 were waited for; matrix products, arithmetic and copies ran while one was open for 3% of the time, Pallas kernels for 21%

profile of v14, /device:TPU:0, one launch (start us, length us, event | category | flops | bytes accessed | tf_op | source)
XLA Modules:
  0.0 209.9 jit_solution(12134767497441767700)
XLA Ops:
  7.2 0.0 all-gather.7.cloned.1.call-start
  7.2 0.7 convert_element_type.26
  7.9 0.1 convert_element_type.27
  8.0 2.7 %constant_dynamic-slice_fusion.1 = (bf16[32,128,128]{2,1,0:T(8,128)(2,1)}, bf16[32,128,128]{2,1,0:T(8,128)(2,1)S(1)}) fusion(bf16[64,128,128]{2,1,0:T(8,128)(2,1)} %own.1, s32[]{:T(128)S(6)} %select_n.23, s32[]{:T(128)S(6)} %select_n.22), kind=kLoop, calls=%fused_computation.9 | loop fusion | bytes 4194312 | tf_op jit(solution)/shard_map/dynamic_slice | solution.py:446
  10.7 0.1 pad_maximum_fusion
  10.8 1.1 constant_dynamic-slice_fusion
  11.9 0.1 pad_maximum_fusion.1
  12.0 5.0 %collective-permute-start = (bf16[33,128,128]{2,1,0:T(8,128)(2,1)S(1)}, bf16[33,128,128]{2,1,0:T(8,128)(2,1)S(1)}, u32[]{:S(2)}, u32[]{:S(2)}) collective-permute-start(bf16[33,128,128]{2,1,0:T(8,128)(2,1)S(1)} %pad_maximum_fusion), channel_id=1, source_target_pairs={{0,4},{12,8},{1,5},{13,9},{2,6},{14,10},{3,7},{15,11},{16,20},{28,... | collective-permute-start | bytes 3244040 | tf_op jit(solution)/shard_map/ppermute | solution.py:452
  17.0 0.7 collective-permute-start.1
  17.8 22.3 %collective-permute-done.near_a = bf16[33,128,128]{2,1,0:T(8,128)(2,1)S(1)} collective-permute-done((bf16[33,128,128]{2,1,0:T(8,128)(2,1)S(1)}, bf16[33,128,128]{2,1,0:T(8,128)(2,1)S(1)}, u32[]{:S(2)}, u32[]{:S(2)}) %collective-permute-start) | collective-permute-done | bytes 1081376 | tf_op jit(solution)/shard_map/ppermute | solution.py:452
  40.1 0.7 collective-permute-start.3
  40.8 1.6 collective-permute-start.4
  42.4 6.5 %collective-permute-start.2 = (bf16[512,1024]{1,0:T(8,128)(2,1)S(1)}, bf16[512,1024]{1,0:T(8,128)(2,1)S(1)}, u32[]{:S(2)}, u32[]{:S(2)}) collective-permute-start(bf16[512,1024]{1,0:T(8,128)(2,1)S(1)} %pad_maximum_fusion.1), channel_id=1, source_target_pairs={{0,4},{12,8},{4,0},{8,12},{1,5},{13,9},{5,1},{9,13},{2,6},{14,10},... | collective-permute-start | bytes 3145736 | tf_op jit(solution)/shard_map/ppermute | solution.py:458
  48.9 21.7 %collective-permute-done.2 = bf16[512,1024]{1,0:T(8,128)(2,1)S(1)} collective-permute-done((bf16[512,1024]{1,0:T(8,128)(2,1)S(1)}, bf16[512,1024]{1,0:T(8,128)(2,1)S(1)}, u32[]{:S(2)}, u32[]{:S(2)}) %collective-permute-start.2) | collective-permute-done | bytes 1048608 | tf_op jit(solution)/shard_map/ppermute | solution.py:458
  70.6 1.0 copy-done.6
  71.6 1.0 fusion
  72.7 0.0 all-gather.9.cloned.1.call-start
  72.7 0.6 collective-permute-start.6
  73.3 4.6 %collective-permute-start.5 = (bf16[32,128,128]{2,1,0:T(8,128)(2,1)}, bf16[32,128,128]{2,1,0:T(8,128)(2,1)}, u32[]{:S(2)}, u32[]{:S(2)}) collective-permute-start(bf16[32,128,128]{2,1,0:T(8,128)(2,1)} %get-tuple-element.60), channel_id=1, source_target_pairs={{0,4},{12,8},{1,5},{13,9},{2,6},{14,10},{3,7},{15,11},{16,20},{28,... | collective-permute-start | bytes 3145736 | tf_op jit(solution)/shard_map/ppermute | solution.py:462
  77.9 1.7 collective-permute-start.7
  79.7 0.7 pad_add_fusion.place_of
  80.3 0.6 bitcast_convert_fusion
  80.9 0.6 bitcast_convert_fusion.1.ids_3
  81.5 8.8 %place_first.1 = (bf16[4096,1024]{1,0:T(8,128)(2,1)}, bf16[1024,4096]{1,0:T(8,128)(2,1)}) custom-call(s32[4]{0:T(128)} %pad_add_fusion.place_of, s32[64]{0:T(128)} %ids.5, s32[64]{0:T(128)} %get-tuple-element.110.ids_1, s32[64]{0:T(128)} %get-tuple-element.109.ids_2, s32[64]{0:T(128)} %bitcast_convert_fusion.1.ids_3, bf16[64,128,128]{2,1,0:T(8,128)(2,1)} %own.1, ...), custom_call_target="tpu_custom_call" | custom-call | bytes 25165824 | tf_op jit(solution)/shard_map/place_first/pallas_call | solution.py:177
  90.3 6.8 %collective-permute-done.5.near_b = bf16[32,128,128]{2,1,0:T(8,128)(2,1)} collective-permute-done((bf16[32,128,128]{2,1,0:T(8,128)(2,1)}, bf16[32,128,128]{2,1,0:T(8,128)(2,1)}, u32[]{:S(2)}, u32[]{:S(2)}) %collective-permute-start.5) | collective-permute-done | bytes 1048608 | tf_op jit(solution)/shard_map/ppermute | solution.py:462
  97.1 0.7 collective-permute-start.10
  97.9 1.3 collective-permute-start.11
  99.2 3.9 %project_back.1 = (bf16[2,256,1024]{2,1,0:T(8,128)(2,1)}, bf16[2,256,1024]{2,1,0:T(8,128)(2,1)}, bf16[2,256,1024]{2,1,0:T(8,128)(2,1)}, bf16[256,1024]{1,0:T(8,128)(2,1)}, bf16[256,1024]{1,0:T(8,128)(2,1)}) custom-call(s32[4]{0:T(128)} %pad_add_fusion.place_of, s32[64]{0:T(128)} %get-tuple-element.110.ids_1, s32[64]{0:T(128)} %bitcast_convert_fusion.1.ids_3, ...), custom_call_target="tpu_custom_call" | custom-call | flops 4294967296 | bytes 13631488 | tf_op jit(solution)/shard_map/project_back/pallas_call | solution.py:235
  103.1 0.1 collective-permute-start.8
  103.1 0.5 collective-permute-start.9
  103.6 1.6 collective-permute-done.8.refs_0_
  105.2 0.7 collective-permute-done.9.refs_1_
  106.0 0.0 copy-done.13
  106.0 0.8 copy-done.15
  106.8 3.0 %add_split.2 = (bf16[256,1024]{1,0:T(8,128)(2,1)}, bf16[256,1024]{1,0:T(8,128)(2,1)}) custom-call(s32[4]{0:T(128)} %pad_add_fusion.place_of, bf16[2,256,1024]{2,1,0:T(8,128)(2,1)} %get-tuple-element.69.keep, bf16[256,1024]{1,0:T(8,128)(2,1)} %copy-done.13, bf16[256,1024]{1,0:T(8,128)(2,1)} %copy-done.15), custom_call_target="tpu_custom_call" | custom-call | flops 524288 | bytes 3145728 | tf_op jit(solution)/shard_map/add_split/pallas_call | solution.py:326
  109.8 14.5 %collective-permute-done.11 = bf16[512,1024]{1,0:T(8,128)(2,1)S(1)} collective-permute-done((bf16[512,1024]{1,0:T(8,128)(2,1)}, bf16[512,1024]{1,0:T(8,128)(2,1)S(1)}, u32[]{:S(2)}, u32[]{:S(2)}) %collective-permute-start.11) | collective-permute-done | bytes 1048608 | tf_op jit(solution)/shard_map/ppermute | solution.py:475
  124.3 2.3 %slice_add_fusion.2 = (bf16[256,1024]{1,0:T(8,128)(2,1)}, bf16[256,1024]{1,0:T(8,128)(2,1)}) fusion(bf16[512,1024]{1,0:T(8,128)(2,1)S(1)} %collective-permute-done.11, bf16[512,1024]{1,0:T(8,128)(2,1)} %collective-permute-done.7), kind=kLoop, calls=%fused_computation.4 | loop fusion | flops 524288 | bytes 3145728 | tf_op jit(solution)/shard_map/add | solution.py:489
  126.6 0.0 all-gather.11.cloned.1.call-start
  126.7 0.1 collective-permute-start.13
  126.8 1.6 collective-permute-start.12
  128.3 1.3 collective-permute-start.16
  129.6 10.0 %line_grads.3.refs_2_ = bf16[64,128,128]{2,1,0:T(8,128)(2,1)} custom-call(s32[64]{0:T(128)} %ids.5, bf16[256,4096]{1,0:T(8,128)(2,1)} %tokens.1, bf16[256,1024]{1,0:T(8,128)(2,1)} %refs_1_.1, bf16[4,256,1024]{2,1,0:T(8,128)(2,1)} %bitcast.18, bf16[256,1024]{1,0:T(8,128)(2,1)} %get-tuple-element.107.end_upstream.refs_3_), custom_call_target="tpu_custom_call" | custom-call | flops 1073741824 | bytes 9437184 | tf_op jit(solution)/shard_map/line_grads/pallas_call | solution.py:398
  139.7 1.0 copy-done.5
  140.6 3.0 %add_split.3 = (bf16[256,1024]{1,0:T(8,128)(2,1)}, bf16[256,1024]{1,0:T(8,128)(2,1)}) custom-call(s32[4]{0:T(128)} %pad_add_fusion.place_of, bf16[2,256,1024]{2,1,0:T(8,128)(2,1)} %get-tuple-element.79.keep, bf16[2,256,1024]{2,1,0:T(8,128)(2,1)} %copy-done.5), custom_call_target="tpu_custom_call" | custom-call | flops 524288 | bytes 3145728 | tf_op jit(solution)/shard_map/add_split/pallas_call | solution.py:326
  143.7 0.2 collective-permute-done.12
  143.9 2.0 add.34
  145.9 1.3 collective-permute-start.14
  147.2 2.5 %collective-permute-start.15 = (bf16[256,1024]{1,0:T(8,128)(2,1)}, bf16[256,1024]{1,0:T(8,128)(2,1)S(1)}, u32[]{:S(2)}, u32[]{:S(2)}) collective-permute-start(bf16[256,1024]{1,0:T(8,128)(2,1)} %get-tuple-element.85), channel_id=1, source_target_pairs={{0,2},{2,0},{1,3},{3,1},{4,6},{6,4},{5,7},{7,5},{8,10},{10,8},{9,1... | collective-permute-start | bytes 1572872 | tf_op jit(solution)/shard_map/ppermute | solution.py:495
  149.7 3.9 %project_forward.1 = (bf16[256,1024]{1,0:T(8,128)(2,1)}, bf16[256,1024]{1,0:T(8,128)(2,1)}) custom-call(s32[4]{0:T(128)} %pad_add_fusion.place_of, s32[64]{0:T(128)} %get-tuple-element.110.ids_1, s32[64]{0:T(128)} %bitcast_convert_fusion.1.ids_3, bf16[4096,1024]{1,0:T(8,128)(2,1)} %get-tuple-element.87.partial, ...), custom_call_target="tpu_custom_call" | custom-call | flops 4294967296 | bytes 13631488 | tf_op jit(solution)/shard_map/project_forward/pallas_call | solution.py:292
  153.6 2.6 %collective-permute-done.16 = bf16[512,1024]{1,0:T(8,128)(2,1)S(1)} collective-permute-done((bf16[512,1024]{1,0:T(8,128)(2,1)S(1)}, bf16[512,1024]{1,0:T(8,128)(2,1)S(1)}, u32[]{:S(2)}, u32[]{:S(2)}) %collective-permute-start.16) | collective-permute-done | bytes 1048608 | tf_op jit(solution)/shard_map/ppermute | solution.py:487
  156.3 10.7 %collective-permute-done.14 = bf16[256,1024]{1,0:T(8,128)(2,1)S(1)} collective-permute-done((bf16[256,1024]{1,0:T(8,128)(2,1)}, bf16[256,1024]{1,0:T(8,128)(2,1)S(1)}, u32[]{:S(2)}, u32[]{:S(2)}) %collective-permute-start.14) | collective-permute-done | bytes 524320 | tf_op jit(solution)/shard_map/ppermute | solution.py:494
  167.0 1.2 slice_add_fusion
  168.1 1.1 add_select_fusion.own
  169.3 0.9 collective-permute-start.18
  170.2 1.3 collective-permute-start.17
  171.6 7.9 %line_grads.4.refs_2_ = bf16[64,128,128]{2,1,0:T(8,128)(2,1)} custom-call(s32[64]{0:T(128)} %ids.5, bf16[4,256,1024]{2,1,0:T(8,128)(2,1)} %bitcast.16, bf16[256,1024]{1,0:T(8,128)(2,1)} %get-tuple-element.103.refs_1_, bf16[64,128,128]{2,1,0:T(8,128)(2,1)} %line_grads.3.refs_2_), custom_call_target="tpu_custom_call" | custom-call | flops 536870912 | bytes 8912896 | tf_op jit(solution)/shard_map/line_grads/pallas_call | solution.py:398
  179.5 8.2 %collective-permute-done.18.by_tensor = bf16[256,1024]{1,0:T(8,128)(2,1)S(1)} collective-permute-done((bf16[256,1024]{1,0:T(8,128)(2,1)S(1)}, bf16[256,1024]{1,0:T(8,128)(2,1)S(1)}, u32[]{:S(2)}, u32[]{:S(2)}) %collective-permute-start.18) | collective-permute-done | bytes 524320 | tf_op jit(solution)/shard_map/ppermute | solution.py:504
  187.6 0.1 collective-permute-start.20
  187.7 1.0 broadcast_select_fusion
  188.7 0.9 collective-permute-done.20.by_both
  189.6 0.8 copy-done.14
  190.4 3.0 %assemble.1 = bf16[256,4096]{1,0:T(8,128)(2,1)} custom-call(s32[4]{0:T(128)} %pad_add_fusion.place_of, bf16[256,1024]{1,0:T(8,128)(2,1)} %copy-done, bf16[256,1024]{1,0:T(8,128)(2,1)} %copy-done.11, bf16[256,1024]{1,0:T(8,128)(2,1)} %copy-done.10, bf16[256,1024]{1,0:T(8,128)(2,1)} %copy-done.14), custom_call_target="tpu_custom_call" | custom-call | bytes 4194304 | tf_op jit(solution)/shard_map/assemble/pallas_call | solution.py:351
  193.4 2.1 all-gather.11.cloned.1.call-done
  195.5 7.8 %line_grads.5 = bf16[64,128,128]{2,1,0:T(8,128)(2,1)} custom-call(s32[64]{0:T(128)} %ids.5, bf16[4,256,1024]{2,1,0:T(8,128)(2,1)} %bitcast.17, bf16[256,1024]{1,0:T(8,128)(2,1)} %get-tuple-element.101.refs_1_, bf16[64,128,128]{2,1,0:T(8,128)(2,1)} %line_grads.4.refs_2_), custom_call_target="tpu_custom_call" | custom-call | flops 536870912 | bytes 8912896 | tf_op jit(solution)/shard_map/line_grads/pallas_call | solution.py:398
  (47 shorter events, 0.2 us)
Async XLA Ops:
  7.2 90.0 %all-gather.7.cloned.1.call-start = ((), (), s32[]{:S(2)}) async-start(), calls=%async_computation | async-start | bytes 2621440 | tf_op jit(solution)/shard_map/all_gather | solution.py:465
  10.7 1.2 copy-start.1
  12.0 60.6 %copy-start.7 = (bf16[512,1024]{1,0:T(8,128)(2,1)}, bf16[512,1024]{1,0:T(8,128)(2,1)S(1)}, u32[]{:S(2)}) copy-start(bf16[512,1024]{1,0:T(8,128)(2,1)S(1)} %pad_maximum_fusion.1) | copy-start | bytes 3145732
  12.0 28.0 %collective-permute-start = (bf16[33,128,128]{2,1,0:T(8,128)(2,1)S(1)}, bf16[33,128,128]{2,1,0:T(8,128)(2,1)S(1)}, u32[]{:S(2)}, u32[]{:S(2)}) collective-permute-start(bf16[33,128,128]{2,1,0:T(8,128)(2,1)S(1)} %pad_maximum_fusion), channel_id=1, source_target_pairs={{0,4},{12,8},{1,5},{13,9},{2,6},{14,10},{3,7},{15,11},{16,20},{28,... | collective-permute-start | bytes 3244040 | tf_op jit(solution)/shard_map/ppermute | solution.py:452
  17.0 23.0 %collective-permute-start.1 = (bf16[33,128,128]{2,1,0:T(8,128)(2,1)S(1)}, bf16[33,128,128]{2,1,0:T(8,128)(2,1)S(1)}, u32[]{:S(2)}, u32[]{:S(2)}) collective-permute-start(bf16[33,128,128]{2,1,0:T(8,128)(2,1)S(1)} %pad_maximum_fusion), channel_id=1, source_target_pairs={{4,8},{8,4},{5,9},{9,5},{6,10},{10,6},{7,11},{11,7},{20,24},{24,20... | collective-permute-start | bytes 3244040 | tf_op jit(solution)/shard_map/ppermute | solution.py:453
  40.1 41.5 %copy-start.2 = (bf16[33,128,128]{2,1,0:T(8,128)(2,1)}, bf16[33,128,128]{2,1,0:T(8,128)(2,1)S(1)}, u32[]{:S(2)}) copy-start(bf16[33,128,128]{2,1,0:T(8,128)(2,1)S(1)} %collective-permute-done.near_a) | copy-start | bytes 3244036
  40.1 41.5 %copy-start.3 = (bf16[33,128,128]{2,1,0:T(8,128)(2,1)}, bf16[33,128,128]{2,1,0:T(8,128)(2,1)S(1)}, u32[]{:S(2)}) copy-start(bf16[33,128,128]{2,1,0:T(8,128)(2,1)S(1)} %collective-permute-done.1.far_a) | copy-start | bytes 3244036
  40.1 30.6 %collective-permute-start.3 = (bf16[33,128,128]{2,1,0:T(8,128)(2,1)S(1)}, bf16[33,128,128]{2,1,0:T(8,128)(2,1)S(1)}, u32[]{:S(2)}, u32[]{:S(2)}) collective-permute-start(bf16[33,128,128]{2,1,0:T(8,128)(2,1)S(1)} %collective-permute-done.near_a), channel_id=1, source_target_pairs={{4,8},{8,4},{5,9},{9,5},{6,10},{10,6},{7,11},{11,7},{20,24},{24,20... | collective-permute-start | bytes 3244040 | tf_op jit(solution)/shard_map/ppermute | solution.py:456
  40.8 29.9 %collective-permute-start.4 = (bf16[33,128,128]{2,1,0:T(8,128)(2,1)S(1)}, bf16[33,128,128]{2,1,0:T(8,128)(2,1)}, u32[]{:S(2)}, u32[]{:S(2)}) collective-permute-start(bf16[33,128,128]{2,1,0:T(8,128)(2,1)S(1)} %collective-permute-done.1.far_a), channel_id=1, source_target_pairs={{0,16},{16,0},{1,17},{17,1},{2,18},{18,2},{3,19},{19,3},{4,20},{20... | collective-permute-start | bytes 3244040 | tf_op jit(solution)/shard_map/ppermute | solution.py:457
  42.4 28.3 %collective-permute-start.2 = (bf16[512,1024]{1,0:T(8,128)(2,1)S(1)}, bf16[512,1024]{1,0:T(8,128)(2,1)S(1)}, u32[]{:S(2)}, u32[]{:S(2)}) collective-permute-start(bf16[512,1024]{1,0:T(8,128)(2,1)S(1)} %pad_maximum_fusion.1), channel_id=1, source_target_pairs={{0,4},{12,8},{4,0},{8,12},{1,5},{13,9},{5,1},{9,13},{2,6},{14,10},... | collective-permute-start | bytes 3145736 | tf_op jit(solution)/shard_map/ppermute | solution.py:458
  70.6 1.0 copy-start.6
  70.6 10.9 %copy-start.4 = (bf16[33,128,128]{2,1,0:T(8,128)(2,1)}, bf16[33,128,128]{2,1,0:T(8,128)(2,1)S(1)}, u32[]{:S(2)}) copy-start(bf16[33,128,128]{2,1,0:T(8,128)(2,1)S(1)} %collective-permute-done.3.end_a) | copy-start | bytes 3244036
  72.7 98.9 %all-gather.9.cloned.1.call-start = ((), (), s32[]{:S(2)}) async-start(), calls=%async_computation.1 | async-start | bytes 2621440 | tf_op jit(solution)/shard_map/all_gather | solution.py:488
  72.7 24.4 %collective-permute-start.6 = (bf16[33,128,128]{2,1,0:T(8,128)(2,1)S(1)}, bf16[33,128,128]{2,1,0:T(8,128)(2,1)}, u32[]{:S(2)}, u32[]{:S(2)}) collective-permute-start(bf16[33,128,128]{2,1,0:T(8,128)(2,1)S(1)} %collective-permute-done.3.end_a), channel_id=1, source_target_pairs={{0,16},{16,0},{1,17},{17,1},{2,18},{18,2},{3,19},{19,3},{4,20},{20... | collective-permute-start | bytes 3244040 | tf_op jit(solution)/shard_map/ppermute | solution.py:463
  73.3 23.8 %collective-permute-start.5 = (bf16[32,128,128]{2,1,0:T(8,128)(2,1)}, bf16[32,128,128]{2,1,0:T(8,128)(2,1)}, u32[]{:S(2)}, u32[]{:S(2)}) collective-permute-start(bf16[32,128,128]{2,1,0:T(8,128)(2,1)} %get-tuple-element.60), channel_id=1, source_target_pairs={{0,4},{12,8},{1,5},{13,9},{2,6},{14,10},{3,7},{15,11},{16,20},{28,... | collective-permute-start | bytes 3145736 | tf_op jit(solution)/shard_map/ppermute | solution.py:462
  77.9 19.2 %collective-permute-start.7 = (bf16[512,1024]{1,0:T(8,128)(2,1)}, bf16[512,1024]{1,0:T(8,128)(2,1)}, u32[]{:S(2)}, u32[]{:S(2)}) collective-permute-start(bf16[512,1024]{1,0:T(8,128)(2,1)} %copy-done.7), channel_id=1, source_target_pairs={{4,8},{8,4},{5,9},{9,5},{6,10},{10,6},{7,11},{11,7},{20,24},{24,20... | collective-permute-start | bytes 3145736 | tf_op jit(solution)/shard_map/ppermute | solution.py:464
  97.1 12.7 %collective-permute-start.10 = (bf16[512,1024]{1,0:T(8,128)(2,1)}, bf16[512,1024]{1,0:T(8,128)(2,1)S(1)}, u32[]{:S(2)}, u32[]{:S(2)}) collective-permute-start(bf16[512,1024]{1,0:T(8,128)(2,1)} %copy-done.6), channel_id=1, source_target_pairs={{4,8},{8,4},{5,9},{9,5},{6,10},{10,6},{7,11},{11,7},{20,24},{24,20... | collective-permute-start | bytes 3145736 | tf_op jit(solution)/shard_map/ppermute | solution.py:474
  97.9 26.5 %collective-permute-start.11 = (bf16[512,1024]{1,0:T(8,128)(2,1)}, bf16[512,1024]{1,0:T(8,128)(2,1)S(1)}, u32[]{:S(2)}, u32[]{:S(2)}) collective-permute-start(bf16[512,1024]{1,0:T(8,128)(2,1)} %collective-permute-done.7), channel_id=1, source_target_pairs={{4,0},{8,12},{5,1},{9,13},{6,2},{10,14},{7,3},{11,15},{20,16},{24,... | collective-permute-start | bytes 3145736 | tf_op jit(solution)/shard_map/ppermute | solution.py:475
  103.1 2.2 %collective-permute-start.8 = (bf16[256,1024]{1,0:T(8,128)(2,1)}, bf16[256,1024]{1,0:T(8,128)(2,1)S(1)}, u32[]{:S(2)}, u32[]{:S(2)}) collective-permute-start(bf16[256,1024]{1,0:T(8,128)(2,1)} %get-tuple-element.70), channel_id=1, source_target_pairs={{0,1},{1,0},{2,3},{3,2},{4,5},{5,4},{6,7},{7,6},{8,9},{9,8},{10,11... | collective-permute-start | bytes 1572872 | tf_op jit(solution)/shard_map/ppermute | solution.py:480
  103.1 2.9 %collective-permute-start.9 = (bf16[256,1024]{1,0:T(8,128)(2,1)}, bf16[256,1024]{1,0:T(8,128)(2,1)S(1)}, u32[]{:S(2)}, u32[]{:S(2)}) collective-permute-start(bf16[256,1024]{1,0:T(8,128)(2,1)} %get-tuple-element.71), channel_id=1, source_target_pairs={{0,1},{1,0},{2,3},{3,2},{4,5},{5,4},{6,7},{7,6},{8,9},{9,8},{10,11... | collective-permute-start | bytes 1572872 | tf_op jit(solution)/shard_map/ppermute | solution.py:480
  105.2 0.8 copy-start.13
  106.0 0.8 copy-start.15
  126.6 68.8 %all-gather.11.cloned.1.call-start = ((), (), s32[]{:S(2)}) async-start(), calls=%async_computation.2 | async-start | bytes 2621440 | tf_op jit(solution)/shard_map/all_gather | solution.py:499
  126.7 13.0 %collective-permute-start.13 = (bf16[2,256,1024]{2,1,0:T(8,128)(2,1)}, bf16[2,256,1024]{2,1,0:T(8,128)(2,1)S(1)}, u32[]{:S(2)}, u32[]{:S(2)}) collective-permute-start(bf16[2,256,1024]{2,1,0:T(8,128)(2,1)} %get-tuple-element.80), channel_id=1, source_target_pairs={{0,1},{1,0},{2,3},{3,2},{4,5},{5,4},{6,7},{7,6},{8,9},{9,8},{10,11... | collective-permute-start | bytes 3145736 | tf_op jit(solution)/shard_map/ppermute | solution.py:486
  126.8 17.1 %collective-permute-start.12 = (bf16[256,1024]{1,0:T(8,128)(2,1)}, bf16[256,1024]{1,0:T(8,128)(2,1)}, u32[]{:S(2)}, u32[]{:S(2)}) collective-permute-start(bf16[256,1024]{1,0:T(8,128)(2,1)} %get-tuple-element.78), channel_id=1, source_target_pairs={{0,2},{2,0},{1,3},{3,1},{4,6},{6,4},{5,7},{7,5},{8,10},{10,8},{9,1... | collective-permute-start | bytes 1572872 | tf_op jit(solution)/shard_map/ppermute | solution.py:485
  128.3 27.9 %collective-permute-start.16 = (bf16[512,1024]{1,0:T(8,128)(2,1)S(1)}, bf16[512,1024]{1,0:T(8,128)(2,1)S(1)}, u32[]{:S(2)}, u32[]{:S(2)}) collective-permute-start(bf16[512,1024]{1,0:T(8,128)(2,1)S(1)} %collective-permute-done.10), channel_id=1, source_target_pairs={{4,0},{8,12},{5,1},{9,13},{6,2},{10,14},{7,3},{11,15},{20,16},{24,... | collective-permute-start | bytes 3145736 | tf_op jit(solution)/shard_map/ppermute | solution.py:487
  139.6 4.2 %copy-start.8 = (bf16[256,1024]{1,0:T(8,128)(2,1)S(1)}, bf16[256,1024]{1,0:T(8,128)(2,1)}, u32[]{:S(2)}) copy-start(bf16[256,1024]{1,0:T(8,128)(2,1)} %get-tuple-element.77) | copy-start | bytes 1572868
  139.7 1.0 copy-start.5
  145.9 21.1 %collective-permute-start.14 = (bf16[256,1024]{1,0:T(8,128)(2,1)}, bf16[256,1024]{1,0:T(8,128)(2,1)S(1)}, u32[]{:S(2)}, u32[]{:S(2)}) collective-permute-start(bf16[256,1024]{1,0:T(8,128)(2,1)} %add.34), channel_id=1, source_target_pairs={{4,0},{8,12},{5,1},{9,13},{6,2},{10,14},{7,3},{11,15},{20,16},{24,... | collective-permute-start | bytes 1572872 | tf_op jit(solution)/shard_map/ppermute | solution.py:494
  147.2 19.8 %collective-permute-start.15 = (bf16[256,1024]{1,0:T(8,128)(2,1)}, bf16[256,1024]{1,0:T(8,128)(2,1)S(1)}, u32[]{:S(2)}, u32[]{:S(2)}) collective-permute-start(bf16[256,1024]{1,0:T(8,128)(2,1)} %get-tuple-element.85), channel_id=1, source_target_pairs={{0,2},{2,0},{1,3},{3,1},{4,6},{6,4},{5,7},{7,5},{8,10},{10,8},{9,1... | collective-permute-start | bytes 1572872 | tf_op jit(solution)/shard_map/ppermute | solution.py:495
  153.6 14.5 %copy-start.9 = (bf16[256,1024]{1,0:T(8,128)(2,1)S(1)}, bf16[256,1024]{1,0:T(8,128)(2,1)}, u32[]{:S(2)}) copy-start(bf16[256,1024]{1,0:T(8,128)(2,1)} %get-tuple-element.92) | copy-start | bytes 1572868
  166.9 1.2 copy-start.12
  169.3 10.2 %copy-start = (bf16[256,1024]{1,0:T(8,128)(2,1)}, bf16[256,1024]{1,0:T(8,128)(2,1)S(1)}, u32[]{:S(2)}) copy-start(bf16[256,1024]{1,0:T(8,128)(2,1)S(1)} %add_select_fusion.own) | copy-start | bytes 1572868
  169.3 18.3 %collective-permute-start.18 = (bf16[256,1024]{1,0:T(8,128)(2,1)S(1)}, bf16[256,1024]{1,0:T(8,128)(2,1)S(1)}, u32[]{:S(2)}, u32[]{:S(2)}) collective-permute-start(bf16[256,1024]{1,0:T(8,128)(2,1)S(1)} %add_select_fusion.own), channel_id=1, source_target_pairs={{0,2},{2,0},{1,3},{3,1},{4,6},{6,4},{5,7},{7,5},{8,10},{10,8},{9,1... | collective-permute-start | bytes 1572872 | tf_op jit(solution)/shard_map/ppermute | solution.py:504
  170.2 17.4 %collective-permute-start.19 = (bf16[256,1024]{1,0:T(8,128)(2,1)S(1)}, bf16[256,1024]{1,0:T(8,128)(2,1)S(1)}, u32[]{:S(2)}, u32[]{:S(2)}) collective-permute-start(bf16[256,1024]{1,0:T(8,128)(2,1)S(1)} %add_select_fusion.own), channel_id=1, source_target_pairs={{0,1},{1,0},{2,3},{3,2},{4,5},{5,4},{6,7},{7,6},{8,9},{9,8},{10,11... | collective-permute-start | bytes 1572872 | tf_op jit(solution)/shard_map/ppermute | solution.py:504
  170.2 17.5 %collective-permute-start.17 = (bf16[256,1024]{1,0:T(8,128)(2,1)}, bf16[256,1024]{1,0:T(8,128)(2,1)S(1)}, u32[]{:S(2)}, u32[]{:S(2)}) collective-permute-start(bf16[256,1024]{1,0:T(8,128)(2,1)} %get-tuple-element.91), channel_id=1, source_target_pairs={{4,0},{8,12},{5,1},{9,13},{6,2},{10,14},{7,3},{11,15},{20,16},{24,... | collective-permute-start | bytes 1572872 | tf_op jit(solution)/shard_map/ppermute | solution.py:502
  171.5 16.2 %copy-start.16 = (bf16[256,1024]{1,0:T(8,128)(2,1)S(1)}, bf16[256,1024]{1,0:T(8,128)(2,1)}, u32[]{:S(2)}) copy-start(bf16[256,1024]{1,0:T(8,128)(2,1)} %get-tuple-element.90) | copy-start | bytes 1572868
  187.6 2.0 copy-start.10
  187.6 2.0 copy-start.11
  187.6 2.0 collective-permute-start.20
  189.6 0.8 copy-start.14
Sparse Core Ops, SparseCore 0:
  72.8 21.0 all-gather.6
  126.8 29.3 all-gather.8
  168.3 27.1 all-gather.10

commit v15 on v14

--- a/solution.py
+++ b/solution.py
@@ -140,19 +140,23 @@
     depth, width = turned.shape[::-1] if weight is None else weight.shape
     cols_n = width // size
     total = (depth // size) * cols_n
-
-    @pl.loop(0, slots, unroll=4)
-    def place(s):
-        b = ids[first + s]
-
-        @pl.when(b < total)
-        def put():
-            r = pl.multiple_of((b // cols_n) * size, size)
-            c = pl.multiple_of((b % cols_n) * size, size)
-            if weight is not None:
-                weight[pl.ds(r, size), pl.ds(c, size)] = blocks[s]
-            if turned is not None:
-                turned[pl.ds(c, size), pl.ds(r, size)] = blocks[s].T
+    group = math.gcd(slots, 8)
+
+    @pl.loop(0, slots // group)
+    def place(g):
+        some = [g * group + j for j in range(group)]
+        flipped = [None if turned is None else blocks[s].T for s in some]
+        for s, flip in zip(some, flipped):
+            b = ids[first + s]
+
+            @pl.when(b < total)
+            def put(s=s, flip=flip, b=b):
+                r = pl.multiple_of((b // cols_n) * size, size)
+                c = pl.multiple_of((b % cols_n) * size, size)
+                if weight is not None:
+                    weight[pl.ds(r, size), pl.ds(c, size)] = blocks[s]
+                if turned is not None:
+                    turned[pl.ds(c, size), pl.ds(r, size)] = flip
 
 
 def place_kernel(
@@ -362,9 +366,18 @@
 
 
 def line_grads_kernel(pairs_n, ids, *refs):
-    pairs = [(refs[2 * k], refs[2 * k + 1]) for k in range(pairs_n)]
-    grads = refs[-1]
-    start = refs[2 * pairs_n] if len(refs) > 2 * pairs_n + 1 else None
+    refs = list(refs)
+    pairs = []
+    for k in range(pairs_n):
+        x, d = refs.pop(0), refs.pop(0)
+        if d.shape[0] > x.shape[-2]:
+            rows, other = x.shape[-2], refs.pop(0)
+            total_d = refs.pop()
+            total_d[...] = d[rows:] + other[rows:]
+            d = total_d
+        pairs.append((x, d))
+    start = refs.pop(0) if len(refs) == 2 else None
+    (grads,) = refs
     slots, size = grads.shape[0], grads.shape[1]
     first = pairs[0][0]
     cols_n = pairs[0][1].shape[1] // size
@@ -393,17 +406,20 @@
 
 def line_grads(ids, pairs, start, size):
     slots = ids.shape[0]
-    rows = pairs[0][1].shape[0]
     flat = [a for pair in pairs for a in pair] + ([] if start is None else [start])
+    sums = [
+        pltpu.VMEM((p[0].shape[-2], p[1].shape[1]), jnp.bfloat16) for p in pairs if len(p) == 3
+    ]
     return pl.pallas_call(
         functools.partial(line_grads_kernel, len(pairs)),
         out_shape=jax.ShapeDtypeStruct((slots, size, size), jnp.bfloat16),
         in_specs=[whole(pltpu.SMEM)] + [whole()] * len(flat),
         out_specs=whole(),
-        compiler_params=pltpu.CompilerParams(vmem_limit_bytes=VMEM_LIMIT),
-        cost_estimate=pl.CostEstimate(
-            flops=2 * len(pairs) * slots * rows * size * size,
-            bytes_accessed=sum(2 * a.size for a in flat) + 4 * slots * size * size,
+        scratch_shapes=sums,
+        compiler_params=pltpu.CompilerParams(vmem_limit_bytes=VMEM_LIMIT),
+        cost_estimate=pl.CostEstimate(
+            flops=512 * len(pairs) * slots * size * size,
+            bytes_accessed=sum(2 * a.size for a in flat) + 2 * slots * size * size,
             transcendentals=0,
         ),
         name="line_grads",
@@ -443,15 +459,16 @@
     stage = lax.optimization_barrier
 
     mine = lax.dynamic_slice_in_dim(blocks, half * half_slots, half_slots, 0)
-    other = lax.dynamic_slice_in_dim(blocks, (1 - half) * half_slots, half_slots, 0)
     mine = jnp.concatenate([mine, ids_block(block_ids, size).astype(jnp.bfloat16)])
+    mine, late_blocks = stage((mine, blocks))
+
+    near_a = along(mine, perm=INWARD)
+    far_a = along(mine, perm=MIDDLE)
+    other = lax.dynamic_slice_in_dim(late_blocks, (1 - half) * half_slots, half_slots, 0)
     part = lax.dynamic_slice_in_dim(tokens, lax.axis_index(INNER) * part_width, part_width, 1)
     both = jnp.concatenate([part, upstream])
-    mine, other, both = stage((mine, other, both))
-
-    near_a = along(mine, perm=INWARD)
-    far_a = along(mine, perm=MIDDLE)
-    near_a, far_a, both, other = stage((near_a, far_a, both, other))
+    grads = line_grads(block_ids, ((tokens, upstream),), None, size)
+    near_a, far_a, both, other, grads = stage((near_a, far_a, both, other, grads))
 
     end_a = along(near_a, perm=MIDDLE)
     far_b = across(far_a)
@@ -486,9 +503,7 @@
     own_keep, own_give = add_split(place_of, own_keep, cores(own_give))
     both_3o = along(both_3m, perm=OUTWARD)
     tokens_2 = lax.all_gather(both_2m[:rows] + both_2o[:rows], INNER)
-    upstream_2 = both_2m[rows:] + both_2o[rows:]
-    pairs = ((tokens, upstream), (tokens_1, upstream_1))
-    grads = line_grads(block_ids, pairs, None, size)
+    grads = line_grads(block_ids, ((tokens_1, upstream_1),), grads, size)
     end_got, own_give, own_keep, grads = stage((end_got, own_give, own_keep, grads))
 
     sum_out = along(end_keep + end_got, perm=OUTWARD)
@@ -497,15 +512,14 @@
     sum_out, own_got, both_3o, proj, end_proj = stage((sum_out, own_got, both_3o, proj, end_proj))
 
     tokens_3 = lax.all_gather(both_3m[:rows] + both_3o[:rows], INNER)
-    upstream_3 = both_3m[rows:] + both_3o[rows:]
     quarter = jnp.where(middle, own_keep + own_got, sum_out)
     proj_out = along(end_proj, perm=OUTWARD)
-    grads = line_grads(block_ids, ((tokens_2, upstream_2),), grads, size)
+    grads = line_grads(block_ids, ((tokens_2, both_2m, both_2o),), grads, size)
     by_tensor, by_core, grads = stage((sideways(quarter), cores(quarter), grads))
     by_both = cores(by_tensor)
     projected = jnp.where(middle, proj, proj_out)
     token_grad = assemble(place_of, (quarter, by_core, by_tensor, by_both))
-    grads = line_grads(block_ids, ((tokens_3, upstream_3),), grads, size)
+    grads = line_grads(block_ids, ((tokens_3, both_3m, both_3o),), grads, size)
     return projected, token_grad, grads
 
 

time: 211 us -> 207 us (0.981)
  waiting for transfers between devices: 92.5 us -> 85.7 us
  Pallas kernels: 51.4 us -> 57.6 us
    ppermute x1, waiting for transfers between devices: 22.3 us -> 12.7 us  [line_body(): near_a = along(mine, perm=INWARD)]
    pallas_call x3 -> x4, Pallas kernels: 25.8 us -> 31.7 us  [line_grads(): pl.pallas_call(functools.partial(line_grads_kernel, len(pairs)), out_shap...]
    ppermute x1, waiting for transfers between devices: 0.16 us -> 5.38 us  [line_body(): end_got = sideways(end_give)]
    ppermute x1, waiting for transfers between devices: 2.63 us -> 0.26 us  [line_body(): both_3o = along(both_3m, perm=OUTWARD)]
  transfers between devices with their start and end apart: 24 -> 24, of which waited for: 12 -> 12; matrix products, arithmetic and copies ran while one was open for 3% -> 5% of each run, Pallas kernels for 21% -> 24%
where the time goes in v15:
time: 207 us
  waiting for transfers between devices  85.7 us (41%)
  Pallas kernels  57.6 us (28%)
  starting transfers between devices  31.7 us (15%)
  between operations  14 us (7%)
  other arithmetic  10.2 us (5%)
  local copies, waits for them, and re-layouts  7.22 us (3%)
    pallas_call x4, Pallas kernels, line_grads(): pl.pallas_call(functools.partial(line_grads_kernel, len(pairs)), out_shap...  31.7 us
    ppermute x1, waiting for transfers between devices, line_body(): both_1 = along(both, perm=PAIRS)  21.7 us
    ppermute x1, waiting for transfers between devices, line_body(): both_2o = along(both_2m, perm=OUTWARD)  14.7 us
    ppermute x1, waiting for transfers between devices, line_body(): near_a = along(mine, perm=INWARD)  12.7 us
    ppermute x1, waiting for transfers between devices, line_body(): sum_out = along(end_keep + end_got, perm=OUTWARD)  10.5 us
    ppermute x1, waiting for transfers between devices, line_body(): sideways(quarter)  9.46 us
    pallas_call x1, Pallas kernels, place_first(): pl.pallas_call(place_kernel, out_shape=(jax.ShapeDtypeStruct((depth, widt...  8.74 us
    ppermute x1, waiting for transfers between devices, line_body(): near_b = along(other, perm=INWARD)  7.24 us
  transfers between devices with their start and end apart: 24, of which 12 were waited for; matrix products, arithmetic and copies ran while one was open for 5% of the time, Pallas kernels for 24%

profile of v15, /device:TPU:0, one launch (start us, length us, event | category | flops | bytes accessed | tf_op | source)
XLA Modules:
  0.0 206.6 jit_solution(9662161477276742452)
XLA Ops:
  7.2 0.0 all-gather.7.cloned.1.call-start
  7.2 0.7 convert_element_type.26
  7.9 0.1 convert_element_type.27
  8.0 1.3 constant_dynamic-slice_fusion.2
  9.3 1.1 pad_maximum_fusion
  10.4 5.0 %collective-permute-start = (bf16[33,128,128]{2,1,0:T(8,128)(2,1)}, bf16[33,128,128]{2,1,0:T(8,128)(2,1)S(1)}, u32[]{:S(2)}, u32[]{:S(2)}) collective-permute-start(bf16[33,128,128]{2,1,0:T(8,128)(2,1)} %pad_maximum_fusion), channel_id=1, source_target_pairs={{0,4},{12,8},{1,5},{13,9},{2,6},{14,10},{3,7},{15,11},{16,20},{28,... | collective-permute-start | bytes 3244040 | tf_op jit(solution)/shard_map/ppermute | solution.py:465
  15.4 0.7 collective-permute-start.1
  16.1 6.9 %line_grads.4.refs_2_ = bf16[64,128,128]{2,1,0:T(8,128)(2,1)} custom-call(s32[64]{0:T(128)} %ids.7, bf16[256,4096]{1,0:T(8,128)(2,1)} %tokens.1, bf16[256,1024]{1,0:T(8,128)(2,1)} %upstream.1), custom_call_target="tpu_custom_call" | custom-call | flops 536870912 | bytes 4718592 | tf_op jit(solution)/shard_map/line_grads/pallas_call | solution.py:413
  23.0 1.2 constant_dynamic-slice_fusion.1
  24.3 0.1 pad_maximum_fusion.1
  24.4 0.4 copy-done
  24.8 1.2 constant_dynamic-slice_fusion
  26.0 12.7 %collective-permute-done.near_a = bf16[33,128,128]{2,1,0:T(8,128)(2,1)S(1)} collective-permute-done((bf16[33,128,128]{2,1,0:T(8,128)(2,1)}, bf16[33,128,128]{2,1,0:T(8,128)(2,1)S(1)}, u32[]{:S(2)}, u32[]{:S(2)}) %collective-permute-start) | collective-permute-done | bytes 1081376 | tf_op jit(solution)/shard_map/ppermute | solution.py:465
  38.7 1.7 collective-permute-start.3
  40.4 1.5 collective-permute-start.4
  42.0 5.5 %collective-permute-start.2 = (bf16[512,1024]{1,0:T(8,128)(2,1)S(1)}, bf16[512,1024]{1,0:T(8,128)(2,1)S(1)}, u32[]{:S(2)}, u32[]{:S(2)}) collective-permute-start(bf16[512,1024]{1,0:T(8,128)(2,1)S(1)} %pad_maximum_fusion.1), channel_id=1, source_target_pairs={{0,4},{12,8},{4,0},{8,12},{1,5},{13,9},{5,1},{9,13},{2,6},{14,10},... | collective-permute-start | bytes 3145736 | tf_op jit(solution)/shard_map/ppermute | solution.py:475
  47.5 21.7 %collective-permute-done.2 = bf16[512,1024]{1,0:T(8,128)(2,1)S(1)} collective-permute-done((bf16[512,1024]{1,0:T(8,128)(2,1)S(1)}, bf16[512,1024]{1,0:T(8,128)(2,1)S(1)}, u32[]{:S(2)}, u32[]{:S(2)}) %collective-permute-start.2) | collective-permute-done | bytes 1048608 | tf_op jit(solution)/shard_map/ppermute | solution.py:475
  69.2 1.1 copy-done.9
  70.3 1.0 fusion
  71.3 0.0 all-gather.9.cloned.1.call-start
  71.4 0.6 collective-permute-start.6
  72.0 4.6 %collective-permute-start.5 = (bf16[32,128,128]{2,1,0:T(8,128)(2,1)}, bf16[32,128,128]{2,1,0:T(8,128)(2,1)}, u32[]{:S(2)}, u32[]{:S(2)}) collective-permute-start(bf16[32,128,128]{2,1,0:T(8,128)(2,1)} %constant_dynamic-slice_fusion), channel_id=1, source_target_pairs={{0,4},{12,8},{1,5},{13,9},{2,6},{14,10},{3,7},{15,11},{16,20},{28,... | collective-permute-start | bytes 3145736 | tf_op jit(solution)/shard_map/ppermute | solution.py:479
  76.6 0.7 collective-permute-start.7
  77.3 0.7 pad_add_fusion.place_of
  78.0 0.6 bitcast_convert_fusion
  78.6 1.2 bitcast_convert_fusion.1.ids_3
  79.8 8.7 %place_first.1 = (bf16[4096,1024]{1,0:T(8,128)(2,1)}, bf16[1024,4096]{1,0:T(8,128)(2,1)}) custom-call(s32[4]{0:T(128)} %pad_add_fusion.place_of, s32[64]{0:T(128)} %ids.7, s32[64]{0:T(128)} %get-tuple-element.104.ids_1, s32[64]{0:T(128)} %get-tuple-element.103.ids_2, s32[64]{0:T(128)} %bitcast_convert_fusion.1.ids_3, bf16[64,128,128]{2,1,0:T(8,128)(2,1)} %own.1, ...), custom_call_target="tpu_custom_call" | custom-call | bytes 25165824 | tf_op jit(solution)/shard_map/place_first/pallas_call | solution.py:181
  88.6 7.2 %collective-permute-done.5.near_b = bf16[32,128,128]{2,1,0:T(8,128)(2,1)} collective-permute-done((bf16[32,128,128]{2,1,0:T(8,128)(2,1)}, bf16[32,128,128]{2,1,0:T(8,128)(2,1)}, u32[]{:S(2)}, u32[]{:S(2)}) %collective-permute-start.5) | collective-permute-done | bytes 1048608 | tf_op jit(solution)/shard_map/ppermute | solution.py:479
  95.8 0.7 collective-permute-start.10
  96.6 1.3 collective-permute-start.11
  97.9 3.9 %project_back.1 = (bf16[2,256,1024]{2,1,0:T(8,128)(2,1)}, bf16[2,256,1024]{2,1,0:T(8,128)(2,1)}, bf16[2,256,1024]{2,1,0:T(8,128)(2,1)}, bf16[256,1024]{1,0:T(8,128)(2,1)}, bf16[256,1024]{1,0:T(8,128)(2,1)}) custom-call(s32[4]{0:T(128)} %pad_add_fusion.place_of, s32[64]{0:T(128)} %get-tuple-element.104.ids_1, s32[64]{0:T(128)} %bitcast_convert_fusion.1.ids_3, ...), custom_call_target="tpu_custom_call" | custom-call | flops 4294967296 | bytes 13631488 | tf_op jit(solution)/shard_map/project_back/pallas_call | solution.py:239
  101.7 0.1 collective-permute-start.8
  101.8 0.5 collective-permute-start.9
  102.3 1.6 collective-permute-done.8.refs_0_
  103.9 0.9 collective-permute-done.9.refs_1_
  104.8 3.1 %add_split.2 = (bf16[256,1024]{1,0:T(8,128)(2,1)}, bf16[256,1024]{1,0:T(8,128)(2,1)}) custom-call(s32[4]{0:T(128)} %pad_add_fusion.place_of, bf16[2,256,1024]{2,1,0:T(8,128)(2,1)} %get-tuple-element.68.keep, bf16[256,1024]{1,0:T(8,128)(2,1)} %copy-done.15, bf16[256,1024]{1,0:T(8,128)(2,1)} %collective-permute-done.9.refs_1_), custom_call_target="tpu_custom_call" | custom-call | flops 524288 | bytes 3145728 | tf_op jit(solution)/shard_map/add_split/pallas_call | solution.py:330
  107.9 14.7 %collective-permute-done.11.refs_2_ = bf16[512,1024]{1,0:T(8,128)(2,1)S(1)} collective-permute-done((bf16[512,1024]{1,0:T(8,128)(2,1)S(1)}, bf16[512,1024]{1,0:T(8,128)(2,1)S(1)}, u32[]{:S(2)}, u32[]{:S(2)}) %collective-permute-start.11) | collective-permute-done | bytes 1048608 | tf_op jit(solution)/shard_map/ppermute | solution.py:492
  122.6 0.9 slice_add_fusion.1
  123.6 0.0 all-gather.11.cloned.1.call-start
  123.6 0.1 collective-permute-start.13
  123.7 1.6 collective-permute-start.12
  125.3 1.3 collective-permute-start.16
  126.6 7.8 %line_grads.5.refs_3_ = bf16[64,128,128]{2,1,0:T(8,128)(2,1)} custom-call(s32[64]{0:T(128)} %ids.7, bf16[4,256,1024]{2,1,0:T(8,128)(2,1)} %bitcast.16, bf16[256,1024]{1,0:T(8,128)(2,1)} %get-tuple-element.101.end_upstream.refs_1_, bf16[64,128,128]{2,1,0:T(8,128)(2,1)} %line_grads.4.refs_2_), custom_call_target="tpu_custom_call" | custom-call | flops 536870912 | bytes 6815744 | tf_op jit(solution)/shard_map/line_grads/pallas_call | solution.py:413
  134.4 3.1 %add_split.3 = (bf16[256,1024]{1,0:T(8,128)(2,1)}, bf16[256,1024]{1,0:T(8,128)(2,1)}) custom-call(s32[4]{0:T(128)} %pad_add_fusion.place_of, bf16[2,256,1024]{2,1,0:T(8,128)(2,1)} %get-tuple-element.78.keep, bf16[2,256,1024]{2,1,0:T(8,128)(2,1)} %collective-permute-done.13.refs_0_), custom_call_target="tpu_custom_call" | custom-call | flops 524288 | bytes 3145728 | tf_op jit(solution)/shard_map/add_split/pallas_call | solution.py:330
  137.6 5.4 %collective-permute-done.12 = bf16[256,1024]{1,0:T(8,128)(2,1)} collective-permute-done((bf16[256,1024]{1,0:T(8,128)(2,1)}, bf16[256,1024]{1,0:T(8,128)(2,1)}, u32[]{:S(2)}, u32[]{:S(2)}) %collective-permute-start.12) | collective-permute-done | bytes 524320 | tf_op jit(solution)/shard_map/ppermute | solution.py:502
  142.9 2.0 add.28
  145.0 1.3 collective-permute-start.14
  146.3 2.5 %collective-permute-start.15 = (bf16[256,1024]{1,0:T(8,128)(2,1)}, bf16[256,1024]{1,0:T(8,128)(2,1)}, u32[]{:S(2)}, u32[]{:S(2)}) collective-permute-start(bf16[256,1024]{1,0:T(8,128)(2,1)} %get-tuple-element.85), channel_id=1, source_target_pairs={{0,2},{2,0},{1,3},{3,1},{4,6},{6,4},{5,7},{7,5},{8,10},{10,8},{9,1... | collective-permute-start | bytes 1572872 | tf_op jit(solution)/shard_map/ppermute | solution.py:510
  148.8 4.1 %project_forward.1 = (bf16[256,1024]{1,0:T(8,128)(2,1)}, bf16[256,1024]{1,0:T(8,128)(2,1)}) custom-call(s32[4]{0:T(128)} %pad_add_fusion.place_of, s32[64]{0:T(128)} %get-tuple-element.104.ids_1, s32[64]{0:T(128)} %bitcast_convert_fusion.1.ids_3, bf16[4096,1024]{1,0:T(8,128)(2,1)} %get-tuple-element.87.partial, ...), custom_call_target="tpu_custom_call" | custom-call | flops 4294967296 | bytes 13631488 | tf_op jit(solution)/shard_map/project_forward/pallas_call | solution.py:296
  152.9 0.3 collective-permute-done.16.refs_2_
  153.2 10.5 %collective-permute-done.14 = bf16[256,1024]{1,0:T(8,128)(2,1)S(1)} collective-permute-done((bf16[256,1024]{1,0:T(8,128)(2,1)}, bf16[256,1024]{1,0:T(8,128)(2,1)S(1)}, u32[]{:S(2)}, u32[]{:S(2)}) %collective-permute-start.14) | collective-permute-done | bytes 524320 | tf_op jit(solution)/shard_map/ppermute | solution.py:509
  163.6 0.9 slice_add_fusion
  164.5 1.1 add_select_fusion.own
  165.7 0.6 collective-permute-start.18
  166.3 1.3 collective-permute-start.17
  167.6 8.6 %line_grads.6.refs_3_ = bf16[64,128,128]{2,1,0:T(8,128)(2,1)} custom-call(s32[64]{0:T(128)} %ids.7, bf16[4,256,1024]{2,1,0:T(8,128)(2,1)} %bitcast.18, bf16[512,1024]{1,0:T(8,128)(2,1)} %copy-done.1, bf16[512,1024]{1,0:T(8,128)(2,1)} %copy-done.3, bf16[64,128,128]{2,1,0:T(8,128)(2,1)} %line_grads.5.refs_3_), custom_call_target="tpu_custom_call" | custom-call | flops 536870912 | bytes 8388608 | tf_op jit(solution)/shard_map/line_grads/pallas_call | solution.py:413
  176.2 9.5 %collective-permute-done.18.by_tensor = bf16[256,1024]{1,0:T(8,128)(2,1)S(1)} collective-permute-done((bf16[256,1024]{1,0:T(8,128)(2,1)S(1)}, bf16[256,1024]{1,0:T(8,128)(2,1)S(1)}, u32[]{:S(2)}, u32[]{:S(2)}) %collective-permute-start.18) | collective-permute-done | bytes 524320 | tf_op jit(solution)/shard_map/ppermute | solution.py:518
  185.7 0.1 collective-permute-start.20
  185.8 1.0 broadcast_select_fusion
  186.8 0.9 collective-permute-done.20.by_both
  187.7 0.8 copy-done.16
  188.5 3.0 %assemble.1 = bf16[256,4096]{1,0:T(8,128)(2,1)} custom-call(s32[4]{0:T(128)} %pad_add_fusion.place_of, bf16[256,1024]{1,0:T(8,128)(2,1)} %copy-done.5, bf16[256,1024]{1,0:T(8,128)(2,1)} %copy-done.14, bf16[256,1024]{1,0:T(8,128)(2,1)} %copy-done.13, bf16[256,1024]{1,0:T(8,128)(2,1)} %copy-done.16), custom_call_target="tpu_custom_call" | custom-call | bytes 4194304 | tf_op jit(solution)/shard_map/assemble/pallas_call | solution.py:355
  191.4 0.2 all-gather.11.cloned.1.call-done
  191.7 8.4 %line_grads.7 = bf16[64,128,128]{2,1,0:T(8,128)(2,1)} custom-call(s32[64]{0:T(128)} %ids.7, bf16[4,256,1024]{2,1,0:T(8,128)(2,1)} %bitcast.19, bf16[512,1024]{1,0:T(8,128)(2,1)} %copy-done.2, bf16[512,1024]{1,0:T(8,128)(2,1)} %copy-done.4, bf16[64,128,128]{2,1,0:T(8,128)(2,1)} %line_grads.6.refs_3_), custom_call_target="tpu_custom_call" | custom-call | flops 536870912 | bytes 8388608 | tf_op jit(solution)/shard_map/line_grads/pallas_call | solution.py:413
  (51 shorter events, 0.2 us)
Async XLA Ops:
  7.2 88.7 %all-gather.7.cloned.1.call-start = ((), (), s32[]{:S(2)}) async-start(), calls=%async_computation | async-start | bytes 2621440 | tf_op jit(solution)/shard_map/all_gather | solution.py:482
  10.4 28.3 %collective-permute-start = (bf16[33,128,128]{2,1,0:T(8,128)(2,1)}, bf16[33,128,128]{2,1,0:T(8,128)(2,1)S(1)}, u32[]{:S(2)}, u32[]{:S(2)}) collective-permute-start(bf16[33,128,128]{2,1,0:T(8,128)(2,1)} %pad_maximum_fusion), channel_id=1, source_target_pairs={{0,4},{12,8},{1,5},{13,9},{2,6},{14,10},{3,7},{15,11},{16,20},{28,... | collective-permute-start | bytes 3244040 | tf_op jit(solution)/shard_map/ppermute | solution.py:465
  15.4 23.4 %collective-permute-start.1 = (bf16[33,128,128]{2,1,0:T(8,128)(2,1)}, bf16[33,128,128]{2,1,0:T(8,128)(2,1)S(1)}, u32[]{:S(2)}, u32[]{:S(2)}) collective-permute-start(bf16[33,128,128]{2,1,0:T(8,128)(2,1)} %pad_maximum_fusion), channel_id=1, source_target_pairs={{4,8},{8,4},{5,9},{9,5},{6,10},{10,6},{7,11},{11,7},{20,24},{24,20... | collective-permute-start | bytes 3244040 | tf_op jit(solution)/shard_map/ppermute | solution.py:466
  16.1 8.1 %copy-start.6 = (bf16[256,1024]{1,0:T(8,128)(2,1)S(1)}, bf16[256,1024]{1,0:T(8,128)(2,1)}, u32[]{:S(2)}) copy-start(bf16[256,1024]{1,0:T(8,128)(2,1)} %upstream.1) | copy-start | bytes 1572868
  23.0 1.8 copy-start
  24.8 46.5 %copy-start.10 = (bf16[512,1024]{1,0:T(8,128)(2,1)}, bf16[512,1024]{1,0:T(8,128)(2,1)S(1)}, u32[]{:S(2)}) copy-start(bf16[512,1024]{1,0:T(8,128)(2,1)S(1)} %pad_maximum_fusion.1) | copy-start | bytes 3145732
  38.7 41.1 %copy-start.7 = (bf16[33,128,128]{2,1,0:T(8,128)(2,1)}, bf16[33,128,128]{2,1,0:T(8,128)(2,1)S(1)}, u32[]{:S(2)}) copy-start(bf16[33,128,128]{2,1,0:T(8,128)(2,1)S(1)} %collective-permute-done.near_a) | copy-start | bytes 3244036
  38.7 41.1 %copy-start.8 = (bf16[33,128,128]{2,1,0:T(8,128)(2,1)}, bf16[33,128,128]{2,1,0:T(8,128)(2,1)S(1)}, u32[]{:S(2)}) copy-start(bf16[33,128,128]{2,1,0:T(8,128)(2,1)S(1)} %collective-permute-done.1.far_a) | copy-start | bytes 3244036
  38.7 30.5 %collective-permute-start.3 = (bf16[33,128,128]{2,1,0:T(8,128)(2,1)S(1)}, bf16[33,128,128]{2,1,0:T(8,128)(2,1)}, u32[]{:S(2)}, u32[]{:S(2)}) collective-permute-start(bf16[33,128,128]{2,1,0:T(8,128)(2,1)S(1)} %collective-permute-done.near_a), channel_id=1, source_target_pairs={{4,8},{8,4},{5,9},{9,5},{6,10},{10,6},{7,11},{11,7},{20,24},{24,20... | collective-permute-start | bytes 3244040 | tf_op jit(solution)/shard_map/ppermute | solution.py:473
  40.4 28.8 %collective-permute-start.4 = (bf16[33,128,128]{2,1,0:T(8,128)(2,1)S(1)}, bf16[33,128,128]{2,1,0:T(8,128)(2,1)}, u32[]{:S(2)}, u32[]{:S(2)}) collective-permute-start(bf16[33,128,128]{2,1,0:T(8,128)(2,1)S(1)} %collective-permute-done.1.far_a), channel_id=1, source_target_pairs={{0,16},{16,0},{1,17},{17,1},{2,18},{18,2},{3,19},{19,3},{4,20},{20... | collective-permute-start | bytes 3244040 | tf_op jit(solution)/shard_map/ppermute | solution.py:474
  42.0 27.2 %collective-permute-start.2 = (bf16[512,1024]{1,0:T(8,128)(2,1)S(1)}, bf16[512,1024]{1,0:T(8,128)(2,1)S(1)}, u32[]{:S(2)}, u32[]{:S(2)}) collective-permute-start(bf16[512,1024]{1,0:T(8,128)(2,1)S(1)} %pad_maximum_fusion.1), channel_id=1, source_target_pairs={{0,4},{12,8},{4,0},{8,12},{1,5},{13,9},{5,1},{9,13},{2,6},{14,10},... | collective-permute-start | bytes 3145736 | tf_op jit(solution)/shard_map/ppermute | solution.py:475
  69.2 1.1 copy-start.9
  71.3 96.2 %all-gather.9.cloned.1.call-start = ((), (), s32[]{:S(2)}) async-start(), calls=%async_computation.1 | async-start | bytes 2621440 | tf_op jit(solution)/shard_map/all_gather | solution.py:505
  71.4 24.4 %collective-permute-start.6 = (bf16[33,128,128]{2,1,0:T(8,128)(2,1)}, bf16[33,128,128]{2,1,0:T(8,128)(2,1)}, u32[]{:S(2)}, u32[]{:S(2)}) collective-permute-start(bf16[33,128,128]{2,1,0:T(8,128)(2,1)} %collective-permute-done.3.end_a), channel_id=1, source_target_pairs={{0,16},{16,0},{1,17},{17,1},{2,18},{18,2},{3,19},{19,3},{4,20},{20... | collective-permute-start | bytes 3244040 | tf_op jit(solution)/shard_map/ppermute | solution.py:480
  72.0 23.8 %collective-permute-start.5 = (bf16[32,128,128]{2,1,0:T(8,128)(2,1)}, bf16[32,128,128]{2,1,0:T(8,128)(2,1)}, u32[]{:S(2)}, u32[]{:S(2)}) collective-permute-start(bf16[32,128,128]{2,1,0:T(8,128)(2,1)} %constant_dynamic-slice_fusion), channel_id=1, source_target_pairs={{0,4},{12,8},{1,5},{13,9},{2,6},{14,10},{3,7},{15,11},{16,20},{28,... | collective-permute-start | bytes 3145736 | tf_op jit(solution)/shard_map/ppermute | solution.py:479
  76.6 19.2 %collective-permute-start.7 = (bf16[512,1024]{1,0:T(8,128)(2,1)}, bf16[512,1024]{1,0:T(8,128)(2,1)S(1)}, u32[]{:S(2)}, u32[]{:S(2)}) collective-permute-start(bf16[512,1024]{1,0:T(8,128)(2,1)} %copy-done.10), channel_id=1, source_target_pairs={{4,8},{8,4},{5,9},{9,5},{6,10},{10,6},{7,11},{11,7},{20,24},{24,20... | collective-permute-start | bytes 3145736 | tf_op jit(solution)/shard_map/ppermute | solution.py:481
  95.8 26.9 %copy-start.1 = (bf16[512,1024]{1,0:T(8,128)(2,1)}, bf16[512,1024]{1,0:T(8,128)(2,1)S(1)}, u32[]{:S(2)}) copy-start(bf16[512,1024]{1,0:T(8,128)(2,1)S(1)} %collective-permute-done.7.refs_1_) | copy-start | bytes 3145732
  95.8 12.1 %collective-permute-start.10 = (bf16[512,1024]{1,0:T(8,128)(2,1)}, bf16[512,1024]{1,0:T(8,128)(2,1)S(1)}, u32[]{:S(2)}, u32[]{:S(2)}) collective-permute-start(bf16[512,1024]{1,0:T(8,128)(2,1)} %copy-done.9), channel_id=1, source_target_pairs={{4,8},{8,4},{5,9},{9,5},{6,10},{10,6},{7,11},{11,7},{20,24},{24,20... | collective-permute-start | bytes 3145736 | tf_op jit(solution)/shard_map/ppermute | solution.py:491
  96.6 26.1 %collective-permute-start.11 = (bf16[512,1024]{1,0:T(8,128)(2,1)S(1)}, bf16[512,1024]{1,0:T(8,128)(2,1)S(1)}, u32[]{:S(2)}, u32[]{:S(2)}) collective-permute-start(bf16[512,1024]{1,0:T(8,128)(2,1)S(1)} %collective-permute-done.7.refs_1_), channel_id=1, source_target_pairs={{4,0},{8,12},{5,1},{9,13},{6,2},{10,14},{7,3},{11,15},{20,16},{24,... | collective-permute-start | bytes 3145736 | tf_op jit(solution)/shard_map/ppermute | solution.py:492
  101.7 2.2 %collective-permute-start.8 = (bf16[256,1024]{1,0:T(8,128)(2,1)}, bf16[256,1024]{1,0:T(8,128)(2,1)S(1)}, u32[]{:S(2)}, u32[]{:S(2)}) collective-permute-start(bf16[256,1024]{1,0:T(8,128)(2,1)} %get-tuple-element.69), channel_id=1, source_target_pairs={{0,1},{1,0},{2,3},{3,2},{4,5},{5,4},{6,7},{7,6},{8,9},{9,8},{10,11... | collective-permute-start | bytes 1572872 | tf_op jit(solution)/shard_map/ppermute | solution.py:497
  101.8 3.0 %collective-permute-start.9 = (bf16[256,1024]{1,0:T(8,128)(2,1)}, bf16[256,1024]{1,0:T(8,128)(2,1)}, u32[]{:S(2)}, u32[]{:S(2)}) collective-permute-start(bf16[256,1024]{1,0:T(8,128)(2,1)} %get-tuple-element.70), channel_id=1, source_target_pairs={{0,1},{1,0},{2,3},{3,2},{4,5},{5,4},{6,7},{7,6},{8,9},{9,8},{10,11... | collective-permute-start | bytes 1572872 | tf_op jit(solution)/shard_map/ppermute | solution.py:497
  103.9 0.9 copy-start.15
  107.9 55.7 %copy-start.2 = (bf16[512,1024]{1,0:T(8,128)(2,1)}, bf16[512,1024]{1,0:T(8,128)(2,1)S(1)}, u32[]{:S(2)}) copy-start(bf16[512,1024]{1,0:T(8,128)(2,1)S(1)} %collective-permute-done.10.refs_1_) | copy-start | bytes 3145732
  122.6 11.8 %copy-start.3 = (bf16[512,1024]{1,0:T(8,128)(2,1)}, bf16[512,1024]{1,0:T(8,128)(2,1)S(1)}, u32[]{:S(2)}) copy-start(bf16[512,1024]{1,0:T(8,128)(2,1)S(1)} %collective-permute-done.11.refs_2_) | copy-start | bytes 3145732
  123.6 68.1 %all-gather.11.cloned.1.call-start = ((), (), s32[]{:S(2)}) async-start(), calls=%async_computation.2 | async-start | bytes 2621440 | tf_op jit(solution)/shard_map/all_gather | solution.py:514
  123.6 10.8 %collective-permute-start.13 = (bf16[2,256,1024]{2,1,0:T(8,128)(2,1)}, bf16[2,256,1024]{2,1,0:T(8,128)(2,1)}, u32[]{:S(2)}, u32[]{:S(2)}) collective-permute-start(bf16[2,256,1024]{2,1,0:T(8,128)(2,1)} %get-tuple-element.79), channel_id=1, source_target_pairs={{0,1},{1,0},{2,3},{3,2},{4,5},{5,4},{6,7},{7,6},{8,9},{9,8},{10,11... | collective-permute-start | bytes 3145736 | tf_op jit(solution)/shard_map/ppermute | solution.py:503
  123.7 19.2 %collective-permute-start.12 = (bf16[256,1024]{1,0:T(8,128)(2,1)}, bf16[256,1024]{1,0:T(8,128)(2,1)}, u32[]{:S(2)}, u32[]{:S(2)}) collective-permute-start(bf16[256,1024]{1,0:T(8,128)(2,1)} %get-tuple-element.77), channel_id=1, source_target_pairs={{0,2},{2,0},{1,3},{3,1},{4,6},{6,4},{5,7},{7,5},{8,10},{10,8},{9,1... | collective-permute-start | bytes 1572872 | tf_op jit(solution)/shard_map/ppermute | solution.py:502
  125.3 27.9 %collective-permute-start.16 = (bf16[512,1024]{1,0:T(8,128)(2,1)S(1)}, bf16[512,1024]{1,0:T(8,128)(2,1)S(1)}, u32[]{:S(2)}, u32[]{:S(2)}) collective-permute-start(bf16[512,1024]{1,0:T(8,128)(2,1)S(1)} %collective-permute-done.10.refs_1_), channel_id=1, source_target_pairs={{4,0},{8,12},{5,1},{9,13},{6,2},{10,14},{7,3},{11,15},{20,16},{24,... | collective-permute-start | bytes 3145736 | tf_op jit(solution)/shard_map/ppermute | solution.py:504
  134.4 8.5 %copy-start.11 = (bf16[256,1024]{1,0:T(8,128)(2,1)S(1)}, bf16[256,1024]{1,0:T(8,128)(2,1)}, u32[]{:S(2)}) copy-start(bf16[256,1024]{1,0:T(8,128)(2,1)} %get-tuple-element.76) | copy-start | bytes 1572868
  145.0 18.7 %collective-permute-start.14 = (bf16[256,1024]{1,0:T(8,128)(2,1)}, bf16[256,1024]{1,0:T(8,128)(2,1)S(1)}, u32[]{:S(2)}, u32[]{:S(2)}) collective-permute-start(bf16[256,1024]{1,0:T(8,128)(2,1)} %add.28), channel_id=1, source_target_pairs={{4,0},{8,12},{5,1},{9,13},{6,2},{10,14},{7,3},{11,15},{20,16},{24,... | collective-permute-start | bytes 1572872 | tf_op jit(solution)/shard_map/ppermute | solution.py:509
  146.3 17.4 %collective-permute-start.15 = (bf16[256,1024]{1,0:T(8,128)(2,1)}, bf16[256,1024]{1,0:T(8,128)(2,1)}, u32[]{:S(2)}, u32[]{:S(2)}) collective-permute-start(bf16[256,1024]{1,0:T(8,128)(2,1)} %get-tuple-element.85), channel_id=1, source_target_pairs={{0,2},{2,0},{1,3},{3,1},{4,6},{6,4},{5,7},{7,5},{8,10},{10,8},{9,1... | collective-permute-start | bytes 1572872 | tf_op jit(solution)/shard_map/ppermute | solution.py:510
  152.9 11.6 %copy-start.12 = (bf16[256,1024]{1,0:T(8,128)(2,1)S(1)}, bf16[256,1024]{1,0:T(8,128)(2,1)}, u32[]{:S(2)}) copy-start(bf16[256,1024]{1,0:T(8,128)(2,1)} %get-tuple-element.92) | copy-start | bytes 1572868
  153.2 12.5 %copy-start.4 = (bf16[512,1024]{1,0:T(8,128)(2,1)}, bf16[512,1024]{1,0:T(8,128)(2,1)S(1)}, u32[]{:S(2)}) copy-start(bf16[512,1024]{1,0:T(8,128)(2,1)S(1)} %collective-permute-done.16.refs_2_) | copy-start | bytes 3145732
  165.7 10.6 %copy-start.5 = (bf16[256,1024]{1,0:T(8,128)(2,1)}, bf16[256,1024]{1,0:T(8,128)(2,1)S(1)}, u32[]{:S(2)}) copy-start(bf16[256,1024]{1,0:T(8,128)(2,1)S(1)} %add_select_fusion.own) | copy-start | bytes 1572868
  165.7 20.0 %collective-permute-start.18 = (bf16[256,1024]{1,0:T(8,128)(2,1)S(1)}, bf16[256,1024]{1,0:T(8,128)(2,1)S(1)}, u32[]{:S(2)}, u32[]{:S(2)}) collective-permute-start(bf16[256,1024]{1,0:T(8,128)(2,1)S(1)} %add_select_fusion.own), channel_id=1, source_target_pairs={{0,2},{2,0},{1,3},{3,1},{4,6},{6,4},{5,7},{7,5},{8,10},{10,8},{9,1... | collective-permute-start | bytes 1572872 | tf_op jit(solution)/shard_map/ppermute | solution.py:518
  166.3 19.4 %collective-permute-start.19 = (bf16[256,1024]{1,0:T(8,128)(2,1)S(1)}, bf16[256,1024]{1,0:T(8,128)(2,1)S(1)}, u32[]{:S(2)}, u32[]{:S(2)}) collective-permute-start(bf16[256,1024]{1,0:T(8,128)(2,1)S(1)} %add_select_fusion.own), channel_id=1, source_target_pairs={{0,1},{1,0},{2,3},{3,2},{4,5},{5,4},{6,7},{7,6},{8,9},{9,8},{10,11... | collective-permute-start | bytes 1572872 | tf_op jit(solution)/shard_map/ppermute | solution.py:518
  166.3 19.5 %collective-permute-start.17 = (bf16[256,1024]{1,0:T(8,128)(2,1)}, bf16[256,1024]{1,0:T(8,128)(2,1)S(1)}, u32[]{:S(2)}, u32[]{:S(2)}) collective-permute-start(bf16[256,1024]{1,0:T(8,128)(2,1)} %get-tuple-element.91), channel_id=1, source_target_pairs={{4,0},{8,12},{5,1},{9,13},{6,2},{10,14},{7,3},{11,15},{20,16},{24,... | collective-permute-start | bytes 1572872 | tf_op jit(solution)/shard_map/ppermute | solution.py:516
  167.6 18.2 %copy-start.17 = (bf16[256,1024]{1,0:T(8,128)(2,1)S(1)}, bf16[256,1024]{1,0:T(8,128)(2,1)}, u32[]{:S(2)}) copy-start(bf16[256,1024]{1,0:T(8,128)(2,1)} %get-tuple-element.90) | copy-start | bytes 1572868
  185.7 2.0 copy-start.13
  185.7 2.0 copy-start.14
  185.7 2.0 collective-permute-start.20
  187.7 0.8 copy-start.16
Sparse Core Ops, SparseCore 0:
  71.5 21.0 all-gather.6
  123.7 27.7 all-gather.8
  164.6 26.9 all-gather.10

commit v16 on v15

--- a/solution.py
+++ b/solution.py
@@ -301,9 +301,7 @@
         scratch_shapes=[pltpu.VMEM((depth, width), jnp.bfloat16), pltpu.SemaphoreType.DMA],
         compiler_params=pltpu.CompilerParams(vmem_limit_bytes=VMEM_LIMIT),
         cost_estimate=pl.CostEstimate(
-            flops=4 * rows * depth * width,
-            bytes_accessed=depth * width * 2 + rows * (depth + width) * 4,
-            transcendentals=0,
+            flops=rows * depth * width // 2, bytes_accessed=depth * width, transcendentals=0
         ),
         name="project_forward",
     )(place_of, ids_1, ids_3, partial, near_b, end_b, tokens, gathered)
@@ -503,13 +501,15 @@
     own_keep, own_give = add_split(place_of, own_keep, cores(own_give))
     both_3o = along(both_3m, perm=OUTWARD)
     tokens_2 = lax.all_gather(both_2m[:rows] + both_2o[:rows], INNER)
-    grads = line_grads(block_ids, ((tokens_1, upstream_1),), grads, size)
-    end_got, own_give, own_keep, grads = stage((end_got, own_give, own_keep, grads))
+    proj, end_proj = project_forward(place_of, ids_1, ids_3, partial, *last, tokens, tokens_1)
+    end_got, own_give, own_keep, proj, end_proj = stage(
+        (end_got, own_give, own_keep, proj, end_proj)
+    )
 
     sum_out = along(end_keep + end_got, perm=OUTWARD)
     own_got = sideways(own_give)
-    proj, end_proj = project_forward(place_of, ids_1, ids_3, partial, *last, tokens, tokens_1)
-    sum_out, own_got, both_3o, proj, end_proj = stage((sum_out, own_got, both_3o, proj, end_proj))
+    grads = line_grads(block_ids, ((tokens_1, upstream_1),), grads, size)
+    sum_out, own_got, both_3o, grads = stage((sum_out, own_got, both_3o, grads))
 
     tokens_3 = lax.all_gather(both_3m[:rows] + both_3o[:rows], INNER)
     quarter = jnp.where(middle, own_keep + own_got, sum_out)

time: 207 us -> 207 us (level)
    ppermute x1, waiting for transfers between devices: 5.38 us -> 9.69 us  [line_body(): end_got = sideways(end_give)]
    ppermute x1, waiting for transfers between devices: 10.5 us -> 6.24 us  [line_body(): sum_out = along(end_keep + end_got, perm=OUTWARD)]
  transfers between devices with their start and end apart: 24 -> 24, of which waited for: 12 -> 11; matrix products, arithmetic and copies ran while one was open for 5% -> 5% of each run, Pallas kernels for 24% -> 24%
where the time goes in v16:
time: 207 us
  waiting for transfers between devices  84 us (41%)
  Pallas kernels  57.5 us (28%)
  starting transfers between devices  32.1 us (16%)
  between operations  14 us (7%)
  other arithmetic  10.9 us (5%)
  local copies, waits for them, and re-layouts  8.18 us (4%)
    pallas_call x4, Pallas kernels, line_grads(): pl.pallas_call(functools.partial(line_grads_kernel, len(pairs)), out_shap...  31.7 us
    ppermute x1, waiting for transfers between devices, line_body(): both_1 = along(both, perm=PAIRS)  21.7 us
    ppermute x1, waiting for transfers between devices, line_body(): both_2o = along(both_2m, perm=OUTWARD)  13.9 us
    ppermute x1, waiting for transfers between devices, line_body(): near_a = along(mine, perm=INWARD)  11.9 us
    ppermute x1, waiting for transfers between devices, line_body(): end_got = sideways(end_give)  9.69 us
    ppermute x1, waiting for transfers between devices, line_body(): sideways(quarter)  9.46 us
    pallas_call x1, Pallas kernels, place_first(): pl.pallas_call(place_kernel, out_shape=(jax.ShapeDtypeStruct((depth, widt...  8.74 us
    ppermute x1, waiting for transfers between devices, line_body(): near_b = along(other, perm=INWARD)  7.5 us
  transfers between devices with their start and end apart: 24, of which 11 were waited for; matrix products, arithmetic and copies ran while one was open for 5% of the time, Pallas kernels for 24%

profile of v16, /device:TPU:0, one launch (start us, length us, event | category | flops | bytes accessed | tf_op | source)
XLA Modules:
  0.0 206.7 jit_solution(15826431335095345759)
XLA Ops:
  7.2 0.0 all-gather.7.cloned.1.call-start
  7.2 0.7 convert_element_type.26
  7.9 0.1 convert_element_type.27
  8.0 1.3 constant_dynamic-slice_fusion.2
  9.3 1.1 pad_maximum_fusion
  10.4 5.0 %collective-permute-start = (bf16[33,128,128]{2,1,0:T(8,128)(2,1)}, bf16[33,128,128]{2,1,0:T(8,128)(2,1)S(1)}, u32[]{:S(2)}, u32[]{:S(2)}) collective-permute-start(bf16[33,128,128]{2,1,0:T(8,128)(2,1)} %pad_maximum_fusion), channel_id=1, source_target_pairs={{0,4},{12,8},{1,5},{13,9},{2,6},{14,10},{3,7},{15,11},{16,20},{28,... | collective-permute-start | bytes 3244040 | tf_op jit(solution)/shard_map/ppermute | solution.py:463
  15.4 1.7 collective-permute-start.1
  17.0 6.9 %line_grads.4.refs_2_ = bf16[64,128,128]{2,1,0:T(8,128)(2,1)} custom-call(s32[64]{0:T(128)} %ids.7, bf16[256,4096]{1,0:T(8,128)(2,1)} %tokens.1, bf16[256,1024]{1,0:T(8,128)(2,1)} %upstream.1), custom_call_target="tpu_custom_call" | custom-call | flops 536870912 | bytes 4718592 | tf_op jit(solution)/shard_map/line_grads/pallas_call | solution.py:411
  23.9 1.2 constant_dynamic-slice_fusion.1
  25.2 0.1 pad_maximum_fusion.1
  25.3 0.4 copy-done
  25.7 1.2 constant_dynamic-slice_fusion
  26.9 11.9 %collective-permute-done.near_a = bf16[33,128,128]{2,1,0:T(8,128)(2,1)S(1)} collective-permute-done((bf16[33,128,128]{2,1,0:T(8,128)(2,1)}, bf16[33,128,128]{2,1,0:T(8,128)(2,1)S(1)}, u32[]{:S(2)}, u32[]{:S(2)}) %collective-permute-start) | collective-permute-done | bytes 1081376 | tf_op jit(solution)/shard_map/ppermute | solution.py:463
  38.7 1.7 collective-permute-start.3
  40.4 1.5 collective-permute-start.4
  41.9 5.6 %collective-permute-start.2 = (bf16[512,1024]{1,0:T(8,128)(2,1)S(1)}, bf16[512,1024]{1,0:T(8,128)(2,1)S(1)}, u32[]{:S(2)}, u32[]{:S(2)}) collective-permute-start(bf16[512,1024]{1,0:T(8,128)(2,1)S(1)} %pad_maximum_fusion.1), channel_id=1, source_target_pairs={{0,4},{12,8},{4,0},{8,12},{1,5},{13,9},{5,1},{9,13},{2,6},{14,10},... | collective-permute-start | bytes 3145736 | tf_op jit(solution)/shard_map/ppermute | solution.py:473
  47.6 21.7 %collective-permute-done.2 = bf16[512,1024]{1,0:T(8,128)(2,1)S(1)} collective-permute-done((bf16[512,1024]{1,0:T(8,128)(2,1)S(1)}, bf16[512,1024]{1,0:T(8,128)(2,1)S(1)}, u32[]{:S(2)}, u32[]{:S(2)}) %collective-permute-start.2) | collective-permute-done | bytes 1048608 | tf_op jit(solution)/shard_map/ppermute | solution.py:473
  69.3 1.1 copy-done.9
  70.4 1.0 fusion
  71.4 0.0 all-gather.9.cloned.1.call-start
  71.5 0.6 collective-permute-start.6
  72.0 3.7 %collective-permute-start.5 = (bf16[32,128,128]{2,1,0:T(8,128)(2,1)}, bf16[32,128,128]{2,1,0:T(8,128)(2,1)S(1)}, u32[]{:S(2)}, u32[]{:S(2)}) collective-permute-start(bf16[32,128,128]{2,1,0:T(8,128)(2,1)} %constant_dynamic-slice_fusion), channel_id=1, source_target_pairs={{0,4},{12,8},{1,5},{13,9},{2,6},{14,10},{3,7},{15,11},{16,20},{28,... | collective-permute-start | bytes 3145736 | tf_op jit(solution)/shard_map/ppermute | solution.py:477
  75.8 0.7 collective-permute-start.7
  76.5 0.7 pad_add_fusion.place_of
  77.2 1.2 bitcast_convert_fusion
  78.4 1.3 bitcast_convert_fusion.1.ids_3
  79.6 8.7 %place_first.1 = (bf16[4096,1024]{1,0:T(8,128)(2,1)}, bf16[1024,4096]{1,0:T(8,128)(2,1)}) custom-call(s32[4]{0:T(128)} %pad_add_fusion.place_of, s32[64]{0:T(128)} %ids.7, s32[64]{0:T(128)} %get-tuple-element.104.ids_1, s32[64]{0:T(128)} %get-tuple-element.103.ids_2, s32[64]{0:T(128)} %bitcast_convert_fusion.1.ids_3, bf16[64,128,128]{2,1,0:T(8,128)(2,1)} %own.1, ...), custom_call_target="tpu_custom_call" | custom-call | bytes 25165824 | tf_op jit(solution)/shard_map/place_first/pallas_call | solution.py:181
  88.4 7.5 %collective-permute-done.5.near_b = bf16[32,128,128]{2,1,0:T(8,128)(2,1)S(1)} collective-permute-done((bf16[32,128,128]{2,1,0:T(8,128)(2,1)}, bf16[32,128,128]{2,1,0:T(8,128)(2,1)S(1)}, u32[]{:S(2)}, u32[]{:S(2)}) %collective-permute-start.5) | collective-permute-done | bytes 1048608 | tf_op jit(solution)/shard_map/ppermute | solution.py:477
  95.9 0.9 copy-done.8
  96.9 0.7 collective-permute-start.10
  97.6 1.3 collective-permute-start.11
  98.9 3.9 %project_back.1 = (bf16[2,256,1024]{2,1,0:T(8,128)(2,1)}, bf16[2,256,1024]{2,1,0:T(8,128)(2,1)}, bf16[2,256,1024]{2,1,0:T(8,128)(2,1)}, bf16[256,1024]{1,0:T(8,128)(2,1)}, bf16[256,1024]{1,0:T(8,128)(2,1)}) custom-call(s32[4]{0:T(128)} %pad_add_fusion.place_of, s32[64]{0:T(128)} %get-tuple-element.104.ids_1, s32[64]{0:T(128)} %bitcast_convert_fusion.1.ids_3, ...), custom_call_target="tpu_custom_call" | custom-call | flops 4294967296 | bytes 13631488 | tf_op jit(solution)/shard_map/project_back/pallas_call | solution.py:239
  102.7 0.1 collective-permute-start.8
  102.8 0.5 collective-permute-start.9
  103.3 1.6 collective-permute-done.8.refs_0_
  104.9 0.9 collective-permute-done.9.refs_1_
  105.8 3.0 %add_split.2 = (bf16[256,1024]{1,0:T(8,128)(2,1)}, bf16[256,1024]{1,0:T(8,128)(2,1)}) custom-call(s32[4]{0:T(128)} %pad_add_fusion.place_of, bf16[2,256,1024]{2,1,0:T(8,128)(2,1)} %get-tuple-element.68.keep, bf16[256,1024]{1,0:T(8,128)(2,1)} %copy-done.15, bf16[256,1024]{1,0:T(8,128)(2,1)} %collective-permute-done.9.refs_1_), custom_call_target="tpu_custom_call" | custom-call | flops 524288 | bytes 3145728 | tf_op jit(solution)/shard_map/add_split/pallas_call | solution.py:328
  108.8 13.9 %collective-permute-done.11.refs_2_ = bf16[512,1024]{1,0:T(8,128)(2,1)S(1)} collective-permute-done((bf16[512,1024]{1,0:T(8,128)(2,1)S(1)}, bf16[512,1024]{1,0:T(8,128)(2,1)S(1)}, u32[]{:S(2)}, u32[]{:S(2)}) %collective-permute-start.11) | collective-permute-done | bytes 1048608 | tf_op jit(solution)/shard_map/ppermute | solution.py:490
  122.7 0.9 slice_add_fusion.1
  123.7 0.0 all-gather.11.cloned.1.call-start
  123.8 0.1 collective-permute-start.13
  123.8 1.6 collective-permute-start.12
  125.4 1.3 collective-permute-start.17
  126.7 3.9 %project_forward.1 = (bf16[256,1024]{1,0:T(8,128)(2,1)}, bf16[256,1024]{1,0:T(8,128)(2,1)}) custom-call(s32[4]{0:T(128)} %pad_add_fusion.place_of, s32[64]{0:T(128)} %get-tuple-element.104.ids_1, s32[64]{0:T(128)} %bitcast_convert_fusion.1.ids_3, bf16[4096,1024]{1,0:T(8,128)(2,1)} %get-tuple-element.81.partial, bf16[32,128,128]{2,1,0:T(8,128)(2,1)} %copy-done.8, ...), custom_call_target="tpu_custom_call" | custom-call | flops 536870912 | bytes 4194304 | tf_op jit(solution)/shard_map/project_forward/pallas_call | solution.py:296
  130.6 3.3 %add_split.3 = (bf16[256,1024]{1,0:T(8,128)(2,1)}, bf16[256,1024]{1,0:T(8,128)(2,1)}) custom-call(s32[4]{0:T(128)} %pad_add_fusion.place_of, bf16[2,256,1024]{2,1,0:T(8,128)(2,1)} %get-tuple-element.77.keep, bf16[2,256,1024]{2,1,0:T(8,128)(2,1)} %collective-permute-done.13.refs_0_), custom_call_target="tpu_custom_call" | custom-call | flops 524288 | bytes 3145728 | tf_op jit(solution)/shard_map/add_split/pallas_call | solution.py:328
  133.9 9.7 %collective-permute-done.12 = bf16[256,1024]{1,0:T(8,128)(2,1)} collective-permute-done((bf16[256,1024]{1,0:T(8,128)(2,1)}, bf16[256,1024]{1,0:T(8,128)(2,1)}, u32[]{:S(2)}, u32[]{:S(2)}) %collective-permute-start.12) | collective-permute-done | bytes 524320 | tf_op jit(solution)/shard_map/ppermute | solution.py:500
  143.6 2.0 add.28
  145.6 1.5 collective-permute-start.15
  147.1 2.5 %collective-permute-start.16 = (bf16[256,1024]{1,0:T(8,128)(2,1)}, bf16[256,1024]{1,0:T(8,128)(2,1)}, u32[]{:S(2)}, u32[]{:S(2)}) collective-permute-start(bf16[256,1024]{1,0:T(8,128)(2,1)} %get-tuple-element.90), channel_id=1, source_target_pairs={{0,2},{2,0},{1,3},{3,1},{4,6},{6,4},{5,7},{7,5},{8,10},{10,8},{9,1... | collective-permute-start | bytes 1572872 | tf_op jit(solution)/shard_map/ppermute | solution.py:510
  149.6 7.9 %line_grads.5.refs_3_ = bf16[64,128,128]{2,1,0:T(8,128)(2,1)} custom-call(s32[64]{0:T(128)} %ids.7, bf16[4,256,1024]{2,1,0:T(8,128)(2,1)} %bitcast.17, bf16[256,1024]{1,0:T(8,128)(2,1)} %get-tuple-element.101.end_upstream.refs_1_, bf16[64,128,128]{2,1,0:T(8,128)(2,1)} %line_grads.4.refs_2_), custom_call_target="tpu_custom_call" | custom-call | flops 536870912 | bytes 6815744 | tf_op jit(solution)/shard_map/line_grads/pallas_call | solution.py:411
  157.5 6.2 %collective-permute-done.15 = bf16[256,1024]{1,0:T(8,128)(2,1)S(1)} collective-permute-done((bf16[256,1024]{1,0:T(8,128)(2,1)}, bf16[256,1024]{1,0:T(8,128)(2,1)S(1)}, u32[]{:S(2)}, u32[]{:S(2)}) %collective-permute-start.15) | collective-permute-done | bytes 524320 | tf_op jit(solution)/shard_map/ppermute | solution.py:509
  163.7 0.9 slice_add_fusion
  164.6 1.1 add_select_fusion.own
  165.8 0.6 collective-permute-start.18
  166.4 1.3 collective-permute-start.14
  167.7 8.6 %line_grads.6.refs_3_ = bf16[64,128,128]{2,1,0:T(8,128)(2,1)} custom-call(s32[64]{0:T(128)} %ids.7, bf16[4,256,1024]{2,1,0:T(8,128)(2,1)} %bitcast.18, bf16[512,1024]{1,0:T(8,128)(2,1)} %copy-done.1, bf16[512,1024]{1,0:T(8,128)(2,1)} %copy-done.3, bf16[64,128,128]{2,1,0:T(8,128)(2,1)} %line_grads.5.refs_3_), custom_call_target="tpu_custom_call" | custom-call | flops 536870912 | bytes 8388608 | tf_op jit(solution)/shard_map/line_grads/pallas_call | solution.py:411
  176.3 9.5 %collective-permute-done.18.by_tensor = bf16[256,1024]{1,0:T(8,128)(2,1)S(1)} collective-permute-done((bf16[256,1024]{1,0:T(8,128)(2,1)S(1)}, bf16[256,1024]{1,0:T(8,128)(2,1)S(1)}, u32[]{:S(2)}, u32[]{:S(2)}) %collective-permute-start.18) | collective-permute-done | bytes 524320 | tf_op jit(solution)/shard_map/ppermute | solution.py:518
  185.8 0.1 collective-permute-start.20
  185.9 1.0 broadcast_select_fusion
  186.9 0.9 collective-permute-done.20.by_both
  187.8 0.9 copy-done.16
  188.6 3.0 %assemble.1 = bf16[256,4096]{1,0:T(8,128)(2,1)} custom-call(s32[4]{0:T(128)} %pad_add_fusion.place_of, bf16[256,1024]{1,0:T(8,128)(2,1)} %copy-done.5, bf16[256,1024]{1,0:T(8,128)(2,1)} %copy-done.14, bf16[256,1024]{1,0:T(8,128)(2,1)} %copy-done.13, bf16[256,1024]{1,0:T(8,128)(2,1)} %copy-done.16), custom_call_target="tpu_custom_call" | custom-call | bytes 4194304 | tf_op jit(solution)/shard_map/assemble/pallas_call | solution.py:353
  191.6 0.1 all-gather.11.cloned.1.call-done
  191.8 8.4 %line_grads.7 = bf16[64,128,128]{2,1,0:T(8,128)(2,1)} custom-call(s32[64]{0:T(128)} %ids.7, bf16[4,256,1024]{2,1,0:T(8,128)(2,1)} %bitcast.19, bf16[512,1024]{1,0:T(8,128)(2,1)} %copy-done.2, bf16[512,1024]{1,0:T(8,128)(2,1)} %copy-done.4, bf16[64,128,128]{2,1,0:T(8,128)(2,1)} %line_grads.6.refs_3_), custom_call_target="tpu_custom_call" | custom-call | flops 536870912 | bytes 8388608 | tf_op jit(solution)/shard_map/line_grads/pallas_call | solution.py:411
  (51 shorter events, 0.2 us)
Async XLA Ops:
  7.2 88.8 %all-gather.7.cloned.1.call-start = ((), (), s32[]{:S(2)}) async-start(), calls=%async_computation | async-start | bytes 2621440 | tf_op jit(solution)/shard_map/all_gather | solution.py:480
  10.4 28.3 %collective-permute-start = (bf16[33,128,128]{2,1,0:T(8,128)(2,1)}, bf16[33,128,128]{2,1,0:T(8,128)(2,1)S(1)}, u32[]{:S(2)}, u32[]{:S(2)}) collective-permute-start(bf16[33,128,128]{2,1,0:T(8,128)(2,1)} %pad_maximum_fusion), channel_id=1, source_target_pairs={{0,4},{12,8},{1,5},{13,9},{2,6},{14,10},{3,7},{15,11},{16,20},{28,... | collective-permute-start | bytes 3244040 | tf_op jit(solution)/shard_map/ppermute | solution.py:463
  15.4 23.4 %collective-permute-start.1 = (bf16[33,128,128]{2,1,0:T(8,128)(2,1)}, bf16[33,128,128]{2,1,0:T(8,128)(2,1)}, u32[]{:S(2)}, u32[]{:S(2)}) collective-permute-start(bf16[33,128,128]{2,1,0:T(8,128)(2,1)} %pad_maximum_fusion), channel_id=1, source_target_pairs={{4,8},{8,4},{5,9},{9,5},{6,10},{10,6},{7,11},{11,7},{20,24},{24,20... | collective-permute-start | bytes 3244040 | tf_op jit(solution)/shard_map/ppermute | solution.py:464
  17.0 8.1 %copy-start.6 = (bf16[256,1024]{1,0:T(8,128)(2,1)S(1)}, bf16[256,1024]{1,0:T(8,128)(2,1)}, u32[]{:S(2)}) copy-start(bf16[256,1024]{1,0:T(8,128)(2,1)} %upstream.1) | copy-start | bytes 1572868
  23.9 1.8 copy-start
  25.7 45.7 %copy-start.10 = (bf16[512,1024]{1,0:T(8,128)(2,1)}, bf16[512,1024]{1,0:T(8,128)(2,1)S(1)}, u32[]{:S(2)}) copy-start(bf16[512,1024]{1,0:T(8,128)(2,1)S(1)} %pad_maximum_fusion.1) | copy-start | bytes 3145732
  38.7 40.9 %copy-start.7 = (bf16[33,128,128]{2,1,0:T(8,128)(2,1)}, bf16[33,128,128]{2,1,0:T(8,128)(2,1)S(1)}, u32[]{:S(2)}) copy-start(bf16[33,128,128]{2,1,0:T(8,128)(2,1)S(1)} %collective-permute-done.near_a) | copy-start | bytes 3244036
  38.7 30.6 %collective-permute-start.3 = (bf16[33,128,128]{2,1,0:T(8,128)(2,1)S(1)}, bf16[33,128,128]{2,1,0:T(8,128)(2,1)}, u32[]{:S(2)}, u32[]{:S(2)}) collective-permute-start(bf16[33,128,128]{2,1,0:T(8,128)(2,1)S(1)} %collective-permute-done.near_a), channel_id=1, source_target_pairs={{4,8},{8,4},{5,9},{9,5},{6,10},{10,6},{7,11},{11,7},{20,24},{24,20... | collective-permute-start | bytes 3244040 | tf_op jit(solution)/shard_map/ppermute | solution.py:471
  40.4 28.9 %collective-permute-start.4 = (bf16[33,128,128]{2,1,0:T(8,128)(2,1)}, bf16[33,128,128]{2,1,0:T(8,128)(2,1)}, u32[]{:S(2)}, u32[]{:S(2)}) collective-permute-start(bf16[33,128,128]{2,1,0:T(8,128)(2,1)} %collective-permute-done.1.far_a), channel_id=1, source_target_pairs={{0,16},{16,0},{1,17},{17,1},{2,18},{18,2},{3,19},{19,3},{4,20},{20... | collective-permute-start | bytes 3244040 | tf_op jit(solution)/shard_map/ppermute | solution.py:472
  41.9 27.4 %collective-permute-start.2 = (bf16[512,1024]{1,0:T(8,128)(2,1)S(1)}, bf16[512,1024]{1,0:T(8,128)(2,1)S(1)}, u32[]{:S(2)}, u32[]{:S(2)}) collective-permute-start(bf16[512,1024]{1,0:T(8,128)(2,1)S(1)} %pad_maximum_fusion.1), channel_id=1, source_target_pairs={{0,4},{12,8},{4,0},{8,12},{1,5},{13,9},{5,1},{9,13},{2,6},{14,10},... | collective-permute-start | bytes 3145736 | tf_op jit(solution)/shard_map/ppermute | solution.py:473
  69.3 1.1 copy-start.9
  71.4 96.3 %all-gather.9.cloned.1.call-start = ((), (), s32[]{:S(2)}) async-start(), calls=%async_computation.1 | async-start | bytes 2621440 | tf_op jit(solution)/shard_map/all_gather | solution.py:503
  71.5 24.4 %collective-permute-start.6 = (bf16[33,128,128]{2,1,0:T(8,128)(2,1)}, bf16[33,128,128]{2,1,0:T(8,128)(2,1)}, u32[]{:S(2)}, u32[]{:S(2)}) collective-permute-start(bf16[33,128,128]{2,1,0:T(8,128)(2,1)} %collective-permute-done.3.end_a), channel_id=1, source_target_pairs={{0,16},{16,0},{1,17},{17,1},{2,18},{18,2},{3,19},{19,3},{4,20},{20... | collective-permute-start | bytes 3244040 | tf_op jit(solution)/shard_map/ppermute | solution.py:478
  72.0 23.8 %collective-permute-start.5 = (bf16[32,128,128]{2,1,0:T(8,128)(2,1)}, bf16[32,128,128]{2,1,0:T(8,128)(2,1)S(1)}, u32[]{:S(2)}, u32[]{:S(2)}) collective-permute-start(bf16[32,128,128]{2,1,0:T(8,128)(2,1)} %constant_dynamic-slice_fusion), channel_id=1, source_target_pairs={{0,4},{12,8},{1,5},{13,9},{2,6},{14,10},{3,7},{15,11},{16,20},{28,... | collective-permute-start | bytes 3145736 | tf_op jit(solution)/shard_map/ppermute | solution.py:477
  75.8 20.1 %collective-permute-start.7 = (bf16[512,1024]{1,0:T(8,128)(2,1)}, bf16[512,1024]{1,0:T(8,128)(2,1)S(1)}, u32[]{:S(2)}, u32[]{:S(2)}) collective-permute-start(bf16[512,1024]{1,0:T(8,128)(2,1)} %copy-done.10), channel_id=1, source_target_pairs={{4,8},{8,4},{5,9},{9,5},{6,10},{10,6},{7,11},{11,7},{20,24},{24,20... | collective-permute-start | bytes 3145736 | tf_op jit(solution)/shard_map/ppermute | solution.py:479
  95.9 1.0 copy-start.8
  95.9 26.9 %copy-start.1 = (bf16[512,1024]{1,0:T(8,128)(2,1)}, bf16[512,1024]{1,0:T(8,128)(2,1)S(1)}, u32[]{:S(2)}) copy-start(bf16[512,1024]{1,0:T(8,128)(2,1)S(1)} %collective-permute-done.7.refs_1_) | copy-start | bytes 3145732
  96.9 12.0 %collective-permute-start.10 = (bf16[512,1024]{1,0:T(8,128)(2,1)}, bf16[512,1024]{1,0:T(8,128)(2,1)S(1)}, u32[]{:S(2)}, u32[]{:S(2)}) collective-permute-start(bf16[512,1024]{1,0:T(8,128)(2,1)} %copy-done.9), channel_id=1, source_target_pairs={{4,8},{8,4},{5,9},{9,5},{6,10},{10,6},{7,11},{11,7},{20,24},{24,20... | collective-permute-start | bytes 3145736 | tf_op jit(solution)/shard_map/ppermute | solution.py:489
  97.6 25.2 %collective-permute-start.11 = (bf16[512,1024]{1,0:T(8,128)(2,1)S(1)}, bf16[512,1024]{1,0:T(8,128)(2,1)S(1)}, u32[]{:S(2)}, u32[]{:S(2)}) collective-permute-start(bf16[512,1024]{1,0:T(8,128)(2,1)S(1)} %collective-permute-done.7.refs_1_), channel_id=1, source_target_pairs={{4,0},{8,12},{5,1},{9,13},{6,2},{10,14},{7,3},{11,15},{20,16},{24,... | collective-permute-start | bytes 3145736 | tf_op jit(solution)/shard_map/ppermute | solution.py:490
  102.7 2.2 %collective-permute-start.8 = (bf16[256,1024]{1,0:T(8,128)(2,1)}, bf16[256,1024]{1,0:T(8,128)(2,1)S(1)}, u32[]{:S(2)}, u32[]{:S(2)}) collective-permute-start(bf16[256,1024]{1,0:T(8,128)(2,1)} %get-tuple-element.69), channel_id=1, source_target_pairs={{0,1},{1,0},{2,3},{3,2},{4,5},{5,4},{6,7},{7,6},{8,9},{9,8},{10,11... | collective-permute-start | bytes 1572872 | tf_op jit(solution)/shard_map/ppermute | solution.py:495
  102.8 3.0 %collective-permute-start.9 = (bf16[256,1024]{1,0:T(8,128)(2,1)}, bf16[256,1024]{1,0:T(8,128)(2,1)}, u32[]{:S(2)}, u32[]{:S(2)}) collective-permute-start(bf16[256,1024]{1,0:T(8,128)(2,1)} %get-tuple-element.70), channel_id=1, source_target_pairs={{0,1},{1,0},{2,3},{3,2},{4,5},{5,4},{6,7},{7,6},{8,9},{9,8},{10,11... | collective-permute-start | bytes 1572872 | tf_op jit(solution)/shard_map/ppermute | solution.py:495
  104.9 0.9 copy-start.15
  108.8 54.9 %copy-start.2 = (bf16[512,1024]{1,0:T(8,128)(2,1)}, bf16[512,1024]{1,0:T(8,128)(2,1)S(1)}, u32[]{:S(2)}) copy-start(bf16[512,1024]{1,0:T(8,128)(2,1)S(1)} %collective-permute-done.10.refs_1_) | copy-start | bytes 3145732
  122.7 7.8 %copy-start.3 = (bf16[512,1024]{1,0:T(8,128)(2,1)}, bf16[512,1024]{1,0:T(8,128)(2,1)S(1)}, u32[]{:S(2)}) copy-start(bf16[512,1024]{1,0:T(8,128)(2,1)S(1)} %collective-permute-done.11.refs_2_) | copy-start | bytes 3145732
  123.7 68.1 %all-gather.11.cloned.1.call-start = ((), (), s32[]{:S(2)}) async-start(), calls=%async_computation.2 | async-start | bytes 2621440 | tf_op jit(solution)/shard_map/all_gather | solution.py:514
  123.8 6.8 %collective-permute-start.13 = (bf16[2,256,1024]{2,1,0:T(8,128)(2,1)}, bf16[2,256,1024]{2,1,0:T(8,128)(2,1)}, u32[]{:S(2)}, u32[]{:S(2)}) collective-permute-start(bf16[2,256,1024]{2,1,0:T(8,128)(2,1)} %get-tuple-element.78), channel_id=1, source_target_pairs={{0,1},{1,0},{2,3},{3,2},{4,5},{5,4},{6,7},{7,6},{8,9},{9,8},{10,11... | collective-permute-start | bytes 3145736 | tf_op jit(solution)/shard_map/ppermute | solution.py:501
  123.8 19.7 %collective-permute-start.12 = (bf16[256,1024]{1,0:T(8,128)(2,1)}, bf16[256,1024]{1,0:T(8,128)(2,1)}, u32[]{:S(2)}, u32[]{:S(2)}) collective-permute-start(bf16[256,1024]{1,0:T(8,128)(2,1)} %get-tuple-element.76), channel_id=1, source_target_pairs={{0,2},{2,0},{1,3},{3,1},{4,6},{6,4},{5,7},{7,5},{8,10},{10,8},{9,1... | collective-permute-start | bytes 1572872 | tf_op jit(solution)/shard_map/ppermute | solution.py:500
  125.4 32.1 %collective-permute-start.17 = (bf16[512,1024]{1,0:T(8,128)(2,1)S(1)}, bf16[512,1024]{1,0:T(8,128)(2,1)S(1)}, u32[]{:S(2)}, u32[]{:S(2)}) collective-permute-start(bf16[512,1024]{1,0:T(8,128)(2,1)S(1)} %collective-permute-done.10.refs_1_), channel_id=1, source_target_pairs={{4,0},{8,12},{5,1},{9,13},{6,2},{10,14},{7,3},{11,15},{20,16},{24,... | collective-permute-start | bytes 3145736 | tf_op jit(solution)/shard_map/ppermute | solution.py:502
  130.6 13.0 %copy-start.11 = (bf16[256,1024]{1,0:T(8,128)(2,1)S(1)}, bf16[256,1024]{1,0:T(8,128)(2,1)}, u32[]{:S(2)}) copy-start(bf16[256,1024]{1,0:T(8,128)(2,1)} %get-tuple-element.88) | copy-start | bytes 1572868
  145.6 18.1 %collective-permute-start.15 = (bf16[256,1024]{1,0:T(8,128)(2,1)}, bf16[256,1024]{1,0:T(8,128)(2,1)S(1)}, u32[]{:S(2)}, u32[]{:S(2)}) collective-permute-start(bf16[256,1024]{1,0:T(8,128)(2,1)} %add.28), channel_id=1, source_target_pairs={{4,0},{8,12},{5,1},{9,13},{6,2},{10,14},{7,3},{11,15},{20,16},{24,... | collective-permute-start | bytes 1572872 | tf_op jit(solution)/shard_map/ppermute | solution.py:509
  147.1 16.7 %collective-permute-start.16 = (bf16[256,1024]{1,0:T(8,128)(2,1)}, bf16[256,1024]{1,0:T(8,128)(2,1)}, u32[]{:S(2)}, u32[]{:S(2)}) collective-permute-start(bf16[256,1024]{1,0:T(8,128)(2,1)} %get-tuple-element.90), channel_id=1, source_target_pairs={{0,2},{2,0},{1,3},{3,1},{4,6},{6,4},{5,7},{7,5},{8,10},{10,8},{9,1... | collective-permute-start | bytes 1572872 | tf_op jit(solution)/shard_map/ppermute | solution.py:510
  157.5 7.1 %copy-start.12 = (bf16[256,1024]{1,0:T(8,128)(2,1)S(1)}, bf16[256,1024]{1,0:T(8,128)(2,1)}, u32[]{:S(2)}) copy-start(bf16[256,1024]{1,0:T(8,128)(2,1)} %get-tuple-element.87) | copy-start | bytes 1572868
  157.5 8.3 %copy-start.4 = (bf16[512,1024]{1,0:T(8,128)(2,1)}, bf16[512,1024]{1,0:T(8,128)(2,1)S(1)}, u32[]{:S(2)}) copy-start(bf16[512,1024]{1,0:T(8,128)(2,1)S(1)} %collective-permute-done.17.refs_2_) | copy-start | bytes 3145732
  165.8 10.6 %copy-start.5 = (bf16[256,1024]{1,0:T(8,128)(2,1)}, bf16[256,1024]{1,0:T(8,128)(2,1)S(1)}, u32[]{:S(2)}) copy-start(bf16[256,1024]{1,0:T(8,128)(2,1)S(1)} %add_select_fusion.own) | copy-start | bytes 1572868
  165.8 20.0 %collective-permute-start.18 = (bf16[256,1024]{1,0:T(8,128)(2,1)S(1)}, bf16[256,1024]{1,0:T(8,128)(2,1)S(1)}, u32[]{:S(2)}, u32[]{:S(2)}) collective-permute-start(bf16[256,1024]{1,0:T(8,128)(2,1)S(1)} %add_select_fusion.own), channel_id=1, source_target_pairs={{0,2},{2,0},{1,3},{3,1},{4,6},{6,4},{5,7},{7,5},{8,10},{10,8},{9,1... | collective-permute-start | bytes 1572872 | tf_op jit(solution)/shard_map/ppermute | solution.py:518
  166.4 19.4 %collective-permute-start.19 = (bf16[256,1024]{1,0:T(8,128)(2,1)S(1)}, bf16[256,1024]{1,0:T(8,128)(2,1)S(1)}, u32[]{:S(2)}, u32[]{:S(2)}) collective-permute-start(bf16[256,1024]{1,0:T(8,128)(2,1)S(1)} %add_select_fusion.own), channel_id=1, source_target_pairs={{0,1},{1,0},{2,3},{3,2},{4,5},{5,4},{6,7},{7,6},{8,9},{9,8},{10,11... | collective-permute-start | bytes 1572872 | tf_op jit(solution)/shard_map/ppermute | solution.py:518
  166.4 19.5 %collective-permute-start.14 = (bf16[256,1024]{1,0:T(8,128)(2,1)}, bf16[256,1024]{1,0:T(8,128)(2,1)S(1)}, u32[]{:S(2)}, u32[]{:S(2)}) collective-permute-start(bf16[256,1024]{1,0:T(8,128)(2,1)} %get-tuple-element.86), channel_id=1, source_target_pairs={{4,0},{8,12},{5,1},{9,13},{6,2},{10,14},{7,3},{11,15},{20,16},{24,... | collective-permute-start | bytes 1572872 | tf_op jit(solution)/shard_map/ppermute | solution.py:516
  167.7 18.2 %copy-start.17 = (bf16[256,1024]{1,0:T(8,128)(2,1)S(1)}, bf16[256,1024]{1,0:T(8,128)(2,1)}, u32[]{:S(2)}) copy-start(bf16[256,1024]{1,0:T(8,128)(2,1)} %get-tuple-element.85) | copy-start | bytes 1572868
  185.8 2.0 copy-start.13
  185.8 2.0 copy-start.14
  185.8 2.0 collective-permute-start.20
  187.8 0.9 copy-start.16
Sparse Core Ops, SparseCore 0:
  71.5 21.0 all-gather.6
  123.8 27.3 all-gather.8
  164.7 26.9 all-gather.10

commit v17 on v16

--- a/solution.py
+++ b/solution.py
@@ -508,10 +508,11 @@
 
     sum_out = along(end_keep + end_got, perm=OUTWARD)
     own_got = sideways(own_give)
+    part_3, upstream_1 = stage((both_3m[:rows] + both_3o[:rows], upstream_1))
+    tokens_3 = lax.all_gather(part_3, INNER)
     grads = line_grads(block_ids, ((tokens_1, upstream_1),), grads, size)
-    sum_out, own_got, both_3o, grads = stage((sum_out, own_got, both_3o, grads))
-
-    tokens_3 = lax.all_gather(both_3m[:rows] + both_3o[:rows], INNER)
+    sum_out, own_got, grads = stage((sum_out, own_got, grads))
+
     quarter = jnp.where(middle, own_keep + own_got, sum_out)
     proj_out = along(end_proj, perm=OUTWARD)
     grads = line_grads(block_ids, ((tokens_2, both_2m, both_2o),), grads, size)

time: 207 us -> 226 us (1.092)
  waiting for transfers between devices: 84 us -> 105 us
  other arithmetic: 10.9 us -> 7.92 us
    ppermute x1, waiting for transfers between devices: 0.01 us -> 24.7 us  [line_body(): both_3o = along(both_3m, perm=OUTWARD)]
    ppermute x1, waiting for transfers between devices: 9.46 us -> 1.81 us  [line_body(): sideways(quarter)]
    ppermute x1, waiting for transfers between devices: 0.01 us -> 4.57 us  [line_body(): proj_out = along(end_proj, perm=OUTWARD)]
    ppermute x1, waiting for transfers between devices: 6.24 us -> 2.69 us  [line_body(): sum_out = along(end_keep + end_got, perm=OUTWARD)]
  transfers between devices with their start and end apart: 24 -> 24, of which waited for: 11 -> 12; matrix products, arithmetic and copies ran while one was open for 5% -> 3% of each run, Pallas kernels for 24% -> 22%
where the time goes in v17:
time: 226 us
  waiting for transfers between devices  105 us (46%)
  Pallas kernels  57.3 us (25%)
  starting transfers between devices  33.6 us (15%)
  between operations  14 us (6%)
  local copies, waits for them, and re-layouts  8.11 us (4%)
  other arithmetic  7.92 us (4%)
    pallas_call x4, Pallas kernels, line_grads(): pl.pallas_call(functools.partial(line_grads_kernel, len(pairs)), out_shap...  31.5 us
    ppermute x1, waiting for transfers between devices, line_body(): both_3o = along(both_3m, perm=OUTWARD)  24.7 us
    ppermute x1, waiting for transfers between devices, line_body(): both_1 = along(both, perm=PAIRS)  21.7 us
    ppermute x1, waiting for transfers between devices, line_body(): both_2o = along(both_2m, perm=OUTWARD)  13.9 us
    ppermute x1, waiting for transfers between devices, line_body(): near_a = along(mine, perm=INWARD)  11.9 us
    ppermute x1, waiting for transfers between devices, line_body(): end_got = sideways(end_give)  10.9 us
    pallas_call x1, Pallas kernels, place_first(): pl.pallas_call(place_kernel, out_shape=(jax.ShapeDtypeStruct((depth, widt...  8.73 us
    ppermute x1, waiting for transfers between devices, line_body(): near_b = along(other, perm=INWARD)  7.54 us
  transfers between devices with their start and end apart: 24, of which 12 were waited for; matrix products, arithmetic and copies ran while one was open for 3% of the time, Pallas kernels for 22%

profile of v17, /device:TPU:0, one launch (start us, length us, event | category | flops | bytes accessed | tf_op | source)
XLA Modules:
  0.0 225.6 jit_solution(14975457762202994278)
XLA Ops:
  7.2 0.7 convert_element_type.26
  7.9 0.1 convert_element_type.27
  8.0 1.3 constant_dynamic-slice_fusion.2
  9.3 1.1 pad_maximum_fusion
  10.4 5.0 %collective-permute-start = (bf16[33,128,128]{2,1,0:T(8,128)(2,1)}, bf16[33,128,128]{2,1,0:T(8,128)(2,1)S(1)}, u32[]{:S(2)}, u32[]{:S(2)}) collective-permute-start(bf16[33,128,128]{2,1,0:T(8,128)(2,1)} %pad_maximum_fusion), channel_id=1, source_target_pairs={{0,4},{12,8},{1,5},{13,9},{2,6},{14,10},{3,7},{15,11},{16,20},{28,... | collective-permute-start | bytes 3244040 | tf_op jit(solution)/shard_map/ppermute | solution.py:463
  15.4 1.7 collective-permute-start.1
  17.0 6.9 %line_grads.4.refs_2_ = bf16[64,128,128]{2,1,0:T(8,128)(2,1)} custom-call(s32[64]{0:T(128)} %ids.7, bf16[256,4096]{1,0:T(8,128)(2,1)} %tokens.1, bf16[256,1024]{1,0:T(8,128)(2,1)} %upstream.1), custom_call_target="tpu_custom_call" | custom-call | flops 536870912 | bytes 4718592 | tf_op jit(solution)/shard_map/line_grads/pallas_call | solution.py:411
  23.9 1.2 constant_dynamic-slice_fusion.1
  25.2 0.1 pad_maximum_fusion.1
  25.3 0.4 copy-done
  25.7 1.2 constant_dynamic-slice_fusion
  26.9 11.9 %collective-permute-done.near_a = bf16[33,128,128]{2,1,0:T(8,128)(2,1)S(1)} collective-permute-done((bf16[33,128,128]{2,1,0:T(8,128)(2,1)}, bf16[33,128,128]{2,1,0:T(8,128)(2,1)S(1)}, u32[]{:S(2)}, u32[]{:S(2)}) %collective-permute-start) | collective-permute-done | bytes 1081376 | tf_op jit(solution)/shard_map/ppermute | solution.py:463
  38.7 1.7 collective-permute-start.3
  40.4 1.5 collective-permute-start.4
  41.9 5.7 %collective-permute-start.2 = (bf16[512,1024]{1,0:T(8,128)(2,1)S(1)}, bf16[512,1024]{1,0:T(8,128)(2,1)S(1)}, u32[]{:S(2)}, u32[]{:S(2)}) collective-permute-start(bf16[512,1024]{1,0:T(8,128)(2,1)S(1)} %pad_maximum_fusion.1), channel_id=1, source_target_pairs={{0,4},{12,8},{4,0},{8,12},{1,5},{13,9},{5,1},{9,13},{2,6},{14,10},... | collective-permute-start | bytes 3145736 | tf_op jit(solution)/shard_map/ppermute | solution.py:473
  47.6 21.7 %collective-permute-done.2 = bf16[512,1024]{1,0:T(8,128)(2,1)S(1)} collective-permute-done((bf16[512,1024]{1,0:T(8,128)(2,1)S(1)}, bf16[512,1024]{1,0:T(8,128)(2,1)S(1)}, u32[]{:S(2)}, u32[]{:S(2)}) %collective-permute-start.2) | collective-permute-done | bytes 1048608 | tf_op jit(solution)/shard_map/ppermute | solution.py:473
  69.3 1.0 copy-done.9
  70.4 1.0 fusion
  71.4 0.0 all-gather.9.cloned.1.call-start
  71.5 0.6 collective-permute-start.6
  72.0 3.7 %collective-permute-start.5 = (bf16[32,128,128]{2,1,0:T(8,128)(2,1)}, bf16[32,128,128]{2,1,0:T(8,128)(2,1)S(1)}, u32[]{:S(2)}, u32[]{:S(2)}) collective-permute-start(bf16[32,128,128]{2,1,0:T(8,128)(2,1)} %constant_dynamic-slice_fusion), channel_id=1, source_target_pairs={{0,4},{12,8},{1,5},{13,9},{2,6},{14,10},{3,7},{15,11},{16,20},{28,... | collective-permute-start | bytes 3145736 | tf_op jit(solution)/shard_map/ppermute | solution.py:477
  75.7 0.7 collective-permute-start.7
  76.5 0.6 pad_add_fusion.place_of
  77.1 1.3 bitcast_convert_fusion
  78.4 1.2 bitcast_convert_fusion.1.ids_3
  79.6 8.7 %place_first.1 = (bf16[4096,1024]{1,0:T(8,128)(2,1)}, bf16[1024,4096]{1,0:T(8,128)(2,1)}) custom-call(s32[4]{0:T(128)} %pad_add_fusion.place_of, s32[64]{0:T(128)} %ids.7, s32[64]{0:T(128)} %get-tuple-element.106.ids_1, s32[64]{0:T(128)} %get-tuple-element.105.ids_2, s32[64]{0:T(128)} %bitcast_convert_fusion.1.ids_3, bf16[64,128,128]{2,1,0:T(8,128)(2,1)} %own.1, ...), custom_call_target="tpu_custom_call" | custom-call | bytes 25165824 | tf_op jit(solution)/shard_map/place_first/pallas_call | solution.py:181
  88.3 7.5 %collective-permute-done.5.near_b = bf16[32,128,128]{2,1,0:T(8,128)(2,1)S(1)} collective-permute-done((bf16[32,128,128]{2,1,0:T(8,128)(2,1)}, bf16[32,128,128]{2,1,0:T(8,128)(2,1)S(1)}, u32[]{:S(2)}, u32[]{:S(2)}) %collective-permute-start.5) | collective-permute-done | bytes 1048608 | tf_op jit(solution)/shard_map/ppermute | solution.py:477
  95.9 0.9 copy-done.8
  96.8 0.7 collective-permute-start.10
  97.5 1.3 collective-permute-start.11
  98.8 3.8 %project_back.1 = (bf16[2,256,1024]{2,1,0:T(8,128)(2,1)}, bf16[2,256,1024]{2,1,0:T(8,128)(2,1)}, bf16[2,256,1024]{2,1,0:T(8,128)(2,1)}, bf16[256,1024]{1,0:T(8,128)(2,1)}, bf16[256,1024]{1,0:T(8,128)(2,1)}) custom-call(s32[4]{0:T(128)} %pad_add_fusion.place_of, s32[64]{0:T(128)} %get-tuple-element.106.ids_1, s32[64]{0:T(128)} %bitcast_convert_fusion.1.ids_3, ...), custom_call_target="tpu_custom_call" | custom-call | flops 4294967296 | bytes 13631488 | tf_op jit(solution)/shard_map/project_back/pallas_call | solution.py:239
  102.7 0.1 collective-permute-start.8
  102.8 0.5 collective-permute-start.9
  103.3 1.6 collective-permute-done.8.refs_0_
  104.9 0.9 collective-permute-done.9.refs_1_
  105.8 3.0 %add_split.2 = (bf16[256,1024]{1,0:T(8,128)(2,1)}, bf16[256,1024]{1,0:T(8,128)(2,1)}) custom-call(s32[4]{0:T(128)} %pad_add_fusion.place_of, bf16[2,256,1024]{2,1,0:T(8,128)(2,1)} %get-tuple-element.69.keep, bf16[256,1024]{1,0:T(8,128)(2,1)} %copy-done.15, bf16[256,1024]{1,0:T(8,128)(2,1)} %collective-permute-done.9.refs_1_), custom_call_target="tpu_custom_call" | custom-call | flops 524288 | bytes 3145728 | tf_op jit(solution)/shard_map/add_split/pallas_call | solution.py:328
  108.8 13.9 %collective-permute-done.11.refs_2_ = bf16[512,1024]{1,0:T(8,128)(2,1)S(1)} collective-permute-done((bf16[512,1024]{1,0:T(8,128)(2,1)S(1)}, bf16[512,1024]{1,0:T(8,128)(2,1)S(1)}, u32[]{:S(2)}, u32[]{:S(2)}) %collective-permute-start.11) | collective-permute-done | bytes 1048608 | tf_op jit(solution)/shard_map/ppermute | solution.py:490
  122.7 1.0 slice_add_fusion.1
  123.7 0.0 all-gather.11.cloned.1.call-start
  123.8 1.3 collective-permute-start.17
  125.1 24.7 %collective-permute-done.17.refs_2_ = bf16[512,1024]{1,0:T(8,128)(2,1)S(1)} collective-permute-done((bf16[512,1024]{1,0:T(8,128)(2,1)S(1)}, bf16[512,1024]{1,0:T(8,128)(2,1)S(1)}, u32[]{:S(2)}, u32[]{:S(2)}) %collective-permute-start.17) | collective-permute-done | bytes 1048608 | tf_op jit(solution)/shard_map/ppermute | solution.py:502
  149.8 0.9 slice_add_fusion
  150.8 0.1 collective-permute-start.13
  150.8 1.9 collective-permute-start.12
  152.7 3.9 %project_forward.1 = (bf16[256,1024]{1,0:T(8,128)(2,1)}, bf16[256,1024]{1,0:T(8,128)(2,1)}) custom-call(s32[4]{0:T(128)} %pad_add_fusion.place_of, s32[64]{0:T(128)} %get-tuple-element.106.ids_1, s32[64]{0:T(128)} %bitcast_convert_fusion.1.ids_3, bf16[4096,1024]{1,0:T(8,128)(2,1)} %get-tuple-element.82.partial, bf16[32,128,128]{2,1,0:T(8,128)(2,1)} %copy-done.8, ...), custom_call_target="tpu_custom_call" | custom-call | flops 536870912 | bytes 4194304 | tf_op jit(solution)/shard_map/project_forward/pallas_call | solution.py:296
  156.7 3.3 %add_split.3 = (bf16[256,1024]{1,0:T(8,128)(2,1)}, bf16[256,1024]{1,0:T(8,128)(2,1)}) custom-call(s32[4]{0:T(128)} %pad_add_fusion.place_of, bf16[2,256,1024]{2,1,0:T(8,128)(2,1)} %get-tuple-element.78.keep, bf16[2,256,1024]{2,1,0:T(8,128)(2,1)} %collective-permute-done.13.refs_0_), custom_call_target="tpu_custom_call" | custom-call | flops 524288 | bytes 3145728 | tf_op jit(solution)/shard_map/add_split/pallas_call | solution.py:328
  159.9 10.9 %collective-permute-done.12 = bf16[256,1024]{1,0:T(8,128)(2,1)S(1)} collective-permute-done((bf16[256,1024]{1,0:T(8,128)(2,1)}, bf16[256,1024]{1,0:T(8,128)(2,1)S(1)}, u32[]{:S(2)}, u32[]{:S(2)}) %collective-permute-start.12) | collective-permute-done | bytes 524320 | tf_op jit(solution)/shard_map/ppermute | solution.py:500
  170.9 0.2 add.28
  171.1 1.6 collective-permute-start.15
  172.7 2.4 %collective-permute-start.16 = (bf16[256,1024]{1,0:T(8,128)(2,1)}, bf16[256,1024]{1,0:T(8,128)(2,1)S(1)}, u32[]{:S(2)}, u32[]{:S(2)}) collective-permute-start(bf16[256,1024]{1,0:T(8,128)(2,1)} %get-tuple-element.91), channel_id=1, source_target_pairs={{0,2},{2,0},{1,3},{3,1},{4,6},{6,4},{5,7},{7,5},{8,10},{10,8},{9,1... | collective-permute-start | bytes 1572872 | tf_op jit(solution)/shard_map/ppermute | solution.py:510
  175.1 7.9 %line_grads.5.refs_3_ = bf16[64,128,128]{2,1,0:T(8,128)(2,1)} custom-call(s32[64]{0:T(128)} %ids.7, bf16[4,256,1024]{2,1,0:T(8,128)(2,1)} %bitcast.17, bf16[256,1024]{1,0:T(8,128)(2,1)} %get-tuple-element.93.end_upstream.refs_1_, bf16[64,128,128]{2,1,0:T(8,128)(2,1)} %line_grads.4.refs_2_), custom_call_target="tpu_custom_call" | custom-call | flops 536870912 | bytes 6815744 | tf_op jit(solution)/shard_map/line_grads/pallas_call | solution.py:411
  183.0 2.7 %collective-permute-done.15 = bf16[256,1024]{1,0:T(8,128)(2,1)S(1)} collective-permute-done((bf16[256,1024]{1,0:T(8,128)(2,1)S(1)}, bf16[256,1024]{1,0:T(8,128)(2,1)S(1)}, u32[]{:S(2)}, u32[]{:S(2)}) %collective-permute-start.15) | collective-permute-done | bytes 524320 | tf_op jit(solution)/shard_map/ppermute | solution.py:509
  185.7 2.2 collective-permute-done.16
  187.9 0.1 add_select_fusion.own
  188.0 1.8 collective-permute-start.18
  189.8 1.3 collective-permute-start.14
  191.2 8.4 %line_grads.6.refs_3_ = bf16[64,128,128]{2,1,0:T(8,128)(2,1)} custom-call(s32[64]{0:T(128)} %ids.7, bf16[4,256,1024]{2,1,0:T(8,128)(2,1)} %bitcast.19, bf16[512,1024]{1,0:T(8,128)(2,1)} %copy-done.1, bf16[512,1024]{1,0:T(8,128)(2,1)} %copy-done.3, bf16[64,128,128]{2,1,0:T(8,128)(2,1)} %line_grads.5.refs_3_), custom_call_target="tpu_custom_call" | custom-call | flops 536870912 | bytes 8388608 | tf_op jit(solution)/shard_map/line_grads/pallas_call | solution.py:411
  199.6 1.8 collective-permute-done.18.by_tensor
  201.4 0.1 collective-permute-start.20
  201.5 4.6 %collective-permute-done.14 = bf16[256,1024]{1,0:T(8,128)(2,1)S(1)} collective-permute-done((bf16[256,1024]{1,0:T(8,128)(2,1)S(1)}, bf16[256,1024]{1,0:T(8,128)(2,1)S(1)}, u32[]{:S(2)}, u32[]{:S(2)}) %collective-permute-start.14) | collective-permute-done | bytes 524320 | tf_op jit(solution)/shard_map/ppermute | solution.py:517
  206.0 0.8 broadcast_select_fusion
  206.9 0.8 copy-done.16
  207.7 3.0 %assemble.1 = bf16[256,4096]{1,0:T(8,128)(2,1)} custom-call(s32[4]{0:T(128)} %pad_add_fusion.place_of, bf16[256,1024]{1,0:T(8,128)(2,1)} %copy-done.5, bf16[256,1024]{1,0:T(8,128)(2,1)} %copy-done.13, bf16[256,1024]{1,0:T(8,128)(2,1)} %copy-done.12, bf16[256,1024]{1,0:T(8,128)(2,1)} %copy-done.16), custom_call_target="tpu_custom_call" | custom-call | bytes 4194304 | tf_op jit(solution)/shard_map/assemble/pallas_call | solution.py:353
  210.7 8.4 %line_grads.7 = bf16[64,128,128]{2,1,0:T(8,128)(2,1)} custom-call(s32[64]{0:T(128)} %ids.7, bf16[4,256,1024]{2,1,0:T(8,128)(2,1)} %bitcast.18, bf16[512,1024]{1,0:T(8,128)(2,1)} %copy-done.2, bf16[512,1024]{1,0:T(8,128)(2,1)} %copy-done.4, bf16[64,128,128]{2,1,0:T(8,128)(2,1)} %line_grads.6.refs_3_), custom_call_target="tpu_custom_call" | custom-call | flops 536870912 | bytes 8388608 | tf_op jit(solution)/shard_map/line_grads/pallas_call | solution.py:411
  (53 shorter events, 0.2 us)
Async XLA Ops:
  7.2 88.7 %all-gather.7.cloned.1.call-start = ((), (), s32[]{:S(2)}) async-start(), calls=%async_computation | async-start | bytes 2621440 | tf_op jit(solution)/shard_map/all_gather | solution.py:480
  10.4 28.3 %collective-permute-start = (bf16[33,128,128]{2,1,0:T(8,128)(2,1)}, bf16[33,128,128]{2,1,0:T(8,128)(2,1)S(1)}, u32[]{:S(2)}, u32[]{:S(2)}) collective-permute-start(bf16[33,128,128]{2,1,0:T(8,128)(2,1)} %pad_maximum_fusion), channel_id=1, source_target_pairs={{0,4},{12,8},{1,5},{13,9},{2,6},{14,10},{3,7},{15,11},{16,20},{28,... | collective-permute-start | bytes 3244040 | tf_op jit(solution)/shard_map/ppermute | solution.py:463
  15.4 23.4 %collective-permute-start.1 = (bf16[33,128,128]{2,1,0:T(8,128)(2,1)}, bf16[33,128,128]{2,1,0:T(8,128)(2,1)}, u32[]{:S(2)}, u32[]{:S(2)}) collective-permute-start(bf16[33,128,128]{2,1,0:T(8,128)(2,1)} %pad_maximum_fusion), channel_id=1, source_target_pairs={{4,8},{8,4},{5,9},{9,5},{6,10},{10,6},{7,11},{11,7},{20,24},{24,20... | collective-permute-start | bytes 3244040 | tf_op jit(solution)/shard_map/ppermute | solution.py:464
  17.0 8.1 %copy-start.6 = (bf16[256,1024]{1,0:T(8,128)(2,1)S(1)}, bf16[256,1024]{1,0:T(8,128)(2,1)}, u32[]{:S(2)}) copy-start(bf16[256,1024]{1,0:T(8,128)(2,1)} %upstream.1) | copy-start | bytes 1572868
  23.9 1.8 copy-start
  25.7 45.7 %copy-start.10 = (bf16[512,1024]{1,0:T(8,128)(2,1)}, bf16[512,1024]{1,0:T(8,128)(2,1)S(1)}, u32[]{:S(2)}) copy-start(bf16[512,1024]{1,0:T(8,128)(2,1)S(1)} %pad_maximum_fusion.1) | copy-start | bytes 3145732
  38.7 40.9 %copy-start.7 = (bf16[33,128,128]{2,1,0:T(8,128)(2,1)}, bf16[33,128,128]{2,1,0:T(8,128)(2,1)S(1)}, u32[]{:S(2)}) copy-start(bf16[33,128,128]{2,1,0:T(8,128)(2,1)S(1)} %collective-permute-done.near_a) | copy-start | bytes 3244036
  38.7 30.6 %collective-permute-start.3 = (bf16[33,128,128]{2,1,0:T(8,128)(2,1)S(1)}, bf16[33,128,128]{2,1,0:T(8,128)(2,1)}, u32[]{:S(2)}, u32[]{:S(2)}) collective-permute-start(bf16[33,128,128]{2,1,0:T(8,128)(2,1)S(1)} %collective-permute-done.near_a), channel_id=1, source_target_pairs={{4,8},{8,4},{5,9},{9,5},{6,10},{10,6},{7,11},{11,7},{20,24},{24,20... | collective-permute-start | bytes 3244040 | tf_op jit(solution)/shard_map/ppermute | solution.py:471
  40.4 28.9 %collective-permute-start.4 = (bf16[33,128,128]{2,1,0:T(8,128)(2,1)}, bf16[33,128,128]{2,1,0:T(8,128)(2,1)}, u32[]{:S(2)}, u32[]{:S(2)}) collective-permute-start(bf16[33,128,128]{2,1,0:T(8,128)(2,1)} %collective-permute-done.1.far_a), channel_id=1, source_target_pairs={{0,16},{16,0},{1,17},{17,1},{2,18},{18,2},{3,19},{19,3},{4,20},{20... | collective-permute-start | bytes 3244040 | tf_op jit(solution)/shard_map/ppermute | solution.py:472
  41.9 27.4 %collective-permute-start.2 = (bf16[512,1024]{1,0:T(8,128)(2,1)S(1)}, bf16[512,1024]{1,0:T(8,128)(2,1)S(1)}, u32[]{:S(2)}, u32[]{:S(2)}) collective-permute-start(bf16[512,1024]{1,0:T(8,128)(2,1)S(1)} %pad_maximum_fusion.1), channel_id=1, source_target_pairs={{0,4},{12,8},{4,0},{8,12},{1,5},{13,9},{5,1},{9,13},{2,6},{14,10},... | collective-permute-start | bytes 3145736 | tf_op jit(solution)/shard_map/ppermute | solution.py:473
  69.3 1.0 copy-start.9
  71.4 119.7 %all-gather.9.cloned.1.call-start = ((), (), s32[]{:S(2)}) async-start(), calls=%async_computation.1 | async-start | bytes 2621440 | tf_op jit(solution)/shard_map/all_gather | solution.py:503
  71.5 24.4 %collective-permute-start.6 = (bf16[33,128,128]{2,1,0:T(8,128)(2,1)}, bf16[33,128,128]{2,1,0:T(8,128)(2,1)}, u32[]{:S(2)}, u32[]{:S(2)}) collective-permute-start(bf16[33,128,128]{2,1,0:T(8,128)(2,1)} %collective-permute-done.3.end_a), channel_id=1, source_target_pairs={{0,16},{16,0},{1,17},{17,1},{2,18},{18,2},{3,19},{19,3},{4,20},{20... | collective-permute-start | bytes 3244040 | tf_op jit(solution)/shard_map/ppermute | solution.py:478
  72.0 23.8 %collective-permute-start.5 = (bf16[32,128,128]{2,1,0:T(8,128)(2,1)}, bf16[32,128,128]{2,1,0:T(8,128)(2,1)S(1)}, u32[]{:S(2)}, u32[]{:S(2)}) collective-permute-start(bf16[32,128,128]{2,1,0:T(8,128)(2,1)} %constant_dynamic-slice_fusion), channel_id=1, source_target_pairs={{0,4},{12,8},{1,5},{13,9},{2,6},{14,10},{3,7},{15,11},{16,20},{28,... | collective-permute-start | bytes 3145736 | tf_op jit(solution)/shard_map/ppermute | solution.py:477
  75.7 20.1 %collective-permute-start.7 = (bf16[512,1024]{1,0:T(8,128)(2,1)}, bf16[512,1024]{1,0:T(8,128)(2,1)S(1)}, u32[]{:S(2)}, u32[]{:S(2)}) collective-permute-start(bf16[512,1024]{1,0:T(8,128)(2,1)} %copy-done.10), channel_id=1, source_target_pairs={{4,8},{8,4},{5,9},{9,5},{6,10},{10,6},{7,11},{11,7},{20,24},{24,20... | collective-permute-start | bytes 3145736 | tf_op jit(solution)/shard_map/ppermute | solution.py:479
  95.9 1.0 copy-start.8
  95.9 26.9 %copy-start.1 = (bf16[512,1024]{1,0:T(8,128)(2,1)}, bf16[512,1024]{1,0:T(8,128)(2,1)S(1)}, u32[]{:S(2)}) copy-start(bf16[512,1024]{1,0:T(8,128)(2,1)S(1)} %collective-permute-done.7.refs_1_) | copy-start | bytes 3145732
  96.8 12.0 %collective-permute-start.10 = (bf16[512,1024]{1,0:T(8,128)(2,1)}, bf16[512,1024]{1,0:T(8,128)(2,1)S(1)}, u32[]{:S(2)}, u32[]{:S(2)}) collective-permute-start(bf16[512,1024]{1,0:T(8,128)(2,1)} %copy-done.9), channel_id=1, source_target_pairs={{4,8},{8,4},{5,9},{9,5},{6,10},{10,6},{7,11},{11,7},{20,24},{24,20... | collective-permute-start | bytes 3145736 | tf_op jit(solution)/shard_map/ppermute | solution.py:489
  97.5 25.2 %collective-permute-start.11 = (bf16[512,1024]{1,0:T(8,128)(2,1)S(1)}, bf16[512,1024]{1,0:T(8,128)(2,1)S(1)}, u32[]{:S(2)}, u32[]{:S(2)}) collective-permute-start(bf16[512,1024]{1,0:T(8,128)(2,1)S(1)} %collective-permute-done.7.refs_1_), channel_id=1, source_target_pairs={{4,0},{8,12},{5,1},{9,13},{6,2},{10,14},{7,3},{11,15},{20,16},{24,... | collective-permute-start | bytes 3145736 | tf_op jit(solution)/shard_map/ppermute | solution.py:490
  102.7 2.2 collective-permute-start.8
  102.8 3.0 %collective-permute-start.9 = (bf16[256,1024]{1,0:T(8,128)(2,1)}, bf16[256,1024]{1,0:T(8,128)(2,1)}, u32[]{:S(2)}, u32[]{:S(2)}) collective-permute-start(bf16[256,1024]{1,0:T(8,128)(2,1)} %get-tuple-element.71), channel_id=1, source_target_pairs={{0,1},{1,0},{2,3},{3,2},{4,5},{5,4},{6,7},{7,6},{8,9},{9,8},{10,11... | collective-permute-start | bytes 1572872 | tf_op jit(solution)/shard_map/ppermute | solution.py:495
  104.9 0.9 copy-start.15
  108.8 41.9 %copy-start.2 = (bf16[512,1024]{1,0:T(8,128)(2,1)}, bf16[512,1024]{1,0:T(8,128)(2,1)S(1)}, u32[]{:S(2)}) copy-start(bf16[512,1024]{1,0:T(8,128)(2,1)S(1)} %collective-permute-done.10.refs_1_) | copy-start | bytes 3145732
  122.7 28.0 %copy-start.3 = (bf16[512,1024]{1,0:T(8,128)(2,1)}, bf16[512,1024]{1,0:T(8,128)(2,1)S(1)}, u32[]{:S(2)}) copy-start(bf16[512,1024]{1,0:T(8,128)(2,1)S(1)} %collective-permute-done.11.refs_2_) | copy-start | bytes 3145732
  123.7 87.0 %all-gather.11.cloned.1.call-start = ((), (), s32[]{:S(2)}) async-start(), calls=%async_computation.2 | async-start | bytes 2621440 | tf_op jit(solution)/shard_map/all_gather | solution.py:512
  123.8 26.0 %collective-permute-start.17 = (bf16[512,1024]{1,0:T(8,128)(2,1)S(1)}, bf16[512,1024]{1,0:T(8,128)(2,1)S(1)}, u32[]{:S(2)}, u32[]{:S(2)}) collective-permute-start(bf16[512,1024]{1,0:T(8,128)(2,1)S(1)} %collective-permute-done.10.refs_1_), channel_id=1, source_target_pairs={{4,0},{8,12},{5,1},{9,13},{6,2},{10,14},{7,3},{11,15},{20,16},{24,... | collective-permute-start | bytes 3145736 | tf_op jit(solution)/shard_map/ppermute | solution.py:502
  149.8 6.8 %copy-start.4 = (bf16[512,1024]{1,0:T(8,128)(2,1)}, bf16[512,1024]{1,0:T(8,128)(2,1)S(1)}, u32[]{:S(2)}) copy-start(bf16[512,1024]{1,0:T(8,128)(2,1)S(1)} %collective-permute-done.17.refs_2_) | copy-start | bytes 3145732
  150.8 5.9 %collective-permute-start.13 = (bf16[2,256,1024]{2,1,0:T(8,128)(2,1)}, bf16[2,256,1024]{2,1,0:T(8,128)(2,1)}, u32[]{:S(2)}, u32[]{:S(2)}) collective-permute-start(bf16[2,256,1024]{2,1,0:T(8,128)(2,1)} %get-tuple-element.79), channel_id=1, source_target_pairs={{0,1},{1,0},{2,3},{3,2},{4,5},{5,4},{6,7},{7,6},{8,9},{9,8},{10,11... | collective-permute-start | bytes 3145736 | tf_op jit(solution)/shard_map/ppermute | solution.py:501
  150.8 20.0 %collective-permute-start.12 = (bf16[256,1024]{1,0:T(8,128)(2,1)}, bf16[256,1024]{1,0:T(8,128)(2,1)S(1)}, u32[]{:S(2)}, u32[]{:S(2)}) collective-permute-start(bf16[256,1024]{1,0:T(8,128)(2,1)} %get-tuple-element.77), channel_id=1, source_target_pairs={{0,2},{2,0},{1,3},{3,1},{4,6},{6,4},{5,7},{7,5},{8,10},{10,8},{9,1... | collective-permute-start | bytes 1572872 | tf_op jit(solution)/shard_map/ppermute | solution.py:500
  156.7 14.2 %copy-start.11 = (bf16[256,1024]{1,0:T(8,128)(2,1)S(1)}, bf16[256,1024]{1,0:T(8,128)(2,1)}, u32[]{:S(2)}) copy-start(bf16[256,1024]{1,0:T(8,128)(2,1)} %get-tuple-element.89) | copy-start | bytes 1572868
  171.1 16.8 %copy-start.14 = (bf16[256,1024]{1,0:T(8,128)(2,1)S(1)}, bf16[256,1024]{1,0:T(8,128)(2,1)}, u32[]{:S(2)}) copy-start(bf16[256,1024]{1,0:T(8,128)(2,1)} %get-tuple-element.88) | copy-start | bytes 1572868
  171.1 14.6 %collective-permute-start.15 = (bf16[256,1024]{1,0:T(8,128)(2,1)S(1)}, bf16[256,1024]{1,0:T(8,128)(2,1)S(1)}, u32[]{:S(2)}, u32[]{:S(2)}) collective-permute-start(bf16[256,1024]{1,0:T(8,128)(2,1)S(1)} %add.28), channel_id=1, source_target_pairs={{4,0},{8,12},{5,1},{9,13},{6,2},{10,14},{7,3},{11,15},{20,16},{24,... | collective-permute-start | bytes 1572872 | tf_op jit(solution)/shard_map/ppermute | solution.py:509
  172.7 15.2 %collective-permute-start.16 = (bf16[256,1024]{1,0:T(8,128)(2,1)}, bf16[256,1024]{1,0:T(8,128)(2,1)S(1)}, u32[]{:S(2)}, u32[]{:S(2)}) collective-permute-start(bf16[256,1024]{1,0:T(8,128)(2,1)} %get-tuple-element.91), channel_id=1, source_target_pairs={{0,2},{2,0},{1,3},{3,1},{4,6},{6,4},{5,7},{7,5},{8,10},{10,8},{9,1... | collective-permute-start | bytes 1572872 | tf_op jit(solution)/shard_map/ppermute | solution.py:510
  183.0 6.8 %copy-start.18 = (bf16[256,1024]{1,0:T(8,128)(2,1)S(1)}, bf16[256,1024]{1,0:T(8,128)(2,1)}, u32[]{:S(2)}) copy-start(bf16[256,1024]{1,0:T(8,128)(2,1)} %get-tuple-element.87) | copy-start | bytes 1572868
  188.0 11.6 %copy-start.5 = (bf16[256,1024]{1,0:T(8,128)(2,1)}, bf16[256,1024]{1,0:T(8,128)(2,1)S(1)}, u32[]{:S(2)}) copy-start(bf16[256,1024]{1,0:T(8,128)(2,1)S(1)} %add_select_fusion.own) | copy-start | bytes 1572868
  188.0 13.4 %collective-permute-start.18 = (bf16[256,1024]{1,0:T(8,128)(2,1)S(1)}, bf16[256,1024]{1,0:T(8,128)(2,1)S(1)}, u32[]{:S(2)}, u32[]{:S(2)}) collective-permute-start(bf16[256,1024]{1,0:T(8,128)(2,1)S(1)} %add_select_fusion.own), channel_id=1, source_target_pairs={{0,2},{2,0},{1,3},{3,1},{4,6},{6,4},{5,7},{7,5},{8,10},{10,8},{9,1... | collective-permute-start | bytes 1572872 | tf_op jit(solution)/shard_map/ppermute | solution.py:519
  189.8 11.6 %collective-permute-start.19 = (bf16[256,1024]{1,0:T(8,128)(2,1)S(1)}, bf16[256,1024]{1,0:T(8,128)(2,1)S(1)}, u32[]{:S(2)}, u32[]{:S(2)}) collective-permute-start(bf16[256,1024]{1,0:T(8,128)(2,1)S(1)} %add_select_fusion.own), channel_id=1, source_target_pairs={{0,1},{1,0},{2,3},{3,2},{4,5},{5,4},{6,7},{7,6},{8,9},{9,8},{10,11... | collective-permute-start | bytes 1572872 | tf_op jit(solution)/shard_map/ppermute | solution.py:519
  189.8 16.2 %collective-permute-start.14 = (bf16[256,1024]{1,0:T(8,128)(2,1)S(1)}, bf16[256,1024]{1,0:T(8,128)(2,1)S(1)}, u32[]{:S(2)}, u32[]{:S(2)}) collective-permute-start(bf16[256,1024]{1,0:T(8,128)(2,1)S(1)} %copy-done.18), channel_id=1, source_target_pairs={{4,0},{8,12},{5,1},{9,13},{6,2},{10,14},{7,3},{11,15},{20,16},{24,... | collective-permute-start | bytes 1572872 | tf_op jit(solution)/shard_map/ppermute | solution.py:517
  191.1 14.9 %copy-start.17 = (bf16[256,1024]{1,0:T(8,128)(2,1)S(1)}, bf16[256,1024]{1,0:T(8,128)(2,1)}, u32[]{:S(2)}) copy-start(bf16[256,1024]{1,0:T(8,128)(2,1)} %get-tuple-element.86) | copy-start | bytes 1572868
  201.4 5.5 %copy-start.12 = (bf16[256,1024]{1,0:T(8,128)(2,1)}, bf16[256,1024]{1,0:T(8,128)(2,1)S(1)}, u32[]{:S(2)}) copy-start(bf16[256,1024]{1,0:T(8,128)(2,1)S(1)} %collective-permute-done.18.by_tensor) | copy-start | bytes 1572868
  201.4 5.5 %copy-start.13 = (bf16[256,1024]{1,0:T(8,128)(2,1)}, bf16[256,1024]{1,0:T(8,128)(2,1)S(1)}, u32[]{:S(2)}) copy-start(bf16[256,1024]{1,0:T(8,128)(2,1)S(1)} %collective-permute-done.19.by_core) | copy-start | bytes 1572868
  201.4 5.5 %collective-permute-start.20 = (bf16[256,1024]{1,0:T(8,128)(2,1)S(1)}, bf16[256,1024]{1,0:T(8,128)(2,1)S(1)}, u32[]{:S(2)}, u32[]{:S(2)}) collective-permute-start(bf16[256,1024]{1,0:T(8,128)(2,1)S(1)} %collective-permute-done.18.by_tensor), channel_id=1, source_target_pairs={{0,1},{1,0},{2,3},{3,2},{4,5},{5,4},{6,7},{7,6},{8,9},{9,8},{10,11... | collective-permute-start | bytes 1572872 | tf_op jit(solution)/shard_map/ppermute | solution.py:520
  206.9 0.8 copy-start.16
Sparse Core Ops, SparseCore 0:
  71.5 21.0 all-gather.6
  123.8 22.8 all-gather.8
  150.9 28.3 all-gather.10

commit v18 on v17

--- a/solution.py
+++ b/solution.py
@@ -371,7 +371,7 @@
         if d.shape[0] > x.shape[-2]:
             rows, other = x.shape[-2], refs.pop(0)
             total_d = refs.pop()
-            total_d[...] = d[rows:] + other[rows:]
+            total_d[...] = d[rows:] + other[other.shape[0] - rows :]
             d = total_d
         pairs.append((x, d))
     start = refs.pop(0) if len(refs) == 2 else None
@@ -499,17 +499,17 @@
 
     end_got = sideways(end_give)
     own_keep, own_give = add_split(place_of, own_keep, cores(own_give))
-    both_3o = along(both_3m, perm=OUTWARD)
+    part_3o = along(both_3m[:rows], perm=OUTWARD)
     tokens_2 = lax.all_gather(both_2m[:rows] + both_2o[:rows], INNER)
     proj, end_proj = project_forward(place_of, ids_1, ids_3, partial, *last, tokens, tokens_1)
-    end_got, own_give, own_keep, proj, end_proj = stage(
-        (end_got, own_give, own_keep, proj, end_proj)
+    end_got, own_give, own_keep, part_3o, proj, end_proj = stage(
+        (end_got, own_give, own_keep, part_3o, proj, end_proj)
     )
 
     sum_out = along(end_keep + end_got, perm=OUTWARD)
     own_got = sideways(own_give)
-    part_3, upstream_1 = stage((both_3m[:rows] + both_3o[:rows], upstream_1))
-    tokens_3 = lax.all_gather(part_3, INNER)
+    tokens_3 = lax.all_gather(both_3m[:rows] + part_3o, INNER)
+    upstream_3o = along(both_3m[rows:], perm=OUTWARD)
     grads = line_grads(block_ids, ((tokens_1, upstream_1),), grads, size)
     sum_out, own_got, grads = stage((sum_out, own_got, grads))
 
@@ -520,7 +520,7 @@
     by_both = cores(by_tensor)
     projected = jnp.where(middle, proj, proj_out)
     token_grad = assemble(place_of, (quarter, by_core, by_tensor, by_both))
-    grads = line_grads(block_ids, ((tokens_3, both_3m, both_3o),), grads, size)
+    grads = line_grads(block_ids, ((tokens_3, both_3m, upstream_3o),), grads, size)
     return projected, token_grad, grads
 
 

time: 226 us -> 223 us (0.987)
  waiting for transfers between devices: 105 us -> 94.8 us
  local copies, waits for them, and re-layouts: 8.11 us -> 10.7 us
    ppermute x1 -> x2, waiting for transfers between devices: 24.7 us -> 13.2 us  [the longest x1 7.57 us: line_body(): upstream_3o = along(both_3m[rows:], perm=OUTWARD)]
    ppermute x1, waiting for transfers between devices: 1.81 us -> 8.57 us  [line_body(): sideways(quarter)]
    ppermute x1, waiting for transfers between devices: 10.9 us -> 6.49 us  [line_body(): end_got = sideways(end_give)]
    unnamed x38 -> x42, local copies, waits for them, and re-layouts: 3.27 us -> 5.01 us
  transfers between devices with their start and end apart: 24 -> 25, of which waited for: 12 -> 13; matrix products, arithmetic and copies ran while one was open for 3% -> 5% of each run, Pallas kernels for 22% -> 22%
where the time goes in v18:
time: 223 us; the launch traced here: 222 us
  waiting for transfers between devices  94.8 us (43%)
  Pallas kernels  57.1 us (26%)
  starting transfers between devices  35.3 us (16%)
  between operations  14.1 us (6%)
  local copies, waits for them, and re-layouts  10.7 us (5%)
  other arithmetic  10.1 us (5%)
    pallas_call x4, Pallas kernels, line_grads(): pl.pallas_call(functools.partial(line_grads_kernel, len(pairs)), out_shap...  31.4 us
    ppermute x1, waiting for transfers between devices, line_body(): both_1 = along(both, perm=PAIRS)  21.7 us
    ppermute x1, waiting for transfers between devices, line_body(): both_2o = along(both_2m, perm=OUTWARD)  13.9 us
    ppermute x1, waiting for transfers between devices, line_body(): near_a = along(mine, perm=INWARD)  11.9 us
    pallas_call x1, Pallas kernels, place_first(): pl.pallas_call(place_kernel, out_shape=(jax.ShapeDtypeStruct((depth, widt...  8.75 us
    ppermute x1, waiting for transfers between devices, line_body(): sideways(quarter)  8.57 us
    ppermute x1, waiting for transfers between devices, line_body(): near_b = along(other, perm=INWARD)  7.6 us
    ppermute x1, waiting for transfers between devices, line_body(): upstream_3o = along(both_3m[rows:], perm=OUTWARD)  7.57 us
  transfers between devices with their start and end apart: 25, of which 13 were waited for; matrix products, arithmetic and copies ran while one was open for 5% of the time, Pallas kernels for 22%

profile of v18, /device:TPU:0, one launch (start us, length us, event | category | flops | bytes accessed | tf_op | source)
XLA Modules:
  0.0 222.0 jit_solution(1895198736539847358)
XLA Ops:
  7.2 0.7 convert_element_type.26
  7.9 0.1 convert_element_type.27
  8.0 1.3 constant_dynamic-slice_fusion.2
  9.3 1.1 pad_maximum_fusion
  10.4 5.0 %collective-permute-start = (bf16[33,128,128]{2,1,0:T(8,128)(2,1)}, bf16[33,128,128]{2,1,0:T(8,128)(2,1)S(1)}, u32[]{:S(2)}, u32[]{:S(2)}) collective-permute-start(bf16[33,128,128]{2,1,0:T(8,128)(2,1)} %pad_maximum_fusion), channel_id=1, source_target_pairs={{0,4},{12,8},{1,5},{13,9},{2,6},{14,10},{3,7},{15,11},{16,20},{28,... | collective-permute-start | bytes 3244040 | tf_op jit(solution)/shard_map/ppermute | solution.py:463
  15.4 1.7 collective-permute-start.1
  17.0 6.9 %line_grads.4.refs_2_ = bf16[64,128,128]{2,1,0:T(8,128)(2,1)} custom-call(s32[64]{0:T(128)} %ids.7, bf16[256,4096]{1,0:T(8,128)(2,1)} %tokens.1, bf16[256,1024]{1,0:T(8,128)(2,1)} %upstream.1), custom_call_target="tpu_custom_call" | custom-call | flops 536870912 | bytes 4718592 | tf_op jit(solution)/shard_map/line_grads/pallas_call | solution.py:411
  23.9 1.2 constant_dynamic-slice_fusion.1
  25.2 0.1 pad_maximum_fusion.1
  25.3 0.4 copy-done
  25.7 1.2 constant_dynamic-slice_fusion
  26.9 11.9 %collective-permute-done.near_a = bf16[33,128,128]{2,1,0:T(8,128)(2,1)S(1)} collective-permute-done((bf16[33,128,128]{2,1,0:T(8,128)(2,1)}, bf16[33,128,128]{2,1,0:T(8,128)(2,1)S(1)}, u32[]{:S(2)}, u32[]{:S(2)}) %collective-permute-start) | collective-permute-done | bytes 1081376 | tf_op jit(solution)/shard_map/ppermute | solution.py:463
  38.7 1.7 collective-permute-start.3
  40.4 1.5 collective-permute-start.4
  41.9 5.7 %collective-permute-start.2 = (bf16[512,1024]{1,0:T(8,128)(2,1)S(1)}, bf16[512,1024]{1,0:T(8,128)(2,1)S(1)}, u32[]{:S(2)}, u32[]{:S(2)}) collective-permute-start(bf16[512,1024]{1,0:T(8,128)(2,1)S(1)} %pad_maximum_fusion.1), channel_id=1, source_target_pairs={{0,4},{12,8},{4,0},{8,12},{1,5},{13,9},{5,1},{9,13},{2,6},{14,10},... | collective-permute-start | bytes 3145736 | tf_op jit(solution)/shard_map/ppermute | solution.py:473
  47.6 21.7 %collective-permute-done.2 = bf16[512,1024]{1,0:T(8,128)(2,1)S(1)} collective-permute-done((bf16[512,1024]{1,0:T(8,128)(2,1)S(1)}, bf16[512,1024]{1,0:T(8,128)(2,1)S(1)}, u32[]{:S(2)}, u32[]{:S(2)}) %collective-permute-start.2) | collective-permute-done | bytes 1048608 | tf_op jit(solution)/shard_map/ppermute | solution.py:473
  69.3 1.0 copy-done.9
  70.3 1.0 fusion.1
  71.4 0.6 collective-permute-start.6
  72.0 3.7 %collective-permute-start.5 = (bf16[32,128,128]{2,1,0:T(8,128)(2,1)}, bf16[32,128,128]{2,1,0:T(8,128)(2,1)S(1)}, u32[]{:S(2)}, u32[]{:S(2)}) collective-permute-start(bf16[32,128,128]{2,1,0:T(8,128)(2,1)} %constant_dynamic-slice_fusion), channel_id=1, source_target_pairs={{0,4},{12,8},{1,5},{13,9},{2,6},{14,10},{3,7},{15,11},{16,20},{28,... | collective-permute-start | bytes 3145736 | tf_op jit(solution)/shard_map/ppermute | solution.py:477
  75.7 0.7 collective-permute-start.7
  76.5 0.7 pad_add_fusion.place_of
  77.1 1.2 bitcast_convert_fusion
  78.3 1.2 bitcast_convert_fusion.1.ids_3
  79.5 8.7 %place_first.1 = (bf16[4096,1024]{1,0:T(8,128)(2,1)}, bf16[1024,4096]{1,0:T(8,128)(2,1)}) custom-call(s32[4]{0:T(128)} %pad_add_fusion.place_of, s32[64]{0:T(128)} %ids.7, s32[64]{0:T(128)} %get-tuple-element.106.ids_1, s32[64]{0:T(128)} %get-tuple-element.105.ids_2, s32[64]{0:T(128)} %bitcast_convert_fusion.1.ids_3, bf16[64,128,128]{2,1,0:T(8,128)(2,1)} %own.1, ...), custom_call_target="tpu_custom_call" | custom-call | bytes 25165824 | tf_op jit(solution)/shard_map/place_first/pallas_call | solution.py:181
  88.2 7.6 %collective-permute-done.5.near_b = bf16[32,128,128]{2,1,0:T(8,128)(2,1)S(1)} collective-permute-done((bf16[32,128,128]{2,1,0:T(8,128)(2,1)}, bf16[32,128,128]{2,1,0:T(8,128)(2,1)S(1)}, u32[]{:S(2)}, u32[]{:S(2)}) %collective-permute-start.5) | collective-permute-done | bytes 1048608 | tf_op jit(solution)/shard_map/ppermute | solution.py:477
  95.9 0.9 copy-done.7
  96.8 0.7 collective-permute-start.10
  97.5 1.3 collective-permute-start.11
  98.8 3.9 %project_back.1 = (bf16[2,256,1024]{2,1,0:T(8,128)(2,1)}, bf16[2,256,1024]{2,1,0:T(8,128)(2,1)}, bf16[2,256,1024]{2,1,0:T(8,128)(2,1)}, bf16[256,1024]{1,0:T(8,128)(2,1)}, bf16[256,1024]{1,0:T(8,128)(2,1)}) custom-call(s32[4]{0:T(128)} %pad_add_fusion.place_of, s32[64]{0:T(128)} %get-tuple-element.106.ids_1, s32[64]{0:T(128)} %bitcast_convert_fusion.1.ids_3, ...), custom_call_target="tpu_custom_call" | custom-call | flops 4294967296 | bytes 13631488 | tf_op jit(solution)/shard_map/project_back/pallas_call | solution.py:239
  102.8 0.5 collective-permute-start.9
  103.3 1.6 collective-permute-done.8.refs_0_
  104.9 0.9 collective-permute-done.9.refs_1_
  105.8 3.0 %add_split.2 = (bf16[256,1024]{1,0:T(8,128)(2,1)}, bf16[256,1024]{1,0:T(8,128)(2,1)}) custom-call(s32[4]{0:T(128)} %pad_add_fusion.place_of, bf16[2,256,1024]{2,1,0:T(8,128)(2,1)} %get-tuple-element.68.keep, bf16[256,1024]{1,0:T(8,128)(2,1)} %copy-done.18, bf16[256,1024]{1,0:T(8,128)(2,1)} %collective-permute-done.9.refs_1_), custom_call_target="tpu_custom_call" | custom-call | flops 524288 | bytes 3145728 | tf_op jit(solution)/shard_map/add_split/pallas_call | solution.py:328
  108.8 13.9 %collective-permute-done.11.refs_2_ = bf16[512,1024]{1,0:T(8,128)(2,1)S(1)} collective-permute-done((bf16[512,1024]{1,0:T(8,128)(2,1)S(1)}, bf16[512,1024]{1,0:T(8,128)(2,1)S(1)}, u32[]{:S(2)}, u32[]{:S(2)}) %collective-permute-start.11) | collective-permute-done | bytes 1048608 | tf_op jit(solution)/shard_map/ppermute | solution.py:490
  122.7 0.9 slice_add_fusion
  123.8 0.8 slice.33
  124.6 1.3 collective-permute-start.14
  125.9 1.6 collective-permute-start.12
  127.4 4.0 %project_forward.1 = (bf16[256,1024]{1,0:T(8,128)(2,1)}, bf16[256,1024]{1,0:T(8,128)(2,1)}) custom-call(s32[4]{0:T(128)} %pad_add_fusion.place_of, s32[64]{0:T(128)} %get-tuple-element.106.ids_1, s32[64]{0:T(128)} %bitcast_convert_fusion.1.ids_3, bf16[4096,1024]{1,0:T(8,128)(2,1)} %get-tuple-element.82.partial, bf16[32,128,128]{2,1,0:T(8,128)(2,1)} %copy-done.7, ...), custom_call_target="tpu_custom_call" | custom-call | flops 536870912 | bytes 4194304 | tf_op jit(solution)/shard_map/project_forward/pallas_call | solution.py:296
  131.5 1.0 copy-done.8
  132.4 3.1 %add_split.3 = (bf16[256,1024]{1,0:T(8,128)(2,1)}, bf16[256,1024]{1,0:T(8,128)(2,1)}) custom-call(s32[4]{0:T(128)} %pad_add_fusion.place_of, bf16[2,256,1024]{2,1,0:T(8,128)(2,1)} %get-tuple-element.77.keep, bf16[2,256,1024]{2,1,0:T(8,128)(2,1)} %copy-done.8), custom_call_target="tpu_custom_call" | custom-call | flops 524288 | bytes 3145728 | tf_op jit(solution)/shard_map/add_split/pallas_call | solution.py:328
  135.5 5.6 %collective-permute-done.14 = bf16[256,1024]{1,0:T(8,128)(2,1)} collective-permute-done((bf16[256,1024]{1,0:T(8,128)(2,1)}, bf16[256,1024]{1,0:T(8,128)(2,1)}, u32[]{:S(2)}, u32[]{:S(2)}) %collective-permute-start.14) | collective-permute-done | bytes 524320 | tf_op jit(solution)/shard_map/ppermute | solution.py:502
  141.1 6.5 %collective-permute-done.12 = bf16[256,1024]{1,0:T(8,128)(2,1)S(1)} collective-permute-done((bf16[256,1024]{1,0:T(8,128)(2,1)}, bf16[256,1024]{1,0:T(8,128)(2,1)S(1)}, u32[]{:S(2)}, u32[]{:S(2)}) %collective-permute-start.12) | collective-permute-done | bytes 524320 | tf_op jit(solution)/shard_map/ppermute | solution.py:500
  147.6 2.2 fusion
  149.8 1.2 add.28
  151.1 1.6 collective-permute-start.16
  152.7 2.4 %collective-permute-start.17 = (bf16[256,1024]{1,0:T(8,128)(2,1)S(1)}, bf16[256,1024]{1,0:T(8,128)(2,1)S(1)}, u32[]{:S(2)}, u32[]{:S(2)}) collective-permute-start(bf16[256,1024]{1,0:T(8,128)(2,1)S(1)} %copy-done.20), channel_id=1, source_target_pairs={{0,2},{2,0},{1,3},{3,1},{4,6},{6,4},{5,7},{7,5},{8,10},{10,8},{9,1... | collective-permute-start | bytes 1572872 | tf_op jit(solution)/shard_map/ppermute | solution.py:510
  155.1 7.8 %line_grads.5.refs_3_ = bf16[64,128,128]{2,1,0:T(8,128)(2,1)} custom-call(s32[64]{0:T(128)} %ids.7, bf16[4,256,1024]{2,1,0:T(8,128)(2,1)} %bitcast.17, bf16[256,1024]{1,0:T(8,128)(2,1)} %get-tuple-element.103.end_upstream.refs_1_, bf16[64,128,128]{2,1,0:T(8,128)(2,1)} %line_grads.4.refs_2_), custom_call_target="tpu_custom_call" | custom-call | flops 536870912 | bytes 6815744 | tf_op jit(solution)/shard_map/line_grads/pallas_call | solution.py:411
  163.0 4.4 %collective-permute-done.16 = bf16[256,1024]{1,0:T(8,128)(2,1)S(1)} collective-permute-done((bf16[256,1024]{1,0:T(8,128)(2,1)S(1)}, bf16[256,1024]{1,0:T(8,128)(2,1)S(1)}, u32[]{:S(2)}, u32[]{:S(2)}) %collective-permute-start.16) | collective-permute-done | bytes 524320 | tf_op jit(solution)/shard_map/ppermute | solution.py:509
  167.3 0.5 collective-permute-done.17
  167.9 0.1 add_select_fusion.own
  168.0 2.5 %collective-permute-start.18 = (bf16[256,1024]{1,0:T(8,128)(2,1)S(1)}, bf16[256,1024]{1,0:T(8,128)(2,1)S(1)}, u32[]{:S(2)}, u32[]{:S(2)}) collective-permute-start(bf16[256,1024]{1,0:T(8,128)(2,1)S(1)} %add_select_fusion.own), channel_id=1, source_target_pairs={{0,2},{2,0},{1,3},{3,1},{4,6},{6,4},{5,7},{7,5},{8,10},{10,8},{9,1... | collective-permute-start | bytes 1572872 | tf_op jit(solution)/shard_map/ppermute | solution.py:519
  170.5 1.3 collective-permute-start.15
  171.8 8.5 %line_grads.6.refs_3_ = bf16[64,128,128]{2,1,0:T(8,128)(2,1)} custom-call(s32[64]{0:T(128)} %ids.7, bf16[4,256,1024]{2,1,0:T(8,128)(2,1)} %bitcast.18, bf16[512,1024]{1,0:T(8,128)(2,1)} %copy-done.2, bf16[512,1024]{1,0:T(8,128)(2,1)} %copy-done.3, bf16[64,128,128]{2,1,0:T(8,128)(2,1)} %line_grads.5.refs_3_), custom_call_target="tpu_custom_call" | custom-call | flops 536870912 | bytes 8388608 | tf_op jit(solution)/shard_map/line_grads/pallas_call | solution.py:411
  180.3 8.6 %collective-permute-done.18.by_tensor = bf16[256,1024]{1,0:T(8,128)(2,1)S(1)} collective-permute-done((bf16[256,1024]{1,0:T(8,128)(2,1)S(1)}, bf16[256,1024]{1,0:T(8,128)(2,1)S(1)}, u32[]{:S(2)}, u32[]{:S(2)}) %collective-permute-start.18) | collective-permute-done | bytes 524320 | tf_op jit(solution)/shard_map/ppermute | solution.py:519
  189.0 1.3 collective-permute-start.21
  190.3 4.0 %collective-permute-done.15 = bf16[256,1024]{1,0:T(8,128)(2,1)S(1)} collective-permute-done((bf16[256,1024]{1,0:T(8,128)(2,1)}, bf16[256,1024]{1,0:T(8,128)(2,1)S(1)}, u32[]{:S(2)}, u32[]{:S(2)}) %collective-permute-start.15) | collective-permute-done | bytes 524320 | tf_op jit(solution)/shard_map/ppermute | solution.py:517
  194.3 0.8 broadcast_select_fusion
  195.2 0.8 copy-done.17
  195.9 3.0 %assemble.1 = bf16[256,4096]{1,0:T(8,128)(2,1)} custom-call(s32[4]{0:T(128)} %pad_add_fusion.place_of, bf16[256,1024]{1,0:T(8,128)(2,1)} %copy-done.4, bf16[256,1024]{1,0:T(8,128)(2,1)} %copy-done.14, bf16[256,1024]{1,0:T(8,128)(2,1)} %copy-done.13, bf16[256,1024]{1,0:T(8,128)(2,1)} %copy-done.17), custom_call_target="tpu_custom_call" | custom-call | bytes 4194304 | tf_op jit(solution)/shard_map/assemble/pallas_call | solution.py:353
  198.9 7.6 %collective-permute-done.21.refs_2_ = bf16[256,1024]{1,0:T(8,128)(2,1)S(1)} collective-permute-done((bf16[256,1024]{1,0:T(8,128)(2,1)S(1)}, bf16[256,1024]{1,0:T(8,128)(2,1)S(1)}, u32[]{:S(2)}, u32[]{:S(2)}) %collective-permute-start.21) | collective-permute-done | bytes 524320 | tf_op jit(solution)/shard_map/ppermute | solution.py:512
  206.5 0.8 copy-done.16
  207.3 8.2 %line_grads.7 = bf16[64,128,128]{2,1,0:T(8,128)(2,1)} custom-call(s32[64]{0:T(128)} %ids.7, bf16[4,256,1024]{2,1,0:T(8,128)(2,1)} %bitcast.19, bf16[512,1024]{1,0:T(8,128)(2,1)} %copy-done.1, bf16[256,1024]{1,0:T(8,128)(2,1)} %copy-done.16, bf16[64,128,128]{2,1,0:T(8,128)(2,1)} %line_grads.6.refs_3_), custom_call_target="tpu_custom_call" | custom-call | flops 536870912 | bytes 7864320 | tf_op jit(solution)/shard_map/line_grads/pallas_call | solution.py:411
  (60 shorter events, 0.5 us)
Async XLA Ops:
  7.2 88.7 %all-gather.7.cloned.1.call-start = ((), (), s32[]{:S(2)}) async-start(), calls=%async_computation | async-start | bytes 2621440 | tf_op jit(solution)/shard_map/all_gather | solution.py:480
  10.4 28.3 %collective-permute-start = (bf16[33,128,128]{2,1,0:T(8,128)(2,1)}, bf16[33,128,128]{2,1,0:T(8,128)(2,1)S(1)}, u32[]{:S(2)}, u32[]{:S(2)}) collective-permute-start(bf16[33,128,128]{2,1,0:T(8,128)(2,1)} %pad_maximum_fusion), channel_id=1, source_target_pairs={{0,4},{12,8},{1,5},{13,9},{2,6},{14,10},{3,7},{15,11},{16,20},{28,... | collective-permute-start | bytes 3244040 | tf_op jit(solution)/shard_map/ppermute | solution.py:463
  15.4 23.4 %collective-permute-start.1 = (bf16[33,128,128]{2,1,0:T(8,128)(2,1)}, bf16[33,128,128]{2,1,0:T(8,128)(2,1)}, u32[]{:S(2)}, u32[]{:S(2)}) collective-permute-start(bf16[33,128,128]{2,1,0:T(8,128)(2,1)} %pad_maximum_fusion), channel_id=1, source_target_pairs={{4,8},{8,4},{5,9},{9,5},{6,10},{10,6},{7,11},{11,7},{20,24},{24,20... | collective-permute-start | bytes 3244040 | tf_op jit(solution)/shard_map/ppermute | solution.py:464
  17.0 8.1 %copy-start.5 = (bf16[256,1024]{1,0:T(8,128)(2,1)S(1)}, bf16[256,1024]{1,0:T(8,128)(2,1)}, u32[]{:S(2)}) copy-start(bf16[256,1024]{1,0:T(8,128)(2,1)} %upstream.1) | copy-start | bytes 1572868
  23.9 1.8 copy-start
  25.7 45.7 %copy-start.10 = (bf16[512,1024]{1,0:T(8,128)(2,1)}, bf16[512,1024]{1,0:T(8,128)(2,1)S(1)}, u32[]{:S(2)}) copy-start(bf16[512,1024]{1,0:T(8,128)(2,1)S(1)} %pad_maximum_fusion.1) | copy-start | bytes 3145732
  38.7 40.8 %copy-start.6 = (bf16[33,128,128]{2,1,0:T(8,128)(2,1)}, bf16[33,128,128]{2,1,0:T(8,128)(2,1)S(1)}, u32[]{:S(2)}) copy-start(bf16[33,128,128]{2,1,0:T(8,128)(2,1)S(1)} %collective-permute-done.near_a) | copy-start | bytes 3244036
  38.7 30.6 %collective-permute-start.3 = (bf16[33,128,128]{2,1,0:T(8,128)(2,1)S(1)}, bf16[33,128,128]{2,1,0:T(8,128)(2,1)}, u32[]{:S(2)}, u32[]{:S(2)}) collective-permute-start(bf16[33,128,128]{2,1,0:T(8,128)(2,1)S(1)} %collective-permute-done.near_a), channel_id=1, source_target_pairs={{4,8},{8,4},{5,9},{9,5},{6,10},{10,6},{7,11},{11,7},{20,24},{24,20... | collective-permute-start | bytes 3244040 | tf_op jit(solution)/shard_map/ppermute | solution.py:471
  40.4 28.9 %collective-permute-start.4 = (bf16[33,128,128]{2,1,0:T(8,128)(2,1)}, bf16[33,128,128]{2,1,0:T(8,128)(2,1)}, u32[]{:S(2)}, u32[]{:S(2)}) collective-permute-start(bf16[33,128,128]{2,1,0:T(8,128)(2,1)} %collective-permute-done.1.far_a), channel_id=1, source_target_pairs={{0,16},{16,0},{1,17},{17,1},{2,18},{18,2},{3,19},{19,3},{4,20},{20... | collective-permute-start | bytes 3244040 | tf_op jit(solution)/shard_map/ppermute | solution.py:472
  41.9 27.4 %collective-permute-start.2 = (bf16[512,1024]{1,0:T(8,128)(2,1)S(1)}, bf16[512,1024]{1,0:T(8,128)(2,1)S(1)}, u32[]{:S(2)}, u32[]{:S(2)}) collective-permute-start(bf16[512,1024]{1,0:T(8,128)(2,1)S(1)} %pad_maximum_fusion.1), channel_id=1, source_target_pairs={{0,4},{12,8},{4,0},{8,12},{1,5},{13,9},{5,1},{9,13},{2,6},{14,10},... | collective-permute-start | bytes 3145736 | tf_op jit(solution)/shard_map/ppermute | solution.py:473
  69.3 1.0 copy-start.9
  71.4 100.4 %all-gather.9.cloned.1.call-start = ((), (), s32[]{:S(2)}) async-start(), calls=%async_computation.1 | async-start | bytes 2621440 | tf_op jit(solution)/shard_map/all_gather | solution.py:503
  71.4 24.4 %collective-permute-start.6 = (bf16[33,128,128]{2,1,0:T(8,128)(2,1)}, bf16[33,128,128]{2,1,0:T(8,128)(2,1)}, u32[]{:S(2)}, u32[]{:S(2)}) collective-permute-start(bf16[33,128,128]{2,1,0:T(8,128)(2,1)} %collective-permute-done.3.end_a), channel_id=1, source_target_pairs={{0,16},{16,0},{1,17},{17,1},{2,18},{18,2},{3,19},{19,3},{4,20},{20... | collective-permute-start | bytes 3244040 | tf_op jit(solution)/shard_map/ppermute | solution.py:478
  72.0 23.8 %collective-permute-start.5 = (bf16[32,128,128]{2,1,0:T(8,128)(2,1)}, bf16[32,128,128]{2,1,0:T(8,128)(2,1)S(1)}, u32[]{:S(2)}, u32[]{:S(2)}) collective-permute-start(bf16[32,128,128]{2,1,0:T(8,128)(2,1)} %constant_dynamic-slice_fusion), channel_id=1, source_target_pairs={{0,4},{12,8},{1,5},{13,9},{2,6},{14,10},{3,7},{15,11},{16,20},{28,... | collective-permute-start | bytes 3145736 | tf_op jit(solution)/shard_map/ppermute | solution.py:477
  75.7 20.1 %collective-permute-start.7 = (bf16[512,1024]{1,0:T(8,128)(2,1)}, bf16[512,1024]{1,0:T(8,128)(2,1)S(1)}, u32[]{:S(2)}, u32[]{:S(2)}) collective-permute-start(bf16[512,1024]{1,0:T(8,128)(2,1)} %copy-done.10), channel_id=1, source_target_pairs={{4,8},{8,4},{5,9},{9,5},{6,10},{10,6},{7,11},{11,7},{20,24},{24,20... | collective-permute-start | bytes 3145736 | tf_op jit(solution)/shard_map/ppermute | solution.py:479
  95.8 1.0 copy-start.7
  95.8 26.9 %copy-start.2 = (bf16[512,1024]{1,0:T(8,128)(2,1)}, bf16[512,1024]{1,0:T(8,128)(2,1)S(1)}, u32[]{:S(2)}) copy-start(bf16[512,1024]{1,0:T(8,128)(2,1)S(1)} %collective-permute-done.7.refs_1_) | copy-start | bytes 3145732
  96.8 12.0 %collective-permute-start.10 = (bf16[512,1024]{1,0:T(8,128)(2,1)}, bf16[512,1024]{1,0:T(8,128)(2,1)S(1)}, u32[]{:S(2)}, u32[]{:S(2)}) collective-permute-start(bf16[512,1024]{1,0:T(8,128)(2,1)} %copy-done.9), channel_id=1, source_target_pairs={{4,8},{8,4},{5,9},{9,5},{6,10},{10,6},{7,11},{11,7},{20,24},{24,20... | collective-permute-start | bytes 3145736 | tf_op jit(solution)/shard_map/ppermute | solution.py:489
  97.5 25.2 %collective-permute-start.11 = (bf16[512,1024]{1,0:T(8,128)(2,1)S(1)}, bf16[512,1024]{1,0:T(8,128)(2,1)S(1)}, u32[]{:S(2)}, u32[]{:S(2)}) collective-permute-start(bf16[512,1024]{1,0:T(8,128)(2,1)S(1)} %collective-permute-done.7.refs_1_), channel_id=1, source_target_pairs={{4,0},{8,12},{5,1},{9,13},{6,2},{10,14},{7,3},{11,15},{20,16},{24,... | collective-permute-start | bytes 3145736 | tf_op jit(solution)/shard_map/ppermute | solution.py:490
  102.7 2.2 collective-permute-start.8
  102.8 3.0 %collective-permute-start.9 = (bf16[256,1024]{1,0:T(8,128)(2,1)}, bf16[256,1024]{1,0:T(8,128)(2,1)}, u32[]{:S(2)}, u32[]{:S(2)}) collective-permute-start(bf16[256,1024]{1,0:T(8,128)(2,1)} %get-tuple-element.70), channel_id=1, source_target_pairs={{0,1},{1,0},{2,3},{3,2},{4,5},{5,4},{6,7},{7,6},{8,9},{9,8},{10,11... | collective-permute-start | bytes 1572872 | tf_op jit(solution)/shard_map/ppermute | solution.py:495
  104.9 0.9 copy-start.18
  108.8 38.8 %copy-start.1 = (bf16[512,1024]{1,0:T(8,128)(2,1)}, bf16[512,1024]{1,0:T(8,128)(2,1)S(1)}, u32[]{:S(2)}) copy-start(bf16[512,1024]{1,0:T(8,128)(2,1)S(1)} %collective-permute-done.10.refs_1_) | copy-start | bytes 3145732
  122.7 8.7 %copy-start.3 = (bf16[512,1024]{1,0:T(8,128)(2,1)}, bf16[512,1024]{1,0:T(8,128)(2,1)S(1)}, u32[]{:S(2)}) copy-start(bf16[512,1024]{1,0:T(8,128)(2,1)S(1)} %collective-permute-done.11.refs_2_) | copy-start | bytes 3145732
  123.6 82.9 %all-gather.11.cloned.1.call-start = ((), (), s32[]{:S(2)}) async-start(), calls=%async_computation.2 | async-start | bytes 2621440 | tf_op jit(solution)/shard_map/all_gather | solution.py:511
  123.7 7.8 %collective-permute-start.13 = (bf16[2,256,1024]{2,1,0:T(8,128)(2,1)}, bf16[2,256,1024]{2,1,0:T(8,128)(2,1)S(1)}, u32[]{:S(2)}, u32[]{:S(2)}) collective-permute-start(bf16[2,256,1024]{2,1,0:T(8,128)(2,1)} %get-tuple-element.78), channel_id=1, source_target_pairs={{0,1},{1,0},{2,3},{3,2},{4,5},{5,4},{6,7},{7,6},{8,9},{9,8},{10,11... | collective-permute-start | bytes 3145736 | tf_op jit(solution)/shard_map/ppermute | solution.py:501
  124.6 16.5 %collective-permute-start.14 = (bf16[256,1024]{1,0:T(8,128)(2,1)}, bf16[256,1024]{1,0:T(8,128)(2,1)}, u32[]{:S(2)}, u32[]{:S(2)}) collective-permute-start(bf16[256,1024]{1,0:T(8,128)(2,1)} %slice.33), channel_id=1, source_target_pairs={{4,0},{8,12},{5,1},{9,13},{6,2},{10,14},{7,3},{11,15},{20,16},{24,... | collective-permute-start | bytes 1572872 | tf_op jit(solution)/shard_map/ppermute | solution.py:502
  125.9 21.7 %collective-permute-start.12 = (bf16[256,1024]{1,0:T(8,128)(2,1)}, bf16[256,1024]{1,0:T(8,128)(2,1)S(1)}, u32[]{:S(2)}, u32[]{:S(2)}) collective-permute-start(bf16[256,1024]{1,0:T(8,128)(2,1)} %get-tuple-element.76), channel_id=1, source_target_pairs={{0,2},{2,0},{1,3},{3,1},{4,6},{6,4},{5,7},{7,5},{8,10},{10,8},{9,1... | collective-permute-start | bytes 1572872 | tf_op jit(solution)/shard_map/ppermute | solution.py:500
  131.5 1.0 copy-start.8
  135.5 14.3 %copy-start.11 = (bf16[256,1024]{1,0:T(8,128)(2,1)S(1)}, bf16[256,1024]{1,0:T(8,128)(2,1)}, u32[]{:S(2)}) copy-start(bf16[256,1024]{1,0:T(8,128)(2,1)} %get-tuple-element.89) | copy-start | bytes 1572868
  147.6 2.2 copy-start.15
  147.6 5.1 %copy-start.20 = (bf16[256,1024]{1,0:T(8,128)(2,1)S(1)}, bf16[256,1024]{1,0:T(8,128)(2,1)}, u32[]{:S(2)}) copy-start(bf16[256,1024]{1,0:T(8,128)(2,1)} %get-tuple-element.91) | copy-start | bytes 1572868
  151.1 16.8 %copy-start.12 = (bf16[256,1024]{1,0:T(8,128)(2,1)S(1)}, bf16[256,1024]{1,0:T(8,128)(2,1)}, u32[]{:S(2)}) copy-start(bf16[256,1024]{1,0:T(8,128)(2,1)} %get-tuple-element.88) | copy-start | bytes 1572868
  151.1 16.3 %collective-permute-start.16 = (bf16[256,1024]{1,0:T(8,128)(2,1)S(1)}, bf16[256,1024]{1,0:T(8,128)(2,1)S(1)}, u32[]{:S(2)}, u32[]{:S(2)}) collective-permute-start(bf16[256,1024]{1,0:T(8,128)(2,1)S(1)} %add.28), channel_id=1, source_target_pairs={{4,0},{8,12},{5,1},{9,13},{6,2},{10,14},{7,3},{11,15},{20,16},{24,... | collective-permute-start | bytes 1572872 | tf_op jit(solution)/shard_map/ppermute | solution.py:509
  152.7 15.2 %collective-permute-start.17 = (bf16[256,1024]{1,0:T(8,128)(2,1)S(1)}, bf16[256,1024]{1,0:T(8,128)(2,1)S(1)}, u32[]{:S(2)}, u32[]{:S(2)}) collective-permute-start(bf16[256,1024]{1,0:T(8,128)(2,1)S(1)} %copy-done.20), channel_id=1, source_target_pairs={{0,2},{2,0},{1,3},{3,1},{4,6},{6,4},{5,7},{7,5},{8,10},{10,8},{9,1... | collective-permute-start | bytes 1572872 | tf_op jit(solution)/shard_map/ppermute | solution.py:510
  168.0 12.4 %copy-start.4 = (bf16[256,1024]{1,0:T(8,128)(2,1)}, bf16[256,1024]{1,0:T(8,128)(2,1)S(1)}, u32[]{:S(2)}) copy-start(bf16[256,1024]{1,0:T(8,128)(2,1)S(1)} %add_select_fusion.own) | copy-start | bytes 1572868
  168.0 20.9 %collective-permute-start.18 = (bf16[256,1024]{1,0:T(8,128)(2,1)S(1)}, bf16[256,1024]{1,0:T(8,128)(2,1)S(1)}, u32[]{:S(2)}, u32[]{:S(2)}) collective-permute-start(bf16[256,1024]{1,0:T(8,128)(2,1)S(1)} %add_select_fusion.own), channel_id=1, source_target_pairs={{0,2},{2,0},{1,3},{3,1},{4,6},{6,4},{5,7},{7,5},{8,10},{10,8},{9,1... | collective-permute-start | bytes 1572872 | tf_op jit(solution)/shard_map/ppermute | solution.py:519
  170.5 18.4 %collective-permute-start.19 = (bf16[256,1024]{1,0:T(8,128)(2,1)S(1)}, bf16[256,1024]{1,0:T(8,128)(2,1)S(1)}, u32[]{:S(2)}, u32[]{:S(2)}) collective-permute-start(bf16[256,1024]{1,0:T(8,128)(2,1)S(1)} %add_select_fusion.own), channel_id=1, source_target_pairs={{0,1},{1,0},{2,3},{3,2},{4,5},{5,4},{6,7},{7,6},{8,9},{9,8},{10,11... | collective-permute-start | bytes 1572872 | tf_op jit(solution)/shard_map/ppermute | solution.py:519
  170.5 23.8 %collective-permute-start.15 = (bf16[256,1024]{1,0:T(8,128)(2,1)}, bf16[256,1024]{1,0:T(8,128)(2,1)S(1)}, u32[]{:S(2)}, u32[]{:S(2)}) collective-permute-start(bf16[256,1024]{1,0:T(8,128)(2,1)} %get-tuple-element.87), channel_id=1, source_target_pairs={{4,0},{8,12},{5,1},{9,13},{6,2},{10,14},{7,3},{11,15},{20,16},{24,... | collective-permute-start | bytes 1572872 | tf_op jit(solution)/shard_map/ppermute | solution.py:517
  171.8 22.4 %copy-start.19 = (bf16[256,1024]{1,0:T(8,128)(2,1)S(1)}, bf16[256,1024]{1,0:T(8,128)(2,1)}, u32[]{:S(2)}) copy-start(bf16[256,1024]{1,0:T(8,128)(2,1)} %get-tuple-element.86) | copy-start | bytes 1572868
  188.9 6.3 %copy-start.13 = (bf16[256,1024]{1,0:T(8,128)(2,1)}, bf16[256,1024]{1,0:T(8,128)(2,1)S(1)}, u32[]{:S(2)}) copy-start(bf16[256,1024]{1,0:T(8,128)(2,1)S(1)} %collective-permute-done.18.by_tensor) | copy-start | bytes 1572868
  188.9 6.2 %copy-start.14 = (bf16[256,1024]{1,0:T(8,128)(2,1)}, bf16[256,1024]{1,0:T(8,128)(2,1)S(1)}, u32[]{:S(2)}) copy-start(bf16[256,1024]{1,0:T(8,128)(2,1)S(1)} %collective-permute-done.19.by_core) | copy-start | bytes 1572868
  188.9 6.2 %collective-permute-start.20 = (bf16[256,1024]{1,0:T(8,128)(2,1)S(1)}, bf16[256,1024]{1,0:T(8,128)(2,1)S(1)}, u32[]{:S(2)}, u32[]{:S(2)}) collective-permute-start(bf16[256,1024]{1,0:T(8,128)(2,1)S(1)} %collective-permute-done.18.by_tensor), channel_id=1, source_target_pairs={{0,1},{1,0},{2,3},{3,2},{4,5},{5,4},{6,7},{7,6},{8,9},{9,8},{10,11... | collective-permute-start | bytes 1572872 | tf_op jit(solution)/shard_map/ppermute | solution.py:520
  189.0 17.5 %collective-permute-start.21 = (bf16[256,1024]{1,0:T(8,128)(2,1)S(1)}, bf16[256,1024]{1,0:T(8,128)(2,1)S(1)}, u32[]{:S(2)}, u32[]{:S(2)}) collective-permute-start(bf16[256,1024]{1,0:T(8,128)(2,1)S(1)} %get-tuple-element.101), channel_id=1, source_target_pairs={{4,0},{8,12},{5,1},{9,13},{6,2},{10,14},{7,3},{11,15},{20,16},{24,... | collective-permute-start | bytes 1572872 | tf_op jit(solution)/shard_map/ppermute | solution.py:512
  195.1 0.8 copy-start.17
  206.5 0.8 copy-start.16
Sparse Core Ops, SparseCore 0:
  71.5 21.0 all-gather.6
  123.8 29.4 all-gather.8
  154.8 32.6 all-gather.10

commit v19 on v16

--- a/solution.py
+++ b/solution.py
@@ -363,24 +363,24 @@
     )(place_of, *quarters)
 
 
-def line_grads_kernel(pairs_n, ids, *refs):
+def line_grads_kernel(kind, place_of, ids, *refs):
     refs = list(refs)
-    pairs = []
-    for k in range(pairs_n):
+    if kind == "plain":
         x, d = refs.pop(0), refs.pop(0)
-        if d.shape[0] > x.shape[-2]:
-            rows, other = x.shape[-2], refs.pop(0)
-            total_d = refs.pop()
-            total_d[...] = d[rows:] + other[rows:]
-            d = total_d
-        pairs.append((x, d))
+    else:
+        mine, theirs, before, after = (refs.pop(0) for _ in range(4))
+        x, d = refs.pop(), refs.pop()
+        rows = x.shape[1]
+        for at in range(2):
+            x[2 * at + place_of[3]] = mine[at]
+            x[2 * at + 1 - place_of[3]] = theirs[at]
+        d[...] = before[rows:] + after[rows:]
     start = refs.pop(0) if len(refs) == 2 else None
     (grads,) = refs
     slots, size = grads.shape[0], grads.shape[1]
-    first = pairs[0][0]
-    cols_n = pairs[0][1].shape[1] // size
-    rows_n = first.shape[-1] // size * (first.shape[0] if len(first.shape) == 3 else 1)
-    total = rows_n * cols_n
+    cols_n = d.shape[1] // size
+    per_part = x.shape[-1] // size
+    total = per_part * (x.shape[0] if len(x.shape) == 3 else 1) * cols_n
     group = math.gcd(slots, 8)
 
     @pl.loop(0, slots // group)
@@ -388,40 +388,43 @@
         for s in [g * group + j for j in range(group)]:
             b = jnp.minimum(ids[s], total - 1)
             row = b // cols_n
-            c = pl.ds(pl.multiple_of((b % cols_n) * size, size), size)
-            acc = jnp.zeros((size, size), jnp.float32) if start is None else start[s].astype(jnp.float32)
-            for x, d in pairs:
-                per_part = x.shape[-1] // size
-                at = pl.ds(pl.multiple_of((row % per_part) * size, size), size)
-                acc += lax.dot_general(
-                    x[row // per_part, :, at] if len(x.shape) == 3 else x[:, at],
-                    d[:, c],
-                    (((0,), (0,)), ((), ())),
-                    preferred_element_type=jnp.float32,
-                )
+            at = pl.ds(pl.multiple_of((row % per_part) * size, size), size)
+            acc = lax.dot_general(
+                x[row // per_part, :, at] if len(x.shape) == 3 else x[:, at],
+                d[:, pl.ds(pl.multiple_of((b % cols_n) * size, size), size)],
+                (((0,), (0,)), ((), ())),
+                preferred_element_type=jnp.float32,
+            )
+            if start is not None:
+                acc += start[s].astype(jnp.float32)
             grads[s] = jnp.where(ids[s] < total, acc, 0.0).astype(grads.dtype)
 
 
-def line_grads(ids, pairs, start, size):
+def line_grads(place_of, ids, operands, start, size):
     slots = ids.shape[0]
-    flat = [a for pair in pairs for a in pair] + ([] if start is None else [start])
-    sums = [
-        pltpu.VMEM((p[0].shape[-2], p[1].shape[1]), jnp.bfloat16) for p in pairs if len(p) == 3
-    ]
-    return pl.pallas_call(
-        functools.partial(line_grads_kernel, len(pairs)),
+    kind = "plain" if len(operands) == 2 else "split"
+    flat = list(operands) + ([] if start is None else [start])
+    scratch = []
+    if kind == "split":
+        _, rows, part_width = operands[0].shape
+        scratch = [
+            pltpu.VMEM((rows, operands[2].shape[1]), jnp.bfloat16),
+            pltpu.VMEM((4, rows, part_width), jnp.bfloat16),
+        ]
+    return pl.pallas_call(
+        functools.partial(line_grads_kernel, kind),
         out_shape=jax.ShapeDtypeStruct((slots, size, size), jnp.bfloat16),
-        in_specs=[whole(pltpu.SMEM)] + [whole()] * len(flat),
+        in_specs=[whole(pltpu.SMEM)] * 2 + [whole()] * len(flat),
         out_specs=whole(),
-        scratch_shapes=sums,
-        compiler_params=pltpu.CompilerParams(vmem_limit_bytes=VMEM_LIMIT),
-        cost_estimate=pl.CostEstimate(
-            flops=512 * len(pairs) * slots * size * size,
+        scratch_shapes=scratch,
+        compiler_params=pltpu.CompilerParams(vmem_limit_bytes=VMEM_LIMIT),
+        cost_estimate=pl.CostEstimate(
+            flops=512 * slots * size * size,
             bytes_accessed=sum(2 * a.size for a in flat) + 2 * slots * size * size,
             transcendentals=0,
         ),
         name="line_grads",
-    )(ids, *flat)
+    )(place_of, ids, *flat)
 
 
 INWARD = ((0, 1), (3, 2))
@@ -465,7 +468,7 @@
     other = lax.dynamic_slice_in_dim(late_blocks, (1 - half) * half_slots, half_slots, 0)
     part = lax.dynamic_slice_in_dim(tokens, lax.axis_index(INNER) * part_width, part_width, 1)
     both = jnp.concatenate([part, upstream])
-    grads = line_grads(block_ids, ((tokens, upstream),), None, size)
+    grads = line_grads(place_of, block_ids, (tokens, upstream), None, size)
     near_a, far_a, both, other, grads = stage((near_a, far_a, both, other, grads))
 
     end_a = along(near_a, perm=MIDDLE)
@@ -500,26 +503,35 @@
     end_got = sideways(end_give)
     own_keep, own_give = add_split(place_of, own_keep, cores(own_give))
     both_3o = along(both_3m, perm=OUTWARD)
-    tokens_2 = lax.all_gather(both_2m[:rows] + both_2o[:rows], INNER)
+    side_2 = lax.all_gather(both_2m[:rows] + both_2o[:rows], "tensor")
     proj, end_proj = project_forward(place_of, ids_1, ids_3, partial, *last, tokens, tokens_1)
-    end_got, own_give, own_keep, proj, end_proj = stage(
-        (end_got, own_give, own_keep, proj, end_proj)
+    end_got, own_give, own_keep, proj, end_proj, side_2 = stage(
+        (end_got, own_give, own_keep, proj, end_proj, side_2)
     )
 
     sum_out = along(end_keep + end_got, perm=OUTWARD)
     own_got = sideways(own_give)
-    grads = line_grads(block_ids, ((tokens_1, upstream_1),), grads, size)
-    sum_out, own_got, both_3o, grads = stage((sum_out, own_got, both_3o, grads))
-
-    tokens_3 = lax.all_gather(both_3m[:rows] + both_3o[:rows], INNER)
+    grads = line_grads(place_of, block_ids, (tokens_1, upstream_1), grads, size)
+    theirs_2 = cores(side_2)
+    sum_out, own_got, both_3o, grads, theirs_2 = stage(
+        (sum_out, own_got, both_3o, grads, theirs_2)
+    )
+
+    side_3 = lax.all_gather(both_3m[:rows] + both_3o[:rows], "tensor")
     quarter = jnp.where(middle, own_keep + own_got, sum_out)
     proj_out = along(end_proj, perm=OUTWARD)
-    grads = line_grads(block_ids, ((tokens_2, both_2m, both_2o),), grads, size)
-    by_tensor, by_core, grads = stage((sideways(quarter), cores(quarter), grads))
+    grads = line_grads(
+        place_of, block_ids, (side_2, theirs_2, both_2m, both_2o), grads, size
+    )
+    by_tensor, by_core, grads, side_3, proj_out = stage(
+        (sideways(quarter), cores(quarter), grads, side_3, proj_out)
+    )
     by_both = cores(by_tensor)
     projected = jnp.where(middle, proj, proj_out)
     token_grad = assemble(place_of, (quarter, by_core, by_tensor, by_both))
-    grads = line_grads(block_ids, ((tokens_3, both_3m, both_3o),), grads, size)
+    grads = line_grads(
+        place_of, block_ids, (side_3, cores(side_3), both_3m, both_3o), grads, size
+    )
     return projected, token_grad, grads
 
 

time: 207 us -> 230 us (1.11)
  waiting for transfers between devices: 84 us -> 104 us
    all_gather x2, waiting for transfers between devices: 0.17 us -> 10.5 us  [the longest x1 7.15 us: line_body(): side_2 = lax.all_gather(both_2m[:rows] + both_2o[:rows], 'tensor')]
    ppermute x1, waiting for transfers between devices: 6.24 us -> 10.9 us  [line_body(): sum_out = along(end_keep + end_got, perm=OUTWARD)]
    ppermute x1, waiting for transfers between devices: 0.01 us -> 4.02 us  [line_body(): proj_out = along(end_proj, perm=OUTWARD)]
    ppermute x1, waiting for transfers between devices: 0.01 us -> 2.65 us  [line_body(): both_3o = along(both_3m, perm=OUTWARD)]
    unnamed x36 -> x40, local copies, waits for them, and re-layouts: 3.33 us -> 5.09 us
  transfers between devices with their start and end apart: 24 -> 26, of which waited for: 11 -> 14; matrix products, arithmetic and copies ran while one was open for 5% -> 5% of each run, Pallas kernels for 24% -> 21%
where the time goes in v19:
time: 230 us; the launch traced here: 229 us
  waiting for transfers between devices  104 us (45%)
  Pallas kernels  57.6 us (25%)
  starting transfers between devices  31.2 us (14%)
  between operations  14 us (6%)
  other arithmetic  12.4 us (5%)
  local copies, waits for them, and re-layouts  9.94 us (4%)
    pallas_call x4, Pallas kernels, line_grads(): pl.pallas_call(functools.partial(line_grads_kernel, kind), out_shape=jax....  31.9 us
    ppermute x1, waiting for transfers between devices, line_body(): both_1 = along(both, perm=PAIRS)  21.7 us
    ppermute x1, waiting for transfers between devices, line_body(): both_2o = along(both_2m, perm=OUTWARD)  13.9 us
    ppermute x1, waiting for transfers between devices, line_body(): near_a = along(mine, perm=INWARD)  11.3 us
    ppermute x1, waiting for transfers between devices, line_body(): sum_out = along(end_keep + end_got, perm=OUTWARD)  10.9 us
    ppermute x1, waiting for transfers between devices, line_body(): end_got = sideways(end_give)  8.91 us
    ppermute x1, waiting for transfers between devices, line_body(): sideways(quarter)  8.85 us
    pallas_call x1, Pallas kernels, place_first(): pl.pallas_call(place_kernel, out_shape=(jax.ShapeDtypeStruct((depth, widt...  8.73 us
  transfers between devices with their start and end apart: 26, of which 14 were waited for; matrix products, arithmetic and copies ran while one was open for 5% of the time, Pallas kernels for 21%

profile of v19, /device:TPU:0, one launch (start us, length us, event | category | flops | bytes accessed | tf_op | source)
XLA Modules:
  0.0 229.4 jit_solution(5825882112945198907)
XLA Ops:
  7.2 0.7 convert_element_type.26
  7.9 0.1 convert_element_type.27
  8.0 1.3 constant_dynamic-slice_fusion.2
  9.3 1.1 pad_maximum_fusion
  10.4 5.0 %collective-permute-start = (bf16[33,128,128]{2,1,0:T(8,128)(2,1)}, bf16[33,128,128]{2,1,0:T(8,128)(2,1)S(1)}, u32[]{:S(2)}, u32[]{:S(2)}) collective-permute-start(bf16[33,128,128]{2,1,0:T(8,128)(2,1)} %pad_maximum_fusion), channel_id=1, source_target_pairs={{0,4},{12,8},{1,5},{13,9},{2,6},{14,10},{3,7},{15,11},{16,20},{28,... | collective-permute-start | bytes 3244040 | tf_op jit(solution)/shard_map/ppermute | solution.py:466
  15.4 1.7 collective-permute-start.1
  17.0 0.6 pad_add_fusion.place_of
  17.6 6.9 %line_grads.4.refs_2_ = bf16[64,128,128]{2,1,0:T(8,128)(2,1)} custom-call(s32[4]{0:T(128)} %pad_add_fusion.place_of, s32[64]{0:T(128)} %ids.7, bf16[256,4096]{1,0:T(8,128)(2,1)} %tokens.1, bf16[256,1024]{1,0:T(8,128)(2,1)} %upstream.1), custom_call_target="tpu_custom_call" | custom-call | flops 536870912 | bytes 4718592 | tf_op jit(solution)/shard_map/line_grads/pallas_call | solution.py:414
  24.5 1.2 constant_dynamic-slice_fusion.1
  25.8 0.1 pad_maximum_fusion.1
  25.9 0.4 copy-done
  26.3 1.2 constant_dynamic-slice_fusion
  27.5 11.3 %collective-permute-done.near_a = bf16[33,128,128]{2,1,0:T(8,128)(2,1)S(1)} collective-permute-done((bf16[33,128,128]{2,1,0:T(8,128)(2,1)}, bf16[33,128,128]{2,1,0:T(8,128)(2,1)S(1)}, u32[]{:S(2)}, u32[]{:S(2)}) %collective-permute-start) | collective-permute-done | bytes 1081376 | tf_op jit(solution)/shard_map/ppermute | solution.py:466
  38.7 1.7 collective-permute-start.3
  40.4 1.5 collective-permute-start.4
  41.9 5.6 %collective-permute-start.2 = (bf16[512,1024]{1,0:T(8,128)(2,1)S(1)}, bf16[512,1024]{1,0:T(8,128)(2,1)S(1)}, u32[]{:S(2)}, u32[]{:S(2)}) collective-permute-start(bf16[512,1024]{1,0:T(8,128)(2,1)S(1)} %pad_maximum_fusion.1), channel_id=1, source_target_pairs={{0,4},{12,8},{4,0},{8,12},{1,5},{13,9},{5,1},{9,13},{2,6},{14,10},... | collective-permute-start | bytes 3145736 | tf_op jit(solution)/shard_map/ppermute | solution.py:476
  47.6 21.7 %collective-permute-done.2 = bf16[512,1024]{1,0:T(8,128)(2,1)S(1)} collective-permute-done((bf16[512,1024]{1,0:T(8,128)(2,1)S(1)}, bf16[512,1024]{1,0:T(8,128)(2,1)S(1)}, u32[]{:S(2)}, u32[]{:S(2)}) %collective-permute-start.2) | collective-permute-done | bytes 1048608 | tf_op jit(solution)/shard_map/ppermute | solution.py:476
  69.3 1.0 copy-done.11
  70.3 1.0 fusion
  71.5 0.6 collective-permute-start.6
  72.0 3.7 %collective-permute-start.5 = (bf16[32,128,128]{2,1,0:T(8,128)(2,1)}, bf16[32,128,128]{2,1,0:T(8,128)(2,1)S(1)}, u32[]{:S(2)}, u32[]{:S(2)}) collective-permute-start(bf16[32,128,128]{2,1,0:T(8,128)(2,1)} %constant_dynamic-slice_fusion), channel_id=1, source_target_pairs={{0,4},{12,8},{1,5},{13,9},{2,6},{14,10},{3,7},{15,11},{16,20},{28,... | collective-permute-start | bytes 3145736 | tf_op jit(solution)/shard_map/ppermute | solution.py:480
  75.7 0.7 collective-permute-start.7
  76.5 1.3 bitcast_convert_fusion
  77.7 1.2 bitcast_convert_fusion.1.ids_3
  79.0 8.7 %place_first.1 = (bf16[4096,1024]{1,0:T(8,128)(2,1)}, bf16[1024,4096]{1,0:T(8,128)(2,1)}) custom-call(s32[4]{0:T(128)} %pad_add_fusion.place_of, s32[64]{0:T(128)} %ids.7, s32[64]{0:T(128)} %get-tuple-element.112.ids_1, s32[64]{0:T(128)} %get-tuple-element.111.ids_2, s32[64]{0:T(128)} %bitcast_convert_fusion.1.ids_3, bf16[64,128,128]{2,1,0:T(8,128)(2,1)} %own.1, ...), custom_call_target="tpu_custom_call" | custom-call | bytes 25165824 | tf_op jit(solution)/shard_map/place_first/pallas_call | solution.py:181
  87.7 8.2 %collective-permute-done.5.near_b = bf16[32,128,128]{2,1,0:T(8,128)(2,1)S(1)} collective-permute-done((bf16[32,128,128]{2,1,0:T(8,128)(2,1)}, bf16[32,128,128]{2,1,0:T(8,128)(2,1)S(1)}, u32[]{:S(2)}, u32[]{:S(2)}) %collective-permute-start.5) | collective-permute-done | bytes 1048608 | tf_op jit(solution)/shard_map/ppermute | solution.py:480
  95.9 1.0 copy-done.8
  96.8 0.7 collective-permute-start.10
  97.6 1.3 collective-permute-start.11
  98.9 3.8 %project_back.1 = (bf16[2,256,1024]{2,1,0:T(8,128)(2,1)}, bf16[2,256,1024]{2,1,0:T(8,128)(2,1)}, bf16[2,256,1024]{2,1,0:T(8,128)(2,1)}, bf16[256,1024]{1,0:T(8,128)(2,1)}, bf16[256,1024]{1,0:T(8,128)(2,1)}) custom-call(s32[4]{0:T(128)} %pad_add_fusion.place_of, s32[64]{0:T(128)} %get-tuple-element.112.ids_1, s32[64]{0:T(128)} %bitcast_convert_fusion.1.ids_3, ...), custom_call_target="tpu_custom_call" | custom-call | flops 4294967296 | bytes 13631488 | tf_op jit(solution)/shard_map/project_back/pallas_call | solution.py:239
  102.8 0.5 collective-permute-start.9
  103.3 1.6 collective-permute-done.8.refs_0_
  104.9 0.9 collective-permute-done.9.refs_1_
  105.8 3.0 %add_split.2 = (bf16[256,1024]{1,0:T(8,128)(2,1)}, bf16[256,1024]{1,0:T(8,128)(2,1)}) custom-call(s32[4]{0:T(128)} %pad_add_fusion.place_of, bf16[2,256,1024]{2,1,0:T(8,128)(2,1)} %get-tuple-element.72.keep, bf16[256,1024]{1,0:T(8,128)(2,1)} %copy-done.16, bf16[256,1024]{1,0:T(8,128)(2,1)} %collective-permute-done.9.refs_1_), custom_call_target="tpu_custom_call" | custom-call | flops 524288 | bytes 3145728 | tf_op jit(solution)/shard_map/add_split/pallas_call | solution.py:328
  108.8 13.9 %collective-permute-done.11.refs_3_ = bf16[512,1024]{1,0:T(8,128)(2,1)S(1)} collective-permute-done((bf16[512,1024]{1,0:T(8,128)(2,1)S(1)}, bf16[512,1024]{1,0:T(8,128)(2,1)S(1)}, u32[]{:S(2)}, u32[]{:S(2)}) %collective-permute-start.11) | collective-permute-done | bytes 1048608 | tf_op jit(solution)/shard_map/ppermute | solution.py:493
  122.8 1.0 slice_add_fusion.1
  123.8 1.6 collective-permute-start.12
  125.3 3.9 %project_forward.1 = (bf16[256,1024]{1,0:T(8,128)(2,1)}, bf16[256,1024]{1,0:T(8,128)(2,1)}) custom-call(s32[4]{0:T(128)} %pad_add_fusion.place_of, s32[64]{0:T(128)} %get-tuple-element.112.ids_1, s32[64]{0:T(128)} %bitcast_convert_fusion.1.ids_3, bf16[4096,1024]{1,0:T(8,128)(2,1)} %get-tuple-element.85.partial, bf16[32,128,128]{2,1,0:T(8,128)(2,1)} %copy-done.8, ...), custom_call_target="tpu_custom_call" | custom-call | flops 536870912 | bytes 4194304 | tf_op jit(solution)/shard_map/project_forward/pallas_call | solution.py:296
  129.2 1.3 collective-permute-start.16
  130.6 3.2 %add_split.3 = (bf16[256,1024]{1,0:T(8,128)(2,1)}, bf16[256,1024]{1,0:T(8,128)(2,1)}) custom-call(s32[4]{0:T(128)} %pad_add_fusion.place_of, bf16[2,256,1024]{2,1,0:T(8,128)(2,1)} %get-tuple-element.81.keep, bf16[2,256,1024]{2,1,0:T(8,128)(2,1)} %collective-permute-done.13.refs_0_), custom_call_target="tpu_custom_call" | custom-call | flops 524288 | bytes 3145728 | tf_op jit(solution)/shard_map/add_split/pallas_call | solution.py:328
  133.8 8.9 %collective-permute-done.12 = bf16[256,1024]{1,0:T(8,128)(2,1)} collective-permute-done((bf16[256,1024]{1,0:T(8,128)(2,1)}, bf16[256,1024]{1,0:T(8,128)(2,1)}, u32[]{:S(2)}, u32[]{:S(2)}) %collective-permute-start.12) | collective-permute-done | bytes 524320 | tf_op jit(solution)/shard_map/ppermute | solution.py:503
  142.7 7.1 %all-gather.9.cloned.1.call-done = bf16[512,1024]{1,0:T(8,128)(2,1)} async-done(((bf16[256,1024]{1,0:T(8,128)(2,1)}), bf16[512,1024]{1,0:T(8,128)(2,1)}) %all-gather.9.cloned.1.call-update) | async-done | bytes 1048592 | tf_op jit(solution)/shard_map/all_gather | solution.py:506
  149.9 2.2 add.29
  152.1 1.5 collective-permute-start.14
  153.6 1.6 collective-permute-start.15
  155.1 7.8 %line_grads.5.refs_4_ = bf16[64,128,128]{2,1,0:T(8,128)(2,1)} custom-call(s32[4]{0:T(128)} %pad_add_fusion.place_of, s32[64]{0:T(128)} %ids.7, bf16[4,256,1024]{2,1,0:T(8,128)(2,1)} %bitcast.17, bf16[256,1024]{1,0:T(8,128)(2,1)} %get-tuple-element.109.end_upstream.refs_1_, bf16[64,128,128]{2,1,0:T(8,128)(2,1)} %line_grads.4.refs_2_), custom_call_target="tpu_custom_call" | custom-call | flops 536870912 | bytes 6815744 | tf_op jit(solution)/shard_map/line_grads/pallas_call | solution.py:414
  163.0 2.6 %collective-permute-done.16.refs_3_ = bf16[512,1024]{1,0:T(8,128)(2,1)S(1)} collective-permute-done((bf16[512,1024]{1,0:T(8,128)(2,1)S(1)}, bf16[512,1024]{1,0:T(8,128)(2,1)S(1)}, u32[]{:S(2)}, u32[]{:S(2)}) %collective-permute-start.16) | collective-permute-done | bytes 1048608 | tf_op jit(solution)/shard_map/ppermute | solution.py:505
  165.6 10.9 %collective-permute-done.14 = bf16[256,1024]{1,0:T(8,128)(2,1)S(1)} collective-permute-done((bf16[256,1024]{1,0:T(8,128)(2,1)}, bf16[256,1024]{1,0:T(8,128)(2,1)S(1)}, u32[]{:S(2)}, u32[]{:S(2)}) %collective-permute-start.14) | collective-permute-done | bytes 524320 | tf_op jit(solution)/shard_map/ppermute | solution.py:512
  176.6 0.8 copy-done.15
  177.4 0.9 slice_add_fusion
  178.3 1.3 collective-permute-start.20
  179.6 1.4 add_select_fusion.own
  181.1 0.3 collective-permute-start.18
  181.4 8.7 %line_grads.6.refs_4_ = bf16[64,128,128]{2,1,0:T(8,128)(2,1)} custom-call(s32[4]{0:T(128)} %pad_add_fusion.place_of, s32[64]{0:T(128)} %ids.7, bf16[2,256,1024]{2,1,0:T(8,128)(2,1)} %bitcast.19, bf16[2,256,1024]{2,1,0:T(8,128)(2,1)} %copy-done.9, bf16[512,1024]{1,0:T(8,128)(2,1)} %copy-done.2, bf16[512,1024]{1,0:T(8,128)(2,1)} %copy-done.3, ...), custom_call_target="tpu_custom_call" | custom-call | flops 536870912 | bytes 8388608 | tf_op jit(solution)/shard_map/line_grads/pallas_call | solution.py:414
  190.1 4.0 %collective-permute-done.20 = bf16[256,1024]{1,0:T(8,128)(2,1)S(1)} collective-permute-done((bf16[256,1024]{1,0:T(8,128)(2,1)}, bf16[256,1024]{1,0:T(8,128)(2,1)S(1)}, u32[]{:S(2)}, u32[]{:S(2)}) %collective-permute-start.20) | collective-permute-done | bytes 524320 | tf_op jit(solution)/shard_map/ppermute | solution.py:522
  194.1 8.8 %collective-permute-done.18.by_tensor = bf16[256,1024]{1,0:T(8,128)(2,1)S(1)} collective-permute-done((bf16[256,1024]{1,0:T(8,128)(2,1)S(1)}, bf16[256,1024]{1,0:T(8,128)(2,1)S(1)}, u32[]{:S(2)}, u32[]{:S(2)}) %collective-permute-start.18) | collective-permute-done | bytes 524320 | tf_op jit(solution)/shard_map/ppermute | solution.py:527
  203.0 3.4 %all-gather.11.cloned.1.call-done = bf16[512,1024]{1,0:T(8,128)(2,1)} async-done(((bf16[256,1024]{1,0:T(8,128)(2,1)}), bf16[512,1024]{1,0:T(8,128)(2,1)}) %all-gather.11.cloned.1.call-update) | async-done | bytes 1048592 | tf_op jit(solution)/shard_map/all_gather | solution.py:520
  206.4 0.5 collective-permute-start.21
  206.8 1.9 broadcast_select_fusion
  208.7 0.8 collective-permute-done.21.by_both
  209.5 0.8 copy-done.17
  210.4 3.0 %assemble.1 = bf16[256,4096]{1,0:T(8,128)(2,1)} custom-call(s32[4]{0:T(128)} %pad_add_fusion.place_of, bf16[256,1024]{1,0:T(8,128)(2,1)} %copy-done.5, bf16[256,1024]{1,0:T(8,128)(2,1)} %copy-done.14, bf16[256,1024]{1,0:T(8,128)(2,1)} %copy-done.13, bf16[256,1024]{1,0:T(8,128)(2,1)} %copy-done.17), custom_call_target="tpu_custom_call" | custom-call | bytes 4194304 | tf_op jit(solution)/shard_map/assemble/pallas_call | solution.py:353
  213.4 1.0 copy-done.10
  214.3 8.5 %line_grads.7 = bf16[64,128,128]{2,1,0:T(8,128)(2,1)} custom-call(s32[4]{0:T(128)} %pad_add_fusion.place_of, s32[64]{0:T(128)} %ids.7, bf16[2,256,1024]{2,1,0:T(8,128)(2,1)} %bitcast.21, bf16[2,256,1024]{2,1,0:T(8,128)(2,1)} %copy-done.10, bf16[512,1024]{1,0:T(8,128)(2,1)} %copy-done.1, bf16[512,1024]{1,0:T(8,128)(2,1)} %copy-done.4, ...), custom_call_target="tpu_custom_call" | custom-call | flops 536870912 | bytes 8388608 | tf_op jit(solution)/shard_map/line_grads/pallas_call | solution.py:414
  (59 shorter events, 0.5 us)
Async XLA Ops:
  7.2 89.7 %all-gather.7.cloned.1.call-start = ((), (), s32[]{:S(2)}) async-start(), calls=%async_computation | async-start | bytes 2621440 | tf_op jit(solution)/shard_map/all_gather | solution.py:483
  10.4 28.3 %collective-permute-start = (bf16[33,128,128]{2,1,0:T(8,128)(2,1)}, bf16[33,128,128]{2,1,0:T(8,128)(2,1)S(1)}, u32[]{:S(2)}, u32[]{:S(2)}) collective-permute-start(bf16[33,128,128]{2,1,0:T(8,128)(2,1)} %pad_maximum_fusion), channel_id=1, source_target_pairs={{0,4},{12,8},{1,5},{13,9},{2,6},{14,10},{3,7},{15,11},{16,20},{28,... | collective-permute-start | bytes 3244040 | tf_op jit(solution)/shard_map/ppermute | solution.py:466
  15.4 23.4 %collective-permute-start.1 = (bf16[33,128,128]{2,1,0:T(8,128)(2,1)}, bf16[33,128,128]{2,1,0:T(8,128)(2,1)}, u32[]{:S(2)}, u32[]{:S(2)}) collective-permute-start(bf16[33,128,128]{2,1,0:T(8,128)(2,1)} %pad_maximum_fusion), channel_id=1, source_target_pairs={{4,8},{8,4},{5,9},{9,5},{6,10},{10,6},{7,11},{11,7},{20,24},{24,20... | collective-permute-start | bytes 3244040 | tf_op jit(solution)/shard_map/ppermute | solution.py:467
  17.6 8.1 %copy-start.6 = (bf16[256,1024]{1,0:T(8,128)(2,1)S(1)}, bf16[256,1024]{1,0:T(8,128)(2,1)}, u32[]{:S(2)}) copy-start(bf16[256,1024]{1,0:T(8,128)(2,1)} %upstream.1) | copy-start | bytes 1572868
  24.5 1.8 copy-start
  26.3 45.1 %copy-start.12 = (bf16[512,1024]{1,0:T(8,128)(2,1)}, bf16[512,1024]{1,0:T(8,128)(2,1)S(1)}, u32[]{:S(2)}) copy-start(bf16[512,1024]{1,0:T(8,128)(2,1)S(1)} %pad_maximum_fusion.1) | copy-start | bytes 3145732
  38.7 40.2 %copy-start.7 = (bf16[33,128,128]{2,1,0:T(8,128)(2,1)}, bf16[33,128,128]{2,1,0:T(8,128)(2,1)S(1)}, u32[]{:S(2)}) copy-start(bf16[33,128,128]{2,1,0:T(8,128)(2,1)S(1)} %collective-permute-done.near_a) | copy-start | bytes 3244036
  38.7 30.6 %collective-permute-start.3 = (bf16[33,128,128]{2,1,0:T(8,128)(2,1)S(1)}, bf16[33,128,128]{2,1,0:T(8,128)(2,1)}, u32[]{:S(2)}, u32[]{:S(2)}) collective-permute-start(bf16[33,128,128]{2,1,0:T(8,128)(2,1)S(1)} %collective-permute-done.near_a), channel_id=1, source_target_pairs={{4,8},{8,4},{5,9},{9,5},{6,10},{10,6},{7,11},{11,7},{20,24},{24,20... | collective-permute-start | bytes 3244040 | tf_op jit(solution)/shard_map/ppermute | solution.py:474
  40.4 28.9 %collective-permute-start.4 = (bf16[33,128,128]{2,1,0:T(8,128)(2,1)}, bf16[33,128,128]{2,1,0:T(8,128)(2,1)}, u32[]{:S(2)}, u32[]{:S(2)}) collective-permute-start(bf16[33,128,128]{2,1,0:T(8,128)(2,1)} %collective-permute-done.1.far_a), channel_id=1, source_target_pairs={{0,16},{16,0},{1,17},{17,1},{2,18},{18,2},{3,19},{19,3},{4,20},{20... | collective-permute-start | bytes 3244040 | tf_op jit(solution)/shard_map/ppermute | solution.py:475
  41.9 27.4 %collective-permute-start.2 = (bf16[512,1024]{1,0:T(8,128)(2,1)S(1)}, bf16[512,1024]{1,0:T(8,128)(2,1)S(1)}, u32[]{:S(2)}, u32[]{:S(2)}) collective-permute-start(bf16[512,1024]{1,0:T(8,128)(2,1)S(1)} %pad_maximum_fusion.1), channel_id=1, source_target_pairs={{0,4},{12,8},{4,0},{8,12},{1,5},{13,9},{5,1},{9,13},{2,6},{14,10},... | collective-permute-start | bytes 3145736 | tf_op jit(solution)/shard_map/ppermute | solution.py:476
  69.3 1.0 copy-start.11
  71.4 78.4 %all-gather.9.cloned.1.call-start = ((), (), s32[]{:S(2)}) async-start(), calls=%async_computation.1 | async-start | bytes 1572864 | tf_op jit(solution)/shard_map/all_gather | solution.py:506
  71.5 25.4 %collective-permute-start.6 = (bf16[33,128,128]{2,1,0:T(8,128)(2,1)}, bf16[33,128,128]{2,1,0:T(8,128)(2,1)}, u32[]{:S(2)}, u32[]{:S(2)}) collective-permute-start(bf16[33,128,128]{2,1,0:T(8,128)(2,1)} %collective-permute-done.3.end_a), channel_id=1, source_target_pairs={{0,16},{16,0},{1,17},{17,1},{2,18},{18,2},{3,19},{19,3},{4,20},{20... | collective-permute-start | bytes 3244040 | tf_op jit(solution)/shard_map/ppermute | solution.py:481
  72.0 23.8 %collective-permute-start.5 = (bf16[32,128,128]{2,1,0:T(8,128)(2,1)}, bf16[32,128,128]{2,1,0:T(8,128)(2,1)S(1)}, u32[]{:S(2)}, u32[]{:S(2)}) collective-permute-start(bf16[32,128,128]{2,1,0:T(8,128)(2,1)} %constant_dynamic-slice_fusion), channel_id=1, source_target_pairs={{0,4},{12,8},{1,5},{13,9},{2,6},{14,10},{3,7},{15,11},{16,20},{28,... | collective-permute-start | bytes 3145736 | tf_op jit(solution)/shard_map/ppermute | solution.py:480
  75.7 20.1 %collective-permute-start.7 = (bf16[512,1024]{1,0:T(8,128)(2,1)}, bf16[512,1024]{1,0:T(8,128)(2,1)S(1)}, u32[]{:S(2)}, u32[]{:S(2)}) collective-permute-start(bf16[512,1024]{1,0:T(8,128)(2,1)} %copy-done.12), channel_id=1, source_target_pairs={{4,8},{8,4},{5,9},{9,5},{6,10},{10,6},{7,11},{11,7},{20,24},{24,20... | collective-permute-start | bytes 3145736 | tf_op jit(solution)/shard_map/ppermute | solution.py:482
  95.9 1.0 copy-start.8
  96.8 25.9 %copy-start.2 = (bf16[512,1024]{1,0:T(8,128)(2,1)}, bf16[512,1024]{1,0:T(8,128)(2,1)S(1)}, u32[]{:S(2)}) copy-start(bf16[512,1024]{1,0:T(8,128)(2,1)S(1)} %collective-permute-done.7.refs_2_) | copy-start | bytes 3145732
  96.8 12.0 %collective-permute-start.10 = (bf16[512,1024]{1,0:T(8,128)(2,1)}, bf16[512,1024]{1,0:T(8,128)(2,1)S(1)}, u32[]{:S(2)}, u32[]{:S(2)}) collective-permute-start(bf16[512,1024]{1,0:T(8,128)(2,1)} %copy-done.11), channel_id=1, source_target_pairs={{4,8},{8,4},{5,9},{9,5},{6,10},{10,6},{7,11},{11,7},{20,24},{24,20... | collective-permute-start | bytes 3145736 | tf_op jit(solution)/shard_map/ppermute | solution.py:492
  97.6 25.2 %collective-permute-start.11 = (bf16[512,1024]{1,0:T(8,128)(2,1)S(1)}, bf16[512,1024]{1,0:T(8,128)(2,1)S(1)}, u32[]{:S(2)}, u32[]{:S(2)}) collective-permute-start(bf16[512,1024]{1,0:T(8,128)(2,1)S(1)} %collective-permute-done.7.refs_2_), channel_id=1, source_target_pairs={{4,0},{8,12},{5,1},{9,13},{6,2},{10,14},{7,3},{11,15},{20,16},{24,... | collective-permute-start | bytes 3145736 | tf_op jit(solution)/shard_map/ppermute | solution.py:493
  102.7 2.2 collective-permute-start.8
  102.8 3.0 %collective-permute-start.9 = (bf16[256,1024]{1,0:T(8,128)(2,1)}, bf16[256,1024]{1,0:T(8,128)(2,1)}, u32[]{:S(2)}, u32[]{:S(2)}) collective-permute-start(bf16[256,1024]{1,0:T(8,128)(2,1)} %get-tuple-element.74), channel_id=1, source_target_pairs={{0,1},{1,0},{2,3},{3,2},{4,5},{5,4},{6,7},{7,6},{8,9},{9,8},{10,11... | collective-permute-start | bytes 1572872 | tf_op jit(solution)/shard_map/ppermute | solution.py:498
  104.9 0.9 copy-start.16
  108.8 67.8 %copy-start.1 = (bf16[512,1024]{1,0:T(8,128)(2,1)}, bf16[512,1024]{1,0:T(8,128)(2,1)S(1)}, u32[]{:S(2)}) copy-start(bf16[512,1024]{1,0:T(8,128)(2,1)S(1)} %collective-permute-done.10.refs_2_) | copy-start | bytes 3145732
  122.7 6.5 %copy-start.3 = (bf16[512,1024]{1,0:T(8,128)(2,1)}, bf16[512,1024]{1,0:T(8,128)(2,1)S(1)}, u32[]{:S(2)}) copy-start(bf16[512,1024]{1,0:T(8,128)(2,1)S(1)} %collective-permute-done.11.refs_3_) | copy-start | bytes 3145732
  122.7 7.8 %collective-permute-start.13 = (bf16[2,256,1024]{2,1,0:T(8,128)(2,1)}, bf16[2,256,1024]{2,1,0:T(8,128)(2,1)}, u32[]{:S(2)}, u32[]{:S(2)}) collective-permute-start(bf16[2,256,1024]{2,1,0:T(8,128)(2,1)} %get-tuple-element.82), channel_id=1, source_target_pairs={{0,1},{1,0},{2,3},{3,2},{4,5},{5,4},{6,7},{7,6},{8,9},{9,8},{10,11... | collective-permute-start | bytes 3145736 | tf_op jit(solution)/shard_map/ppermute | solution.py:504
  123.7 82.6 %all-gather.11.cloned.1.call-start = ((), (), s32[]{:S(2)}) async-start(), calls=%async_computation.2 | async-start | bytes 1572864 | tf_op jit(solution)/shard_map/all_gather | solution.py:520
  123.8 18.9 %collective-permute-start.12 = (bf16[256,1024]{1,0:T(8,128)(2,1)}, bf16[256,1024]{1,0:T(8,128)(2,1)}, u32[]{:S(2)}, u32[]{:S(2)}) collective-permute-start(bf16[256,1024]{1,0:T(8,128)(2,1)} %get-tuple-element.80), channel_id=1, source_target_pairs={{0,2},{2,0},{1,3},{3,1},{4,6},{6,4},{5,7},{7,5},{8,10},{10,8},{9,1... | collective-permute-start | bytes 1572872 | tf_op jit(solution)/shard_map/ppermute | solution.py:503
  129.2 36.4 %collective-permute-start.16 = (bf16[512,1024]{1,0:T(8,128)(2,1)S(1)}, bf16[512,1024]{1,0:T(8,128)(2,1)S(1)}, u32[]{:S(2)}, u32[]{:S(2)}) collective-permute-start(bf16[512,1024]{1,0:T(8,128)(2,1)S(1)} %collective-permute-done.10.refs_2_), channel_id=1, source_target_pairs={{4,0},{8,12},{5,1},{9,13},{6,2},{10,14},{7,3},{11,15},{20,16},{24,... | collective-permute-start | bytes 3145736 | tf_op jit(solution)/shard_map/ppermute | solution.py:505
  149.8 26.8 %collective-permute-start.17 = (bf16[2,256,1024]{2,1,0:T(8,128)(2,1)}, bf16[2,256,1024]{2,1,0:T(8,128)(2,1)S(1)}, u32[]{:S(2)}, u32[]{:S(2)}) collective-permute-start(bf16[2,256,1024]{2,1,0:T(8,128)(2,1)} %bitcast.18), channel_id=1, source_target_pairs={{0,1},{1,0},{2,3},{3,2},{4,5},{5,4},{6,7},{7,6},{8,9},{9,8},{10,11... | collective-permute-start | bytes 3145736 | tf_op jit(solution)/shard_map/ppermute | solution.py:515
  152.1 24.5 %collective-permute-start.14 = (bf16[256,1024]{1,0:T(8,128)(2,1)}, bf16[256,1024]{1,0:T(8,128)(2,1)S(1)}, u32[]{:S(2)}, u32[]{:S(2)}) collective-permute-start(bf16[256,1024]{1,0:T(8,128)(2,1)} %add.29), channel_id=1, source_target_pairs={{4,0},{8,12},{5,1},{9,13},{6,2},{10,14},{7,3},{11,15},{20,16},{24,... | collective-permute-start | bytes 1572872 | tf_op jit(solution)/shard_map/ppermute | solution.py:512
  153.6 23.0 %collective-permute-start.15 = (bf16[256,1024]{1,0:T(8,128)(2,1)}, bf16[256,1024]{1,0:T(8,128)(2,1)}, u32[]{:S(2)}, u32[]{:S(2)}) collective-permute-start(bf16[256,1024]{1,0:T(8,128)(2,1)} %get-tuple-element.94), channel_id=1, source_target_pairs={{0,2},{2,0},{1,3},{3,1},{4,6},{6,4},{5,7},{7,5},{8,10},{10,8},{9,1... | collective-permute-start | bytes 1572872 | tf_op jit(solution)/shard_map/ppermute | solution.py:513
  165.6 15.5 %copy-start.4 = (bf16[512,1024]{1,0:T(8,128)(2,1)}, bf16[512,1024]{1,0:T(8,128)(2,1)S(1)}, u32[]{:S(2)}) copy-start(bf16[512,1024]{1,0:T(8,128)(2,1)S(1)} %collective-permute-done.16.refs_3_) | copy-start | bytes 3145732
  176.6 0.8 copy-start.15
  177.4 3.7 %copy-start.9 = (bf16[2,256,1024]{2,1,0:T(8,128)(2,1)}, bf16[2,256,1024]{2,1,0:T(8,128)(2,1)S(1)}, u32[]{:S(2)}) copy-start(bf16[2,256,1024]{2,1,0:T(8,128)(2,1)S(1)} %collective-permute-done.17.refs_1_) | copy-start | bytes 3145732
  178.3 15.8 %collective-permute-start.20 = (bf16[256,1024]{1,0:T(8,128)(2,1)}, bf16[256,1024]{1,0:T(8,128)(2,1)S(1)}, u32[]{:S(2)}, u32[]{:S(2)}) collective-permute-start(bf16[256,1024]{1,0:T(8,128)(2,1)} %get-tuple-element.103), channel_id=1, source_target_pairs={{4,0},{8,12},{5,1},{9,13},{6,2},{10,14},{7,3},{11,15},{20,16},{24,... | collective-permute-start | bytes 1572872 | tf_op jit(solution)/shard_map/ppermute | solution.py:522
  181.1 9.0 %copy-start.5 = (bf16[256,1024]{1,0:T(8,128)(2,1)}, bf16[256,1024]{1,0:T(8,128)(2,1)S(1)}, u32[]{:S(2)}) copy-start(bf16[256,1024]{1,0:T(8,128)(2,1)S(1)} %add_select_fusion.own) | copy-start | bytes 1572868
  181.1 21.8 %collective-permute-start.18 = (bf16[256,1024]{1,0:T(8,128)(2,1)S(1)}, bf16[256,1024]{1,0:T(8,128)(2,1)S(1)}, u32[]{:S(2)}, u32[]{:S(2)}) collective-permute-start(bf16[256,1024]{1,0:T(8,128)(2,1)S(1)} %add_select_fusion.own), channel_id=1, source_target_pairs={{0,2},{2,0},{1,3},{3,1},{4,6},{6,4},{5,7},{7,5},{8,10},{10,8},{9,1... | collective-permute-start | bytes 1572872 | tf_op jit(solution)/shard_map/ppermute | solution.py:527
  181.4 25.5 %copy-start.18 = (bf16[256,1024]{1,0:T(8,128)(2,1)S(1)}, bf16[256,1024]{1,0:T(8,128)(2,1)}, u32[]{:S(2)}) copy-start(bf16[256,1024]{1,0:T(8,128)(2,1)} %get-tuple-element.90) | copy-start | bytes 1572868
  181.4 21.6 %collective-permute-start.19 = (bf16[256,1024]{1,0:T(8,128)(2,1)S(1)}, bf16[256,1024]{1,0:T(8,128)(2,1)S(1)}, u32[]{:S(2)}, u32[]{:S(2)}) collective-permute-start(bf16[256,1024]{1,0:T(8,128)(2,1)S(1)} %add_select_fusion.own), channel_id=1, source_target_pairs={{0,1},{1,0},{2,3},{3,2},{4,5},{5,4},{6,7},{7,6},{8,9},{9,8},{10,11... | collective-permute-start | bytes 1572872 | tf_op jit(solution)/shard_map/ppermute | solution.py:527
  194.1 8.9 %copy-start.19 = (bf16[256,1024]{1,0:T(8,128)(2,1)}, bf16[256,1024]{1,0:T(8,128)(2,1)S(1)}, u32[]{:S(2)}) copy-start(bf16[256,1024]{1,0:T(8,128)(2,1)S(1)} %collective-permute-done.20) | copy-start | bytes 1572868
  202.9 6.6 %copy-start.13 = (bf16[256,1024]{1,0:T(8,128)(2,1)}, bf16[256,1024]{1,0:T(8,128)(2,1)S(1)}, u32[]{:S(2)}) copy-start(bf16[256,1024]{1,0:T(8,128)(2,1)S(1)} %collective-permute-done.18.by_tensor) | copy-start | bytes 1572868
  202.9 6.6 %copy-start.14 = (bf16[256,1024]{1,0:T(8,128)(2,1)}, bf16[256,1024]{1,0:T(8,128)(2,1)S(1)}, u32[]{:S(2)}) copy-start(bf16[256,1024]{1,0:T(8,128)(2,1)S(1)} %collective-permute-done.19.by_core) | copy-start | bytes 1572868
  206.3 7.0 %collective-permute-start.22 = (bf16[2,256,1024]{2,1,0:T(8,128)(2,1)}, bf16[2,256,1024]{2,1,0:T(8,128)(2,1)S(1)}, u32[]{:S(2)}, u32[]{:S(2)}) collective-permute-start(bf16[2,256,1024]{2,1,0:T(8,128)(2,1)} %bitcast.20), channel_id=1, source_target_pairs={{0,1},{1,0},{2,3},{3,2},{4,5},{5,4},{6,7},{7,6},{8,9},{9,8},{10,11... | collective-permute-start | bytes 3145736 | tf_op jit(solution)/shard_map/ppermute | solution.py:533
  206.4 3.2 %collective-permute-start.21 = (bf16[256,1024]{1,0:T(8,128)(2,1)S(1)}, bf16[256,1024]{1,0:T(8,128)(2,1)S(1)}, u32[]{:S(2)}, u32[]{:S(2)}) collective-permute-start(bf16[256,1024]{1,0:T(8,128)(2,1)S(1)} %collective-permute-done.18.by_tensor), channel_id=1, source_target_pairs={{0,1},{1,0},{2,3},{3,2},{4,5},{5,4},{6,7},{7,6},{8,9},{9,8},{10,11... | collective-permute-start | bytes 1572872 | tf_op jit(solution)/shard_map/ppermute | solution.py:529
  209.5 0.8 copy-start.17
  213.4 1.0 copy-start.10
Sparse Core Ops, SparseCore 0:
  71.5 21.0 all-gather.6
  123.9 25.9 all-gather.8
  178.5 27.8 all-gather.10

commit v20 on v17

--- a/solution.py
+++ b/solution.py
@@ -502,25 +502,24 @@
     both_3o = along(both_3m, perm=OUTWARD)
     tokens_2 = lax.all_gather(both_2m[:rows] + both_2o[:rows], INNER)
     proj, end_proj = project_forward(place_of, ids_1, ids_3, partial, *last, tokens, tokens_1)
-    end_got, own_give, own_keep, proj, end_proj = stage(
-        (end_got, own_give, own_keep, proj, end_proj)
+    end_got, own_give, own_keep, proj, end_proj, both_3m = stage(
+        (end_got, own_give, own_keep, proj, end_proj, both_3m)
     )
 
     sum_out = along(end_keep + end_got, perm=OUTWARD)
     own_got = sideways(own_give)
-    part_3, upstream_1 = stage((both_3m[:rows] + both_3o[:rows], upstream_1))
-    tokens_3 = lax.all_gather(part_3, INNER)
     grads = line_grads(block_ids, ((tokens_1, upstream_1),), grads, size)
+    tokens_3 = lax.all_gather(both_3m[:rows] + both_3o[:rows], INNER)
     sum_out, own_got, grads = stage((sum_out, own_got, grads))
 
     quarter = jnp.where(middle, own_keep + own_got, sum_out)
     proj_out = along(end_proj, perm=OUTWARD)
     grads = line_grads(block_ids, ((tokens_2, both_2m, both_2o),), grads, size)
+    grads = line_grads(block_ids, ((tokens_3, both_3m, both_3o),), grads, size)
     by_tensor, by_core, grads = stage((sideways(quarter), cores(quarter), grads))
     by_both = cores(by_tensor)
     projected = jnp.where(middle, proj, proj_out)
     token_grad = assemble(place_of, (quarter, by_core, by_tensor, by_both))
-    grads = line_grads(block_ids, ((tokens_3, both_3m, both_3o),), grads, size)
     return projected, token_grad, grads
 
 

time: 226 us -> 210 us (0.929)
  waiting for transfers between devices: 105 us -> 85.9 us
    ppermute x1, waiting for transfers between devices: 24.7 us -> 5.22 us  [line_body(): both_3o = along(both_3m, perm=OUTWARD)]
    ppermute x1, waiting for transfers between devices: 4.57 us -> 0.01 us  [line_body(): proj_out = along(end_proj, perm=OUTWARD)]
    ppermute x1, waiting for transfers between devices: 2.23 us -> 5.43 us  [line_body(): own_got = sideways(own_give)]
  transfers between devices with their start and end apart: 24 -> 24, of which waited for: 12 -> 11; matrix products, arithmetic and copies ran while one was open for 3% -> 4% of each run, Pallas kernels for 22% -> 26%
where the time goes in v20:
time: 210 us; the launch traced here: 208 us
  waiting for transfers between devices  85.9 us (41%)
  Pallas kernels  57.3 us (27%)
  starting transfers between devices  33.6 us (16%)
  between operations  14 us (7%)
  other arithmetic  8.9 us (4%)
  local copies, waits for them, and re-layouts  8.13 us (4%)
    pallas_call x4, Pallas kernels, line_grads(): pl.pallas_call(functools.partial(line_grads_kernel, len(pairs)), out_shap...  31.6 us
    ppermute x1, waiting for transfers between devices, line_body(): both_1 = along(both, perm=PAIRS)  21.7 us
    ppermute x1, waiting for transfers between devices, line_body(): both_2o = along(both_2m, perm=OUTWARD)  13.9 us
    ppermute x1, waiting for transfers between devices, line_body(): end_got = sideways(end_give)  12.2 us
    ppermute x1, waiting for transfers between devices, line_body(): near_a = along(mine, perm=INWARD)  11.8 us
    pallas_call x1, Pallas kernels, place_first(): pl.pallas_call(place_kernel, out_shape=(jax.ShapeDtypeStruct((depth, widt...  8.74 us
    ppermute x1, waiting for transfers between devices, line_body(): near_b = along(other, perm=INWARD)  7.55 us
    pallas_call x2, Pallas kernels, add_split(): pl.pallas_call(split_kernel, out_shape=(out, out), in_specs=[whole(pltpu....  6.24 us
  transfers between devices with their start and end apart: 24, of which 11 were waited for; matrix products, arithmetic and copies ran while one was open for 4% of the time, Pallas kernels for 26%

profile of v20, /device:TPU:0, one launch (start us, length us, event | category | flops | bytes accessed | tf_op | source)
XLA Modules:
  0.0 207.7 jit_solution(3365186202418869183)
XLA Ops:
  7.2 0.0 all-gather.7.cloned.1.call-start
  7.2 0.7 convert_element_type.26
  7.9 0.1 convert_element_type.27
  8.0 1.3 constant_dynamic-slice_fusion.2
  9.3 1.1 pad_maximum_fusion
  10.4 5.0 %collective-permute-start = (bf16[33,128,128]{2,1,0:T(8,128)(2,1)}, bf16[33,128,128]{2,1,0:T(8,128)(2,1)S(1)}, u32[]{:S(2)}, u32[]{:S(2)}) collective-permute-start(bf16[33,128,128]{2,1,0:T(8,128)(2,1)} %pad_maximum_fusion), channel_id=1, source_target_pairs={{0,4},{12,8},{1,5},{13,9},{2,6},{14,10},{3,7},{15,11},{16,20},{28,... | collective-permute-start | bytes 3244040 | tf_op jit(solution)/shard_map/ppermute | solution.py:463
  15.4 1.7 collective-permute-start.1
  17.1 6.9 %line_grads.4.refs_2_ = bf16[64,128,128]{2,1,0:T(8,128)(2,1)} custom-call(s32[64]{0:T(128)} %ids.7, bf16[256,4096]{1,0:T(8,128)(2,1)} %tokens.1, bf16[256,1024]{1,0:T(8,128)(2,1)} %upstream.1), custom_call_target="tpu_custom_call" | custom-call | flops 536870912 | bytes 4718592 | tf_op jit(solution)/shard_map/line_grads/pallas_call | solution.py:411
  24.0 1.2 constant_dynamic-slice_fusion.1
  25.2 0.1 pad_maximum_fusion.1
  25.3 0.4 copy-done
  25.7 1.2 constant_dynamic-slice_fusion
  26.9 11.8 %collective-permute-done.near_a = bf16[33,128,128]{2,1,0:T(8,128)(2,1)S(1)} collective-permute-done((bf16[33,128,128]{2,1,0:T(8,128)(2,1)}, bf16[33,128,128]{2,1,0:T(8,128)(2,1)S(1)}, u32[]{:S(2)}, u32[]{:S(2)}) %collective-permute-start) | collective-permute-done | bytes 1081376 | tf_op jit(solution)/shard_map/ppermute | solution.py:463
  38.7 1.7 collective-permute-start.3
  40.4 1.5 collective-permute-start.4
  41.9 5.7 %collective-permute-start.2 = (bf16[512,1024]{1,0:T(8,128)(2,1)S(1)}, bf16[512,1024]{1,0:T(8,128)(2,1)S(1)}, u32[]{:S(2)}, u32[]{:S(2)}) collective-permute-start(bf16[512,1024]{1,0:T(8,128)(2,1)S(1)} %pad_maximum_fusion.1), channel_id=1, source_target_pairs={{0,4},{12,8},{4,0},{8,12},{1,5},{13,9},{5,1},{9,13},{2,6},{14,10},... | collective-permute-start | bytes 3145736 | tf_op jit(solution)/shard_map/ppermute | solution.py:473
  47.6 21.7 %collective-permute-done.2 = bf16[512,1024]{1,0:T(8,128)(2,1)S(1)} collective-permute-done((bf16[512,1024]{1,0:T(8,128)(2,1)S(1)}, bf16[512,1024]{1,0:T(8,128)(2,1)S(1)}, u32[]{:S(2)}, u32[]{:S(2)}) %collective-permute-start.2) | collective-permute-done | bytes 1048608 | tf_op jit(solution)/shard_map/ppermute | solution.py:473
  69.3 1.0 copy-done.9
  70.4 1.0 fusion
  71.4 0.0 all-gather.11.cloned.1.call-start
  71.5 0.6 collective-permute-start.6
  72.0 3.7 %collective-permute-start.5 = (bf16[32,128,128]{2,1,0:T(8,128)(2,1)}, bf16[32,128,128]{2,1,0:T(8,128)(2,1)S(1)}, u32[]{:S(2)}, u32[]{:S(2)}) collective-permute-start(bf16[32,128,128]{2,1,0:T(8,128)(2,1)} %constant_dynamic-slice_fusion), channel_id=1, source_target_pairs={{0,4},{12,8},{1,5},{13,9},{2,6},{14,10},{3,7},{15,11},{16,20},{28,... | collective-permute-start | bytes 3145736 | tf_op jit(solution)/shard_map/ppermute | solution.py:477
  75.7 0.7 collective-permute-start.7
  76.5 0.7 pad_add_fusion.place_of
  77.2 1.2 bitcast_convert_fusion
  78.4 1.2 bitcast_convert_fusion.1.ids_3
  79.6 8.7 %place_first.1 = (bf16[4096,1024]{1,0:T(8,128)(2,1)}, bf16[1024,4096]{1,0:T(8,128)(2,1)}) custom-call(s32[4]{0:T(128)} %pad_add_fusion.place_of, s32[64]{0:T(128)} %ids.7, s32[64]{0:T(128)} %get-tuple-element.104.ids_1, s32[64]{0:T(128)} %get-tuple-element.103.ids_2, s32[64]{0:T(128)} %bitcast_convert_fusion.1.ids_3, bf16[64,128,128]{2,1,0:T(8,128)(2,1)} %own.1, ...), custom_call_target="tpu_custom_call" | custom-call | bytes 25165824 | tf_op jit(solution)/shard_map/place_first/pallas_call | solution.py:181
  88.3 7.6 %collective-permute-done.5.near_b = bf16[32,128,128]{2,1,0:T(8,128)(2,1)S(1)} collective-permute-done((bf16[32,128,128]{2,1,0:T(8,128)(2,1)}, bf16[32,128,128]{2,1,0:T(8,128)(2,1)S(1)}, u32[]{:S(2)}, u32[]{:S(2)}) %collective-permute-start.5) | collective-permute-done | bytes 1048608 | tf_op jit(solution)/shard_map/ppermute | solution.py:477
  95.9 0.9 copy-done.8
  96.8 0.7 collective-permute-start.10
  97.6 1.3 collective-permute-start.11
  98.9 3.8 %project_back.1 = (bf16[2,256,1024]{2,1,0:T(8,128)(2,1)}, bf16[2,256,1024]{2,1,0:T(8,128)(2,1)}, bf16[2,256,1024]{2,1,0:T(8,128)(2,1)}, bf16[256,1024]{1,0:T(8,128)(2,1)}, bf16[256,1024]{1,0:T(8,128)(2,1)}) custom-call(s32[4]{0:T(128)} %pad_add_fusion.place_of, s32[64]{0:T(128)} %get-tuple-element.104.ids_1, s32[64]{0:T(128)} %bitcast_convert_fusion.1.ids_3, ...), custom_call_target="tpu_custom_call" | custom-call | flops 4294967296 | bytes 13631488 | tf_op jit(solution)/shard_map/project_back/pallas_call | solution.py:239
  102.7 0.1 collective-permute-start.8
  102.8 0.5 collective-permute-start.9
  103.3 1.6 collective-permute-done.8.refs_0_
  104.9 0.9 collective-permute-done.9.refs_1_
  105.8 3.0 %add_split.2 = (bf16[256,1024]{1,0:T(8,128)(2,1)}, bf16[256,1024]{1,0:T(8,128)(2,1)}) custom-call(s32[4]{0:T(128)} %pad_add_fusion.place_of, bf16[2,256,1024]{2,1,0:T(8,128)(2,1)} %get-tuple-element.68.keep, bf16[256,1024]{1,0:T(8,128)(2,1)} %copy-done.16, bf16[256,1024]{1,0:T(8,128)(2,1)} %collective-permute-done.9.refs_1_), custom_call_target="tpu_custom_call" | custom-call | flops 524288 | bytes 3145728 | tf_op jit(solution)/shard_map/add_split/pallas_call | solution.py:328
  108.8 13.9 %collective-permute-done.11.refs_2_ = bf16[512,1024]{1,0:T(8,128)(2,1)S(1)} collective-permute-done((bf16[512,1024]{1,0:T(8,128)(2,1)S(1)}, bf16[512,1024]{1,0:T(8,128)(2,1)S(1)}, u32[]{:S(2)}, u32[]{:S(2)}) %collective-permute-start.11) | collective-permute-done | bytes 1048608 | tf_op jit(solution)/shard_map/ppermute | solution.py:490
  122.7 0.9 slice_add_fusion.1
  123.7 0.0 all-gather.9.cloned.1.call-start
  123.7 0.1 collective-permute-start.13
  123.8 1.3 collective-permute-start.19
  125.1 1.6 collective-permute-start.12
  126.7 3.9 %project_forward.1 = (bf16[256,1024]{1,0:T(8,128)(2,1)}, bf16[256,1024]{1,0:T(8,128)(2,1)}) custom-call(s32[4]{0:T(128)} %pad_add_fusion.place_of, s32[64]{0:T(128)} %get-tuple-element.104.ids_1, s32[64]{0:T(128)} %bitcast_convert_fusion.1.ids_3, bf16[4096,1024]{1,0:T(8,128)(2,1)} %get-tuple-element.81.partial, bf16[32,128,128]{2,1,0:T(8,128)(2,1)} %copy-done.8, ...), custom_call_target="tpu_custom_call" | custom-call | flops 536870912 | bytes 4194304 | tf_op jit(solution)/shard_map/project_forward/pallas_call | solution.py:296
  130.6 3.2 %add_split.3 = (bf16[256,1024]{1,0:T(8,128)(2,1)}, bf16[256,1024]{1,0:T(8,128)(2,1)}) custom-call(s32[4]{0:T(128)} %pad_add_fusion.place_of, bf16[2,256,1024]{2,1,0:T(8,128)(2,1)} %get-tuple-element.77.keep, bf16[2,256,1024]{2,1,0:T(8,128)(2,1)} %collective-permute-done.13.refs_0_), custom_call_target="tpu_custom_call" | custom-call | flops 524288 | bytes 3145728 | tf_op jit(solution)/shard_map/add_split/pallas_call | solution.py:328
  133.8 12.2 %collective-permute-done.12 = bf16[256,1024]{1,0:T(8,128)(2,1)S(1)} collective-permute-done((bf16[256,1024]{1,0:T(8,128)(2,1)}, bf16[256,1024]{1,0:T(8,128)(2,1)S(1)}, u32[]{:S(2)}, u32[]{:S(2)}) %collective-permute-start.12) | collective-permute-done | bytes 524320 | tf_op jit(solution)/shard_map/ppermute | solution.py:500
  146.0 5.2 %collective-permute-done.19.refs_2_ = bf16[512,1024]{1,0:T(8,128)(2,1)S(1)} collective-permute-done((bf16[512,1024]{1,0:T(8,128)(2,1)S(1)}, bf16[512,1024]{1,0:T(8,128)(2,1)S(1)}, u32[]{:S(2)}, u32[]{:S(2)}) %collective-permute-start.19) | collective-permute-done | bytes 1048608 | tf_op jit(solution)/shard_map/ppermute | solution.py:502
  151.3 0.9 slice_add_fusion
  152.2 1.2 add.28
  153.5 1.6 collective-permute-start.15
  155.1 1.6 collective-permute-start.16
  156.7 7.8 %line_grads.5.refs_3_ = bf16[64,128,128]{2,1,0:T(8,128)(2,1)} custom-call(s32[64]{0:T(128)} %ids.7, bf16[4,256,1024]{2,1,0:T(8,128)(2,1)} %bitcast.17, bf16[256,1024]{1,0:T(8,128)(2,1)} %get-tuple-element.101.end_upstream.refs_1_, bf16[64,128,128]{2,1,0:T(8,128)(2,1)} %line_grads.4.refs_2_), custom_call_target="tpu_custom_call" | custom-call | flops 536870912 | bytes 6815744 | tf_op jit(solution)/shard_map/line_grads/pallas_call | solution.py:411
  164.5 4.7 %collective-permute-done.15 = bf16[256,1024]{1,0:T(8,128)(2,1)S(1)} collective-permute-done((bf16[256,1024]{1,0:T(8,128)(2,1)S(1)}, bf16[256,1024]{1,0:T(8,128)(2,1)S(1)}, u32[]{:S(2)}, u32[]{:S(2)}) %collective-permute-start.15) | collective-permute-done | bytes 524320 | tf_op jit(solution)/shard_map/ppermute | solution.py:509
  169.1 5.4 %collective-permute-done.16 = bf16[256,1024]{1,0:T(8,128)(2,1)S(1)} collective-permute-done((bf16[256,1024]{1,0:T(8,128)(2,1)}, bf16[256,1024]{1,0:T(8,128)(2,1)S(1)}, u32[]{:S(2)}, u32[]{:S(2)}) %collective-permute-start.16) | collective-permute-done | bytes 524320 | tf_op jit(solution)/shard_map/ppermute | solution.py:510
  174.6 0.1 add_select_fusion.own
  174.7 2.4 %collective-permute-start.17 = (bf16[256,1024]{1,0:T(8,128)(2,1)S(1)}, bf16[256,1024]{1,0:T(8,128)(2,1)S(1)}, u32[]{:S(2)}, u32[]{:S(2)}) collective-permute-start(bf16[256,1024]{1,0:T(8,128)(2,1)S(1)} %add_select_fusion.own), channel_id=1, source_target_pairs={{0,2},{2,0},{1,3},{3,1},{4,6},{6,4},{5,7},{7,5},{8,10},{10,8},{9,1... | collective-permute-start | bytes 1572872 | tf_op jit(solution)/shard_map/ppermute | solution.py:519
  177.1 1.3 collective-permute-start.14
  178.4 8.4 %line_grads.6.refs_3_ = bf16[64,128,128]{2,1,0:T(8,128)(2,1)} custom-call(s32[64]{0:T(128)} %ids.7, bf16[4,256,1024]{2,1,0:T(8,128)(2,1)} %bitcast.18, bf16[512,1024]{1,0:T(8,128)(2,1)} %copy-done.1, bf16[512,1024]{1,0:T(8,128)(2,1)} %copy-done.3, bf16[64,128,128]{2,1,0:T(8,128)(2,1)} %line_grads.5.refs_3_), custom_call_target="tpu_custom_call" | custom-call | flops 536870912 | bytes 8388608 | tf_op jit(solution)/shard_map/line_grads/pallas_call | solution.py:411
  186.9 8.4 %line_grads.7 = bf16[64,128,128]{2,1,0:T(8,128)(2,1)} custom-call(s32[64]{0:T(128)} %ids.7, bf16[4,256,1024]{2,1,0:T(8,128)(2,1)} %bitcast.19, bf16[512,1024]{1,0:T(8,128)(2,1)} %copy-done.2, bf16[512,1024]{1,0:T(8,128)(2,1)} %copy-done.4, bf16[64,128,128]{2,1,0:T(8,128)(2,1)} %line_grads.6.refs_3_), custom_call_target="tpu_custom_call" | custom-call | flops 536870912 | bytes 8388608 | tf_op jit(solution)/shard_map/line_grads/pallas_call | solution.py:411
  195.3 0.6 collective-permute-start.20
  195.9 0.9 broadcast_select_fusion
  196.7 0.7 collective-permute-done.20.by_both
  197.4 0.8 copy-done.17
  198.2 3.0 %assemble.1 = bf16[256,4096]{1,0:T(8,128)(2,1)} custom-call(s32[4]{0:T(128)} %pad_add_fusion.place_of, bf16[256,1024]{1,0:T(8,128)(2,1)} %copy-done.5, bf16[256,1024]{1,0:T(8,128)(2,1)} %copy-done.13, bf16[256,1024]{1,0:T(8,128)(2,1)} %copy-done.12, bf16[256,1024]{1,0:T(8,128)(2,1)} %copy-done.17), custom_call_target="tpu_custom_call" | custom-call | bytes 4194304 | tf_op jit(solution)/shard_map/assemble/pallas_call | solution.py:353
  (55 shorter events, 0.2 us)
Async XLA Ops:
  7.2 88.7 %all-gather.7.cloned.1.call-start = ((), (), s32[]{:S(2)}) async-start(), calls=%async_computation | async-start | bytes 2621440 | tf_op jit(solution)/shard_map/all_gather | solution.py:480
  10.4 28.3 %collective-permute-start = (bf16[33,128,128]{2,1,0:T(8,128)(2,1)}, bf16[33,128,128]{2,1,0:T(8,128)(2,1)S(1)}, u32[]{:S(2)}, u32[]{:S(2)}) collective-permute-start(bf16[33,128,128]{2,1,0:T(8,128)(2,1)} %pad_maximum_fusion), channel_id=1, source_target_pairs={{0,4},{12,8},{1,5},{13,9},{2,6},{14,10},{3,7},{15,11},{16,20},{28,... | collective-permute-start | bytes 3244040 | tf_op jit(solution)/shard_map/ppermute | solution.py:463
  15.4 23.4 %collective-permute-start.1 = (bf16[33,128,128]{2,1,0:T(8,128)(2,1)}, bf16[33,128,128]{2,1,0:T(8,128)(2,1)}, u32[]{:S(2)}, u32[]{:S(2)}) collective-permute-start(bf16[33,128,128]{2,1,0:T(8,128)(2,1)} %pad_maximum_fusion), channel_id=1, source_target_pairs={{4,8},{8,4},{5,9},{9,5},{6,10},{10,6},{7,11},{11,7},{20,24},{24,20... | collective-permute-start | bytes 3244040 | tf_op jit(solution)/shard_map/ppermute | solution.py:464
  17.1 8.1 %copy-start.6 = (bf16[256,1024]{1,0:T(8,128)(2,1)S(1)}, bf16[256,1024]{1,0:T(8,128)(2,1)}, u32[]{:S(2)}) copy-start(bf16[256,1024]{1,0:T(8,128)(2,1)} %upstream.1) | copy-start | bytes 1572868
  24.0 1.8 copy-start
  25.7 45.7 %copy-start.10 = (bf16[512,1024]{1,0:T(8,128)(2,1)}, bf16[512,1024]{1,0:T(8,128)(2,1)S(1)}, u32[]{:S(2)}) copy-start(bf16[512,1024]{1,0:T(8,128)(2,1)S(1)} %pad_maximum_fusion.1) | copy-start | bytes 3145732
  38.7 40.8 %copy-start.7 = (bf16[33,128,128]{2,1,0:T(8,128)(2,1)}, bf16[33,128,128]{2,1,0:T(8,128)(2,1)S(1)}, u32[]{:S(2)}) copy-start(bf16[33,128,128]{2,1,0:T(8,128)(2,1)S(1)} %collective-permute-done.near_a) | copy-start | bytes 3244036
  38.7 30.6 %collective-permute-start.3 = (bf16[33,128,128]{2,1,0:T(8,128)(2,1)S(1)}, bf16[33,128,128]{2,1,0:T(8,128)(2,1)}, u32[]{:S(2)}, u32[]{:S(2)}) collective-permute-start(bf16[33,128,128]{2,1,0:T(8,128)(2,1)S(1)} %collective-permute-done.near_a), channel_id=1, source_target_pairs={{4,8},{8,4},{5,9},{9,5},{6,10},{10,6},{7,11},{11,7},{20,24},{24,20... | collective-permute-start | bytes 3244040 | tf_op jit(solution)/shard_map/ppermute | solution.py:471
  40.4 28.9 %collective-permute-start.4 = (bf16[33,128,128]{2,1,0:T(8,128)(2,1)}, bf16[33,128,128]{2,1,0:T(8,128)(2,1)}, u32[]{:S(2)}, u32[]{:S(2)}) collective-permute-start(bf16[33,128,128]{2,1,0:T(8,128)(2,1)} %collective-permute-done.1.far_a), channel_id=1, source_target_pairs={{0,16},{16,0},{1,17},{17,1},{2,18},{18,2},{3,19},{19,3},{4,20},{20... | collective-permute-start | bytes 3244040 | tf_op jit(solution)/shard_map/ppermute | solution.py:472
  41.9 27.4 %collective-permute-start.2 = (bf16[512,1024]{1,0:T(8,128)(2,1)S(1)}, bf16[512,1024]{1,0:T(8,128)(2,1)S(1)}, u32[]{:S(2)}, u32[]{:S(2)}) collective-permute-start(bf16[512,1024]{1,0:T(8,128)(2,1)S(1)} %pad_maximum_fusion.1), channel_id=1, source_target_pairs={{0,4},{12,8},{4,0},{8,12},{1,5},{13,9},{5,1},{9,13},{2,6},{14,10},... | collective-permute-start | bytes 3145736 | tf_op jit(solution)/shard_map/ppermute | solution.py:473
  69.3 1.1 copy-start.9
  71.4 107.0 %all-gather.11.cloned.1.call-start = ((), (), s32[]{:S(2)}) async-start(), calls=%async_computation.2 | async-start | bytes 2621440 | tf_op jit(solution)/shard_map/all_gather | solution.py:503
  71.5 24.4 %collective-permute-start.6 = (bf16[33,128,128]{2,1,0:T(8,128)(2,1)}, bf16[33,128,128]{2,1,0:T(8,128)(2,1)}, u32[]{:S(2)}, u32[]{:S(2)}) collective-permute-start(bf16[33,128,128]{2,1,0:T(8,128)(2,1)} %collective-permute-done.3.end_a), channel_id=1, source_target_pairs={{0,16},{16,0},{1,17},{17,1},{2,18},{18,2},{3,19},{19,3},{4,20},{20... | collective-permute-start | bytes 3244040 | tf_op jit(solution)/shard_map/ppermute | solution.py:478
  72.0 23.8 %collective-permute-start.5 = (bf16[32,128,128]{2,1,0:T(8,128)(2,1)}, bf16[32,128,128]{2,1,0:T(8,128)(2,1)S(1)}, u32[]{:S(2)}, u32[]{:S(2)}) collective-permute-start(bf16[32,128,128]{2,1,0:T(8,128)(2,1)} %constant_dynamic-slice_fusion), channel_id=1, source_target_pairs={{0,4},{12,8},{1,5},{13,9},{2,6},{14,10},{3,7},{15,11},{16,20},{28,... | collective-permute-start | bytes 3145736 | tf_op jit(solution)/shard_map/ppermute | solution.py:477
  75.7 20.1 %collective-permute-start.7 = (bf16[512,1024]{1,0:T(8,128)(2,1)}, bf16[512,1024]{1,0:T(8,128)(2,1)S(1)}, u32[]{:S(2)}, u32[]{:S(2)}) collective-permute-start(bf16[512,1024]{1,0:T(8,128)(2,1)} %copy-done.10), channel_id=1, source_target_pairs={{4,8},{8,4},{5,9},{9,5},{6,10},{10,6},{7,11},{11,7},{20,24},{24,20... | collective-permute-start | bytes 3145736 | tf_op jit(solution)/shard_map/ppermute | solution.py:479
  95.9 1.0 copy-start.8
  95.9 26.9 %copy-start.1 = (bf16[512,1024]{1,0:T(8,128)(2,1)}, bf16[512,1024]{1,0:T(8,128)(2,1)S(1)}, u32[]{:S(2)}) copy-start(bf16[512,1024]{1,0:T(8,128)(2,1)S(1)} %collective-permute-done.7.refs_1_) | copy-start | bytes 3145732
  96.8 12.0 %collective-permute-start.10 = (bf16[512,1024]{1,0:T(8,128)(2,1)}, bf16[512,1024]{1,0:T(8,128)(2,1)S(1)}, u32[]{:S(2)}, u32[]{:S(2)}) collective-permute-start(bf16[512,1024]{1,0:T(8,128)(2,1)} %copy-done.9), channel_id=1, source_target_pairs={{4,8},{8,4},{5,9},{9,5},{6,10},{10,6},{7,11},{11,7},{20,24},{24,20... | collective-permute-start | bytes 3145736 | tf_op jit(solution)/shard_map/ppermute | solution.py:489
  97.6 25.2 %collective-permute-start.11 = (bf16[512,1024]{1,0:T(8,128)(2,1)S(1)}, bf16[512,1024]{1,0:T(8,128)(2,1)S(1)}, u32[]{:S(2)}, u32[]{:S(2)}) collective-permute-start(bf16[512,1024]{1,0:T(8,128)(2,1)S(1)} %collective-permute-done.7.refs_1_), channel_id=1, source_target_pairs={{4,0},{8,12},{5,1},{9,13},{6,2},{10,14},{7,3},{11,15},{20,16},{24,... | collective-permute-start | bytes 3145736 | tf_op jit(solution)/shard_map/ppermute | solution.py:490
  102.7 2.2 %collective-permute-start.8 = (bf16[256,1024]{1,0:T(8,128)(2,1)}, bf16[256,1024]{1,0:T(8,128)(2,1)S(1)}, u32[]{:S(2)}, u32[]{:S(2)}) collective-permute-start(bf16[256,1024]{1,0:T(8,128)(2,1)} %get-tuple-element.69), channel_id=1, source_target_pairs={{0,1},{1,0},{2,3},{3,2},{4,5},{5,4},{6,7},{7,6},{8,9},{9,8},{10,11... | collective-permute-start | bytes 1572872 | tf_op jit(solution)/shard_map/ppermute | solution.py:495
  102.8 3.0 %collective-permute-start.9 = (bf16[256,1024]{1,0:T(8,128)(2,1)}, bf16[256,1024]{1,0:T(8,128)(2,1)}, u32[]{:S(2)}, u32[]{:S(2)}) collective-permute-start(bf16[256,1024]{1,0:T(8,128)(2,1)} %get-tuple-element.70), channel_id=1, source_target_pairs={{0,1},{1,0},{2,3},{3,2},{4,5},{5,4},{6,7},{7,6},{8,9},{9,8},{10,11... | collective-permute-start | bytes 1572872 | tf_op jit(solution)/shard_map/ppermute | solution.py:495
  104.9 0.9 copy-start.16
  108.8 42.4 %copy-start.2 = (bf16[512,1024]{1,0:T(8,128)(2,1)}, bf16[512,1024]{1,0:T(8,128)(2,1)S(1)}, u32[]{:S(2)}) copy-start(bf16[512,1024]{1,0:T(8,128)(2,1)S(1)} %collective-permute-done.10.refs_1_) | copy-start | bytes 3145732
  122.7 7.8 %copy-start.3 = (bf16[512,1024]{1,0:T(8,128)(2,1)}, bf16[512,1024]{1,0:T(8,128)(2,1)S(1)}, u32[]{:S(2)}) copy-start(bf16[512,1024]{1,0:T(8,128)(2,1)S(1)} %collective-permute-done.11.refs_2_) | copy-start | bytes 3145732
  123.7 63.2 %all-gather.9.cloned.1.call-start = ((), (), s32[]{:S(2)}) async-start(), calls=%async_computation.1 | async-start | bytes 2621440 | tf_op jit(solution)/shard_map/all_gather | solution.py:512
  123.7 6.8 %collective-permute-start.13 = (bf16[2,256,1024]{2,1,0:T(8,128)(2,1)}, bf16[2,256,1024]{2,1,0:T(8,128)(2,1)}, u32[]{:S(2)}, u32[]{:S(2)}) collective-permute-start(bf16[2,256,1024]{2,1,0:T(8,128)(2,1)} %get-tuple-element.78), channel_id=1, source_target_pairs={{0,1},{1,0},{2,3},{3,2},{4,5},{5,4},{6,7},{7,6},{8,9},{9,8},{10,11... | collective-permute-start | bytes 3145736 | tf_op jit(solution)/shard_map/ppermute | solution.py:501
  123.8 27.4 %collective-permute-start.19 = (bf16[512,1024]{1,0:T(8,128)(2,1)S(1)}, bf16[512,1024]{1,0:T(8,128)(2,1)S(1)}, u32[]{:S(2)}, u32[]{:S(2)}) collective-permute-start(bf16[512,1024]{1,0:T(8,128)(2,1)S(1)} %collective-permute-done.10.refs_1_), channel_id=1, source_target_pairs={{4,0},{8,12},{5,1},{9,13},{6,2},{10,14},{7,3},{11,15},{20,16},{24,... | collective-permute-start | bytes 3145736 | tf_op jit(solution)/shard_map/ppermute | solution.py:502
  125.1 20.9 %collective-permute-start.12 = (bf16[256,1024]{1,0:T(8,128)(2,1)}, bf16[256,1024]{1,0:T(8,128)(2,1)S(1)}, u32[]{:S(2)}, u32[]{:S(2)}) collective-permute-start(bf16[256,1024]{1,0:T(8,128)(2,1)} %get-tuple-element.76), channel_id=1, source_target_pairs={{0,2},{2,0},{1,3},{3,1},{4,6},{6,4},{5,7},{7,5},{8,10},{10,8},{9,1... | collective-permute-start | bytes 1572872 | tf_op jit(solution)/shard_map/ppermute | solution.py:500
  130.6 21.6 %copy-start.11 = (bf16[256,1024]{1,0:T(8,128)(2,1)S(1)}, bf16[256,1024]{1,0:T(8,128)(2,1)}, u32[]{:S(2)}) copy-start(bf16[256,1024]{1,0:T(8,128)(2,1)} %get-tuple-element.89) | copy-start | bytes 1572868
  146.0 5.2 %copy-start.15 = (bf16[256,1024]{1,0:T(8,128)(2,1)}, bf16[256,1024]{1,0:T(8,128)(2,1)S(1)}, u32[]{:S(2)}) copy-start(bf16[256,1024]{1,0:T(8,128)(2,1)S(1)} %collective-permute-done.12) | copy-start | bytes 1572868
  151.3 13.2 %copy-start.4 = (bf16[512,1024]{1,0:T(8,128)(2,1)}, bf16[512,1024]{1,0:T(8,128)(2,1)S(1)}, u32[]{:S(2)}) copy-start(bf16[512,1024]{1,0:T(8,128)(2,1)S(1)} %collective-permute-done.19.refs_2_) | copy-start | bytes 3145732
  153.5 21.1 %copy-start.14 = (bf16[256,1024]{1,0:T(8,128)(2,1)S(1)}, bf16[256,1024]{1,0:T(8,128)(2,1)}, u32[]{:S(2)}) copy-start(bf16[256,1024]{1,0:T(8,128)(2,1)} %get-tuple-element.88) | copy-start | bytes 1572868
  153.5 15.7 %collective-permute-start.15 = (bf16[256,1024]{1,0:T(8,128)(2,1)S(1)}, bf16[256,1024]{1,0:T(8,128)(2,1)S(1)}, u32[]{:S(2)}, u32[]{:S(2)}) collective-permute-start(bf16[256,1024]{1,0:T(8,128)(2,1)S(1)} %add.28), channel_id=1, source_target_pairs={{4,0},{8,12},{5,1},{9,13},{6,2},{10,14},{7,3},{11,15},{20,16},{24,... | collective-permute-start | bytes 1572872 | tf_op jit(solution)/shard_map/ppermute | solution.py:509
  155.1 19.5 %collective-permute-start.16 = (bf16[256,1024]{1,0:T(8,128)(2,1)}, bf16[256,1024]{1,0:T(8,128)(2,1)S(1)}, u32[]{:S(2)}, u32[]{:S(2)}) collective-permute-start(bf16[256,1024]{1,0:T(8,128)(2,1)} %get-tuple-element.91), channel_id=1, source_target_pairs={{0,2},{2,0},{1,3},{3,1},{4,6},{6,4},{5,7},{7,5},{8,10},{10,8},{9,1... | collective-permute-start | bytes 1572872 | tf_op jit(solution)/shard_map/ppermute | solution.py:510
  164.5 12.6 %copy-start.19 = (bf16[256,1024]{1,0:T(8,128)(2,1)S(1)}, bf16[256,1024]{1,0:T(8,128)(2,1)}, u32[]{:S(2)}) copy-start(bf16[256,1024]{1,0:T(8,128)(2,1)} %get-tuple-element.87) | copy-start | bytes 1572868
  174.7 12.2 %copy-start.5 = (bf16[256,1024]{1,0:T(8,128)(2,1)}, bf16[256,1024]{1,0:T(8,128)(2,1)S(1)}, u32[]{:S(2)}) copy-start(bf16[256,1024]{1,0:T(8,128)(2,1)S(1)} %add_select_fusion.own) | copy-start | bytes 1572868
  174.7 20.6 %collective-permute-start.17 = (bf16[256,1024]{1,0:T(8,128)(2,1)S(1)}, bf16[256,1024]{1,0:T(8,128)(2,1)S(1)}, u32[]{:S(2)}, u32[]{:S(2)}) collective-permute-start(bf16[256,1024]{1,0:T(8,128)(2,1)S(1)} %add_select_fusion.own), channel_id=1, source_target_pairs={{0,2},{2,0},{1,3},{3,1},{4,6},{6,4},{5,7},{7,5},{8,10},{10,8},{9,1... | collective-permute-start | bytes 1572872 | tf_op jit(solution)/shard_map/ppermute | solution.py:519
  177.1 18.2 %collective-permute-start.18 = (bf16[256,1024]{1,0:T(8,128)(2,1)S(1)}, bf16[256,1024]{1,0:T(8,128)(2,1)S(1)}, u32[]{:S(2)}, u32[]{:S(2)}) collective-permute-start(bf16[256,1024]{1,0:T(8,128)(2,1)S(1)} %add_select_fusion.own), channel_id=1, source_target_pairs={{0,1},{1,0},{2,3},{3,2},{4,5},{5,4},{6,7},{7,6},{8,9},{9,8},{10,11... | collective-permute-start | bytes 1572872 | tf_op jit(solution)/shard_map/ppermute | solution.py:519
  177.1 18.8 %collective-permute-start.14 = (bf16[256,1024]{1,0:T(8,128)(2,1)S(1)}, bf16[256,1024]{1,0:T(8,128)(2,1)S(1)}, u32[]{:S(2)}, u32[]{:S(2)}) collective-permute-start(bf16[256,1024]{1,0:T(8,128)(2,1)S(1)} %copy-done.19), channel_id=1, source_target_pairs={{4,0},{8,12},{5,1},{9,13},{6,2},{10,14},{7,3},{11,15},{20,16},{24,... | collective-permute-start | bytes 1572872 | tf_op jit(solution)/shard_map/ppermute | solution.py:516
  186.9 9.0 %copy-start.18 = (bf16[256,1024]{1,0:T(8,128)(2,1)S(1)}, bf16[256,1024]{1,0:T(8,128)(2,1)}, u32[]{:S(2)}) copy-start(bf16[256,1024]{1,0:T(8,128)(2,1)} %get-tuple-element.86) | copy-start | bytes 1572868
  195.3 2.1 %copy-start.12 = (bf16[256,1024]{1,0:T(8,128)(2,1)}, bf16[256,1024]{1,0:T(8,128)(2,1)S(1)}, u32[]{:S(2)}) copy-start(bf16[256,1024]{1,0:T(8,128)(2,1)S(1)} %collective-permute-done.17.by_tensor) | copy-start | bytes 1572868
  195.3 2.1 %copy-start.13 = (bf16[256,1024]{1,0:T(8,128)(2,1)}, bf16[256,1024]{1,0:T(8,128)(2,1)S(1)}, u32[]{:S(2)}) copy-start(bf16[256,1024]{1,0:T(8,128)(2,1)S(1)} %collective-permute-done.18.by_core) | copy-start | bytes 1572868
  195.3 2.1 %collective-permute-start.20 = (bf16[256,1024]{1,0:T(8,128)(2,1)S(1)}, bf16[256,1024]{1,0:T(8,128)(2,1)S(1)}, u32[]{:S(2)}, u32[]{:S(2)}) collective-permute-start(bf16[256,1024]{1,0:T(8,128)(2,1)S(1)} %collective-permute-done.17.by_tensor), channel_id=1, source_target_pairs={{0,1},{1,0},{2,3},{3,2},{4,5},{5,4},{6,7},{7,6},{8,9},{9,8},{10,11... | collective-permute-start | bytes 1572872 | tf_op jit(solution)/shard_map/ppermute | solution.py:520
  197.4 0.8 copy-start.17
Sparse Core Ops, SparseCore 0:
  71.5 21.0 all-gather.6
  123.8 28.6 all-gather.10
  154.0 32.1 all-gather.8

commit v21 on v19

--- a/solution.py
+++ b/solution.py
@@ -363,18 +363,23 @@
     )(place_of, *quarters)
 
 
-def line_grads_kernel(kind, place_of, ids, *refs):
+def line_grads_kernel(kind, ids, *refs):
     refs = list(refs)
-    if kind == "plain":
-        x, d = refs.pop(0), refs.pop(0)
-    else:
+    if kind == "halves":
+        place_of = refs.pop(0)
         mine, theirs, before, after = (refs.pop(0) for _ in range(4))
         x, d = refs.pop(), refs.pop()
-        rows = x.shape[1]
         for at in range(2):
-            x[2 * at + place_of[3]] = mine[at]
-            x[2 * at + 1 - place_of[3]] = theirs[at]
+            x[2 * place_of[3] + at] = mine[at]
+            x[2 - 2 * place_of[3] + at] = theirs[at]
+        d[...] = before[...] + after[...]
+    elif kind == "sums":
+        x, before, after = (refs.pop(0) for _ in range(3))
+        d = refs.pop()
+        rows = x.shape[-2]
         d[...] = before[rows:] + after[rows:]
+    else:
+        x, d = refs.pop(0), refs.pop(0)
     start = refs.pop(0) if len(refs) == 2 else None
     (grads,) = refs
     slots, size = grads.shape[0], grads.shape[1]
@@ -400,21 +405,24 @@
             grads[s] = jnp.where(ids[s] < total, acc, 0.0).astype(grads.dtype)
 
 
-def line_grads(place_of, ids, operands, start, size):
+def line_grads(kind, ids, operands, start, size):
     slots = ids.shape[0]
-    kind = "plain" if len(operands) == 2 else "split"
     flat = list(operands) + ([] if start is None else [start])
+    specs = [whole(pltpu.SMEM)] + [whole()] * len(flat)
     scratch = []
-    if kind == "split":
-        _, rows, part_width = operands[0].shape
+    if kind == "sums":
+        scratch = [pltpu.VMEM((operands[0].shape[-2], operands[-1].shape[1]), jnp.bfloat16)]
+    if kind == "halves":
+        specs[1] = whole(pltpu.SMEM)
+        _, rows, part_width = operands[1].shape
         scratch = [
-            pltpu.VMEM((rows, operands[2].shape[1]), jnp.bfloat16),
+            pltpu.VMEM((rows, operands[-1].shape[1]), jnp.bfloat16),
             pltpu.VMEM((4, rows, part_width), jnp.bfloat16),
         ]
     return pl.pallas_call(
         functools.partial(line_grads_kernel, kind),
         out_shape=jax.ShapeDtypeStruct((slots, size, size), jnp.bfloat16),
-        in_specs=[whole(pltpu.SMEM)] * 2 + [whole()] * len(flat),
+        in_specs=specs,
         out_specs=whole(),
         scratch_shapes=scratch,
         compiler_params=pltpu.CompilerParams(vmem_limit_bytes=VMEM_LIMIT),
@@ -424,7 +432,7 @@
             transcendentals=0,
         ),
         name="line_grads",
-    )(place_of, ids, *flat)
+    )(ids, *flat)
 
 
 INWARD = ((0, 1), (3, 2))
@@ -468,7 +476,7 @@
     other = lax.dynamic_slice_in_dim(late_blocks, (1 - half) * half_slots, half_slots, 0)
     part = lax.dynamic_slice_in_dim(tokens, lax.axis_index(INNER) * part_width, part_width, 1)
     both = jnp.concatenate([part, upstream])
-    grads = line_grads(place_of, block_ids, (tokens, upstream), None, size)
+    grads = line_grads("plain", block_ids, (tokens, upstream), None, size)
     near_a, far_a, both, other, grads = stage((near_a, far_a, both, other, grads))
 
     end_a = along(near_a, perm=MIDDLE)
@@ -485,53 +493,51 @@
     partial, turned = place_first(
         place_of, (block_ids, ids_1, ids_2, ids_3), (blocks, near_a, far_a, far_b, end_a), depth, width
     )
-    near_b, end_b, both_2m, both_1, tokens_1, partial, turned = stage(
-        (near_b, end_b, both_2m, both_1, tokens_1, partial, turned)
-    )
-
-    both_3m = along(both_1, perm=MIDDLE)
+    half_1 = lax.dynamic_slice_in_dim(tokens_1, 2 * at_replica, 2, 0)
+    near_b, end_b, both_2m, half_1, upstream_1, tokens_1, partial, turned = stage(
+        (near_b, end_b, both_2m, half_1, upstream_1, tokens_1, partial, turned)
+    )
+
+    half_3m = along(half_1, perm=MIDDLE)
     both_2o = along(both_2m, perm=OUTWARD)
     last = (near_b, end_b)
     end_keep, own_keep, own_give, *end_give = project_back(
         place_of, ids_1, ids_3, turned, *last, upstream_1, upstream
     )
     end_keep, end_give = add_split(place_of, end_keep, *[cores(a) for a in end_give])
-    end_keep, end_give, own_give, both_3m, both_2o = stage(
-        (end_keep, end_give, own_give, both_3m, both_2o)
+    end_keep, end_give, own_give, half_3m, both_2o = stage(
+        (end_keep, end_give, own_give, half_3m, both_2o)
     )
 
     end_got = sideways(end_give)
     own_keep, own_give = add_split(place_of, own_keep, cores(own_give))
-    both_3o = along(both_3m, perm=OUTWARD)
-    side_2 = lax.all_gather(both_2m[:rows] + both_2o[:rows], "tensor")
+    half_3o = along(half_3m, perm=OUTWARD)
+    upstream_3m = along(upstream_1, perm=MIDDLE)
+    tokens_2 = lax.all_gather(both_2m[:rows] + both_2o[:rows], INNER)
     proj, end_proj = project_forward(place_of, ids_1, ids_3, partial, *last, tokens, tokens_1)
-    end_got, own_give, own_keep, proj, end_proj, side_2 = stage(
-        (end_got, own_give, own_keep, proj, end_proj, side_2)
+    end_got, own_give, own_keep, proj, end_proj, upstream_3m = stage(
+        (end_got, own_give, own_keep, proj, end_proj, upstream_3m)
     )
 
     sum_out = along(end_keep + end_got, perm=OUTWARD)
     own_got = sideways(own_give)
-    grads = line_grads(place_of, block_ids, (tokens_1, upstream_1), grads, size)
-    theirs_2 = cores(side_2)
-    sum_out, own_got, both_3o, grads, theirs_2 = stage(
-        (sum_out, own_got, both_3o, grads, theirs_2)
-    )
-
-    side_3 = lax.all_gather(both_3m[:rows] + both_3o[:rows], "tensor")
+    grads = line_grads("plain", block_ids, (tokens_1, upstream_1), grads, size)
+    half_3 = half_3m + half_3o
+    sum_out, own_got, half_3, grads = stage((sum_out, own_got, half_3, grads))
+
     quarter = jnp.where(middle, own_keep + own_got, sum_out)
+    theirs_3 = cores(half_3)
+    upstream_3o = along(upstream_3m, perm=OUTWARD)
+    grads = line_grads("sums", block_ids, (tokens_2, both_2m, both_2o), grads, size)
+    end_proj, grads = stage((end_proj, grads))
     proj_out = along(end_proj, perm=OUTWARD)
     grads = line_grads(
-        place_of, block_ids, (side_2, theirs_2, both_2m, both_2o), grads, size
-    )
-    by_tensor, by_core, grads, side_3, proj_out = stage(
-        (sideways(quarter), cores(quarter), grads, side_3, proj_out)
-    )
+        "halves", block_ids, (place_of, half_3, theirs_3, upstream_3m, upstream_3o), grads, size
+    )
+    by_tensor, by_core, grads = stage((sideways(quarter), cores(quarter), grads))
     by_both = cores(by_tensor)
+    token_grad = assemble(place_of, (quarter, by_core, by_tensor, by_both))
     projected = jnp.where(middle, proj, proj_out)
-    token_grad = assemble(place_of, (quarter, by_core, by_tensor, by_both))
-    grads = line_grads(
-        place_of, block_ids, (side_3, cores(side_3), both_3m, both_3o), grads, size
-    )
     return projected, token_grad, grads
 
 

time: 230 us -> 217 us (0.943)
  waiting for transfers between devices: 104 us -> 91.2 us
  starting transfers between devices: 31.2 us -> 35.4 us
  other arithmetic: 12.4 us -> 8.59 us
    all_gather x2 -> x1, waiting for transfers between devices: 10.5 us -> 0.01 us  [line_body(): tokens_2 = lax.all_gather(both_2m[:rows] + both_2o[:rows], INNER)]
    ppermute x1, waiting for transfers between devices: 8.85 us -> 0.01 us  [line_body(): sideways(quarter)]
    ppermute x1, waiting for transfers between devices: 8.16 us -> 1.24 us  [line_body(): near_b = along(other, perm=INWARD)]
    ppermute x1, waiting for transfers between devices: 4.02 us -> 10.7 us  [line_body(): proj_out = along(end_proj, perm=OUTWARD)]
    ppermute x1, waiting for transfers between devices: 10.9 us -> 6.12 us  [line_body(): sum_out = along(end_keep + end_got, perm=OUTWARD)]
    all_gather x1, waiting for transfers between devices: 0.01 us -> 4.24 us  [line_body(): tokens_1 = lax.all_gather(both_1[:rows], INNER)]
    ppermute x4 -> x5, starting transfers between devices: 2.12 us -> 5.71 us  [the longest x1 1.66 us: line_body(): half_3m = along(half_1, perm=MIDDLE)]
    ppermute x4 -> x5, waiting for transfers between devices: 2.66 us -> 5.91 us  [the longest x1 5.9 us: line_body(): upstream_3o = along(upstream_3m, perm=OUTWARD)]
  transfers between devices with their start and end apart: 26 -> 26, of which waited for: 14 -> 12; matrix products, arithmetic and copies ran while one was open for 5% -> 5% of each run, Pallas kernels for 21% -> 26%
where the time goes in v21:
time: 217 us
  waiting for transfers between devices  91.2 us (42%)
  Pallas kernels  57.2 us (26%)
  starting transfers between devices  35.4 us (16%)
  between operations  14.3 us (7%)
  local copies, waits for them, and re-layouts  10.2 us (5%)
  other arithmetic  8.59 us (4%)
    pallas_call x4, Pallas kernels, line_grads(): pl.pallas_call(functools.partial(line_grads_kernel, kind), out_shape=jax....  31.3 us
    ppermute x1, waiting for transfers between devices, line_body(): both_1 = along(both, perm=PAIRS)  21.7 us
    ppermute x1, waiting for transfers between devices, line_body(): both_2o = along(both_2m, perm=OUTWARD)  14.6 us
    ppermute x1, waiting for transfers between devices, line_body(): end_got = sideways(end_give)  12 us
    ppermute x1, waiting for transfers between devices, line_body(): near_a = along(mine, perm=INWARD)  11.8 us
    ppermute x1, waiting for transfers between devices, line_body(): proj_out = along(end_proj, perm=OUTWARD)  10.7 us
    pallas_call x1, Pallas kernels, place_first(): pl.pallas_call(place_kernel, out_shape=(jax.ShapeDtypeStruct((depth, widt...  8.74 us
    pallas_call x2, Pallas kernels, add_split(): pl.pallas_call(split_kernel, out_shape=(out, out), in_specs=[whole(pltpu....  6.18 us
  transfers between devices with their start and end apart: 26, of which 12 were waited for; matrix products, arithmetic and copies ran while one was open for 5% of the time, Pallas kernels for 26%

profile of v21, /device:TPU:0, one launch (start us, length us, event | category | flops | bytes accessed | tf_op | source)
XLA Modules:
  0.0 216.9 jit_solution(11027224892465161217)
XLA Ops:
  7.2 0.7 convert_element_type.26
  7.9 0.1 convert_element_type.27
  8.0 1.3 constant_dynamic-slice_fusion.3
  9.3 1.1 pad_maximum_fusion
  10.4 5.0 %collective-permute-start = (bf16[33,128,128]{2,1,0:T(8,128)(2,1)}, bf16[33,128,128]{2,1,0:T(8,128)(2,1)S(1)}, u32[]{:S(2)}, u32[]{:S(2)}) collective-permute-start(bf16[33,128,128]{2,1,0:T(8,128)(2,1)} %pad_maximum_fusion), channel_id=1, source_target_pairs={{0,4},{12,8},{1,5},{13,9},{2,6},{14,10},{3,7},{15,11},{16,20},{28,... | collective-permute-start | bytes 3244040 | tf_op jit(solution)/shard_map/ppermute | solution.py:474
  15.4 1.7 collective-permute-start.1
  17.1 6.9 %line_grads.4.refs_2_ = bf16[64,128,128]{2,1,0:T(8,128)(2,1)} custom-call(s32[64]{0:T(128)} %ids.7, bf16[256,4096]{1,0:T(8,128)(2,1)} %tokens.1, bf16[256,1024]{1,0:T(8,128)(2,1)} %upstream.1), custom_call_target="tpu_custom_call" | custom-call | flops 536870912 | bytes 4718592 | tf_op jit(solution)/shard_map/line_grads/pallas_call | solution.py:422
  24.0 1.2 constant_dynamic-slice_fusion.2
  25.2 0.1 pad_maximum_fusion.1
  25.3 0.4 copy-done
  25.7 1.2 constant_dynamic-slice_fusion.1
  27.0 11.8 %collective-permute-done.near_a = bf16[33,128,128]{2,1,0:T(8,128)(2,1)S(1)} collective-permute-done((bf16[33,128,128]{2,1,0:T(8,128)(2,1)}, bf16[33,128,128]{2,1,0:T(8,128)(2,1)S(1)}, u32[]{:S(2)}, u32[]{:S(2)}) %collective-permute-start) | collective-permute-done | bytes 1081376 | tf_op jit(solution)/shard_map/ppermute | solution.py:474
  38.7 1.7 collective-permute-start.3
  40.4 1.5 collective-permute-start.4
  41.9 5.7 %collective-permute-start.2 = (bf16[512,1024]{1,0:T(8,128)(2,1)S(1)}, bf16[512,1024]{1,0:T(8,128)(2,1)S(1)}, u32[]{:S(2)}, u32[]{:S(2)}) collective-permute-start(bf16[512,1024]{1,0:T(8,128)(2,1)S(1)} %pad_maximum_fusion.1), channel_id=1, source_target_pairs={{0,4},{12,8},{4,0},{8,12},{1,5},{13,9},{5,1},{9,13},{2,6},{14,10},... | collective-permute-start | bytes 3145736 | tf_op jit(solution)/shard_map/ppermute | solution.py:484
  47.6 21.7 %collective-permute-done.2 = bf16[512,1024]{1,0:T(8,128)(2,1)S(1)} collective-permute-done((bf16[512,1024]{1,0:T(8,128)(2,1)S(1)}, bf16[512,1024]{1,0:T(8,128)(2,1)S(1)}, u32[]{:S(2)}, u32[]{:S(2)}) %collective-permute-start.2) | collective-permute-done | bytes 1048608 | tf_op jit(solution)/shard_map/ppermute | solution.py:484
  69.3 1.0 fusion
  70.4 0.6 collective-permute-start.6
  71.0 4.5 %collective-permute-start.5 = (bf16[32,128,128]{2,1,0:T(8,128)(2,1)}, bf16[32,128,128]{2,1,0:T(8,128)(2,1)S(1)}, u32[]{:S(2)}, u32[]{:S(2)}) collective-permute-start(bf16[32,128,128]{2,1,0:T(8,128)(2,1)} %constant_dynamic-slice_fusion.1), channel_id=1, source_target_pairs={{0,4},{12,8},{1,5},{13,9},{2,6},{14,10},{3,7},{15,11},{16,20},{28,... | collective-permute-start | bytes 3145736 | tf_op jit(solution)/shard_map/ppermute | solution.py:488
  75.5 0.7 collective-permute-start.7
  76.2 0.6 pad_add_fusion.place_of.refs_0_
  76.9 1.2 bitcast_convert_fusion
  78.1 1.2 bitcast_convert_fusion.1.ids_3
  79.3 8.7 %place_first.1 = (bf16[4096,1024]{1,0:T(8,128)(2,1)}, bf16[1024,4096]{1,0:T(8,128)(2,1)}) custom-call(s32[4]{0:T(128)} %pad_add_fusion.place_of.refs_0_, s32[64]{0:T(128)} %ids.7, s32[64]{0:T(128)} %get-tuple-element.112.ids_1, s32[64]{0:T(128)} %get-tuple-element.111.ids_2, s32[64]{0:T(128)} %bitcast_convert_fusion.1.ids_3, bf16[64,128,128]{2,1,0:T(8,128)(2,1)} %own.1, ...), custom_call_target="tpu_custom_call" | custom-call | bytes 25165824 | tf_op jit(solution)/shard_map/place_first/pallas_call | solution.py:181
  88.0 4.2 %all-gather.5.cloned.1.call-done = bf16[1024,1024]{1,0:T(8,128)(2,1)} async-done(((bf16[256,1024]{1,0:T(8,128)(2,1)}), bf16[1024,1024]{1,0:T(8,128)(2,1)}) %all-gather.5.cloned.1.call-update) | async-done | bytes 2097168 | tf_op jit(solution)/shard_map/all_gather | solution.py:491
  92.3 2.3 %constant_dynamic-slice_fusion = bf16[2,256,1024]{2,1,0:T(8,128)(2,1)} fusion(bf16[4,256,1024]{2,1,0:T(8,128)(2,1)} %bitcast.15, s32[]{:T(128)S(6)} %select_n.28), kind=kLoop, calls=%fused_computation.5 | loop fusion | bytes 2097156 | tf_op jit(solution)/shard_map/dynamic_slice | solution.py:496
  94.5 1.2 collective-permute-done.5.near_b
  95.8 1.7 collective-permute-start.10
  97.5 1.3 collective-permute-start.11
  98.8 3.9 %project_back.1 = (bf16[2,256,1024]{2,1,0:T(8,128)(2,1)}, bf16[2,256,1024]{2,1,0:T(8,128)(2,1)}, bf16[2,256,1024]{2,1,0:T(8,128)(2,1)}, bf16[256,1024]{1,0:T(8,128)(2,1)}, bf16[256,1024]{1,0:T(8,128)(2,1)}) custom-call(s32[4]{0:T(128)} %pad_add_fusion.place_of.refs_0_, s32[64]{0:T(128)} %get-tuple-element.112.ids_1, s32[64]{0:T(128)} %bitcast_convert_fusion.1.ids_3, ...), custom_call_target="tpu_custom_call" | custom-call | flops 4294967296 | bytes 13631488 | tf_op jit(solution)/shard_map/project_back/pallas_call | solution.py:239
  102.7 0.5 collective-permute-start.9
  103.2 1.6 collective-permute-done.8.refs_0_
  104.8 0.7 collective-permute-done.9.refs_1_
  105.6 0.8 copy-done.15
  106.4 3.1 %add_split.2 = (bf16[256,1024]{1,0:T(8,128)(2,1)}, bf16[256,1024]{1,0:T(8,128)(2,1)}) custom-call(s32[4]{0:T(128)} %pad_add_fusion.place_of.refs_0_, bf16[2,256,1024]{2,1,0:T(8,128)(2,1)} %get-tuple-element.73.keep, bf16[256,1024]{1,0:T(8,128)(2,1)} %copy-done.14, bf16[256,1024]{1,0:T(8,128)(2,1)} %copy-done.15), custom_call_target="tpu_custom_call" | custom-call | flops 524288 | bytes 3145728 | tf_op jit(solution)/shard_map/add_split/pallas_call | solution.py:328
  109.5 14.6 %collective-permute-done.11.refs_2_ = bf16[512,1024]{1,0:T(8,128)(2,1)S(1)} collective-permute-done((bf16[512,1024]{1,0:T(8,128)(2,1)S(1)}, bf16[512,1024]{1,0:T(8,128)(2,1)S(1)}, u32[]{:S(2)}, u32[]{:S(2)}) %collective-permute-start.11) | collective-permute-done | bytes 1048608 | tf_op jit(solution)/shard_map/ppermute | solution.py:502
  124.0 0.9 slice_add_fusion
  125.0 0.1 collective-permute-start.13
  125.0 1.5 collective-permute-start.14
  126.5 0.9 collective-permute-start.12
  127.5 1.3 collective-permute-start.17
  128.8 4.2 %project_forward.1 = (bf16[256,1024]{1,0:T(8,128)(2,1)}, bf16[256,1024]{1,0:T(8,128)(2,1)}) custom-call(s32[4]{0:T(128)} %pad_add_fusion.place_of.refs_0_, s32[64]{0:T(128)} %get-tuple-element.112.ids_1, s32[64]{0:T(128)} %bitcast_convert_fusion.1.ids_3, bf16[4096,1024]{1,0:T(8,128)(2,1)} %get-tuple-element.86.partial, bf16[32,128,128]{2,1,0:T(8,128)(2,1)} %copy-done.8, ...), custom_call_target="tpu_custom_call" | custom-call | flops 536870912 | bytes 4194304 | tf_op jit(solution)/shard_map/project_forward/pallas_call | solution.py:296
  133.0 3.1 %add_split.3 = (bf16[256,1024]{1,0:T(8,128)(2,1)}, bf16[256,1024]{1,0:T(8,128)(2,1)}) custom-call(s32[4]{0:T(128)} %pad_add_fusion.place_of.refs_0_, bf16[2,256,1024]{2,1,0:T(8,128)(2,1)} %get-tuple-element.82.keep, bf16[2,256,1024]{2,1,0:T(8,128)(2,1)} %collective-permute-done.13.refs_0_), custom_call_target="tpu_custom_call" | custom-call | flops 524288 | bytes 3145728 | tf_op jit(solution)/shard_map/add_split/pallas_call | solution.py:328
  136.1 12.0 %collective-permute-done.12 = bf16[256,1024]{1,0:T(8,128)(2,1)S(1)} collective-permute-done((bf16[256,1024]{1,0:T(8,128)(2,1)}, bf16[256,1024]{1,0:T(8,128)(2,1)S(1)}, u32[]{:S(2)}, u32[]{:S(2)}) %collective-permute-start.12) | collective-permute-done | bytes 524320 | tf_op jit(solution)/shard_map/ppermute | solution.py:512
  148.0 0.2 add.33
  148.2 1.5 collective-permute-start.15
  149.7 1.6 collective-permute-start.16
  151.4 7.8 %line_grads.5.refs_3_ = bf16[64,128,128]{2,1,0:T(8,128)(2,1)} custom-call(s32[64]{0:T(128)} %ids.7, bf16[4,256,1024]{2,1,0:T(8,128)(2,1)} %bitcast.17, bf16[256,1024]{1,0:T(8,128)(2,1)} %get-tuple-element.72.end_upstream.refs_1_, bf16[64,128,128]{2,1,0:T(8,128)(2,1)} %line_grads.4.refs_2_), custom_call_target="tpu_custom_call" | custom-call | flops 536870912 | bytes 6815744 | tf_op jit(solution)/shard_map/line_grads/pallas_call | solution.py:422
  159.2 1.7 add.34.refs_1_
  160.9 6.1 %collective-permute-done.15 = bf16[256,1024]{1,0:T(8,128)(2,1)S(1)} collective-permute-done((bf16[256,1024]{1,0:T(8,128)(2,1)S(1)}, bf16[256,1024]{1,0:T(8,128)(2,1)S(1)}, u32[]{:S(2)}, u32[]{:S(2)}) %collective-permute-start.15) | collective-permute-done | bytes 524320 | tf_op jit(solution)/shard_map/ppermute | solution.py:522
  167.0 1.3 collective-permute-start.22
  168.3 0.1 add_select_fusion.own
  168.4 0.6 collective-permute-start.19
  169.0 0.2 collective-permute-start.20
  169.3 8.4 %line_grads.6.refs_5_ = bf16[64,128,128]{2,1,0:T(8,128)(2,1)} custom-call(s32[64]{0:T(128)} %ids.7, bf16[4,256,1024]{2,1,0:T(8,128)(2,1)} %bitcast.18, bf16[512,1024]{1,0:T(8,128)(2,1)} %copy-done.2, bf16[512,1024]{1,0:T(8,128)(2,1)} %copy-done.3, bf16[64,128,128]{2,1,0:T(8,128)(2,1)} %line_grads.5.refs_3_), custom_call_target="tpu_custom_call" | custom-call | flops 536870912 | bytes 8388608 | tf_op jit(solution)/shard_map/line_grads/pallas_call | solution.py:422
  177.6 5.9 %collective-permute-done.22.refs_4_ = bf16[256,1024]{1,0:T(8,128)(2,1)} collective-permute-done((bf16[256,1024]{1,0:T(8,128)(2,1)}, bf16[256,1024]{1,0:T(8,128)(2,1)}, u32[]{:S(2)}, u32[]{:S(2)}) %collective-permute-start.22) | collective-permute-done | bytes 524320 | tf_op jit(solution)/shard_map/ppermute | solution.py:530
  183.6 1.0 copy-done.10
  184.5 8.2 %line_grads.7 = bf16[64,128,128]{2,1,0:T(8,128)(2,1)} custom-call(s32[64]{0:T(128)} %ids.7, s32[4]{0:T(128)} %pad_add_fusion.place_of.refs_0_, bf16[2,256,1024]{2,1,0:T(8,128)(2,1)} %copy-done.1, bf16[2,256,1024]{2,1,0:T(8,128)(2,1)} %copy-done.10, bf16[256,1024]{1,0:T(8,128)(2,1)} %collective-permute-done.14.refs_3_, ...), custom_call_target="tpu_custom_call" | custom-call | flops 536870912 | bytes 7340040 | tf_op jit(solution)/shard_map/line_grads/pallas_call | solution.py:422
  192.8 1.4 collective-permute-start.18
  194.2 0.5 collective-permute-done.23.by_both
  194.7 0.8 copy-done.16
  195.5 3.0 %assemble.1 = bf16[256,4096]{1,0:T(8,128)(2,1)} custom-call(s32[4]{0:T(128)} %pad_add_fusion.place_of.refs_0_, bf16[256,1024]{1,0:T(8,128)(2,1)} %copy-done.4, bf16[256,1024]{1,0:T(8,128)(2,1)} %collective-permute-done.20.by_core, bf16[256,1024]{1,0:T(8,128)(2,1)} %copy-done.13, bf16[256,1024]{1,0:T(8,128)(2,1)} %copy-done.16), custom_call_target="tpu_custom_call" | custom-call | bytes 4194304 | tf_op jit(solution)/shard_map/assemble/pallas_call | solution.py:353
  198.5 10.7 %collective-permute-done.18 = bf16[256,1024]{1,0:T(8,128)(2,1)S(1)} collective-permute-done((bf16[256,1024]{1,0:T(8,128)(2,1)}, bf16[256,1024]{1,0:T(8,128)(2,1)S(1)}, u32[]{:S(2)}, u32[]{:S(2)}) %collective-permute-start.18) | collective-permute-done | bytes 524320 | tf_op jit(solution)/shard_map/ppermute | solution.py:533
  209.2 0.8 broadcast_select_fusion
  (55 shorter events, 0.4 us)
Async XLA Ops:
  7.2 85.1 %all-gather.5.cloned.1.call-start = ((), (), s32[]{:S(2)}) async-start(), calls=%async_computation | async-start | bytes 2621440 | tf_op jit(solution)/shard_map/all_gather | solution.py:491
  10.4 28.3 %collective-permute-start = (bf16[33,128,128]{2,1,0:T(8,128)(2,1)}, bf16[33,128,128]{2,1,0:T(8,128)(2,1)S(1)}, u32[]{:S(2)}, u32[]{:S(2)}) collective-permute-start(bf16[33,128,128]{2,1,0:T(8,128)(2,1)} %pad_maximum_fusion), channel_id=1, source_target_pairs={{0,4},{12,8},{1,5},{13,9},{2,6},{14,10},{3,7},{15,11},{16,20},{28,... | collective-permute-start | bytes 3244040 | tf_op jit(solution)/shard_map/ppermute | solution.py:474
  15.4 23.4 %collective-permute-start.1 = (bf16[33,128,128]{2,1,0:T(8,128)(2,1)}, bf16[33,128,128]{2,1,0:T(8,128)(2,1)}, u32[]{:S(2)}, u32[]{:S(2)}) collective-permute-start(bf16[33,128,128]{2,1,0:T(8,128)(2,1)} %pad_maximum_fusion), channel_id=1, source_target_pairs={{4,8},{8,4},{5,9},{9,5},{6,10},{10,6},{7,11},{11,7},{20,24},{24,20... | collective-permute-start | bytes 3244040 | tf_op jit(solution)/shard_map/ppermute | solution.py:475
  17.1 8.1 %copy-start.5 = (bf16[256,1024]{1,0:T(8,128)(2,1)S(1)}, bf16[256,1024]{1,0:T(8,128)(2,1)}, u32[]{:S(2)}) copy-start(bf16[256,1024]{1,0:T(8,128)(2,1)} %upstream.1) | copy-start | bytes 1572868
  24.0 1.8 copy-start
  25.7 44.6 %copy-start.9 = (bf16[512,1024]{1,0:T(8,128)(2,1)}, bf16[512,1024]{1,0:T(8,128)(2,1)S(1)}, u32[]{:S(2)}) copy-start(bf16[512,1024]{1,0:T(8,128)(2,1)S(1)} %pad_maximum_fusion.1) | copy-start | bytes 3145732
  38.7 40.6 %copy-start.7 = (bf16[33,128,128]{2,1,0:T(8,128)(2,1)}, bf16[33,128,128]{2,1,0:T(8,128)(2,1)S(1)}, u32[]{:S(2)}) copy-start(bf16[33,128,128]{2,1,0:T(8,128)(2,1)S(1)} %collective-permute-done.near_a) | copy-start | bytes 3244036
  38.7 30.6 %collective-permute-start.3 = (bf16[33,128,128]{2,1,0:T(8,128)(2,1)S(1)}, bf16[33,128,128]{2,1,0:T(8,128)(2,1)}, u32[]{:S(2)}, u32[]{:S(2)}) collective-permute-start(bf16[33,128,128]{2,1,0:T(8,128)(2,1)S(1)} %collective-permute-done.near_a), channel_id=1, source_target_pairs={{4,8},{8,4},{5,9},{9,5},{6,10},{10,6},{7,11},{11,7},{20,24},{24,20... | collective-permute-start | bytes 3244040 | tf_op jit(solution)/shard_map/ppermute | solution.py:482
  40.4 28.9 %collective-permute-start.4 = (bf16[33,128,128]{2,1,0:T(8,128)(2,1)}, bf16[33,128,128]{2,1,0:T(8,128)(2,1)}, u32[]{:S(2)}, u32[]{:S(2)}) collective-permute-start(bf16[33,128,128]{2,1,0:T(8,128)(2,1)} %collective-permute-done.1.far_a), channel_id=1, source_target_pairs={{0,16},{16,0},{1,17},{17,1},{2,18},{18,2},{3,19},{19,3},{4,20},{20... | collective-permute-start | bytes 3244040 | tf_op jit(solution)/shard_map/ppermute | solution.py:483
  41.9 27.4 %collective-permute-start.2 = (bf16[512,1024]{1,0:T(8,128)(2,1)S(1)}, bf16[512,1024]{1,0:T(8,128)(2,1)S(1)}, u32[]{:S(2)}, u32[]{:S(2)}) collective-permute-start(bf16[512,1024]{1,0:T(8,128)(2,1)S(1)} %pad_maximum_fusion.1), channel_id=1, source_target_pairs={{0,4},{12,8},{4,0},{8,12},{1,5},{13,9},{5,1},{9,13},{2,6},{14,10},... | collective-permute-start | bytes 3145736 | tf_op jit(solution)/shard_map/ppermute | solution.py:484
  70.4 98.9 %all-gather.7.cloned.1.call-start = ((), (), s32[]{:S(2)}) async-start(), calls=%async_computation.1 | async-start | bytes 2621440 | tf_op jit(solution)/shard_map/all_gather | solution.py:516
  70.4 25.4 %collective-permute-start.6 = (bf16[33,128,128]{2,1,0:T(8,128)(2,1)}, bf16[33,128,128]{2,1,0:T(8,128)(2,1)}, u32[]{:S(2)}, u32[]{:S(2)}) collective-permute-start(bf16[33,128,128]{2,1,0:T(8,128)(2,1)} %collective-permute-done.3.end_a), channel_id=1, source_target_pairs={{0,16},{16,0},{1,17},{17,1},{2,18},{18,2},{3,19},{19,3},{4,20},{20... | collective-permute-start | bytes 3244040 | tf_op jit(solution)/shard_map/ppermute | solution.py:489
  71.0 24.8 %collective-permute-start.5 = (bf16[32,128,128]{2,1,0:T(8,128)(2,1)}, bf16[32,128,128]{2,1,0:T(8,128)(2,1)S(1)}, u32[]{:S(2)}, u32[]{:S(2)}) collective-permute-start(bf16[32,128,128]{2,1,0:T(8,128)(2,1)} %constant_dynamic-slice_fusion.1), channel_id=1, source_target_pairs={{0,4},{12,8},{1,5},{13,9},{2,6},{14,10},{3,7},{15,11},{16,20},{28,... | collective-permute-start | bytes 3145736 | tf_op jit(solution)/shard_map/ppermute | solution.py:488
  75.5 20.3 %collective-permute-start.7 = (bf16[512,1024]{1,0:T(8,128)(2,1)}, bf16[512,1024]{1,0:T(8,128)(2,1)S(1)}, u32[]{:S(2)}, u32[]{:S(2)}) collective-permute-start(bf16[512,1024]{1,0:T(8,128)(2,1)} %copy-done.9), channel_id=1, source_target_pairs={{4,8},{8,4},{5,9},{9,5},{6,10},{10,6},{7,11},{11,7},{20,24},{24,20... | collective-permute-start | bytes 3145736 | tf_op jit(solution)/shard_map/ppermute | solution.py:490
  95.8 3.0 %copy-start.8 = (bf16[32,128,128]{2,1,0:T(8,128)(2,1)}, bf16[32,128,128]{2,1,0:T(8,128)(2,1)S(1)}, u32[]{:S(2)}) copy-start(bf16[32,128,128]{2,1,0:T(8,128)(2,1)S(1)} %collective-permute-done.5.near_b) | copy-start | bytes 3145732
  95.8 28.2 %copy-start.2 = (bf16[512,1024]{1,0:T(8,128)(2,1)}, bf16[512,1024]{1,0:T(8,128)(2,1)S(1)}, u32[]{:S(2)}) copy-start(bf16[512,1024]{1,0:T(8,128)(2,1)S(1)} %collective-permute-done.7.refs_1_) | copy-start | bytes 3145732
  95.8 13.7 %collective-permute-start.10 = (bf16[2,256,1024]{2,1,0:T(8,128)(2,1)}, bf16[2,256,1024]{2,1,0:T(8,128)(2,1)}, u32[]{:S(2)}, u32[]{:S(2)}) collective-permute-start(bf16[2,256,1024]{2,1,0:T(8,128)(2,1)} %constant_dynamic-slice_fusion), channel_id=1, source_target_pairs={{4,8},{8,4},{5,9},{9,5},{6,10},{10,6},{7,11},{11,7},{20,24},{24,20... | collective-permute-start | bytes 3145736 | tf_op jit(solution)/shard_map/ppermute | solution.py:501
  97.5 26.6 %collective-permute-start.11 = (bf16[512,1024]{1,0:T(8,128)(2,1)S(1)}, bf16[512,1024]{1,0:T(8,128)(2,1)S(1)}, u32[]{:S(2)}, u32[]{:S(2)}) collective-permute-start(bf16[512,1024]{1,0:T(8,128)(2,1)S(1)} %collective-permute-done.7.refs_1_), channel_id=1, source_target_pairs={{4,0},{8,12},{5,1},{9,13},{6,2},{10,14},{7,3},{11,15},{20,16},{24,... | collective-permute-start | bytes 3145736 | tf_op jit(solution)/shard_map/ppermute | solution.py:502
  102.6 2.2 %collective-permute-start.8 = (bf16[256,1024]{1,0:T(8,128)(2,1)}, bf16[256,1024]{1,0:T(8,128)(2,1)S(1)}, u32[]{:S(2)}, u32[]{:S(2)}) collective-permute-start(bf16[256,1024]{1,0:T(8,128)(2,1)} %get-tuple-element.74), channel_id=1, source_target_pairs={{0,1},{1,0},{2,3},{3,2},{4,5},{5,4},{6,7},{7,6},{8,9},{9,8},{10,11... | collective-permute-start | bytes 1572872 | tf_op jit(solution)/shard_map/ppermute | solution.py:507
  102.7 2.9 %collective-permute-start.9 = (bf16[256,1024]{1,0:T(8,128)(2,1)}, bf16[256,1024]{1,0:T(8,128)(2,1)S(1)}, u32[]{:S(2)}, u32[]{:S(2)}) collective-permute-start(bf16[256,1024]{1,0:T(8,128)(2,1)} %get-tuple-element.75), channel_id=1, source_target_pairs={{0,1},{1,0},{2,3},{3,2},{4,5},{5,4},{6,7},{7,6},{8,9},{9,8},{10,11... | collective-permute-start | bytes 1572872 | tf_op jit(solution)/shard_map/ppermute | solution.py:507
  104.8 0.8 copy-start.14
  105.6 0.8 copy-start.15
  106.4 18.7 %copy-start.6 = (bf16[256,1024]{1,0:T(8,128)(2,1)S(1)}, bf16[256,1024]{1,0:T(8,128)(2,1)}, u32[]{:S(2)}) copy-start(bf16[256,1024]{1,0:T(8,128)(2,1)} %get-tuple-element.72.end_upstream.refs_1_) | copy-start | bytes 1572868
  124.0 8.9 %copy-start.3 = (bf16[512,1024]{1,0:T(8,128)(2,1)}, bf16[512,1024]{1,0:T(8,128)(2,1)S(1)}, u32[]{:S(2)}) copy-start(bf16[512,1024]{1,0:T(8,128)(2,1)S(1)} %collective-permute-done.11.refs_2_) | copy-start | bytes 3145732
  125.0 8.0 %collective-permute-start.13 = (bf16[2,256,1024]{2,1,0:T(8,128)(2,1)}, bf16[2,256,1024]{2,1,0:T(8,128)(2,1)}, u32[]{:S(2)}, u32[]{:S(2)}) collective-permute-start(bf16[2,256,1024]{2,1,0:T(8,128)(2,1)} %get-tuple-element.83), channel_id=1, source_target_pairs={{0,1},{1,0},{2,3},{3,2},{4,5},{5,4},{6,7},{7,6},{8,9},{9,8},{10,11... | collective-permute-start | bytes 3145736 | tf_op jit(solution)/shard_map/ppermute | solution.py:513
  125.0 11.0 %collective-permute-start.14 = (bf16[256,1024]{1,0:T(8,128)(2,1)S(1)}, bf16[256,1024]{1,0:T(8,128)(2,1)}, u32[]{:S(2)}, u32[]{:S(2)}) collective-permute-start(bf16[256,1024]{1,0:T(8,128)(2,1)S(1)} %copy-done.6), channel_id=1, source_target_pairs={{4,8},{8,4},{5,9},{9,5},{6,10},{10,6},{7,11},{11,7},{20,24},{24,20... | collective-permute-start | bytes 1572872 | tf_op jit(solution)/shard_map/ppermute | solution.py:515
  126.5 21.5 %collective-permute-start.12 = (bf16[256,1024]{1,0:T(8,128)(2,1)}, bf16[256,1024]{1,0:T(8,128)(2,1)S(1)}, u32[]{:S(2)}, u32[]{:S(2)}) collective-permute-start(bf16[256,1024]{1,0:T(8,128)(2,1)} %get-tuple-element.81), channel_id=1, source_target_pairs={{0,2},{2,0},{1,3},{3,1},{4,6},{6,4},{5,7},{7,5},{8,10},{10,8},{9,1... | collective-permute-start | bytes 1572872 | tf_op jit(solution)/shard_map/ppermute | solution.py:512
  127.5 31.7 %collective-permute-start.17 = (bf16[2,256,1024]{2,1,0:T(8,128)(2,1)}, bf16[2,256,1024]{2,1,0:T(8,128)(2,1)S(1)}, u32[]{:S(2)}, u32[]{:S(2)}) collective-permute-start(bf16[2,256,1024]{2,1,0:T(8,128)(2,1)} %collective-permute-done.10), channel_id=1, source_target_pairs={{4,0},{8,12},{5,1},{9,13},{6,2},{10,14},{7,3},{11,15},{20,16},{24,... | collective-permute-start | bytes 3145736 | tf_op jit(solution)/shard_map/ppermute | solution.py:514
  132.9 15.1 %copy-start.11 = (bf16[256,1024]{1,0:T(8,128)(2,1)S(1)}, bf16[256,1024]{1,0:T(8,128)(2,1)}, u32[]{:S(2)}) copy-start(bf16[256,1024]{1,0:T(8,128)(2,1)} %get-tuple-element.93) | copy-start | bytes 1572868
  148.2 18.8 %collective-permute-start.15 = (bf16[256,1024]{1,0:T(8,128)(2,1)S(1)}, bf16[256,1024]{1,0:T(8,128)(2,1)S(1)}, u32[]{:S(2)}, u32[]{:S(2)}) collective-permute-start(bf16[256,1024]{1,0:T(8,128)(2,1)S(1)} %add.33), channel_id=1, source_target_pairs={{4,0},{8,12},{5,1},{9,13},{6,2},{10,14},{7,3},{11,15},{20,16},{24,... | collective-permute-start | bytes 1572872 | tf_op jit(solution)/shard_map/ppermute | solution.py:522
  149.7 17.3 %collective-permute-start.16 = (bf16[256,1024]{1,0:T(8,128)(2,1)}, bf16[256,1024]{1,0:T(8,128)(2,1)S(1)}, u32[]{:S(2)}, u32[]{:S(2)}) collective-permute-start(bf16[256,1024]{1,0:T(8,128)(2,1)} %get-tuple-element.95), channel_id=1, source_target_pairs={{0,2},{2,0},{1,3},{3,1},{4,6},{6,4},{5,7},{7,5},{8,10},{10,8},{9,1... | collective-permute-start | bytes 1572872 | tf_op jit(solution)/shard_map/ppermute | solution.py:523
  159.2 9.1 %copy-start.12 = (bf16[256,1024]{1,0:T(8,128)(2,1)S(1)}, bf16[256,1024]{1,0:T(8,128)(2,1)}, u32[]{:S(2)}) copy-start(bf16[256,1024]{1,0:T(8,128)(2,1)} %get-tuple-element.100) | copy-start | bytes 1572868
  160.9 16.8 %copy-start.1 = (bf16[2,256,1024]{2,1,0:T(8,128)(2,1)}, bf16[2,256,1024]{2,1,0:T(8,128)(2,1)S(1)}, u32[]{:S(2)}) copy-start(bf16[2,256,1024]{2,1,0:T(8,128)(2,1)S(1)} %add.34.refs_1_) | copy-start | bytes 3145732
  167.0 16.5 %collective-permute-start.21 = (bf16[2,256,1024]{2,1,0:T(8,128)(2,1)S(1)}, bf16[2,256,1024]{2,1,0:T(8,128)(2,1)S(1)}, u32[]{:S(2)}, u32[]{:S(2)}) collective-permute-start(bf16[2,256,1024]{2,1,0:T(8,128)(2,1)S(1)} %add.34.refs_1_), channel_id=1, source_target_pairs={{0,1},{1,0},{2,3},{3,2},{4,5},{5,4},{6,7},{7,6},{8,9},{9,8},{10,11... | collective-permute-start | bytes 3145736 | tf_op jit(solution)/shard_map/ppermute | solution.py:529
  167.0 16.5 %collective-permute-start.22 = (bf16[256,1024]{1,0:T(8,128)(2,1)}, bf16[256,1024]{1,0:T(8,128)(2,1)}, u32[]{:S(2)}, u32[]{:S(2)}) collective-permute-start(bf16[256,1024]{1,0:T(8,128)(2,1)} %collective-permute-done.14.refs_3_), channel_id=1, source_target_pairs={{4,0},{8,12},{5,1},{9,13},{6,2},{10,14},{7,3},{11,15},{20,16},{24,... | collective-permute-start | bytes 1572872 | tf_op jit(solution)/shard_map/ppermute | solution.py:530
  168.4 9.2 %copy-start.4 = (bf16[256,1024]{1,0:T(8,128)(2,1)}, bf16[256,1024]{1,0:T(8,128)(2,1)S(1)}, u32[]{:S(2)}) copy-start(bf16[256,1024]{1,0:T(8,128)(2,1)S(1)} %add_select_fusion.own) | copy-start | bytes 1572868
  168.4 24.3 %collective-permute-start.19 = (bf16[256,1024]{1,0:T(8,128)(2,1)S(1)}, bf16[256,1024]{1,0:T(8,128)(2,1)S(1)}, u32[]{:S(2)}, u32[]{:S(2)}) collective-permute-start(bf16[256,1024]{1,0:T(8,128)(2,1)S(1)} %add_select_fusion.own), channel_id=1, source_target_pairs={{0,2},{2,0},{1,3},{3,1},{4,6},{6,4},{5,7},{7,5},{8,10},{10,8},{9,1... | collective-permute-start | bytes 1572872 | tf_op jit(solution)/shard_map/ppermute | solution.py:537
  169.0 23.7 %collective-permute-start.20 = (bf16[256,1024]{1,0:T(8,128)(2,1)S(1)}, bf16[256,1024]{1,0:T(8,128)(2,1)}, u32[]{:S(2)}, u32[]{:S(2)}) collective-permute-start(bf16[256,1024]{1,0:T(8,128)(2,1)S(1)} %add_select_fusion.own), channel_id=1, source_target_pairs={{0,1},{1,0},{2,3},{3,2},{4,5},{5,4},{6,7},{7,6},{8,9},{9,8},{10,11... | collective-permute-start | bytes 1572872 | tf_op jit(solution)/shard_map/ppermute | solution.py:537
  183.6 1.0 copy-start.10
  192.7 16.5 %copy-start.17 = (bf16[256,1024]{1,0:T(8,128)(2,1)S(1)}, bf16[256,1024]{1,0:T(8,128)(2,1)}, u32[]{:S(2)}) copy-start(bf16[256,1024]{1,0:T(8,128)(2,1)} %get-tuple-element.90) | copy-start | bytes 1572868
  192.7 2.0 copy-start.13
  192.7 2.0 collective-permute-start.23
  192.8 16.4 %collective-permute-start.18 = (bf16[256,1024]{1,0:T(8,128)(2,1)}, bf16[256,1024]{1,0:T(8,128)(2,1)S(1)}, u32[]{:S(2)}, u32[]{:S(2)}) collective-permute-start(bf16[256,1024]{1,0:T(8,128)(2,1)} %get-tuple-element.99), channel_id=1, source_target_pairs={{4,0},{8,12},{5,1},{9,13},{6,2},{10,14},{7,3},{11,15},{20,16},{24,... | collective-permute-start | bytes 1572872 | tf_op jit(solution)/shard_map/ppermute | solution.py:533
  194.7 0.8 copy-start.16
Sparse Core Ops, SparseCore 0:
  70.5 21.7 all-gather.4
  125.1 29.0 all-gather.6

commit v22 on v21

--- a/solution.py
+++ b/solution.py
@@ -521,23 +521,26 @@
 
     sum_out = along(end_keep + end_got, perm=OUTWARD)
     own_got = sideways(own_give)
+    upstream_3o = along(upstream_3m, perm=OUTWARD)
     grads = line_grads("plain", block_ids, (tokens_1, upstream_1), grads, size)
     half_3 = half_3m + half_3o
-    sum_out, own_got, half_3, grads = stage((sum_out, own_got, half_3, grads))
+    theirs_3 = cores(half_3)
+    grads = line_grads("sums", block_ids, (tokens_2, both_2m, both_2o), grads, size)
+    sum_out, own_got, half_3, theirs_3, upstream_3o, grads = stage(
+        (sum_out, own_got, half_3, theirs_3, upstream_3o, grads)
+    )
 
     quarter = jnp.where(middle, own_keep + own_got, sum_out)
-    theirs_3 = cores(half_3)
-    upstream_3o = along(upstream_3m, perm=OUTWARD)
-    grads = line_grads("sums", block_ids, (tokens_2, both_2m, both_2o), grads, size)
-    end_proj, grads = stage((end_proj, grads))
     proj_out = along(end_proj, perm=OUTWARD)
     grads = line_grads(
         "halves", block_ids, (place_of, half_3, theirs_3, upstream_3m, upstream_3o), grads, size
     )
-    by_tensor, by_core, grads = stage((sideways(quarter), cores(quarter), grads))
+    by_tensor, by_core, proj_out, grads = stage(
+        (sideways(quarter), cores(quarter), proj_out, grads)
+    )
     by_both = cores(by_tensor)
+    projected = jnp.where(middle, proj, proj_out)
     token_grad = assemble(place_of, (quarter, by_core, by_tensor, by_both))
-    projected = jnp.where(middle, proj, proj_out)
     return projected, token_grad, grads
 
 

time: 217 us -> 225 us (1.037)
  other arithmetic: 8.59 us -> 13.1 us
  waiting for transfers between devices: 91.2 us -> 94.5 us
    ppermute x1, waiting for transfers between devices: 0.01 us -> 21.6 us  [line_body(): half_3o = along(half_3m, perm=OUTWARD)]
    ppermute x1, waiting for transfers between devices: 12 us -> 0.01 us  [line_body(): end_got = sideways(end_give)]
    ppermute x1, waiting for transfers between devices: 10.7 us -> 0.06 us  [line_body(): proj_out = along(end_proj, perm=OUTWARD)]
    ppermute x1, waiting for transfers between devices: 5.9 us -> 11.3 us  [line_body(): upstream_3o = along(upstream_3m, perm=OUTWARD)]
    ppermute x1, waiting for transfers between devices: 6.12 us -> 0.95 us  [line_body(): sum_out = along(end_keep + end_got, perm=OUTWARD)]
    ppermute x1, waiting for transfers between devices: 0.01 us -> 4.45 us  [line_body(): sideways(quarter)]
  transfers between devices with their start and end apart: 26 -> 26, of which waited for: 12 -> 12; matrix products, arithmetic and copies ran while one was open for 5% -> 7% of each run, Pallas kernels for 26% -> 24%
where the time goes in v22:
time: 225 us
  waiting for transfers between devices  94.5 us (42%)
  Pallas kernels  57.4 us (26%)
  starting transfers between devices  36.1 us (16%)
  between operations  14.4 us (6%)
  other arithmetic  13.1 us (6%)
  local copies, waits for them, and re-layouts  9.26 us (4%)
    pallas_call x4, Pallas kernels, line_grads(): pl.pallas_call(functools.partial(line_grads_kernel, kind), out_shape=jax....  31.4 us
    ppermute x1, waiting for transfers between devices, line_body(): both_1 = along(both, perm=PAIRS)  21.7 us
    ppermute x1, waiting for transfers between devices, line_body(): half_3o = along(half_3m, perm=OUTWARD)  21.6 us
    ppermute x1, waiting for transfers between devices, line_body(): both_2o = along(both_2m, perm=OUTWARD)  14.6 us
    ppermute x1, waiting for transfers between devices, line_body(): near_a = along(mine, perm=INWARD)  11.8 us
    ppermute x1, waiting for transfers between devices, line_body(): upstream_3o = along(upstream_3m, perm=OUTWARD)  11.3 us
    pallas_call x1, Pallas kernels, place_first(): pl.pallas_call(place_kernel, out_shape=(jax.ShapeDtypeStruct((depth, widt...  8.74 us
    pallas_call x2, Pallas kernels, add_split(): pl.pallas_call(split_kernel, out_shape=(out, out), in_specs=[whole(pltpu....  6.3 us
  transfers between devices with their start and end apart: 26, of which 12 were waited for; matrix products, arithmetic and copies ran while one was open for 7% of the time, Pallas kernels for 24%

profile of v22, /device:TPU:0, one launch (start us, length us, event | category | flops | bytes accessed | tf_op | source)
XLA Modules:
  0.0 224.7 jit_solution(11209561199979701130)
XLA Ops:
  7.2 0.7 convert_element_type.26
  7.9 0.1 convert_element_type.27
  8.0 1.3 constant_dynamic-slice_fusion.3
  9.3 1.1 pad_maximum_fusion
  10.4 5.0 %collective-permute-start = (bf16[33,128,128]{2,1,0:T(8,128)(2,1)}, bf16[33,128,128]{2,1,0:T(8,128)(2,1)S(1)}, u32[]{:S(2)}, u32[]{:S(2)}) collective-permute-start(bf16[33,128,128]{2,1,0:T(8,128)(2,1)} %pad_maximum_fusion), channel_id=1, source_target_pairs={{0,4},{12,8},{1,5},{13,9},{2,6},{14,10},{3,7},{15,11},{16,20},{28,... | collective-permute-start | bytes 3244040 | tf_op jit(solution)/shard_map/ppermute | solution.py:474
  15.4 1.7 collective-permute-start.1
  17.1 6.9 %line_grads.4.refs_2_ = bf16[64,128,128]{2,1,0:T(8,128)(2,1)} custom-call(s32[64]{0:T(128)} %ids.7, bf16[256,4096]{1,0:T(8,128)(2,1)} %tokens.1, bf16[256,1024]{1,0:T(8,128)(2,1)} %upstream.1), custom_call_target="tpu_custom_call" | custom-call | flops 536870912 | bytes 4718592 | tf_op jit(solution)/shard_map/line_grads/pallas_call | solution.py:422
  24.0 1.2 constant_dynamic-slice_fusion.2
  25.2 0.1 pad_maximum_fusion.1
  25.3 0.4 copy-done
  25.7 1.2 constant_dynamic-slice_fusion.1
  27.0 11.8 %collective-permute-done.near_a = bf16[33,128,128]{2,1,0:T(8,128)(2,1)S(1)} collective-permute-done((bf16[33,128,128]{2,1,0:T(8,128)(2,1)}, bf16[33,128,128]{2,1,0:T(8,128)(2,1)S(1)}, u32[]{:S(2)}, u32[]{:S(2)}) %collective-permute-start) | collective-permute-done | bytes 1081376 | tf_op jit(solution)/shard_map/ppermute | solution.py:474
  38.7 1.7 collective-permute-start.3
  40.4 1.5 collective-permute-start.4
  41.9 5.7 %collective-permute-start.2 = (bf16[512,1024]{1,0:T(8,128)(2,1)S(1)}, bf16[512,1024]{1,0:T(8,128)(2,1)S(1)}, u32[]{:S(2)}, u32[]{:S(2)}) collective-permute-start(bf16[512,1024]{1,0:T(8,128)(2,1)S(1)} %pad_maximum_fusion.1), channel_id=1, source_target_pairs={{0,4},{12,8},{4,0},{8,12},{1,5},{13,9},{5,1},{9,13},{2,6},{14,10},... | collective-permute-start | bytes 3145736 | tf_op jit(solution)/shard_map/ppermute | solution.py:484
  47.6 21.7 %collective-permute-done.2 = bf16[512,1024]{1,0:T(8,128)(2,1)S(1)} collective-permute-done((bf16[512,1024]{1,0:T(8,128)(2,1)S(1)}, bf16[512,1024]{1,0:T(8,128)(2,1)S(1)}, u32[]{:S(2)}, u32[]{:S(2)}) %collective-permute-start.2) | collective-permute-done | bytes 1048608 | tf_op jit(solution)/shard_map/ppermute | solution.py:484
  69.3 1.0 fusion
  70.4 0.6 collective-permute-start.6
  71.0 4.5 %collective-permute-start.5 = (bf16[32,128,128]{2,1,0:T(8,128)(2,1)}, bf16[32,128,128]{2,1,0:T(8,128)(2,1)S(1)}, u32[]{:S(2)}, u32[]{:S(2)}) collective-permute-start(bf16[32,128,128]{2,1,0:T(8,128)(2,1)} %constant_dynamic-slice_fusion.1), channel_id=1, source_target_pairs={{0,4},{12,8},{1,5},{13,9},{2,6},{14,10},{3,7},{15,11},{16,20},{28,... | collective-permute-start | bytes 3145736 | tf_op jit(solution)/shard_map/ppermute | solution.py:488
  75.5 0.7 collective-permute-start.7
  76.2 0.6 pad_add_fusion.place_of.refs_0_
  76.9 1.2 bitcast_convert_fusion
  78.1 1.2 bitcast_convert_fusion.1.ids_3
  79.3 8.7 %place_first.1 = (bf16[4096,1024]{1,0:T(8,128)(2,1)}, bf16[1024,4096]{1,0:T(8,128)(2,1)}) custom-call(s32[4]{0:T(128)} %pad_add_fusion.place_of.refs_0_, s32[64]{0:T(128)} %ids.7, s32[64]{0:T(128)} %get-tuple-element.114.ids_1, s32[64]{0:T(128)} %get-tuple-element.113.ids_2, s32[64]{0:T(128)} %bitcast_convert_fusion.1.ids_3, bf16[64,128,128]{2,1,0:T(8,128)(2,1)} %own.1, ...), custom_call_target="tpu_custom_call" | custom-call | bytes 25165824 | tf_op jit(solution)/shard_map/place_first/pallas_call | solution.py:181
  88.0 4.2 %all-gather.5.cloned.1.call-done = bf16[1024,1024]{1,0:T(8,128)(2,1)} async-done(((bf16[256,1024]{1,0:T(8,128)(2,1)}), bf16[1024,1024]{1,0:T(8,128)(2,1)}) %all-gather.5.cloned.1.call-update) | async-done | bytes 2097168 | tf_op jit(solution)/shard_map/all_gather | solution.py:491
  92.3 2.3 %constant_dynamic-slice_fusion = bf16[2,256,1024]{2,1,0:T(8,128)(2,1)} fusion(bf16[4,256,1024]{2,1,0:T(8,128)(2,1)} %bitcast.15, s32[]{:T(128)S(6)} %select_n.28), kind=kLoop, calls=%fused_computation.5 | loop fusion | bytes 2097156 | tf_op jit(solution)/shard_map/dynamic_slice | solution.py:496
  94.5 1.2 collective-permute-done.5.near_b
  95.8 1.7 collective-permute-start.10
  97.5 1.3 collective-permute-start.11
  98.8 3.9 %project_back.1 = (bf16[2,256,1024]{2,1,0:T(8,128)(2,1)}, bf16[2,256,1024]{2,1,0:T(8,128)(2,1)}, bf16[2,256,1024]{2,1,0:T(8,128)(2,1)}, bf16[256,1024]{1,0:T(8,128)(2,1)}, bf16[256,1024]{1,0:T(8,128)(2,1)}) custom-call(s32[4]{0:T(128)} %pad_add_fusion.place_of.refs_0_, s32[64]{0:T(128)} %get-tuple-element.114.ids_1, s32[64]{0:T(128)} %bitcast_convert_fusion.1.ids_3, ...), custom_call_target="tpu_custom_call" | custom-call | flops 4294967296 | bytes 13631488 | tf_op jit(solution)/shard_map/project_back/pallas_call | solution.py:239
  102.6 0.1 collective-permute-start.8
  102.7 0.5 collective-permute-start.9
  103.2 1.6 collective-permute-done.8.refs_0_
  104.8 0.7 collective-permute-done.9.refs_1_
  105.6 0.8 copy-done.15
  106.4 3.0 %add_split.2 = (bf16[256,1024]{1,0:T(8,128)(2,1)}, bf16[256,1024]{1,0:T(8,128)(2,1)}) custom-call(s32[4]{0:T(128)} %pad_add_fusion.place_of.refs_0_, bf16[2,256,1024]{2,1,0:T(8,128)(2,1)} %get-tuple-element.74.keep, bf16[256,1024]{1,0:T(8,128)(2,1)} %copy-done.14, bf16[256,1024]{1,0:T(8,128)(2,1)} %copy-done.15), custom_call_target="tpu_custom_call" | custom-call | flops 524288 | bytes 3145728 | tf_op jit(solution)/shard_map/add_split/pallas_call | solution.py:328
  109.4 14.6 %collective-permute-done.11.refs_2_ = bf16[512,1024]{1,0:T(8,128)(2,1)S(1)} collective-permute-done((bf16[512,1024]{1,0:T(8,128)(2,1)S(1)}, bf16[512,1024]{1,0:T(8,128)(2,1)S(1)}, u32[]{:S(2)}, u32[]{:S(2)}) %collective-permute-start.11) | collective-permute-done | bytes 1048608 | tf_op jit(solution)/shard_map/ppermute | solution.py:502
  124.0 0.9 slice_add_fusion
  125.0 1.3 collective-permute-start.17
  126.3 0.1 collective-permute-start.13
  126.3 1.5 collective-permute-start.14
  127.8 1.4 collective-permute-start.12
  129.2 21.6 %collective-permute-done.17 = bf16[2,256,1024]{2,1,0:T(8,128)(2,1)S(1)} collective-permute-done((bf16[2,256,1024]{2,1,0:T(8,128)(2,1)}, bf16[2,256,1024]{2,1,0:T(8,128)(2,1)S(1)}, u32[]{:S(2)}, u32[]{:S(2)}) %collective-permute-start.17) | collective-permute-done | bytes 1048608 | tf_op jit(solution)/shard_map/ppermute | solution.py:514
  150.8 1.6 add.33.refs_1_
  152.4 0.1 collective-permute-start.18
  152.5 4.2 %project_forward.1 = (bf16[256,1024]{1,0:T(8,128)(2,1)}, bf16[256,1024]{1,0:T(8,128)(2,1)}) custom-call(s32[4]{0:T(128)} %pad_add_fusion.place_of.refs_0_, s32[64]{0:T(128)} %get-tuple-element.114.ids_1, s32[64]{0:T(128)} %bitcast_convert_fusion.1.ids_3, bf16[4096,1024]{1,0:T(8,128)(2,1)} %get-tuple-element.87.partial, bf16[32,128,128]{2,1,0:T(8,128)(2,1)} %copy-done.7, ...), custom_call_target="tpu_custom_call" | custom-call | flops 536870912 | bytes 4194304 | tf_op jit(solution)/shard_map/project_forward/pallas_call | solution.py:296
  156.8 3.3 %add_split.3 = (bf16[256,1024]{1,0:T(8,128)(2,1)}, bf16[256,1024]{1,0:T(8,128)(2,1)}) custom-call(s32[4]{0:T(128)} %pad_add_fusion.place_of.refs_0_, bf16[2,256,1024]{2,1,0:T(8,128)(2,1)} %get-tuple-element.83.keep, bf16[2,256,1024]{2,1,0:T(8,128)(2,1)} %collective-permute-done.13.refs_0_), custom_call_target="tpu_custom_call" | custom-call | flops 524288 | bytes 3145728 | tf_op jit(solution)/shard_map/add_split/pallas_call | solution.py:328
  160.1 2.0 add.32
  162.1 1.3 collective-permute-start.15
  163.4 1.5 collective-permute-start.16
  164.9 1.3 collective-permute-start.19
  166.2 7.8 %line_grads.5.refs_3_ = bf16[64,128,128]{2,1,0:T(8,128)(2,1)} custom-call(s32[64]{0:T(128)} %ids.7, bf16[4,256,1024]{2,1,0:T(8,128)(2,1)} %bitcast.17, bf16[256,1024]{1,0:T(8,128)(2,1)} %get-tuple-element.73.end_upstream.refs_1_, bf16[64,128,128]{2,1,0:T(8,128)(2,1)} %line_grads.4.refs_2_), custom_call_target="tpu_custom_call" | custom-call | flops 536870912 | bytes 6815744 | tf_op jit(solution)/shard_map/line_grads/pallas_call | solution.py:422
  174.0 1.3 collective-permute-start.22
  175.3 8.4 %line_grads.6.refs_5_ = bf16[64,128,128]{2,1,0:T(8,128)(2,1)} custom-call(s32[64]{0:T(128)} %ids.7, bf16[4,256,1024]{2,1,0:T(8,128)(2,1)} %bitcast.18, bf16[512,1024]{1,0:T(8,128)(2,1)} %copy-done.2, bf16[512,1024]{1,0:T(8,128)(2,1)} %copy-done.3, bf16[64,128,128]{2,1,0:T(8,128)(2,1)} %line_grads.5.refs_3_), custom_call_target="tpu_custom_call" | custom-call | flops 536870912 | bytes 8388608 | tf_op jit(solution)/shard_map/line_grads/pallas_call | solution.py:422
  183.8 0.9 collective-permute-done.15
  184.7 11.3 %collective-permute-done.19.refs_4_ = bf16[256,1024]{1,0:T(8,128)(2,1)} collective-permute-done((bf16[256,1024]{1,0:T(8,128)(2,1)}, bf16[256,1024]{1,0:T(8,128)(2,1)}, u32[]{:S(2)}, u32[]{:S(2)}) %collective-permute-start.19) | collective-permute-done | bytes 524320 | tf_op jit(solution)/shard_map/ppermute | solution.py:524
  196.1 1.5 add_select_fusion.own
  197.6 1.4 collective-permute-start.20
  199.0 8.2 %line_grads.7 = bf16[64,128,128]{2,1,0:T(8,128)(2,1)} custom-call(s32[64]{0:T(128)} %ids.7, s32[4]{0:T(128)} %pad_add_fusion.place_of.refs_0_, bf16[2,256,1024]{2,1,0:T(8,128)(2,1)} %copy-done.1, bf16[2,256,1024]{2,1,0:T(8,128)(2,1)} %copy-done.9, bf16[256,1024]{1,0:T(8,128)(2,1)} %collective-permute-done.14.refs_3_, ...), custom_call_target="tpu_custom_call" | custom-call | flops 536870912 | bytes 7340040 | tf_op jit(solution)/shard_map/line_grads/pallas_call | solution.py:422
  207.3 4.4 %collective-permute-done.20.by_tensor = bf16[256,1024]{1,0:T(8,128)(2,1)S(1)} collective-permute-done((bf16[256,1024]{1,0:T(8,128)(2,1)S(1)}, bf16[256,1024]{1,0:T(8,128)(2,1)S(1)}, u32[]{:S(2)}, u32[]{:S(2)}) %collective-permute-start.20) | collective-permute-done | bytes 524320 | tf_op jit(solution)/shard_map/ppermute | solution.py:539
  211.8 0.1 collective-permute-start.23
  211.8 2.2 broadcast_select_fusion
  214.0 0.8 copy-done.16
  214.8 3.0 %assemble.1 = bf16[256,4096]{1,0:T(8,128)(2,1)} custom-call(s32[4]{0:T(128)} %pad_add_fusion.place_of.refs_0_, bf16[256,1024]{1,0:T(8,128)(2,1)} %copy-done.4, bf16[256,1024]{1,0:T(8,128)(2,1)} %copy-done.13, bf16[256,1024]{1,0:T(8,128)(2,1)} %copy-done.12, bf16[256,1024]{1,0:T(8,128)(2,1)} %copy-done.16), custom_call_target="tpu_custom_call" | custom-call | bytes 4194304 | tf_op jit(solution)/shard_map/assemble/pallas_call | solution.py:353
  (55 shorter events, 0.4 us)
Async XLA Ops:
  7.2 85.1 %all-gather.5.cloned.1.call-start = ((), (), s32[]{:S(2)}) async-start(), calls=%async_computation | async-start | bytes 2621440 | tf_op jit(solution)/shard_map/all_gather | solution.py:491
  10.4 28.3 %collective-permute-start = (bf16[33,128,128]{2,1,0:T(8,128)(2,1)}, bf16[33,128,128]{2,1,0:T(8,128)(2,1)S(1)}, u32[]{:S(2)}, u32[]{:S(2)}) collective-permute-start(bf16[33,128,128]{2,1,0:T(8,128)(2,1)} %pad_maximum_fusion), channel_id=1, source_target_pairs={{0,4},{12,8},{1,5},{13,9},{2,6},{14,10},{3,7},{15,11},{16,20},{28,... | collective-permute-start | bytes 3244040 | tf_op jit(solution)/shard_map/ppermute | solution.py:474
  15.4 23.4 %collective-permute-start.1 = (bf16[33,128,128]{2,1,0:T(8,128)(2,1)}, bf16[33,128,128]{2,1,0:T(8,128)(2,1)}, u32[]{:S(2)}, u32[]{:S(2)}) collective-permute-start(bf16[33,128,128]{2,1,0:T(8,128)(2,1)} %pad_maximum_fusion), channel_id=1, source_target_pairs={{4,8},{8,4},{5,9},{9,5},{6,10},{10,6},{7,11},{11,7},{20,24},{24,20... | collective-permute-start | bytes 3244040 | tf_op jit(solution)/shard_map/ppermute | solution.py:475
  17.1 8.1 %copy-start.5 = (bf16[256,1024]{1,0:T(8,128)(2,1)S(1)}, bf16[256,1024]{1,0:T(8,128)(2,1)}, u32[]{:S(2)}) copy-start(bf16[256,1024]{1,0:T(8,128)(2,1)} %upstream.1) | copy-start | bytes 1572868
  24.0 1.8 copy-start
  25.7 44.6 %copy-start.8 = (bf16[512,1024]{1,0:T(8,128)(2,1)}, bf16[512,1024]{1,0:T(8,128)(2,1)S(1)}, u32[]{:S(2)}) copy-start(bf16[512,1024]{1,0:T(8,128)(2,1)S(1)} %pad_maximum_fusion.1) | copy-start | bytes 3145732
  38.7 40.6 %copy-start.6 = (bf16[33,128,128]{2,1,0:T(8,128)(2,1)}, bf16[33,128,128]{2,1,0:T(8,128)(2,1)S(1)}, u32[]{:S(2)}) copy-start(bf16[33,128,128]{2,1,0:T(8,128)(2,1)S(1)} %collective-permute-done.near_a) | copy-start | bytes 3244036
  38.7 30.6 %collective-permute-start.3 = (bf16[33,128,128]{2,1,0:T(8,128)(2,1)S(1)}, bf16[33,128,128]{2,1,0:T(8,128)(2,1)}, u32[]{:S(2)}, u32[]{:S(2)}) collective-permute-start(bf16[33,128,128]{2,1,0:T(8,128)(2,1)S(1)} %collective-permute-done.near_a), channel_id=1, source_target_pairs={{4,8},{8,4},{5,9},{9,5},{6,10},{10,6},{7,11},{11,7},{20,24},{24,20... | collective-permute-start | bytes 3244040 | tf_op jit(solution)/shard_map/ppermute | solution.py:482
  40.4 28.9 %collective-permute-start.4 = (bf16[33,128,128]{2,1,0:T(8,128)(2,1)}, bf16[33,128,128]{2,1,0:T(8,128)(2,1)}, u32[]{:S(2)}, u32[]{:S(2)}) collective-permute-start(bf16[33,128,128]{2,1,0:T(8,128)(2,1)} %collective-permute-done.1.far_a), channel_id=1, source_target_pairs={{0,16},{16,0},{1,17},{17,1},{2,18},{18,2},{3,19},{19,3},{4,20},{20... | collective-permute-start | bytes 3244040 | tf_op jit(solution)/shard_map/ppermute | solution.py:483
  41.9 27.4 %collective-permute-start.2 = (bf16[512,1024]{1,0:T(8,128)(2,1)S(1)}, bf16[512,1024]{1,0:T(8,128)(2,1)S(1)}, u32[]{:S(2)}, u32[]{:S(2)}) collective-permute-start(bf16[512,1024]{1,0:T(8,128)(2,1)S(1)} %pad_maximum_fusion.1), channel_id=1, source_target_pairs={{0,4},{12,8},{4,0},{8,12},{1,5},{13,9},{5,1},{9,13},{2,6},{14,10},... | collective-permute-start | bytes 3145736 | tf_op jit(solution)/shard_map/ppermute | solution.py:484
  70.4 104.9 %all-gather.7.cloned.1.call-start = ((), (), s32[]{:S(2)}) async-start(), calls=%async_computation.1 | async-start | bytes 2621440 | tf_op jit(solution)/shard_map/all_gather | solution.py:516
  70.4 25.4 %collective-permute-start.6 = (bf16[33,128,128]{2,1,0:T(8,128)(2,1)}, bf16[33,128,128]{2,1,0:T(8,128)(2,1)}, u32[]{:S(2)}, u32[]{:S(2)}) collective-permute-start(bf16[33,128,128]{2,1,0:T(8,128)(2,1)} %collective-permute-done.3.end_a), channel_id=1, source_target_pairs={{0,16},{16,0},{1,17},{17,1},{2,18},{18,2},{3,19},{19,3},{4,20},{20... | collective-permute-start | bytes 3244040 | tf_op jit(solution)/shard_map/ppermute | solution.py:489
  71.0 24.8 %collective-permute-start.5 = (bf16[32,128,128]{2,1,0:T(8,128)(2,1)}, bf16[32,128,128]{2,1,0:T(8,128)(2,1)S(1)}, u32[]{:S(2)}, u32[]{:S(2)}) collective-permute-start(bf16[32,128,128]{2,1,0:T(8,128)(2,1)} %constant_dynamic-slice_fusion.1), channel_id=1, source_target_pairs={{0,4},{12,8},{1,5},{13,9},{2,6},{14,10},{3,7},{15,11},{16,20},{28,... | collective-permute-start | bytes 3145736 | tf_op jit(solution)/shard_map/ppermute | solution.py:488
  75.5 20.3 %collective-permute-start.7 = (bf16[512,1024]{1,0:T(8,128)(2,1)}, bf16[512,1024]{1,0:T(8,128)(2,1)S(1)}, u32[]{:S(2)}, u32[]{:S(2)}) collective-permute-start(bf16[512,1024]{1,0:T(8,128)(2,1)} %copy-done.8), channel_id=1, source_target_pairs={{4,8},{8,4},{5,9},{9,5},{6,10},{10,6},{7,11},{11,7},{20,24},{24,20... | collective-permute-start | bytes 3145736 | tf_op jit(solution)/shard_map/ppermute | solution.py:490
  95.8 3.0 %copy-start.7 = (bf16[32,128,128]{2,1,0:T(8,128)(2,1)}, bf16[32,128,128]{2,1,0:T(8,128)(2,1)S(1)}, u32[]{:S(2)}) copy-start(bf16[32,128,128]{2,1,0:T(8,128)(2,1)S(1)} %collective-permute-done.5.near_b) | copy-start | bytes 3145732
  95.8 28.2 %copy-start.2 = (bf16[512,1024]{1,0:T(8,128)(2,1)}, bf16[512,1024]{1,0:T(8,128)(2,1)S(1)}, u32[]{:S(2)}) copy-start(bf16[512,1024]{1,0:T(8,128)(2,1)S(1)} %collective-permute-done.7.refs_1_) | copy-start | bytes 3145732
  95.8 13.6 %collective-permute-start.10 = (bf16[2,256,1024]{2,1,0:T(8,128)(2,1)}, bf16[2,256,1024]{2,1,0:T(8,128)(2,1)}, u32[]{:S(2)}, u32[]{:S(2)}) collective-permute-start(bf16[2,256,1024]{2,1,0:T(8,128)(2,1)} %constant_dynamic-slice_fusion), channel_id=1, source_target_pairs={{4,8},{8,4},{5,9},{9,5},{6,10},{10,6},{7,11},{11,7},{20,24},{24,20... | collective-permute-start | bytes 3145736 | tf_op jit(solution)/shard_map/ppermute | solution.py:501
  97.5 26.6 %collective-permute-start.11 = (bf16[512,1024]{1,0:T(8,128)(2,1)S(1)}, bf16[512,1024]{1,0:T(8,128)(2,1)S(1)}, u32[]{:S(2)}, u32[]{:S(2)}) collective-permute-start(bf16[512,1024]{1,0:T(8,128)(2,1)S(1)} %collective-permute-done.7.refs_1_), channel_id=1, source_target_pairs={{4,0},{8,12},{5,1},{9,13},{6,2},{10,14},{7,3},{11,15},{20,16},{24,... | collective-permute-start | bytes 3145736 | tf_op jit(solution)/shard_map/ppermute | solution.py:502
  102.6 2.2 collective-permute-start.8
  102.7 2.9 %collective-permute-start.9 = (bf16[256,1024]{1,0:T(8,128)(2,1)}, bf16[256,1024]{1,0:T(8,128)(2,1)S(1)}, u32[]{:S(2)}, u32[]{:S(2)}) collective-permute-start(bf16[256,1024]{1,0:T(8,128)(2,1)} %get-tuple-element.76), channel_id=1, source_target_pairs={{0,1},{1,0},{2,3},{3,2},{4,5},{5,4},{6,7},{7,6},{8,9},{9,8},{10,11... | collective-permute-start | bytes 1572872 | tf_op jit(solution)/shard_map/ppermute | solution.py:507
  104.8 0.8 copy-start.14
  105.6 0.8 copy-start.15
  124.0 28.4 %copy-start.3 = (bf16[512,1024]{1,0:T(8,128)(2,1)}, bf16[512,1024]{1,0:T(8,128)(2,1)S(1)}, u32[]{:S(2)}) copy-start(bf16[512,1024]{1,0:T(8,128)(2,1)S(1)} %collective-permute-done.11.refs_2_) | copy-start | bytes 3145732
  125.0 25.8 %collective-permute-start.17 = (bf16[2,256,1024]{2,1,0:T(8,128)(2,1)}, bf16[2,256,1024]{2,1,0:T(8,128)(2,1)S(1)}, u32[]{:S(2)}, u32[]{:S(2)}) collective-permute-start(bf16[2,256,1024]{2,1,0:T(8,128)(2,1)} %collective-permute-done.10), channel_id=1, source_target_pairs={{4,0},{8,12},{5,1},{9,13},{6,2},{10,14},{7,3},{11,15},{20,16},{24,... | collective-permute-start | bytes 3145736 | tf_op jit(solution)/shard_map/ppermute | solution.py:514
  126.3 30.5 %collective-permute-start.13 = (bf16[2,256,1024]{2,1,0:T(8,128)(2,1)}, bf16[2,256,1024]{2,1,0:T(8,128)(2,1)}, u32[]{:S(2)}, u32[]{:S(2)}) collective-permute-start(bf16[2,256,1024]{2,1,0:T(8,128)(2,1)} %get-tuple-element.84), channel_id=1, source_target_pairs={{0,1},{1,0},{2,3},{3,2},{4,5},{5,4},{6,7},{7,6},{8,9},{9,8},{10,11... | collective-permute-start | bytes 3145736 | tf_op jit(solution)/shard_map/ppermute | solution.py:513
  126.3 33.7 %collective-permute-start.14 = (bf16[256,1024]{1,0:T(8,128)(2,1)}, bf16[256,1024]{1,0:T(8,128)(2,1)}, u32[]{:S(2)}, u32[]{:S(2)}) collective-permute-start(bf16[256,1024]{1,0:T(8,128)(2,1)} %get-tuple-element.73.end_upstream.refs_1_), channel_id=1, source_target_pairs={{4,8},{8,4},{5,9},{9,5},{6,10},{10,6},{7,11},{11,7},{20,24},{24,20... | collective-permute-start | bytes 1572872 | tf_op jit(solution)/shard_map/ppermute | solution.py:515
  127.8 32.2 %collective-permute-start.12 = (bf16[256,1024]{1,0:T(8,128)(2,1)}, bf16[256,1024]{1,0:T(8,128)(2,1)}, u32[]{:S(2)}, u32[]{:S(2)}) collective-permute-start(bf16[256,1024]{1,0:T(8,128)(2,1)} %get-tuple-element.82), channel_id=1, source_target_pairs={{0,2},{2,0},{1,3},{3,1},{4,6},{6,4},{5,7},{7,5},{8,10},{10,8},{9,1... | collective-permute-start | bytes 1572872 | tf_op jit(solution)/shard_map/ppermute | solution.py:512
  152.4 4.3 %copy-start.1 = (bf16[2,256,1024]{2,1,0:T(8,128)(2,1)}, bf16[2,256,1024]{2,1,0:T(8,128)(2,1)S(1)}, u32[]{:S(2)}) copy-start(bf16[2,256,1024]{2,1,0:T(8,128)(2,1)S(1)} %add.33.refs_1_) | copy-start | bytes 3145732
  152.4 43.6 %collective-permute-start.18 = (bf16[2,256,1024]{2,1,0:T(8,128)(2,1)S(1)}, bf16[2,256,1024]{2,1,0:T(8,128)(2,1)S(1)}, u32[]{:S(2)}, u32[]{:S(2)}) collective-permute-start(bf16[2,256,1024]{2,1,0:T(8,128)(2,1)S(1)} %add.33.refs_1_), channel_id=1, source_target_pairs={{0,1},{1,0},{2,3},{3,2},{4,5},{5,4},{6,7},{7,6},{8,9},{9,8},{10,11... | collective-permute-start | bytes 3145736 | tf_op jit(solution)/shard_map/ppermute | solution.py:527
  156.7 3.3 %copy-start.10 = (bf16[256,1024]{1,0:T(8,128)(2,1)S(1)}, bf16[256,1024]{1,0:T(8,128)(2,1)}, u32[]{:S(2)}) copy-start(bf16[256,1024]{1,0:T(8,128)(2,1)} %get-tuple-element.93) | copy-start | bytes 1572868
  162.1 22.6 %collective-permute-start.15 = (bf16[256,1024]{1,0:T(8,128)(2,1)}, bf16[256,1024]{1,0:T(8,128)(2,1)S(1)}, u32[]{:S(2)}, u32[]{:S(2)}) collective-permute-start(bf16[256,1024]{1,0:T(8,128)(2,1)} %add.32), channel_id=1, source_target_pairs={{4,0},{8,12},{5,1},{9,13},{6,2},{10,14},{7,3},{11,15},{20,16},{24,... | collective-permute-start | bytes 1572872 | tf_op jit(solution)/shard_map/ppermute | solution.py:522
  163.4 21.4 %collective-permute-start.16 = (bf16[256,1024]{1,0:T(8,128)(2,1)}, bf16[256,1024]{1,0:T(8,128)(2,1)}, u32[]{:S(2)}, u32[]{:S(2)}) collective-permute-start(bf16[256,1024]{1,0:T(8,128)(2,1)} %get-tuple-element.95), channel_id=1, source_target_pairs={{0,2},{2,0},{1,3},{3,1},{4,6},{6,4},{5,7},{7,5},{8,10},{10,8},{9,1... | collective-permute-start | bytes 1572872 | tf_op jit(solution)/shard_map/ppermute | solution.py:523
  164.9 31.2 %collective-permute-start.19 = (bf16[256,1024]{1,0:T(8,128)(2,1)}, bf16[256,1024]{1,0:T(8,128)(2,1)}, u32[]{:S(2)}, u32[]{:S(2)}) collective-permute-start(bf16[256,1024]{1,0:T(8,128)(2,1)} %collective-permute-done.14.refs_3_), channel_id=1, source_target_pairs={{4,0},{8,12},{5,1},{9,13},{6,2},{10,14},{7,3},{11,15},{20,16},{24,... | collective-permute-start | bytes 1572872 | tf_op jit(solution)/shard_map/ppermute | solution.py:524
  174.0 33.3 %collective-permute-start.22 = (bf16[256,1024]{1,0:T(8,128)(2,1)}, bf16[256,1024]{1,0:T(8,128)(2,1)}, u32[]{:S(2)}, u32[]{:S(2)}) collective-permute-start(bf16[256,1024]{1,0:T(8,128)(2,1)} %get-tuple-element.102), channel_id=1, source_target_pairs={{4,0},{8,12},{5,1},{9,13},{6,2},{10,14},{7,3},{11,15},{20,16},{24,... | collective-permute-start | bytes 1572872 | tf_op jit(solution)/shard_map/ppermute | solution.py:534
  175.3 20.7 %copy-start.11 = (bf16[256,1024]{1,0:T(8,128)(2,1)S(1)}, bf16[256,1024]{1,0:T(8,128)(2,1)}, u32[]{:S(2)}) copy-start(bf16[256,1024]{1,0:T(8,128)(2,1)} %get-tuple-element.92) | copy-start | bytes 1572868
  196.1 3.0 %copy-start.9 = (bf16[2,256,1024]{2,1,0:T(8,128)(2,1)}, bf16[2,256,1024]{2,1,0:T(8,128)(2,1)S(1)}, u32[]{:S(2)}) copy-start(bf16[2,256,1024]{2,1,0:T(8,128)(2,1)S(1)} %collective-permute-done.18.refs_2_) | copy-start | bytes 3145732
  197.6 9.7 %copy-start.4 = (bf16[256,1024]{1,0:T(8,128)(2,1)}, bf16[256,1024]{1,0:T(8,128)(2,1)S(1)}, u32[]{:S(2)}) copy-start(bf16[256,1024]{1,0:T(8,128)(2,1)S(1)} %add_select_fusion.own) | copy-start | bytes 1572868
  197.6 14.2 %copy-start.17 = (bf16[256,1024]{1,0:T(8,128)(2,1)S(1)}, bf16[256,1024]{1,0:T(8,128)(2,1)}, u32[]{:S(2)}) copy-start(bf16[256,1024]{1,0:T(8,128)(2,1)} %get-tuple-element.91) | copy-start | bytes 1572868
  197.6 14.1 %collective-permute-start.20 = (bf16[256,1024]{1,0:T(8,128)(2,1)S(1)}, bf16[256,1024]{1,0:T(8,128)(2,1)S(1)}, u32[]{:S(2)}, u32[]{:S(2)}) collective-permute-start(bf16[256,1024]{1,0:T(8,128)(2,1)S(1)} %add_select_fusion.own), channel_id=1, source_target_pairs={{0,2},{2,0},{1,3},{3,1},{4,6},{6,4},{5,7},{7,5},{8,10},{10,8},{9,1... | collective-permute-start | bytes 1572872 | tf_op jit(solution)/shard_map/ppermute | solution.py:539
  199.0 12.7 %collective-permute-start.21 = (bf16[256,1024]{1,0:T(8,128)(2,1)S(1)}, bf16[256,1024]{1,0:T(8,128)(2,1)S(1)}, u32[]{:S(2)}, u32[]{:S(2)}) collective-permute-start(bf16[256,1024]{1,0:T(8,128)(2,1)S(1)} %add_select_fusion.own), channel_id=1, source_target_pairs={{0,1},{1,0},{2,3},{3,2},{4,5},{5,4},{6,7},{7,6},{8,9},{9,8},{10,11... | collective-permute-start | bytes 1572872 | tf_op jit(solution)/shard_map/ppermute | solution.py:539
  211.7 2.3 %copy-start.12 = (bf16[256,1024]{1,0:T(8,128)(2,1)}, bf16[256,1024]{1,0:T(8,128)(2,1)S(1)}, u32[]{:S(2)}) copy-start(bf16[256,1024]{1,0:T(8,128)(2,1)S(1)} %collective-permute-done.20.by_tensor) | copy-start | bytes 1572868
  211.8 2.3 %copy-start.13 = (bf16[256,1024]{1,0:T(8,128)(2,1)}, bf16[256,1024]{1,0:T(8,128)(2,1)S(1)}, u32[]{:S(2)}) copy-start(bf16[256,1024]{1,0:T(8,128)(2,1)S(1)} %collective-permute-done.21.by_core) | copy-start | bytes 1572868
  211.8 2.3 %collective-permute-start.23 = (bf16[256,1024]{1,0:T(8,128)(2,1)S(1)}, bf16[256,1024]{1,0:T(8,128)(2,1)S(1)}, u32[]{:S(2)}, u32[]{:S(2)}) collective-permute-start(bf16[256,1024]{1,0:T(8,128)(2,1)S(1)} %collective-permute-done.20.by_tensor), channel_id=1, source_target_pairs={{0,1},{1,0},{2,3},{3,2},{4,5},{5,4},{6,7},{7,6},{8,9},{9,8},{10,11... | collective-permute-start | bytes 1572872 | tf_op jit(solution)/shard_map/ppermute | solution.py:541
  214.0 0.8 copy-start.16
Sparse Core Ops, SparseCore 0:
  70.5 21.7 all-gather.4
  125.1 30.2 all-gather.6

commit v23 on v22

--- a/solution.py
+++ b/solution.py
@@ -515,14 +515,15 @@
     upstream_3m = along(upstream_1, perm=MIDDLE)
     tokens_2 = lax.all_gather(both_2m[:rows] + both_2o[:rows], INNER)
     proj, end_proj = project_forward(place_of, ids_1, ids_3, partial, *last, tokens, tokens_1)
-    end_got, own_give, own_keep, proj, end_proj, upstream_3m = stage(
-        (end_got, own_give, own_keep, proj, end_proj, upstream_3m)
+    end_got, own_give, own_keep, proj, end_proj, upstream_3m, upstream_1 = stage(
+        (end_got, own_give, own_keep, proj, end_proj, upstream_3m, upstream_1)
     )
 
     sum_out = along(end_keep + end_got, perm=OUTWARD)
     own_got = sideways(own_give)
     upstream_3o = along(upstream_3m, perm=OUTWARD)
     grads = line_grads("plain", block_ids, (tokens_1, upstream_1), grads, size)
+    half_3m, grads = stage((half_3m, grads))
     half_3 = half_3m + half_3o
     theirs_3 = cores(half_3)
     grads = line_grads("sums", block_ids, (tokens_2, both_2m, both_2o), grads, size)

time: 225 us -> 223 us (level)
    ppermute x1, waiting for transfers between devices: 21.6 us -> 0.01 us  [line_body(): half_3o = along(half_3m, perm=OUTWARD)]
    ppermute x1, waiting for transfers between devices: 0.01 us -> 13.6 us  [line_body(): end_got = sideways(end_give)]
    ppermute x1, waiting for transfers between devices: 0.95 us -> 7.24 us  [line_body(): sum_out = along(end_keep + end_got, perm=OUTWARD)]
  transfers between devices with their start and end apart: 26 -> 26, of which waited for: 12 -> 12; matrix products, arithmetic and copies ran while one was open for 7% -> 6% of each run, Pallas kernels for 24% -> 25%
where the time goes in v23:
time: 223 us; the launch traced here: 222 us
  waiting for transfers between devices  92.9 us (42%)
  Pallas kernels  57.5 us (26%)
  starting transfers between devices  35.8 us (16%)
  between operations  14.4 us (6%)
  other arithmetic  12.2 us (5%)
  local copies, waits for them, and re-layouts  9.23 us (4%)
    pallas_call x4, Pallas kernels, line_grads(): pl.pallas_call(functools.partial(line_grads_kernel, kind), out_shape=jax....  31.4 us
    ppermute x1, waiting for transfers between devices, line_body(): both_1 = along(both, perm=PAIRS)  21.7 us
    ppermute x1, waiting for transfers between devices, line_body(): both_2o = along(both_2m, perm=OUTWARD)  14.6 us
    ppermute x1, waiting for transfers between devices, line_body(): end_got = sideways(end_give)  13.6 us
    ppermute x1, waiting for transfers between devices, line_body(): near_a = along(mine, perm=INWARD)  11.8 us
    ppermute x1, waiting for transfers between devices, line_body(): upstream_3o = along(upstream_3m, perm=OUTWARD)  11.3 us
    pallas_call x1, Pallas kernels, place_first(): pl.pallas_call(place_kernel, out_shape=(jax.ShapeDtypeStruct((depth, widt...  8.74 us
    ppermute x1, waiting for transfers between devices, line_body(): sum_out = along(end_keep + end_got, perm=OUTWARD)  7.24 us
  transfers between devices with their start and end apart: 26, of which 12 were waited for; matrix products, arithmetic and copies ran while one was open for 6% of the time, Pallas kernels for 25%

profile of v23, /device:TPU:0, one launch (start us, length us, event | category | flops | bytes accessed | tf_op | source)
XLA Modules:
  0.0 222.1 jit_solution(1140939395077847523)
XLA Ops:
  7.2 0.7 convert_element_type.26
  7.9 0.1 convert_element_type.27
  8.0 1.3 constant_dynamic-slice_fusion.3
  9.3 1.1 pad_maximum_fusion
  10.4 5.0 %collective-permute-start = (bf16[33,128,128]{2,1,0:T(8,128)(2,1)}, bf16[33,128,128]{2,1,0:T(8,128)(2,1)S(1)}, u32[]{:S(2)}, u32[]{:S(2)}) collective-permute-start(bf16[33,128,128]{2,1,0:T(8,128)(2,1)} %pad_maximum_fusion), channel_id=1, source_target_pairs={{0,4},{12,8},{1,5},{13,9},{2,6},{14,10},{3,7},{15,11},{16,20},{28,... | collective-permute-start | bytes 3244040 | tf_op jit(solution)/shard_map/ppermute | solution.py:474
  15.4 1.7 collective-permute-start.1
  17.1 6.9 %line_grads.4.refs_2_ = bf16[64,128,128]{2,1,0:T(8,128)(2,1)} custom-call(s32[64]{0:T(128)} %ids.7, bf16[256,4096]{1,0:T(8,128)(2,1)} %tokens.1, bf16[256,1024]{1,0:T(8,128)(2,1)} %upstream.1), custom_call_target="tpu_custom_call" | custom-call | flops 536870912 | bytes 4718592 | tf_op jit(solution)/shard_map/line_grads/pallas_call | solution.py:422
  24.0 1.2 constant_dynamic-slice_fusion.2
  25.2 0.1 pad_maximum_fusion.1
  25.3 0.4 copy-done
  25.7 1.2 constant_dynamic-slice_fusion.1
  26.9 11.8 %collective-permute-done.near_a = bf16[33,128,128]{2,1,0:T(8,128)(2,1)S(1)} collective-permute-done((bf16[33,128,128]{2,1,0:T(8,128)(2,1)}, bf16[33,128,128]{2,1,0:T(8,128)(2,1)S(1)}, u32[]{:S(2)}, u32[]{:S(2)}) %collective-permute-start) | collective-permute-done | bytes 1081376 | tf_op jit(solution)/shard_map/ppermute | solution.py:474
  38.7 1.7 collective-permute-start.3
  40.4 1.5 collective-permute-start.4
  41.9 5.7 %collective-permute-start.2 = (bf16[512,1024]{1,0:T(8,128)(2,1)S(1)}, bf16[512,1024]{1,0:T(8,128)(2,1)S(1)}, u32[]{:S(2)}, u32[]{:S(2)}) collective-permute-start(bf16[512,1024]{1,0:T(8,128)(2,1)S(1)} %pad_maximum_fusion.1), channel_id=1, source_target_pairs={{0,4},{12,8},{4,0},{8,12},{1,5},{13,9},{5,1},{9,13},{2,6},{14,10},... | collective-permute-start | bytes 3145736 | tf_op jit(solution)/shard_map/ppermute | solution.py:484
  47.6 21.7 %collective-permute-done.2 = bf16[512,1024]{1,0:T(8,128)(2,1)S(1)} collective-permute-done((bf16[512,1024]{1,0:T(8,128)(2,1)S(1)}, bf16[512,1024]{1,0:T(8,128)(2,1)S(1)}, u32[]{:S(2)}, u32[]{:S(2)}) %collective-permute-start.2) | collective-permute-done | bytes 1048608 | tf_op jit(solution)/shard_map/ppermute | solution.py:484
  69.3 1.0 fusion
  70.4 0.6 collective-permute-start.6
  71.0 4.5 %collective-permute-start.5 = (bf16[32,128,128]{2,1,0:T(8,128)(2,1)}, bf16[32,128,128]{2,1,0:T(8,128)(2,1)S(1)}, u32[]{:S(2)}, u32[]{:S(2)}) collective-permute-start(bf16[32,128,128]{2,1,0:T(8,128)(2,1)} %constant_dynamic-slice_fusion.1), channel_id=1, source_target_pairs={{0,4},{12,8},{1,5},{13,9},{2,6},{14,10},{3,7},{15,11},{16,20},{28,... | collective-permute-start | bytes 3145736 | tf_op jit(solution)/shard_map/ppermute | solution.py:488
  75.5 0.7 collective-permute-start.7
  76.2 0.6 pad_add_fusion.place_of.refs_0_
  76.9 1.2 bitcast_convert_fusion
  78.1 1.2 bitcast_convert_fusion.1.ids_3
  79.3 8.7 %place_first.1 = (bf16[4096,1024]{1,0:T(8,128)(2,1)}, bf16[1024,4096]{1,0:T(8,128)(2,1)}) custom-call(s32[4]{0:T(128)} %pad_add_fusion.place_of.refs_0_, s32[64]{0:T(128)} %ids.7, s32[64]{0:T(128)} %get-tuple-element.120.ids_1, s32[64]{0:T(128)} %get-tuple-element.119.ids_2, s32[64]{0:T(128)} %bitcast_convert_fusion.1.ids_3, bf16[64,128,128]{2,1,0:T(8,128)(2,1)} %own.1, ...), custom_call_target="tpu_custom_call" | custom-call | bytes 25165824 | tf_op jit(solution)/shard_map/place_first/pallas_call | solution.py:181
  88.0 4.2 %all-gather.5.cloned.1.call-done = bf16[1024,1024]{1,0:T(8,128)(2,1)} async-done(((bf16[256,1024]{1,0:T(8,128)(2,1)}), bf16[1024,1024]{1,0:T(8,128)(2,1)}) %all-gather.5.cloned.1.call-update) | async-done | bytes 2097168 | tf_op jit(solution)/shard_map/all_gather | solution.py:491
  92.3 2.3 %constant_dynamic-slice_fusion = bf16[2,256,1024]{2,1,0:T(8,128)(2,1)} fusion(bf16[4,256,1024]{2,1,0:T(8,128)(2,1)} %bitcast.15, s32[]{:T(128)S(6)} %select_n.28), kind=kLoop, calls=%fused_computation.5 | loop fusion | bytes 2097156 | tf_op jit(solution)/shard_map/dynamic_slice | solution.py:496
  94.5 1.2 collective-permute-done.5.near_b
  95.8 1.7 collective-permute-start.10
  97.5 1.3 collective-permute-start.11
  98.8 3.9 %project_back.1 = (bf16[2,256,1024]{2,1,0:T(8,128)(2,1)}, bf16[2,256,1024]{2,1,0:T(8,128)(2,1)}, bf16[2,256,1024]{2,1,0:T(8,128)(2,1)}, bf16[256,1024]{1,0:T(8,128)(2,1)}, bf16[256,1024]{1,0:T(8,128)(2,1)}) custom-call(s32[4]{0:T(128)} %pad_add_fusion.place_of.refs_0_, s32[64]{0:T(128)} %get-tuple-element.120.ids_1, s32[64]{0:T(128)} %bitcast_convert_fusion.1.ids_3, ...), custom_call_target="tpu_custom_call" | custom-call | flops 4294967296 | bytes 13631488 | tf_op jit(solution)/shard_map/project_back/pallas_call | solution.py:239
  102.6 0.1 collective-permute-start.8
  102.7 0.5 collective-permute-start.9
  103.2 1.6 collective-permute-done.8.refs_0_
  104.8 0.7 collective-permute-done.9.refs_1_
  105.6 0.7 copy-done.16
  106.3 3.1 %add_split.2 = (bf16[256,1024]{1,0:T(8,128)(2,1)}, bf16[256,1024]{1,0:T(8,128)(2,1)}) custom-call(s32[4]{0:T(128)} %pad_add_fusion.place_of.refs_0_, bf16[2,256,1024]{2,1,0:T(8,128)(2,1)} %get-tuple-element.77.keep, bf16[256,1024]{1,0:T(8,128)(2,1)} %copy-done.15, bf16[256,1024]{1,0:T(8,128)(2,1)} %copy-done.16), custom_call_target="tpu_custom_call" | custom-call | flops 524288 | bytes 3145728 | tf_op jit(solution)/shard_map/add_split/pallas_call | solution.py:328
  109.4 14.6 %collective-permute-done.11.refs_2_ = bf16[512,1024]{1,0:T(8,128)(2,1)S(1)} collective-permute-done((bf16[512,1024]{1,0:T(8,128)(2,1)S(1)}, bf16[512,1024]{1,0:T(8,128)(2,1)S(1)}, u32[]{:S(2)}, u32[]{:S(2)}) %collective-permute-start.11) | collective-permute-done | bytes 1048608 | tf_op jit(solution)/shard_map/ppermute | solution.py:502
  124.0 1.0 slice_add_fusion
  125.0 0.1 collective-permute-start.13
  125.1 1.3 collective-permute-start.17
  126.4 1.5 collective-permute-start.14
  127.9 1.3 collective-permute-start.12
  129.2 4.2 %project_forward.1 = (bf16[256,1024]{1,0:T(8,128)(2,1)}, bf16[256,1024]{1,0:T(8,128)(2,1)}) custom-call(s32[4]{0:T(128)} %pad_add_fusion.place_of.refs_0_, s32[64]{0:T(128)} %get-tuple-element.120.ids_1, s32[64]{0:T(128)} %bitcast_convert_fusion.1.ids_3, bf16[4096,1024]{1,0:T(8,128)(2,1)} %get-tuple-element.90.partial, bf16[32,128,128]{2,1,0:T(8,128)(2,1)} %copy-done.8, ...), custom_call_target="tpu_custom_call" | custom-call | flops 536870912 | bytes 4194304 | tf_op jit(solution)/shard_map/project_forward/pallas_call | solution.py:296
  133.4 3.3 %add_split.3 = (bf16[256,1024]{1,0:T(8,128)(2,1)}, bf16[256,1024]{1,0:T(8,128)(2,1)}) custom-call(s32[4]{0:T(128)} %pad_add_fusion.place_of.refs_0_, bf16[2,256,1024]{2,1,0:T(8,128)(2,1)} %get-tuple-element.86.keep, bf16[2,256,1024]{2,1,0:T(8,128)(2,1)} %collective-permute-done.13.refs_0_), custom_call_target="tpu_custom_call" | custom-call | flops 524288 | bytes 3145728 | tf_op jit(solution)/shard_map/add_split/pallas_call | solution.py:328
  136.7 13.6 %collective-permute-done.12 = bf16[256,1024]{1,0:T(8,128)(2,1)S(1)} collective-permute-done((bf16[256,1024]{1,0:T(8,128)(2,1)S(1)}, bf16[256,1024]{1,0:T(8,128)(2,1)S(1)}, u32[]{:S(2)}, u32[]{:S(2)}) %collective-permute-start.12) | collective-permute-done | bytes 524320 | tf_op jit(solution)/shard_map/ppermute | solution.py:512
  150.3 7.9 %line_grads.5.refs_3_ = bf16[64,128,128]{2,1,0:T(8,128)(2,1)} custom-call(s32[64]{0:T(128)} %ids.7, bf16[4,256,1024]{2,1,0:T(8,128)(2,1)} %bitcast.17, bf16[256,1024]{1,0:T(8,128)(2,1)} %get-tuple-element.100.end_upstream.refs_1_, bf16[64,128,128]{2,1,0:T(8,128)(2,1)} %line_grads.4.refs_2_), custom_call_target="tpu_custom_call" | custom-call | flops 536870912 | bytes 6815744 | tf_op jit(solution)/shard_map/line_grads/pallas_call | solution.py:422
  158.2 1.7 add.33.refs_1_
  159.9 0.1 collective-permute-start.18
  160.0 1.0 add.32
  161.0 1.3 collective-permute-start.15
  162.3 2.2 %collective-permute-start.16 = (bf16[256,1024]{1,0:T(8,128)(2,1)}, bf16[256,1024]{1,0:T(8,128)(2,1)}, u32[]{:S(2)}, u32[]{:S(2)}) collective-permute-start(bf16[256,1024]{1,0:T(8,128)(2,1)} %get-tuple-element.98), channel_id=1, source_target_pairs={{0,2},{2,0},{1,3},{3,1},{4,6},{6,4},{5,7},{7,5},{8,10},{10,8},{9,1... | collective-permute-start | bytes 1572872 | tf_op jit(solution)/shard_map/ppermute | solution.py:523
  164.5 1.3 collective-permute-start.19
  165.8 1.3 collective-permute-start.22
  167.2 8.4 %line_grads.6.refs_5_ = bf16[64,128,128]{2,1,0:T(8,128)(2,1)} custom-call(s32[64]{0:T(128)} %ids.7, bf16[4,256,1024]{2,1,0:T(8,128)(2,1)} %bitcast.18, bf16[512,1024]{1,0:T(8,128)(2,1)} %copy-done.2, bf16[512,1024]{1,0:T(8,128)(2,1)} %copy-done.3, bf16[64,128,128]{2,1,0:T(8,128)(2,1)} %line_grads.5.refs_3_), custom_call_target="tpu_custom_call" | custom-call | flops 536870912 | bytes 8388608 | tf_op jit(solution)/shard_map/line_grads/pallas_call | solution.py:422
  175.6 7.2 %collective-permute-done.15 = bf16[256,1024]{1,0:T(8,128)(2,1)S(1)} collective-permute-done((bf16[256,1024]{1,0:T(8,128)(2,1)}, bf16[256,1024]{1,0:T(8,128)(2,1)S(1)}, u32[]{:S(2)}, u32[]{:S(2)}) %collective-permute-start.15) | collective-permute-done | bytes 524320 | tf_op jit(solution)/shard_map/ppermute | solution.py:522
  182.9 11.3 %collective-permute-done.19.refs_4_ = bf16[256,1024]{1,0:T(8,128)(2,1)} collective-permute-done((bf16[256,1024]{1,0:T(8,128)(2,1)}, bf16[256,1024]{1,0:T(8,128)(2,1)}, u32[]{:S(2)}, u32[]{:S(2)}) %collective-permute-start.19) | collective-permute-done | bytes 524320 | tf_op jit(solution)/shard_map/ppermute | solution.py:524
  194.2 1.5 add_select_fusion.own
  195.7 0.6 collective-permute-start.20
  196.4 8.2 %line_grads.7 = bf16[64,128,128]{2,1,0:T(8,128)(2,1)} custom-call(s32[64]{0:T(128)} %ids.7, s32[4]{0:T(128)} %pad_add_fusion.place_of.refs_0_, bf16[2,256,1024]{2,1,0:T(8,128)(2,1)} %copy-done.1, bf16[2,256,1024]{2,1,0:T(8,128)(2,1)} %copy-done.10, bf16[256,1024]{1,0:T(8,128)(2,1)} %collective-permute-done.14.refs_3_, ...), custom_call_target="tpu_custom_call" | custom-call | flops 536870912 | bytes 7340040 | tf_op jit(solution)/shard_map/line_grads/pallas_call | solution.py:422
  204.5 0.6 collective-permute-done.22
  205.2 4.1 %collective-permute-done.20.by_tensor = bf16[256,1024]{1,0:T(8,128)(2,1)S(1)} collective-permute-done((bf16[256,1024]{1,0:T(8,128)(2,1)S(1)}, bf16[256,1024]{1,0:T(8,128)(2,1)S(1)}, u32[]{:S(2)}, u32[]{:S(2)}) %collective-permute-start.20) | collective-permute-done | bytes 524320 | tf_op jit(solution)/shard_map/ppermute | solution.py:540
  209.3 2.2 broadcast_select_fusion
  211.5 0.8 copy-done.17
  212.3 3.0 %assemble.1 = bf16[256,4096]{1,0:T(8,128)(2,1)} custom-call(s32[4]{0:T(128)} %pad_add_fusion.place_of.refs_0_, bf16[256,1024]{1,0:T(8,128)(2,1)} %copy-done.4, bf16[256,1024]{1,0:T(8,128)(2,1)} %copy-done.14, bf16[256,1024]{1,0:T(8,128)(2,1)} %copy-done.13, bf16[256,1024]{1,0:T(8,128)(2,1)} %copy-done.17), custom_call_target="tpu_custom_call" | custom-call | bytes 4194304 | tf_op jit(solution)/shard_map/assemble/pallas_call | solution.py:353
  (59 shorter events, 0.4 us)
Async XLA Ops:
  7.2 85.1 %all-gather.5.cloned.1.call-start = ((), (), s32[]{:S(2)}) async-start(), calls=%async_computation | async-start | bytes 2621440 | tf_op jit(solution)/shard_map/all_gather | solution.py:491
  10.4 28.3 %collective-permute-start = (bf16[33,128,128]{2,1,0:T(8,128)(2,1)}, bf16[33,128,128]{2,1,0:T(8,128)(2,1)S(1)}, u32[]{:S(2)}, u32[]{:S(2)}) collective-permute-start(bf16[33,128,128]{2,1,0:T(8,128)(2,1)} %pad_maximum_fusion), channel_id=1, source_target_pairs={{0,4},{12,8},{1,5},{13,9},{2,6},{14,10},{3,7},{15,11},{16,20},{28,... | collective-permute-start | bytes 3244040 | tf_op jit(solution)/shard_map/ppermute | solution.py:474
  15.4 23.4 %collective-permute-start.1 = (bf16[33,128,128]{2,1,0:T(8,128)(2,1)}, bf16[33,128,128]{2,1,0:T(8,128)(2,1)}, u32[]{:S(2)}, u32[]{:S(2)}) collective-permute-start(bf16[33,128,128]{2,1,0:T(8,128)(2,1)} %pad_maximum_fusion), channel_id=1, source_target_pairs={{4,8},{8,4},{5,9},{9,5},{6,10},{10,6},{7,11},{11,7},{20,24},{24,20... | collective-permute-start | bytes 3244040 | tf_op jit(solution)/shard_map/ppermute | solution.py:475
  17.1 8.1 %copy-start.5 = (bf16[256,1024]{1,0:T(8,128)(2,1)S(1)}, bf16[256,1024]{1,0:T(8,128)(2,1)}, u32[]{:S(2)}) copy-start(bf16[256,1024]{1,0:T(8,128)(2,1)} %upstream.1) | copy-start | bytes 1572868
  24.0 1.8 copy-start
  25.7 44.6 %copy-start.9 = (bf16[512,1024]{1,0:T(8,128)(2,1)}, bf16[512,1024]{1,0:T(8,128)(2,1)S(1)}, u32[]{:S(2)}) copy-start(bf16[512,1024]{1,0:T(8,128)(2,1)S(1)} %pad_maximum_fusion.1) | copy-start | bytes 3145732
  38.7 40.6 %copy-start.7 = (bf16[33,128,128]{2,1,0:T(8,128)(2,1)}, bf16[33,128,128]{2,1,0:T(8,128)(2,1)S(1)}, u32[]{:S(2)}) copy-start(bf16[33,128,128]{2,1,0:T(8,128)(2,1)S(1)} %collective-permute-done.near_a) | copy-start | bytes 3244036
  38.7 30.6 %collective-permute-start.3 = (bf16[33,128,128]{2,1,0:T(8,128)(2,1)S(1)}, bf16[33,128,128]{2,1,0:T(8,128)(2,1)}, u32[]{:S(2)}, u32[]{:S(2)}) collective-permute-start(bf16[33,128,128]{2,1,0:T(8,128)(2,1)S(1)} %collective-permute-done.near_a), channel_id=1, source_target_pairs={{4,8},{8,4},{5,9},{9,5},{6,10},{10,6},{7,11},{11,7},{20,24},{24,20... | collective-permute-start | bytes 3244040 | tf_op jit(solution)/shard_map/ppermute | solution.py:482
  40.4 28.9 %collective-permute-start.4 = (bf16[33,128,128]{2,1,0:T(8,128)(2,1)}, bf16[33,128,128]{2,1,0:T(8,128)(2,1)}, u32[]{:S(2)}, u32[]{:S(2)}) collective-permute-start(bf16[33,128,128]{2,1,0:T(8,128)(2,1)} %collective-permute-done.1.far_a), channel_id=1, source_target_pairs={{0,16},{16,0},{1,17},{17,1},{2,18},{18,2},{3,19},{19,3},{4,20},{20... | collective-permute-start | bytes 3244040 | tf_op jit(solution)/shard_map/ppermute | solution.py:483
  41.9 27.4 %collective-permute-start.2 = (bf16[512,1024]{1,0:T(8,128)(2,1)S(1)}, bf16[512,1024]{1,0:T(8,128)(2,1)S(1)}, u32[]{:S(2)}, u32[]{:S(2)}) collective-permute-start(bf16[512,1024]{1,0:T(8,128)(2,1)S(1)} %pad_maximum_fusion.1), channel_id=1, source_target_pairs={{0,4},{12,8},{4,0},{8,12},{1,5},{13,9},{5,1},{9,13},{2,6},{14,10},... | collective-permute-start | bytes 3145736 | tf_op jit(solution)/shard_map/ppermute | solution.py:484
  70.4 96.8 %all-gather.7.cloned.1.call-start = ((), (), s32[]{:S(2)}) async-start(), calls=%async_computation.1 | async-start | bytes 2621440 | tf_op jit(solution)/shard_map/all_gather | solution.py:516
  70.4 25.4 %collective-permute-start.6 = (bf16[33,128,128]{2,1,0:T(8,128)(2,1)}, bf16[33,128,128]{2,1,0:T(8,128)(2,1)}, u32[]{:S(2)}, u32[]{:S(2)}) collective-permute-start(bf16[33,128,128]{2,1,0:T(8,128)(2,1)} %collective-permute-done.3.end_a), channel_id=1, source_target_pairs={{0,16},{16,0},{1,17},{17,1},{2,18},{18,2},{3,19},{19,3},{4,20},{20... | collective-permute-start | bytes 3244040 | tf_op jit(solution)/shard_map/ppermute | solution.py:489
  71.0 24.8 %collective-permute-start.5 = (bf16[32,128,128]{2,1,0:T(8,128)(2,1)}, bf16[32,128,128]{2,1,0:T(8,128)(2,1)S(1)}, u32[]{:S(2)}, u32[]{:S(2)}) collective-permute-start(bf16[32,128,128]{2,1,0:T(8,128)(2,1)} %constant_dynamic-slice_fusion.1), channel_id=1, source_target_pairs={{0,4},{12,8},{1,5},{13,9},{2,6},{14,10},{3,7},{15,11},{16,20},{28,... | collective-permute-start | bytes 3145736 | tf_op jit(solution)/shard_map/ppermute | solution.py:488
  75.5 20.3 %collective-permute-start.7 = (bf16[512,1024]{1,0:T(8,128)(2,1)}, bf16[512,1024]{1,0:T(8,128)(2,1)S(1)}, u32[]{:S(2)}, u32[]{:S(2)}) collective-permute-start(bf16[512,1024]{1,0:T(8,128)(2,1)} %copy-done.9), channel_id=1, source_target_pairs={{4,8},{8,4},{5,9},{9,5},{6,10},{10,6},{7,11},{11,7},{20,24},{24,20... | collective-permute-start | bytes 3145736 | tf_op jit(solution)/shard_map/ppermute | solution.py:490
  95.8 3.0 %copy-start.8 = (bf16[32,128,128]{2,1,0:T(8,128)(2,1)}, bf16[32,128,128]{2,1,0:T(8,128)(2,1)S(1)}, u32[]{:S(2)}) copy-start(bf16[32,128,128]{2,1,0:T(8,128)(2,1)S(1)} %collective-permute-done.5.near_b) | copy-start | bytes 3145732
  95.8 28.2 %copy-start.2 = (bf16[512,1024]{1,0:T(8,128)(2,1)}, bf16[512,1024]{1,0:T(8,128)(2,1)S(1)}, u32[]{:S(2)}) copy-start(bf16[512,1024]{1,0:T(8,128)(2,1)S(1)} %collective-permute-done.7.refs_1_) | copy-start | bytes 3145732
  95.8 13.6 %collective-permute-start.10 = (bf16[2,256,1024]{2,1,0:T(8,128)(2,1)}, bf16[2,256,1024]{2,1,0:T(8,128)(2,1)}, u32[]{:S(2)}, u32[]{:S(2)}) collective-permute-start(bf16[2,256,1024]{2,1,0:T(8,128)(2,1)} %constant_dynamic-slice_fusion), channel_id=1, source_target_pairs={{4,8},{8,4},{5,9},{9,5},{6,10},{10,6},{7,11},{11,7},{20,24},{24,20... | collective-permute-start | bytes 3145736 | tf_op jit(solution)/shard_map/ppermute | solution.py:501
  97.5 26.6 %collective-permute-start.11 = (bf16[512,1024]{1,0:T(8,128)(2,1)S(1)}, bf16[512,1024]{1,0:T(8,128)(2,1)S(1)}, u32[]{:S(2)}, u32[]{:S(2)}) collective-permute-start(bf16[512,1024]{1,0:T(8,128)(2,1)S(1)} %collective-permute-done.7.refs_1_), channel_id=1, source_target_pairs={{4,0},{8,12},{5,1},{9,13},{6,2},{10,14},{7,3},{11,15},{20,16},{24,... | collective-permute-start | bytes 3145736 | tf_op jit(solution)/shard_map/ppermute | solution.py:502
  102.6 2.2 collective-permute-start.8
  102.7 2.9 %collective-permute-start.9 = (bf16[256,1024]{1,0:T(8,128)(2,1)}, bf16[256,1024]{1,0:T(8,128)(2,1)S(1)}, u32[]{:S(2)}, u32[]{:S(2)}) collective-permute-start(bf16[256,1024]{1,0:T(8,128)(2,1)} %get-tuple-element.79), channel_id=1, source_target_pairs={{0,1},{1,0},{2,3},{3,2},{4,5},{5,4},{6,7},{7,6},{8,9},{9,8},{10,11... | collective-permute-start | bytes 1572872 | tf_op jit(solution)/shard_map/ppermute | solution.py:507
  104.8 0.8 copy-start.15
  105.5 0.8 copy-start.16
  106.3 20.1 %copy-start.6 = (bf16[256,1024]{1,0:T(8,128)(2,1)S(1)}, bf16[256,1024]{1,0:T(8,128)(2,1)}, u32[]{:S(2)}) copy-start(bf16[256,1024]{1,0:T(8,128)(2,1)} %get-tuple-element.100.end_upstream.refs_1_) | copy-start | bytes 1572868
  109.4 18.5 %copy-start.19 = (bf16[256,1024]{1,0:T(8,128)(2,1)S(1)}, bf16[256,1024]{1,0:T(8,128)(2,1)}, u32[]{:S(2)}) copy-start(bf16[256,1024]{1,0:T(8,128)(2,1)} %get-tuple-element.85) | copy-start | bytes 1572868
  124.0 9.4 %copy-start.3 = (bf16[512,1024]{1,0:T(8,128)(2,1)}, bf16[512,1024]{1,0:T(8,128)(2,1)S(1)}, u32[]{:S(2)}) copy-start(bf16[512,1024]{1,0:T(8,128)(2,1)S(1)} %collective-permute-done.11.refs_2_) | copy-start | bytes 3145732
  125.0 8.4 %collective-permute-start.13 = (bf16[2,256,1024]{2,1,0:T(8,128)(2,1)}, bf16[2,256,1024]{2,1,0:T(8,128)(2,1)}, u32[]{:S(2)}, u32[]{:S(2)}) collective-permute-start(bf16[2,256,1024]{2,1,0:T(8,128)(2,1)} %get-tuple-element.87), channel_id=1, source_target_pairs={{0,1},{1,0},{2,3},{3,2},{4,5},{5,4},{6,7},{7,6},{8,9},{9,8},{10,11... | collective-permute-start | bytes 3145736 | tf_op jit(solution)/shard_map/ppermute | solution.py:513
  125.1 33.1 %collective-permute-start.17 = (bf16[2,256,1024]{2,1,0:T(8,128)(2,1)}, bf16[2,256,1024]{2,1,0:T(8,128)(2,1)S(1)}, u32[]{:S(2)}, u32[]{:S(2)}) collective-permute-start(bf16[2,256,1024]{2,1,0:T(8,128)(2,1)} %collective-permute-done.10), channel_id=1, source_target_pairs={{4,0},{8,12},{5,1},{9,13},{6,2},{10,14},{7,3},{11,15},{20,16},{24,... | collective-permute-start | bytes 3145736 | tf_op jit(solution)/shard_map/ppermute | solution.py:514
  126.4 10.3 %collective-permute-start.14 = (bf16[256,1024]{1,0:T(8,128)(2,1)S(1)}, bf16[256,1024]{1,0:T(8,128)(2,1)}, u32[]{:S(2)}, u32[]{:S(2)}) collective-permute-start(bf16[256,1024]{1,0:T(8,128)(2,1)S(1)} %copy-done.6), channel_id=1, source_target_pairs={{4,8},{8,4},{5,9},{9,5},{6,10},{10,6},{7,11},{11,7},{20,24},{24,20... | collective-permute-start | bytes 1572872 | tf_op jit(solution)/shard_map/ppermute | solution.py:515
  127.9 22.4 %collective-permute-start.12 = (bf16[256,1024]{1,0:T(8,128)(2,1)S(1)}, bf16[256,1024]{1,0:T(8,128)(2,1)S(1)}, u32[]{:S(2)}, u32[]{:S(2)}) collective-permute-start(bf16[256,1024]{1,0:T(8,128)(2,1)S(1)} %copy-done.19), channel_id=1, source_target_pairs={{0,2},{2,0},{1,3},{3,1},{4,6},{6,4},{5,7},{7,5},{8,10},{10,8},{9,1... | collective-permute-start | bytes 1572872 | tf_op jit(solution)/shard_map/ppermute | solution.py:512
  158.2 1.8 copy-start.11
  159.9 15.8 %copy-start.1 = (bf16[2,256,1024]{2,1,0:T(8,128)(2,1)}, bf16[2,256,1024]{2,1,0:T(8,128)(2,1)S(1)}, u32[]{:S(2)}) copy-start(bf16[2,256,1024]{2,1,0:T(8,128)(2,1)S(1)} %add.33.refs_1_) | copy-start | bytes 3145732
  159.9 34.3 %collective-permute-start.18 = (bf16[2,256,1024]{2,1,0:T(8,128)(2,1)S(1)}, bf16[2,256,1024]{2,1,0:T(8,128)(2,1)S(1)}, u32[]{:S(2)}, u32[]{:S(2)}) collective-permute-start(bf16[2,256,1024]{2,1,0:T(8,128)(2,1)S(1)} %add.33.refs_1_), channel_id=1, source_target_pairs={{0,1},{1,0},{2,3},{3,2},{4,5},{5,4},{6,7},{7,6},{8,9},{9,8},{10,11... | collective-permute-start | bytes 3145736 | tf_op jit(solution)/shard_map/ppermute | solution.py:528
  161.0 21.9 %collective-permute-start.15 = (bf16[256,1024]{1,0:T(8,128)(2,1)}, bf16[256,1024]{1,0:T(8,128)(2,1)S(1)}, u32[]{:S(2)}, u32[]{:S(2)}) collective-permute-start(bf16[256,1024]{1,0:T(8,128)(2,1)} %add.32), channel_id=1, source_target_pairs={{4,0},{8,12},{5,1},{9,13},{6,2},{10,14},{7,3},{11,15},{20,16},{24,... | collective-permute-start | bytes 1572872 | tf_op jit(solution)/shard_map/ppermute | solution.py:522
  162.3 20.6 %collective-permute-start.16 = (bf16[256,1024]{1,0:T(8,128)(2,1)}, bf16[256,1024]{1,0:T(8,128)(2,1)}, u32[]{:S(2)}, u32[]{:S(2)}) collective-permute-start(bf16[256,1024]{1,0:T(8,128)(2,1)} %get-tuple-element.98), channel_id=1, source_target_pairs={{0,2},{2,0},{1,3},{3,1},{4,6},{6,4},{5,7},{7,5},{8,10},{10,8},{9,1... | collective-permute-start | bytes 1572872 | tf_op jit(solution)/shard_map/ppermute | solution.py:523
  164.5 29.7 %collective-permute-start.19 = (bf16[256,1024]{1,0:T(8,128)(2,1)}, bf16[256,1024]{1,0:T(8,128)(2,1)}, u32[]{:S(2)}, u32[]{:S(2)}) collective-permute-start(bf16[256,1024]{1,0:T(8,128)(2,1)} %collective-permute-done.14.refs_3_), channel_id=1, source_target_pairs={{4,0},{8,12},{5,1},{9,13},{6,2},{10,14},{7,3},{11,15},{20,16},{24,... | collective-permute-start | bytes 1572872 | tf_op jit(solution)/shard_map/ppermute | solution.py:524
  165.8 39.4 %collective-permute-start.22 = (bf16[256,1024]{1,0:T(8,128)(2,1)}, bf16[256,1024]{1,0:T(8,128)(2,1)}, u32[]{:S(2)}, u32[]{:S(2)}) collective-permute-start(bf16[256,1024]{1,0:T(8,128)(2,1)} %get-tuple-element.108), channel_id=1, source_target_pairs={{4,0},{8,12},{5,1},{9,13},{6,2},{10,14},{7,3},{11,15},{20,16},{24,... | collective-permute-start | bytes 1572872 | tf_op jit(solution)/shard_map/ppermute | solution.py:535
  167.2 27.0 %copy-start.12 = (bf16[256,1024]{1,0:T(8,128)(2,1)S(1)}, bf16[256,1024]{1,0:T(8,128)(2,1)}, u32[]{:S(2)}) copy-start(bf16[256,1024]{1,0:T(8,128)(2,1)} %get-tuple-element.95) | copy-start | bytes 1572868
  194.2 2.2 copy-start.10
  195.7 8.8 %copy-start.4 = (bf16[256,1024]{1,0:T(8,128)(2,1)}, bf16[256,1024]{1,0:T(8,128)(2,1)S(1)}, u32[]{:S(2)}) copy-start(bf16[256,1024]{1,0:T(8,128)(2,1)S(1)} %add_select_fusion.own) | copy-start | bytes 1572868
  195.7 13.6 %copy-start.18 = (bf16[256,1024]{1,0:T(8,128)(2,1)S(1)}, bf16[256,1024]{1,0:T(8,128)(2,1)}, u32[]{:S(2)}) copy-start(bf16[256,1024]{1,0:T(8,128)(2,1)} %get-tuple-element.94) | copy-start | bytes 1572868
  195.7 13.5 %collective-permute-start.20 = (bf16[256,1024]{1,0:T(8,128)(2,1)S(1)}, bf16[256,1024]{1,0:T(8,128)(2,1)S(1)}, u32[]{:S(2)}, u32[]{:S(2)}) collective-permute-start(bf16[256,1024]{1,0:T(8,128)(2,1)S(1)} %add_select_fusion.own), channel_id=1, source_target_pairs={{0,2},{2,0},{1,3},{3,1},{4,6},{6,4},{5,7},{7,5},{8,10},{10,8},{9,1... | collective-permute-start | bytes 1572872 | tf_op jit(solution)/shard_map/ppermute | solution.py:540
  196.4 12.9 %collective-permute-start.21 = (bf16[256,1024]{1,0:T(8,128)(2,1)S(1)}, bf16[256,1024]{1,0:T(8,128)(2,1)S(1)}, u32[]{:S(2)}, u32[]{:S(2)}) collective-permute-start(bf16[256,1024]{1,0:T(8,128)(2,1)S(1)} %add_select_fusion.own), channel_id=1, source_target_pairs={{0,1},{1,0},{2,3},{3,2},{4,5},{5,4},{6,7},{7,6},{8,9},{9,8},{10,11... | collective-permute-start | bytes 1572872 | tf_op jit(solution)/shard_map/ppermute | solution.py:540
  209.2 2.3 %copy-start.13 = (bf16[256,1024]{1,0:T(8,128)(2,1)}, bf16[256,1024]{1,0:T(8,128)(2,1)S(1)}, u32[]{:S(2)}) copy-start(bf16[256,1024]{1,0:T(8,128)(2,1)S(1)} %collective-permute-done.20.by_tensor) | copy-start | bytes 1572868
  209.2 2.3 %copy-start.14 = (bf16[256,1024]{1,0:T(8,128)(2,1)}, bf16[256,1024]{1,0:T(8,128)(2,1)S(1)}, u32[]{:S(2)}) copy-start(bf16[256,1024]{1,0:T(8,128)(2,1)S(1)} %collective-permute-done.21.by_core) | copy-start | bytes 1572868
  209.2 2.3 %collective-permute-start.23 = (bf16[256,1024]{1,0:T(8,128)(2,1)S(1)}, bf16[256,1024]{1,0:T(8,128)(2,1)S(1)}, u32[]{:S(2)}, u32[]{:S(2)}) collective-permute-start(bf16[256,1024]{1,0:T(8,128)(2,1)S(1)} %collective-permute-done.20.by_tensor), channel_id=1, source_target_pairs={{0,1},{1,0},{2,3},{3,2},{4,5},{5,4},{6,7},{7,6},{8,9},{9,8},{10,11... | collective-permute-start | bytes 1572872 | tf_op jit(solution)/shard_map/ppermute | solution.py:542
  211.5 0.8 copy-start.17
Sparse Core Ops, SparseCore 0:
  70.5 21.7 all-gather.4
  125.1 29.7 all-gather.6

commit v24 on v16

--- a/solution.py
+++ b/solution.py
@@ -381,7 +381,7 @@
     cols_n = pairs[0][1].shape[1] // size
     rows_n = first.shape[-1] // size * (first.shape[0] if len(first.shape) == 3 else 1)
     total = rows_n * cols_n
-    group = math.gcd(slots, 8)
+    group = math.gcd(slots, 16)
 
     @pl.loop(0, slots // group)
     def some(g):
@@ -515,9 +515,11 @@
     quarter = jnp.where(middle, own_keep + own_got, sum_out)
     proj_out = along(end_proj, perm=OUTWARD)
     grads = line_grads(block_ids, ((tokens_2, both_2m, both_2o),), grads, size)
-    by_tensor, by_core, grads = stage((sideways(quarter), cores(quarter), grads))
+    projected = jnp.where(middle, proj, proj_out)
+    by_tensor, by_core, grads, projected = stage(
+        (sideways(quarter), cores(quarter), grads, projected)
+    )
     by_both = cores(by_tensor)
-    projected = jnp.where(middle, proj, proj_out)
     token_grad = assemble(place_of, (quarter, by_core, by_tensor, by_both))
     grads = line_grads(block_ids, ((tokens_3, both_3m, both_3o),), grads, size)
     return projected, token_grad, grads

time: 207 us -> 210 us (1.014)
  waiting for transfers between devices: 84 us -> 88.9 us
  Pallas kernels: 57.5 us -> 54.7 us
    ppermute x1, waiting for transfers between devices: 0.01 us -> 12.1 us  [line_body(): proj_out = along(end_proj, perm=OUTWARD)]
    ppermute x1, waiting for transfers between devices: 9.46 us -> 0.01 us  [line_body(): sideways(quarter)]
    pallas_call x4, Pallas kernels: 31.7 us -> 28.7 us  [line_grads(): pl.pallas_call(functools.partial(line_grads_kernel, len(pairs)), out_shap...]
  transfers between devices with their start and end apart: 24 -> 24, of which waited for: 11 -> 10; matrix products, arithmetic and copies ran while one was open for 5% -> 5% of each run, Pallas kernels for 24% -> 23%
where the time goes in v24:
time: 210 us; the launch traced here: 208 us
  waiting for transfers between devices  88.9 us (42%)
  Pallas kernels  54.7 us (26%)
  starting transfers between devices  31.9 us (15%)
  between operations  14 us (7%)
  other arithmetic  10.8 us (5%)
  local copies, waits for them, and re-layouts  8.14 us (4%)
    pallas_call x4, Pallas kernels, line_grads(): pl.pallas_call(functools.partial(line_grads_kernel, len(pairs)), out_shap...  28.7 us
    ppermute x1, waiting for transfers between devices, line_body(): both_1 = along(both, perm=PAIRS)  21.7 us
    ppermute x1, waiting for transfers between devices, line_body(): both_2o = along(both_2m, perm=OUTWARD)  14 us
    ppermute x1, waiting for transfers between devices, line_body(): near_a = along(mine, perm=INWARD)  12.4 us
    ppermute x1, waiting for transfers between devices, line_body(): proj_out = along(end_proj, perm=OUTWARD)  12.1 us
    ppermute x1, waiting for transfers between devices, line_body(): end_got = sideways(end_give)  9.48 us
    pallas_call x1, Pallas kernels, place_first(): pl.pallas_call(place_kernel, out_shape=(jax.ShapeDtypeStruct((depth, widt...  8.72 us
    ppermute x1, waiting for transfers between devices, line_body(): near_b = along(other, perm=INWARD)  7.51 us
  transfers between devices with their start and end apart: 24, of which 10 were waited for; matrix products, arithmetic and copies ran while one was open for 5% of the time, Pallas kernels for 23%

profile of v24, /device:TPU:0, one launch (start us, length us, event | category | flops | bytes accessed | tf_op | source)
XLA Modules:
  0.0 208.4 jit_solution(17225988935422087843)
XLA Ops:
  7.2 0.0 all-gather.7.cloned.1.call-start
  7.2 0.7 convert_element_type.26
  7.9 0.1 convert_element_type.27
  8.0 1.3 constant_dynamic-slice_fusion.2
  9.3 1.1 pad_maximum_fusion
  10.4 5.0 %collective-permute-start = (bf16[33,128,128]{2,1,0:T(8,128)(2,1)}, bf16[33,128,128]{2,1,0:T(8,128)(2,1)S(1)}, u32[]{:S(2)}, u32[]{:S(2)}) collective-permute-start(bf16[33,128,128]{2,1,0:T(8,128)(2,1)} %pad_maximum_fusion), channel_id=1, source_target_pairs={{0,4},{12,8},{1,5},{13,9},{2,6},{14,10},{3,7},{15,11},{16,20},{28,... | collective-permute-start | bytes 3244040 | tf_op jit(solution)/shard_map/ppermute | solution.py:463
  15.4 1.6 collective-permute-start.1
  17.0 6.3 %line_grads.4.refs_2_ = bf16[64,128,128]{2,1,0:T(8,128)(2,1)} custom-call(s32[64]{0:T(128)} %ids.7, bf16[256,4096]{1,0:T(8,128)(2,1)} %tokens.1, bf16[256,1024]{1,0:T(8,128)(2,1)} %upstream.1), custom_call_target="tpu_custom_call" | custom-call | flops 536870912 | bytes 4718592 | tf_op jit(solution)/shard_map/line_grads/pallas_call | solution.py:411
  23.4 1.2 constant_dynamic-slice_fusion.1
  24.6 0.1 pad_maximum_fusion.1
  24.7 0.4 copy-done
  25.1 1.2 constant_dynamic-slice_fusion
  26.3 12.4 %collective-permute-done.near_a = bf16[33,128,128]{2,1,0:T(8,128)(2,1)S(1)} collective-permute-done((bf16[33,128,128]{2,1,0:T(8,128)(2,1)}, bf16[33,128,128]{2,1,0:T(8,128)(2,1)S(1)}, u32[]{:S(2)}, u32[]{:S(2)}) %collective-permute-start) | collective-permute-done | bytes 1081376 | tf_op jit(solution)/shard_map/ppermute | solution.py:463
  38.7 1.7 collective-permute-start.3
  40.4 1.5 collective-permute-start.4
  41.9 5.7 %collective-permute-start.2 = (bf16[512,1024]{1,0:T(8,128)(2,1)S(1)}, bf16[512,1024]{1,0:T(8,128)(2,1)S(1)}, u32[]{:S(2)}, u32[]{:S(2)}) collective-permute-start(bf16[512,1024]{1,0:T(8,128)(2,1)S(1)} %pad_maximum_fusion.1), channel_id=1, source_target_pairs={{0,4},{12,8},{4,0},{8,12},{1,5},{13,9},{5,1},{9,13},{2,6},{14,10},... | collective-permute-start | bytes 3145736 | tf_op jit(solution)/shard_map/ppermute | solution.py:473
  47.6 21.7 %collective-permute-done.2 = bf16[512,1024]{1,0:T(8,128)(2,1)S(1)} collective-permute-done((bf16[512,1024]{1,0:T(8,128)(2,1)S(1)}, bf16[512,1024]{1,0:T(8,128)(2,1)S(1)}, u32[]{:S(2)}, u32[]{:S(2)}) %collective-permute-start.2) | collective-permute-done | bytes 1048608 | tf_op jit(solution)/shard_map/ppermute | solution.py:473
  69.3 1.1 copy-done.9
  70.4 1.0 fusion
  71.4 0.0 all-gather.9.cloned.1.call-start
  71.5 0.6 collective-permute-start.6
  72.1 3.7 %collective-permute-start.5 = (bf16[32,128,128]{2,1,0:T(8,128)(2,1)}, bf16[32,128,128]{2,1,0:T(8,128)(2,1)S(1)}, u32[]{:S(2)}, u32[]{:S(2)}) collective-permute-start(bf16[32,128,128]{2,1,0:T(8,128)(2,1)} %constant_dynamic-slice_fusion), channel_id=1, source_target_pairs={{0,4},{12,8},{1,5},{13,9},{2,6},{14,10},{3,7},{15,11},{16,20},{28,... | collective-permute-start | bytes 3145736 | tf_op jit(solution)/shard_map/ppermute | solution.py:477
  75.8 0.7 collective-permute-start.7
  76.5 0.7 pad_add_fusion.place_of
  77.2 1.3 bitcast_convert_fusion
  78.4 1.2 bitcast_convert_fusion.1.ids_3
  79.6 8.7 %place_first.1 = (bf16[4096,1024]{1,0:T(8,128)(2,1)}, bf16[1024,4096]{1,0:T(8,128)(2,1)}) custom-call(s32[4]{0:T(128)} %pad_add_fusion.place_of, s32[64]{0:T(128)} %ids.7, s32[64]{0:T(128)} %get-tuple-element.106.ids_1, s32[64]{0:T(128)} %get-tuple-element.105.ids_2, s32[64]{0:T(128)} %bitcast_convert_fusion.1.ids_3, bf16[64,128,128]{2,1,0:T(8,128)(2,1)} %own.1, ...), custom_call_target="tpu_custom_call" | custom-call | bytes 25165824 | tf_op jit(solution)/shard_map/place_first/pallas_call | solution.py:181
  88.4 7.5 %collective-permute-done.5.near_b = bf16[32,128,128]{2,1,0:T(8,128)(2,1)S(1)} collective-permute-done((bf16[32,128,128]{2,1,0:T(8,128)(2,1)}, bf16[32,128,128]{2,1,0:T(8,128)(2,1)S(1)}, u32[]{:S(2)}, u32[]{:S(2)}) %collective-permute-start.5) | collective-permute-done | bytes 1048608 | tf_op jit(solution)/shard_map/ppermute | solution.py:477
  95.9 0.0 all-gather.7.cloned.1.call-done
  95.9 0.9 copy-done.8
  96.9 0.7 collective-permute-start.10
  97.6 1.3 collective-permute-start.11
  98.9 3.8 %project_back.1 = (bf16[2,256,1024]{2,1,0:T(8,128)(2,1)}, bf16[2,256,1024]{2,1,0:T(8,128)(2,1)}, bf16[2,256,1024]{2,1,0:T(8,128)(2,1)}, bf16[256,1024]{1,0:T(8,128)(2,1)}, bf16[256,1024]{1,0:T(8,128)(2,1)}) custom-call(s32[4]{0:T(128)} %pad_add_fusion.place_of, s32[64]{0:T(128)} %get-tuple-element.106.ids_1, s32[64]{0:T(128)} %bitcast_convert_fusion.1.ids_3, ...), custom_call_target="tpu_custom_call" | custom-call | flops 4294967296 | bytes 13631488 | tf_op jit(solution)/shard_map/project_back/pallas_call | solution.py:239
  102.7 0.1 collective-permute-start.8
  102.8 0.5 collective-permute-start.9
  103.3 1.6 collective-permute-done.8.refs_0_
  104.9 0.9 collective-permute-done.9.refs_1_
  105.8 3.0 %add_split.2 = (bf16[256,1024]{1,0:T(8,128)(2,1)}, bf16[256,1024]{1,0:T(8,128)(2,1)}) custom-call(s32[4]{0:T(128)} %pad_add_fusion.place_of, bf16[2,256,1024]{2,1,0:T(8,128)(2,1)} %get-tuple-element.69.keep, bf16[256,1024]{1,0:T(8,128)(2,1)} %copy-done.15, bf16[256,1024]{1,0:T(8,128)(2,1)} %collective-permute-done.9.refs_1_), custom_call_target="tpu_custom_call" | custom-call | flops 524288 | bytes 3145728 | tf_op jit(solution)/shard_map/add_split/pallas_call | solution.py:328
  108.8 14.0 %collective-permute-done.11.refs_2_ = bf16[512,1024]{1,0:T(8,128)(2,1)S(1)} collective-permute-done((bf16[512,1024]{1,0:T(8,128)(2,1)S(1)}, bf16[512,1024]{1,0:T(8,128)(2,1)S(1)}, u32[]{:S(2)}, u32[]{:S(2)}) %collective-permute-start.11) | collective-permute-done | bytes 1048608 | tf_op jit(solution)/shard_map/ppermute | solution.py:490
  122.8 0.9 slice_add_fusion.1
  123.8 0.0 all-gather.11.cloned.1.call-start
  123.8 0.1 collective-permute-start.13
  123.9 1.5 collective-permute-start.12
  125.4 1.3 collective-permute-start.16
  126.7 3.9 %project_forward.1 = (bf16[256,1024]{1,0:T(8,128)(2,1)}, bf16[256,1024]{1,0:T(8,128)(2,1)}) custom-call(s32[4]{0:T(128)} %pad_add_fusion.place_of, s32[64]{0:T(128)} %get-tuple-element.106.ids_1, s32[64]{0:T(128)} %bitcast_convert_fusion.1.ids_3, bf16[4096,1024]{1,0:T(8,128)(2,1)} %get-tuple-element.82.partial, bf16[32,128,128]{2,1,0:T(8,128)(2,1)} %copy-done.8, ...), custom_call_target="tpu_custom_call" | custom-call | flops 536870912 | bytes 4194304 | tf_op jit(solution)/shard_map/project_forward/pallas_call | solution.py:296
  130.6 3.5 %add_split.3 = (bf16[256,1024]{1,0:T(8,128)(2,1)}, bf16[256,1024]{1,0:T(8,128)(2,1)}) custom-call(s32[4]{0:T(128)} %pad_add_fusion.place_of, bf16[2,256,1024]{2,1,0:T(8,128)(2,1)} %get-tuple-element.78.keep, bf16[2,256,1024]{2,1,0:T(8,128)(2,1)} %collective-permute-done.13.refs_0_), custom_call_target="tpu_custom_call" | custom-call | flops 524288 | bytes 3145728 | tf_op jit(solution)/shard_map/add_split/pallas_call | solution.py:328
  134.1 9.5 %collective-permute-done.12 = bf16[256,1024]{1,0:T(8,128)(2,1)} collective-permute-done((bf16[256,1024]{1,0:T(8,128)(2,1)}, bf16[256,1024]{1,0:T(8,128)(2,1)}, u32[]{:S(2)}, u32[]{:S(2)}) %collective-permute-start.12) | collective-permute-done | bytes 524320 | tf_op jit(solution)/shard_map/ppermute | solution.py:500
  143.6 2.0 add.28
  145.6 1.3 collective-permute-start.14
  146.9 2.5 %collective-permute-start.15 = (bf16[256,1024]{1,0:T(8,128)(2,1)}, bf16[256,1024]{1,0:T(8,128)(2,1)}, u32[]{:S(2)}, u32[]{:S(2)}) collective-permute-start(bf16[256,1024]{1,0:T(8,128)(2,1)} %get-tuple-element.89), channel_id=1, source_target_pairs={{0,2},{2,0},{1,3},{3,1},{4,6},{6,4},{5,7},{7,5},{8,10},{10,8},{9,1... | collective-permute-start | bytes 1572872 | tf_op jit(solution)/shard_map/ppermute | solution.py:510
  149.5 7.1 %line_grads.5.refs_3_ = bf16[64,128,128]{2,1,0:T(8,128)(2,1)} custom-call(s32[64]{0:T(128)} %ids.7, bf16[4,256,1024]{2,1,0:T(8,128)(2,1)} %bitcast.17, bf16[256,1024]{1,0:T(8,128)(2,1)} %get-tuple-element.103.end_upstream.refs_1_, bf16[64,128,128]{2,1,0:T(8,128)(2,1)} %line_grads.4.refs_2_), custom_call_target="tpu_custom_call" | custom-call | flops 536870912 | bytes 6815744 | tf_op jit(solution)/shard_map/line_grads/pallas_call | solution.py:411
  156.6 7.2 %collective-permute-done.14 = bf16[256,1024]{1,0:T(8,128)(2,1)S(1)} collective-permute-done((bf16[256,1024]{1,0:T(8,128)(2,1)}, bf16[256,1024]{1,0:T(8,128)(2,1)S(1)}, u32[]{:S(2)}, u32[]{:S(2)}) %collective-permute-start.14) | collective-permute-done | bytes 524320 | tf_op jit(solution)/shard_map/ppermute | solution.py:509
  163.7 0.9 slice_add_fusion
  164.6 1.3 collective-permute-start.19
  165.9 1.1 add_select_fusion.own
  167.1 0.7 collective-permute-start.17
  167.8 12.1 %collective-permute-done.19 = bf16[256,1024]{1,0:T(8,128)(2,1)S(1)} collective-permute-done((bf16[256,1024]{1,0:T(8,128)(2,1)}, bf16[256,1024]{1,0:T(8,128)(2,1)S(1)}, u32[]{:S(2)}, u32[]{:S(2)}) %collective-permute-start.19) | collective-permute-done | bytes 524320 | tf_op jit(solution)/shard_map/ppermute | solution.py:516
  179.9 0.9 broadcast_select_fusion
  180.8 7.7 %line_grads.6.refs_3_ = bf16[64,128,128]{2,1,0:T(8,128)(2,1)} custom-call(s32[64]{0:T(128)} %ids.7, bf16[4,256,1024]{2,1,0:T(8,128)(2,1)} %bitcast.18, bf16[512,1024]{1,0:T(8,128)(2,1)} %copy-done.1, bf16[512,1024]{1,0:T(8,128)(2,1)} %copy-done.3, bf16[64,128,128]{2,1,0:T(8,128)(2,1)} %line_grads.5.refs_3_), custom_call_target="tpu_custom_call" | custom-call | flops 536870912 | bytes 8388608 | tf_op jit(solution)/shard_map/line_grads/pallas_call | solution.py:411
  188.4 0.1 collective-permute-start.20
  188.5 1.9 collective-permute-done.20.by_both
  190.4 0.8 copy-done.16
  191.2 3.0 %assemble.1 = bf16[256,4096]{1,0:T(8,128)(2,1)} custom-call(s32[4]{0:T(128)} %pad_add_fusion.place_of, bf16[256,1024]{1,0:T(8,128)(2,1)} %copy-done.5, bf16[256,1024]{1,0:T(8,128)(2,1)} %copy-done.14, bf16[256,1024]{1,0:T(8,128)(2,1)} %copy-done.13, bf16[256,1024]{1,0:T(8,128)(2,1)} %copy-done.16), custom_call_target="tpu_custom_call" | custom-call | bytes 4194304 | tf_op jit(solution)/shard_map/assemble/pallas_call | solution.py:353
  194.2 7.6 %line_grads.7 = bf16[64,128,128]{2,1,0:T(8,128)(2,1)} custom-call(s32[64]{0:T(128)} %ids.7, bf16[4,256,1024]{2,1,0:T(8,128)(2,1)} %bitcast.19, bf16[512,1024]{1,0:T(8,128)(2,1)} %copy-done.2, bf16[512,1024]{1,0:T(8,128)(2,1)} %copy-done.4, bf16[64,128,128]{2,1,0:T(8,128)(2,1)} %line_grads.6.refs_3_), custom_call_target="tpu_custom_call" | custom-call | flops 536870912 | bytes 8388608 | tf_op jit(solution)/shard_map/line_grads/pallas_call | solution.py:411
  (49 shorter events, 0.2 us)
Async XLA Ops:
  7.2 88.8 %all-gather.7.cloned.1.call-start = ((), (), s32[]{:S(2)}) async-start(), calls=%async_computation | async-start | bytes 2621440 | tf_op jit(solution)/shard_map/all_gather | solution.py:480
  10.4 28.3 %collective-permute-start = (bf16[33,128,128]{2,1,0:T(8,128)(2,1)}, bf16[33,128,128]{2,1,0:T(8,128)(2,1)S(1)}, u32[]{:S(2)}, u32[]{:S(2)}) collective-permute-start(bf16[33,128,128]{2,1,0:T(8,128)(2,1)} %pad_maximum_fusion), channel_id=1, source_target_pairs={{0,4},{12,8},{1,5},{13,9},{2,6},{14,10},{3,7},{15,11},{16,20},{28,... | collective-permute-start | bytes 3244040 | tf_op jit(solution)/shard_map/ppermute | solution.py:463
  15.4 23.4 %collective-permute-start.1 = (bf16[33,128,128]{2,1,0:T(8,128)(2,1)}, bf16[33,128,128]{2,1,0:T(8,128)(2,1)}, u32[]{:S(2)}, u32[]{:S(2)}) collective-permute-start(bf16[33,128,128]{2,1,0:T(8,128)(2,1)} %pad_maximum_fusion), channel_id=1, source_target_pairs={{4,8},{8,4},{5,9},{9,5},{6,10},{10,6},{7,11},{11,7},{20,24},{24,20... | collective-permute-start | bytes 3244040 | tf_op jit(solution)/shard_map/ppermute | solution.py:464
  17.0 7.6 %copy-start.6 = (bf16[256,1024]{1,0:T(8,128)(2,1)S(1)}, bf16[256,1024]{1,0:T(8,128)(2,1)}, u32[]{:S(2)}) copy-start(bf16[256,1024]{1,0:T(8,128)(2,1)} %upstream.1) | copy-start | bytes 1572868
  23.4 1.8 copy-start
  25.1 46.3 %copy-start.10 = (bf16[512,1024]{1,0:T(8,128)(2,1)}, bf16[512,1024]{1,0:T(8,128)(2,1)S(1)}, u32[]{:S(2)}) copy-start(bf16[512,1024]{1,0:T(8,128)(2,1)S(1)} %pad_maximum_fusion.1) | copy-start | bytes 3145732
  38.7 40.9 %copy-start.7 = (bf16[33,128,128]{2,1,0:T(8,128)(2,1)}, bf16[33,128,128]{2,1,0:T(8,128)(2,1)S(1)}, u32[]{:S(2)}) copy-start(bf16[33,128,128]{2,1,0:T(8,128)(2,1)S(1)} %collective-permute-done.near_a) | copy-start | bytes 3244036
  38.7 30.6 %collective-permute-start.3 = (bf16[33,128,128]{2,1,0:T(8,128)(2,1)S(1)}, bf16[33,128,128]{2,1,0:T(8,128)(2,1)}, u32[]{:S(2)}, u32[]{:S(2)}) collective-permute-start(bf16[33,128,128]{2,1,0:T(8,128)(2,1)S(1)} %collective-permute-done.near_a), channel_id=1, source_target_pairs={{4,8},{8,4},{5,9},{9,5},{6,10},{10,6},{7,11},{11,7},{20,24},{24,20... | collective-permute-start | bytes 3244040 | tf_op jit(solution)/shard_map/ppermute | solution.py:471
  40.4 28.9 %collective-permute-start.4 = (bf16[33,128,128]{2,1,0:T(8,128)(2,1)}, bf16[33,128,128]{2,1,0:T(8,128)(2,1)}, u32[]{:S(2)}, u32[]{:S(2)}) collective-permute-start(bf16[33,128,128]{2,1,0:T(8,128)(2,1)} %collective-permute-done.1.far_a), channel_id=1, source_target_pairs={{0,16},{16,0},{1,17},{17,1},{2,18},{18,2},{3,19},{19,3},{4,20},{20... | collective-permute-start | bytes 3244040 | tf_op jit(solution)/shard_map/ppermute | solution.py:472
  41.9 27.4 %collective-permute-start.2 = (bf16[512,1024]{1,0:T(8,128)(2,1)S(1)}, bf16[512,1024]{1,0:T(8,128)(2,1)S(1)}, u32[]{:S(2)}, u32[]{:S(2)}) collective-permute-start(bf16[512,1024]{1,0:T(8,128)(2,1)S(1)} %pad_maximum_fusion.1), channel_id=1, source_target_pairs={{0,4},{12,8},{4,0},{8,12},{1,5},{13,9},{5,1},{9,13},{2,6},{14,10},... | collective-permute-start | bytes 3145736 | tf_op jit(solution)/shard_map/ppermute | solution.py:473
  69.3 1.1 copy-start.9
  71.4 109.3 %all-gather.9.cloned.1.call-start = ((), (), s32[]{:S(2)}) async-start(), calls=%async_computation.1 | async-start | bytes 2621440 | tf_op jit(solution)/shard_map/all_gather | solution.py:503
  71.5 24.4 %collective-permute-start.6 = (bf16[33,128,128]{2,1,0:T(8,128)(2,1)}, bf16[33,128,128]{2,1,0:T(8,128)(2,1)}, u32[]{:S(2)}, u32[]{:S(2)}) collective-permute-start(bf16[33,128,128]{2,1,0:T(8,128)(2,1)} %collective-permute-done.3.end_a), channel_id=1, source_target_pairs={{0,16},{16,0},{1,17},{17,1},{2,18},{18,2},{3,19},{19,3},{4,20},{20... | collective-permute-start | bytes 3244040 | tf_op jit(solution)/shard_map/ppermute | solution.py:478
  72.1 23.8 %collective-permute-start.5 = (bf16[32,128,128]{2,1,0:T(8,128)(2,1)}, bf16[32,128,128]{2,1,0:T(8,128)(2,1)S(1)}, u32[]{:S(2)}, u32[]{:S(2)}) collective-permute-start(bf16[32,128,128]{2,1,0:T(8,128)(2,1)} %constant_dynamic-slice_fusion), channel_id=1, source_target_pairs={{0,4},{12,8},{1,5},{13,9},{2,6},{14,10},{3,7},{15,11},{16,20},{28,... | collective-permute-start | bytes 3145736 | tf_op jit(solution)/shard_map/ppermute | solution.py:477
  75.8 20.1 %collective-permute-start.7 = (bf16[512,1024]{1,0:T(8,128)(2,1)}, bf16[512,1024]{1,0:T(8,128)(2,1)S(1)}, u32[]{:S(2)}, u32[]{:S(2)}) collective-permute-start(bf16[512,1024]{1,0:T(8,128)(2,1)} %copy-done.10), channel_id=1, source_target_pairs={{4,8},{8,4},{5,9},{9,5},{6,10},{10,6},{7,11},{11,7},{20,24},{24,20... | collective-permute-start | bytes 3145736 | tf_op jit(solution)/shard_map/ppermute | solution.py:479
  95.9 1.0 copy-start.8
  95.9 26.9 %copy-start.1 = (bf16[512,1024]{1,0:T(8,128)(2,1)}, bf16[512,1024]{1,0:T(8,128)(2,1)S(1)}, u32[]{:S(2)}) copy-start(bf16[512,1024]{1,0:T(8,128)(2,1)S(1)} %collective-permute-done.7.refs_1_) | copy-start | bytes 3145732
  96.9 12.0 %collective-permute-start.10 = (bf16[512,1024]{1,0:T(8,128)(2,1)}, bf16[512,1024]{1,0:T(8,128)(2,1)S(1)}, u32[]{:S(2)}, u32[]{:S(2)}) collective-permute-start(bf16[512,1024]{1,0:T(8,128)(2,1)} %copy-done.9), channel_id=1, source_target_pairs={{4,8},{8,4},{5,9},{9,5},{6,10},{10,6},{7,11},{11,7},{20,24},{24,20... | collective-permute-start | bytes 3145736 | tf_op jit(solution)/shard_map/ppermute | solution.py:489
  97.6 25.2 %collective-permute-start.11 = (bf16[512,1024]{1,0:T(8,128)(2,1)S(1)}, bf16[512,1024]{1,0:T(8,128)(2,1)S(1)}, u32[]{:S(2)}, u32[]{:S(2)}) collective-permute-start(bf16[512,1024]{1,0:T(8,128)(2,1)S(1)} %collective-permute-done.7.refs_1_), channel_id=1, source_target_pairs={{4,0},{8,12},{5,1},{9,13},{6,2},{10,14},{7,3},{11,15},{20,16},{24,... | collective-permute-start | bytes 3145736 | tf_op jit(solution)/shard_map/ppermute | solution.py:490
  102.7 2.2 %collective-permute-start.8 = (bf16[256,1024]{1,0:T(8,128)(2,1)}, bf16[256,1024]{1,0:T(8,128)(2,1)S(1)}, u32[]{:S(2)}, u32[]{:S(2)}) collective-permute-start(bf16[256,1024]{1,0:T(8,128)(2,1)} %get-tuple-element.70), channel_id=1, source_target_pairs={{0,1},{1,0},{2,3},{3,2},{4,5},{5,4},{6,7},{7,6},{8,9},{9,8},{10,11... | collective-permute-start | bytes 1572872 | tf_op jit(solution)/shard_map/ppermute | solution.py:495
  102.8 3.0 %collective-permute-start.9 = (bf16[256,1024]{1,0:T(8,128)(2,1)}, bf16[256,1024]{1,0:T(8,128)(2,1)}, u32[]{:S(2)}, u32[]{:S(2)}) collective-permute-start(bf16[256,1024]{1,0:T(8,128)(2,1)} %get-tuple-element.71), channel_id=1, source_target_pairs={{0,1},{1,0},{2,3},{3,2},{4,5},{5,4},{6,7},{7,6},{8,9},{9,8},{10,11... | collective-permute-start | bytes 1572872 | tf_op jit(solution)/shard_map/ppermute | solution.py:495
  104.9 0.9 copy-start.15
  108.8 54.9 %copy-start.2 = (bf16[512,1024]{1,0:T(8,128)(2,1)}, bf16[512,1024]{1,0:T(8,128)(2,1)S(1)}, u32[]{:S(2)}) copy-start(bf16[512,1024]{1,0:T(8,128)(2,1)S(1)} %collective-permute-done.10.refs_1_) | copy-start | bytes 3145732
  122.8 7.8 %copy-start.3 = (bf16[512,1024]{1,0:T(8,128)(2,1)}, bf16[512,1024]{1,0:T(8,128)(2,1)S(1)}, u32[]{:S(2)}) copy-start(bf16[512,1024]{1,0:T(8,128)(2,1)S(1)} %collective-permute-done.11.refs_2_) | copy-start | bytes 3145732
  123.8 70.5 %all-gather.11.cloned.1.call-start = ((), (), s32[]{:S(2)}) async-start(), calls=%async_computation.2 | async-start | bytes 2621440 | tf_op jit(solution)/shard_map/all_gather | solution.py:514
  123.8 6.8 %collective-permute-start.13 = (bf16[2,256,1024]{2,1,0:T(8,128)(2,1)}, bf16[2,256,1024]{2,1,0:T(8,128)(2,1)}, u32[]{:S(2)}, u32[]{:S(2)}) collective-permute-start(bf16[2,256,1024]{2,1,0:T(8,128)(2,1)} %get-tuple-element.79), channel_id=1, source_target_pairs={{0,1},{1,0},{2,3},{3,2},{4,5},{5,4},{6,7},{7,6},{8,9},{9,8},{10,11... | collective-permute-start | bytes 3145736 | tf_op jit(solution)/shard_map/ppermute | solution.py:501
  123.9 19.7 %collective-permute-start.12 = (bf16[256,1024]{1,0:T(8,128)(2,1)}, bf16[256,1024]{1,0:T(8,128)(2,1)}, u32[]{:S(2)}, u32[]{:S(2)}) collective-permute-start(bf16[256,1024]{1,0:T(8,128)(2,1)} %get-tuple-element.77), channel_id=1, source_target_pairs={{0,2},{2,0},{1,3},{3,1},{4,6},{6,4},{5,7},{7,5},{8,10},{10,8},{9,1... | collective-permute-start | bytes 1572872 | tf_op jit(solution)/shard_map/ppermute | solution.py:500
  125.4 31.2 %collective-permute-start.16 = (bf16[512,1024]{1,0:T(8,128)(2,1)S(1)}, bf16[512,1024]{1,0:T(8,128)(2,1)S(1)}, u32[]{:S(2)}, u32[]{:S(2)}) collective-permute-start(bf16[512,1024]{1,0:T(8,128)(2,1)S(1)} %collective-permute-done.10.refs_1_), channel_id=1, source_target_pairs={{4,0},{8,12},{5,1},{9,13},{6,2},{10,14},{7,3},{11,15},{20,16},{24,... | collective-permute-start | bytes 3145736 | tf_op jit(solution)/shard_map/ppermute | solution.py:502
  130.6 13.0 %copy-start.11 = (bf16[256,1024]{1,0:T(8,128)(2,1)S(1)}, bf16[256,1024]{1,0:T(8,128)(2,1)}, u32[]{:S(2)}) copy-start(bf16[256,1024]{1,0:T(8,128)(2,1)} %get-tuple-element.87) | copy-start | bytes 1572868
  145.6 18.1 %collective-permute-start.14 = (bf16[256,1024]{1,0:T(8,128)(2,1)}, bf16[256,1024]{1,0:T(8,128)(2,1)S(1)}, u32[]{:S(2)}, u32[]{:S(2)}) collective-permute-start(bf16[256,1024]{1,0:T(8,128)(2,1)} %add.28), channel_id=1, source_target_pairs={{4,0},{8,12},{5,1},{9,13},{6,2},{10,14},{7,3},{11,15},{20,16},{24,... | collective-permute-start | bytes 1572872 | tf_op jit(solution)/shard_map/ppermute | solution.py:509
  146.9 16.8 %collective-permute-start.15 = (bf16[256,1024]{1,0:T(8,128)(2,1)}, bf16[256,1024]{1,0:T(8,128)(2,1)}, u32[]{:S(2)}, u32[]{:S(2)}) collective-permute-start(bf16[256,1024]{1,0:T(8,128)(2,1)} %get-tuple-element.89), channel_id=1, source_target_pairs={{0,2},{2,0},{1,3},{3,1},{4,6},{6,4},{5,7},{7,5},{8,10},{10,8},{9,1... | collective-permute-start | bytes 1572872 | tf_op jit(solution)/shard_map/ppermute | solution.py:510
  156.6 9.4 %copy-start.12 = (bf16[256,1024]{1,0:T(8,128)(2,1)S(1)}, bf16[256,1024]{1,0:T(8,128)(2,1)}, u32[]{:S(2)}) copy-start(bf16[256,1024]{1,0:T(8,128)(2,1)} %get-tuple-element.86) | copy-start | bytes 1572868
  156.6 10.5 %copy-start.4 = (bf16[512,1024]{1,0:T(8,128)(2,1)}, bf16[512,1024]{1,0:T(8,128)(2,1)S(1)}, u32[]{:S(2)}) copy-start(bf16[512,1024]{1,0:T(8,128)(2,1)S(1)} %collective-permute-done.16.refs_2_) | copy-start | bytes 3145732
  164.6 15.3 %collective-permute-start.19 = (bf16[256,1024]{1,0:T(8,128)(2,1)}, bf16[256,1024]{1,0:T(8,128)(2,1)S(1)}, u32[]{:S(2)}, u32[]{:S(2)}) collective-permute-start(bf16[256,1024]{1,0:T(8,128)(2,1)} %get-tuple-element.97), channel_id=1, source_target_pairs={{4,0},{8,12},{5,1},{9,13},{6,2},{10,14},{7,3},{11,15},{20,16},{24,... | collective-permute-start | bytes 1572872 | tf_op jit(solution)/shard_map/ppermute | solution.py:516
  167.1 21.3 %copy-start.5 = (bf16[256,1024]{1,0:T(8,128)(2,1)}, bf16[256,1024]{1,0:T(8,128)(2,1)S(1)}, u32[]{:S(2)}) copy-start(bf16[256,1024]{1,0:T(8,128)(2,1)S(1)} %add_select_fusion.own) | copy-start | bytes 1572868
  167.1 21.3 %collective-permute-start.17 = (bf16[256,1024]{1,0:T(8,128)(2,1)S(1)}, bf16[256,1024]{1,0:T(8,128)(2,1)S(1)}, u32[]{:S(2)}, u32[]{:S(2)}) collective-permute-start(bf16[256,1024]{1,0:T(8,128)(2,1)S(1)} %add_select_fusion.own), channel_id=1, source_target_pairs={{0,2},{2,0},{1,3},{3,1},{4,6},{6,4},{5,7},{7,5},{8,10},{10,8},{9,1... | collective-permute-start | bytes 1572872 | tf_op jit(solution)/shard_map/ppermute | solution.py:520
  167.8 20.7 %collective-permute-start.18 = (bf16[256,1024]{1,0:T(8,128)(2,1)S(1)}, bf16[256,1024]{1,0:T(8,128)(2,1)S(1)}, u32[]{:S(2)}, u32[]{:S(2)}) collective-permute-start(bf16[256,1024]{1,0:T(8,128)(2,1)S(1)} %add_select_fusion.own), channel_id=1, source_target_pairs={{0,1},{1,0},{2,3},{3,2},{4,5},{5,4},{6,7},{7,6},{8,9},{9,8},{10,11... | collective-permute-start | bytes 1572872 | tf_op jit(solution)/shard_map/ppermute | solution.py:520
  188.4 2.0 copy-start.13
  188.4 2.0 copy-start.14
  188.4 2.0 collective-permute-start.20
  190.4 0.8 copy-start.16
Sparse Core Ops, SparseCore 0:
  71.6 21.0 all-gather.6
  123.9 27.4 all-gather.8
  164.7 28.2 all-gather.10

commit v25 on v16

--- a/solution.py
+++ b/solution.py
@@ -381,7 +381,7 @@
     cols_n = pairs[0][1].shape[1] // size
     rows_n = first.shape[-1] // size * (first.shape[0] if len(first.shape) == 3 else 1)
     total = rows_n * cols_n
-    group = math.gcd(slots, 8)
+    group = math.gcd(slots, 32)
 
     @pl.loop(0, slots // group)
     def some(g):

time: 207 us -> 206 us (level)
  Pallas kernels: 57.5 us -> 53.8 us
  waiting for transfers between devices: 84 us -> 86.9 us
    pallas_call x4, Pallas kernels: 31.7 us -> 27.9 us  [line_grads(): pl.pallas_call(functools.partial(line_grads_kernel, len(pairs)), out_shap...]
  transfers between devices with their start and end apart: 24 -> 24, of which waited for: 11 -> 11; matrix products, arithmetic and copies ran while one was open for 5% -> 5% of each run, Pallas kernels for 24% -> 23%
where the time goes in v25:
time: 206 us
  waiting for transfers between devices  86.9 us (42%)
  Pallas kernels  53.8 us (26%)
  starting transfers between devices  31.9 us (15%)
  between operations  14 us (7%)
  other arithmetic  10.9 us (5%)
  local copies, waits for them, and re-layouts  8.18 us (4%)
    pallas_call x4, Pallas kernels, line_grads(): pl.pallas_call(functools.partial(line_grads_kernel, len(pairs)), out_shap...  27.9 us
    ppermute x1, waiting for transfers between devices, line_body(): both_1 = along(both, perm=PAIRS)  21.7 us
    ppermute x1, waiting for transfers between devices, line_body(): both_2o = along(both_2m, perm=OUTWARD)  13.9 us
    ppermute x1, waiting for transfers between devices, line_body(): near_a = along(mine, perm=INWARD)  12.6 us
    ppermute x1, waiting for transfers between devices, line_body(): sideways(quarter)  10.5 us
    ppermute x1, waiting for transfers between devices, line_body(): end_got = sideways(end_give)  9.44 us
    pallas_call x1, Pallas kernels, place_first(): pl.pallas_call(place_kernel, out_shape=(jax.ShapeDtypeStruct((depth, widt...  8.74 us
    ppermute x1, waiting for transfers between devices, line_body(): sum_out = along(end_keep + end_got, perm=OUTWARD)  7.58 us
  transfers between devices with their start and end apart: 24, of which 11 were waited for; matrix products, arithmetic and copies ran while one was open for 5% of the time, Pallas kernels for 23%

profile of v25, /device:TPU:0, one launch (start us, length us, event | category | flops | bytes accessed | tf_op | source)
XLA Modules:
  0.0 205.7 jit_solution(12932497815211166986)
XLA Ops:
  7.2 0.0 all-gather.7.cloned.1.call-start
  7.2 0.7 convert_element_type.26
  7.9 0.1 convert_element_type.27
  8.0 1.3 constant_dynamic-slice_fusion.2
  9.3 1.1 pad_maximum_fusion
  10.4 5.0 %collective-permute-start = (bf16[33,128,128]{2,1,0:T(8,128)(2,1)}, bf16[33,128,128]{2,1,0:T(8,128)(2,1)S(1)}, u32[]{:S(2)}, u32[]{:S(2)}) collective-permute-start(bf16[33,128,128]{2,1,0:T(8,128)(2,1)} %pad_maximum_fusion), channel_id=1, source_target_pairs={{0,4},{12,8},{1,5},{13,9},{2,6},{14,10},{3,7},{15,11},{16,20},{28,... | collective-permute-start | bytes 3244040 | tf_op jit(solution)/shard_map/ppermute | solution.py:463
  15.4 1.7 collective-permute-start.1
  17.0 6.1 %line_grads.4.refs_2_ = bf16[64,128,128]{2,1,0:T(8,128)(2,1)} custom-call(s32[64]{0:T(128)} %ids.7, bf16[256,4096]{1,0:T(8,128)(2,1)} %tokens.1, bf16[256,1024]{1,0:T(8,128)(2,1)} %upstream.1), custom_call_target="tpu_custom_call" | custom-call | flops 536870912 | bytes 4718592 | tf_op jit(solution)/shard_map/line_grads/pallas_call | solution.py:411
  23.2 1.2 constant_dynamic-slice_fusion.1
  24.4 0.1 pad_maximum_fusion.1
  24.5 0.4 copy-done
  24.9 1.2 constant_dynamic-slice_fusion
  26.1 12.6 %collective-permute-done.near_a = bf16[33,128,128]{2,1,0:T(8,128)(2,1)S(1)} collective-permute-done((bf16[33,128,128]{2,1,0:T(8,128)(2,1)}, bf16[33,128,128]{2,1,0:T(8,128)(2,1)S(1)}, u32[]{:S(2)}, u32[]{:S(2)}) %collective-permute-start) | collective-permute-done | bytes 1081376 | tf_op jit(solution)/shard_map/ppermute | solution.py:463
  38.7 1.7 collective-permute-start.3
  40.4 1.5 collective-permute-start.4
  41.9 5.6 %collective-permute-start.2 = (bf16[512,1024]{1,0:T(8,128)(2,1)S(1)}, bf16[512,1024]{1,0:T(8,128)(2,1)S(1)}, u32[]{:S(2)}, u32[]{:S(2)}) collective-permute-start(bf16[512,1024]{1,0:T(8,128)(2,1)S(1)} %pad_maximum_fusion.1), channel_id=1, source_target_pairs={{0,4},{12,8},{4,0},{8,12},{1,5},{13,9},{5,1},{9,13},{2,6},{14,10},... | collective-permute-start | bytes 3145736 | tf_op jit(solution)/shard_map/ppermute | solution.py:473
  47.6 21.7 %collective-permute-done.2 = bf16[512,1024]{1,0:T(8,128)(2,1)S(1)} collective-permute-done((bf16[512,1024]{1,0:T(8,128)(2,1)S(1)}, bf16[512,1024]{1,0:T(8,128)(2,1)S(1)}, u32[]{:S(2)}, u32[]{:S(2)}) %collective-permute-start.2) | collective-permute-done | bytes 1048608 | tf_op jit(solution)/shard_map/ppermute | solution.py:473
  69.3 1.1 copy-done.9
  70.4 1.0 fusion
  71.4 0.0 all-gather.9.cloned.1.call-start
  71.5 0.6 collective-permute-start.6
  72.0 3.7 %collective-permute-start.5 = (bf16[32,128,128]{2,1,0:T(8,128)(2,1)}, bf16[32,128,128]{2,1,0:T(8,128)(2,1)S(1)}, u32[]{:S(2)}, u32[]{:S(2)}) collective-permute-start(bf16[32,128,128]{2,1,0:T(8,128)(2,1)} %constant_dynamic-slice_fusion), channel_id=1, source_target_pairs={{0,4},{12,8},{1,5},{13,9},{2,6},{14,10},{3,7},{15,11},{16,20},{28,... | collective-permute-start | bytes 3145736 | tf_op jit(solution)/shard_map/ppermute | solution.py:477
  75.8 0.7 collective-permute-start.7
  76.5 0.7 pad_add_fusion.place_of
  77.2 1.2 bitcast_convert_fusion
  78.4 1.3 bitcast_convert_fusion.1.ids_3
  79.6 8.7 %place_first.1 = (bf16[4096,1024]{1,0:T(8,128)(2,1)}, bf16[1024,4096]{1,0:T(8,128)(2,1)}) custom-call(s32[4]{0:T(128)} %pad_add_fusion.place_of, s32[64]{0:T(128)} %ids.7, s32[64]{0:T(128)} %get-tuple-element.104.ids_1, s32[64]{0:T(128)} %get-tuple-element.103.ids_2, s32[64]{0:T(128)} %bitcast_convert_fusion.1.ids_3, bf16[64,128,128]{2,1,0:T(8,128)(2,1)} %own.1, ...), custom_call_target="tpu_custom_call" | custom-call | bytes 25165824 | tf_op jit(solution)/shard_map/place_first/pallas_call | solution.py:181
  88.4 7.5 %collective-permute-done.5.near_b = bf16[32,128,128]{2,1,0:T(8,128)(2,1)S(1)} collective-permute-done((bf16[32,128,128]{2,1,0:T(8,128)(2,1)}, bf16[32,128,128]{2,1,0:T(8,128)(2,1)S(1)}, u32[]{:S(2)}, u32[]{:S(2)}) %collective-permute-start.5) | collective-permute-done | bytes 1048608 | tf_op jit(solution)/shard_map/ppermute | solution.py:477
  95.9 0.9 copy-done.8
  96.9 0.7 collective-permute-start.10
  97.6 1.3 collective-permute-start.11
  98.9 3.9 %project_back.1 = (bf16[2,256,1024]{2,1,0:T(8,128)(2,1)}, bf16[2,256,1024]{2,1,0:T(8,128)(2,1)}, bf16[2,256,1024]{2,1,0:T(8,128)(2,1)}, bf16[256,1024]{1,0:T(8,128)(2,1)}, bf16[256,1024]{1,0:T(8,128)(2,1)}) custom-call(s32[4]{0:T(128)} %pad_add_fusion.place_of, s32[64]{0:T(128)} %get-tuple-element.104.ids_1, s32[64]{0:T(128)} %bitcast_convert_fusion.1.ids_3, ...), custom_call_target="tpu_custom_call" | custom-call | flops 4294967296 | bytes 13631488 | tf_op jit(solution)/shard_map/project_back/pallas_call | solution.py:239
  102.7 0.1 collective-permute-start.8
  102.8 0.5 collective-permute-start.9
  103.3 1.6 collective-permute-done.8.refs_0_
  104.9 0.9 collective-permute-done.9.refs_1_
  105.8 3.0 %add_split.2 = (bf16[256,1024]{1,0:T(8,128)(2,1)}, bf16[256,1024]{1,0:T(8,128)(2,1)}) custom-call(s32[4]{0:T(128)} %pad_add_fusion.place_of, bf16[2,256,1024]{2,1,0:T(8,128)(2,1)} %get-tuple-element.68.keep, bf16[256,1024]{1,0:T(8,128)(2,1)} %copy-done.15, bf16[256,1024]{1,0:T(8,128)(2,1)} %collective-permute-done.9.refs_1_), custom_call_target="tpu_custom_call" | custom-call | flops 524288 | bytes 3145728 | tf_op jit(solution)/shard_map/add_split/pallas_call | solution.py:328
  108.8 13.9 %collective-permute-done.11.refs_2_ = bf16[512,1024]{1,0:T(8,128)(2,1)S(1)} collective-permute-done((bf16[512,1024]{1,0:T(8,128)(2,1)S(1)}, bf16[512,1024]{1,0:T(8,128)(2,1)S(1)}, u32[]{:S(2)}, u32[]{:S(2)}) %collective-permute-start.11) | collective-permute-done | bytes 1048608 | tf_op jit(solution)/shard_map/ppermute | solution.py:490
  122.7 0.9 slice_add_fusion.1
  123.7 0.0 all-gather.11.cloned.1.call-start
  123.8 0.1 collective-permute-start.13
  123.8 1.6 collective-permute-start.12
  125.4 1.3 collective-permute-start.17
  126.7 3.9 %project_forward.1 = (bf16[256,1024]{1,0:T(8,128)(2,1)}, bf16[256,1024]{1,0:T(8,128)(2,1)}) custom-call(s32[4]{0:T(128)} %pad_add_fusion.place_of, s32[64]{0:T(128)} %get-tuple-element.104.ids_1, s32[64]{0:T(128)} %bitcast_convert_fusion.1.ids_3, bf16[4096,1024]{1,0:T(8,128)(2,1)} %get-tuple-element.81.partial, bf16[32,128,128]{2,1,0:T(8,128)(2,1)} %copy-done.8, ...), custom_call_target="tpu_custom_call" | custom-call | flops 536870912 | bytes 4194304 | tf_op jit(solution)/shard_map/project_forward/pallas_call | solution.py:296
  130.6 3.4 %add_split.3 = (bf16[256,1024]{1,0:T(8,128)(2,1)}, bf16[256,1024]{1,0:T(8,128)(2,1)}) custom-call(s32[4]{0:T(128)} %pad_add_fusion.place_of, bf16[2,256,1024]{2,1,0:T(8,128)(2,1)} %get-tuple-element.77.keep, bf16[2,256,1024]{2,1,0:T(8,128)(2,1)} %collective-permute-done.13.refs_0_), custom_call_target="tpu_custom_call" | custom-call | flops 524288 | bytes 3145728 | tf_op jit(solution)/shard_map/add_split/pallas_call | solution.py:328
  134.0 9.4 %collective-permute-done.12 = bf16[256,1024]{1,0:T(8,128)(2,1)} collective-permute-done((bf16[256,1024]{1,0:T(8,128)(2,1)}, bf16[256,1024]{1,0:T(8,128)(2,1)}, u32[]{:S(2)}, u32[]{:S(2)}) %collective-permute-start.12) | collective-permute-done | bytes 524320 | tf_op jit(solution)/shard_map/ppermute | solution.py:500
  143.4 2.0 add.28
  145.5 1.3 collective-permute-start.15
  146.7 2.5 %collective-permute-start.16 = (bf16[256,1024]{1,0:T(8,128)(2,1)}, bf16[256,1024]{1,0:T(8,128)(2,1)}, u32[]{:S(2)}, u32[]{:S(2)}) collective-permute-start(bf16[256,1024]{1,0:T(8,128)(2,1)} %get-tuple-element.90), channel_id=1, source_target_pairs={{0,2},{2,0},{1,3},{3,1},{4,6},{6,4},{5,7},{7,5},{8,10},{10,8},{9,1... | collective-permute-start | bytes 1572872 | tf_op jit(solution)/shard_map/ppermute | solution.py:510
  149.3 6.9 %line_grads.5.refs_3_ = bf16[64,128,128]{2,1,0:T(8,128)(2,1)} custom-call(s32[64]{0:T(128)} %ids.7, bf16[4,256,1024]{2,1,0:T(8,128)(2,1)} %bitcast.17, bf16[256,1024]{1,0:T(8,128)(2,1)} %get-tuple-element.101.end_upstream.refs_1_, bf16[64,128,128]{2,1,0:T(8,128)(2,1)} %line_grads.4.refs_2_), custom_call_target="tpu_custom_call" | custom-call | flops 536870912 | bytes 6815744 | tf_op jit(solution)/shard_map/line_grads/pallas_call | solution.py:411
  156.2 7.6 %collective-permute-done.15 = bf16[256,1024]{1,0:T(8,128)(2,1)S(1)} collective-permute-done((bf16[256,1024]{1,0:T(8,128)(2,1)}, bf16[256,1024]{1,0:T(8,128)(2,1)S(1)}, u32[]{:S(2)}, u32[]{:S(2)}) %collective-permute-start.15) | collective-permute-done | bytes 524320 | tf_op jit(solution)/shard_map/ppermute | solution.py:509
  163.7 0.9 slice_add_fusion
  164.6 1.1 add_select_fusion.own
  165.8 0.6 collective-permute-start.18
  166.4 1.3 collective-permute-start.14
  167.7 7.6 %line_grads.6.refs_3_ = bf16[64,128,128]{2,1,0:T(8,128)(2,1)} custom-call(s32[64]{0:T(128)} %ids.7, bf16[4,256,1024]{2,1,0:T(8,128)(2,1)} %bitcast.18, bf16[512,1024]{1,0:T(8,128)(2,1)} %copy-done.1, bf16[512,1024]{1,0:T(8,128)(2,1)} %copy-done.3, bf16[64,128,128]{2,1,0:T(8,128)(2,1)} %line_grads.5.refs_3_), custom_call_target="tpu_custom_call" | custom-call | flops 536870912 | bytes 8388608 | tf_op jit(solution)/shard_map/line_grads/pallas_call | solution.py:411
  175.3 10.5 %collective-permute-done.18.by_tensor = bf16[256,1024]{1,0:T(8,128)(2,1)S(1)} collective-permute-done((bf16[256,1024]{1,0:T(8,128)(2,1)S(1)}, bf16[256,1024]{1,0:T(8,128)(2,1)S(1)}, u32[]{:S(2)}, u32[]{:S(2)}) %collective-permute-start.18) | collective-permute-done | bytes 524320 | tf_op jit(solution)/shard_map/ppermute | solution.py:518
  185.8 0.1 collective-permute-start.20
  185.9 1.0 broadcast_select_fusion
  186.9 0.9 collective-permute-done.20.by_both
  187.8 0.9 copy-done.16
  188.6 3.0 %assemble.1 = bf16[256,4096]{1,0:T(8,128)(2,1)} custom-call(s32[4]{0:T(128)} %pad_add_fusion.place_of, bf16[256,1024]{1,0:T(8,128)(2,1)} %copy-done.5, bf16[256,1024]{1,0:T(8,128)(2,1)} %copy-done.14, bf16[256,1024]{1,0:T(8,128)(2,1)} %copy-done.13, bf16[256,1024]{1,0:T(8,128)(2,1)} %copy-done.16), custom_call_target="tpu_custom_call" | custom-call | bytes 4194304 | tf_op jit(solution)/shard_map/assemble/pallas_call | solution.py:353
  191.6 0.1 all-gather.11.cloned.1.call-done
  191.8 7.4 %line_grads.7 = bf16[64,128,128]{2,1,0:T(8,128)(2,1)} custom-call(s32[64]{0:T(128)} %ids.7, bf16[4,256,1024]{2,1,0:T(8,128)(2,1)} %bitcast.19, bf16[512,1024]{1,0:T(8,128)(2,1)} %copy-done.2, bf16[512,1024]{1,0:T(8,128)(2,1)} %copy-done.4, bf16[64,128,128]{2,1,0:T(8,128)(2,1)} %line_grads.6.refs_3_), custom_call_target="tpu_custom_call" | custom-call | flops 536870912 | bytes 8388608 | tf_op jit(solution)/shard_map/line_grads/pallas_call | solution.py:411
  (51 shorter events, 0.2 us)
Async XLA Ops:
  7.2 88.8 %all-gather.7.cloned.1.call-start = ((), (), s32[]{:S(2)}) async-start(), calls=%async_computation | async-start | bytes 2621440 | tf_op jit(solution)/shard_map/all_gather | solution.py:480
  10.4 28.3 %collective-permute-start = (bf16[33,128,128]{2,1,0:T(8,128)(2,1)}, bf16[33,128,128]{2,1,0:T(8,128)(2,1)S(1)}, u32[]{:S(2)}, u32[]{:S(2)}) collective-permute-start(bf16[33,128,128]{2,1,0:T(8,128)(2,1)} %pad_maximum_fusion), channel_id=1, source_target_pairs={{0,4},{12,8},{1,5},{13,9},{2,6},{14,10},{3,7},{15,11},{16,20},{28,... | collective-permute-start | bytes 3244040 | tf_op jit(solution)/shard_map/ppermute | solution.py:463
  15.4 23.4 %collective-permute-start.1 = (bf16[33,128,128]{2,1,0:T(8,128)(2,1)}, bf16[33,128,128]{2,1,0:T(8,128)(2,1)}, u32[]{:S(2)}, u32[]{:S(2)}) collective-permute-start(bf16[33,128,128]{2,1,0:T(8,128)(2,1)} %pad_maximum_fusion), channel_id=1, source_target_pairs={{4,8},{8,4},{5,9},{9,5},{6,10},{10,6},{7,11},{11,7},{20,24},{24,20... | collective-permute-start | bytes 3244040 | tf_op jit(solution)/shard_map/ppermute | solution.py:464
  17.0 7.3 %copy-start.6 = (bf16[256,1024]{1,0:T(8,128)(2,1)S(1)}, bf16[256,1024]{1,0:T(8,128)(2,1)}, u32[]{:S(2)}) copy-start(bf16[256,1024]{1,0:T(8,128)(2,1)} %upstream.1) | copy-start | bytes 1572868
  23.2 1.8 copy-start
  24.9 46.5 %copy-start.10 = (bf16[512,1024]{1,0:T(8,128)(2,1)}, bf16[512,1024]{1,0:T(8,128)(2,1)S(1)}, u32[]{:S(2)}) copy-start(bf16[512,1024]{1,0:T(8,128)(2,1)S(1)} %pad_maximum_fusion.1) | copy-start | bytes 3145732
  38.7 40.9 %copy-start.7 = (bf16[33,128,128]{2,1,0:T(8,128)(2,1)}, bf16[33,128,128]{2,1,0:T(8,128)(2,1)S(1)}, u32[]{:S(2)}) copy-start(bf16[33,128,128]{2,1,0:T(8,128)(2,1)S(1)} %collective-permute-done.near_a) | copy-start | bytes 3244036
  38.7 30.6 %collective-permute-start.3 = (bf16[33,128,128]{2,1,0:T(8,128)(2,1)S(1)}, bf16[33,128,128]{2,1,0:T(8,128)(2,1)}, u32[]{:S(2)}, u32[]{:S(2)}) collective-permute-start(bf16[33,128,128]{2,1,0:T(8,128)(2,1)S(1)} %collective-permute-done.near_a), channel_id=1, source_target_pairs={{4,8},{8,4},{5,9},{9,5},{6,10},{10,6},{7,11},{11,7},{20,24},{24,20... | collective-permute-start | bytes 3244040 | tf_op jit(solution)/shard_map/ppermute | solution.py:471
  40.4 28.9 %collective-permute-start.4 = (bf16[33,128,128]{2,1,0:T(8,128)(2,1)}, bf16[33,128,128]{2,1,0:T(8,128)(2,1)}, u32[]{:S(2)}, u32[]{:S(2)}) collective-permute-start(bf16[33,128,128]{2,1,0:T(8,128)(2,1)} %collective-permute-done.1.far_a), channel_id=1, source_target_pairs={{0,16},{16,0},{1,17},{17,1},{2,18},{18,2},{3,19},{19,3},{4,20},{20... | collective-permute-start | bytes 3244040 | tf_op jit(solution)/shard_map/ppermute | solution.py:472
  41.9 27.4 %collective-permute-start.2 = (bf16[512,1024]{1,0:T(8,128)(2,1)S(1)}, bf16[512,1024]{1,0:T(8,128)(2,1)S(1)}, u32[]{:S(2)}, u32[]{:S(2)}) collective-permute-start(bf16[512,1024]{1,0:T(8,128)(2,1)S(1)} %pad_maximum_fusion.1), channel_id=1, source_target_pairs={{0,4},{12,8},{4,0},{8,12},{1,5},{13,9},{5,1},{9,13},{2,6},{14,10},... | collective-permute-start | bytes 3145736 | tf_op jit(solution)/shard_map/ppermute | solution.py:473
  69.3 1.1 copy-start.9
  71.4 96.3 %all-gather.9.cloned.1.call-start = ((), (), s32[]{:S(2)}) async-start(), calls=%async_computation.1 | async-start | bytes 2621440 | tf_op jit(solution)/shard_map/all_gather | solution.py:503
  71.5 24.4 %collective-permute-start.6 = (bf16[33,128,128]{2,1,0:T(8,128)(2,1)}, bf16[33,128,128]{2,1,0:T(8,128)(2,1)}, u32[]{:S(2)}, u32[]{:S(2)}) collective-permute-start(bf16[33,128,128]{2,1,0:T(8,128)(2,1)} %collective-permute-done.3.end_a), channel_id=1, source_target_pairs={{0,16},{16,0},{1,17},{17,1},{2,18},{18,2},{3,19},{19,3},{4,20},{20... | collective-permute-start | bytes 3244040 | tf_op jit(solution)/shard_map/ppermute | solution.py:478
  72.0 23.8 %collective-permute-start.5 = (bf16[32,128,128]{2,1,0:T(8,128)(2,1)}, bf16[32,128,128]{2,1,0:T(8,128)(2,1)S(1)}, u32[]{:S(2)}, u32[]{:S(2)}) collective-permute-start(bf16[32,128,128]{2,1,0:T(8,128)(2,1)} %constant_dynamic-slice_fusion), channel_id=1, source_target_pairs={{0,4},{12,8},{1,5},{13,9},{2,6},{14,10},{3,7},{15,11},{16,20},{28,... | collective-permute-start | bytes 3145736 | tf_op jit(solution)/shard_map/ppermute | solution.py:477
  75.8 20.1 %collective-permute-start.7 = (bf16[512,1024]{1,0:T(8,128)(2,1)}, bf16[512,1024]{1,0:T(8,128)(2,1)S(1)}, u32[]{:S(2)}, u32[]{:S(2)}) collective-permute-start(bf16[512,1024]{1,0:T(8,128)(2,1)} %copy-done.10), channel_id=1, source_target_pairs={{4,8},{8,4},{5,9},{9,5},{6,10},{10,6},{7,11},{11,7},{20,24},{24,20... | collective-permute-start | bytes 3145736 | tf_op jit(solution)/shard_map/ppermute | solution.py:479
  95.9 1.0 copy-start.8
  95.9 26.9 %copy-start.1 = (bf16[512,1024]{1,0:T(8,128)(2,1)}, bf16[512,1024]{1,0:T(8,128)(2,1)S(1)}, u32[]{:S(2)}) copy-start(bf16[512,1024]{1,0:T(8,128)(2,1)S(1)} %collective-permute-done.7.refs_1_) | copy-start | bytes 3145732
  96.9 12.0 %collective-permute-start.10 = (bf16[512,1024]{1,0:T(8,128)(2,1)}, bf16[512,1024]{1,0:T(8,128)(2,1)S(1)}, u32[]{:S(2)}, u32[]{:S(2)}) collective-permute-start(bf16[512,1024]{1,0:T(8,128)(2,1)} %copy-done.9), channel_id=1, source_target_pairs={{4,8},{8,4},{5,9},{9,5},{6,10},{10,6},{7,11},{11,7},{20,24},{24,20... | collective-permute-start | bytes 3145736 | tf_op jit(solution)/shard_map/ppermute | solution.py:489
  97.6 25.2 %collective-permute-start.11 = (bf16[512,1024]{1,0:T(8,128)(2,1)S(1)}, bf16[512,1024]{1,0:T(8,128)(2,1)S(1)}, u32[]{:S(2)}, u32[]{:S(2)}) collective-permute-start(bf16[512,1024]{1,0:T(8,128)(2,1)S(1)} %collective-permute-done.7.refs_1_), channel_id=1, source_target_pairs={{4,0},{8,12},{5,1},{9,13},{6,2},{10,14},{7,3},{11,15},{20,16},{24,... | collective-permute-start | bytes 3145736 | tf_op jit(solution)/shard_map/ppermute | solution.py:490
  102.7 2.2 %collective-permute-start.8 = (bf16[256,1024]{1,0:T(8,128)(2,1)}, bf16[256,1024]{1,0:T(8,128)(2,1)S(1)}, u32[]{:S(2)}, u32[]{:S(2)}) collective-permute-start(bf16[256,1024]{1,0:T(8,128)(2,1)} %get-tuple-element.69), channel_id=1, source_target_pairs={{0,1},{1,0},{2,3},{3,2},{4,5},{5,4},{6,7},{7,6},{8,9},{9,8},{10,11... | collective-permute-start | bytes 1572872 | tf_op jit(solution)/shard_map/ppermute | solution.py:495
  102.8 3.0 %collective-permute-start.9 = (bf16[256,1024]{1,0:T(8,128)(2,1)}, bf16[256,1024]{1,0:T(8,128)(2,1)}, u32[]{:S(2)}, u32[]{:S(2)}) collective-permute-start(bf16[256,1024]{1,0:T(8,128)(2,1)} %get-tuple-element.70), channel_id=1, source_target_pairs={{0,1},{1,0},{2,3},{3,2},{4,5},{5,4},{6,7},{7,6},{8,9},{9,8},{10,11... | collective-permute-start | bytes 1572872 | tf_op jit(solution)/shard_map/ppermute | solution.py:495
  104.9 0.9 copy-start.15
  108.8 54.9 %copy-start.2 = (bf16[512,1024]{1,0:T(8,128)(2,1)}, bf16[512,1024]{1,0:T(8,128)(2,1)S(1)}, u32[]{:S(2)}) copy-start(bf16[512,1024]{1,0:T(8,128)(2,1)S(1)} %collective-permute-done.10.refs_1_) | copy-start | bytes 3145732
  122.7 7.8 %copy-start.3 = (bf16[512,1024]{1,0:T(8,128)(2,1)}, bf16[512,1024]{1,0:T(8,128)(2,1)S(1)}, u32[]{:S(2)}) copy-start(bf16[512,1024]{1,0:T(8,128)(2,1)S(1)} %collective-permute-done.11.refs_2_) | copy-start | bytes 3145732
  123.7 68.1 %all-gather.11.cloned.1.call-start = ((), (), s32[]{:S(2)}) async-start(), calls=%async_computation.2 | async-start | bytes 2621440 | tf_op jit(solution)/shard_map/all_gather | solution.py:514
  123.8 6.8 %collective-permute-start.13 = (bf16[2,256,1024]{2,1,0:T(8,128)(2,1)}, bf16[2,256,1024]{2,1,0:T(8,128)(2,1)}, u32[]{:S(2)}, u32[]{:S(2)}) collective-permute-start(bf16[2,256,1024]{2,1,0:T(8,128)(2,1)} %get-tuple-element.78), channel_id=1, source_target_pairs={{0,1},{1,0},{2,3},{3,2},{4,5},{5,4},{6,7},{7,6},{8,9},{9,8},{10,11... | collective-permute-start | bytes 3145736 | tf_op jit(solution)/shard_map/ppermute | solution.py:501
  123.8 19.6 %collective-permute-start.12 = (bf16[256,1024]{1,0:T(8,128)(2,1)}, bf16[256,1024]{1,0:T(8,128)(2,1)}, u32[]{:S(2)}, u32[]{:S(2)}) collective-permute-start(bf16[256,1024]{1,0:T(8,128)(2,1)} %get-tuple-element.76), channel_id=1, source_target_pairs={{0,2},{2,0},{1,3},{3,1},{4,6},{6,4},{5,7},{7,5},{8,10},{10,8},{9,1... | collective-permute-start | bytes 1572872 | tf_op jit(solution)/shard_map/ppermute | solution.py:500
  125.4 30.8 %collective-permute-start.17 = (bf16[512,1024]{1,0:T(8,128)(2,1)S(1)}, bf16[512,1024]{1,0:T(8,128)(2,1)S(1)}, u32[]{:S(2)}, u32[]{:S(2)}) collective-permute-start(bf16[512,1024]{1,0:T(8,128)(2,1)S(1)} %collective-permute-done.10.refs_1_), channel_id=1, source_target_pairs={{4,0},{8,12},{5,1},{9,13},{6,2},{10,14},{7,3},{11,15},{20,16},{24,... | collective-permute-start | bytes 3145736 | tf_op jit(solution)/shard_map/ppermute | solution.py:502
  130.6 12.8 %copy-start.11 = (bf16[256,1024]{1,0:T(8,128)(2,1)S(1)}, bf16[256,1024]{1,0:T(8,128)(2,1)}, u32[]{:S(2)}) copy-start(bf16[256,1024]{1,0:T(8,128)(2,1)} %get-tuple-element.88) | copy-start | bytes 1572868
  145.5 18.3 %collective-permute-start.15 = (bf16[256,1024]{1,0:T(8,128)(2,1)}, bf16[256,1024]{1,0:T(8,128)(2,1)S(1)}, u32[]{:S(2)}, u32[]{:S(2)}) collective-permute-start(bf16[256,1024]{1,0:T(8,128)(2,1)} %add.28), channel_id=1, source_target_pairs={{4,0},{8,12},{5,1},{9,13},{6,2},{10,14},{7,3},{11,15},{20,16},{24,... | collective-permute-start | bytes 1572872 | tf_op jit(solution)/shard_map/ppermute | solution.py:509
  146.7 17.0 %collective-permute-start.16 = (bf16[256,1024]{1,0:T(8,128)(2,1)}, bf16[256,1024]{1,0:T(8,128)(2,1)}, u32[]{:S(2)}, u32[]{:S(2)}) collective-permute-start(bf16[256,1024]{1,0:T(8,128)(2,1)} %get-tuple-element.90), channel_id=1, source_target_pairs={{0,2},{2,0},{1,3},{3,1},{4,6},{6,4},{5,7},{7,5},{8,10},{10,8},{9,1... | collective-permute-start | bytes 1572872 | tf_op jit(solution)/shard_map/ppermute | solution.py:510
  156.1 8.5 %copy-start.12 = (bf16[256,1024]{1,0:T(8,128)(2,1)S(1)}, bf16[256,1024]{1,0:T(8,128)(2,1)}, u32[]{:S(2)}) copy-start(bf16[256,1024]{1,0:T(8,128)(2,1)} %get-tuple-element.87) | copy-start | bytes 1572868
  156.1 9.6 %copy-start.4 = (bf16[512,1024]{1,0:T(8,128)(2,1)}, bf16[512,1024]{1,0:T(8,128)(2,1)S(1)}, u32[]{:S(2)}) copy-start(bf16[512,1024]{1,0:T(8,128)(2,1)S(1)} %collective-permute-done.17.refs_2_) | copy-start | bytes 3145732
  165.8 9.5 %copy-start.5 = (bf16[256,1024]{1,0:T(8,128)(2,1)}, bf16[256,1024]{1,0:T(8,128)(2,1)S(1)}, u32[]{:S(2)}) copy-start(bf16[256,1024]{1,0:T(8,128)(2,1)S(1)} %add_select_fusion.own) | copy-start | bytes 1572868
  165.8 20.0 %collective-permute-start.18 = (bf16[256,1024]{1,0:T(8,128)(2,1)S(1)}, bf16[256,1024]{1,0:T(8,128)(2,1)S(1)}, u32[]{:S(2)}, u32[]{:S(2)}) collective-permute-start(bf16[256,1024]{1,0:T(8,128)(2,1)S(1)} %add_select_fusion.own), channel_id=1, source_target_pairs={{0,2},{2,0},{1,3},{3,1},{4,6},{6,4},{5,7},{7,5},{8,10},{10,8},{9,1... | collective-permute-start | bytes 1572872 | tf_op jit(solution)/shard_map/ppermute | solution.py:518
  166.4 19.4 %collective-permute-start.19 = (bf16[256,1024]{1,0:T(8,128)(2,1)S(1)}, bf16[256,1024]{1,0:T(8,128)(2,1)S(1)}, u32[]{:S(2)}, u32[]{:S(2)}) collective-permute-start(bf16[256,1024]{1,0:T(8,128)(2,1)S(1)} %add_select_fusion.own), channel_id=1, source_target_pairs={{0,1},{1,0},{2,3},{3,2},{4,5},{5,4},{6,7},{7,6},{8,9},{9,8},{10,11... | collective-permute-start | bytes 1572872 | tf_op jit(solution)/shard_map/ppermute | solution.py:518
  166.4 19.5 %collective-permute-start.14 = (bf16[256,1024]{1,0:T(8,128)(2,1)}, bf16[256,1024]{1,0:T(8,128)(2,1)S(1)}, u32[]{:S(2)}, u32[]{:S(2)}) collective-permute-start(bf16[256,1024]{1,0:T(8,128)(2,1)} %get-tuple-element.86), channel_id=1, source_target_pairs={{4,0},{8,12},{5,1},{9,13},{6,2},{10,14},{7,3},{11,15},{20,16},{24,... | collective-permute-start | bytes 1572872 | tf_op jit(solution)/shard_map/ppermute | solution.py:516
  167.7 18.2 %copy-start.17 = (bf16[256,1024]{1,0:T(8,128)(2,1)S(1)}, bf16[256,1024]{1,0:T(8,128)(2,1)}, u32[]{:S(2)}) copy-start(bf16[256,1024]{1,0:T(8,128)(2,1)} %get-tuple-element.85) | copy-start | bytes 1572868
  185.8 2.0 copy-start.13
  185.8 2.0 copy-start.14
  185.8 2.0 collective-permute-start.20
  187.8 0.9 copy-start.16
Sparse Core Ops, SparseCore 0:
  71.5 21.0 all-gather.6
  123.8 27.5 all-gather.8
  164.7 26.9 all-gather.10

commit v26 on v20

--- a/solution.py
+++ b/solution.py
@@ -381,7 +381,7 @@
     cols_n = pairs[0][1].shape[1] // size
     rows_n = first.shape[-1] // size * (first.shape[0] if len(first.shape) == 3 else 1)
     total = rows_n * cols_n
-    group = math.gcd(slots, 8)
+    group = math.gcd(slots, 32)
 
     @pl.loop(0, slots // group)
     def some(g):
@@ -510,11 +510,11 @@
     own_got = sideways(own_give)
     grads = line_grads(block_ids, ((tokens_1, upstream_1),), grads, size)
     tokens_3 = lax.all_gather(both_3m[:rows] + both_3o[:rows], INNER)
+    grads = line_grads(block_ids, ((tokens_2, both_2m, both_2o),), grads, size)
     sum_out, own_got, grads = stage((sum_out, own_got, grads))
 
     quarter = jnp.where(middle, own_keep + own_got, sum_out)
     proj_out = along(end_proj, perm=OUTWARD)
-    grads = line_grads(block_ids, ((tokens_2, both_2m, both_2o),), grads, size)
     grads = line_grads(block_ids, ((tokens_3, both_3m, both_3o),), grads, size)
     by_tensor, by_core, grads = stage((sideways(quarter), cores(quarter), grads))
     by_both = cores(by_tensor)

time: 210 us -> 207 us (0.986)
  Pallas kernels: 57.3 us -> 53.8 us
  waiting for transfers between devices: 85.9 us -> 88.1 us
    all_gather x1, waiting for transfers between devices: 0.01 us -> 8.43 us  [line_body(): tokens_3 = lax.all_gather(both_3m[:rows] + both_3o[:rows], INNER)]
    ppermute x1, waiting for transfers between devices: 4.66 us -> 0.01 us  [line_body(): sum_out = along(end_keep + end_got, perm=OUTWARD)]
    pallas_call x4, Pallas kernels: 31.6 us -> 27.8 us  [line_grads(): pl.pallas_call(functools.partial(line_grads_kernel, len(pairs)), out_shap...]
  transfers between devices with their start and end apart: 24 -> 24, of which waited for: 11 -> 12; matrix products, arithmetic and copies ran while one was open for 4% -> 4% of each run, Pallas kernels for 26% -> 25%
where the time goes in v26:
time: 207 us; the launch traced here: 206 us
  waiting for transfers between devices  88.1 us (43%)
  Pallas kernels  53.8 us (26%)
  starting transfers between devices  33 us (16%)
  between operations  14 us (7%)
  other arithmetic  8.9 us (4%)
  local copies, waits for them, and re-layouts  8.11 us (4%)
    pallas_call x4, Pallas kernels, line_grads(): pl.pallas_call(functools.partial(line_grads_kernel, len(pairs)), out_shap...  27.8 us
    ppermute x1, waiting for transfers between devices, line_body(): both_1 = along(both, perm=PAIRS)  21.7 us
    ppermute x1, waiting for transfers between devices, line_body(): both_2o = along(both_2m, perm=OUTWARD)  13.9 us
    ppermute x1, waiting for transfers between devices, line_body(): near_a = along(mine, perm=INWARD)  12.6 us
    ppermute x1, waiting for transfers between devices, line_body(): end_got = sideways(end_give)  12.1 us
    pallas_call x1, Pallas kernels, place_first(): pl.pallas_call(place_kernel, out_shape=(jax.ShapeDtypeStruct((depth, widt...  8.74 us
    all_gather x1, waiting for transfers between devices, line_body(): tokens_3 = lax.all_gather(both_3m[:rows] + both_3o[:rows], INNER)  8.43 us
    ppermute x1, waiting for transfers between devices, line_body(): near_b = along(other, perm=INWARD)  7.55 us
  transfers between devices with their start and end apart: 24, of which 12 were waited for; matrix products, arithmetic and copies ran while one was open for 4% of the time, Pallas kernels for 25%

profile of v26, /device:TPU:0, one launch (start us, length us, event | category | flops | bytes accessed | tf_op | source)
XLA Modules:
  0.0 205.9 jit_solution(2542565375337922484)
XLA Ops:
  7.2 0.7 convert_element_type.26
  7.9 0.1 convert_element_type.27
  8.0 1.3 constant_dynamic-slice_fusion.2
  9.3 1.1 pad_maximum_fusion
  10.4 5.0 %collective-permute-start = (bf16[33,128,128]{2,1,0:T(8,128)(2,1)}, bf16[33,128,128]{2,1,0:T(8,128)(2,1)S(1)}, u32[]{:S(2)}, u32[]{:S(2)}) collective-permute-start(bf16[33,128,128]{2,1,0:T(8,128)(2,1)} %pad_maximum_fusion), channel_id=1, source_target_pairs={{0,4},{12,8},{1,5},{13,9},{2,6},{14,10},{3,7},{15,11},{16,20},{28,... | collective-permute-start | bytes 3244040 | tf_op jit(solution)/shard_map/ppermute | solution.py:463
  15.4 1.7 collective-permute-start.1
  17.1 6.1 %line_grads.4.refs_2_ = bf16[64,128,128]{2,1,0:T(8,128)(2,1)} custom-call(s32[64]{0:T(128)} %ids.7, bf16[256,4096]{1,0:T(8,128)(2,1)} %tokens.1, bf16[256,1024]{1,0:T(8,128)(2,1)} %upstream.1), custom_call_target="tpu_custom_call" | custom-call | flops 536870912 | bytes 4718592 | tf_op jit(solution)/shard_map/line_grads/pallas_call | solution.py:411
  23.2 1.2 constant_dynamic-slice_fusion.1
  24.4 0.1 pad_maximum_fusion.1
  24.5 0.4 copy-done
  24.9 1.2 constant_dynamic-slice_fusion
  26.1 12.6 %collective-permute-done.near_a = bf16[33,128,128]{2,1,0:T(8,128)(2,1)S(1)} collective-permute-done((bf16[33,128,128]{2,1,0:T(8,128)(2,1)}, bf16[33,128,128]{2,1,0:T(8,128)(2,1)S(1)}, u32[]{:S(2)}, u32[]{:S(2)}) %collective-permute-start) | collective-permute-done | bytes 1081376 | tf_op jit(solution)/shard_map/ppermute | solution.py:463
  38.7 1.7 collective-permute-start.3
  40.4 1.5 collective-permute-start.4
  41.9 5.7 %collective-permute-start.2 = (bf16[512,1024]{1,0:T(8,128)(2,1)S(1)}, bf16[512,1024]{1,0:T(8,128)(2,1)S(1)}, u32[]{:S(2)}, u32[]{:S(2)}) collective-permute-start(bf16[512,1024]{1,0:T(8,128)(2,1)S(1)} %pad_maximum_fusion.1), channel_id=1, source_target_pairs={{0,4},{12,8},{4,0},{8,12},{1,5},{13,9},{5,1},{9,13},{2,6},{14,10},... | collective-permute-start | bytes 3145736 | tf_op jit(solution)/shard_map/ppermute | solution.py:473
  47.6 21.7 %collective-permute-done.2 = bf16[512,1024]{1,0:T(8,128)(2,1)S(1)} collective-permute-done((bf16[512,1024]{1,0:T(8,128)(2,1)S(1)}, bf16[512,1024]{1,0:T(8,128)(2,1)S(1)}, u32[]{:S(2)}, u32[]{:S(2)}) %collective-permute-start.2) | collective-permute-done | bytes 1048608 | tf_op jit(solution)/shard_map/ppermute | solution.py:473
  69.3 1.0 copy-done.9
  70.4 1.0 fusion
  71.4 0.0 all-gather.9.cloned.1.call-start
  71.5 0.6 collective-permute-start.6
  72.0 3.7 %collective-permute-start.5 = (bf16[32,128,128]{2,1,0:T(8,128)(2,1)}, bf16[32,128,128]{2,1,0:T(8,128)(2,1)S(1)}, u32[]{:S(2)}, u32[]{:S(2)}) collective-permute-start(bf16[32,128,128]{2,1,0:T(8,128)(2,1)} %constant_dynamic-slice_fusion), channel_id=1, source_target_pairs={{0,4},{12,8},{1,5},{13,9},{2,6},{14,10},{3,7},{15,11},{16,20},{28,... | collective-permute-start | bytes 3145736 | tf_op jit(solution)/shard_map/ppermute | solution.py:477
  75.7 0.7 collective-permute-start.7
  76.5 0.7 pad_add_fusion.place_of
  77.2 1.2 bitcast_convert_fusion
  78.4 1.2 bitcast_convert_fusion.1.ids_3
  79.6 8.7 %place_first.1 = (bf16[4096,1024]{1,0:T(8,128)(2,1)}, bf16[1024,4096]{1,0:T(8,128)(2,1)}) custom-call(s32[4]{0:T(128)} %pad_add_fusion.place_of, s32[64]{0:T(128)} %ids.7, s32[64]{0:T(128)} %get-tuple-element.104.ids_1, s32[64]{0:T(128)} %get-tuple-element.103.ids_2, s32[64]{0:T(128)} %bitcast_convert_fusion.1.ids_3, bf16[64,128,128]{2,1,0:T(8,128)(2,1)} %own.1, ...), custom_call_target="tpu_custom_call" | custom-call | bytes 25165824 | tf_op jit(solution)/shard_map/place_first/pallas_call | solution.py:181
  88.3 7.6 %collective-permute-done.5.near_b = bf16[32,128,128]{2,1,0:T(8,128)(2,1)S(1)} collective-permute-done((bf16[32,128,128]{2,1,0:T(8,128)(2,1)}, bf16[32,128,128]{2,1,0:T(8,128)(2,1)S(1)}, u32[]{:S(2)}, u32[]{:S(2)}) %collective-permute-start.5) | collective-permute-done | bytes 1048608 | tf_op jit(solution)/shard_map/ppermute | solution.py:477
  95.9 0.9 copy-done.8
  96.8 0.7 collective-permute-start.10
  97.6 1.3 collective-permute-start.11
  98.9 3.8 %project_back.1 = (bf16[2,256,1024]{2,1,0:T(8,128)(2,1)}, bf16[2,256,1024]{2,1,0:T(8,128)(2,1)}, bf16[2,256,1024]{2,1,0:T(8,128)(2,1)}, bf16[256,1024]{1,0:T(8,128)(2,1)}, bf16[256,1024]{1,0:T(8,128)(2,1)}) custom-call(s32[4]{0:T(128)} %pad_add_fusion.place_of, s32[64]{0:T(128)} %get-tuple-element.104.ids_1, s32[64]{0:T(128)} %bitcast_convert_fusion.1.ids_3, ...), custom_call_target="tpu_custom_call" | custom-call | flops 4294967296 | bytes 13631488 | tf_op jit(solution)/shard_map/project_back/pallas_call | solution.py:239
  102.7 0.1 collective-permute-start.8
  102.8 0.5 collective-permute-start.9
  103.3 1.6 collective-permute-done.8.refs_0_
  104.9 0.9 collective-permute-done.9.refs_1_
  105.8 3.0 %add_split.2 = (bf16[256,1024]{1,0:T(8,128)(2,1)}, bf16[256,1024]{1,0:T(8,128)(2,1)}) custom-call(s32[4]{0:T(128)} %pad_add_fusion.place_of, bf16[2,256,1024]{2,1,0:T(8,128)(2,1)} %get-tuple-element.68.keep, bf16[256,1024]{1,0:T(8,128)(2,1)} %copy-done.16, bf16[256,1024]{1,0:T(8,128)(2,1)} %collective-permute-done.9.refs_1_), custom_call_target="tpu_custom_call" | custom-call | flops 524288 | bytes 3145728 | tf_op jit(solution)/shard_map/add_split/pallas_call | solution.py:328
  108.8 13.9 %collective-permute-done.11.refs_2_ = bf16[512,1024]{1,0:T(8,128)(2,1)S(1)} collective-permute-done((bf16[512,1024]{1,0:T(8,128)(2,1)S(1)}, bf16[512,1024]{1,0:T(8,128)(2,1)S(1)}, u32[]{:S(2)}, u32[]{:S(2)}) %collective-permute-start.11) | collective-permute-done | bytes 1048608 | tf_op jit(solution)/shard_map/ppermute | solution.py:490
  122.7 0.9 slice_add_fusion.1
  123.7 0.0 all-gather.11.cloned.1.call-start
  123.7 0.1 collective-permute-start.13
  123.8 1.3 collective-permute-start.19
  125.1 1.6 collective-permute-start.12
  126.7 3.9 %project_forward.1 = (bf16[256,1024]{1,0:T(8,128)(2,1)}, bf16[256,1024]{1,0:T(8,128)(2,1)}) custom-call(s32[4]{0:T(128)} %pad_add_fusion.place_of, s32[64]{0:T(128)} %get-tuple-element.104.ids_1, s32[64]{0:T(128)} %bitcast_convert_fusion.1.ids_3, bf16[4096,1024]{1,0:T(8,128)(2,1)} %get-tuple-element.81.partial, bf16[32,128,128]{2,1,0:T(8,128)(2,1)} %copy-done.8, ...), custom_call_target="tpu_custom_call" | custom-call | flops 536870912 | bytes 4194304 | tf_op jit(solution)/shard_map/project_forward/pallas_call | solution.py:296
  130.6 3.5 %add_split.3 = (bf16[256,1024]{1,0:T(8,128)(2,1)}, bf16[256,1024]{1,0:T(8,128)(2,1)}) custom-call(s32[4]{0:T(128)} %pad_add_fusion.place_of, bf16[2,256,1024]{2,1,0:T(8,128)(2,1)} %get-tuple-element.77.keep, bf16[2,256,1024]{2,1,0:T(8,128)(2,1)} %collective-permute-done.13.refs_0_), custom_call_target="tpu_custom_call" | custom-call | flops 524288 | bytes 3145728 | tf_op jit(solution)/shard_map/add_split/pallas_call | solution.py:328
  134.1 12.1 %collective-permute-done.12 = bf16[256,1024]{1,0:T(8,128)(2,1)S(1)} collective-permute-done((bf16[256,1024]{1,0:T(8,128)(2,1)}, bf16[256,1024]{1,0:T(8,128)(2,1)S(1)}, u32[]{:S(2)}, u32[]{:S(2)}) %collective-permute-start.12) | collective-permute-done | bytes 524320 | tf_op jit(solution)/shard_map/ppermute | solution.py:500
  146.2 5.1 %collective-permute-done.19.refs_2_ = bf16[512,1024]{1,0:T(8,128)(2,1)S(1)} collective-permute-done((bf16[512,1024]{1,0:T(8,128)(2,1)S(1)}, bf16[512,1024]{1,0:T(8,128)(2,1)S(1)}, u32[]{:S(2)}, u32[]{:S(2)}) %collective-permute-start.19) | collective-permute-done | bytes 1048608 | tf_op jit(solution)/shard_map/ppermute | solution.py:502
  151.3 0.9 slice_add_fusion
  152.2 1.2 add.28
  153.5 1.3 collective-permute-start.15
  154.8 1.6 collective-permute-start.16
  156.3 6.8 %line_grads.5.refs_3_ = bf16[64,128,128]{2,1,0:T(8,128)(2,1)} custom-call(s32[64]{0:T(128)} %ids.7, bf16[4,256,1024]{2,1,0:T(8,128)(2,1)} %bitcast.17, bf16[256,1024]{1,0:T(8,128)(2,1)} %get-tuple-element.101.end_upstream.refs_1_, bf16[64,128,128]{2,1,0:T(8,128)(2,1)} %line_grads.4.refs_2_), custom_call_target="tpu_custom_call" | custom-call | flops 536870912 | bytes 6815744 | tf_op jit(solution)/shard_map/line_grads/pallas_call | solution.py:411
  163.2 7.4 %line_grads.6.refs_3_ = bf16[64,128,128]{2,1,0:T(8,128)(2,1)} custom-call(s32[64]{0:T(128)} %ids.7, bf16[4,256,1024]{2,1,0:T(8,128)(2,1)} %bitcast.18, bf16[512,1024]{1,0:T(8,128)(2,1)} %copy-done.1, bf16[512,1024]{1,0:T(8,128)(2,1)} %copy-done.3, bf16[64,128,128]{2,1,0:T(8,128)(2,1)} %line_grads.5.refs_3_), custom_call_target="tpu_custom_call" | custom-call | flops 536870912 | bytes 8388608 | tf_op jit(solution)/shard_map/line_grads/pallas_call | solution.py:411
  170.6 3.3 %collective-permute-done.16 = bf16[256,1024]{1,0:T(8,128)(2,1)S(1)} collective-permute-done((bf16[256,1024]{1,0:T(8,128)(2,1)}, bf16[256,1024]{1,0:T(8,128)(2,1)S(1)}, u32[]{:S(2)}, u32[]{:S(2)}) %collective-permute-start.16) | collective-permute-done | bytes 524320 | tf_op jit(solution)/shard_map/ppermute | solution.py:510
  173.9 0.1 add_select_fusion.own
  174.0 2.4 %collective-permute-start.17 = (bf16[256,1024]{1,0:T(8,128)(2,1)S(1)}, bf16[256,1024]{1,0:T(8,128)(2,1)S(1)}, u32[]{:S(2)}, u32[]{:S(2)}) collective-permute-start(bf16[256,1024]{1,0:T(8,128)(2,1)S(1)} %add_select_fusion.own), channel_id=1, source_target_pairs={{0,2},{2,0},{1,3},{3,1},{4,6},{6,4},{5,7},{7,5},{8,10},{10,8},{9,1... | collective-permute-start | bytes 1572872 | tf_op jit(solution)/shard_map/ppermute | solution.py:519
  176.5 1.3 collective-permute-start.14
  177.8 8.4 %all-gather.11.cloned.1.call-done = bf16[1024,1024]{1,0:T(8,128)(2,1)} async-done(((bf16[256,1024]{1,0:T(8,128)(2,1)}), bf16[1024,1024]{1,0:T(8,128)(2,1)}) %all-gather.11.cloned.1.call-update) | async-done | bytes 2097168 | tf_op jit(solution)/shard_map/all_gather | solution.py:512
  186.2 7.4 %line_grads.7 = bf16[64,128,128]{2,1,0:T(8,128)(2,1)} custom-call(s32[64]{0:T(128)} %ids.7, bf16[4,256,1024]{2,1,0:T(8,128)(2,1)} %bitcast.19, bf16[512,1024]{1,0:T(8,128)(2,1)} %copy-done.2, bf16[512,1024]{1,0:T(8,128)(2,1)} %copy-done.4, bf16[64,128,128]{2,1,0:T(8,128)(2,1)} %line_grads.6.refs_3_), custom_call_target="tpu_custom_call" | custom-call | flops 536870912 | bytes 8388608 | tf_op jit(solution)/shard_map/line_grads/pallas_call | solution.py:411
  193.6 0.3 collective-permute-start.20
  193.9 0.1 collective-permute-done.14
  194.0 0.8 broadcast_select_fusion
  194.9 0.7 collective-permute-done.20.by_both
  195.6 0.8 copy-done.17
  196.4 3.0 %assemble.1 = bf16[256,4096]{1,0:T(8,128)(2,1)} custom-call(s32[4]{0:T(128)} %pad_add_fusion.place_of, bf16[256,1024]{1,0:T(8,128)(2,1)} %copy-done.5, bf16[256,1024]{1,0:T(8,128)(2,1)} %copy-done.15, bf16[256,1024]{1,0:T(8,128)(2,1)} %copy-done.13, bf16[256,1024]{1,0:T(8,128)(2,1)} %copy-done.17), custom_call_target="tpu_custom_call" | custom-call | bytes 4194304 | tf_op jit(solution)/shard_map/assemble/pallas_call | solution.py:353
  (55 shorter events, 0.2 us)
Async XLA Ops:
  7.2 88.7 %all-gather.7.cloned.1.call-start = ((), (), s32[]{:S(2)}) async-start(), calls=%async_computation | async-start | bytes 2621440 | tf_op jit(solution)/shard_map/all_gather | solution.py:480
  10.4 28.3 %collective-permute-start = (bf16[33,128,128]{2,1,0:T(8,128)(2,1)}, bf16[33,128,128]{2,1,0:T(8,128)(2,1)S(1)}, u32[]{:S(2)}, u32[]{:S(2)}) collective-permute-start(bf16[33,128,128]{2,1,0:T(8,128)(2,1)} %pad_maximum_fusion), channel_id=1, source_target_pairs={{0,4},{12,8},{1,5},{13,9},{2,6},{14,10},{3,7},{15,11},{16,20},{28,... | collective-permute-start | bytes 3244040 | tf_op jit(solution)/shard_map/ppermute | solution.py:463
  15.4 23.4 %collective-permute-start.1 = (bf16[33,128,128]{2,1,0:T(8,128)(2,1)}, bf16[33,128,128]{2,1,0:T(8,128)(2,1)}, u32[]{:S(2)}, u32[]{:S(2)}) collective-permute-start(bf16[33,128,128]{2,1,0:T(8,128)(2,1)} %pad_maximum_fusion), channel_id=1, source_target_pairs={{4,8},{8,4},{5,9},{9,5},{6,10},{10,6},{7,11},{11,7},{20,24},{24,20... | collective-permute-start | bytes 3244040 | tf_op jit(solution)/shard_map/ppermute | solution.py:464
  17.1 7.3 %copy-start.6 = (bf16[256,1024]{1,0:T(8,128)(2,1)S(1)}, bf16[256,1024]{1,0:T(8,128)(2,1)}, u32[]{:S(2)}) copy-start(bf16[256,1024]{1,0:T(8,128)(2,1)} %upstream.1) | copy-start | bytes 1572868
  23.2 1.8 copy-start
  24.9 46.5 %copy-start.10 = (bf16[512,1024]{1,0:T(8,128)(2,1)}, bf16[512,1024]{1,0:T(8,128)(2,1)S(1)}, u32[]{:S(2)}) copy-start(bf16[512,1024]{1,0:T(8,128)(2,1)S(1)} %pad_maximum_fusion.1) | copy-start | bytes 3145732
  38.7 40.8 %copy-start.7 = (bf16[33,128,128]{2,1,0:T(8,128)(2,1)}, bf16[33,128,128]{2,1,0:T(8,128)(2,1)S(1)}, u32[]{:S(2)}) copy-start(bf16[33,128,128]{2,1,0:T(8,128)(2,1)S(1)} %collective-permute-done.near_a) | copy-start | bytes 3244036
  38.7 30.6 %collective-permute-start.3 = (bf16[33,128,128]{2,1,0:T(8,128)(2,1)S(1)}, bf16[33,128,128]{2,1,0:T(8,128)(2,1)}, u32[]{:S(2)}, u32[]{:S(2)}) collective-permute-start(bf16[33,128,128]{2,1,0:T(8,128)(2,1)S(1)} %collective-permute-done.near_a), channel_id=1, source_target_pairs={{4,8},{8,4},{5,9},{9,5},{6,10},{10,6},{7,11},{11,7},{20,24},{24,20... | collective-permute-start | bytes 3244040 | tf_op jit(solution)/shard_map/ppermute | solution.py:471
  40.4 28.9 %collective-permute-start.4 = (bf16[33,128,128]{2,1,0:T(8,128)(2,1)}, bf16[33,128,128]{2,1,0:T(8,128)(2,1)}, u32[]{:S(2)}, u32[]{:S(2)}) collective-permute-start(bf16[33,128,128]{2,1,0:T(8,128)(2,1)} %collective-permute-done.1.far_a), channel_id=1, source_target_pairs={{0,16},{16,0},{1,17},{17,1},{2,18},{18,2},{3,19},{19,3},{4,20},{20... | collective-permute-start | bytes 3244040 | tf_op jit(solution)/shard_map/ppermute | solution.py:472
  41.9 27.4 %collective-permute-start.2 = (bf16[512,1024]{1,0:T(8,128)(2,1)S(1)}, bf16[512,1024]{1,0:T(8,128)(2,1)S(1)}, u32[]{:S(2)}, u32[]{:S(2)}) collective-permute-start(bf16[512,1024]{1,0:T(8,128)(2,1)S(1)} %pad_maximum_fusion.1), channel_id=1, source_target_pairs={{0,4},{12,8},{4,0},{8,12},{1,5},{13,9},{5,1},{9,13},{2,6},{14,10},... | collective-permute-start | bytes 3145736 | tf_op jit(solution)/shard_map/ppermute | solution.py:473
  69.3 1.1 copy-start.9
  71.4 91.7 %all-gather.9.cloned.1.call-start = ((), (), s32[]{:S(2)}) async-start(), calls=%async_computation.1 | async-start | bytes 2621440 | tf_op jit(solution)/shard_map/all_gather | solution.py:503
  71.5 24.4 %collective-permute-start.6 = (bf16[33,128,128]{2,1,0:T(8,128)(2,1)}, bf16[33,128,128]{2,1,0:T(8,128)(2,1)}, u32[]{:S(2)}, u32[]{:S(2)}) collective-permute-start(bf16[33,128,128]{2,1,0:T(8,128)(2,1)} %collective-permute-done.3.end_a), channel_id=1, source_target_pairs={{0,16},{16,0},{1,17},{17,1},{2,18},{18,2},{3,19},{19,3},{4,20},{20... | collective-permute-start | bytes 3244040 | tf_op jit(solution)/shard_map/ppermute | solution.py:478
  72.0 23.8 %collective-permute-start.5 = (bf16[32,128,128]{2,1,0:T(8,128)(2,1)}, bf16[32,128,128]{2,1,0:T(8,128)(2,1)S(1)}, u32[]{:S(2)}, u32[]{:S(2)}) collective-permute-start(bf16[32,128,128]{2,1,0:T(8,128)(2,1)} %constant_dynamic-slice_fusion), channel_id=1, source_target_pairs={{0,4},{12,8},{1,5},{13,9},{2,6},{14,10},{3,7},{15,11},{16,20},{28,... | collective-permute-start | bytes 3145736 | tf_op jit(solution)/shard_map/ppermute | solution.py:477
  75.7 20.1 %collective-permute-start.7 = (bf16[512,1024]{1,0:T(8,128)(2,1)}, bf16[512,1024]{1,0:T(8,128)(2,1)S(1)}, u32[]{:S(2)}, u32[]{:S(2)}) collective-permute-start(bf16[512,1024]{1,0:T(8,128)(2,1)} %copy-done.10), channel_id=1, source_target_pairs={{4,8},{8,4},{5,9},{9,5},{6,10},{10,6},{7,11},{11,7},{20,24},{24,20... | collective-permute-start | bytes 3145736 | tf_op jit(solution)/shard_map/ppermute | solution.py:479
  95.9 1.0 copy-start.8
  95.9 26.9 %copy-start.1 = (bf16[512,1024]{1,0:T(8,128)(2,1)}, bf16[512,1024]{1,0:T(8,128)(2,1)S(1)}, u32[]{:S(2)}) copy-start(bf16[512,1024]{1,0:T(8,128)(2,1)S(1)} %collective-permute-done.7.refs_1_) | copy-start | bytes 3145732
  96.8 12.0 %collective-permute-start.10 = (bf16[512,1024]{1,0:T(8,128)(2,1)}, bf16[512,1024]{1,0:T(8,128)(2,1)S(1)}, u32[]{:S(2)}, u32[]{:S(2)}) collective-permute-start(bf16[512,1024]{1,0:T(8,128)(2,1)} %copy-done.9), channel_id=1, source_target_pairs={{4,8},{8,4},{5,9},{9,5},{6,10},{10,6},{7,11},{11,7},{20,24},{24,20... | collective-permute-start | bytes 3145736 | tf_op jit(solution)/shard_map/ppermute | solution.py:489
  97.6 25.2 %collective-permute-start.11 = (bf16[512,1024]{1,0:T(8,128)(2,1)S(1)}, bf16[512,1024]{1,0:T(8,128)(2,1)S(1)}, u32[]{:S(2)}, u32[]{:S(2)}) collective-permute-start(bf16[512,1024]{1,0:T(8,128)(2,1)S(1)} %collective-permute-done.7.refs_1_), channel_id=1, source_target_pairs={{4,0},{8,12},{5,1},{9,13},{6,2},{10,14},{7,3},{11,15},{20,16},{24,... | collective-permute-start | bytes 3145736 | tf_op jit(solution)/shard_map/ppermute | solution.py:490
  102.7 2.2 %collective-permute-start.8 = (bf16[256,1024]{1,0:T(8,128)(2,1)}, bf16[256,1024]{1,0:T(8,128)(2,1)S(1)}, u32[]{:S(2)}, u32[]{:S(2)}) collective-permute-start(bf16[256,1024]{1,0:T(8,128)(2,1)} %get-tuple-element.69), channel_id=1, source_target_pairs={{0,1},{1,0},{2,3},{3,2},{4,5},{5,4},{6,7},{7,6},{8,9},{9,8},{10,11... | collective-permute-start | bytes 1572872 | tf_op jit(solution)/shard_map/ppermute | solution.py:495
  102.8 3.0 %collective-permute-start.9 = (bf16[256,1024]{1,0:T(8,128)(2,1)}, bf16[256,1024]{1,0:T(8,128)(2,1)}, u32[]{:S(2)}, u32[]{:S(2)}) collective-permute-start(bf16[256,1024]{1,0:T(8,128)(2,1)} %get-tuple-element.70), channel_id=1, source_target_pairs={{0,1},{1,0},{2,3},{3,2},{4,5},{5,4},{6,7},{7,6},{8,9},{9,8},{10,11... | collective-permute-start | bytes 1572872 | tf_op jit(solution)/shard_map/ppermute | solution.py:495
  104.9 0.9 copy-start.16
  108.8 42.4 %copy-start.2 = (bf16[512,1024]{1,0:T(8,128)(2,1)}, bf16[512,1024]{1,0:T(8,128)(2,1)S(1)}, u32[]{:S(2)}) copy-start(bf16[512,1024]{1,0:T(8,128)(2,1)S(1)} %collective-permute-done.10.refs_1_) | copy-start | bytes 3145732
  122.7 7.9 %copy-start.3 = (bf16[512,1024]{1,0:T(8,128)(2,1)}, bf16[512,1024]{1,0:T(8,128)(2,1)S(1)}, u32[]{:S(2)}) copy-start(bf16[512,1024]{1,0:T(8,128)(2,1)S(1)} %collective-permute-done.11.refs_2_) | copy-start | bytes 3145732
  123.7 62.5 %all-gather.11.cloned.1.call-start = ((), (), s32[]{:S(2)}) async-start(), calls=%async_computation.2 | async-start | bytes 2621440 | tf_op jit(solution)/shard_map/all_gather | solution.py:512
  123.7 6.9 %collective-permute-start.13 = (bf16[2,256,1024]{2,1,0:T(8,128)(2,1)}, bf16[2,256,1024]{2,1,0:T(8,128)(2,1)}, u32[]{:S(2)}, u32[]{:S(2)}) collective-permute-start(bf16[2,256,1024]{2,1,0:T(8,128)(2,1)} %get-tuple-element.78), channel_id=1, source_target_pairs={{0,1},{1,0},{2,3},{3,2},{4,5},{5,4},{6,7},{7,6},{8,9},{9,8},{10,11... | collective-permute-start | bytes 3145736 | tf_op jit(solution)/shard_map/ppermute | solution.py:501
  123.8 27.4 %collective-permute-start.19 = (bf16[512,1024]{1,0:T(8,128)(2,1)S(1)}, bf16[512,1024]{1,0:T(8,128)(2,1)S(1)}, u32[]{:S(2)}, u32[]{:S(2)}) collective-permute-start(bf16[512,1024]{1,0:T(8,128)(2,1)S(1)} %collective-permute-done.10.refs_1_), channel_id=1, source_target_pairs={{4,0},{8,12},{5,1},{9,13},{6,2},{10,14},{7,3},{11,15},{20,16},{24,... | collective-permute-start | bytes 3145736 | tf_op jit(solution)/shard_map/ppermute | solution.py:502
  125.1 21.0 %collective-permute-start.12 = (bf16[256,1024]{1,0:T(8,128)(2,1)}, bf16[256,1024]{1,0:T(8,128)(2,1)S(1)}, u32[]{:S(2)}, u32[]{:S(2)}) collective-permute-start(bf16[256,1024]{1,0:T(8,128)(2,1)} %get-tuple-element.76), channel_id=1, source_target_pairs={{0,2},{2,0},{1,3},{3,1},{4,6},{6,4},{5,7},{7,5},{8,10},{10,8},{9,1... | collective-permute-start | bytes 1572872 | tf_op jit(solution)/shard_map/ppermute | solution.py:500
  130.6 21.6 %copy-start.11 = (bf16[256,1024]{1,0:T(8,128)(2,1)S(1)}, bf16[256,1024]{1,0:T(8,128)(2,1)}, u32[]{:S(2)}) copy-start(bf16[256,1024]{1,0:T(8,128)(2,1)} %get-tuple-element.89) | copy-start | bytes 1572868
  146.2 5.1 %copy-start.14 = (bf16[256,1024]{1,0:T(8,128)(2,1)}, bf16[256,1024]{1,0:T(8,128)(2,1)S(1)}, u32[]{:S(2)}) copy-start(bf16[256,1024]{1,0:T(8,128)(2,1)S(1)} %collective-permute-done.12) | copy-start | bytes 1572868
  151.3 11.9 %copy-start.4 = (bf16[512,1024]{1,0:T(8,128)(2,1)}, bf16[512,1024]{1,0:T(8,128)(2,1)S(1)}, u32[]{:S(2)}) copy-start(bf16[512,1024]{1,0:T(8,128)(2,1)S(1)} %collective-permute-done.19.refs_2_) | copy-start | bytes 3145732
  153.5 17.1 %collective-permute-start.15 = (bf16[256,1024]{1,0:T(8,128)(2,1)S(1)}, bf16[256,1024]{1,0:T(8,128)(2,1)S(1)}, u32[]{:S(2)}, u32[]{:S(2)}) collective-permute-start(bf16[256,1024]{1,0:T(8,128)(2,1)S(1)} %add.28), channel_id=1, source_target_pairs={{4,0},{8,12},{5,1},{9,13},{6,2},{10,14},{7,3},{11,15},{20,16},{24,... | collective-permute-start | bytes 1572872 | tf_op jit(solution)/shard_map/ppermute | solution.py:509
  154.8 19.2 %collective-permute-start.16 = (bf16[256,1024]{1,0:T(8,128)(2,1)}, bf16[256,1024]{1,0:T(8,128)(2,1)S(1)}, u32[]{:S(2)}, u32[]{:S(2)}) collective-permute-start(bf16[256,1024]{1,0:T(8,128)(2,1)} %get-tuple-element.91), channel_id=1, source_target_pairs={{0,2},{2,0},{1,3},{3,1},{4,6},{6,4},{5,7},{7,5},{8,10},{10,8},{9,1... | collective-permute-start | bytes 1572872 | tf_op jit(solution)/shard_map/ppermute | solution.py:510
  163.2 10.8 %copy-start.12 = (bf16[256,1024]{1,0:T(8,128)(2,1)S(1)}, bf16[256,1024]{1,0:T(8,128)(2,1)}, u32[]{:S(2)}) copy-start(bf16[256,1024]{1,0:T(8,128)(2,1)} %get-tuple-element.88) | copy-start | bytes 1572868
  170.6 5.9 %copy-start.19 = (bf16[256,1024]{1,0:T(8,128)(2,1)S(1)}, bf16[256,1024]{1,0:T(8,128)(2,1)}, u32[]{:S(2)}) copy-start(bf16[256,1024]{1,0:T(8,128)(2,1)} %get-tuple-element.87) | copy-start | bytes 1572868
  174.0 19.6 %copy-start.5 = (bf16[256,1024]{1,0:T(8,128)(2,1)}, bf16[256,1024]{1,0:T(8,128)(2,1)S(1)}, u32[]{:S(2)}) copy-start(bf16[256,1024]{1,0:T(8,128)(2,1)S(1)} %add_select_fusion.own) | copy-start | bytes 1572868
  174.0 19.6 %collective-permute-start.17 = (bf16[256,1024]{1,0:T(8,128)(2,1)S(1)}, bf16[256,1024]{1,0:T(8,128)(2,1)S(1)}, u32[]{:S(2)}, u32[]{:S(2)}) collective-permute-start(bf16[256,1024]{1,0:T(8,128)(2,1)S(1)} %add_select_fusion.own), channel_id=1, source_target_pairs={{0,2},{2,0},{1,3},{3,1},{4,6},{6,4},{5,7},{7,5},{8,10},{10,8},{9,1... | collective-permute-start | bytes 1572872 | tf_op jit(solution)/shard_map/ppermute | solution.py:519
  176.5 17.1 %collective-permute-start.18 = (bf16[256,1024]{1,0:T(8,128)(2,1)S(1)}, bf16[256,1024]{1,0:T(8,128)(2,1)S(1)}, u32[]{:S(2)}, u32[]{:S(2)}) collective-permute-start(bf16[256,1024]{1,0:T(8,128)(2,1)S(1)} %add_select_fusion.own), channel_id=1, source_target_pairs={{0,1},{1,0},{2,3},{3,2},{4,5},{5,4},{6,7},{7,6},{8,9},{9,8},{10,11... | collective-permute-start | bytes 1572872 | tf_op jit(solution)/shard_map/ppermute | solution.py:519
  176.5 17.5 %collective-permute-start.14 = (bf16[256,1024]{1,0:T(8,128)(2,1)S(1)}, bf16[256,1024]{1,0:T(8,128)(2,1)S(1)}, u32[]{:S(2)}, u32[]{:S(2)}) collective-permute-start(bf16[256,1024]{1,0:T(8,128)(2,1)S(1)} %copy-done.19), channel_id=1, source_target_pairs={{4,0},{8,12},{5,1},{9,13},{6,2},{10,14},{7,3},{11,15},{20,16},{24,... | collective-permute-start | bytes 1572872 | tf_op jit(solution)/shard_map/ppermute | solution.py:517
  186.2 7.8 %copy-start.18 = (bf16[256,1024]{1,0:T(8,128)(2,1)S(1)}, bf16[256,1024]{1,0:T(8,128)(2,1)}, u32[]{:S(2)}) copy-start(bf16[256,1024]{1,0:T(8,128)(2,1)} %get-tuple-element.86) | copy-start | bytes 1572868
  193.6 2.0 copy-start.13
  193.6 2.0 copy-start.15
  193.6 2.0 collective-permute-start.20
  195.6 0.8 copy-start.17
Sparse Core Ops, SparseCore 0:
  71.5 21.0 all-gather.6
  123.8 28.6 all-gather.8
  154.0 32.1 all-gather.10

commit v27 on v26

--- a/solution.py
+++ b/solution.py
@@ -451,7 +451,14 @@
     middle = (at_z == 1) | (at_z == 2)
     place_of = jnp.stack([middle.astype(jnp.int32), half, at_tensor, at_replica])
     along = functools.partial(lax.ppermute, axis_name="dp")
-    across = functools.partial(lax.ppermute, axis_name="groups", perm=SWAP)
+    across = functools.partial(
+        lax.ppermute, axis_name=("groups", "dp"), perm=((1, 5), (5, 1), (2, 6), (6, 2))
+    )
+    middle_swap = ((2, 3), (3, 2), (4, 5), (5, 4))
+    middle_sideways = functools.partial(
+        lax.ppermute, axis_name=("dp", "tensor"), perm=middle_swap
+    )
+    middle_cores = functools.partial(lax.ppermute, axis_name=("dp", "replica"), perm=middle_swap)
     sideways = functools.partial(lax.ppermute, axis_name="tensor", perm=SWAP)
     cores = functools.partial(lax.ppermute, axis_name="replica", perm=SWAP)
     stage = lax.optimization_barrier
@@ -492,13 +499,13 @@
     end_keep, own_keep, own_give, *end_give = project_back(
         place_of, ids_1, ids_3, turned, *last, upstream_1, upstream
     )
-    end_keep, end_give = add_split(place_of, end_keep, *[cores(a) for a in end_give])
+    end_keep, end_give = add_split(place_of, end_keep, *[middle_cores(a) for a in end_give])
     end_keep, end_give, own_give, both_3m, both_2o = stage(
         (end_keep, end_give, own_give, both_3m, both_2o)
     )
 
-    end_got = sideways(end_give)
-    own_keep, own_give = add_split(place_of, own_keep, cores(own_give))
+    end_got = middle_sideways(end_give)
+    own_keep, own_give = add_split(place_of, own_keep, middle_cores(own_give))
     both_3o = along(both_3m, perm=OUTWARD)
     tokens_2 = lax.all_gather(both_2m[:rows] + both_2o[:rows], INNER)
     proj, end_proj = project_forward(place_of, ids_1, ids_3, partial, *last, tokens, tokens_1)
@@ -507,7 +514,7 @@
     )
 
     sum_out = along(end_keep + end_got, perm=OUTWARD)
-    own_got = sideways(own_give)
+    own_got = middle_sideways(own_give)
     grads = line_grads(block_ids, ((tokens_1, upstream_1),), grads, size)
     tokens_3 = lax.all_gather(both_3m[:rows] + both_3o[:rows], INNER)
     grads = line_grads(block_ids, ((tokens_2, both_2m, both_2o),), grads, size)

time: 207 us -> 219 us (1.058)
  waiting for transfers between devices: 88.1 us -> 94.8 us
  starting transfers between devices: 33 us -> 37.5 us
    ppermute x5, waiting for transfers between devices: 17.9 us -> 0.01 us  [the longest x2 0.01 us: line_body(): middle_cores(a)]
    ppermute x1, waiting for transfers between devices: 5.1 us -> 20.7 us  [line_body(): both_3o = along(both_3m, perm=OUTWARD)]
    ppermute x1, waiting for transfers between devices: 0.09 us -> 5.52 us  [line_body(): proj_out = along(end_proj, perm=OUTWARD)]
    all_gather x1, waiting for transfers between devices: 8.43 us -> 12.6 us  [line_body(): tokens_3 = lax.all_gather(both_3m[:rows] + both_3o[:rows], INNER)]
  transfers between devices with their start and end apart: 24 -> 24, of which waited for: 12 -> 7; matrix products, arithmetic and copies ran while one was open for 4% -> 4% of each run, Pallas kernels for 25% -> 23%
where the time goes in v27:
time: 219 us; the launch traced here: 218 us
  waiting for transfers between devices  94.8 us (43%)
  Pallas kernels  54 us (25%)
  starting transfers between devices  37.5 us (17%)
  between operations  14 us (6%)
  other arithmetic  8.9 us (4%)
  local copies, waits for them, and re-layouts  8.9 us (4%)
    pallas_call x4, Pallas kernels, line_grads(): pl.pallas_call(functools.partial(line_grads_kernel, len(pairs)), out_shap...  28.1 us
    ppermute x1, waiting for transfers between devices, line_body(): both_1 = along(both, perm=PAIRS)  21.7 us
    ppermute x1, waiting for transfers between devices, line_body(): both_3o = along(both_3m, perm=OUTWARD)  20.7 us
    ppermute x1, waiting for transfers between devices, line_body(): both_2o = along(both_2m, perm=OUTWARD)  14 us
    ppermute x1, waiting for transfers between devices, line_body(): near_a = along(mine, perm=INWARD)  12.6 us
    all_gather x1, waiting for transfers between devices, line_body(): tokens_3 = lax.all_gather(both_3m[:rows] + both_3o[:rows], INNER)  12.6 us
    pallas_call x1, Pallas kernels, place_first(): pl.pallas_call(place_kernel, out_shape=(jax.ShapeDtypeStruct((depth, widt...  8.79 us
    ppermute x1, waiting for transfers between devices, line_body(): near_b = along(other, perm=INWARD)  7.51 us
  transfers between devices with their start and end apart: 24, of which 7 were waited for; matrix products, arithmetic and copies ran while one was open for 4% of the time, Pallas kernels for 23%

profile of v27, /device:TPU:0, one launch (start us, length us, event | category | flops | bytes accessed | tf_op | source)
XLA Modules:
  0.0 218.2 jit_solution(18075167619493033742)
XLA Ops:
  7.2 0.0 all-gather.7.cloned.1.call-start
  7.2 0.7 convert_element_type.26
  7.9 0.1 convert_element_type.27
  8.0 1.3 constant_dynamic-slice_fusion.2
  9.3 1.1 pad_maximum_fusion
  10.4 5.0 %collective-permute-start = (bf16[33,128,128]{2,1,0:T(8,128)(2,1)}, bf16[33,128,128]{2,1,0:T(8,128)(2,1)S(1)}, u32[]{:S(2)}, u32[]{:S(2)}) collective-permute-start(bf16[33,128,128]{2,1,0:T(8,128)(2,1)} %pad_maximum_fusion), channel_id=1, source_target_pairs={{0,4},{12,8},{1,5},{13,9},{2,6},{14,10},{3,7},{15,11},{16,20},{28,... | collective-permute-start | bytes 3244040 | tf_op jit(solution)/shard_map/ppermute | solution.py:470
  15.4 1.7 collective-permute-start.1
  17.1 6.1 %line_grads.4.refs_2_ = bf16[64,128,128]{2,1,0:T(8,128)(2,1)} custom-call(s32[64]{0:T(128)} %ids.7, bf16[256,4096]{1,0:T(8,128)(2,1)} %tokens.1, bf16[256,1024]{1,0:T(8,128)(2,1)} %upstream.1), custom_call_target="tpu_custom_call" | custom-call | flops 536870912 | bytes 4718592 | tf_op jit(solution)/shard_map/line_grads/pallas_call | solution.py:411
  23.2 1.2 constant_dynamic-slice_fusion.1
  24.4 0.1 pad_maximum_fusion.1
  24.5 0.4 copy-done
  24.9 1.2 constant_dynamic-slice_fusion
  26.1 12.6 %collective-permute-done.near_a = bf16[33,128,128]{2,1,0:T(8,128)(2,1)S(1)} collective-permute-done((bf16[33,128,128]{2,1,0:T(8,128)(2,1)}, bf16[33,128,128]{2,1,0:T(8,128)(2,1)S(1)}, u32[]{:S(2)}, u32[]{:S(2)}) %collective-permute-start) | collective-permute-done | bytes 1081376 | tf_op jit(solution)/shard_map/ppermute | solution.py:470
  38.7 1.7 collective-permute-start.3
  40.4 1.7 collective-permute-start.4
  42.1 7.4 %collective-permute-start.2 = (bf16[512,1024]{1,0:T(8,128)(2,1)S(1)}, bf16[512,1024]{1,0:T(8,128)(2,1)S(1)}, u32[]{:S(2)}, u32[]{:S(2)}) collective-permute-start(bf16[512,1024]{1,0:T(8,128)(2,1)S(1)} %pad_maximum_fusion.1), channel_id=1, source_target_pairs={{0,4},{12,8},{4,0},{8,12},{1,5},{13,9},{5,1},{9,13},{2,6},{14,10},... | collective-permute-start | bytes 3145736 | tf_op jit(solution)/shard_map/ppermute | solution.py:480
  49.5 21.7 %collective-permute-done.2 = bf16[512,1024]{1,0:T(8,128)(2,1)S(1)} collective-permute-done((bf16[512,1024]{1,0:T(8,128)(2,1)S(1)}, bf16[512,1024]{1,0:T(8,128)(2,1)S(1)}, u32[]{:S(2)}, u32[]{:S(2)}) %collective-permute-start.2) | collective-permute-done | bytes 1048608 | tf_op jit(solution)/shard_map/ppermute | solution.py:480
  71.2 1.0 copy-done.9
  72.3 1.0 fusion
  73.3 0.0 all-gather.7.cloned.1.call-update
  73.3 0.0 all-gather.9.cloned.1.call-start
  73.4 1.7 collective-permute-start.6
  75.0 4.5 %collective-permute-start.5 = (bf16[32,128,128]{2,1,0:T(8,128)(2,1)}, bf16[32,128,128]{2,1,0:T(8,128)(2,1)S(1)}, u32[]{:S(2)}, u32[]{:S(2)}) collective-permute-start(bf16[32,128,128]{2,1,0:T(8,128)(2,1)} %constant_dynamic-slice_fusion), channel_id=1, source_target_pairs={{0,4},{12,8},{1,5},{13,9},{2,6},{14,10},{3,7},{15,11},{16,20},{28,... | collective-permute-start | bytes 3145736 | tf_op jit(solution)/shard_map/ppermute | solution.py:484
  79.5 0.7 collective-permute-start.7
  80.3 0.7 pad_add_fusion.place_of
  80.9 1.2 bitcast_convert_fusion
  82.2 1.2 bitcast_convert_fusion.1.ids_3
  83.4 8.8 %place_first.1 = (bf16[4096,1024]{1,0:T(8,128)(2,1)}, bf16[1024,4096]{1,0:T(8,128)(2,1)}) custom-call(s32[4]{0:T(128)} %pad_add_fusion.place_of, s32[64]{0:T(128)} %ids.7, s32[64]{0:T(128)} %get-tuple-element.104.ids_1, s32[64]{0:T(128)} %get-tuple-element.103.ids_2, s32[64]{0:T(128)} %bitcast_convert_fusion.1.ids_3, bf16[64,128,128]{2,1,0:T(8,128)(2,1)} %own.1, ...), custom_call_target="tpu_custom_call" | custom-call | bytes 25165824 | tf_op jit(solution)/shard_map/place_first/pallas_call | solution.py:181
  92.1 7.5 %collective-permute-done.5.near_b = bf16[32,128,128]{2,1,0:T(8,128)(2,1)S(1)} collective-permute-done((bf16[32,128,128]{2,1,0:T(8,128)(2,1)}, bf16[32,128,128]{2,1,0:T(8,128)(2,1)S(1)}, u32[]{:S(2)}, u32[]{:S(2)}) %collective-permute-start.5) | collective-permute-done | bytes 1048608 | tf_op jit(solution)/shard_map/ppermute | solution.py:484
  99.7 0.0 all-gather.7.cloned.1.call-done
  99.7 0.9 copy-done.8
  100.6 0.7 collective-permute-start.10
  101.3 1.3 collective-permute-start.11
  102.6 3.8 %project_back.1 = (bf16[2,256,1024]{2,1,0:T(8,128)(2,1)}, bf16[2,256,1024]{2,1,0:T(8,128)(2,1)}, bf16[2,256,1024]{2,1,0:T(8,128)(2,1)}, bf16[256,1024]{1,0:T(8,128)(2,1)}, bf16[256,1024]{1,0:T(8,128)(2,1)}) custom-call(s32[4]{0:T(128)} %pad_add_fusion.place_of, s32[64]{0:T(128)} %get-tuple-element.104.ids_1, s32[64]{0:T(128)} %bitcast_convert_fusion.1.ids_3, ...), custom_call_target="tpu_custom_call" | custom-call | flops 4294967296 | bytes 13631488 | tf_op jit(solution)/shard_map/project_back/pallas_call | solution.py:239
  106.5 0.7 collective-permute-start.8
  107.2 1.5 collective-permute-start.9
  108.7 0.8 copy-done.16
  109.5 3.0 %add_split.2 = (bf16[256,1024]{1,0:T(8,128)(2,1)}, bf16[256,1024]{1,0:T(8,128)(2,1)}) custom-call(s32[4]{0:T(128)} %pad_add_fusion.place_of, bf16[2,256,1024]{2,1,0:T(8,128)(2,1)} %get-tuple-element.68.keep, bf16[256,1024]{1,0:T(8,128)(2,1)} %copy-done.16, bf16[256,1024]{1,0:T(8,128)(2,1)} %collective-permute-done.9.refs_1_), custom_call_target="tpu_custom_call" | custom-call | flops 524288 | bytes 3145728 | tf_op jit(solution)/shard_map/add_split/pallas_call | solution.py:328
  112.5 14.0 %collective-permute-done.11.refs_2_ = bf16[512,1024]{1,0:T(8,128)(2,1)S(1)} collective-permute-done((bf16[512,1024]{1,0:T(8,128)(2,1)S(1)}, bf16[512,1024]{1,0:T(8,128)(2,1)S(1)}, u32[]{:S(2)}, u32[]{:S(2)}) %collective-permute-start.11) | collective-permute-done | bytes 1048608 | tf_op jit(solution)/shard_map/ppermute | solution.py:497
  126.5 0.9 slice_add_fusion.1
  127.4 0.0 all-gather.9.cloned.1.call-update
  127.5 0.0 all-gather.11.cloned.1.call-start
  127.5 1.6 collective-permute-start.13
  129.2 1.3 collective-permute-start.19
  130.4 0.7 collective-permute-start.12
  131.1 4.1 %project_forward.1 = (bf16[256,1024]{1,0:T(8,128)(2,1)}, bf16[256,1024]{1,0:T(8,128)(2,1)}) custom-call(s32[4]{0:T(128)} %pad_add_fusion.place_of, s32[64]{0:T(128)} %get-tuple-element.104.ids_1, s32[64]{0:T(128)} %bitcast_convert_fusion.1.ids_3, bf16[4096,1024]{1,0:T(8,128)(2,1)} %get-tuple-element.81.partial, bf16[32,128,128]{2,1,0:T(8,128)(2,1)} %copy-done.8, ...), custom_call_target="tpu_custom_call" | custom-call | flops 536870912 | bytes 4194304 | tf_op jit(solution)/shard_map/project_forward/pallas_call | solution.py:296
  135.3 3.1 %add_split.3 = (bf16[256,1024]{1,0:T(8,128)(2,1)}, bf16[256,1024]{1,0:T(8,128)(2,1)}) custom-call(s32[4]{0:T(128)} %pad_add_fusion.place_of, bf16[2,256,1024]{2,1,0:T(8,128)(2,1)} %get-tuple-element.77.keep, bf16[2,256,1024]{2,1,0:T(8,128)(2,1)} %collective-permute-done.13.refs_0_), custom_call_target="tpu_custom_call" | custom-call | flops 524288 | bytes 3145728 | tf_op jit(solution)/shard_map/add_split/pallas_call | solution.py:328
  138.4 20.7 %collective-permute-done.19.refs_2_ = bf16[512,1024]{1,0:T(8,128)(2,1)S(1)} collective-permute-done((bf16[512,1024]{1,0:T(8,128)(2,1)S(1)}, bf16[512,1024]{1,0:T(8,128)(2,1)S(1)}, u32[]{:S(2)}, u32[]{:S(2)}) %collective-permute-start.19) | collective-permute-done | bytes 1048608 | tf_op jit(solution)/shard_map/ppermute | solution.py:509
  159.1 0.9 slice_add_fusion
  160.1 1.2 add.28
  161.3 1.3 collective-permute-start.15
  162.6 0.7 collective-permute-start.16
  163.3 6.8 %line_grads.5.refs_3_ = bf16[64,128,128]{2,1,0:T(8,128)(2,1)} custom-call(s32[64]{0:T(128)} %ids.7, bf16[4,256,1024]{2,1,0:T(8,128)(2,1)} %bitcast.17, bf16[256,1024]{1,0:T(8,128)(2,1)} %get-tuple-element.101.end_upstream.refs_1_, bf16[64,128,128]{2,1,0:T(8,128)(2,1)} %line_grads.4.refs_2_), custom_call_target="tpu_custom_call" | custom-call | flops 536870912 | bytes 6815744 | tf_op jit(solution)/shard_map/line_grads/pallas_call | solution.py:411
  170.2 7.8 %line_grads.6.refs_3_ = bf16[64,128,128]{2,1,0:T(8,128)(2,1)} custom-call(s32[64]{0:T(128)} %ids.7, bf16[4,256,1024]{2,1,0:T(8,128)(2,1)} %bitcast.18, bf16[512,1024]{1,0:T(8,128)(2,1)} %copy-done.1, bf16[512,1024]{1,0:T(8,128)(2,1)} %copy-done.3, bf16[64,128,128]{2,1,0:T(8,128)(2,1)} %line_grads.5.refs_3_), custom_call_target="tpu_custom_call" | custom-call | flops 536870912 | bytes 8388608 | tf_op jit(solution)/shard_map/line_grads/pallas_call | solution.py:411
  178.0 0.1 add_select_fusion.own
  178.1 1.8 collective-permute-start.17
  179.8 1.3 collective-permute-start.14
  181.1 12.6 %all-gather.11.cloned.1.call-done = bf16[1024,1024]{1,0:T(8,128)(2,1)} async-done(((bf16[256,1024]{1,0:T(8,128)(2,1)}), bf16[1024,1024]{1,0:T(8,128)(2,1)}) %all-gather.11.cloned.1.call-update) | async-done | bytes 2097168 | tf_op jit(solution)/shard_map/all_gather | solution.py:519
  193.7 7.4 %line_grads.7 = bf16[64,128,128]{2,1,0:T(8,128)(2,1)} custom-call(s32[64]{0:T(128)} %ids.7, bf16[4,256,1024]{2,1,0:T(8,128)(2,1)} %bitcast.19, bf16[512,1024]{1,0:T(8,128)(2,1)} %copy-done.2, bf16[512,1024]{1,0:T(8,128)(2,1)} %copy-done.4, bf16[64,128,128]{2,1,0:T(8,128)(2,1)} %line_grads.6.refs_3_), custom_call_target="tpu_custom_call" | custom-call | flops 536870912 | bytes 8388608 | tf_op jit(solution)/shard_map/line_grads/pallas_call | solution.py:411
  201.2 0.3 collective-permute-start.20
  201.5 5.5 %collective-permute-done.14 = bf16[256,1024]{1,0:T(8,128)(2,1)S(1)} collective-permute-done((bf16[256,1024]{1,0:T(8,128)(2,1)S(1)}, bf16[256,1024]{1,0:T(8,128)(2,1)S(1)}, u32[]{:S(2)}, u32[]{:S(2)}) %collective-permute-start.14) | collective-permute-done | bytes 524320 | tf_op jit(solution)/shard_map/ppermute | solution.py:524
  207.0 0.8 broadcast_select_fusion
  207.9 0.8 copy-done.17
  208.7 3.0 %assemble.1 = bf16[256,4096]{1,0:T(8,128)(2,1)} custom-call(s32[4]{0:T(128)} %pad_add_fusion.place_of, bf16[256,1024]{1,0:T(8,128)(2,1)} %copy-done.5, bf16[256,1024]{1,0:T(8,128)(2,1)} %copy-done.15, bf16[256,1024]{1,0:T(8,128)(2,1)} %copy-done.13, bf16[256,1024]{1,0:T(8,128)(2,1)} %copy-done.17), custom_call_target="tpu_custom_call" | custom-call | bytes 4194304 | tf_op jit(solution)/shard_map/assemble/pallas_call | solution.py:353
  (55 shorter events, 0.1 us)
Async XLA Ops:
  7.2 92.5 %all-gather.7.cloned.1.call-start = ((), (), s32[]{:S(2)}) async-start(), calls=%async_computation | async-start | bytes 2621440 | tf_op jit(solution)/shard_map/all_gather | solution.py:487
  10.4 28.3 %collective-permute-start = (bf16[33,128,128]{2,1,0:T(8,128)(2,1)}, bf16[33,128,128]{2,1,0:T(8,128)(2,1)S(1)}, u32[]{:S(2)}, u32[]{:S(2)}) collective-permute-start(bf16[33,128,128]{2,1,0:T(8,128)(2,1)} %pad_maximum_fusion), channel_id=1, source_target_pairs={{0,4},{12,8},{1,5},{13,9},{2,6},{14,10},{3,7},{15,11},{16,20},{28,... | collective-permute-start | bytes 3244040 | tf_op jit(solution)/shard_map/ppermute | solution.py:470
  15.4 23.4 %collective-permute-start.1 = (bf16[33,128,128]{2,1,0:T(8,128)(2,1)}, bf16[33,128,128]{2,1,0:T(8,128)(2,1)}, u32[]{:S(2)}, u32[]{:S(2)}) collective-permute-start(bf16[33,128,128]{2,1,0:T(8,128)(2,1)} %pad_maximum_fusion), channel_id=1, source_target_pairs={{4,8},{8,4},{5,9},{9,5},{6,10},{10,6},{7,11},{11,7},{20,24},{24,20... | collective-permute-start | bytes 3244040 | tf_op jit(solution)/shard_map/ppermute | solution.py:471
  17.1 7.3 %copy-start.6 = (bf16[256,1024]{1,0:T(8,128)(2,1)S(1)}, bf16[256,1024]{1,0:T(8,128)(2,1)}, u32[]{:S(2)}) copy-start(bf16[256,1024]{1,0:T(8,128)(2,1)} %upstream.1) | copy-start | bytes 1572868
  23.2 1.8 copy-start
  24.9 48.4 %copy-start.10 = (bf16[512,1024]{1,0:T(8,128)(2,1)}, bf16[512,1024]{1,0:T(8,128)(2,1)S(1)}, u32[]{:S(2)}) copy-start(bf16[512,1024]{1,0:T(8,128)(2,1)S(1)} %pad_maximum_fusion.1) | copy-start | bytes 3145732
  38.7 44.6 %copy-start.7 = (bf16[33,128,128]{2,1,0:T(8,128)(2,1)}, bf16[33,128,128]{2,1,0:T(8,128)(2,1)S(1)}, u32[]{:S(2)}) copy-start(bf16[33,128,128]{2,1,0:T(8,128)(2,1)S(1)} %collective-permute-done.near_a) | copy-start | bytes 3244036
  38.7 32.5 %collective-permute-start.3 = (bf16[33,128,128]{2,1,0:T(8,128)(2,1)S(1)}, bf16[33,128,128]{2,1,0:T(8,128)(2,1)}, u32[]{:S(2)}, u32[]{:S(2)}) collective-permute-start(bf16[33,128,128]{2,1,0:T(8,128)(2,1)S(1)} %collective-permute-done.near_a), channel_id=1, source_target_pairs={{4,8},{8,4},{5,9},{9,5},{6,10},{10,6},{7,11},{11,7},{20,24},{24,20... | collective-permute-start | bytes 3244040 | tf_op jit(solution)/shard_map/ppermute | solution.py:478
  40.4 30.8 %collective-permute-start.4 = (bf16[33,128,128]{2,1,0:T(8,128)(2,1)}, bf16[33,128,128]{2,1,0:T(8,128)(2,1)}, u32[]{:S(2)}, u32[]{:S(2)}) collective-permute-start(bf16[33,128,128]{2,1,0:T(8,128)(2,1)} %collective-permute-done.1.far_a), channel_id=1, source_target_pairs={{4,20},{20,4},{8,24},{24,8},{5,21},{21,5},{9,25},{25,9},{6,22},{22... | collective-permute-start | bytes 3244040 | tf_op jit(solution)/shard_map/ppermute | solution.py:479
  42.1 29.2 %collective-permute-start.2 = (bf16[512,1024]{1,0:T(8,128)(2,1)S(1)}, bf16[512,1024]{1,0:T(8,128)(2,1)S(1)}, u32[]{:S(2)}, u32[]{:S(2)}) collective-permute-start(bf16[512,1024]{1,0:T(8,128)(2,1)S(1)} %pad_maximum_fusion.1), channel_id=1, source_target_pairs={{0,4},{12,8},{4,0},{8,12},{1,5},{13,9},{5,1},{9,13},{2,6},{14,10},... | collective-permute-start | bytes 3145736 | tf_op jit(solution)/shard_map/ppermute | solution.py:480
  71.2 1.1 copy-start.9
  73.3 96.8 %all-gather.9.cloned.1.call-start = ((), (), s32[]{:S(2)}) async-start(), calls=%async_computation.1 | async-start | bytes 2621440 | tf_op jit(solution)/shard_map/all_gather | solution.py:510
  73.4 26.3 %collective-permute-start.6 = (bf16[33,128,128]{2,1,0:T(8,128)(2,1)}, bf16[33,128,128]{2,1,0:T(8,128)(2,1)}, u32[]{:S(2)}, u32[]{:S(2)}) collective-permute-start(bf16[33,128,128]{2,1,0:T(8,128)(2,1)} %collective-permute-done.3.end_a), channel_id=1, source_target_pairs={{4,20},{20,4},{8,24},{24,8},{5,21},{21,5},{9,25},{25,9},{6,22},{22... | collective-permute-start | bytes 3244040 | tf_op jit(solution)/shard_map/ppermute | solution.py:485
  75.0 24.6 %collective-permute-start.5 = (bf16[32,128,128]{2,1,0:T(8,128)(2,1)}, bf16[32,128,128]{2,1,0:T(8,128)(2,1)S(1)}, u32[]{:S(2)}, u32[]{:S(2)}) collective-permute-start(bf16[32,128,128]{2,1,0:T(8,128)(2,1)} %constant_dynamic-slice_fusion), channel_id=1, source_target_pairs={{0,4},{12,8},{1,5},{13,9},{2,6},{14,10},{3,7},{15,11},{16,20},{28,... | collective-permute-start | bytes 3145736 | tf_op jit(solution)/shard_map/ppermute | solution.py:484
  79.5 20.1 %collective-permute-start.7 = (bf16[512,1024]{1,0:T(8,128)(2,1)}, bf16[512,1024]{1,0:T(8,128)(2,1)S(1)}, u32[]{:S(2)}, u32[]{:S(2)}) collective-permute-start(bf16[512,1024]{1,0:T(8,128)(2,1)} %copy-done.10), channel_id=1, source_target_pairs={{4,8},{8,4},{5,9},{9,5},{6,10},{10,6},{7,11},{11,7},{20,24},{24,20... | collective-permute-start | bytes 3145736 | tf_op jit(solution)/shard_map/ppermute | solution.py:486
  99.7 1.0 copy-start.8
  99.7 26.9 %copy-start.1 = (bf16[512,1024]{1,0:T(8,128)(2,1)}, bf16[512,1024]{1,0:T(8,128)(2,1)S(1)}, u32[]{:S(2)}) copy-start(bf16[512,1024]{1,0:T(8,128)(2,1)S(1)} %collective-permute-done.7.refs_1_) | copy-start | bytes 3145732
  100.6 11.9 %collective-permute-start.10 = (bf16[512,1024]{1,0:T(8,128)(2,1)}, bf16[512,1024]{1,0:T(8,128)(2,1)S(1)}, u32[]{:S(2)}, u32[]{:S(2)}) collective-permute-start(bf16[512,1024]{1,0:T(8,128)(2,1)} %copy-done.9), channel_id=1, source_target_pairs={{4,8},{8,4},{5,9},{9,5},{6,10},{10,6},{7,11},{11,7},{20,24},{24,20... | collective-permute-start | bytes 3145736 | tf_op jit(solution)/shard_map/ppermute | solution.py:496
  101.3 25.2 %collective-permute-start.11 = (bf16[512,1024]{1,0:T(8,128)(2,1)S(1)}, bf16[512,1024]{1,0:T(8,128)(2,1)S(1)}, u32[]{:S(2)}, u32[]{:S(2)}) collective-permute-start(bf16[512,1024]{1,0:T(8,128)(2,1)S(1)} %collective-permute-done.7.refs_1_), channel_id=1, source_target_pairs={{4,0},{8,12},{5,1},{9,13},{6,2},{10,14},{7,3},{11,15},{20,16},{24,... | collective-permute-start | bytes 3145736 | tf_op jit(solution)/shard_map/ppermute | solution.py:497
  106.5 2.2 collective-permute-start.8
  107.2 1.5 collective-permute-start.9
  108.7 0.8 copy-start.16
  112.5 46.6 %copy-start.2 = (bf16[512,1024]{1,0:T(8,128)(2,1)}, bf16[512,1024]{1,0:T(8,128)(2,1)S(1)}, u32[]{:S(2)}) copy-start(bf16[512,1024]{1,0:T(8,128)(2,1)S(1)} %collective-permute-done.10.refs_1_) | copy-start | bytes 3145732
  126.5 8.7 %copy-start.3 = (bf16[512,1024]{1,0:T(8,128)(2,1)}, bf16[512,1024]{1,0:T(8,128)(2,1)S(1)}, u32[]{:S(2)}) copy-start(bf16[512,1024]{1,0:T(8,128)(2,1)S(1)} %collective-permute-done.11.refs_2_) | copy-start | bytes 3145732
  127.5 66.3 %all-gather.11.cloned.1.call-start = ((), (), s32[]{:S(2)}) async-start(), calls=%async_computation.2 | async-start | bytes 2621440 | tf_op jit(solution)/shard_map/all_gather | solution.py:519
  127.5 7.7 %collective-permute-start.13 = (bf16[2,256,1024]{2,1,0:T(8,128)(2,1)}, bf16[2,256,1024]{2,1,0:T(8,128)(2,1)}, u32[]{:S(2)}, u32[]{:S(2)}) collective-permute-start(bf16[2,256,1024]{2,1,0:T(8,128)(2,1)} %get-tuple-element.78), channel_id=1, source_target_pairs={{4,5},{5,4},{8,9},{9,8},{6,7},{7,6},{10,11},{11,10},{20,21},{21,20... | collective-permute-start | bytes 3145736 | tf_op jit(solution)/shard_map/ppermute | solution.py:508
  129.2 30.0 %collective-permute-start.19 = (bf16[512,1024]{1,0:T(8,128)(2,1)S(1)}, bf16[512,1024]{1,0:T(8,128)(2,1)S(1)}, u32[]{:S(2)}, u32[]{:S(2)}) collective-permute-start(bf16[512,1024]{1,0:T(8,128)(2,1)S(1)} %collective-permute-done.10.refs_1_), channel_id=1, source_target_pairs={{4,0},{8,12},{5,1},{9,13},{6,2},{10,14},{7,3},{11,15},{20,16},{24,... | collective-permute-start | bytes 3145736 | tf_op jit(solution)/shard_map/ppermute | solution.py:509
  130.4 8.0 %collective-permute-start.12 = (bf16[256,1024]{1,0:T(8,128)(2,1)}, bf16[256,1024]{1,0:T(8,128)(2,1)S(1)}, u32[]{:S(2)}, u32[]{:S(2)}) collective-permute-start(bf16[256,1024]{1,0:T(8,128)(2,1)} %get-tuple-element.76), channel_id=1, source_target_pairs={{4,6},{6,4},{8,10},{10,8},{5,7},{7,5},{9,11},{11,9},{20,22},{22,20... | collective-permute-start | bytes 1572872 | tf_op jit(solution)/shard_map/ppermute | solution.py:507
  135.3 24.8 %copy-start.11 = (bf16[256,1024]{1,0:T(8,128)(2,1)S(1)}, bf16[256,1024]{1,0:T(8,128)(2,1)}, u32[]{:S(2)}) copy-start(bf16[256,1024]{1,0:T(8,128)(2,1)} %get-tuple-element.89) | copy-start | bytes 1572868
  138.4 20.7 %copy-start.14 = (bf16[256,1024]{1,0:T(8,128)(2,1)}, bf16[256,1024]{1,0:T(8,128)(2,1)S(1)}, u32[]{:S(2)}) copy-start(bf16[256,1024]{1,0:T(8,128)(2,1)S(1)} %collective-permute-done.12) | copy-start | bytes 1572868
  159.1 11.1 %copy-start.4 = (bf16[512,1024]{1,0:T(8,128)(2,1)}, bf16[512,1024]{1,0:T(8,128)(2,1)S(1)}, u32[]{:S(2)}) copy-start(bf16[512,1024]{1,0:T(8,128)(2,1)S(1)} %collective-permute-done.19.refs_2_) | copy-start | bytes 3145732
  161.3 16.6 %collective-permute-start.15 = (bf16[256,1024]{1,0:T(8,128)(2,1)S(1)}, bf16[256,1024]{1,0:T(8,128)(2,1)S(1)}, u32[]{:S(2)}, u32[]{:S(2)}) collective-permute-start(bf16[256,1024]{1,0:T(8,128)(2,1)S(1)} %add.28), channel_id=1, source_target_pairs={{4,0},{8,12},{5,1},{9,13},{6,2},{10,14},{7,3},{11,15},{20,16},{24,... | collective-permute-start | bytes 1572872 | tf_op jit(solution)/shard_map/ppermute | solution.py:516
  162.6 15.3 %collective-permute-start.16 = (bf16[256,1024]{1,0:T(8,128)(2,1)}, bf16[256,1024]{1,0:T(8,128)(2,1)S(1)}, u32[]{:S(2)}, u32[]{:S(2)}) collective-permute-start(bf16[256,1024]{1,0:T(8,128)(2,1)} %get-tuple-element.91), channel_id=1, source_target_pairs={{4,6},{6,4},{8,10},{10,8},{5,7},{7,5},{9,11},{11,9},{20,22},{22,20... | collective-permute-start | bytes 1572872 | tf_op jit(solution)/shard_map/ppermute | solution.py:517
  170.2 7.8 %copy-start.12 = (bf16[256,1024]{1,0:T(8,128)(2,1)S(1)}, bf16[256,1024]{1,0:T(8,128)(2,1)}, u32[]{:S(2)}) copy-start(bf16[256,1024]{1,0:T(8,128)(2,1)} %get-tuple-element.88) | copy-start | bytes 1572868
  178.0 1.9 copy-start.19
  178.1 23.1 %copy-start.5 = (bf16[256,1024]{1,0:T(8,128)(2,1)}, bf16[256,1024]{1,0:T(8,128)(2,1)S(1)}, u32[]{:S(2)}) copy-start(bf16[256,1024]{1,0:T(8,128)(2,1)S(1)} %add_select_fusion.own) | copy-start | bytes 1572868
  178.1 23.1 %collective-permute-start.17 = (bf16[256,1024]{1,0:T(8,128)(2,1)S(1)}, bf16[256,1024]{1,0:T(8,128)(2,1)S(1)}, u32[]{:S(2)}, u32[]{:S(2)}) collective-permute-start(bf16[256,1024]{1,0:T(8,128)(2,1)S(1)} %add_select_fusion.own), channel_id=1, source_target_pairs={{0,2},{2,0},{1,3},{3,1},{4,6},{6,4},{5,7},{7,5},{8,10},{10,8},{9,1... | collective-permute-start | bytes 1572872 | tf_op jit(solution)/shard_map/ppermute | solution.py:526
  179.8 21.3 %collective-permute-start.18 = (bf16[256,1024]{1,0:T(8,128)(2,1)S(1)}, bf16[256,1024]{1,0:T(8,128)(2,1)S(1)}, u32[]{:S(2)}, u32[]{:S(2)}) collective-permute-start(bf16[256,1024]{1,0:T(8,128)(2,1)S(1)} %add_select_fusion.own), channel_id=1, source_target_pairs={{0,1},{1,0},{2,3},{3,2},{4,5},{5,4},{6,7},{7,6},{8,9},{9,8},{10,11... | collective-permute-start | bytes 1572872 | tf_op jit(solution)/shard_map/ppermute | solution.py:526
  179.8 27.2 %collective-permute-start.14 = (bf16[256,1024]{1,0:T(8,128)(2,1)S(1)}, bf16[256,1024]{1,0:T(8,128)(2,1)S(1)}, u32[]{:S(2)}, u32[]{:S(2)}) collective-permute-start(bf16[256,1024]{1,0:T(8,128)(2,1)S(1)} %copy-done.19), channel_id=1, source_target_pairs={{4,0},{8,12},{5,1},{9,13},{6,2},{10,14},{7,3},{11,15},{20,16},{24,... | collective-permute-start | bytes 1572872 | tf_op jit(solution)/shard_map/ppermute | solution.py:524
  193.7 13.3 %copy-start.18 = (bf16[256,1024]{1,0:T(8,128)(2,1)S(1)}, bf16[256,1024]{1,0:T(8,128)(2,1)}, u32[]{:S(2)}) copy-start(bf16[256,1024]{1,0:T(8,128)(2,1)} %get-tuple-element.86) | copy-start | bytes 1572868
  201.1 6.7 %copy-start.13 = (bf16[256,1024]{1,0:T(8,128)(2,1)}, bf16[256,1024]{1,0:T(8,128)(2,1)S(1)}, u32[]{:S(2)}) copy-start(bf16[256,1024]{1,0:T(8,128)(2,1)S(1)} %collective-permute-done.17.by_tensor) | copy-start | bytes 1572868
  201.2 6.7 %copy-start.15 = (bf16[256,1024]{1,0:T(8,128)(2,1)}, bf16[256,1024]{1,0:T(8,128)(2,1)S(1)}, u32[]{:S(2)}) copy-start(bf16[256,1024]{1,0:T(8,128)(2,1)S(1)} %collective-permute-done.18.by_core) | copy-start | bytes 1572868
  201.2 6.7 %collective-permute-start.20 = (bf16[256,1024]{1,0:T(8,128)(2,1)S(1)}, bf16[256,1024]{1,0:T(8,128)(2,1)S(1)}, u32[]{:S(2)}, u32[]{:S(2)}) collective-permute-start(bf16[256,1024]{1,0:T(8,128)(2,1)S(1)} %collective-permute-done.17.by_tensor), channel_id=1, source_target_pairs={{0,1},{1,0},{2,3},{3,2},{4,5},{5,4},{6,7},{7,6},{8,9},{9,8},{10,11... | collective-permute-start | bytes 1572872 | tf_op jit(solution)/shard_map/ppermute | solution.py:527
  207.9 0.8 copy-start.17
Sparse Core Ops, SparseCore 0:
  73.5 21.0 all-gather.6
  127.6 26.3 all-gather.8
  160.2 33.4 all-gather.10

commit v28 on v26

--- a/solution.py
+++ b/solution.py
@@ -363,15 +363,15 @@
     )(place_of, *quarters)
 
 
-def line_grads_kernel(pairs_n, ids, *refs):
+def line_grads_kernel(pairs_n, summed, ids, *refs):
     refs = list(refs)
     pairs = []
     for k in range(pairs_n):
         x, d = refs.pop(0), refs.pop(0)
-        if d.shape[0] > x.shape[-2]:
-            rows, other = x.shape[-2], refs.pop(0)
+        if summed[k]:
+            other = refs.pop(0)
             total_d = refs.pop()
-            total_d[...] = d[rows:] + other[rows:]
+            total_d[...] = d[...] + other[...]
             d = total_d
         pairs.append((x, d))
     start = refs.pop(0) if len(refs) == 2 else None
@@ -405,13 +405,17 @@
 def line_grads(ids, pairs, start, size):
     slots = ids.shape[0]
     flat = [a for pair in pairs for a in pair] + ([] if start is None else [start])
+    lower = [pl.BlockSpec((a.shape[0] // 2, a.shape[1]), lambda _: (1, 0)) for a in pairs[0][1:]]
+    specs = [whole()] + (lower if len(pairs[0]) == 3 else [whole()])
+    specs += [] if start is None else [whole()]
     sums = [
         pltpu.VMEM((p[0].shape[-2], p[1].shape[1]), jnp.bfloat16) for p in pairs if len(p) == 3
     ]
     return pl.pallas_call(
-        functools.partial(line_grads_kernel, len(pairs)),
+        functools.partial(line_grads_kernel, len(pairs), tuple(len(p) == 3 for p in pairs)),
         out_shape=jax.ShapeDtypeStruct((slots, size, size), jnp.bfloat16),
-        in_specs=[whole(pltpu.SMEM)] + [whole()] * len(flat),
+        grid=(1,),
+        in_specs=[whole(pltpu.SMEM)] + specs,
         out_specs=whole(),
         scratch_shapes=sums,
         compiler_params=pltpu.CompilerParams(vmem_limit_bytes=VMEM_LIMIT),

time: 207 us -> 206 us (level)
  transfers between devices with their start and end apart: 24 -> 24, of which waited for: 12 -> 12; matrix products, arithmetic and copies ran while one was open for 4% -> 4% of each run, Pallas kernels for 25% -> 24%
where the time goes in v28:
time: 206 us
  waiting for transfers between devices  88.5 us (43%)
  Pallas kernels  53.1 us (26%)
  starting transfers between devices  33 us (16%)
  between operations  14 us (7%)
  other arithmetic  8.9 us (4%)
  local copies, waits for them, and re-layouts  8.11 us (4%)
    pallas_call x4, Pallas kernels, line_grads(): pl.pallas_call(functools.partial(line_grads_kernel, len(pairs), tuple((le...  27.2 us
    ppermute x1, waiting for transfers between devices, line_body(): both_1 = along(both, perm=PAIRS)  21.7 us
    ppermute x1, waiting for transfers between devices, line_body(): both_2o = along(both_2m, perm=OUTWARD)  13.9 us
    ppermute x1, waiting for transfers between devices, line_body(): near_a = along(mine, perm=INWARD)  12.6 us
    ppermute x1, waiting for transfers between devices, line_body(): end_got = sideways(end_give)  12 us
    pallas_call x1, Pallas kernels, place_first(): pl.pallas_call(place_kernel, out_shape=(jax.ShapeDtypeStruct((depth, widt...  8.74 us
    all_gather x1, waiting for transfers between devices, line_body(): tokens_3 = lax.all_gather(both_3m[:rows] + both_3o[:rows], INNER)  8.43 us
    ppermute x1, waiting for transfers between devices, line_body(): near_b = along(other, perm=INWARD)  7.55 us
  transfers between devices with their start and end apart: 24, of which 12 were waited for; matrix products, arithmetic and copies ran while one was open for 4% of the time, Pallas kernels for 24%

profile of v28, /device:TPU:0, one launch (start us, length us, event | category | flops | bytes accessed | tf_op | source)
XLA Modules:
  0.0 205.6 jit_solution(7310272235540133072)
XLA Ops:
  7.2 0.7 convert_element_type.26
  7.9 0.1 convert_element_type.27
  8.0 1.3 constant_dynamic-slice_fusion.2
  9.3 1.1 pad_maximum_fusion
  10.4 5.0 %collective-permute-start = (bf16[33,128,128]{2,1,0:T(8,128)(2,1)}, bf16[33,128,128]{2,1,0:T(8,128)(2,1)S(1)}, u32[]{:S(2)}, u32[]{:S(2)}) collective-permute-start(bf16[33,128,128]{2,1,0:T(8,128)(2,1)} %pad_maximum_fusion), channel_id=1, source_target_pairs={{0,4},{12,8},{1,5},{13,9},{2,6},{14,10},{3,7},{15,11},{16,20},{28,... | collective-permute-start | bytes 3244040 | tf_op jit(solution)/shard_map/ppermute | solution.py:467
  15.4 1.7 collective-permute-start.1
  17.1 6.1 %line_grads.4.refs_2_ = bf16[64,128,128]{2,1,0:T(8,128)(2,1)} custom-call(s32[64]{0:T(128)} %ids.7, bf16[256,4096]{1,0:T(8,128)(2,1)} %tokens.1, bf16[256,1024]{1,0:T(8,128)(2,1)} %upstream.1), custom_call_target="tpu_custom_call" | custom-call | flops 536870912 | bytes 4718592 | tf_op jit(solution)/shard_map/line_grads/pallas_call | solution.py:414
  23.2 1.2 constant_dynamic-slice_fusion.1
  24.4 0.1 pad_maximum_fusion.1
  24.5 0.4 copy-done
  24.9 1.2 constant_dynamic-slice_fusion
  26.1 12.6 %collective-permute-done.near_a = bf16[33,128,128]{2,1,0:T(8,128)(2,1)S(1)} collective-permute-done((bf16[33,128,128]{2,1,0:T(8,128)(2,1)}, bf16[33,128,128]{2,1,0:T(8,128)(2,1)S(1)}, u32[]{:S(2)}, u32[]{:S(2)}) %collective-permute-start) | collective-permute-done | bytes 1081376 | tf_op jit(solution)/shard_map/ppermute | solution.py:467
  38.7 1.7 collective-permute-start.3
  40.4 1.5 collective-permute-start.4
  41.9 5.7 %collective-permute-start.2 = (bf16[512,1024]{1,0:T(8,128)(2,1)S(1)}, bf16[512,1024]{1,0:T(8,128)(2,1)S(1)}, u32[]{:S(2)}, u32[]{:S(2)}) collective-permute-start(bf16[512,1024]{1,0:T(8,128)(2,1)S(1)} %pad_maximum_fusion.1), channel_id=1, source_target_pairs={{0,4},{12,8},{4,0},{8,12},{1,5},{13,9},{5,1},{9,13},{2,6},{14,10},... | collective-permute-start | bytes 3145736 | tf_op jit(solution)/shard_map/ppermute | solution.py:477
  47.6 21.7 %collective-permute-done.2 = bf16[512,1024]{1,0:T(8,128)(2,1)S(1)} collective-permute-done((bf16[512,1024]{1,0:T(8,128)(2,1)S(1)}, bf16[512,1024]{1,0:T(8,128)(2,1)S(1)}, u32[]{:S(2)}, u32[]{:S(2)}) %collective-permute-start.2) | collective-permute-done | bytes 1048608 | tf_op jit(solution)/shard_map/ppermute | solution.py:477
  69.3 1.0 copy-done.9
  70.4 1.0 fusion
  71.4 0.0 all-gather.9.cloned.1.call-start
  71.5 0.6 collective-permute-start.6
  72.0 3.7 %collective-permute-start.5 = (bf16[32,128,128]{2,1,0:T(8,128)(2,1)}, bf16[32,128,128]{2,1,0:T(8,128)(2,1)S(1)}, u32[]{:S(2)}, u32[]{:S(2)}) collective-permute-start(bf16[32,128,128]{2,1,0:T(8,128)(2,1)} %constant_dynamic-slice_fusion), channel_id=1, source_target_pairs={{0,4},{12,8},{1,5},{13,9},{2,6},{14,10},{3,7},{15,11},{16,20},{28,... | collective-permute-start | bytes 3145736 | tf_op jit(solution)/shard_map/ppermute | solution.py:481
  75.7 0.7 collective-permute-start.7
  76.5 0.7 pad_add_fusion.place_of
  77.2 1.2 bitcast_convert_fusion
  78.4 1.2 bitcast_convert_fusion.1.ids_3
  79.6 8.7 %place_first.1 = (bf16[4096,1024]{1,0:T(8,128)(2,1)}, bf16[1024,4096]{1,0:T(8,128)(2,1)}) custom-call(s32[4]{0:T(128)} %pad_add_fusion.place_of, s32[64]{0:T(128)} %ids.7, s32[64]{0:T(128)} %get-tuple-element.104.ids_1, s32[64]{0:T(128)} %get-tuple-element.103.ids_2, s32[64]{0:T(128)} %bitcast_convert_fusion.1.ids_3, bf16[64,128,128]{2,1,0:T(8,128)(2,1)} %own.1, ...), custom_call_target="tpu_custom_call" | custom-call | bytes 25165824 | tf_op jit(solution)/shard_map/place_first/pallas_call | solution.py:181
  88.3 7.6 %collective-permute-done.5.near_b = bf16[32,128,128]{2,1,0:T(8,128)(2,1)S(1)} collective-permute-done((bf16[32,128,128]{2,1,0:T(8,128)(2,1)}, bf16[32,128,128]{2,1,0:T(8,128)(2,1)S(1)}, u32[]{:S(2)}, u32[]{:S(2)}) %collective-permute-start.5) | collective-permute-done | bytes 1048608 | tf_op jit(solution)/shard_map/ppermute | solution.py:481
  95.9 0.9 copy-done.8
  96.8 0.7 collective-permute-start.10
  97.6 1.3 collective-permute-start.11
  98.9 3.8 %project_back.1 = (bf16[2,256,1024]{2,1,0:T(8,128)(2,1)}, bf16[2,256,1024]{2,1,0:T(8,128)(2,1)}, bf16[2,256,1024]{2,1,0:T(8,128)(2,1)}, bf16[256,1024]{1,0:T(8,128)(2,1)}, bf16[256,1024]{1,0:T(8,128)(2,1)}) custom-call(s32[4]{0:T(128)} %pad_add_fusion.place_of, s32[64]{0:T(128)} %get-tuple-element.104.ids_1, s32[64]{0:T(128)} %bitcast_convert_fusion.1.ids_3, ...), custom_call_target="tpu_custom_call" | custom-call | flops 4294967296 | bytes 13631488 | tf_op jit(solution)/shard_map/project_back/pallas_call | solution.py:239
  102.7 0.1 collective-permute-start.8
  102.8 0.5 collective-permute-start.9
  103.3 1.6 collective-permute-done.8.refs_0_
  104.9 0.9 collective-permute-done.9.refs_1_
  105.8 3.0 %add_split.2 = (bf16[256,1024]{1,0:T(8,128)(2,1)}, bf16[256,1024]{1,0:T(8,128)(2,1)}) custom-call(s32[4]{0:T(128)} %pad_add_fusion.place_of, bf16[2,256,1024]{2,1,0:T(8,128)(2,1)} %get-tuple-element.68.keep, bf16[256,1024]{1,0:T(8,128)(2,1)} %copy-done.16, bf16[256,1024]{1,0:T(8,128)(2,1)} %collective-permute-done.9.refs_1_), custom_call_target="tpu_custom_call" | custom-call | flops 524288 | bytes 3145728 | tf_op jit(solution)/shard_map/add_split/pallas_call | solution.py:328
  108.8 13.9 %collective-permute-done.11.refs_2_ = bf16[512,1024]{1,0:T(8,128)(2,1)S(1)} collective-permute-done((bf16[512,1024]{1,0:T(8,128)(2,1)S(1)}, bf16[512,1024]{1,0:T(8,128)(2,1)S(1)}, u32[]{:S(2)}, u32[]{:S(2)}) %collective-permute-start.11) | collective-permute-done | bytes 1048608 | tf_op jit(solution)/shard_map/ppermute | solution.py:494
  122.7 0.9 slice_add_fusion.1
  123.7 0.0 all-gather.11.cloned.1.call-start
  123.7 0.1 collective-permute-start.13
  123.8 1.3 collective-permute-start.19
  125.1 1.6 collective-permute-start.12
  126.7 3.9 %project_forward.1 = (bf16[256,1024]{1,0:T(8,128)(2,1)}, bf16[256,1024]{1,0:T(8,128)(2,1)}) custom-call(s32[4]{0:T(128)} %pad_add_fusion.place_of, s32[64]{0:T(128)} %get-tuple-element.104.ids_1, s32[64]{0:T(128)} %bitcast_convert_fusion.1.ids_3, bf16[4096,1024]{1,0:T(8,128)(2,1)} %get-tuple-element.81.partial, bf16[32,128,128]{2,1,0:T(8,128)(2,1)} %copy-done.8, ...), custom_call_target="tpu_custom_call" | custom-call | flops 536870912 | bytes 4194304 | tf_op jit(solution)/shard_map/project_forward/pallas_call | solution.py:296
  130.6 3.4 %add_split.3 = (bf16[256,1024]{1,0:T(8,128)(2,1)}, bf16[256,1024]{1,0:T(8,128)(2,1)}) custom-call(s32[4]{0:T(128)} %pad_add_fusion.place_of, bf16[2,256,1024]{2,1,0:T(8,128)(2,1)} %get-tuple-element.77.keep, bf16[2,256,1024]{2,1,0:T(8,128)(2,1)} %collective-permute-done.13.refs_0_), custom_call_target="tpu_custom_call" | custom-call | flops 524288 | bytes 3145728 | tf_op jit(solution)/shard_map/add_split/pallas_call | solution.py:328
  134.0 12.0 %collective-permute-done.12 = bf16[256,1024]{1,0:T(8,128)(2,1)S(1)} collective-permute-done((bf16[256,1024]{1,0:T(8,128)(2,1)}, bf16[256,1024]{1,0:T(8,128)(2,1)S(1)}, u32[]{:S(2)}, u32[]{:S(2)}) %collective-permute-start.12) | collective-permute-done | bytes 524320 | tf_op jit(solution)/shard_map/ppermute | solution.py:504
  146.0 5.2 %collective-permute-done.19.refs_2_ = bf16[512,1024]{1,0:T(8,128)(2,1)S(1)} collective-permute-done((bf16[512,1024]{1,0:T(8,128)(2,1)S(1)}, bf16[512,1024]{1,0:T(8,128)(2,1)S(1)}, u32[]{:S(2)}, u32[]{:S(2)}) %collective-permute-start.19) | collective-permute-done | bytes 1048608 | tf_op jit(solution)/shard_map/ppermute | solution.py:506
  151.3 0.9 slice_add_fusion
  152.2 1.2 add.28
  153.5 1.3 collective-permute-start.15
  154.8 1.6 collective-permute-start.16
  156.3 6.8 %line_grads.5.refs_3_ = bf16[64,128,128]{2,1,0:T(8,128)(2,1)} custom-call(s32[64]{0:T(128)} %ids.7, bf16[4,256,1024]{2,1,0:T(8,128)(2,1)} %bitcast.17, bf16[256,1024]{1,0:T(8,128)(2,1)} %get-tuple-element.101.end_upstream.refs_1_, bf16[64,128,128]{2,1,0:T(8,128)(2,1)} %line_grads.4.refs_2_), custom_call_target="tpu_custom_call" | custom-call | flops 536870912 | bytes 6815744 | tf_op jit(solution)/shard_map/line_grads/pallas_call | solution.py:414
  163.2 7.1 %line_grads.6.refs_3_ = bf16[64,128,128]{2,1,0:T(8,128)(2,1)} custom-call(s32[64]{0:T(128)} %ids.7, bf16[4,256,1024]{2,1,0:T(8,128)(2,1)} %bitcast.18, bf16[512,1024]{1,0:T(8,128)(2,1)} %copy-done.1, bf16[512,1024]{1,0:T(8,128)(2,1)} %copy-done.3, bf16[64,128,128]{2,1,0:T(8,128)(2,1)} %line_grads.5.refs_3_), custom_call_target="tpu_custom_call" | custom-call | flops 536870912 | bytes 8388608 | tf_op jit(solution)/shard_map/line_grads/pallas_call | solution.py:414
  170.3 3.6 %collective-permute-done.16 = bf16[256,1024]{1,0:T(8,128)(2,1)S(1)} collective-permute-done((bf16[256,1024]{1,0:T(8,128)(2,1)}, bf16[256,1024]{1,0:T(8,128)(2,1)S(1)}, u32[]{:S(2)}, u32[]{:S(2)}) %collective-permute-start.16) | collective-permute-done | bytes 524320 | tf_op jit(solution)/shard_map/ppermute | solution.py:514
  173.9 0.1 add_select_fusion.own
  174.0 2.4 %collective-permute-start.17 = (bf16[256,1024]{1,0:T(8,128)(2,1)S(1)}, bf16[256,1024]{1,0:T(8,128)(2,1)S(1)}, u32[]{:S(2)}, u32[]{:S(2)}) collective-permute-start(bf16[256,1024]{1,0:T(8,128)(2,1)S(1)} %add_select_fusion.own), channel_id=1, source_target_pairs={{0,2},{2,0},{1,3},{3,1},{4,6},{6,4},{5,7},{7,5},{8,10},{10,8},{9,1... | collective-permute-start | bytes 1572872 | tf_op jit(solution)/shard_map/ppermute | solution.py:523
  176.5 1.3 collective-permute-start.14
  177.8 8.4 %all-gather.11.cloned.1.call-done = bf16[1024,1024]{1,0:T(8,128)(2,1)} async-done(((bf16[256,1024]{1,0:T(8,128)(2,1)}), bf16[1024,1024]{1,0:T(8,128)(2,1)}) %all-gather.11.cloned.1.call-update) | async-done | bytes 2097168 | tf_op jit(solution)/shard_map/all_gather | solution.py:516
  186.2 7.1 %line_grads.7 = bf16[64,128,128]{2,1,0:T(8,128)(2,1)} custom-call(s32[64]{0:T(128)} %ids.7, bf16[4,256,1024]{2,1,0:T(8,128)(2,1)} %bitcast.19, bf16[512,1024]{1,0:T(8,128)(2,1)} %copy-done.2, bf16[512,1024]{1,0:T(8,128)(2,1)} %copy-done.4, bf16[64,128,128]{2,1,0:T(8,128)(2,1)} %line_grads.6.refs_3_), custom_call_target="tpu_custom_call" | custom-call | flops 536870912 | bytes 8388608 | tf_op jit(solution)/shard_map/line_grads/pallas_call | solution.py:414
  193.3 0.3 collective-permute-start.20
  193.6 0.4 collective-permute-done.14
  194.0 0.8 broadcast_select_fusion
  194.9 0.4 collective-permute-done.20.by_both
  195.3 0.8 copy-done.17
  196.1 3.0 %assemble.1 = bf16[256,4096]{1,0:T(8,128)(2,1)} custom-call(s32[4]{0:T(128)} %pad_add_fusion.place_of, bf16[256,1024]{1,0:T(8,128)(2,1)} %copy-done.5, bf16[256,1024]{1,0:T(8,128)(2,1)} %copy-done.15, bf16[256,1024]{1,0:T(8,128)(2,1)} %copy-done.13, bf16[256,1024]{1,0:T(8,128)(2,1)} %copy-done.17), custom_call_target="tpu_custom_call" | custom-call | bytes 4194304 | tf_op jit(solution)/shard_map/assemble/pallas_call | solution.py:353
  (55 shorter events, 0.2 us)
Async XLA Ops:
  7.2 88.7 %all-gather.7.cloned.1.call-start = ((), (), s32[]{:S(2)}) async-start(), calls=%async_computation | async-start | bytes 2621440 | tf_op jit(solution)/shard_map/all_gather | solution.py:484
  10.4 28.3 %collective-permute-start = (bf16[33,128,128]{2,1,0:T(8,128)(2,1)}, bf16[33,128,128]{2,1,0:T(8,128)(2,1)S(1)}, u32[]{:S(2)}, u32[]{:S(2)}) collective-permute-start(bf16[33,128,128]{2,1,0:T(8,128)(2,1)} %pad_maximum_fusion), channel_id=1, source_target_pairs={{0,4},{12,8},{1,5},{13,9},{2,6},{14,10},{3,7},{15,11},{16,20},{28,... | collective-permute-start | bytes 3244040 | tf_op jit(solution)/shard_map/ppermute | solution.py:467
  15.4 23.4 %collective-permute-start.1 = (bf16[33,128,128]{2,1,0:T(8,128)(2,1)}, bf16[33,128,128]{2,1,0:T(8,128)(2,1)}, u32[]{:S(2)}, u32[]{:S(2)}) collective-permute-start(bf16[33,128,128]{2,1,0:T(8,128)(2,1)} %pad_maximum_fusion), channel_id=1, source_target_pairs={{4,8},{8,4},{5,9},{9,5},{6,10},{10,6},{7,11},{11,7},{20,24},{24,20... | collective-permute-start | bytes 3244040 | tf_op jit(solution)/shard_map/ppermute | solution.py:468
  17.1 7.3 %copy-start.6 = (bf16[256,1024]{1,0:T(8,128)(2,1)S(1)}, bf16[256,1024]{1,0:T(8,128)(2,1)}, u32[]{:S(2)}) copy-start(bf16[256,1024]{1,0:T(8,128)(2,1)} %upstream.1) | copy-start | bytes 1572868
  23.2 1.8 copy-start
  24.9 46.5 %copy-start.10 = (bf16[512,1024]{1,0:T(8,128)(2,1)}, bf16[512,1024]{1,0:T(8,128)(2,1)S(1)}, u32[]{:S(2)}) copy-start(bf16[512,1024]{1,0:T(8,128)(2,1)S(1)} %pad_maximum_fusion.1) | copy-start | bytes 3145732
  38.7 40.8 %copy-start.7 = (bf16[33,128,128]{2,1,0:T(8,128)(2,1)}, bf16[33,128,128]{2,1,0:T(8,128)(2,1)S(1)}, u32[]{:S(2)}) copy-start(bf16[33,128,128]{2,1,0:T(8,128)(2,1)S(1)} %collective-permute-done.near_a) | copy-start | bytes 3244036
  38.7 30.6 %collective-permute-start.3 = (bf16[33,128,128]{2,1,0:T(8,128)(2,1)S(1)}, bf16[33,128,128]{2,1,0:T(8,128)(2,1)}, u32[]{:S(2)}, u32[]{:S(2)}) collective-permute-start(bf16[33,128,128]{2,1,0:T(8,128)(2,1)S(1)} %collective-permute-done.near_a), channel_id=1, source_target_pairs={{4,8},{8,4},{5,9},{9,5},{6,10},{10,6},{7,11},{11,7},{20,24},{24,20... | collective-permute-start | bytes 3244040 | tf_op jit(solution)/shard_map/ppermute | solution.py:475
  40.4 28.9 %collective-permute-start.4 = (bf16[33,128,128]{2,1,0:T(8,128)(2,1)}, bf16[33,128,128]{2,1,0:T(8,128)(2,1)}, u32[]{:S(2)}, u32[]{:S(2)}) collective-permute-start(bf16[33,128,128]{2,1,0:T(8,128)(2,1)} %collective-permute-done.1.far_a), channel_id=1, source_target_pairs={{0,16},{16,0},{1,17},{17,1},{2,18},{18,2},{3,19},{19,3},{4,20},{20... | collective-permute-start | bytes 3244040 | tf_op jit(solution)/shard_map/ppermute | solution.py:476
  41.9 27.4 %collective-permute-start.2 = (bf16[512,1024]{1,0:T(8,128)(2,1)S(1)}, bf16[512,1024]{1,0:T(8,128)(2,1)S(1)}, u32[]{:S(2)}, u32[]{:S(2)}) collective-permute-start(bf16[512,1024]{1,0:T(8,128)(2,1)S(1)} %pad_maximum_fusion.1), channel_id=1, source_target_pairs={{0,4},{12,8},{4,0},{8,12},{1,5},{13,9},{5,1},{9,13},{2,6},{14,10},... | collective-permute-start | bytes 3145736 | tf_op jit(solution)/shard_map/ppermute | solution.py:477
  69.3 1.1 copy-start.9
  71.4 91.7 %all-gather.9.cloned.1.call-start = ((), (), s32[]{:S(2)}) async-start(), calls=%async_computation.1 | async-start | bytes 2621440 | tf_op jit(solution)/shard_map/all_gather | solution.py:507
  71.5 24.4 %collective-permute-start.6 = (bf16[33,128,128]{2,1,0:T(8,128)(2,1)}, bf16[33,128,128]{2,1,0:T(8,128)(2,1)}, u32[]{:S(2)}, u32[]{:S(2)}) collective-permute-start(bf16[33,128,128]{2,1,0:T(8,128)(2,1)} %collective-permute-done.3.end_a), channel_id=1, source_target_pairs={{0,16},{16,0},{1,17},{17,1},{2,18},{18,2},{3,19},{19,3},{4,20},{20... | collective-permute-start | bytes 3244040 | tf_op jit(solution)/shard_map/ppermute | solution.py:482
  72.0 23.8 %collective-permute-start.5 = (bf16[32,128,128]{2,1,0:T(8,128)(2,1)}, bf16[32,128,128]{2,1,0:T(8,128)(2,1)S(1)}, u32[]{:S(2)}, u32[]{:S(2)}) collective-permute-start(bf16[32,128,128]{2,1,0:T(8,128)(2,1)} %constant_dynamic-slice_fusion), channel_id=1, source_target_pairs={{0,4},{12,8},{1,5},{13,9},{2,6},{14,10},{3,7},{15,11},{16,20},{28,... | collective-permute-start | bytes 3145736 | tf_op jit(solution)/shard_map/ppermute | solution.py:481
  75.7 20.1 %collective-permute-start.7 = (bf16[512,1024]{1,0:T(8,128)(2,1)}, bf16[512,1024]{1,0:T(8,128)(2,1)S(1)}, u32[]{:S(2)}, u32[]{:S(2)}) collective-permute-start(bf16[512,1024]{1,0:T(8,128)(2,1)} %copy-done.10), channel_id=1, source_target_pairs={{4,8},{8,4},{5,9},{9,5},{6,10},{10,6},{7,11},{11,7},{20,24},{24,20... | collective-permute-start | bytes 3145736 | tf_op jit(solution)/shard_map/ppermute | solution.py:483
  95.9 1.0 copy-start.8
  95.9 26.9 %copy-start.1 = (bf16[512,1024]{1,0:T(8,128)(2,1)}, bf16[512,1024]{1,0:T(8,128)(2,1)S(1)}, u32[]{:S(2)}) copy-start(bf16[512,1024]{1,0:T(8,128)(2,1)S(1)} %collective-permute-done.7.refs_1_) | copy-start | bytes 3145732
  96.8 12.0 %collective-permute-start.10 = (bf16[512,1024]{1,0:T(8,128)(2,1)}, bf16[512,1024]{1,0:T(8,128)(2,1)S(1)}, u32[]{:S(2)}, u32[]{:S(2)}) collective-permute-start(bf16[512,1024]{1,0:T(8,128)(2,1)} %copy-done.9), channel_id=1, source_target_pairs={{4,8},{8,4},{5,9},{9,5},{6,10},{10,6},{7,11},{11,7},{20,24},{24,20... | collective-permute-start | bytes 3145736 | tf_op jit(solution)/shard_map/ppermute | solution.py:493
  97.6 25.2 %collective-permute-start.11 = (bf16[512,1024]{1,0:T(8,128)(2,1)S(1)}, bf16[512,1024]{1,0:T(8,128)(2,1)S(1)}, u32[]{:S(2)}, u32[]{:S(2)}) collective-permute-start(bf16[512,1024]{1,0:T(8,128)(2,1)S(1)} %collective-permute-done.7.refs_1_), channel_id=1, source_target_pairs={{4,0},{8,12},{5,1},{9,13},{6,2},{10,14},{7,3},{11,15},{20,16},{24,... | collective-permute-start | bytes 3145736 | tf_op jit(solution)/shard_map/ppermute | solution.py:494
  102.7 2.2 %collective-permute-start.8 = (bf16[256,1024]{1,0:T(8,128)(2,1)}, bf16[256,1024]{1,0:T(8,128)(2,1)S(1)}, u32[]{:S(2)}, u32[]{:S(2)}) collective-permute-start(bf16[256,1024]{1,0:T(8,128)(2,1)} %get-tuple-element.69), channel_id=1, source_target_pairs={{0,1},{1,0},{2,3},{3,2},{4,5},{5,4},{6,7},{7,6},{8,9},{9,8},{10,11... | collective-permute-start | bytes 1572872 | tf_op jit(solution)/shard_map/ppermute | solution.py:499
  102.8 3.0 %collective-permute-start.9 = (bf16[256,1024]{1,0:T(8,128)(2,1)}, bf16[256,1024]{1,0:T(8,128)(2,1)}, u32[]{:S(2)}, u32[]{:S(2)}) collective-permute-start(bf16[256,1024]{1,0:T(8,128)(2,1)} %get-tuple-element.70), channel_id=1, source_target_pairs={{0,1},{1,0},{2,3},{3,2},{4,5},{5,4},{6,7},{7,6},{8,9},{9,8},{10,11... | collective-permute-start | bytes 1572872 | tf_op jit(solution)/shard_map/ppermute | solution.py:499
  104.9 0.9 copy-start.16
  108.8 42.4 %copy-start.2 = (bf16[512,1024]{1,0:T(8,128)(2,1)}, bf16[512,1024]{1,0:T(8,128)(2,1)S(1)}, u32[]{:S(2)}) copy-start(bf16[512,1024]{1,0:T(8,128)(2,1)S(1)} %collective-permute-done.10.refs_1_) | copy-start | bytes 3145732
  122.7 7.9 %copy-start.3 = (bf16[512,1024]{1,0:T(8,128)(2,1)}, bf16[512,1024]{1,0:T(8,128)(2,1)S(1)}, u32[]{:S(2)}) copy-start(bf16[512,1024]{1,0:T(8,128)(2,1)S(1)} %collective-permute-done.11.refs_2_) | copy-start | bytes 3145732
  123.7 62.5 %all-gather.11.cloned.1.call-start = ((), (), s32[]{:S(2)}) async-start(), calls=%async_computation.2 | async-start | bytes 2621440 | tf_op jit(solution)/shard_map/all_gather | solution.py:516
  123.7 6.9 %collective-permute-start.13 = (bf16[2,256,1024]{2,1,0:T(8,128)(2,1)}, bf16[2,256,1024]{2,1,0:T(8,128)(2,1)}, u32[]{:S(2)}, u32[]{:S(2)}) collective-permute-start(bf16[2,256,1024]{2,1,0:T(8,128)(2,1)} %get-tuple-element.78), channel_id=1, source_target_pairs={{0,1},{1,0},{2,3},{3,2},{4,5},{5,4},{6,7},{7,6},{8,9},{9,8},{10,11... | collective-permute-start | bytes 3145736 | tf_op jit(solution)/shard_map/ppermute | solution.py:505
  123.8 27.4 %collective-permute-start.19 = (bf16[512,1024]{1,0:T(8,128)(2,1)S(1)}, bf16[512,1024]{1,0:T(8,128)(2,1)S(1)}, u32[]{:S(2)}, u32[]{:S(2)}) collective-permute-start(bf16[512,1024]{1,0:T(8,128)(2,1)S(1)} %collective-permute-done.10.refs_1_), channel_id=1, source_target_pairs={{4,0},{8,12},{5,1},{9,13},{6,2},{10,14},{7,3},{11,15},{20,16},{24,... | collective-permute-start | bytes 3145736 | tf_op jit(solution)/shard_map/ppermute | solution.py:506
  125.1 20.9 %collective-permute-start.12 = (bf16[256,1024]{1,0:T(8,128)(2,1)}, bf16[256,1024]{1,0:T(8,128)(2,1)S(1)}, u32[]{:S(2)}, u32[]{:S(2)}) collective-permute-start(bf16[256,1024]{1,0:T(8,128)(2,1)} %get-tuple-element.76), channel_id=1, source_target_pairs={{0,2},{2,0},{1,3},{3,1},{4,6},{6,4},{5,7},{7,5},{8,10},{10,8},{9,1... | collective-permute-start | bytes 1572872 | tf_op jit(solution)/shard_map/ppermute | solution.py:504
  130.6 21.6 %copy-start.11 = (bf16[256,1024]{1,0:T(8,128)(2,1)S(1)}, bf16[256,1024]{1,0:T(8,128)(2,1)}, u32[]{:S(2)}) copy-start(bf16[256,1024]{1,0:T(8,128)(2,1)} %get-tuple-element.89) | copy-start | bytes 1572868
  146.0 5.2 %copy-start.14 = (bf16[256,1024]{1,0:T(8,128)(2,1)}, bf16[256,1024]{1,0:T(8,128)(2,1)S(1)}, u32[]{:S(2)}) copy-start(bf16[256,1024]{1,0:T(8,128)(2,1)S(1)} %collective-permute-done.12) | copy-start | bytes 1572868
  151.3 11.9 %copy-start.4 = (bf16[512,1024]{1,0:T(8,128)(2,1)}, bf16[512,1024]{1,0:T(8,128)(2,1)S(1)}, u32[]{:S(2)}) copy-start(bf16[512,1024]{1,0:T(8,128)(2,1)S(1)} %collective-permute-done.19.refs_2_) | copy-start | bytes 3145732
  153.5 16.8 %collective-permute-start.15 = (bf16[256,1024]{1,0:T(8,128)(2,1)S(1)}, bf16[256,1024]{1,0:T(8,128)(2,1)S(1)}, u32[]{:S(2)}, u32[]{:S(2)}) collective-permute-start(bf16[256,1024]{1,0:T(8,128)(2,1)S(1)} %add.28), channel_id=1, source_target_pairs={{4,0},{8,12},{5,1},{9,13},{6,2},{10,14},{7,3},{11,15},{20,16},{24,... | collective-permute-start | bytes 1572872 | tf_op jit(solution)/shard_map/ppermute | solution.py:513
  154.8 19.2 %collective-permute-start.16 = (bf16[256,1024]{1,0:T(8,128)(2,1)}, bf16[256,1024]{1,0:T(8,128)(2,1)S(1)}, u32[]{:S(2)}, u32[]{:S(2)}) collective-permute-start(bf16[256,1024]{1,0:T(8,128)(2,1)} %get-tuple-element.91), channel_id=1, source_target_pairs={{0,2},{2,0},{1,3},{3,1},{4,6},{6,4},{5,7},{7,5},{8,10},{10,8},{9,1... | collective-permute-start | bytes 1572872 | tf_op jit(solution)/shard_map/ppermute | solution.py:514
  163.2 10.8 %copy-start.12 = (bf16[256,1024]{1,0:T(8,128)(2,1)S(1)}, bf16[256,1024]{1,0:T(8,128)(2,1)}, u32[]{:S(2)}) copy-start(bf16[256,1024]{1,0:T(8,128)(2,1)} %get-tuple-element.88) | copy-start | bytes 1572868
  170.3 6.2 %copy-start.19 = (bf16[256,1024]{1,0:T(8,128)(2,1)S(1)}, bf16[256,1024]{1,0:T(8,128)(2,1)}, u32[]{:S(2)}) copy-start(bf16[256,1024]{1,0:T(8,128)(2,1)} %get-tuple-element.87) | copy-start | bytes 1572868
  174.0 19.3 %copy-start.5 = (bf16[256,1024]{1,0:T(8,128)(2,1)}, bf16[256,1024]{1,0:T(8,128)(2,1)S(1)}, u32[]{:S(2)}) copy-start(bf16[256,1024]{1,0:T(8,128)(2,1)S(1)} %add_select_fusion.own) | copy-start | bytes 1572868
  174.0 19.3 %collective-permute-start.17 = (bf16[256,1024]{1,0:T(8,128)(2,1)S(1)}, bf16[256,1024]{1,0:T(8,128)(2,1)S(1)}, u32[]{:S(2)}, u32[]{:S(2)}) collective-permute-start(bf16[256,1024]{1,0:T(8,128)(2,1)S(1)} %add_select_fusion.own), channel_id=1, source_target_pairs={{0,2},{2,0},{1,3},{3,1},{4,6},{6,4},{5,7},{7,5},{8,10},{10,8},{9,1... | collective-permute-start | bytes 1572872 | tf_op jit(solution)/shard_map/ppermute | solution.py:523
  176.5 16.8 %collective-permute-start.18 = (bf16[256,1024]{1,0:T(8,128)(2,1)S(1)}, bf16[256,1024]{1,0:T(8,128)(2,1)S(1)}, u32[]{:S(2)}, u32[]{:S(2)}) collective-permute-start(bf16[256,1024]{1,0:T(8,128)(2,1)S(1)} %add_select_fusion.own), channel_id=1, source_target_pairs={{0,1},{1,0},{2,3},{3,2},{4,5},{5,4},{6,7},{7,6},{8,9},{9,8},{10,11... | collective-permute-start | bytes 1572872 | tf_op jit(solution)/shard_map/ppermute | solution.py:523
  176.5 17.5 %collective-permute-start.14 = (bf16[256,1024]{1,0:T(8,128)(2,1)S(1)}, bf16[256,1024]{1,0:T(8,128)(2,1)S(1)}, u32[]{:S(2)}, u32[]{:S(2)}) collective-permute-start(bf16[256,1024]{1,0:T(8,128)(2,1)S(1)} %copy-done.19), channel_id=1, source_target_pairs={{4,0},{8,12},{5,1},{9,13},{6,2},{10,14},{7,3},{11,15},{20,16},{24,... | collective-permute-start | bytes 1572872 | tf_op jit(solution)/shard_map/ppermute | solution.py:521
  186.2 7.8 %copy-start.18 = (bf16[256,1024]{1,0:T(8,128)(2,1)S(1)}, bf16[256,1024]{1,0:T(8,128)(2,1)}, u32[]{:S(2)}) copy-start(bf16[256,1024]{1,0:T(8,128)(2,1)} %get-tuple-element.86) | copy-start | bytes 1572868
  193.3 2.0 copy-start.13
  193.3 2.0 copy-start.15
  193.3 2.0 collective-permute-start.20
  195.3 0.8 copy-start.17
Sparse Core Ops, SparseCore 0:
  71.5 21.0 all-gather.6
  123.8 28.6 all-gather.8
  154.0 32.1 all-gather.10
